TPU v7x, 32 devices: a whole 2x2x4 slice. The times are simulated.
32 devices in a mesh: sess: 8 (over z, x), act: 4 (over y, core).
Axes of the slice: x: 2, y: 2, z: 4, core: 2. Of those that a mesh axis runs over, the one named last changes fastest.
Arguments:
- hist: bfloat16 [4096, 131072], P('sess', 'act'), may hold values from 0.049804688 to 5
- tile_mask: int32 [32, 1024], P('sess', 'act'), may hold values 0 or 1
- planes: bfloat16 [131072, 1024], P('act', 'sess'), may hold values from -0.015625 to 0.015625
- pairs: int32 [128, 2], P('sess'), may hold values from 0 to 31
Outputs:
- scores: float32 [128, 128, 128], P(('sess', 'act'))
All inputs are finite; a program needn't handle non-finite values. No bound on the sum of `tile_mask` on one device may be relied on, other than what follows from the above.
Results may differ from a plain program's by a relative error of at most 0.0003.
Values may be sent and summed in bfloat16 or wider, within the bound.
No kernel may reach another device: no remote copies, remote signals or barrier semaphores. Data moves between devices by JAX's collectives and lax.ppermute only.
A program may use at most 192 MiB of HBM per device.

v0:
```python
import jax
import jax.numpy as jnp
from jax import lax
from jax.sharding import PartitionSpec as P

P_SIZE = 1024


def own_share(values, count):
    place = lax.axis_index("act")
    return lax.dynamic_slice_in_dim(values, place * count, count, 0)


def body(hist, tile_mask, planes, pairs):
    rows, acts = hist.shape
    row_blocks, act_blocks = tile_mask.shape
    blk = rows // row_blocks
    planes_all = P_SIZE
    masked = (
        hist.reshape(row_blocks, blk, act_blocks, blk)
        * tile_mask.astype(jnp.bfloat16)[:, None, :, None]
    ).reshape(rows, acts)
    partial_proj = jnp.dot(
        masked,
        lax.all_gather(planes, "sess", axis=1, tiled=True),
        preferred_element_type=jnp.float32,
    )
    proj = lax.psum_scatter(partial_proj, "act", scatter_dimension=1, tiled=True)
    share = proj.shape[1]
    pair_count = pairs.shape[0]
    own_count = pair_count // lax.axis_size("act")
    left_ids = pairs[:, 0]
    right_ids = pairs[:, 1]
    local_sq = lax.psum(jnp.sum(proj * proj, axis=1), "act")
    everyone, every_sq = (
        lax.all_gather(proj, "sess", axis=0, tiled=True),
        lax.all_gather(local_sq, "sess", axis=0, tiled=True),
    )
    blocks = everyone.reshape(-1, blk, share)
    norm_rows = every_sq.reshape(-1, blk)
    lefts = blocks[left_ids]
    rights = blocks[right_ids]
    dots = jnp.einsum("kuc,kvc->kuv", lefts, rights, precision=lax.Precision.HIGHEST)
    dots_own = lax.psum_scatter(dots, "act", scatter_dimension=0, tiled=True)
    left_sq = own_share(norm_rows[left_ids], own_count)
    right_sq = own_share(norm_rows[right_ids], own_count)
    left_scale = lax.rsqrt(left_sq / planes_all + 1e-06)
    right_scale = lax.rsqrt(right_sq / planes_all + 1e-06)
    return dots_own / planes_all * left_scale[:, :, None] * right_scale[:, None, :]


def solution(mesh):
    placed = (P("sess", "act"), P("sess", "act"), P("act", "sess"), P("sess", None))
    return jax.shard_map(
        body, mesh=mesh, in_specs=placed, out_specs=P(("sess", "act"), None, None), check_vma=False
    )
```

profile of v0, /device:TPU:0, one launch (start us, length us, event | category | flops | bytes accessed | tf_op | source)
XLA Modules:
  0.0 1502.5 jit_solution(10505816260948191745)
XLA Ops:
  6.5 0.0 copy-start.1
  6.5 0.0 all-gather.4.cloned.1.call-start
  6.5 0.7 all-gather.4.cloned.1.call-update
  7.3 0.0 reduce-scatter.3.cloned.1.call-start
  7.3 0.0 copy-done.1
  7.3 1272.5 %all-gather.4.cloned.1.call-done = bf16[32768,1024]{1,0:T(8,128)(2,1)} async-done(((bf16[32768,128]{1,0:T(8,128)(2,1)}), bf16[32768,1024]{1,0:T(8,128)(2,1)}) %all-gather.4.cloned.1.call-update) | async-done | bytes 67108880 | tf_op jit(solution)/shard_map/all_gather | solution.py:25
  1279.8 11.4 mul.36
  1291.2 0.0 copy-start.2
  1291.2 50.7 %fusion = f32[512,1024]{1,0:T(8,128)} fusion(bf16[32768,1024]{1,0:T(8,128)(2,1)} %all-gather.4.cloned.1.call-done, bf16[512,32768]{1,0:T(8,128)(2,1)} %param.4, bf16[64,8,256,128]{3,2,1,0:T(8,128)(2,1)} %bitcast.18), kind=kOutput, calls=%fused_computation.5 | convolution fusion | flops 34376515584 | bytes 136314880 | tf_op jit(solution)/shard_map/dot_general | solution.py:23
  1341.9 0.0 reduce-scatter.3.cloned.1.call-update
  1341.9 0.0 all-gather.6.cloned.1.call-start
  1342.0 31.6 %reduce-scatter.3.cloned.1.call-done = f32[512,256]{1,0:T(8,128)} async-done(((f32[512,1024]{1,0:T(8,128)}), f32[512,256]{1,0:T(8,128)}) %reduce-scatter.3.cloned.1.call-update) | async-done | bytes 524304 | tf_op jit(solution)/shard_map/reduce_scatter | solution.py:28
  1373.6 0.0 all-gather.6.cloned.1.call-update
  1373.6 0.0 reduce-scatter.5.cloned.1.call-start
  1373.7 0.0 copy-done.2
  1373.7 75.7 %all-gather.6.cloned.1.call-done = f32[4096,256]{1,0:T(8,128)} async-done(((f32[512,256]{1,0:T(8,128)}), f32[4096,256]{1,0:T(8,128)}) %all-gather.6.cloned.1.call-update) | async-done | bytes 4194320 | tf_op jit(solution)/shard_map/all_gather | solution.py:36
  1449.4 2.9 gather_fusion
  1452.3 4.2 gather_fusion.1
  1456.5 0.0 copy-start
  1456.5 4.7 fusion.4
  1461.2 0.0 reduce-scatter.5.cloned.1.call-update
  1461.2 0.0 copy-done
  1461.2 0.1 multiply_reduce_fusion
  1461.3 5.7 psum.7
  1467.0 26.0 %all-gather = f32[8,1,512]{2,1,0:T(1,128)S(1)} all-gather(f32[1,1,512]{2,1,0:T(1,128)S(1)} %bitcast.23), channel_id=1, replica_groups=mesh['sess'=8,'act'=4] {'sess'}, dimensions={0}, use_global_device_ids=true | all-gather | bytes 18432 | tf_op jit(solution)/shard_map/all_gather | solution.py:37
  1493.0 0.6 gather_fusion.3
  1493.6 0.6 gather_fusion.2
  1494.2 0.0 reduce-scatter.5.cloned.1.call-done
  1494.2 1.8 multiply_multiply_fusion
  (5 shorter events, 0.1 us)
Async XLA Ops:
  6.5 0.8 copy-start.1
  6.5 1273.2 %all-gather.4.cloned.1.call-start = ((), (), s32[]{:S(2)}) async-start(), calls=%async_computation.2 | async-start | bytes 75497472 | tf_op jit(solution)/shard_map/all_gather | solution.py:25
  7.3 1366.3 %reduce-scatter.3.cloned.1.call-start = ((), (), s32[]{:S(2)}) async-start(), calls=%async_computation.3 | async-start | bytes 2621440 | tf_op jit(solution)/shard_map/reduce_scatter | solution.py:28
  1291.2 82.5 %copy-start.2 = (s32[16,2]{0,1:T(2,128)S(1)}, s32[16,2]{0,1:T(2,128)}, u32[]{:S(2)}) copy-start(s32[16,2]{0,1:T(2,128)} %param.7) | copy-start | bytes 388
  1341.9 107.5 %all-gather.6.cloned.1.call-start = ((), (), s32[]{:S(2)}) async-start(), calls=%async_computation.4 | async-start | bytes 4718592 | tf_op jit(solution)/shard_map/all_gather | solution.py:36
  1373.6 120.6 %reduce-scatter.5.cloned.1.call-start = ((), (), s32[]{:S(2)}) async-start(), calls=%async_computation.5 | async-start | bytes 1310720 | tf_op jit(solution)/shard_map/reduce_scatter | solution.py:44
  1456.5 4.7 copy-start
Sparse Core Ops, SparseCore 0:
  8.8 1270.9 all-gather.3
  1342.1 31.4 reduce-scatter.2
  1375.9 73.4 all-gather.5
  1461.3 23.1 reduce-scatter.4
where the time goes:
time: 1500 us
  waiting for transfers between devices  1380 us (92%)
  matrix products  55.4 us (4%)
  blocking collectives  31.7 us (2%)
  local copies, waits for them, and re-layouts  19.6 us (1%)
    all_gather x1, waiting for transfers between devices, body(): lax.all_gather(planes, 'sess', axis=1, tiled=True)  1270 us
    all_gather x1, waiting for transfers between devices, body(): lax.all_gather(proj, 'sess', axis=0, tiled=True)  75.7 us
    dot_general x1, matrix products, body(): jnp.dot(masked, lax.all_gather(planes, 'sess', axis=1, tiled=True), prefe...  50.7 us
    reduce_scatter x1, waiting for transfers between devices, body(): lax.psum_scatter(partial_proj, 'act', scatter_dimension=1, tiled=True)  31.6 us
  transfers between devices with their start and end apart: 4, of which 3 were waited for; matrix products, arithmetic and copies ran while one was open for 0% of the time, Pallas kernels for 0%

commit v1 on v0

v1 whole, which is shorter than its diff:
```python
import functools

import jax
import jax.numpy as jnp
import numpy as np
from jax import lax
from jax.sharding import Mesh, PartitionSpec as P

P_SIZE = 1024
DEPTH = 4
CORES = 2
CHUNKS = 4
PLANE = ("x", "y", "core")


def ring_order(count):
    return list(range(0, count, 2)) + list(range(1, count, 2))[::-1]


def ring_pairs(count):
    order = ring_order(count)
    return [(order[k], order[(k + 1) % count]) for k in range(count)]


def ring_source(z, step, count):
    order = np.array(ring_order(count))
    place = np.argsort(order)
    table = np.array([[order[(place[d] - s) % count] for s in range(count)] for d in range(count)], np.int32)
    return jnp.asarray(table)[z, step]


def body(hist, tile_mask, planes, pairs):
    rows, acts = hist.shape
    row_blocks, act_blocks = tile_mask.shape
    blk = rows // row_blocks
    own_planes = planes.shape[1]
    wide = lax.axis_size("x")
    deep = lax.axis_size("z")
    x, z = lax.axis_index("x"), lax.axis_index("z")
    span = acts // wide
    step = span // CHUNKS

    def masked_part(owner, chunk):
        start = owner * span + chunk * step
        part = lax.dynamic_slice_in_dim(hist, start, step, 1)
        mask = lax.dynamic_slice_in_dim(tile_mask, start // blk, step // blk, 1).astype(jnp.bfloat16)
        return (part.reshape(row_blocks, blk, step // blk, blk) * mask[:, None, :, None]).reshape(rows, step)

    def planes_part(owner, chunk):
        return lax.dynamic_slice_in_dim(planes, owner * span + chunk * step, step, 0)

    def turn(k):
        return [(d, (d + k) % wide) for d in range(wide)]

    groups = []
    for c in range(CHUNKS):
        parts = [planes_part(x, c)] + [
            lax.ppermute(planes_part((x + k) % wide, c), "x", turn(k)) for k in range(1, wide)
        ]
        whole = jnp.zeros((step, wide * own_planes), planes.dtype)
        for k, part in enumerate(parts):
            whole = lax.dynamic_update_slice_in_dim(whole, part, ((x - k) % wide) * own_planes, 1)
        groups.append(whole)

    hists = [
        [masked_part(x, c)]
        + [lax.ppermute(masked_part((x + k) % wide, c), "x", turn(k)) for k in range(1, wide)]
        for c in range(CHUNKS)
    ]

    order = (x - jnp.arange(wide)) % wide
    shares = []
    for s in range(deep):
        total = []
        for k in range(wide):
            one = 0.0
            for c in range(CHUNKS):
                one = one + jnp.dot(hists[c][k], groups[c], preferred_element_type=jnp.float32)
            total.append(one)
        total = jnp.stack(total)[order].reshape(wide * rows, wide * own_planes)
        shares.append(lax.psum_scatter(total, PLANE, scatter_dimension=1, tiled=True))
        if s < deep - 1:
            groups = [lax.ppermute(g, "z", ring_pairs(deep)) for g in groups]
    shares = jnp.stack(shares)[jnp.argsort(jnp.stack([ring_source(z, s, deep) for s in range(deep)]))]
    proj = jnp.moveaxis(shares, 0, 1).reshape(wide * rows, -1)

    everyone = lax.all_gather(proj, "z", axis=0, tiled=True)
    blocks = everyone.reshape(-1, blk, proj.shape[1])
    all_pairs = lax.all_gather(pairs, "x", axis=0, tiled=True)
    left_ids, right_ids = all_pairs[:, 0], all_pairs[:, 1]
    lefts, rights = blocks[left_ids], blocks[right_ids]
    dots = jnp.einsum("kuc,kvc->kuv", lefts, rights, precision=lax.Precision.HIGHEST)
    sq = jnp.sum(blocks * blocks, axis=2)
    sums = jnp.concatenate([dots, sq[left_ids][:, None], sq[right_ids][:, None]], axis=1)
    own = lax.psum_scatter(sums, PLANE, scatter_dimension=0, tiled=True)
    scale = lax.rsqrt(own[:, blk:] / P_SIZE + 1e-06)
    return own[:, :blk] / P_SIZE * scale[:, 0, :, None] * scale[:, 1, None, :]


def solution(mesh):
    sess, act = mesh.shape["sess"], mesh.shape["act"]
    fine = Mesh(
        mesh.devices.reshape(DEPTH, sess // DEPTH, act // CORES, CORES), ("z", "x", "y", "core")
    )
    sess_axes, act_axes = ("z", "x"), ("y", "core")
    placed = (
        P(sess_axes, act_axes), P(sess_axes, act_axes), P(act_axes, sess_axes), P(sess_axes, None)
    )
    return jax.shard_map(
        body, mesh=fine, in_specs=placed, out_specs=P(sess_axes + act_axes, None, None), check_vma=False
    )
```

time: 1500 us -> 831 us (0.55)
  waiting for transfers between devices: 1380 us -> 552 us
  other arithmetic: 1.99 us -> 54.9 us
  matrix products: 55.4 us -> 104 us
  local copies, waits for them, and re-layouts: 19.6 us -> 60.1 us
  starting transfers between devices: 0.12 us -> 34.5 us
  blocking collectives: 31.7 us -> 4.54 us
    all_gather x2 -> x1, waiting for transfers between devices: 1350 us -> 41.4 us  [body(): everyone = lax.all_gather(proj, 'z', axis=0, tiled=True)]
    ppermute x0 -> x20, waiting for transfers between devices: none -> 437 us  [the longest x12 269 us: body(): groups = [lax.ppermute(g, 'z', ring_pairs(deep)) for g in groups]]
    dot_general x1 -> x32, matrix products: 50.7 us -> 97.6 us  [body(): jnp.dot(hists[c][k], groups[c], preferred_element_type=jnp.float32)]
    mul x2 -> x3, other arithmetic: 1.81 us -> 46 us  [the longest x1 44.2 us: masked_part(): part.reshape(row_blocks, blk, step // blk, blk) * mask[:, None, :, None]]
    reduce_scatter x2 -> x5, waiting for transfers between devices: 31.6 us -> 73.8 us  [the longest x1 40.8 us: body(): own = lax.psum_scatter(sums, PLANE, scatter_dimension=0, tiled=True)]
    ppermute x0 -> x20, starting transfers between devices: none -> 34.3 us  [the longest x12 24.2 us: body(): groups = [lax.ppermute(g, 'z', ring_pairs(deep)) for g in groups]]
    all_gather x1, blocking collectives: 26 us -> 4.54 us  [body(): all_pairs = lax.all_gather(pairs, 'x', axis=0, tiled=True)]
  transfers between devices with their start and end apart: 4 -> 26, of which waited for: 3 -> 15; matrix products, arithmetic and copies ran while one was open for 0% -> 23% of each run, Pallas kernels for 0% -> 0%
where the time goes in v1:
time: 831 us; the launch traced here: 825 us
  waiting for transfers between devices  552 us (66%)
  matrix products  104 us (13%)
  local copies, waits for them, and re-layouts  60.1 us (7%)
  other arithmetic  54.9 us (7%)
  starting transfers between devices  34.5 us (4%)
  between operations  14.7 us (2%)
    ppermute x12, waiting for transfers between devices, body(): groups = [lax.ppermute(g, 'z', ring_pairs(deep)) for g in groups]  269 us
    ppermute x4, waiting for transfers between devices, body(): lax.ppermute(masked_part((x + k) % wide, c), 'x', turn(k))  166 us
    dot_general x32, matrix products, body(): jnp.dot(hists[c][k], groups[c], preferred_element_type=jnp.float32)  97.6 us
    mul x1, other arithmetic, masked_part(): part.reshape(row_blocks, blk, step // blk, blk) * mask[:, None, :, None]  44.2 us
    all_gather x1, waiting for transfers between devices, body(): everyone = lax.all_gather(proj, 'z', axis=0, tiled=True)  41.4 us
    reduce_scatter x1, waiting for transfers between devices, body(): own = lax.psum_scatter(sums, PLANE, scatter_dimension=0, tiled=True)  40.8 us
    reduce_scatter x4, waiting for transfers between devices, body(): lax.psum_scatter(total, PLANE, scatter_dimension=1, tiled=True)  33.1 us
    ppermute x12, starting transfers between devices, body(): groups = [lax.ppermute(g, 'z', ring_pairs(deep)) for g in groups]  24.2 us
  transfers between devices with their start and end apart: 26, of which 15 were waited for; matrix products, arithmetic and copies ran while one was open for 23% of the time, Pallas kernels for 0%

profile of v1, /device:TPU:0, one launch (start us, length us, event | category | flops | bytes accessed | tf_op | source)
XLA Modules:
  0.0 825.2 jit_solution(5356110961877420917)
XLA Ops:
  6.7 4.2 constant_dynamic-slice_fusion.11
  10.9 2.9 collective-permute-start.2
  16.0 2.6 mul.149
  18.6 2.6 mul.155
  21.2 2.7 mul.158
  23.9 2.6 mul.161
  26.5 2.6 mul.164
  29.1 2.6 mul.167
  31.7 2.6 mul.170
  34.3 2.6 mul.173
  36.9 44.2 %bitcast_multiply_fusion.7 = (bf16[512,4096]{1,0:T(8,128)(2,1)}, bf16[512,4096]{1,0:T(8,128)(2,1)}, bf16[512,4096]{1,0:T(8,128)(2,1)}, bf16[512,4096]{1,0:T(8,12...) fusion(bf16[64,8,32,128]{3,2,1,0:T(8,128)(2,1)} %bitcast.146, ...), kind=kLoop, calls=%fused_computation.16 | loop fusion | flops 67108864 | bytes 100663328 | tf_op jit(solution)/shard_map/mul | solution.py:47
  84.6 2.3 dynamic-slice_dynamic-update-slice_fusion.2
  88.4 2.3 dynamic-slice_dynamic-update-slice_fusion
  92.2 2.6 collective-permute-start.10
  94.8 2.3 constant_dynamic-update-slice_fusion.2
  98.7 2.3 constant_dynamic-update-slice_fusion
  110.6 30.3 %collective-permute-done.10 = bf16[4096,256]{1,0:T(8,128)(2,1)} collective-permute-done((bf16[4096,256]{1,0:T(8,128)(2,1)S(1)}, bf16[4096,256]{1,0:T(8,128)(2,1)}, u32[]{:S(2)}, u32[]{:S(2)}) %collective-permute-start.10) | collective-permute-done | bytes 2097184 | tf_op jit(solution)/shard_map/ppermute | solution.py:83
  141.4 2.9 fusion.39
  144.3 41.6 %collective-permute-done.9 = bf16[4096,256]{1,0:T(8,128)(2,1)} collective-permute-done((bf16[4096,256]{1,0:T(8,128)(2,1)}, bf16[4096,256]{1,0:T(8,128)(2,1)}, u32[]{:S(2)}, u32[]{:S(2)}) %collective-permute-start.9) | collective-permute-done | bytes 2097184 | tf_op jit(solution)/shard_map/ppermute | solution.py:83
  186.5 41.8 %collective-permute-done.11 = bf16[4096,256]{1,0:T(8,128)(2,1)} collective-permute-done((bf16[4096,256]{1,0:T(8,128)(2,1)}, bf16[4096,256]{1,0:T(8,128)(2,1)}, u32[]{:S(2)}, u32[]{:S(2)}) %collective-permute-start.11) | collective-permute-done | bytes 2097184 | tf_op jit(solution)/shard_map/ppermute | solution.py:83
  228.3 3.4 collective-permute-start.8
  231.7 2.9 fusion.41
  235.9 2.9 fusion.46
  238.7 2.9 fusion.45
  241.6 2.9 fusion.47
  244.5 29.7 %collective-permute-done.8 = bf16[4096,256]{1,0:T(8,128)(2,1)} collective-permute-done((bf16[4096,256]{1,0:T(8,128)(2,1)S(1)}, bf16[4096,256]{1,0:T(8,128)(2,1)}, u32[]{:S(2)}, u32[]{:S(2)}) %collective-permute-start.8) | collective-permute-done | bytes 2097184 | tf_op jit(solution)/shard_map/ppermute | solution.py:83
  274.2 3.5 collective-permute-start.14
  277.7 2.9 fusion.8
  280.7 3.4 fusion.43
  285.2 3.2 collective-permute-start.15
  288.4 2.9 fusion.42
  291.3 83.9 %collective-permute-done.7 = bf16[512,4096]{1,0:T(8,128)(2,1)} collective-permute-done((bf16[512,4096]{1,0:T(8,128)(2,1)S(1)}, bf16[512,4096]{1,0:T(8,128)(2,1)}, u32[]{:S(2)}, u32[]{:S(2)}) %collective-permute-start.7) | collective-permute-done | bytes 4194336 | tf_op jit(solution)/shard_map/ppermute | solution.py:67
  375.2 3.3 collective-permute-start.12
  378.5 4.1 fusion.44
  382.6 81.5 %collective-permute-done.4 = bf16[512,4096]{1,0:T(8,128)(2,1)S(1)} collective-permute-done((bf16[512,4096]{1,0:T(8,128)(2,1)S(1)}, bf16[512,4096]{1,0:T(8,128)(2,1)S(1)}, u32[]{:S(2)}, u32[]{:S(2)}) %collective-permute-start.4) | collective-permute-done | bytes 4194336 | tf_op jit(solution)/shard_map/ppermute | solution.py:67
  468.3 4.3 fusion.49
  472.6 2.9 fusion.48
  475.5 4.4 fusion.50
  479.9 3.0 fusion.11
  485.0 2.9 collective-permute-start.18
  490.0 4.1 fusion.52
  494.1 3.0 fusion.51
  497.2 3.0 fusion.53
  500.3 3.0 fusion.14
  503.2 4.3 fusion.55
  507.6 2.9 fusion.54
  510.4 4.3 fusion.56
  514.7 2.9 fusion.17
  520.2 14.1 %collective-permute-done.18 = bf16[4096,256]{1,0:T(8,128)(2,1)} collective-permute-done((bf16[4096,256]{1,0:T(8,128)(2,1)}, bf16[4096,256]{1,0:T(8,128)(2,1)}, u32[]{:S(2)}, u32[]{:S(2)}) %collective-permute-start.18) | collective-permute-done | bytes 2097184 | tf_op jit(solution)/shard_map/ppermute | solution.py:83
  534.3 4.2 fusion.58
  538.5 4.3 fusion.61
  542.8 36.4 %collective-permute-done.17 = bf16[4096,256]{1,0:T(8,128)(2,1)} collective-permute-done((bf16[4096,256]{1,0:T(8,128)(2,1)}, bf16[4096,256]{1,0:T(8,128)(2,1)}, u32[]{:S(2)}, u32[]{:S(2)}) %collective-permute-start.17) | collective-permute-done | bytes 2097184 | tf_op jit(solution)/shard_map/ppermute | solution.py:83
  579.2 2.9 fusion.57
  582.2 3.0 fusion.60
  585.2 39.0 %collective-permute-done.19 = bf16[4096,256]{1,0:T(8,128)(2,1)} collective-permute-done((bf16[4096,256]{1,0:T(8,128)(2,1)}, bf16[4096,256]{1,0:T(8,128)(2,1)}, u32[]{:S(2)}, u32[]{:S(2)}) %collective-permute-start.19) | collective-permute-done | bytes 2097184 | tf_op jit(solution)/shard_map/ppermute | solution.py:83
  624.2 2.9 fusion.59
  627.1 4.3 fusion.62
  631.3 35.7 %collective-permute-done.16 = bf16[4096,256]{1,0:T(8,128)(2,1)S(1)} collective-permute-done((bf16[4096,256]{1,0:T(8,128)(2,1)}, bf16[4096,256]{1,0:T(8,128)(2,1)S(1)}, u32[]{:S(2)}, u32[]{:S(2)}) %collective-permute-start.16) | collective-permute-done | bytes 2097184 | tf_op jit(solution)/shard_map/ppermute | solution.py:83
  672.4 2.6 pad_add_fusion
  675.8 33.0 %reduce-scatter.12.cloned.1.call-done = f32[1024,32]{0,1:T(8,128)} async-done(((f32[1024,256]{0,1:T(8,128)}), f32[1024,32]{0,1:T(8,128)}) %reduce-scatter.12.cloned.1.call-update) | async-done | bytes 131088 | tf_op jit(solution)/shard_map/reduce_scatter | solution.py:81
  711.4 4.5 all-gather
  716.1 41.4 %all-gather.3.cloned.1.call-done = f32[4096,128]{0,1:T(8,128)} async-done(((f32[1024,128]{0,1:T(8,128)}), f32[4096,128]{0,1:T(8,128)}) %all-gather.3.cloned.1.call-update) | async-done | bytes 2097168 | tf_op jit(solution)/shard_map/all_gather | solution.py:87
  766.3 6.7 fusion.63
  774.6 40.8 %reduce-scatter.14.cloned.1.call-done = f32[4,130,128]{2,1,0:T(8,128)} async-done(((f32[32,130,128]{2,1,0:T(8,128)}), f32[4,130,128]{2,1,0:T(8,128)}) %reduce-scatter.14.cloned.1.call-update) | async-done | bytes 266256 | tf_op jit(solution)/shard_map/reduce_scatter | solution.py:95
  (134 shorter events, 55.8 us)
Async XLA Ops:
  6.5 669.2 %reduce-scatter.6.cloned.1.call-start = ((), (), s32[]{:S(2)}) async-start(), calls=%async_computation.5 | async-start | bytes 1179648 | tf_op jit(solution)/shard_map/reduce_scatter | solution.py:81
  6.7 9.2 %copy-start.13 = (s32[4,256]{1,0:T(4,128)S(1)}, s32[4,256]{1,0:T(4,128)}, u32[]{:S(2)}) copy-start(s32[4,256]{1,0:T(4,128)} %param.9) | copy-start | bytes 12292
  10.9 79.8 %collective-permute-start.2 = (bf16[4096,128]{1,0:T(8,128)(2,1)}, bf16[4096,128]{1,0:T(8,128)(2,1)}, u32[]{:S(2)}, u32[]{:S(2)}) collective-permute-start(bf16[4096,128]{1,0:T(8,128)(2,1)} %get-tuple-element.16), channel_id=1, source_target_pairs={{0,4},{4,0},{1,5},{5,1},{2,6},{6,2},{3,7},{7,3},{8,12},{12,8},{9,1... | collective-permute-start | bytes 3145736 | tf_op jit(solution)/shard_map/ppermute | solution.py:58
  13.8 81.0 %collective-permute-start.1 = (bf16[4096,128]{1,0:T(8,128)(2,1)}, bf16[4096,128]{1,0:T(8,128)(2,1)}, u32[]{:S(2)}, u32[]{:S(2)}) collective-permute-start(bf16[4096,128]{1,0:T(8,128)(2,1)} %get-tuple-element.18), channel_id=1, source_target_pairs={{0,4},{4,0},{1,5},{5,1},{2,6},{6,2},{3,7},{7,3},{8,12},{12,8},{9,1... | collective-permute-start | bytes 3145736 | tf_op jit(solution)/shard_map/ppermute | solution.py:58
  13.9 84.9 %collective-permute-start.3 = (bf16[4096,128]{1,0:T(8,128)(2,1)}, bf16[4096,128]{1,0:T(8,128)(2,1)}, u32[]{:S(2)}, u32[]{:S(2)}) collective-permute-start(bf16[4096,128]{1,0:T(8,128)(2,1)} %get-tuple-element.19), channel_id=1, source_target_pairs={{0,4},{4,0},{1,5},{5,1},{2,6},{6,2},{3,7},{7,3},{8,12},{12,8},{9,1... | collective-permute-start | bytes 3145736 | tf_op jit(solution)/shard_map/ppermute | solution.py:58
  15.9 89.7 %collective-permute-start = (bf16[4096,128]{1,0:T(8,128)(2,1)S(1)}, bf16[4096,128]{1,0:T(8,128)(2,1)}, u32[]{:S(2)}, u32[]{:S(2)}) collective-permute-start(bf16[4096,128]{1,0:T(8,128)(2,1)S(1)} %get-tuple-element.15), channel_id=1, source_target_pairs={{0,4},{4,0},{1,5},{5,1},{2,6},{6,2},{3,7},{7,3},{8,12},{12,8},{9,1... | collective-permute-start | bytes 3145736 | tf_op jit(solution)/shard_map/ppermute | solution.py:58
  81.0 199.6 %collective-permute-start.6 = (bf16[512,4096]{1,0:T(8,128)(2,1)}, bf16[512,4096]{1,0:T(8,128)(2,1)}, u32[]{:S(2)}, u32[]{:S(2)}) collective-permute-start(bf16[512,4096]{1,0:T(8,128)(2,1)} %get-tuple-element.14), channel_id=1, source_target_pairs={{0,4},{4,0},{1,5},{5,1},{2,6},{6,2},{3,7},{7,3},{8,12},{12,8},{9,1... | collective-permute-start | bytes 12582920 | tf_op jit(solution)/shard_map/ppermute | solution.py:67
  92.2 13.4 %copy-start.12 = (bf16[512,4096]{1,0:T(8,128)(2,1)S(1)}, bf16[512,4096]{1,0:T(8,128)(2,1)}, u32[]{:S(2)}) copy-start(bf16[512,4096]{1,0:T(8,128)(2,1)} %get-tuple-element.8) | copy-start | bytes 12582916
  92.2 48.7 %collective-permute-start.10 = (bf16[4096,256]{1,0:T(8,128)(2,1)S(1)}, bf16[4096,256]{1,0:T(8,128)(2,1)}, u32[]{:S(2)}, u32[]{:S(2)}) collective-permute-start(bf16[4096,256]{1,0:T(8,128)(2,1)S(1)} %constant_dynamic-update-slice_fusion.1), channel_id=1, source_target_pairs={{0,16},{16,24},{24,8},{8,0},{1,17},{17,25},{25,9},{9,1},{2,18},{18... | collective-permute-start | bytes 6291464 | tf_op jit(solution)/shard_map/ppermute | solution.py:83
  97.2 12.1 %copy-start.9 = (bf16[512,4096]{1,0:T(8,128)(2,1)S(1)}, bf16[512,4096]{1,0:T(8,128)(2,1)}, u32[]{:S(2)}) copy-start(bf16[512,4096]{1,0:T(8,128)(2,1)} %get-tuple-element.11) | copy-start | bytes 12582916
  97.2 88.8 %collective-permute-start.9 = (bf16[4096,256]{1,0:T(8,128)(2,1)}, bf16[4096,256]{1,0:T(8,128)(2,1)}, u32[]{:S(2)}, u32[]{:S(2)}) collective-permute-start(bf16[4096,256]{1,0:T(8,128)(2,1)} %constant_dynamic-update-slice_fusion.2), channel_id=1, source_target_pairs={{0,16},{16,24},{24,8},{8,0},{1,17},{17,25},{25,9},{9,1},{2,18},{18... | collective-permute-start | bytes 6291464 | tf_op jit(solution)/shard_map/ppermute | solution.py:83
  101.0 127.3 %collective-permute-start.11 = (bf16[4096,256]{1,0:T(8,128)(2,1)}, bf16[4096,256]{1,0:T(8,128)(2,1)}, u32[]{:S(2)}, u32[]{:S(2)}) collective-permute-start(bf16[4096,256]{1,0:T(8,128)(2,1)} %constant_dynamic-update-slice_fusion), channel_id=1, source_target_pairs={{0,16},{16,24},{24,8},{8,0},{1,17},{17,25},{25,9},{9,1},{2,18},{18... | collective-permute-start | bytes 6291464 | tf_op jit(solution)/shard_map/ppermute | solution.py:83
  105.5 179.7 %collective-permute-start.5 = (bf16[512,4096]{1,0:T(8,128)(2,1)S(1)}, bf16[512,4096]{1,0:T(8,128)(2,1)S(1)}, u32[]{:S(2)}, u32[]{:S(2)}) collective-permute-start(bf16[512,4096]{1,0:T(8,128)(2,1)S(1)} %copy-done.12), channel_id=1, source_target_pairs={{0,4},{4,0},{1,5},{5,1},{2,6},{6,2},{3,7},{7,3},{8,12},{12,8},{9,1... | collective-permute-start | bytes 12582920 | tf_op jit(solution)/shard_map/ppermute | solution.py:67
  107.6 33.3 %copy-start.11 = (bf16[512,4096]{1,0:T(8,128)(2,1)S(1)}, bf16[512,4096]{1,0:T(8,128)(2,1)}, u32[]{:S(2)}) copy-start(bf16[512,4096]{1,0:T(8,128)(2,1)} %get-tuple-element.13) | copy-start | bytes 12582916
  109.2 32.2 %copy-start.6 = (bf16[512,4096]{1,0:T(8,128)(2,1)S(1)}, bf16[512,4096]{1,0:T(8,128)(2,1)}, u32[]{:S(2)}) copy-start(bf16[512,4096]{1,0:T(8,128)(2,1)} %get-tuple-element.12) | copy-start | bytes 12582916
  109.3 76.7 %copy-start.10 = (bf16[512,4096]{1,0:T(8,128)(2,1)S(1)}, bf16[512,4096]{1,0:T(8,128)(2,1)}, u32[]{:S(2)}) copy-start(bf16[512,4096]{1,0:T(8,128)(2,1)} %get-tuple-element.9) | copy-start | bytes 12582916
  110.6 121.1 %copy-start.3 = (bf16[512,4096]{1,0:T(8,128)(2,1)S(1)}, bf16[512,4096]{1,0:T(8,128)(2,1)}, u32[]{:S(2)}) copy-start(bf16[512,4096]{1,0:T(8,128)(2,1)} %get-tuple-element.10) | copy-start | bytes 12582916
  140.9 234.3 %collective-permute-start.7 = (bf16[512,4096]{1,0:T(8,128)(2,1)S(1)}, bf16[512,4096]{1,0:T(8,128)(2,1)}, u32[]{:S(2)}, u32[]{:S(2)}) collective-permute-start(bf16[512,4096]{1,0:T(8,128)(2,1)S(1)} %copy-done.11), channel_id=1, source_target_pairs={{0,4},{4,0},{1,5},{5,1},{2,6},{6,2},{3,7},{7,3},{8,12},{12,8},{9,1... | collective-permute-start | bytes 12582920 | tf_op jit(solution)/shard_map/ppermute | solution.py:67
  144.3 90.3 %copy-start = (bf16[512,4096]{1,0:T(8,128)(2,1)S(1)}, bf16[512,4096]{1,0:T(8,128)(2,1)}, u32[]{:S(2)}) copy-start(bf16[512,4096]{1,0:T(8,128)(2,1)} %get-tuple-element.7) | copy-start | bytes 12582916
  186.0 278.2 %collective-permute-start.4 = (bf16[512,4096]{1,0:T(8,128)(2,1)S(1)}, bf16[512,4096]{1,0:T(8,128)(2,1)S(1)}, u32[]{:S(2)}, u32[]{:S(2)}) collective-permute-start(bf16[512,4096]{1,0:T(8,128)(2,1)S(1)} %copy-done.10), channel_id=1, source_target_pairs={{0,4},{4,0},{1,5},{5,1},{2,6},{6,2},{3,7},{7,3},{8,12},{12,8},{9,1... | collective-permute-start | bytes 12582920 | tf_op jit(solution)/shard_map/ppermute | solution.py:67
  228.3 45.9 %collective-permute-start.8 = (bf16[4096,256]{1,0:T(8,128)(2,1)S(1)}, bf16[4096,256]{1,0:T(8,128)(2,1)}, u32[]{:S(2)}, u32[]{:S(2)}) collective-permute-start(bf16[4096,256]{1,0:T(8,128)(2,1)S(1)} %constant_dynamic-update-slice_fusion.3), channel_id=1, source_target_pairs={{0,16},{16,24},{24,8},{8,0},{1,17},{17,25},{25,9},{9,1},{2,18},{18... | collective-permute-start | bytes 6291464 | tf_op jit(solution)/shard_map/ppermute | solution.py:83
  274.2 210.7 %collective-permute-start.14 = (bf16[4096,256]{1,0:T(8,128)(2,1)}, bf16[4096,256]{1,0:T(8,128)(2,1)}, u32[]{:S(2)}, u32[]{:S(2)}) collective-permute-start(bf16[4096,256]{1,0:T(8,128)(2,1)} %collective-permute-done.10), channel_id=1, source_target_pairs={{0,16},{16,24},{24,8},{8,0},{1,17},{17,25},{25,9},{9,1},{2,18},{18... | collective-permute-start | bytes 6291464 | tf_op jit(solution)/shard_map/ppermute | solution.py:83
  280.6 207.3 %collective-permute-start.13 = (bf16[4096,256]{1,0:T(8,128)(2,1)}, bf16[4096,256]{1,0:T(8,128)(2,1)}, u32[]{:S(2)}, u32[]{:S(2)}) collective-permute-start(bf16[4096,256]{1,0:T(8,128)(2,1)} %collective-permute-done.9), channel_id=1, source_target_pairs={{0,16},{16,24},{24,8},{8,0},{1,17},{17,25},{25,9},{9,1},{2,18},{18... | collective-permute-start | bytes 6291464 | tf_op jit(solution)/shard_map/ppermute | solution.py:83
  285.2 97.4 %copy-start.20 = (bf16[512,4096]{1,0:T(8,128)(2,1)}, bf16[512,4096]{1,0:T(8,128)(2,1)S(1)}, u32[]{:S(2)}) copy-start(bf16[512,4096]{1,0:T(8,128)(2,1)S(1)} %collective-permute-done.5) | copy-start | bytes 12582916
  285.2 204.3 %collective-permute-start.15 = (bf16[4096,256]{1,0:T(8,128)(2,1)}, bf16[4096,256]{1,0:T(8,128)(2,1)}, u32[]{:S(2)}, u32[]{:S(2)}) collective-permute-start(bf16[4096,256]{1,0:T(8,128)(2,1)} %collective-permute-done.11), channel_id=1, source_target_pairs={{0,16},{16,24},{24,8},{8,0},{1,17},{17,25},{25,9},{9,1},{2,18},{18... | collective-permute-start | bytes 6291464 | tf_op jit(solution)/shard_map/ppermute | solution.py:83
  375.2 125.0 %collective-permute-start.12 = (bf16[4096,256]{1,0:T(8,128)(2,1)}, bf16[4096,256]{1,0:T(8,128)(2,1)}, u32[]{:S(2)}, u32[]{:S(2)}) collective-permute-start(bf16[4096,256]{1,0:T(8,128)(2,1)} %collective-permute-done.8), channel_id=1, source_target_pairs={{0,16},{16,24},{24,8},{8,0},{1,17},{17,25},{25,9},{9,1},{2,18},{18... | collective-permute-start | bytes 6291464 | tf_op jit(solution)/shard_map/ppermute | solution.py:83
  464.1 2.0 copy-start.16
  468.2 207.5 %reduce-scatter.8.cloned.1.call-start = ((), (), s32[]{:S(2)}) async-start(), calls=%async_computation.6 | async-start | bytes 1179648 | tf_op jit(solution)/shard_map/reduce_scatter | solution.py:81
  468.3 4.3 copy-start.21
  475.4 4.4 copy-start.17
  484.9 190.9 %reduce-scatter.10.cloned.1.call-start = ((), (), s32[]{:S(2)}) async-start(), calls=%async_computation.7 | async-start | bytes 1179648 | tf_op jit(solution)/shard_map/reduce_scatter | solution.py:81
  485.0 9.1 %copy-start.7 = (bf16[512,4096]{1,0:T(8,128)(2,1)S(1)}, bf16[512,4096]{1,0:T(8,128)(2,1)}, u32[]{:S(2)}) copy-start(bf16[512,4096]{1,0:T(8,128)(2,1)} %get-tuple-element.12) | copy-start | bytes 12582916
  485.0 49.3 %collective-permute-start.18 = (bf16[4096,256]{1,0:T(8,128)(2,1)}, bf16[4096,256]{1,0:T(8,128)(2,1)}, u32[]{:S(2)}, u32[]{:S(2)}) collective-permute-start(bf16[4096,256]{1,0:T(8,128)(2,1)} %collective-permute-done.14), channel_id=1, source_target_pairs={{0,16},{16,24},{24,8},{8,0},{1,17},{17,25},{25,9},{9,1},{2,18},{18... | collective-permute-start | bytes 6291464 | tf_op jit(solution)/shard_map/ppermute | solution.py:83
  487.9 91.3 %collective-permute-start.17 = (bf16[4096,256]{1,0:T(8,128)(2,1)}, bf16[4096,256]{1,0:T(8,128)(2,1)}, u32[]{:S(2)}, u32[]{:S(2)}) collective-permute-start(bf16[4096,256]{1,0:T(8,128)(2,1)} %collective-permute-done.13), channel_id=1, source_target_pairs={{0,16},{16,24},{24,8},{8,0},{1,17},{17,25},{25,9},{9,1},{2,18},{18... | collective-permute-start | bytes 6291464 | tf_op jit(solution)/shard_map/ppermute | solution.py:83
  489.5 134.7 %collective-permute-start.19 = (bf16[4096,256]{1,0:T(8,128)(2,1)}, bf16[4096,256]{1,0:T(8,128)(2,1)}, u32[]{:S(2)}, u32[]{:S(2)}) collective-permute-start(bf16[4096,256]{1,0:T(8,128)(2,1)} %collective-permute-done.15), channel_id=1, source_target_pairs={{0,16},{16,24},{24,8},{8,0},{1,17},{17,25},{25,9},{9,1},{2,18},{18... | collective-permute-start | bytes 6291464 | tf_op jit(solution)/shard_map/ppermute | solution.py:83
  494.1 3.1 copy-start.4
  497.2 3.1 copy-start.1
  503.2 4.3 copy-start.22
  510.4 4.3 copy-start.18
  519.7 189.1 %reduce-scatter.12.cloned.1.call-start = ((), (), s32[]{:S(2)}) async-start(), calls=%async_computation.8 | async-start | bytes 1179648 | tf_op jit(solution)/shard_map/reduce_scatter | solution.py:81
  519.7 147.3 %collective-permute-start.16 = (bf16[4096,256]{1,0:T(8,128)(2,1)}, bf16[4096,256]{1,0:T(8,128)(2,1)S(1)}, u32[]{:S(2)}, u32[]{:S(2)}) collective-permute-start(bf16[4096,256]{1,0:T(8,128)(2,1)} %collective-permute-done.12), channel_id=1, source_target_pairs={{0,16},{16,24},{24,8},{8,0},{1,17},{17,25},{25,9},{9,1},{2,18},{18... | collective-permute-start | bytes 6291464 | tf_op jit(solution)/shard_map/ppermute | solution.py:83
  538.5 40.8 %copy-start.8 = (bf16[512,4096]{1,0:T(8,128)(2,1)S(1)}, bf16[512,4096]{1,0:T(8,128)(2,1)}, u32[]{:S(2)}) copy-start(bf16[512,4096]{1,0:T(8,128)(2,1)} %get-tuple-element.12) | copy-start | bytes 12582916
  542.8 39.3 %copy-start.23 = (bf16[512,4096]{1,0:T(8,128)(2,1)S(1)}, bf16[512,4096]{1,0:T(8,128)(2,1)}, u32[]{:S(2)}) copy-start(bf16[512,4096]{1,0:T(8,128)(2,1)} %copy-done.20) | copy-start | bytes 12582916
  582.1 42.0 %copy-start.5 = (bf16[512,4096]{1,0:T(8,128)(2,1)S(1)}, bf16[512,4096]{1,0:T(8,128)(2,1)}, u32[]{:S(2)}) copy-start(bf16[512,4096]{1,0:T(8,128)(2,1)} %get-tuple-element.10) | copy-start | bytes 12582916
  627.1 40.0 %copy-start.2 = (bf16[512,4096]{1,0:T(8,128)(2,1)S(1)}, bf16[512,4096]{1,0:T(8,128)(2,1)}, u32[]{:S(2)}) copy-start(bf16[512,4096]{1,0:T(8,128)(2,1)} %get-tuple-element.7) | copy-start | bytes 12582916
  631.3 37.0 %copy-start.19 = (bf16[512,4096]{1,0:T(8,128)(2,1)S(1)}, bf16[512,4096]{1,0:T(8,128)(2,1)}, u32[]{:S(2)}) copy-start(bf16[512,4096]{1,0:T(8,128)(2,1)} %copy-done.16) | copy-start | bytes 12582916
  669.6 2.1 copy-start.14
  670.3 41.1 %copy-start.15 = (s32[16,2]{0,1:T(2,128)S(1)}, s32[16,2]{0,1:T(2,128)}, u32[]{:S(2)}) copy-start(s32[16,2]{0,1:T(2,128)} %param.11) | copy-start | bytes 388
  671.6 85.8 %all-gather.3.cloned.1.call-start = ((), (), s32[]{:S(2)}) async-start(), calls=%async_computation.9 | async-start | bytes 2621440 | tf_op jit(solution)/shard_map/all_gather | solution.py:87
  711.4 104.0 %reduce-scatter.14.cloned.1.call-start = ((), (), s32[]{:S(2)}) async-start(), calls=%async_computation.10 | async-start | bytes 2506752 | tf_op jit(solution)/shard_map/reduce_scatter | solution.py:95
Sparse Core Ops, SparseCore 0:
  468.4 37.4 reduce-scatter.5
  509.1 35.9 reduce-scatter.7
  548.3 35.9 reduce-scatter.9
  671.7 37.0 reduce-scatter.11
  711.5 45.9 all-gather.2
  774.7 40.5 reduce-scatter.13

commit v2 on v0

v2 whole, which is shorter than its diff:
```python
import functools

import jax
import jax.numpy as jnp
import numpy as np
from jax import lax
from jax.experimental import pallas as pl
from jax.experimental.pallas import tpu as pltpu
from jax.sharding import Mesh, PartitionSpec as P

P_SIZE = 1024
DEPTH = 4
CORES = 2

NEAR = ((0, 1), (1, 0), (2, 3), (3, 2))
INWARD = ((0, 1), (3, 2))
OUTWARD = ((1, 0), (2, 3))
MIDDLE = ((1, 2), (2, 1))
SOURCE = np.array([[0, 1, 2, 3], [1, 0, 2, 3], [2, 3, 1, 0], [3, 2, 1, 0]], np.int32)
PLACE = np.argsort(SOURCE, axis=1).astype(np.int32)

LENT = (5, 16)


def bounds(total, parts):
    return [total * k // parts for k in range(parts + 1)]


def room(tiles):
    return min(tiles, -(-(tiles // 2 + int(2.6 * tiles**0.5)) // 2) * 2)


def params(**kwargs):
    return pltpu.CompilerParams(**kwargs)


def pack_kernel(blk, row_blocks, columns, slots, info, hist, out, sem):
    base = info[0]

    def one_column(c, used):
        start = pl.multiple_of((base + c) * blk, blk)
        for b in range(row_blocks):
            take = jnp.logical_and(info[1 + c * row_blocks + b] != 0, used < slots)

            @pl.when(take)
            def _():
                pltpu.make_async_copy(
                    hist.at[pl.ds(b * blk, blk), pl.ds(start, blk)], out.at[used], sem
                ).start()

            used = used + take.astype(jnp.int32)
        return used

    used = lax.fori_loop(0, columns, one_column, jnp.int32(0))

    def one_wait(_, carry):
        pltpu.make_async_copy(hist.at[pl.ds(0, blk), pl.ds(0, blk)], out.at[0], sem).wait()
        return carry

    lax.fori_loop(0, used, one_wait, 0)


def pack(hist, mask, base, slots):
    row_blocks, columns = mask.shape
    blk = hist.shape[0] // row_blocks
    info = jnp.concatenate([jnp.reshape(base, (1,)).astype(jnp.int32), mask.T.reshape(-1)])
    return pl.pallas_call(
        functools.partial(pack_kernel, blk, row_blocks, columns, slots),
        out_shape=jax.ShapeDtypeStruct((slots, blk, blk), hist.dtype),
        in_specs=[pl.BlockSpec(memory_space=pltpu.SMEM), pl.BlockSpec(memory_space=pl.ANY)],
        out_specs=pl.BlockSpec(memory_space=pl.ANY),
        scratch_shapes=[pltpu.SemaphoreType.DMA],
        cost_estimate=pl.CostEstimate(flops=0, bytes_accessed=2 * slots * blk * blk * 2, transcendentals=0),
        name="pack_tiles",
    )(info, hist)


def spread_kernel(blk, row_blocks, parts, slots, info, source, *refs):
    outs, (zeros, sem) = refs[: len(parts)], refs[len(parts) :]
    zeros[...] = jnp.zeros_like(zeros)
    base = info[0]
    used = jnp.int32(0)
    first = 0
    for out, columns in zip(outs, parts):

        def one_column(c, used, out=out, first=first):
            start = pl.multiple_of((base + first + c) * blk, blk)
            place = pl.multiple_of(c * blk, blk)
            for b in range(row_blocks):
                there = info[1 + (first + c) * row_blocks + b] != 0
                if slots is not None:
                    there = jnp.logical_and(there, used < slots)
                target = out.at[pl.ds(b * blk, blk), pl.ds(place, blk)]

                @pl.when(there)
                def _():
                    if slots is None:
                        tile = source.at[pl.ds(b * blk, blk), pl.ds(start, blk)]
                    else:
                        tile = source.at[used]
                    pltpu.make_async_copy(tile, target, sem).start()

                @pl.when(jnp.logical_not(there))
                def _():
                    pltpu.make_async_copy(zeros, target, sem).start()

                used = used + there.astype(jnp.int32)
            return used

        used = lax.fori_loop(0, columns, one_column, used)
        first += columns
    for out in outs:
        pltpu.make_async_copy(out, out, sem).wait()


def spread(source, mask, base, parts):
    row_blocks = mask.shape[0]
    packed = base is None
    blk = source.shape[1] if packed else source.shape[0] // row_blocks
    base = 0 if packed else base
    info = jnp.concatenate([jnp.reshape(base, (1,)).astype(jnp.int32), mask.T.reshape(-1)])
    shapes = [jax.ShapeDtypeStruct((row_blocks * blk, columns * blk), source.dtype) for columns in parts]
    return pl.pallas_call(
        functools.partial(spread_kernel, blk, row_blocks, parts, source.shape[0] if packed else None),
        out_shape=shapes,
        in_specs=[pl.BlockSpec(memory_space=pltpu.SMEM), pl.BlockSpec(memory_space=pl.ANY)],
        out_specs=[pl.BlockSpec(memory_space=pl.ANY)] * len(parts),
        scratch_shapes=[pltpu.VMEM((blk, blk), source.dtype), pltpu.SemaphoreType.DMA],
        cost_estimate=pl.CostEstimate(
            flops=0, bytes_accessed=4 * sum(parts) * row_blocks * blk * blk, transcendentals=0
        ),
        name="spread_tiles",
    )(info, source)


def dots_kernel(blk, count, ids, blocks, out):
    rest = jnp.zeros((out.shape[1] - blk - 2, blk), jnp.float32)

    def one(k, carry):
        def side(which):
            start = pl.multiple_of(ids[which, 1, k] * blk, blk)
            return blocks[ids[which, 0, k], :, pl.ds(start, blk)]

        left, right = side(0), side(1)
        out[k, :blk, :] = lax.dot_general(
            left, right, (((0,), (0,)), ((), ())),
            precision=lax.Precision.HIGHEST, preferred_element_type=jnp.float32,
        )
        out[k, blk:, :] = jnp.concatenate(
            [jnp.sum(left * left, axis=0, keepdims=True), jnp.sum(right * right, axis=0, keepdims=True), rest]
        )
        return carry

    lax.fori_loop(0, count, one, 0)


def pair_dots(blocks, ids, blk):
    count = ids.shape[2]
    return pl.pallas_call(
        functools.partial(dots_kernel, blk, count),
        out_shape=jax.ShapeDtypeStruct((count, blk + 8, blk), jnp.float32),
        in_specs=[pl.BlockSpec(memory_space=pltpu.SMEM), pl.BlockSpec(memory_space=pltpu.VMEM)],
        out_specs=pl.BlockSpec(memory_space=pltpu.VMEM),
        compiler_params=params(vmem_limit_bytes=48 << 20),
        name="pair_dots",
    )(ids, blocks)


def turn(count, k):
    return [(d, (d + k) % count) for d in range(count)]


def scatter_sum(values, axis, dim):
    count = lax.axis_size(axis)
    here = lax.axis_index(axis)
    piece = values.shape[dim] // count

    def part(owner):
        return lax.dynamic_slice_in_dim(values, owner * piece, piece, dim)

    total = part(here)
    for k in range(1, count):
        total = total + lax.ppermute(part((here + k) % count), axis, turn(count, k))
    return total


class Lane:
    def __init__(self, depth):
        self.depth = depth
        self.arrived = []

    def send(self, values, axis, pairs):
        if len(self.arrived) >= self.depth:
            values, _ = lax.optimization_barrier((values, self.arrived[-self.depth]))
        got = lax.ppermute(values, axis, pairs)
        self.arrived.append(got)
        return got


def along_line(block, inner):
    near = lax.ppermute(block, "z", NEAR)
    middle = lax.ppermute(block, "z", MIDDLE)
    far = lax.ppermute(near, "z", MIDDLE)
    out1 = lax.ppermute(middle, "z", OUTWARD)
    out2 = lax.ppermute(far, "z", OUTWARD)
    return [block, near, jnp.where(inner, middle, out1), jnp.where(inner, far, out2)]


def dense(hist, tile_mask, planes, pairs):
    sess, act = ("z", "x"), ("y", "core")
    rows, acts = hist.shape
    row_blocks, act_blocks = tile_mask.shape
    blk = rows // row_blocks
    masked = (
        hist.reshape(row_blocks, blk, act_blocks, blk)
        * (tile_mask != 0).astype(jnp.bfloat16)[:, None, :, None]
    ).reshape(rows, acts)
    partial_proj = jnp.dot(
        masked, lax.all_gather(planes, sess, axis=1, tiled=True), preferred_element_type=jnp.float32
    )
    proj = lax.psum_scatter(partial_proj, act, scatter_dimension=1, tiled=True)
    own_count = pairs.shape[0] // lax.axis_size(act)
    place = lax.axis_index(act) * own_count
    sq = lax.psum(jnp.sum(proj * proj, axis=1), act)
    blocks = lax.all_gather(proj, sess, axis=0, tiled=True).reshape(-1, blk, proj.shape[1])
    norms = lax.all_gather(sq, sess, axis=0, tiled=True).reshape(-1, blk)
    dots = jnp.einsum(
        "kuc,kvc->kuv", blocks[pairs[:, 0]], blocks[pairs[:, 1]], precision=lax.Precision.HIGHEST
    )
    dots = lax.psum_scatter(dots, act, scatter_dimension=0, tiled=True)
    own = lax.dynamic_slice_in_dim(pairs, place, own_count, 0)
    scale = lax.rsqrt(norms[own] / P_SIZE + 1e-06)
    return dots / P_SIZE * scale[:, 0, :, None] * scale[:, 1, None, :]


def body(hist, tile_mask, planes, pairs):
    rows, acts = hist.shape
    row_blocks, act_blocks = tile_mask.shape
    blk = rows // row_blocks
    own_planes = planes.shape[1]
    wide = lax.axis_size("x")
    x, z = lax.axis_index("x"), lax.axis_index("z")
    inner = jnp.logical_or(z == 1, z == 2)
    columns = act_blocks // wide
    tile_mask = (tile_mask != 0).astype(jnp.int32)

    lent = columns * LENT[0] // LENT[1]
    kept = columns - lent
    cuts = bounds(kept, 4) + [kept + c for c in bounds(lent, 2)[1:]]
    widths = [b - a for a, b in zip(cuts[:-1], cuts[1:])]
    streams = {"lent": (4, 6), "early": (0, 2), "late": (2, 4)}

    def mask_of(owner):
        return lax.dynamic_slice_in_dim(tile_mask, owner * columns, columns, 1)

    def over_x(make):
        return [lax.ppermute(make((x + k) % wide), "x", turn(wide, k)) for k in range(1, wide)]

    masks = [mask_of(x)] + [lax.ppermute(mask_of((x + k) % wide), "x", turn(wide, k)) for k in range(1, wide)]
    guest_masks = lax.ppermute(jnp.stack([m[:, kept:] for m in masks]), "z", INWARD)

    over_x, ends, middle, ends_out = Lane(2), Lane(1), Lane(2), Lane(2)

    def planes_of(owner, c):
        return lax.dynamic_slice_in_dim(planes, (owner * columns + cuts[c]) * blk, widths[c] * blk, 0)

    def group(c):
        whole = jnp.zeros((widths[c] * blk, wide * own_planes), planes.dtype)
        whole = lax.dynamic_update_slice_in_dim(whole, planes_of(x, c), x * own_planes, 1)
        for k in range(1, wide):
            part = over_x.send(planes_of((x + k) % wide, c), "x", turn(wide, k))
            whole = lax.dynamic_update_slice_in_dim(whole, part, ((x - k) % wide) * own_planes, 1)
        return whole

    def tiles_of(name):
        low, high = (cuts[c] for c in streams[name])
        slots = room((high - low) * row_blocks)
        got = []
        for k in range(1, wide):
            owner = (x + k) % wide
            tiles = pack(hist, mask_of(owner)[:, low:high], owner * columns + low, slots)
            got.append(over_x.send(tiles, "x", turn(wide, k)))
        return got

    groups = [group(c) for c in range(4)]
    tiles = {"lent": tiles_of("lent")}
    groups += [group(c) for c in (4, 5)]
    tiles["early"] = tiles_of("early")
    tiles["late"] = tiles_of("late")

    over = jnp.int32(0)
    sessions = [[None] * 6 for _ in range(wide)]
    for name, (first, last) in streams.items():
        low, high = cuts[first], cuts[last]
        for owner in range(wide):
            count = jnp.sum(tile_mask[:, owner * columns + low : owner * columns + high])
            over = jnp.maximum(over, (count > room((high - low) * row_blocks)).astype(jnp.int32))
        parts = tuple(widths[first:last])
        for k in range(wide):
            mask = masks[k][:, low:high]
            if k == 0:
                sessions[k][first:last] = spread(hist, mask, x * columns + low, parts)
            else:
                sessions[k][first:last] = spread(tiles[name][k - 1], mask, None, parts)

    near, mid, far = {}, {}, {}
    for c in range(4):
        near[c] = ends.send(groups[c], "z", NEAR)
    own_tiles = pack(hist, masks[0][:, kept:], x * columns + kept, room(lent * row_blocks))
    lent_tiles = [ends.send(own_tiles, "z", INWARD)]
    for c in (4, 5):
        near[c] = ends.send(groups[c], "z", INWARD)
    for c in range(6):
        mid[c] = middle.send(groups[c], "z", MIDDLE)
    for c in range(6):
        far[c] = middle.send(near[c], "z", MIDDLE)
    held = [None] * 6
    out1 = [ends_out.send(mid[c], "z", OUTWARD) for c in range(4)]
    lent_tiles += [ends.send(t, "z", INWARD) for t in tiles["lent"]]
    out2 = [ends_out.send(far[c], "z", OUTWARD) for c in range(4)]
    for c in range(6):
        if c < 4:
            held[c] = [groups[c], near[c], jnp.where(inner, mid[c], out1[c]), jnp.where(inner, far[c], out2[c])]
        else:
            held[c] = [groups[c], near[c], mid[c], far[c]]
    guests = [
        spread(t, guest_masks[k], None, tuple(widths[4:])) for k, t in enumerate(lent_tiles)
    ]

    order = (x - jnp.arange(wide)) % wide

    def summed(terms):
        totals = []
        for source in terms:
            total = None
            for a, b in source:
                one = jnp.dot(a, b, preferred_element_type=jnp.float32)
                total = one if total is None else total + one
            totals.append(total)
        whole = jnp.stack(totals)[order].reshape(wide * rows, wide * own_planes).T
        for axis in ("core", "x", "y"):
            whole = scatter_sum(whole, axis, 0)
        return whole

    shares = []
    for s in range(DEPTH):
        share = summed([[(sessions[k][c], held[c][s]) for c in range(6)] for k in range(wide)])
        if s > 0:
            t = 0 if s == 1 else s
            guest = summed([[(guests[k][c - 4], held[c][t]) for c in (4, 5)] for k in range(wide)])
            share = share + lax.ppermute(guest, "z", OUTWARD)
        shares.append(share)
    proj = jnp.stack(shares)[jnp.asarray(PLACE)[z]].reshape(-1, wide * rows)

    blocks = jnp.stack(along_line(proj, inner))
    got = [pairs] + [lax.ppermute(pairs, "x", turn(wide, k)) for k in range(1, wide)]
    all_pairs = jnp.stack(got)[order].reshape(-1, 2).T
    plane_blocks = wide * row_blocks
    ids = jnp.stack([jnp.asarray(PLACE)[z][all_pairs // plane_blocks], all_pairs % plane_blocks], axis=1)
    sums = pair_dots(blocks, ids, blk)
    high, cores = lax.axis_size("y"), lax.axis_size("core")
    sums = sums.reshape((wide, high, cores, -1) + sums.shape[1:])
    for axis, dim in (("core", 2), ("x", 0), ("y", 1)):
        sums = scatter_sum(sums, axis, dim)
    own = sums.reshape((-1,) + sums.shape[4:])
    scale = lax.rsqrt(own[:, blk : blk + 2] / P_SIZE + 1e-06)
    scores = own[:, :blk] / P_SIZE * scale[:, 0, :, None] * scale[:, 1, None, :]

    over = lax.pmax(over, ("z", "x", "y", "core"))
    return lax.cond(over > 0, lambda: dense(hist, tile_mask, planes, pairs), lambda: scores)


def solution(mesh):
    sess, act = mesh.shape["sess"], mesh.shape["act"]
    fine = Mesh(
        mesh.devices.reshape(DEPTH, sess // DEPTH, act // CORES, CORES), ("z", "x", "y", "core")
    )
    sess_axes, act_axes = ("z", "x"), ("y", "core")
    placed = (
        P(sess_axes, act_axes), P(sess_axes, act_axes), P(act_axes, sess_axes), P(sess_axes, None)
    )
    return jax.shard_map(
        body, mesh=fine, in_specs=placed, out_specs=P(sess_axes + act_axes, None, None), check_vma=False
    )
```

time: 1500 us -> 1820 us (1.21)
  waiting for transfers between devices: 1380 us -> 318 us
  Pallas kernels: 0 us -> 899 us
  starting transfers between devices: 0.12 us -> 265 us
  matrix products: 55.4 us -> 152 us
  local copies, waits for them, and re-layouts: 19.6 us -> 91.4 us
  other arithmetic: 1.99 us -> 30.3 us
    all_gather x2 -> x0, waiting for transfers between devices: 1350 us -> none  [the longest x1 1270 us: body(): lax.all_gather(planes, 'sess', axis=1, tiled=True)]
    pallas_call x0 -> x13, Pallas kernels: none -> 899 us  [the longest x8 532 us: spread(): pl.pallas_call(functools.partial(spread_kernel, blk, row_blocks, parts, s...]
    ppermute x0 -> x72, waiting for transfers between devices: none -> 318 us  [the longest x37 144 us: send(): got = lax.ppermute(values, axis, pairs)]
    ppermute x0 -> x72, starting transfers between devices: none -> 265 us  [the longest x37 179 us: send(): got = lax.ppermute(values, axis, pairs)]
    dot_general x2 -> x60, matrix products: 55.4 us -> 152 us  [summed(): one = jnp.dot(a, b, preferred_element_type=jnp.float32)]
    pmax x0 -> x1, blocking collectives: none -> 37.4 us  [body(): over = lax.pmax(over, ('z', 'x', 'y', 'core'))]
    reduce_scatter x2 -> x0, waiting for transfers between devices: 31.6 us -> none  [the longest x1 31.6 us: body(): lax.psum_scatter(partial_proj, 'act', scatter_dimension=1, tiled=True)]
    all_gather x1 -> x0, blocking collectives: 26 us -> none  [body(): lax.all_gather(local_sq, 'sess', axis=0, tiled=True)]
  transfers between devices with their start and end apart: 4 -> 72, of which waited for: 3 -> 27; matrix products, arithmetic and copies ran while one was open for 0% -> 14% of each run, Pallas kernels for 0% -> 49%
where the time goes in v2:
time: 1820 us; the launch traced here: 1810 us
  Pallas kernels  899 us (49%)
  waiting for transfers between devices  318 us (17%)
  starting transfers between devices  265 us (15%)
  matrix products  152 us (8%)
  local copies, waits for them, and re-layouts  91.4 us (5%)
  blocking collectives  37.4 us (2%)
  other arithmetic  30.3 us (2%)
  between operations  20.2 us (1%)
    pallas_call x8, Pallas kernels, spread(): pl.pallas_call(functools.partial(spread_kernel, blk, row_blocks, parts, s...  532 us
    pallas_call x4, Pallas kernels, pack(): pl.pallas_call(functools.partial(pack_kernel, blk, row_blocks, columns, s...  359 us
    ppermute x37, starting transfers between devices, send(): got = lax.ppermute(values, axis, pairs)  179 us
    dot_general x60, matrix products, summed(): one = jnp.dot(a, b, preferred_element_type=jnp.float32)  152 us
    ppermute x37, waiting for transfers between devices, send(): got = lax.ppermute(values, axis, pairs)  144 us
    ppermute x3, waiting for transfers between devices, body(): share = share + lax.ppermute(guest, 'z', OUTWARD)  92.5 us
    ppermute x24, starting transfers between devices, scatter_sum(): total = total + lax.ppermute(part((here + k) % count), axis, turn(count, k))  70.2 us
    ppermute x24, waiting for transfers between devices, scatter_sum(): total = total + lax.ppermute(part((here + k) % count), axis, turn(count, k))  49.6 us
  transfers between devices with their start and end apart: 72, of which 27 were waited for; matrix products, arithmetic and copies ran while one was open for 14% of the time, Pallas kernels for 49%

profile of v2, /device:TPU:0, one launch (start us, length us, event | category | flops | bytes accessed | tf_op | source)
XLA Modules:
  0.0 1813.0 jit_solution(2309062622070873422)
XLA Ops:
  10.3 3.5 dynamic-slice_dynamic-update-slice_fusion.3
  41.1 93.1 %pack_tiles.7 = bf16[112,128,128]{2,1,0:T(8,128)(2,1)} custom-call(s32[161]{0:T(256)} %pad_add_fusion.10.info, bf16[512,32768]{1,0:T(8,128)(2,1)} %hist.7), custom_call_target="tpu_custom_call" | custom-call | bytes 7340032 | tf_op jit(solution)/shard_map/pack_tiles/pallas_call | solution.py:67
  134.3 93.1 %spread_tiles.10 = (bf16[512,2560]{1,0:T(8,128)(2,1)}, bf16[512,2560]{1,0:T(8,128)(2,1)}) custom-call(s32[161]{0:T(256)} %pad_add_fusion.10.info, bf16[512,32768]{1,0:T(8,128)(2,1)} %hist.7), custom_call_target="tpu_custom_call" | custom-call | bytes 10485760 | tf_op jit(solution)/shard_map/spread_tiles/pallas_call | solution.py:123
  227.4 82.2 %pack_tiles.4 = bf16[112,128,128]{2,1,0:T(8,128)(2,1)} custom-call(s32[161]{0:T(256)} %pad_add_fusion.11.info, bf16[512,32768]{1,0:T(8,128)(2,1)} %hist.7), custom_call_target="tpu_custom_call" | custom-call | bytes 7340032 | tf_op jit(solution)/shard_map/pack_tiles/pallas_call | solution.py:67
  309.6 95.1 %pack_tiles.6 = bf16[122,128,128]{2,1,0:T(8,128)(2,1)} custom-call(s32[177]{0:T(256)} %pad_add_fusion.13.info, bf16[512,32768]{1,0:T(8,128)(2,1)} %hist.7), custom_call_target="tpu_custom_call" | custom-call | bytes 7995392 | tf_op jit(solution)/shard_map/pack_tiles/pallas_call | solution.py:67
  404.8 88.2 %pack_tiles.5 = bf16[122,128,128]{2,1,0:T(8,128)(2,1)} custom-call(s32[177]{0:T(256)} %pad_add_fusion.12.info, bf16[512,32768]{1,0:T(8,128)(2,1)} %hist.7), custom_call_target="tpu_custom_call" | custom-call | bytes 7995392 | tf_op jit(solution)/shard_map/pack_tiles/pallas_call | solution.py:67
  492.9 82.2 %spread_tiles.9 = (bf16[512,2816]{1,0:T(8,128)(2,1)}, bf16[512,2816]{1,0:T(8,128)(2,1)}) custom-call(s32[177]{0:T(256)} %pad_add_fusion.9.info, bf16[512,32768]{1,0:T(8,128)(2,1)} %hist.7), custom_call_target="tpu_custom_call" | custom-call | bytes 11534336 | tf_op jit(solution)/shard_map/spread_tiles/pallas_call | solution.py:123
  575.2 90.2 %spread_tiles.8 = (bf16[512,2816]{1,0:T(8,128)(2,1)}, bf16[512,2816]{1,0:T(8,128)(2,1)}) custom-call(s32[177]{0:T(256)} %pad_add_fusion.8.info, bf16[512,32768]{1,0:T(8,128)(2,1)} %hist.7), custom_call_target="tpu_custom_call" | custom-call | bytes 11534336 | tf_op jit(solution)/shard_map/spread_tiles/pallas_call | solution.py:123
  674.8 9.7 collective-permute-done.3
  684.5 4.1 collective-permute-start.24
  708.0 9.1 collective-permute-done.5
  718.4 4.1 fusion.71
  725.0 9.8 collective-permute-done.15
  735.6 3.3 fusion.73
  738.9 3.2 fusion.72
  742.1 29.1 %collective-permute-start.16 = (bf16[2816,256]{1,0:T(8,128)(2,1)}, bf16[2816,256]{1,0:T(8,128)(2,1)}, u32[]{:S(2)}, u32[]{:S(2)}) collective-permute-start(bf16[2816,256]{1,0:T(8,128)(2,1)} %constant_dynamic-update-slice_fusion.3), channel_id=1, source_target_pairs={{0,8},{8,0},{16,24},{24,16},{1,9},{9,1},{17,25},{25,17},{2,10},{10... | collective-permute-start | bytes 4325384 | tf_op jit(solution)/shard_map/ppermute | solution.py:195
  771.2 3.1 fusion.74
  774.3 22.3 %collective-permute-done.31 = bf16[2816,256]{1,0:T(8,128)(2,1)S(1)} collective-permute-done((bf16[2816,256]{1,0:T(8,128)(2,1)S(1)}, bf16[2816,256]{1,0:T(8,128)(2,1)S(1)}, u32[]{:S(2)}, u32[]{:S(2)}) %collective-permute-start.31) | collective-permute-done | bytes 1441824 | tf_op jit(solution)/shard_map/ppermute | solution.py:195
  806.8 20.8 %collective-permute-done.16 = bf16[2816,256]{1,0:T(8,128)(2,1)} collective-permute-done((bf16[2816,256]{1,0:T(8,128)(2,1)}, bf16[2816,256]{1,0:T(8,128)(2,1)}, u32[]{:S(2)}, u32[]{:S(2)}) %collective-permute-start.16) | collective-permute-done | bytes 1441824 | tf_op jit(solution)/shard_map/ppermute | solution.py:195
  829.5 3.1 fusion.82
  832.6 25.7 %collective-permute-done.37 = bf16[2816,256]{1,0:T(8,128)(2,1)S(1)} collective-permute-done((bf16[2816,256]{1,0:T(8,128)(2,1)S(1)}, bf16[2816,256]{1,0:T(8,128)(2,1)S(1)}, u32[]{:S(2)}, u32[]{:S(2)}) %collective-permute-start.37) | collective-permute-done | bytes 1441824 | tf_op jit(solution)/shard_map/ppermute | solution.py:195
  860.1 29.2 %collective-permute-done.35 = bf16[2816,256]{1,0:T(8,128)(2,1)S(1)} collective-permute-done((bf16[2816,256]{1,0:T(8,128)(2,1)}, bf16[2816,256]{1,0:T(8,128)(2,1)S(1)}, u32[]{:S(2)}, u32[]{:S(2)}) %collective-permute-start.35) | collective-permute-done | bytes 1441824 | tf_op jit(solution)/shard_map/ppermute | solution.py:195
  893.0 86.2 %spread_tiles.13 = (bf16[512,2560]{1,0:T(8,128)(2,1)}, bf16[512,2560]{1,0:T(8,128)(2,1)}) custom-call(s32[161]{0:T(256)} %pad_add_fusion.5.info, bf16[112,128,128]{2,1,0:T(8,128)(2,1)} %collective-permute-done.6.source), custom_call_target="tpu_custom_call" | custom-call | bytes 10485760 | tf_op jit(solution)/shard_map/spread_tiles/pallas_call | solution.py:123
  979.3 3.9 fusion.79
  997.4 86.2 %spread_tiles.11 = (bf16[512,2816]{1,0:T(8,128)(2,1)}, bf16[512,2816]{1,0:T(8,128)(2,1)}) custom-call(s32[177]{0:T(256)} %pad_add_fusion.7.info, bf16[122,128,128]{2,1,0:T(8,128)(2,1)} %collective-permute-done.9.source), custom_call_target="tpu_custom_call" | custom-call | bytes 11534336 | tf_op jit(solution)/shard_map/spread_tiles/pallas_call | solution.py:123
  1083.6 4.1 fusion.76
  1087.7 3.2 fusion.86
  1092.6 24.2 %collective-permute-start.18 = (bf16[112,128,128]{2,1,0:T(8,128)(2,1)}, bf16[112,128,128]{2,1,0:T(8,128)(2,1)}, u32[]{:S(2)}, u32[]{:S(2)}) collective-permute-start(bf16[112,128,128]{2,1,0:T(8,128)(2,1)} %pack_tiles.7), channel_id=1, source_target_pairs={{0,8},{24,16},{1,9},{25,17},{2,10},{26,18},{3,11},{27,19},{4,12},{... | collective-permute-start | bytes 11010056 | tf_op jit(solution)/shard_map/ppermute | solution.py:195
  1123.0 3.1 fusion.96
  1134.0 14.9 collective-permute-done.52
  1150.7 87.2 %spread_tiles.12 = (bf16[512,2816]{1,0:T(8,128)(2,1)}, bf16[512,2816]{1,0:T(8,128)(2,1)}) custom-call(s32[177]{0:T(256)} %pad_add_fusion.6.info, bf16[122,128,128]{2,1,0:T(8,128)(2,1)} %collective-permute-done.10.source), custom_call_target="tpu_custom_call" | custom-call | bytes 11534336 | tf_op jit(solution)/shard_map/spread_tiles/pallas_call | solution.py:123
  1237.9 3.3 fusion.57
  1253.9 3.3 fusion.78
  1273.5 4.1 fusion.88
  1277.6 3.2 fusion.87
  1284.1 3.1 fusion.59
  1287.3 3.1 fusion.60
  1290.4 6.8 collective-permute-start.19
  1297.2 3.2 spread_tiles.14
  1300.4 3.1 fusion.91
  1303.6 3.1 fusion.12
  1311.8 23.7 %collective-permute-start.12 = (f32[64,1024]{1,0:T(8,128)S(1)}, f32[64,1024]{1,0:T(8,128)S(1)}, u32[]{:S(2)}, u32[]{:S(2)}) collective-permute-start(f32[64,1024]{1,0:T(8,128)S(1)} %constant_dynamic-slice_fusion.28), channel_id=1, source_target_pairs={{0,4},{4,0},{1,5},{5,1},{2,6},{6,2},{3,7},{7,3},{8,12},{12,8},{9,1... | collective-permute-start | bytes 786440 | tf_op jit(solution)/shard_map/ppermute | solution.py:183
  1336.8 5.9 collective-permute-done.12
  1342.8 4.6 collective-permute-done.41
  1348.9 73.8 %collective-permute-start.20 = (bf16[2560,256]{1,0:T(8,128)(2,1)}, bf16[2560,256]{1,0:T(8,128)(2,1)}, u32[]{:S(2)}, u32[]{:S(2)}) collective-permute-start(bf16[2560,256]{1,0:T(8,128)(2,1)} %constant_dynamic-update-slice_fusion), channel_id=1, source_target_pairs={{0,8},{24,16},{1,9},{25,17},{2,10},{26,18},{3,11},{27,19},{4,12},{... | collective-permute-start | bytes 3932168 | tf_op jit(solution)/shard_map/ppermute | solution.py:195
  1422.7 3.1 fusion.63
  1425.8 3.3 fusion.64
  1437.2 6.3 collective-permute-start.25
  1462.9 21.7 %collective-permute-start.21 = (f32[128,1024]{1,0:T(8,128)}, f32[128,1024]{1,0:T(8,128)}, u32[]{:S(2)}, u32[]{:S(2)}) collective-permute-start(f32[128,1024]{1,0:T(8,128)} %bitcast.296), channel_id=1, source_target_pairs={{0,1},{1,0},{2,3},{3,2},{4,5},{5,4},{6,7},{7,6},{8,9},{9,8},{10,11... | collective-permute-start | bytes 1572872 | tf_op jit(solution)/shard_map/ppermute | solution.py:183
  1514.8 5.8 collective-permute-done.58
  1521.8 3.5 spread_tiles.15
  1525.3 3.9 fusion.92
  1540.6 8.1 collective-permute-start.60
  1569.6 5.8 collective-permute-done.61
  1577.5 3.5 collective-permute-done.44
  1582.7 3.4 collective-permute-done.27
  1588.3 4.2 collective-permute-done.45
  1596.6 90.6 %collective-permute-done.63 = f32[32,1024]{1,0:T(8,128)S(1)} collective-permute-done((f32[32,1024]{1,0:T(8,128)S(1)}, f32[32,1024]{1,0:T(8,128)S(1)}, u32[]{:S(2)}, u32[]{:S(2)}) %collective-permute-start.63) | collective-permute-done | bytes 131104 | tf_op jit(solution)/shard_map/ppermute | solution.py:351
  1693.5 11.4 collective-permute-done.64
  1712.2 7.3 collective-permute-done.66
  1719.5 11.5 collective-permute-done.68
  1731.3 9.0 pair_dots.1
  1746.2 13.3 collective-permute-done.70
  1766.7 37.4 %pmax.7 = s32[]{:T(128)} all-reduce(s32[]{:T(128)S(6)} %max.25), channel_id=1, replica_groups=mesh['z'=4,'x'=2,'y'=2,'core'=2] {'z','x','y','core'}, use_global_device_ids=true, to_apply=%region_6.7 | all-reduce | flops 1 | bytes 8 | tf_op jit(solution)/shard_map/pmax | solution.py:369
  (517 shorter events, 278.5 us)
Async XLA Ops:
  7.2 658.3 %collective-permute-start.8 = (s32[4,128]{1,0:T(4,128)S(1)}, s32[4,128]{1,0:T(4,128)S(1)}, u32[]{:S(2)}, u32[]{:S(2)}) collective-permute-start(s32[4,128]{1,0:T(4,128)S(1)} %get-tuple-element.207), channel_id=1, source_target_pairs={{0,4},{4,0},{1,5},{5,1},{2,6},{6,2},{3,7},{7,3},{8,12},{12,8},{9,1... | collective-permute-start | bytes 6152 | tf_op jit(solution)/shard_map/ppermute | solution.py:259
  13.7 24.1 %collective-permute-start.1 = (bf16[2816,128]{1,0:T(8,128)(2,1)S(1)}, bf16[2816,128]{1,0:T(8,128)(2,1)S(1)}, u32[]{:S(2)}, u32[]{:S(2)}) collective-permute-start(bf16[2816,128]{1,0:T(8,128)(2,1)S(1)} %get-tuple-element.186), channel_id=1, source_target_pairs={{0,4},{4,0},{1,5},{5,1},{2,6},{6,2},{3,7},{7,3},{8,12},{12,8},{9,1... | collective-permute-start | bytes 2162696 | tf_op jit(solution)/shard_map/ppermute | solution.py:195
  14.3 652.5 %collective-permute-start.2 = (bf16[2816,128]{1,0:T(8,128)(2,1)}, bf16[2816,128]{1,0:T(8,128)(2,1)}, u32[]{:S(2)}, u32[]{:S(2)}) collective-permute-start(bf16[2816,128]{1,0:T(8,128)(2,1)} %get-tuple-element.185), channel_id=1, source_target_pairs={{0,4},{4,0},{1,5},{5,1},{2,6},{6,2},{3,7},{7,3},{8,12},{12,8},{9,1... | collective-permute-start | bytes 2162696 | tf_op jit(solution)/shard_map/ppermute | solution.py:195
  38.0 652.7 %collective-permute-start.30 = (bf16[2816,256]{1,0:T(8,128)(2,1)S(1)}, bf16[2816,256]{1,0:T(8,128)(2,1)S(1)}, u32[]{:S(2)}, u32[]{:S(2)}) collective-permute-start(bf16[2816,256]{1,0:T(8,128)(2,1)S(1)} %constant_dynamic-update-slice_fusion.5), channel_id=1, source_target_pairs={{8,16},{16,8},{9,17},{17,9},{10,18},{18,10},{11,19},{19,11},{12,20... | collective-permute-start | bytes 4325384 | tf_op jit(solution)/shard_map/ppermute | solution.py:195
  665.4 34.6 %collective-permute-start.14 = (bf16[2816,256]{1,0:T(8,128)(2,1)S(1)}, bf16[2816,256]{1,0:T(8,128)(2,1)}, u32[]{:S(2)}, u32[]{:S(2)}) collective-permute-start(bf16[2816,256]{1,0:T(8,128)(2,1)S(1)} %constant_dynamic-update-slice_fusion.5), channel_id=1, source_target_pairs={{0,8},{8,0},{16,24},{24,16},{1,9},{9,1},{17,25},{25,17},{2,10},{10... | collective-permute-start | bytes 4325384 | tf_op jit(solution)/shard_map/ppermute | solution.py:195
  665.4 19.1 %collective-permute-start.3 = (bf16[2816,128]{1,0:T(8,128)(2,1)}, bf16[2816,128]{1,0:T(8,128)(2,1)}, u32[]{:S(2)}, u32[]{:S(2)}) collective-permute-start(bf16[2816,128]{1,0:T(8,128)(2,1)} %get-tuple-element.112), channel_id=1, source_target_pairs={{0,4},{4,0},{1,5},{5,1},{2,6},{6,2},{3,7},{7,3},{8,12},{12,8},{9,1... | collective-permute-start | bytes 2162696 | tf_op jit(solution)/shard_map/ppermute | solution.py:195
  666.8 33.1 %collective-permute-start.4 = (bf16[2816,128]{1,0:T(8,128)(2,1)}, bf16[2816,128]{1,0:T(8,128)(2,1)}, u32[]{:S(2)}, u32[]{:S(2)}) collective-permute-start(bf16[2816,128]{1,0:T(8,128)(2,1)} %get-tuple-element.114), channel_id=1, source_target_pairs={{0,4},{4,0},{1,5},{5,1},{2,6},{6,2},{3,7},{7,3},{8,12},{12,8},{9,1... | collective-permute-start | bytes 2162696 | tf_op jit(solution)/shard_map/ppermute | solution.py:195
  670.9 34.4 %collective-permute-start.32 = (bf16[2816,256]{1,0:T(8,128)(2,1)}, bf16[2816,256]{1,0:T(8,128)(2,1)}, u32[]{:S(2)}, u32[]{:S(2)}) collective-permute-start(bf16[2816,256]{1,0:T(8,128)(2,1)} %constant_dynamic-update-slice_fusion.4), channel_id=1, source_target_pairs={{8,16},{16,8},{9,17},{17,9},{10,18},{18,10},{11,19},{19,11},{12,20... | collective-permute-start | bytes 4325384 | tf_op jit(solution)/shard_map/ppermute | solution.py:195
  684.5 17.7 collective-permute-start.24
  690.7 31.8 %collective-permute-start.34 = (bf16[2816,256]{1,0:T(8,128)(2,1)}, bf16[2816,256]{1,0:T(8,128)(2,1)}, u32[]{:S(2)}, u32[]{:S(2)}) collective-permute-start(bf16[2816,256]{1,0:T(8,128)(2,1)} %constant_dynamic-update-slice_fusion.3), channel_id=1, source_target_pairs={{8,16},{16,8},{9,17},{17,9},{10,18},{18,10},{11,19},{19,11},{12,20... | collective-permute-start | bytes 4325384 | tf_op jit(solution)/shard_map/ppermute | solution.py:195
  699.9 17.1 collective-permute-start.5
  699.9 34.9 %collective-permute-start.15 = (bf16[2816,256]{1,0:T(8,128)(2,1)}, bf16[2816,256]{1,0:T(8,128)(2,1)}, u32[]{:S(2)}, u32[]{:S(2)}) collective-permute-start(bf16[2816,256]{1,0:T(8,128)(2,1)} %constant_dynamic-update-slice_fusion.4), channel_id=1, source_target_pairs={{0,8},{8,0},{16,24},{24,16},{1,9},{9,1},{17,25},{25,17},{2,10},{10... | collective-permute-start | bytes 4325384 | tf_op jit(solution)/shard_map/ppermute | solution.py:195
  705.3 36.8 %collective-permute-start.36 = (bf16[2816,256]{1,0:T(8,128)(2,1)}, bf16[2816,256]{1,0:T(8,128)(2,1)S(1)}, u32[]{:S(2)}, u32[]{:S(2)}) collective-permute-start(bf16[2816,256]{1,0:T(8,128)(2,1)} %constant_dynamic-update-slice_fusion.2), channel_id=1, source_target_pairs={{8,16},{16,8},{9,17},{17,9},{10,18},{18,10},{11,19},{19,11},{12,20... | collective-permute-start | bytes 4325384 | tf_op jit(solution)/shard_map/ppermute | solution.py:195
  706.7 67.6 %collective-permute-start.33 = (bf16[2816,256]{1,0:T(8,128)(2,1)}, bf16[2816,256]{1,0:T(8,128)(2,1)S(1)}, u32[]{:S(2)}, u32[]{:S(2)}) collective-permute-start(bf16[2816,256]{1,0:T(8,128)(2,1)} %collective-permute-done.32), channel_id=1, source_target_pairs={{8,0},{16,24},{9,1},{17,25},{10,2},{18,26},{11,3},{19,27},{12,4},{... | collective-permute-start | bytes 4325384 | tf_op jit(solution)/shard_map/ppermute | solution.py:195
  717.0 79.5 %collective-permute-start.31 = (bf16[2816,256]{1,0:T(8,128)(2,1)S(1)}, bf16[2816,256]{1,0:T(8,128)(2,1)S(1)}, u32[]{:S(2)}, u32[]{:S(2)}) collective-permute-start(bf16[2816,256]{1,0:T(8,128)(2,1)S(1)} %collective-permute-done.30), channel_id=1, source_target_pairs={{8,0},{16,24},{9,1},{17,25},{10,2},{18,26},{11,3},{19,27},{12,4},{... | collective-permute-start | bytes 4325384 | tf_op jit(solution)/shard_map/ppermute | solution.py:195
  722.5 168.5 %collective-permute-start.6 = (bf16[112,128,128]{2,1,0:T(8,128)(2,1)S(1)}, bf16[112,128,128]{2,1,0:T(8,128)(2,1)}, u32[]{:S(2)}, u32[]{:S(2)}) collective-permute-start(bf16[112,128,128]{2,1,0:T(8,128)(2,1)S(1)} %copy-done.20), channel_id=1, source_target_pairs={{0,4},{4,0},{1,5},{5,1},{2,6},{6,2},{3,7},{7,3},{8,12},{12,8},{9,1... | collective-permute-start | bytes 11010056 | tf_op jit(solution)/shard_map/ppermute | solution.py:195
  734.9 65.9 %collective-permute-start.38 = (bf16[2560,256]{1,0:T(8,128)(2,1)}, bf16[2560,256]{1,0:T(8,128)(2,1)S(1)}, u32[]{:S(2)}, u32[]{:S(2)}) collective-permute-start(bf16[2560,256]{1,0:T(8,128)(2,1)} %constant_dynamic-update-slice_fusion.1), channel_id=1, source_target_pairs={{8,16},{16,8},{9,17},{17,9},{10,18},{18,10},{11,19},{19,11},{12,20... | collective-permute-start | bytes 3932168 | tf_op jit(solution)/shard_map/ppermute | solution.py:195
  742.1 85.4 %collective-permute-start.16 = (bf16[2816,256]{1,0:T(8,128)(2,1)}, bf16[2816,256]{1,0:T(8,128)(2,1)}, u32[]{:S(2)}, u32[]{:S(2)}) collective-permute-start(bf16[2816,256]{1,0:T(8,128)(2,1)} %constant_dynamic-update-slice_fusion.3), channel_id=1, source_target_pairs={{0,8},{8,0},{16,24},{24,16},{1,9},{9,1},{17,25},{25,17},{2,10},{10... | collective-permute-start | bytes 4325384 | tf_op jit(solution)/shard_map/ppermute | solution.py:195
  774.3 218.8 %collective-permute-start.9 = (bf16[122,128,128]{2,1,0:T(8,128)(2,1)}, bf16[122,128,128]{2,1,0:T(8,128)(2,1)}, u32[]{:S(2)}, u32[]{:S(2)}) collective-permute-start(bf16[122,128,128]{2,1,0:T(8,128)(2,1)} %pack_tiles.5), channel_id=1, source_target_pairs={{0,4},{4,0},{1,5},{5,1},{2,6},{6,2},{3,7},{7,3},{8,12},{12,8},{9,1... | collective-permute-start | bytes 11993096 | tf_op jit(solution)/shard_map/ppermute | solution.py:195
  797.7 60.6 %collective-permute-start.37 = (bf16[2816,256]{1,0:T(8,128)(2,1)S(1)}, bf16[2816,256]{1,0:T(8,128)(2,1)S(1)}, u32[]{:S(2)}, u32[]{:S(2)}) collective-permute-start(bf16[2816,256]{1,0:T(8,128)(2,1)S(1)} %collective-permute-done.36), channel_id=1, source_target_pairs={{8,0},{16,24},{9,1},{17,25},{10,2},{18,26},{11,3},{19,27},{12,4},{... | collective-permute-start | bytes 4325384 | tf_op jit(solution)/shard_map/ppermute | solution.py:195
  800.8 88.5 %collective-permute-start.35 = (bf16[2816,256]{1,0:T(8,128)(2,1)}, bf16[2816,256]{1,0:T(8,128)(2,1)S(1)}, u32[]{:S(2)}, u32[]{:S(2)}) collective-permute-start(bf16[2816,256]{1,0:T(8,128)(2,1)} %collective-permute-done.34), channel_id=1, source_target_pairs={{8,0},{16,24},{9,1},{17,25},{10,2},{18,26},{11,3},{19,27},{12,4},{... | collective-permute-start | bytes 4325384 | tf_op jit(solution)/shard_map/ppermute | solution.py:195
  827.5 163.7 %collective-permute-start.47 = (bf16[2816,256]{1,0:T(8,128)(2,1)}, bf16[2816,256]{1,0:T(8,128)(2,1)}, u32[]{:S(2)}, u32[]{:S(2)}) collective-permute-start(bf16[2816,256]{1,0:T(8,128)(2,1)} %collective-permute-done.14), channel_id=1, source_target_pairs={{8,16},{16,8},{9,17},{17,9},{10,18},{18,10},{11,19},{19,11},{12,20... | collective-permute-start | bytes 4325384 | tf_op jit(solution)/shard_map/ppermute | solution.py:195
  858.3 234.3 %collective-permute-start.17 = (bf16[2816,256]{1,0:T(8,128)(2,1)}, bf16[2816,256]{1,0:T(8,128)(2,1)}, u32[]{:S(2)}, u32[]{:S(2)}) collective-permute-start(bf16[2816,256]{1,0:T(8,128)(2,1)} %constant_dynamic-update-slice_fusion.2), channel_id=1, source_target_pairs={{0,8},{8,0},{16,24},{24,16},{1,9},{9,1},{17,25},{25,17},{2,10},{10... | collective-permute-start | bytes 4325384 | tf_op jit(solution)/shard_map/ppermute | solution.py:195
  891.0 93.9 %collective-permute-start.7 = (bf16[2560,128]{1,0:T(8,128)(2,1)S(1)}, bf16[2560,128]{1,0:T(8,128)(2,1)S(1)}, u32[]{:S(2)}, u32[]{:S(2)}) collective-permute-start(bf16[2560,128]{1,0:T(8,128)(2,1)S(1)} %get-tuple-element.119), channel_id=1, source_target_pairs={{0,4},{4,0},{1,5},{5,1},{2,6},{6,2},{3,7},{7,3},{8,12},{12,8},{9,1... | collective-permute-start | bytes 1966088 | tf_op jit(solution)/shard_map/ppermute | solution.py:195
  985.9 130.9 %collective-permute-start.39 = (bf16[2560,256]{1,0:T(8,128)(2,1)}, bf16[2560,256]{1,0:T(8,128)(2,1)}, u32[]{:S(2)}, u32[]{:S(2)}) collective-permute-start(bf16[2560,256]{1,0:T(8,128)(2,1)} %constant_dynamic-update-slice_fusion), channel_id=1, source_target_pairs={{8,16},{16,8},{9,17},{17,9},{10,18},{18,10},{11,19},{19,11},{12,20... | collective-permute-start | bytes 3932168 | tf_op jit(solution)/shard_map/ppermute | solution.py:195
  987.7 163.0 %collective-permute-start.10 = (bf16[122,128,128]{2,1,0:T(8,128)(2,1)}, bf16[122,128,128]{2,1,0:T(8,128)(2,1)}, u32[]{:S(2)}, u32[]{:S(2)}) collective-permute-start(bf16[122,128,128]{2,1,0:T(8,128)(2,1)} %pack_tiles.6), channel_id=1, source_target_pairs={{0,4},{4,0},{1,5},{5,1},{2,6},{6,2},{3,7},{7,3},{8,12},{12,8},{9,1... | collective-permute-start | bytes 11993096 | tf_op jit(solution)/shard_map/ppermute | solution.py:195
  991.3 127.3 %collective-permute-start.51 = (bf16[2816,256]{1,0:T(8,128)(2,1)}, bf16[2816,256]{1,0:T(8,128)(2,1)}, u32[]{:S(2)}, u32[]{:S(2)}) collective-permute-start(bf16[2816,256]{1,0:T(8,128)(2,1)} %collective-permute-done.16), channel_id=1, source_target_pairs={{8,16},{16,8},{9,17},{17,9},{10,18},{18,10},{11,19},{19,11},{12,20... | collective-permute-start | bytes 4325384 | tf_op jit(solution)/shard_map/ppermute | solution.py:195
  993.1 125.5 %collective-permute-start.48 = (bf16[2816,256]{1,0:T(8,128)(2,1)}, bf16[2816,256]{1,0:T(8,128)(2,1)}, u32[]{:S(2)}, u32[]{:S(2)}) collective-permute-start(bf16[2816,256]{1,0:T(8,128)(2,1)} %collective-permute-done.47), channel_id=1, source_target_pairs={{8,0},{16,24},{9,1},{17,25},{10,2},{18,26},{11,3},{19,27},{12,4},{... | collective-permute-start | bytes 4325384 | tf_op jit(solution)/shard_map/ppermute | solution.py:195
  1092.6 197.8 %collective-permute-start.18 = (bf16[112,128,128]{2,1,0:T(8,128)(2,1)}, bf16[112,128,128]{2,1,0:T(8,128)(2,1)}, u32[]{:S(2)}, u32[]{:S(2)}) collective-permute-start(bf16[112,128,128]{2,1,0:T(8,128)(2,1)} %pack_tiles.7), channel_id=1, source_target_pairs={{0,8},{24,16},{1,9},{25,17},{2,10},{26,18},{3,11},{27,19},{4,12},{... | collective-permute-start | bytes 11010056 | tf_op jit(solution)/shard_map/ppermute | solution.py:195
  1116.8 13.7 collective-permute-start.49
  1118.6 30.4 %collective-permute-start.52 = (bf16[2816,256]{1,0:T(8,128)(2,1)}, bf16[2816,256]{1,0:T(8,128)(2,1)S(1)}, u32[]{:S(2)}, u32[]{:S(2)}) collective-permute-start(bf16[2816,256]{1,0:T(8,128)(2,1)} %collective-permute-done.51), channel_id=1, source_target_pairs={{8,0},{16,24},{9,1},{17,25},{10,2},{18,26},{11,3},{19,27},{12,4},{... | collective-permute-start | bytes 4325384 | tf_op jit(solution)/shard_map/ppermute | solution.py:195
  1130.5 152.0 %collective-permute-start.53 = (bf16[2816,256]{1,0:T(8,128)(2,1)}, bf16[2816,256]{1,0:T(8,128)(2,1)}, u32[]{:S(2)}, u32[]{:S(2)}) collective-permute-start(bf16[2816,256]{1,0:T(8,128)(2,1)} %collective-permute-done.17), channel_id=1, source_target_pairs={{8,16},{16,8},{9,17},{17,9},{10,18},{18,10},{11,19},{19,11},{12,20... | collective-permute-start | bytes 4325384 | tf_op jit(solution)/shard_map/ppermute | solution.py:195
  1132.3 150.2 %collective-permute-start.50 = (bf16[2816,256]{1,0:T(8,128)(2,1)}, bf16[2816,256]{1,0:T(8,128)(2,1)}, u32[]{:S(2)}, u32[]{:S(2)}) collective-permute-start(bf16[2816,256]{1,0:T(8,128)(2,1)} %collective-permute-done.49), channel_id=1, source_target_pairs={{8,0},{16,24},{9,1},{17,25},{10,2},{18,26},{11,3},{19,27},{12,4},{... | collective-permute-start | bytes 4325384 | tf_op jit(solution)/shard_map/ppermute | solution.py:195
  1253.8 81.7 %collective-permute-start.40 = (f32[128,1024]{1,0:T(8,128)}, f32[128,1024]{1,0:T(8,128)}, u32[]{:S(2)}, u32[]{:S(2)}) collective-permute-start(f32[128,1024]{1,0:T(8,128)} %bitcast.290), channel_id=1, source_target_pairs={{0,1},{1,0},{2,3},{3,2},{4,5},{5,4},{6,7},{7,6},{8,9},{9,8},{10,11... | collective-permute-start | bytes 1572872 | tf_op jit(solution)/shard_map/ppermute | solution.py:183
  1271.8 38.9 %collective-permute-start.11 = (f32[128,1024]{1,0:T(8,128)}, f32[128,1024]{1,0:T(8,128)}, u32[]{:S(2)}, u32[]{:S(2)}) collective-permute-start(f32[128,1024]{1,0:T(8,128)} %bitcast.291), channel_id=1, source_target_pairs={{0,1},{1,0},{2,3},{3,2},{4,5},{5,4},{6,7},{7,6},{8,9},{9,8},{10,11... | collective-permute-start | bytes 1572872 | tf_op jit(solution)/shard_map/ppermute | solution.py:183
  1282.6 140.1 %collective-permute-start.54 = (bf16[2816,256]{1,0:T(8,128)(2,1)}, bf16[2816,256]{1,0:T(8,128)(2,1)}, u32[]{:S(2)}, u32[]{:S(2)}) collective-permute-start(bf16[2816,256]{1,0:T(8,128)(2,1)} %collective-permute-done.53), channel_id=1, source_target_pairs={{8,0},{16,24},{9,1},{17,25},{10,2},{18,26},{11,3},{19,27},{12,4},{... | collective-permute-start | bytes 4325384 | tf_op jit(solution)/shard_map/ppermute | solution.py:195
  1290.4 58.5 %collective-permute-start.19 = (bf16[2560,256]{1,0:T(8,128)(2,1)}, bf16[2560,256]{1,0:T(8,128)(2,1)}, u32[]{:S(2)}, u32[]{:S(2)}) collective-permute-start(bf16[2560,256]{1,0:T(8,128)(2,1)} %constant_dynamic-update-slice_fusion.1), channel_id=1, source_target_pairs={{0,8},{24,16},{1,9},{25,17},{2,10},{26,18},{3,11},{27,19},{4,12},{... | collective-permute-start | bytes 3932168 | tf_op jit(solution)/shard_map/ppermute | solution.py:195
  1311.8 30.9 %collective-permute-start.12 = (f32[64,1024]{1,0:T(8,128)S(1)}, f32[64,1024]{1,0:T(8,128)S(1)}, u32[]{:S(2)}, u32[]{:S(2)}) collective-permute-start(f32[64,1024]{1,0:T(8,128)S(1)} %constant_dynamic-slice_fusion.28), channel_id=1, source_target_pairs={{0,4},{4,0},{1,5},{5,1},{2,6},{6,2},{3,7},{7,3},{8,12},{12,8},{9,1... | collective-permute-start | bytes 786440 | tf_op jit(solution)/shard_map/ppermute | solution.py:183
  1336.7 10.7 collective-permute-start.41
  1348.9 339.3 %collective-permute-start.42 = (f32[32,1024]{1,0:T(8,128)}, f32[32,1024]{1,0:T(8,128)}, u32[]{:S(2)}, u32[]{:S(2)}) collective-permute-start(f32[32,1024]{1,0:T(8,128)} %constant_dynamic-slice_fusion.15), channel_id=1, source_target_pairs={{0,2},{2,0},{1,3},{3,1},{4,6},{6,4},{5,7},{7,5},{8,10},{10,8},{9,1... | collective-permute-start | bytes 393224 | tf_op jit(solution)/shard_map/ppermute | solution.py:183
  1348.9 88.3 %collective-permute-start.20 = (bf16[2560,256]{1,0:T(8,128)(2,1)}, bf16[2560,256]{1,0:T(8,128)(2,1)}, u32[]{:S(2)}, u32[]{:S(2)}) collective-permute-start(bf16[2560,256]{1,0:T(8,128)(2,1)} %constant_dynamic-update-slice_fusion), channel_id=1, source_target_pairs={{0,8},{24,16},{1,9},{25,17},{2,10},{26,18},{3,11},{27,19},{4,12},{... | collective-permute-start | bytes 3932168 | tf_op jit(solution)/shard_map/ppermute | solution.py:195
  1429.1 56.6 %collective-permute-start.55 = (bf16[2560,256]{1,0:T(8,128)(2,1)}, bf16[2560,256]{1,0:T(8,128)(2,1)}, u32[]{:S(2)}, u32[]{:S(2)}) collective-permute-start(bf16[2560,256]{1,0:T(8,128)(2,1)} %collective-permute-done.19), channel_id=1, source_target_pairs={{8,16},{16,8},{9,17},{17,9},{10,18},{18,10},{11,19},{19,11},{12,20... | collective-permute-start | bytes 3932168 | tf_op jit(solution)/shard_map/ppermute | solution.py:195
  1437.2 84.5 %collective-permute-start.25 = (bf16[112,128,128]{2,1,0:T(8,128)(2,1)}, bf16[112,128,128]{2,1,0:T(8,128)(2,1)}, u32[]{:S(2)}, u32[]{:S(2)}) collective-permute-start(bf16[112,128,128]{2,1,0:T(8,128)(2,1)} %collective-permute-done.6.source), channel_id=1, source_target_pairs={{0,8},{24,16},{1,9},{25,17},{2,10},{26,18},{3,11},{27,19},{4,12},{... | collective-permute-start | bytes 11010056 | tf_op jit(solution)/shard_map/ppermute | solution.py:195
  1443.5 51.2 %collective-permute-start.56 = (bf16[2560,256]{1,0:T(8,128)(2,1)}, bf16[2560,256]{1,0:T(8,128)(2,1)}, u32[]{:S(2)}, u32[]{:S(2)}) collective-permute-start(bf16[2560,256]{1,0:T(8,128)(2,1)} %collective-permute-done.20), channel_id=1, source_target_pairs={{8,16},{16,8},{9,17},{17,9},{10,18},{18,10},{11,19},{19,11},{12,20... | collective-permute-start | bytes 3932168 | tf_op jit(solution)/shard_map/ppermute | solution.py:195
  1462.9 28.1 %collective-permute-start.21 = (f32[128,1024]{1,0:T(8,128)}, f32[128,1024]{1,0:T(8,128)}, u32[]{:S(2)}, u32[]{:S(2)}) collective-permute-start(f32[128,1024]{1,0:T(8,128)} %bitcast.296), channel_id=1, source_target_pairs={{0,1},{1,0},{2,3},{3,2},{4,5},{5,4},{6,7},{7,6},{8,9},{9,8},{10,11... | collective-permute-start | bytes 1572872 | tf_op jit(solution)/shard_map/ppermute | solution.py:183
  1492.9 12.4 collective-permute-start.22
  1505.3 6.8 collective-permute-start.57
  1507.1 183.5 %collective-permute-start.23 = (f32[32,1024]{1,0:T(8,128)}, f32[32,1024]{1,0:T(8,128)}, u32[]{:S(2)}, u32[]{:S(2)}) collective-permute-start(f32[32,1024]{1,0:T(8,128)} %constant_dynamic-slice_fusion.23), channel_id=1, source_target_pairs={{0,2},{2,0},{1,3},{3,1},{4,6},{6,4},{5,7},{7,5},{8,10},{10,8},{9,1... | collective-permute-start | bytes 393224 | tf_op jit(solution)/shard_map/ppermute | solution.py:183
  1512.2 8.5 collective-permute-start.58
  1521.4 74.0 %collective-permute-start.59 = (f32[32,1024]{1,0:T(8,128)}, f32[32,1024]{1,0:T(8,128)}, u32[]{:S(2)}, u32[]{:S(2)}) collective-permute-start(f32[32,1024]{1,0:T(8,128)} %constant_dynamic-slice_fusion.7), channel_id=1, source_target_pairs={{0,2},{2,0},{1,3},{3,1},{4,6},{6,4},{5,7},{7,5},{8,10},{10,8},{9,1... | collective-permute-start | bytes 393224 | tf_op jit(solution)/shard_map/ppermute | solution.py:183
  1540.6 24.0 %collective-permute-start.60 = (f32[128,1024]{1,0:T(8,128)}, f32[128,1024]{1,0:T(8,128)}, u32[]{:S(2)}, u32[]{:S(2)}) collective-permute-start(f32[128,1024]{1,0:T(8,128)} %bitcast.292), channel_id=1, source_target_pairs={{0,1},{1,0},{2,3},{3,2},{4,5},{5,4},{6,7},{7,6},{8,9},{9,8},{10,11... | collective-permute-start | bytes 1572872 | tf_op jit(solution)/shard_map/ppermute | solution.py:183
  1559.6 6.6 collective-permute-start.43
  1566.2 9.2 collective-permute-start.61
  1569.4 11.6 collective-permute-start.44
  1575.4 10.8 collective-permute-start.27
  1592.6 94.7 %collective-permute-start.63 = (f32[32,1024]{1,0:T(8,128)S(1)}, f32[32,1024]{1,0:T(8,128)S(1)}, u32[]{:S(2)}, u32[]{:S(2)}) collective-permute-start(f32[32,1024]{1,0:T(8,128)S(1)} %dynamic-slice_add_fusion.9), channel_id=1, source_target_pairs={{8,0},{16,24},{9,1},{17,25},{10,2},{18,26},{11,3},{19,27},{12,4},{... | collective-permute-start | bytes 393224 | tf_op jit(solution)/shard_map/ppermute | solution.py:351
  1594.0 95.6 %collective-permute-start.46 = (f32[32,1024]{1,0:T(8,128)S(1)}, f32[32,1024]{1,0:T(8,128)S(1)}, u32[]{:S(2)}, u32[]{:S(2)}) collective-permute-start(f32[32,1024]{1,0:T(8,128)S(1)} %dynamic-slice_add_fusion.10), channel_id=1, source_target_pairs={{8,0},{16,24},{9,1},{17,25},{10,2},{18,26},{11,3},{19,27},{12,4},{... | collective-permute-start | bytes 393224 | tf_op jit(solution)/shard_map/ppermute | solution.py:351
  1595.3 95.7 %collective-permute-start.29 = (f32[32,1024]{1,0:T(8,128)S(1)}, f32[32,1024]{1,0:T(8,128)S(1)}, u32[]{:S(2)}, u32[]{:S(2)}) collective-permute-start(f32[32,1024]{1,0:T(8,128)S(1)} %dynamic-slice_add_fusion.11), channel_id=1, source_target_pairs={{8,0},{16,24},{9,1},{17,25},{10,2},{18,26},{11,3},{19,27},{12,4},{... | collective-permute-start | bytes 393224 | tf_op jit(solution)/shard_map/ppermute | solution.py:351
  1692.7 12.2 collective-permute-start.64
  1692.8 14.2 collective-permute-start.65
  1707.0 12.4 collective-permute-start.66
  1709.9 21.1 %collective-permute-start.68 = (f32[128,1024]{1,0:T(8,128)S(1)}, f32[128,1024]{1,0:T(8,128)S(1)}, u32[]{:S(2)}, u32[]{:S(2)}) collective-permute-start(f32[128,1024]{1,0:T(8,128)S(1)} %collective-permute-done.67), channel_id=1, source_target_pairs={{8,0},{16,24},{9,1},{17,25},{10,2},{18,26},{11,3},{19,27},{12,4},{... | collective-permute-start | bytes 1572872 | tf_op jit(solution)/shard_map/ppermute | solution.py:205
  1744.8 14.7 collective-permute-start.70
  1759.6 45.2 %collective-permute-start.71 = (f32[1,1,1,4,136,128]{5,4,3,2,1,0:T(8,128)S(1)}, f32[1,1,1,4,136,128]{5,4,3,2,1,0:T(8,128)S(1)}, u32[]{:S(2)}, u32[]{:S(2)}) collective-permute-start(f32[1,1,1,4,136,128]{5,4,3,2,1,0:T(8,128)S(1)} %constant_dynamic-slice_fusion), channel_id=1, source_target_pairs={{0,2},{2,0},{1,3},{3,1},{4,6},{6,4},{5,7},{7,5},{8,10},{10,8},{9,1... | collective-permute-start | bytes 835592 | tf_op jit(solution)/shard_map/ppermute | solution.py:183
  (109 other events, 1915.3 us)

commit v3 on v2

--- a/solution.py
+++ b/solution.py
@@ -68,16 +68,16 @@
         functools.partial(pack_kernel, blk, row_blocks, columns, slots),
         out_shape=jax.ShapeDtypeStruct((slots, blk, blk), hist.dtype),
         in_specs=[pl.BlockSpec(memory_space=pltpu.SMEM), pl.BlockSpec(memory_space=pl.ANY)],
-        out_specs=pl.BlockSpec(memory_space=pl.ANY),
+        out_specs=pl.BlockSpec(memory_space=pltpu.VMEM),
         scratch_shapes=[pltpu.SemaphoreType.DMA],
+        compiler_params=params(vmem_limit_bytes=32 << 20),
         cost_estimate=pl.CostEstimate(flops=0, bytes_accessed=2 * slots * blk * blk * 2, transcendentals=0),
         name="pack_tiles",
     )(info, hist)
 
 
 def spread_kernel(blk, row_blocks, parts, slots, info, source, *refs):
-    outs, (zeros, sem) = refs[: len(parts)], refs[len(parts) :]
-    zeros[...] = jnp.zeros_like(zeros)
+    outs, sem = refs[: len(parts)], refs[len(parts)]
     base = info[0]
     used = jnp.int32(0)
     first = 0
@@ -90,27 +90,29 @@
                 there = info[1 + (first + c) * row_blocks + b] != 0
                 if slots is not None:
                     there = jnp.logical_and(there, used < slots)
-                target = out.at[pl.ds(b * blk, blk), pl.ds(place, blk)]
+                rows = pl.ds(b * blk, blk)
 
                 @pl.when(there)
                 def _():
-                    if slots is None:
-                        tile = source.at[pl.ds(b * blk, blk), pl.ds(start, blk)]
-                    else:
-                        tile = source.at[used]
-                    pltpu.make_async_copy(tile, target, sem).start()
+                    tile = source.at[rows, pl.ds(start, blk)] if slots is None else source.at[used]
+                    pltpu.make_async_copy(tile, out.at[rows, pl.ds(place, blk)], sem).start()
 
                 @pl.when(jnp.logical_not(there))
                 def _():
-                    pltpu.make_async_copy(zeros, target, sem).start()
+                    out[rows, pl.ds(place, blk)] = jnp.zeros((blk, blk), out.dtype)
 
                 used = used + there.astype(jnp.int32)
             return used
 
         used = lax.fori_loop(0, columns, one_column, used)
         first += columns
-    for out in outs:
-        pltpu.make_async_copy(out, out, sem).wait()
+
+    def one_wait(_, carry):
+        tile = source.at[pl.ds(0, blk), pl.ds(0, blk)] if slots is None else source.at[0]
+        pltpu.make_async_copy(tile, outs[0].at[pl.ds(0, blk), pl.ds(0, blk)], sem).wait()
+        return carry
+
+    lax.fori_loop(0, used, one_wait, 0)
 
 
 def spread(source, mask, base, parts):
@@ -124,8 +126,9 @@
         functools.partial(spread_kernel, blk, row_blocks, parts, source.shape[0] if packed else None),
         out_shape=shapes,
         in_specs=[pl.BlockSpec(memory_space=pltpu.SMEM), pl.BlockSpec(memory_space=pl.ANY)],
-        out_specs=[pl.BlockSpec(memory_space=pl.ANY)] * len(parts),
-        scratch_shapes=[pltpu.VMEM((blk, blk), source.dtype), pltpu.SemaphoreType.DMA],
+        out_specs=[pl.BlockSpec(memory_space=pltpu.VMEM)] * len(parts),
+        scratch_shapes=[pltpu.SemaphoreType.DMA],
+        compiler_params=params(vmem_limit_bytes=32 << 20),
         cost_estimate=pl.CostEstimate(
             flops=0, bytes_accessed=4 * sum(parts) * row_blocks * blk * blk, transcendentals=0
         ),
@@ -282,11 +285,8 @@
             got.append(over_x.send(tiles, "x", turn(wide, k)))
         return got
 
-    groups = [group(c) for c in range(4)]
-    tiles = {"lent": tiles_of("lent")}
-    groups += [group(c) for c in (4, 5)]
-    tiles["early"] = tiles_of("early")
-    tiles["late"] = tiles_of("late")
+    groups = [group(c) for c in range(6)]
+    tiles = {name: tiles_of(name) for name in ("early", "lent", "late")}
 
     over = jnp.int32(0)
     sessions = [[None] * 6 for _ in range(wide)]

time: 1820 us -> 900 us (0.49)
  Pallas kernels: 899 us -> 48.4 us
  starting transfers between devices: 265 us -> 128 us
  waiting for transfers between devices: 318 us -> 413 us
  matrix products: 152 us -> 114 us
    pallas_call x8, Pallas kernels: 532 us -> 27.3 us  [spread(): pl.pallas_call(functools.partial(spread_kernel, blk, row_blocks, parts, s...]
    pallas_call x4, Pallas kernels: 359 us -> 12.1 us  [pack(): pl.pallas_call(functools.partial(pack_kernel, blk, row_blocks, columns, s...]
    ppermute x37, waiting for transfers between devices: 144 us -> 326 us  [send(): got = lax.ppermute(values, axis, pairs)]
    ppermute x3, waiting for transfers between devices: 92.5 us -> 6.81 us  [body(): share = share + lax.ppermute(guest, 'z', OUTWARD)]
    ppermute x37, starting transfers between devices: 179 us -> 94.4 us  [send(): got = lax.ppermute(values, axis, pairs)]
    ppermute x24, starting transfers between devices: 70.2 us -> 19.4 us  [scatter_sum(): total = total + lax.ppermute(part((here + k) % count), axis, turn(count, k))]
    dot_general x60, matrix products: 152 us -> 114 us  [summed(): one = jnp.dot(a, b, preferred_element_type=jnp.float32)]
    unnamed x216 -> x232, local copies, waits for them, and re-layouts: 20.2 us -> 39.1 us
  transfers between devices with their start and end apart: 72 -> 72, of which waited for: 27 -> 34; matrix products, arithmetic and copies ran while one was open for 14% -> 24% of each run, Pallas kernels for 49% -> 4%
where the time goes in v3:
time: 900 us; the launch traced here: 886 us
  waiting for transfers between devices  413 us (46%)
  starting transfers between devices  128 us (14%)
  matrix products  114 us (13%)
  local copies, waits for them, and re-layouts  101 us (11%)
  Pallas kernels  48.4 us (5%)
  blocking collectives  38.6 us (4%)
  other arithmetic  22.5 us (2%)
  between operations  20.5 us (2%)
    ppermute x37, waiting for transfers between devices, send(): got = lax.ppermute(values, axis, pairs)  326 us
    dot_general x60, matrix products, summed(): one = jnp.dot(a, b, preferred_element_type=jnp.float32)  114 us
    ppermute x37, starting transfers between devices, send(): got = lax.ppermute(values, axis, pairs)  94.4 us
    ppermute x24, waiting for transfers between devices, scatter_sum(): total = total + lax.ppermute(part((here + k) % count), axis, turn(count, k))  47.4 us
    unnamed x232, local copies, waits for them, and re-layouts  39.1 us
    pmax x1, blocking collectives, body(): over = lax.pmax(over, ('z', 'x', 'y', 'core'))  38.6 us
    pallas_call x8, Pallas kernels, spread(): pl.pallas_call(functools.partial(spread_kernel, blk, row_blocks, parts, s...  27.3 us
    ppermute x24, starting transfers between devices, scatter_sum(): total = total + lax.ppermute(part((here + k) % count), axis, turn(count, k))  19.4 us
  transfers between devices with their start and end apart: 72, of which 34 were waited for; matrix products, arithmetic and copies ran while one was open for 24% of the time, Pallas kernels for 4%

profile of v3, /device:TPU:0, one launch (start us, length us, event | category | flops | bytes accessed | tf_op | source)
XLA Modules:
  0.0 886.2 jit_solution(2986485740257560661)
XLA Ops:
  7.2 2.9 collective-permute-start.7
  11.4 3.9 dynamic-slice_dynamic-update-slice_fusion.3
  34.5 4.2 pack_tiles.7
  38.7 3.2 spread_tiles.10
  43.5 2.7 pack_tiles.6
  52.8 3.4 spread_tiles.9
  59.4 3.4 spread_tiles.8
  64.5 3.6 collective-permute-start.24
  90.6 12.5 %collective-permute-done.3 = bf16[2816,128]{1,0:T(8,128)(2,1)} collective-permute-done((bf16[2816,128]{1,0:T(8,128)(2,1)}, bf16[2816,128]{1,0:T(8,128)(2,1)}, u32[]{:S(2)}, u32[]{:S(2)}) %collective-permute-start.3) | collective-permute-done | bytes 720928 | tf_op jit(solution)/shard_map/ppermute | solution.py:198
  111.0 4.6 collective-permute-done.14
  115.6 32.2 %collective-permute-start.15 = (bf16[2816,256]{1,0:T(8,128)(2,1)S(1)}, bf16[2816,256]{1,0:T(8,128)(2,1)}, u32[]{:S(2)}, u32[]{:S(2)}) collective-permute-start(bf16[2816,256]{1,0:T(8,128)(2,1)S(1)} %copy-done.62), channel_id=1, source_target_pairs={{0,8},{8,0},{16,24},{24,16},{1,9},{9,1},{17,25},{25,17},{2,10},{10... | collective-permute-start | bytes 4325384 | tf_op jit(solution)/shard_map/ppermute | solution.py:198
  156.9 23.6 %collective-permute-done.15 = bf16[2816,256]{1,0:T(8,128)(2,1)} collective-permute-done((bf16[2816,256]{1,0:T(8,128)(2,1)S(1)}, bf16[2816,256]{1,0:T(8,128)(2,1)}, u32[]{:S(2)}, u32[]{:S(2)}) %collective-permute-start.15) | collective-permute-done | bytes 1441824 | tf_op jit(solution)/shard_map/ppermute | solution.py:198
  181.0 30.2 %collective-permute-done.33 = bf16[2816,256]{1,0:T(8,128)(2,1)S(1)} collective-permute-done((bf16[2816,256]{1,0:T(8,128)(2,1)}, bf16[2816,256]{1,0:T(8,128)(2,1)S(1)}, u32[]{:S(2)}, u32[]{:S(2)}) %collective-permute-start.33) | collective-permute-done | bytes 1441824 | tf_op jit(solution)/shard_map/ppermute | solution.py:198
  214.1 24.9 %collective-permute-done.31 = bf16[2816,256]{1,0:T(8,128)(2,1)S(1)} collective-permute-done((bf16[2816,256]{1,0:T(8,128)(2,1)}, bf16[2816,256]{1,0:T(8,128)(2,1)S(1)}, u32[]{:S(2)}, u32[]{:S(2)}) %collective-permute-start.31) | collective-permute-done | bytes 1441824 | tf_op jit(solution)/shard_map/ppermute | solution.py:198
  242.9 3.1 fusion.81
  247.6 26.2 %collective-permute-done.16 = bf16[2816,256]{1,0:T(8,128)(2,1)} collective-permute-done((bf16[2816,256]{1,0:T(8,128)(2,1)}, bf16[2816,256]{1,0:T(8,128)(2,1)}, u32[]{:S(2)}, u32[]{:S(2)}) %collective-permute-start.16) | collective-permute-done | bytes 1441824 | tf_op jit(solution)/shard_map/ppermute | solution.py:198
  275.7 29.0 %collective-permute-done.37 = bf16[2816,256]{1,0:T(8,128)(2,1)S(1)} collective-permute-done((bf16[2816,256]{1,0:T(8,128)(2,1)S(1)}, bf16[2816,256]{1,0:T(8,128)(2,1)S(1)}, u32[]{:S(2)}, u32[]{:S(2)}) %collective-permute-start.37) | collective-permute-done | bytes 1441824 | tf_op jit(solution)/shard_map/ppermute | solution.py:198
  306.4 26.2 %collective-permute-done.35 = bf16[2816,256]{1,0:T(8,128)(2,1)S(1)} collective-permute-done((bf16[2816,256]{1,0:T(8,128)(2,1)S(1)}, bf16[2816,256]{1,0:T(8,128)(2,1)S(1)}, u32[]{:S(2)}, u32[]{:S(2)}) %collective-permute-start.35) | collective-permute-done | bytes 1441824 | tf_op jit(solution)/shard_map/ppermute | solution.py:198
  334.7 3.1 fusion.82
  337.8 3.3 spread_tiles.13
  341.1 4.1 fusion.80
  353.2 7.0 collective-permute-done.17
  363.6 4.3 spread_tiles.11
  371.3 38.4 %collective-permute-done.48 = bf16[2816,256]{1,0:T(8,128)(2,1)S(1)} collective-permute-done((bf16[2816,256]{1,0:T(8,128)(2,1)S(1)}, bf16[2816,256]{1,0:T(8,128)(2,1)S(1)}, u32[]{:S(2)}, u32[]{:S(2)}) %collective-permute-start.48) | collective-permute-done | bytes 1441824 | tf_op jit(solution)/shard_map/ppermute | solution.py:198
  411.0 3.1 fusion.86
  414.1 6.5 collective-permute-start.18
  420.5 20.2 %collective-permute-done.50 = bf16[2816,256]{1,0:T(8,128)(2,1)} collective-permute-done((bf16[2816,256]{1,0:T(8,128)(2,1)}, bf16[2816,256]{1,0:T(8,128)(2,1)}, u32[]{:S(2)}, u32[]{:S(2)}) %collective-permute-start.50) | collective-permute-done | bytes 1441824 | tf_op jit(solution)/shard_map/ppermute | solution.py:198
  442.5 3.1 fusion.83
  445.5 3.2 fusion.59
  448.8 3.2 fusion.60
  452.0 19.5 %collective-permute-done.52 = bf16[2816,256]{1,0:T(8,128)(2,1)S(1)} collective-permute-done((bf16[2816,256]{1,0:T(8,128)(2,1)}, bf16[2816,256]{1,0:T(8,128)(2,1)S(1)}, u32[]{:S(2)}, u32[]{:S(2)}) %collective-permute-start.52) | collective-permute-done | bytes 1441824 | tf_op jit(solution)/shard_map/ppermute | solution.py:198
  473.2 19.0 %collective-permute-done.54 = bf16[2816,256]{1,0:T(8,128)(2,1)S(1)} collective-permute-done((bf16[2816,256]{1,0:T(8,128)(2,1)}, bf16[2816,256]{1,0:T(8,128)(2,1)S(1)}, u32[]{:S(2)}, u32[]{:S(2)}) %collective-permute-start.54) | collective-permute-done | bytes 1441824 | tf_op jit(solution)/shard_map/ppermute | solution.py:198
  494.0 4.3 spread_tiles.12
  505.3 2.8 gather_fusion.8
  514.4 3.3 fusion.78
  523.7 2.8 gather_fusion.5
  531.3 3.3 fusion.88
  540.8 8.9 %collective-permute-start.19 = (bf16[2560,256]{1,0:T(8,128)(2,1)S(1)}, bf16[2560,256]{1,0:T(8,128)(2,1)}, u32[]{:S(2)}, u32[]{:S(2)}) collective-permute-start(bf16[2560,256]{1,0:T(8,128)(2,1)S(1)} %copy-done.44), channel_id=1, source_target_pairs={{0,8},{24,16},{1,9},{25,17},{2,10},{26,18},{3,11},{27,19},{4,12},{... | collective-permute-start | bytes 3932168 | tf_op jit(solution)/shard_map/ppermute | solution.py:198
  563.1 6.0 collective-permute-done.12
  569.1 7.7 collective-permute-done.19
  576.8 5.6 collective-permute-start.20
  585.4 3.0 collective-permute-done.13
  594.7 13.9 %collective-permute-done.20 = bf16[2560,256]{1,0:T(8,128)(2,1)} collective-permute-done((bf16[2560,256]{1,0:T(8,128)(2,1)S(1)}, bf16[2560,256]{1,0:T(8,128)(2,1)}, u32[]{:S(2)}, u32[]{:S(2)}) %collective-permute-start.20) | collective-permute-done | bytes 1310752 | tf_op jit(solution)/shard_map/ppermute | solution.py:198
  608.7 6.3 collective-permute-start.25
  625.0 2.8 gather_fusion.6
  632.9 3.1 fusion.101
  664.5 4.4 collective-permute-done.58
  669.9 20.5 %collective-permute-done.25.source = bf16[112,128,128]{2,1,0:T(8,128)(2,1)} collective-permute-done((bf16[112,128,128]{2,1,0:T(8,128)(2,1)}, bf16[112,128,128]{2,1,0:T(8,128)(2,1)}, u32[]{:S(2)}, u32[]{:S(2)}) %collective-permute-start.25) | collective-permute-done | bytes 3670048 | tf_op jit(solution)/shard_map/ppermute | solution.py:198
  690.4 2.7 spread_tiles.15
  700.2 2.8 gather_fusion.11
  706.1 3.0 fusion.98
  711.3 2.8 gather_fusion.9
  727.2 5.8 collective-permute-done.61
  733.6 5.0 collective-permute-done.44
  740.8 2.9 collective-permute-done.27
  746.0 4.2 collective-permute-done.45
  754.4 4.6 collective-permute-done.63
  765.6 11.7 %collective-permute-done.64 = f32[128,1024]{1,0:T(8,128)S(1)} collective-permute-done((f32[128,1024]{1,0:T(8,128)S(1)}, f32[128,1024]{1,0:T(8,128)S(1)}, u32[]{:S(2)}, u32[]{:S(2)}) %collective-permute-start.64) | collective-permute-done | bytes 524320 | tf_op jit(solution)/shard_map/ppermute | solution.py:204
  784.6 9.1 %collective-permute-done.66 = f32[128,1024]{1,0:T(8,128)S(1)} collective-permute-done((f32[128,1024]{1,0:T(8,128)S(1)}, f32[128,1024]{1,0:T(8,128)S(1)}, u32[]{:S(2)}, u32[]{:S(2)}) %collective-permute-start.66) | collective-permute-done | bytes 524320 | tf_op jit(solution)/shard_map/ppermute | solution.py:207
  793.8 10.5 %collective-permute-done.68 = f32[128,1024]{1,0:T(8,128)S(1)} collective-permute-done((f32[128,1024]{1,0:T(8,128)S(1)}, f32[128,1024]{1,0:T(8,128)S(1)}, u32[]{:S(2)}, u32[]{:S(2)}) %collective-permute-start.68) | collective-permute-done | bytes 524320 | tf_op jit(solution)/shard_map/ppermute | solution.py:208
  804.6 9.0 %pair_dots.1 = f32[32,136,128]{2,1,0:T(8,128)S(1)} custom-call(s32[2,2,32]{2,1,0:T(2,128)S(1)} %pad_add_fusion.2.ids, f32[4,128,1024]{2,1,0:T(8,128)S(1)} %pad_maximum_fusion.blocks), custom_call_target="tpu_custom_call" | custom-call | tf_op jit(solution)/shard_map/pair_dots/pallas_call | solution.py:162
  813.7 2.9 collective-permute-done.69
  819.8 12.9 %collective-permute-done.70 = f32[1,2,1,4,136,128]{5,4,3,2,1,0:T(8,128)S(1)} collective-permute-done((f32[1,2,1,4,136,128]{5,4,3,2,1,0:T(8,128)S(1)}, f32[1,2,1,4,136,128]{5,4,3,2,1,0:T(8,128)S(1)}, u32[]{:S(2)}, u32[]{:S(2)}) %collective-permute-start.70) | collective-permute-done | bytes 557088 | tf_op jit(solution)/shard_map/ppermute | solution.py:186
  838.8 38.6 %pmax.7 = s32[]{:T(128)} all-reduce(s32[]{:T(128)S(6)} %max.25), channel_id=1, replica_groups=mesh['z'=4,'x'=2,'y'=2,'core'=2] {'z','x','y','core'}, use_global_device_ids=true, to_apply=%region_6.7 | all-reduce | flops 1 | bytes 8 | tf_op jit(solution)/shard_map/pmax | solution.py:369
  (533 shorter events, 260.5 us)
Async XLA Ops:
  7.2 57.2 %collective-permute-start.7 = (s32[4,128]{1,0:T(4,128)S(1)}, s32[4,128]{1,0:T(4,128)S(1)}, u32[]{:S(2)}, u32[]{:S(2)}) collective-permute-start(s32[4,128]{1,0:T(4,128)S(1)} %get-tuple-element.207), channel_id=1, source_target_pairs={{0,4},{4,0},{1,5},{5,1},{2,6},{6,2},{3,7},{7,3},{8,12},{12,8},{9,1... | collective-permute-start | bytes 6152 | tf_op jit(solution)/shard_map/ppermute | solution.py:262
  15.3 53.1 %collective-permute-start.2 = (bf16[2816,128]{1,0:T(8,128)(2,1)}, bf16[2816,128]{1,0:T(8,128)(2,1)}, u32[]{:S(2)}, u32[]{:S(2)}) collective-permute-start(bf16[2816,128]{1,0:T(8,128)(2,1)} %get-tuple-element.185), channel_id=1, source_target_pairs={{0,4},{4,0},{1,5},{5,1},{2,6},{6,2},{3,7},{7,3},{8,12},{12,8},{9,1... | collective-permute-start | bytes 2162696 | tf_op jit(solution)/shard_map/ppermute | solution.py:198
  15.3 57.2 %collective-permute-start.1 = (bf16[2816,128]{1,0:T(8,128)(2,1)}, bf16[2816,128]{1,0:T(8,128)(2,1)}, u32[]{:S(2)}, u32[]{:S(2)}) collective-permute-start(bf16[2816,128]{1,0:T(8,128)(2,1)} %get-tuple-element.186), channel_id=1, source_target_pairs={{0,4},{4,0},{1,5},{5,1},{2,6},{6,2},{3,7},{7,3},{8,12},{12,8},{9,1... | collective-permute-start | bytes 2162696 | tf_op jit(solution)/shard_map/ppermute | solution.py:198
  64.5 18.9 %collective-permute-start.24 = (s32[2,4,40]{2,1,0:T(4,128)S(1)}, s32[2,4,40]{2,1,0:T(4,128)S(1)}, u32[]{:S(2)}, u32[]{:S(2)}) collective-permute-start(s32[2,4,40]{2,1,0:T(4,128)S(1)} %pad_add_fusion), channel_id=1, source_target_pairs={{0,8},{24,16},{1,9},{25,17},{2,10},{26,18},{3,11},{27,19},{4,12},{... | collective-permute-start | bytes 3848 | tf_op jit(solution)/shard_map/ppermute | solution.py:263
  68.4 19.3 %collective-permute-start.4 = (bf16[2816,128]{1,0:T(8,128)(2,1)}, bf16[2816,128]{1,0:T(8,128)(2,1)}, u32[]{:S(2)}, u32[]{:S(2)}) collective-permute-start(bf16[2816,128]{1,0:T(8,128)(2,1)} %get-tuple-element.114), channel_id=1, source_target_pairs={{0,4},{4,0},{1,5},{5,1},{2,6},{6,2},{3,7},{7,3},{8,12},{12,8},{9,1... | collective-permute-start | bytes 2162696 | tf_op jit(solution)/shard_map/ppermute | solution.py:198
  70.7 19.1 %collective-permute-start.32 = (bf16[2816,256]{1,0:T(8,128)(2,1)}, bf16[2816,256]{1,0:T(8,128)(2,1)}, u32[]{:S(2)}, u32[]{:S(2)}) collective-permute-start(bf16[2816,256]{1,0:T(8,128)(2,1)} %constant_dynamic-update-slice_fusion.4), channel_id=1, source_target_pairs={{8,16},{16,8},{9,17},{17,9},{10,18},{18,10},{11,19},{19,11},{12,20... | collective-permute-start | bytes 4325384 | tf_op jit(solution)/shard_map/ppermute | solution.py:198
  74.6 30.6 %collective-permute-start.30 = (bf16[2816,256]{1,0:T(8,128)(2,1)}, bf16[2816,256]{1,0:T(8,128)(2,1)}, u32[]{:S(2)}, u32[]{:S(2)}) collective-permute-start(bf16[2816,256]{1,0:T(8,128)(2,1)} %constant_dynamic-update-slice_fusion.5), channel_id=1, source_target_pairs={{8,16},{16,8},{9,17},{17,9},{10,18},{18,10},{11,19},{19,11},{12,20... | collective-permute-start | bytes 4325384 | tf_op jit(solution)/shard_map/ppermute | solution.py:198
  81.7 21.5 %collective-permute-start.3 = (bf16[2816,128]{1,0:T(8,128)(2,1)}, bf16[2816,128]{1,0:T(8,128)(2,1)}, u32[]{:S(2)}, u32[]{:S(2)}) collective-permute-start(bf16[2816,128]{1,0:T(8,128)(2,1)} %get-tuple-element.112), channel_id=1, source_target_pairs={{0,4},{4,0},{1,5},{5,1},{2,6},{6,2},{3,7},{7,3},{8,12},{12,8},{9,1... | collective-permute-start | bytes 2162696 | tf_op jit(solution)/shard_map/ppermute | solution.py:198
  83.9 31.7 %collective-permute-start.14 = (bf16[2816,256]{1,0:T(8,128)(2,1)}, bf16[2816,256]{1,0:T(8,128)(2,1)S(1)}, u32[]{:S(2)}, u32[]{:S(2)}) collective-permute-start(bf16[2816,256]{1,0:T(8,128)(2,1)} %constant_dynamic-update-slice_fusion.5), channel_id=1, source_target_pairs={{0,8},{8,0},{16,24},{24,16},{1,9},{9,1},{17,25},{25,17},{2,10},{10... | collective-permute-start | bytes 4325384 | tf_op jit(solution)/shard_map/ppermute | solution.py:198
  87.7 60.2 %collective-permute-start.6 = (bf16[2560,128]{1,0:T(8,128)(2,1)}, bf16[2560,128]{1,0:T(8,128)(2,1)S(1)}, u32[]{:S(2)}, u32[]{:S(2)}) collective-permute-start(bf16[2560,128]{1,0:T(8,128)(2,1)} %get-tuple-element.118), channel_id=1, source_target_pairs={{0,4},{4,0},{1,5},{5,1},{2,6},{6,2},{3,7},{7,3},{8,12},{12,8},{9,1... | collective-permute-start | bytes 1966088 | tf_op jit(solution)/shard_map/ppermute | solution.py:198
  89.9 61.9 %collective-permute-start.36 = (bf16[2816,256]{1,0:T(8,128)(2,1)}, bf16[2816,256]{1,0:T(8,128)(2,1)S(1)}, u32[]{:S(2)}, u32[]{:S(2)}) collective-permute-start(bf16[2816,256]{1,0:T(8,128)(2,1)} %constant_dynamic-update-slice_fusion.2), channel_id=1, source_target_pairs={{8,16},{16,8},{9,17},{17,9},{10,18},{18,10},{11,19},{19,11},{12,20... | collective-permute-start | bytes 4325384 | tf_op jit(solution)/shard_map/ppermute | solution.py:198
  105.2 49.1 %collective-permute-start.34 = (bf16[2816,256]{1,0:T(8,128)(2,1)}, bf16[2816,256]{1,0:T(8,128)(2,1)S(1)}, u32[]{:S(2)}, u32[]{:S(2)}) collective-permute-start(bf16[2816,256]{1,0:T(8,128)(2,1)} %constant_dynamic-update-slice_fusion.3), channel_id=1, source_target_pairs={{8,16},{16,8},{9,17},{17,9},{10,18},{18,10},{11,19},{19,11},{12,20... | collective-permute-start | bytes 4325384 | tf_op jit(solution)/shard_map/ppermute | solution.py:198
  108.4 45.0 %collective-permute-start.5 = (bf16[2560,128]{1,0:T(8,128)(2,1)S(1)}, bf16[2560,128]{1,0:T(8,128)(2,1)S(1)}, u32[]{:S(2)}, u32[]{:S(2)}) collective-permute-start(bf16[2560,128]{1,0:T(8,128)(2,1)S(1)} %copy-done.72), channel_id=1, source_target_pairs={{0,4},{4,0},{1,5},{5,1},{2,6},{6,2},{3,7},{7,3},{8,12},{12,8},{9,1... | collective-permute-start | bytes 1966088 | tf_op jit(solution)/shard_map/ppermute | solution.py:198
  115.6 64.8 %collective-permute-start.15 = (bf16[2816,256]{1,0:T(8,128)(2,1)S(1)}, bf16[2816,256]{1,0:T(8,128)(2,1)}, u32[]{:S(2)}, u32[]{:S(2)}) collective-permute-start(bf16[2816,256]{1,0:T(8,128)(2,1)S(1)} %copy-done.62), channel_id=1, source_target_pairs={{0,8},{8,0},{16,24},{24,16},{1,9},{9,1},{17,25},{25,17},{2,10},{10... | collective-permute-start | bytes 4325384 | tf_op jit(solution)/shard_map/ppermute | solution.py:198
  147.8 63.4 %collective-permute-start.33 = (bf16[2816,256]{1,0:T(8,128)(2,1)}, bf16[2816,256]{1,0:T(8,128)(2,1)S(1)}, u32[]{:S(2)}, u32[]{:S(2)}) collective-permute-start(bf16[2816,256]{1,0:T(8,128)(2,1)} %collective-permute-done.32), channel_id=1, source_target_pairs={{8,0},{16,24},{9,1},{17,25},{10,2},{18,26},{11,3},{19,27},{12,4},{... | collective-permute-start | bytes 4325384 | tf_op jit(solution)/shard_map/ppermute | solution.py:198
  151.8 87.2 %collective-permute-start.31 = (bf16[2816,256]{1,0:T(8,128)(2,1)}, bf16[2816,256]{1,0:T(8,128)(2,1)S(1)}, u32[]{:S(2)}, u32[]{:S(2)}) collective-permute-start(bf16[2816,256]{1,0:T(8,128)(2,1)} %collective-permute-done.30), channel_id=1, source_target_pairs={{8,0},{16,24},{9,1},{17,25},{10,2},{18,26},{11,3},{19,27},{12,4},{... | collective-permute-start | bytes 4325384 | tf_op jit(solution)/shard_map/ppermute | solution.py:198
  153.4 85.7 %collective-permute-start.39 = (bf16[2560,256]{1,0:T(8,128)(2,1)S(1)}, bf16[2560,256]{1,0:T(8,128)(2,1)S(1)}, u32[]{:S(2)}, u32[]{:S(2)}) collective-permute-start(bf16[2560,256]{1,0:T(8,128)(2,1)S(1)} %constant_dynamic-update-slice_fusion), channel_id=1, source_target_pairs={{8,16},{16,8},{9,17},{17,9},{10,18},{18,10},{11,19},{19,11},{12,20... | collective-permute-start | bytes 3932168 | tf_op jit(solution)/shard_map/ppermute | solution.py:198
  154.4 87.0 %collective-permute-start.38 = (bf16[2560,256]{1,0:T(8,128)(2,1)S(1)}, bf16[2560,256]{1,0:T(8,128)(2,1)S(1)}, u32[]{:S(2)}, u32[]{:S(2)}) collective-permute-start(bf16[2560,256]{1,0:T(8,128)(2,1)S(1)} %constant_dynamic-update-slice_fusion.1), channel_id=1, source_target_pairs={{8,16},{16,8},{9,17},{17,9},{10,18},{18,10},{11,19},{19,11},{12,20... | collective-permute-start | bytes 3932168 | tf_op jit(solution)/shard_map/ppermute | solution.py:198
  180.4 157.4 %collective-permute-start.10 = (bf16[112,128,128]{2,1,0:T(8,128)(2,1)S(1)}, bf16[112,128,128]{2,1,0:T(8,128)(2,1)}, u32[]{:S(2)}, u32[]{:S(2)}) collective-permute-start(bf16[112,128,128]{2,1,0:T(8,128)(2,1)S(1)} %copy-done.11), channel_id=1, source_target_pairs={{0,4},{4,0},{1,5},{5,1},{2,6},{6,2},{3,7},{7,3},{8,12},{12,8},{9,1... | collective-permute-start | bytes 11010056 | tf_op jit(solution)/shard_map/ppermute | solution.py:198
  211.2 133.9 %collective-permute-start.8 = (bf16[122,128,128]{2,1,0:T(8,128)(2,1)S(1)}, bf16[122,128,128]{2,1,0:T(8,128)(2,1)S(1)}, u32[]{:S(2)}, u32[]{:S(2)}) collective-permute-start(bf16[122,128,128]{2,1,0:T(8,128)(2,1)S(1)} %copy-done.7), channel_id=1, source_target_pairs={{0,4},{4,0},{1,5},{5,1},{2,6},{6,2},{3,7},{7,3},{8,12},{12,8},{9,1... | collective-permute-start | bytes 11993096 | tf_op jit(solution)/shard_map/ppermute | solution.py:198
  239.0 34.8 %collective-permute-start.16 = (bf16[2816,256]{1,0:T(8,128)(2,1)}, bf16[2816,256]{1,0:T(8,128)(2,1)}, u32[]{:S(2)}, u32[]{:S(2)}) collective-permute-start(bf16[2816,256]{1,0:T(8,128)(2,1)} %constant_dynamic-update-slice_fusion.3), channel_id=1, source_target_pairs={{0,8},{8,0},{16,24},{24,16},{1,9},{9,1},{17,25},{25,17},{2,10},{10... | collective-permute-start | bytes 4325384 | tf_op jit(solution)/shard_map/ppermute | solution.py:198
  239.1 65.6 %collective-permute-start.37 = (bf16[2816,256]{1,0:T(8,128)(2,1)S(1)}, bf16[2816,256]{1,0:T(8,128)(2,1)S(1)}, u32[]{:S(2)}, u32[]{:S(2)}) collective-permute-start(bf16[2816,256]{1,0:T(8,128)(2,1)S(1)} %collective-permute-done.36), channel_id=1, source_target_pairs={{8,0},{16,24},{9,1},{17,25},{10,2},{18,26},{11,3},{19,27},{12,4},{... | collective-permute-start | bytes 4325384 | tf_op jit(solution)/shard_map/ppermute | solution.py:198
  241.3 91.2 %collective-permute-start.35 = (bf16[2816,256]{1,0:T(8,128)(2,1)S(1)}, bf16[2816,256]{1,0:T(8,128)(2,1)S(1)}, u32[]{:S(2)}, u32[]{:S(2)}) collective-permute-start(bf16[2816,256]{1,0:T(8,128)(2,1)S(1)} %collective-permute-done.34), channel_id=1, source_target_pairs={{8,0},{16,24},{9,1},{17,25},{10,2},{18,26},{11,3},{19,27},{12,4},{... | collective-permute-start | bytes 4325384 | tf_op jit(solution)/shard_map/ppermute | solution.py:198
  273.9 78.0 %collective-permute-start.49 = (bf16[2816,256]{1,0:T(8,128)(2,1)}, bf16[2816,256]{1,0:T(8,128)(2,1)}, u32[]{:S(2)}, u32[]{:S(2)}) collective-permute-start(bf16[2816,256]{1,0:T(8,128)(2,1)} %collective-permute-done.15), channel_id=1, source_target_pairs={{8,16},{16,8},{9,17},{17,9},{10,18},{18,10},{11,19},{19,11},{12,20... | collective-permute-start | bytes 4325384 | tf_op jit(solution)/shard_map/ppermute | solution.py:198
  304.7 43.2 %collective-permute-start.47 = (bf16[2816,256]{1,0:T(8,128)(2,1)S(1)}, bf16[2816,256]{1,0:T(8,128)(2,1)S(1)}, u32[]{:S(2)}, u32[]{:S(2)}) collective-permute-start(bf16[2816,256]{1,0:T(8,128)(2,1)S(1)} %collective-permute-done.14), channel_id=1, source_target_pairs={{8,16},{16,8},{9,17},{17,9},{10,18},{18,10},{11,19},{19,11},{12,20... | collective-permute-start | bytes 4325384 | tf_op jit(solution)/shard_map/ppermute | solution.py:198
  332.6 27.6 %collective-permute-start.17 = (bf16[2816,256]{1,0:T(8,128)(2,1)}, bf16[2816,256]{1,0:T(8,128)(2,1)}, u32[]{:S(2)}, u32[]{:S(2)}) collective-permute-start(bf16[2816,256]{1,0:T(8,128)(2,1)} %constant_dynamic-update-slice_fusion.2), channel_id=1, source_target_pairs={{0,8},{8,0},{16,24},{24,16},{1,9},{9,1},{17,25},{25,17},{2,10},{10... | collective-permute-start | bytes 4325384 | tf_op jit(solution)/shard_map/ppermute | solution.py:198
  345.7 148.3 %collective-permute-start.9 = (bf16[122,128,128]{2,1,0:T(8,128)(2,1)S(1)}, bf16[122,128,128]{2,1,0:T(8,128)(2,1)S(1)}, u32[]{:S(2)}, u32[]{:S(2)}) collective-permute-start(bf16[122,128,128]{2,1,0:T(8,128)(2,1)S(1)} %copy-done.9), channel_id=1, source_target_pairs={{0,4},{4,0},{1,5},{5,1},{2,6},{6,2},{3,7},{7,3},{8,12},{12,8},{9,1... | collective-permute-start | bytes 11993096 | tf_op jit(solution)/shard_map/ppermute | solution.py:198
  347.9 23.3 %collective-permute-start.51 = (bf16[2816,256]{1,0:T(8,128)(2,1)}, bf16[2816,256]{1,0:T(8,128)(2,1)}, u32[]{:S(2)}, u32[]{:S(2)}) collective-permute-start(bf16[2816,256]{1,0:T(8,128)(2,1)} %collective-permute-done.16), channel_id=1, source_target_pairs={{8,16},{16,8},{9,17},{17,9},{10,18},{18,10},{11,19},{19,11},{12,20... | collective-permute-start | bytes 4325384 | tf_op jit(solution)/shard_map/ppermute | solution.py:198
  349.7 60.0 %collective-permute-start.48 = (bf16[2816,256]{1,0:T(8,128)(2,1)S(1)}, bf16[2816,256]{1,0:T(8,128)(2,1)S(1)}, u32[]{:S(2)}, u32[]{:S(2)}) collective-permute-start(bf16[2816,256]{1,0:T(8,128)(2,1)S(1)} %collective-permute-done.47), channel_id=1, source_target_pairs={{8,0},{16,24},{9,1},{17,25},{10,2},{18,26},{11,3},{19,27},{12,4},{... | collective-permute-start | bytes 4325384 | tf_op jit(solution)/shard_map/ppermute | solution.py:198
  351.9 88.8 %collective-permute-start.50 = (bf16[2816,256]{1,0:T(8,128)(2,1)}, bf16[2816,256]{1,0:T(8,128)(2,1)}, u32[]{:S(2)}, u32[]{:S(2)}) collective-permute-start(bf16[2816,256]{1,0:T(8,128)(2,1)} %collective-permute-done.49), channel_id=1, source_target_pairs={{8,0},{16,24},{9,1},{17,25},{10,2},{18,26},{11,3},{19,27},{12,4},{... | collective-permute-start | bytes 4325384 | tf_op jit(solution)/shard_map/ppermute | solution.py:198
  360.2 80.5 %collective-permute-start.53 = (bf16[2816,256]{1,0:T(8,128)(2,1)}, bf16[2816,256]{1,0:T(8,128)(2,1)}, u32[]{:S(2)}, u32[]{:S(2)}) collective-permute-start(bf16[2816,256]{1,0:T(8,128)(2,1)} %collective-permute-done.17), channel_id=1, source_target_pairs={{8,16},{16,8},{9,17},{17,9},{10,18},{18,10},{11,19},{19,11},{12,20... | collective-permute-start | bytes 4325384 | tf_op jit(solution)/shard_map/ppermute | solution.py:198
  409.7 61.8 %collective-permute-start.52 = (bf16[2816,256]{1,0:T(8,128)(2,1)}, bf16[2816,256]{1,0:T(8,128)(2,1)S(1)}, u32[]{:S(2)}, u32[]{:S(2)}) collective-permute-start(bf16[2816,256]{1,0:T(8,128)(2,1)} %collective-permute-done.51), channel_id=1, source_target_pairs={{8,0},{16,24},{9,1},{17,25},{10,2},{18,26},{11,3},{19,27},{12,4},{... | collective-permute-start | bytes 4325384 | tf_op jit(solution)/shard_map/ppermute | solution.py:198
  414.1 126.7 %collective-permute-start.18 = (bf16[112,128,128]{2,1,0:T(8,128)(2,1)}, bf16[112,128,128]{2,1,0:T(8,128)(2,1)}, u32[]{:S(2)}, u32[]{:S(2)}) collective-permute-start(bf16[112,128,128]{2,1,0:T(8,128)(2,1)} %pack_tiles.7), channel_id=1, source_target_pairs={{0,8},{24,16},{1,9},{25,17},{2,10},{26,18},{3,11},{27,19},{4,12},{... | collective-permute-start | bytes 11010056 | tf_op jit(solution)/shard_map/ppermute | solution.py:198
  440.7 51.6 %collective-permute-start.54 = (bf16[2816,256]{1,0:T(8,128)(2,1)}, bf16[2816,256]{1,0:T(8,128)(2,1)S(1)}, u32[]{:S(2)}, u32[]{:S(2)}) collective-permute-start(bf16[2816,256]{1,0:T(8,128)(2,1)} %collective-permute-done.53), channel_id=1, source_target_pairs={{8,0},{16,24},{9,1},{17,25},{10,2},{18,26},{11,3},{19,27},{12,4},{... | collective-permute-start | bytes 4325384 | tf_op jit(solution)/shard_map/ppermute | solution.py:198
  512.4 48.0 %collective-permute-start.40 = (f32[128,1024]{1,0:T(8,128)}, f32[128,1024]{1,0:T(8,128)}, u32[]{:S(2)}, u32[]{:S(2)}) collective-permute-start(f32[128,1024]{1,0:T(8,128)} %bitcast.290), channel_id=1, source_target_pairs={{0,1},{1,0},{2,3},{3,2},{4,5},{5,4},{6,7},{7,6},{8,9},{9,8},{10,11... | collective-permute-start | bytes 1572872 | tf_op jit(solution)/shard_map/ppermute | solution.py:186
  529.6 29.0 %collective-permute-start.11 = (f32[128,1024]{1,0:T(8,128)}, f32[128,1024]{1,0:T(8,128)}, u32[]{:S(2)}, u32[]{:S(2)}) collective-permute-start(f32[128,1024]{1,0:T(8,128)} %bitcast.293), channel_id=1, source_target_pairs={{0,1},{1,0},{2,3},{3,2},{4,5},{5,4},{6,7},{7,6},{8,9},{9,8},{10,11... | collective-permute-start | bytes 1572872 | tf_op jit(solution)/shard_map/ppermute | solution.py:186
  540.8 36.0 %collective-permute-start.19 = (bf16[2560,256]{1,0:T(8,128)(2,1)S(1)}, bf16[2560,256]{1,0:T(8,128)(2,1)}, u32[]{:S(2)}, u32[]{:S(2)}) collective-permute-start(bf16[2560,256]{1,0:T(8,128)(2,1)S(1)} %copy-done.44), channel_id=1, source_target_pairs={{0,8},{24,16},{1,9},{25,17},{2,10},{26,18},{3,11},{27,19},{4,12},{... | collective-permute-start | bytes 3932168 | tf_op jit(solution)/shard_map/ppermute | solution.py:198
  559.8 9.3 %collective-permute-start.12 = (f32[64,1024]{1,0:T(8,128)S(1)}, f32[64,1024]{1,0:T(8,128)S(1)}, u32[]{:S(2)}, u32[]{:S(2)}) collective-permute-start(f32[64,1024]{1,0:T(8,128)S(1)} %constant_dynamic-slice_fusion.28), channel_id=1, source_target_pairs={{0,4},{4,0},{1,5},{5,1},{2,6},{6,2},{3,7},{7,3},{8,12},{12,8},{9,1... | collective-permute-start | bytes 786440 | tf_op jit(solution)/shard_map/ppermute | solution.py:186
  561.5 23.1 %collective-permute-start.41 = (f32[64,1024]{1,0:T(8,128)S(1)}, f32[64,1024]{1,0:T(8,128)S(1)}, u32[]{:S(2)}, u32[]{:S(2)}) collective-permute-start(f32[64,1024]{1,0:T(8,128)S(1)} %constant_dynamic-slice_fusion.16), channel_id=1, source_target_pairs={{0,4},{4,0},{1,5},{5,1},{2,6},{6,2},{3,7},{7,3},{8,12},{12,8},{9,1... | collective-permute-start | bytes 786440 | tf_op jit(solution)/shard_map/ppermute | solution.py:186
  576.8 31.8 %collective-permute-start.20 = (bf16[2560,256]{1,0:T(8,128)(2,1)S(1)}, bf16[2560,256]{1,0:T(8,128)(2,1)}, u32[]{:S(2)}, u32[]{:S(2)}) collective-permute-start(bf16[2560,256]{1,0:T(8,128)(2,1)S(1)} %copy-done.66), channel_id=1, source_target_pairs={{0,8},{24,16},{1,9},{25,17},{2,10},{26,18},{3,11},{27,19},{4,12},{... | collective-permute-start | bytes 3932168 | tf_op jit(solution)/shard_map/ppermute | solution.py:198
  585.4 174.6 %collective-permute-start.42 = (f32[32,1024]{1,0:T(8,128)}, f32[32,1024]{1,0:T(8,128)}, u32[]{:S(2)}, u32[]{:S(2)}) collective-permute-start(f32[32,1024]{1,0:T(8,128)} %constant_dynamic-slice_fusion.15), channel_id=1, source_target_pairs={{0,2},{2,0},{1,3},{3,1},{4,6},{6,4},{5,7},{7,5},{8,10},{10,8},{9,1... | collective-permute-start | bytes 393224 | tf_op jit(solution)/shard_map/ppermute | solution.py:186
  588.4 44.5 %collective-permute-start.55 = (bf16[2560,256]{1,0:T(8,128)(2,1)}, bf16[2560,256]{1,0:T(8,128)(2,1)}, u32[]{:S(2)}, u32[]{:S(2)}) collective-permute-start(bf16[2560,256]{1,0:T(8,128)(2,1)} %collective-permute-done.19), channel_id=1, source_target_pairs={{8,16},{16,8},{9,17},{17,9},{10,18},{18,10},{11,19},{19,11},{12,20... | collective-permute-start | bytes 3932168 | tf_op jit(solution)/shard_map/ppermute | solution.py:198
  608.7 81.8 %collective-permute-start.25 = (bf16[112,128,128]{2,1,0:T(8,128)(2,1)}, bf16[112,128,128]{2,1,0:T(8,128)(2,1)}, u32[]{:S(2)}, u32[]{:S(2)}) collective-permute-start(bf16[112,128,128]{2,1,0:T(8,128)(2,1)} %collective-permute-done.10.source), channel_id=1, source_target_pairs={{0,8},{24,16},{1,9},{25,17},{2,10},{26,18},{3,11},{27,19},{4,12},{... | collective-permute-start | bytes 11010056 | tf_op jit(solution)/shard_map/ppermute | solution.py:198
  615.0 25.7 %collective-permute-start.56 = (bf16[2560,256]{1,0:T(8,128)(2,1)}, bf16[2560,256]{1,0:T(8,128)(2,1)}, u32[]{:S(2)}, u32[]{:S(2)}) collective-permute-start(bf16[2560,256]{1,0:T(8,128)(2,1)} %collective-permute-done.20), channel_id=1, source_target_pairs={{8,16},{16,8},{9,17},{17,9},{10,18},{18,10},{11,19},{19,11},{12,20... | collective-permute-start | bytes 3932168 | tf_op jit(solution)/shard_map/ppermute | solution.py:198
  640.2 12.1 %collective-permute-start.22 = (f32[64,1024]{1,0:T(8,128)}, f32[64,1024]{1,0:T(8,128)}, u32[]{:S(2)}, u32[]{:S(2)}) collective-permute-start(f32[64,1024]{1,0:T(8,128)} %constant_dynamic-slice_fusion.24), channel_id=1, source_target_pairs={{0,4},{4,0},{1,5},{5,1},{2,6},{6,2},{3,7},{7,3},{8,12},{12,8},{9,1... | collective-permute-start | bytes 786440 | tf_op jit(solution)/shard_map/ppermute | solution.py:186
  652.1 7.4 collective-permute-start.57
  654.0 108.7 %collective-permute-start.23 = (f32[32,1024]{1,0:T(8,128)}, f32[32,1024]{1,0:T(8,128)}, u32[]{:S(2)}, u32[]{:S(2)}) collective-permute-start(f32[32,1024]{1,0:T(8,128)} %constant_dynamic-slice_fusion.23), channel_id=1, source_target_pairs={{0,2},{2,0},{1,3},{3,1},{4,6},{6,4},{5,7},{7,5},{8,10},{10,8},{9,1... | collective-permute-start | bytes 393224 | tf_op jit(solution)/shard_map/ppermute | solution.py:186
  660.7 8.2 collective-permute-start.58
  669.6 83.5 %collective-permute-start.59 = (f32[32,1024]{1,0:T(8,128)}, f32[32,1024]{1,0:T(8,128)}, u32[]{:S(2)}, u32[]{:S(2)}) collective-permute-start(f32[32,1024]{1,0:T(8,128)} %constant_dynamic-slice_fusion.7), channel_id=1, source_target_pairs={{0,2},{2,0},{1,3},{3,1},{4,6},{6,4},{5,7},{7,5},{8,10},{10,8},{9,1... | collective-permute-start | bytes 393224 | tf_op jit(solution)/shard_map/ppermute | solution.py:186
  706.1 16.4 %collective-permute-start.60 = (f32[128,1024]{1,0:T(8,128)}, f32[128,1024]{1,0:T(8,128)}, u32[]{:S(2)}, u32[]{:S(2)}) collective-permute-start(f32[128,1024]{1,0:T(8,128)} %bitcast.291), channel_id=1, source_target_pairs={{0,1},{1,0},{2,3},{3,2},{4,5},{5,4},{6,7},{7,6},{8,9},{9,8},{10,11... | collective-permute-start | bytes 1572872 | tf_op jit(solution)/shard_map/ppermute | solution.py:186
  717.2 6.6 collective-permute-start.43
  723.8 9.2 %collective-permute-start.61 = (f32[64,1024]{1,0:T(8,128)S(1)}, f32[64,1024]{1,0:T(8,128)S(1)}, u32[]{:S(2)}, u32[]{:S(2)}) collective-permute-start(f32[64,1024]{1,0:T(8,128)S(1)} %constant_dynamic-slice_fusion.4), channel_id=1, source_target_pairs={{0,4},{4,0},{1,5},{5,1},{2,6},{6,2},{3,7},{7,3},{8,12},{12,8},{9,1... | collective-permute-start | bytes 786440 | tf_op jit(solution)/shard_map/ppermute | solution.py:186
  725.6 13.1 %collective-permute-start.44 = (f32[64,1024]{1,0:T(8,128)S(1)}, f32[64,1024]{1,0:T(8,128)S(1)}, u32[]{:S(2)}, u32[]{:S(2)}) collective-permute-start(f32[64,1024]{1,0:T(8,128)S(1)} %constant_dynamic-slice_fusion.12), channel_id=1, source_target_pairs={{0,4},{4,0},{1,5},{5,1},{2,6},{6,2},{3,7},{7,3},{8,12},{12,8},{9,1... | collective-permute-start | bytes 786440 | tf_op jit(solution)/shard_map/ppermute | solution.py:186
  733.0 10.7 %collective-permute-start.27 = (f32[64,1024]{1,0:T(8,128)S(1)}, f32[64,1024]{1,0:T(8,128)S(1)}, u32[]{:S(2)}, u32[]{:S(2)}) collective-permute-start(f32[64,1024]{1,0:T(8,128)S(1)} %constant_dynamic-slice_fusion.20), channel_id=1, source_target_pairs={{0,4},{4,0},{1,5},{5,1},{2,6},{6,2},{3,7},{7,3},{8,12},{12,8},{9,1... | collective-permute-start | bytes 786440 | tf_op jit(solution)/shard_map/ppermute | solution.py:186
  738.6 7.2 collective-permute-start.62
  750.1 8.9 collective-permute-start.63
  751.8 9.9 %collective-permute-start.46 = (f32[32,1024]{1,0:T(8,128)S(1)}, f32[32,1024]{1,0:T(8,128)S(1)}, u32[]{:S(2)}, u32[]{:S(2)}) collective-permute-start(f32[32,1024]{1,0:T(8,128)S(1)} %dynamic-slice_add_fusion.10), channel_id=1, source_target_pairs={{8,0},{16,24},{9,1},{17,25},{10,2},{18,26},{11,3},{19,27},{12,4},{... | collective-permute-start | bytes 393224 | tf_op jit(solution)/shard_map/ppermute | solution.py:351
  753.1 10.0 %collective-permute-start.29 = (f32[32,1024]{1,0:T(8,128)S(1)}, f32[32,1024]{1,0:T(8,128)S(1)}, u32[]{:S(2)}, u32[]{:S(2)}) collective-permute-start(f32[32,1024]{1,0:T(8,128)S(1)} %dynamic-slice_add_fusion.11), channel_id=1, source_target_pairs={{8,0},{16,24},{9,1},{17,25},{10,2},{18,26},{11,3},{19,27},{12,4},{... | collective-permute-start | bytes 393224 | tf_op jit(solution)/shard_map/ppermute | solution.py:351
  764.8 12.5 %collective-permute-start.64 = (f32[128,1024]{1,0:T(8,128)S(1)}, f32[128,1024]{1,0:T(8,128)S(1)}, u32[]{:S(2)}, u32[]{:S(2)}) collective-permute-start(f32[128,1024]{1,0:T(8,128)S(1)} %bitcast.287), channel_id=1, source_target_pairs={{0,8},{8,0},{16,24},{24,16},{1,9},{9,1},{17,25},{25,17},{2,10},{10... | collective-permute-start | bytes 1572872 | tf_op jit(solution)/shard_map/ppermute | solution.py:204
  764.9 14.1 %collective-permute-start.65 = (f32[128,1024]{1,0:T(8,128)S(1)}, f32[128,1024]{1,0:T(8,128)S(1)}, u32[]{:S(2)}, u32[]{:S(2)}) collective-permute-start(f32[128,1024]{1,0:T(8,128)S(1)} %bitcast.288), channel_id=1, source_target_pairs={{8,16},{16,8},{9,17},{17,9},{10,18},{18,10},{11,19},{19,11},{12,20... | collective-permute-start | bytes 1572872 | tf_op jit(solution)/shard_map/ppermute | solution.py:205
  779.0 14.7 %collective-permute-start.66 = (f32[128,1024]{1,0:T(8,128)S(1)}, f32[128,1024]{1,0:T(8,128)S(1)}, u32[]{:S(2)}, u32[]{:S(2)}) collective-permute-start(f32[128,1024]{1,0:T(8,128)S(1)} %collective-permute-done.65), channel_id=1, source_target_pairs={{8,0},{16,24},{9,1},{17,25},{10,2},{18,26},{11,3},{19,27},{12,4},{... | collective-permute-start | bytes 1572872 | tf_op jit(solution)/shard_map/ppermute | solution.py:207
  782.4 21.9 %collective-permute-start.68 = (f32[128,1024]{1,0:T(8,128)S(1)}, f32[128,1024]{1,0:T(8,128)S(1)}, u32[]{:S(2)}, u32[]{:S(2)}) collective-permute-start(f32[128,1024]{1,0:T(8,128)S(1)} %collective-permute-done.67), channel_id=1, source_target_pairs={{8,0},{16,24},{9,1},{17,25},{10,2},{18,26},{11,3},{19,27},{12,4},{... | collective-permute-start | bytes 1572872 | tf_op jit(solution)/shard_map/ppermute | solution.py:208
  818.0 14.7 %collective-permute-start.70 = (f32[1,2,1,4,136,128]{5,4,3,2,1,0:T(8,128)S(1)}, f32[1,2,1,4,136,128]{5,4,3,2,1,0:T(8,128)S(1)}, u32[]{:S(2)}, u32[]{:S(2)}) collective-permute-start(f32[1,2,1,4,136,128]{5,4,3,2,1,0:T(8,128)S(1)} %constant_dynamic-slice_fusion.1), channel_id=1, source_target_pairs={{0,4},{4,0},{1,5},{5,1},{2,6},{6,2},{3,7},{7,3},{8,12},{12,8},{9,1... | collective-permute-start | bytes 1671176 | tf_op jit(solution)/shard_map/ppermute | solution.py:186
  832.9 45.2 %collective-permute-start.71 = (f32[1,1,1,4,136,128]{5,4,3,2,1,0:T(8,128)S(1)}, f32[1,1,1,4,136,128]{5,4,3,2,1,0:T(8,128)S(1)}, u32[]{:S(2)}, u32[]{:S(2)}) collective-permute-start(f32[1,1,1,4,136,128]{5,4,3,2,1,0:T(8,128)S(1)} %constant_dynamic-slice_fusion), channel_id=1, source_target_pairs={{0,2},{2,0},{1,3},{3,1},{4,6},{6,4},{5,7},{7,5},{8,10},{10,8},{9,1... | collective-permute-start | bytes 835592 | tf_op jit(solution)/shard_map/ppermute | solution.py:186
  (117 other events, 1685.8 us)

commit v4 on v3

--- a/solution.py
+++ b/solution.py
@@ -19,7 +19,7 @@
 SOURCE = np.array([[0, 1, 2, 3], [1, 0, 2, 3], [2, 3, 1, 0], [3, 2, 1, 0]], np.int32)
 PLACE = np.argsort(SOURCE, axis=1).astype(np.int32)
 
-LENT = (5, 16)
+LENT = (9, 32)
 
 
 def bounds(total, parts):
@@ -136,22 +136,22 @@
     )(info, source)
 
 
-def dots_kernel(blk, count, ids, blocks, out):
-    rest = jnp.zeros((out.shape[1] - blk - 2, blk), jnp.float32)
+def dots_kernel(blk, count, depth, ids, blocks, out):
+    flag = jnp.sum(blocks[:, depth : depth + 1, :blk], axis=0)
+    rest = jnp.zeros((out.shape[1] - blk - 3, blk), jnp.float32)
 
     def one(k, carry):
         def side(which):
             start = pl.multiple_of(ids[which, 1, k] * blk, blk)
-            return blocks[ids[which, 0, k], :, pl.ds(start, blk)]
+            return blocks[ids[which, 0, k], :depth, pl.ds(start, blk)]
 
         left, right = side(0), side(1)
         out[k, :blk, :] = lax.dot_general(
             left, right, (((0,), (0,)), ((), ())),
             precision=lax.Precision.HIGHEST, preferred_element_type=jnp.float32,
         )
-        out[k, blk:, :] = jnp.concatenate(
-            [jnp.sum(left * left, axis=0, keepdims=True), jnp.sum(right * right, axis=0, keepdims=True), rest]
-        )
+        squares = [jnp.sum(v * v, axis=0, keepdims=True) for v in (left, right)]
+        out[k, blk:, :] = jnp.concatenate(squares + [flag, rest])
         return carry
 
     lax.fori_loop(0, count, one, 0)
@@ -160,7 +160,7 @@
 def pair_dots(blocks, ids, blk):
     count = ids.shape[2]
     return pl.pallas_call(
-        functools.partial(dots_kernel, blk, count),
+        functools.partial(dots_kernel, blk, count, blocks.shape[1] - 8),
         out_shape=jax.ShapeDtypeStruct((count, blk + 8, blk), jnp.float32),
         in_specs=[pl.BlockSpec(memory_space=pltpu.SMEM), pl.BlockSpec(memory_space=pltpu.VMEM)],
         out_specs=pl.BlockSpec(memory_space=pltpu.VMEM),
@@ -187,14 +187,20 @@
     return total
 
 
+def after(values, arrived):
+    return lax.optimization_barrier((values, arrived))[0]
+
+
 class Lane:
     def __init__(self, depth):
         self.depth = depth
         self.arrived = []
 
-    def send(self, values, axis, pairs):
+    def send(self, values, axis, pairs, later=None):
         if len(self.arrived) >= self.depth:
-            values, _ = lax.optimization_barrier((values, self.arrived[-self.depth]))
+            values = after(values, self.arrived[-self.depth])
+        if later is not None:
+            values = after(values, later)
         got = lax.ppermute(values, axis, pairs)
         self.arrived.append(got)
         return got
@@ -262,31 +268,73 @@
     masks = [mask_of(x)] + [lax.ppermute(mask_of((x + k) % wide), "x", turn(wide, k)) for k in range(1, wide)]
     guest_masks = lax.ppermute(jnp.stack([m[:, kept:] for m in masks]), "z", INWARD)
 
-    over_x, ends, middle, ends_out = Lane(2), Lane(1), Lane(2), Lane(2)
+    over_x, inward, outward, middle = Lane(1), Lane(2), Lane(1), Lane(2)
 
     def planes_of(owner, c):
         return lax.dynamic_slice_in_dim(planes, (owner * columns + cuts[c]) * blk, widths[c] * blk, 0)
 
-    def group(c):
-        whole = jnp.zeros((widths[c] * blk, wide * own_planes), planes.dtype)
-        whole = lax.dynamic_update_slice_in_dim(whole, planes_of(x, c), x * own_planes, 1)
-        for k in range(1, wide):
-            part = over_x.send(planes_of((x + k) % wide, c), "x", turn(wide, k))
-            whole = lax.dynamic_update_slice_in_dim(whole, part, ((x - k) % wide) * own_planes, 1)
-        return whole
-
-    def tiles_of(name):
+    def planes_over_x(first, last):
+        def part(owner):
+            start = (owner * columns + cuts[first]) * blk
+            return lax.dynamic_slice_in_dim(planes, start, (cuts[last] - cuts[first]) * blk, 0)
+
+        got = [over_x.send(part((x + k) % wide), "x", turn(wide, k)) for k in range(1, wide)]
+        groups = []
+        for c in range(first, last):
+            whole = jnp.zeros((widths[c] * blk, wide * own_planes), planes.dtype)
+            whole = lax.dynamic_update_slice_in_dim(whole, planes_of(x, c), x * own_planes, 1)
+            for k in range(1, wide):
+                rows_of = slice((cuts[c] - cuts[first]) * blk, (cuts[c + 1] - cuts[first]) * blk)
+                whole = lax.dynamic_update_slice_in_dim(
+                    whole, got[k - 1][rows_of], ((x - k) % wide) * own_planes, 1
+                )
+            groups.append(whole)
+        return groups
+
+    def tiles_of(name, later):
         low, high = (cuts[c] for c in streams[name])
         slots = room((high - low) * row_blocks)
         got = []
         for k in range(1, wide):
             owner = (x + k) % wide
-            tiles = pack(hist, mask_of(owner)[:, low:high], owner * columns + low, slots)
+            mask = after(mask_of(owner)[:, low:high], later)
+            tiles = pack(hist, mask, owner * columns + low, slots)
             got.append(over_x.send(tiles, "x", turn(wide, k)))
         return got
 
-    groups = [group(c) for c in range(6)]
-    tiles = {name: tiles_of(name) for name in ("early", "lent", "late")}
+    groups = planes_over_x(0, 1)
+    groups += planes_over_x(1, 2)
+    groups += planes_over_x(2, 4)
+    tiles = {"early": tiles_of("early", groups[0])}
+    groups += planes_over_x(4, 6)
+    tiles["lent"] = tiles_of("lent", groups[1])
+    tiles["late"] = tiles_of("late", groups[2])
+
+    near, mid, far = {}, {}, {}
+    for c in range(4):
+        near[c] = inward.send(groups[c], "z", NEAR)
+        mid[c] = middle.send(groups[c], "z", MIDDLE)
+    inward.depth = 1
+    outward.arrived = [near[3]]
+    own_tiles = pack(hist, after(masks[0], groups[3])[:, kept:], x * columns + kept, room(lent * row_blocks))
+    lent_tiles = [inward.send(own_tiles, "z", INWARD)]
+    for c in range(4):
+        far[c] = middle.send(near[c], "z", MIDDLE)
+    for c in (4, 5):
+        near[c] = inward.send(groups[c], "z", INWARD)
+    for c in (4, 5):
+        mid[c] = middle.send(groups[c], "z", MIDDLE)
+    for c in (4, 5):
+        far[c] = middle.send(near[c], "z", MIDDLE)
+    out1 = [outward.send(mid[c], "z", OUTWARD) for c in range(4)]
+    out2 = [outward.send(far[c], "z", OUTWARD) for c in range(4)]
+    lent_tiles += [inward.send(t, "z", INWARD) for t in tiles["lent"]]
+    held = []
+    for c in range(6):
+        if c < 4:
+            held.append([groups[c], near[c], jnp.where(inner, mid[c], out1[c]), jnp.where(inner, far[c], out2[c])])
+        else:
+            held.append([groups[c], near[c], mid[c], far[c]])
 
     over = jnp.int32(0)
     sessions = [[None] * 6 for _ in range(wide)]
@@ -299,61 +347,49 @@
         for k in range(wide):
             mask = masks[k][:, low:high]
             if k == 0:
-                sessions[k][first:last] = spread(hist, mask, x * columns + low, parts)
+                later = groups[3] if name == "early" else near[0] if name == "lent" else near[1]
+                sessions[k][first:last] = spread(hist, after(mask, later), x * columns + low, parts)
             else:
                 sessions[k][first:last] = spread(tiles[name][k - 1], mask, None, parts)
-
-    near, mid, far = {}, {}, {}
-    for c in range(4):
-        near[c] = ends.send(groups[c], "z", NEAR)
-    own_tiles = pack(hist, masks[0][:, kept:], x * columns + kept, room(lent * row_blocks))
-    lent_tiles = [ends.send(own_tiles, "z", INWARD)]
-    for c in (4, 5):
-        near[c] = ends.send(groups[c], "z", INWARD)
-    for c in range(6):
-        mid[c] = middle.send(groups[c], "z", MIDDLE)
-    for c in range(6):
-        far[c] = middle.send(near[c], "z", MIDDLE)
-    held = [None] * 6
-    out1 = [ends_out.send(mid[c], "z", OUTWARD) for c in range(4)]
-    lent_tiles += [ends.send(t, "z", INWARD) for t in tiles["lent"]]
-    out2 = [ends_out.send(far[c], "z", OUTWARD) for c in range(4)]
-    for c in range(6):
-        if c < 4:
-            held[c] = [groups[c], near[c], jnp.where(inner, mid[c], out1[c]), jnp.where(inner, far[c], out2[c])]
-        else:
-            held[c] = [groups[c], near[c], mid[c], far[c]]
     guests = [
         spread(t, guest_masks[k], None, tuple(widths[4:])) for k, t in enumerate(lent_tiles)
     ]
 
-    order = (x - jnp.arange(wide)) % wide
-
-    def summed(terms):
-        totals = []
-        for source in terms:
-            total = None
-            for a, b in source:
-                one = jnp.dot(a, b, preferred_element_type=jnp.float32)
-                total = one if total is None else total + one
-            totals.append(total)
-        whole = jnp.stack(totals)[order].reshape(wide * rows, wide * own_planes).T
-        for axis in ("core", "x", "y"):
-            whole = scatter_sum(whole, axis, 0)
-        return whole
-
-    shares = []
-    for s in range(DEPTH):
-        share = summed([[(sessions[k][c], held[c][s]) for c in range(6)] for k in range(wide)])
-        if s > 0:
-            t = 0 if s == 1 else s
-            guest = summed([[(guests[k][c - 4], held[c][t]) for c in (4, 5)] for k in range(wide)])
-            share = share + lax.ppermute(guest, "z", OUTWARD)
-        shares.append(share)
-    proj = jnp.stack(shares)[jnp.asarray(PLACE)[z]].reshape(-1, wide * rows)
+    def total(sources, chunks, s):
+        found = []
+        for source in sources:
+            one = None
+            for c in chunks:
+                term = jnp.dot(source[c], held[c][s], preferred_element_type=jnp.float32)
+                one = term if one is None else one + term
+            found.append(one)
+        rows_in_order = []
+        for owner in range(wide):
+            part = found[0]
+            for k in range(1, wide):
+                part = jnp.where((x - owner) % wide == k, found[k], part)
+            rows_in_order.append(part)
+        return jnp.concatenate(rows_in_order)
+
+    def summed(totals):
+        whole = scatter_sum(jnp.stack(totals), "core", 2)
+        whole = jnp.swapaxes(whole, 1, 2)
+        return scatter_sum(scatter_sum(whole, "x", 1), "y", 1)
+
+    every = range(6)
+    first_three = summed([total(sessions, every, s) for s in range(3)])
+    guest_chunks = [{4: g[0], 5: g[1]} for g in guests]
+    visitors = summed([total(guest_chunks, (4, 5), s) for s in (0, 2, 3)])
+    visitors = lax.ppermute(visitors, "z", OUTWARD)
+    last_one = summed([total(sessions, every, 3)])
+    shares = jnp.concatenate([first_three, last_one]) + jnp.concatenate([jnp.zeros_like(last_one), visitors])
+    proj = shares[jnp.asarray(PLACE)[z]].reshape(-1, wide * rows)
+    flags = jnp.full((8, proj.shape[1]), over.astype(jnp.float32))
+    proj = jnp.concatenate([proj, flags])
 
     blocks = jnp.stack(along_line(proj, inner))
     got = [pairs] + [lax.ppermute(pairs, "x", turn(wide, k)) for k in range(1, wide)]
+    order = (x - jnp.arange(wide)) % wide
     all_pairs = jnp.stack(got)[order].reshape(-1, 2).T
     plane_blocks = wide * row_blocks
     ids = jnp.stack([jnp.asarray(PLACE)[z][all_pairs // plane_blocks], all_pairs % plane_blocks], axis=1)
@@ -365,9 +401,8 @@
     own = sums.reshape((-1,) + sums.shape[4:])
     scale = lax.rsqrt(own[:, blk : blk + 2] / P_SIZE + 1e-06)
     scores = own[:, :blk] / P_SIZE * scale[:, 0, :, None] * scale[:, 1, None, :]
-
-    over = lax.pmax(over, ("z", "x", "y", "core"))
-    return lax.cond(over > 0, lambda: dense(hist, tile_mask, planes, pairs), lambda: scores)
+    crowded = own[0, blk + 2, 0] > 0
+    return lax.cond(crowded, lambda: dense(hist, tile_mask, planes, pairs), lambda: scores)
 
 
 def solution(mesh):

time: 900 us -> 754 us (0.84)
  waiting for transfers between devices: 413 us -> 252 us
  starting transfers between devices: 128 us -> 206 us
  local copies, waits for them, and re-layouts: 101 us -> 60.1 us
  blocking collectives: 38.6 us -> 0 us
  matrix products: 114 us -> 139 us
    ppermute x37 -> x35, waiting for transfers between devices: 326 us -> 131 us  [send(): got = lax.ppermute(values, axis, pairs)]
    ppermute x37 -> x35, starting transfers between devices: 94.4 us -> 151 us  [send(): got = lax.ppermute(values, axis, pairs)]
    pmax x1 -> x0, blocking collectives: 38.6 us -> none  [body(): over = lax.pmax(over, ('z', 'x', 'y', 'core'))]
    ppermute x1, starting transfers between devices: 3.6 us -> 34.3 us  [body(): lax.ppermute(jnp.stack([m[:, kept:] for m in masks]), 'z', INWARD)]
    dot_general x60, matrix products: 114 us -> 139 us  [total(): term = jnp.dot(source[c], held[c][s], preferred_element_type=jnp.float32)]
    unnamed x232 -> x170, local copies, waits for them, and re-layouts: 39.1 us -> 14.8 us
    ppermute x1, waiting for transfers between devices: 0.01 us -> 19.6 us  [body(): lax.ppermute(jnp.stack([m[:, kept:] for m in masks]), 'z', INWARD)]
    ppermute x24 -> x12, waiting for transfers between devices: 47.4 us -> 65.9 us  [scatter_sum(): total = total + lax.ppermute(part((here + k) % count), axis, turn(count, k))]
  transfers between devices with their start and end apart: 72 -> 56, of which waited for: 34 -> 23; matrix products, arithmetic and copies ran while one was open for 24% -> 26% of each run, Pallas kernels for 4% -> 5%
where the time goes in v4:
time: 754 us; the launch traced here: 741 us
  waiting for transfers between devices  252 us (33%)
  starting transfers between devices  206 us (27%)
  matrix products  139 us (18%)
  local copies, waits for them, and re-layouts  60.1 us (8%)
  Pallas kernels  49.2 us (7%)
  between operations  19.8 us (3%)
  other arithmetic  15.7 us (2%)
    ppermute x35, starting transfers between devices, send(): got = lax.ppermute(values, axis, pairs)  151 us
    dot_general x60, matrix products, total(): term = jnp.dot(source[c], held[c][s], preferred_element_type=jnp.float32)  139 us
    ppermute x35, waiting for transfers between devices, send(): got = lax.ppermute(values, axis, pairs)  131 us
    ppermute x12, waiting for transfers between devices, scatter_sum(): total = total + lax.ppermute(part((here + k) % count), axis, turn(count, k))  65.9 us
    ppermute x1, starting transfers between devices, body(): lax.ppermute(jnp.stack([m[:, kept:] for m in masks]), 'z', INWARD)  34.3 us
    pallas_call x8, Pallas kernels, spread(): pl.pallas_call(functools.partial(spread_kernel, blk, row_blocks, parts, s...  28 us
    ppermute x1, waiting for transfers between devices, body(): lax.ppermute(jnp.stack([m[:, kept:] for m in masks]), 'z', INWARD)  19.6 us
  transfers between devices with their start and end apart: 56, of which 23 were waited for; matrix products, arithmetic and copies ran while one was open for 26% of the time, Pallas kernels for 5%

profile of v4, /device:TPU:0, one launch (start us, length us, event | category | flops | bytes accessed | tf_op | source)
XLA Modules:
  0.0 741.3 jit_solution(14186023033435272549)
XLA Ops:
  6.7 3.0 dynamic-slice_dynamic-update-slice_fusion.1
  9.6 2.9 collective-permute-start.2
  22.8 6.9 collective-permute-done.2
  33.0 15.0 %collective-permute-done.3 = bf16[2944,128]{1,0:T(8,128)(2,1)} collective-permute-done((bf16[2944,128]{1,0:T(8,128)(2,1)}, bf16[2944,128]{1,0:T(8,128)(2,1)}, u32[]{:S(2)}, u32[]{:S(2)}) %collective-permute-start.3) | collective-permute-done | bytes 753696 | tf_op jit(solution)/shard_map/ppermute | solution.py:204
  65.5 15.8 %collective-permute-done.4 = bf16[5888,128]{1,0:T(8,128)(2,1)S(1)} collective-permute-done((bf16[5888,128]{1,0:T(8,128)(2,1)S(1)}, bf16[5888,128]{1,0:T(8,128)(2,1)S(1)}, u32[]{:S(2)}, u32[]{:S(2)}) %collective-permute-start.4) | collective-permute-done | bytes 1507360 | tf_op jit(solution)/shard_map/ppermute | solution.py:204
  82.4 5.6 collective-permute-done.9
  91.5 4.6 pack_tiles.4
  97.6 34.3 %collective-permute-start.42 = (s32[2,4,36]{2,1,0:T(4,128)S(1)}, s32[2,4,36]{2,1,0:T(4,128)S(1)}, u32[]{:S(2)}, u32[]{:S(2)}) collective-permute-start(s32[2,4,36]{2,1,0:T(4,128)S(1)} %pad_add_fusion), channel_id=1, source_target_pairs={{0,8},{24,16},{1,9},{25,17},{2,10},{26,18},{3,11},{27,19},{4,12},{... | collective-permute-start | bytes 3464 | tf_op jit(solution)/shard_map/ppermute | solution.py:269
  131.9 19.6 %collective-permute-done.42 = s32[2,4,36]{2,1,0:T(4,128)S(1)} collective-permute-done((s32[2,4,36]{2,1,0:T(4,128)S(1)}, s32[2,4,36]{2,1,0:T(4,128)S(1)}, u32[]{:S(2)}, u32[]{:S(2)}) %collective-permute-start.42) | collective-permute-done | bytes 1184 | tf_op jit(solution)/shard_map/ppermute | solution.py:269
  161.7 3.0 spread_tiles.13
  167.8 6.1 collective-permute-start.11
  178.7 3.5 spread_tiles.12
  183.8 3.4 spread_tiles.11
  189.1 3.5 fusion.65
  198.2 3.2 fusion.63
  201.4 3.2 fusion.73
  204.6 18.6 %collective-permute-done.11 = bf16[2944,256]{1,0:T(8,128)(2,1)} collective-permute-done((bf16[2944,256]{1,0:T(8,128)(2,1)}, bf16[2944,256]{1,0:T(8,128)(2,1)}, u32[]{:S(2)}, u32[]{:S(2)}) %collective-permute-start.11) | collective-permute-done | bytes 1507360 | tf_op jit(solution)/shard_map/ppermute | solution.py:204
  224.6 2.9 pack_tiles.5
  227.5 3.2 fusion.75
  230.7 3.2 fusion.74
  238.2 3.6 spread_tiles.8
  241.8 4.3 fusion.58
  246.1 3.4 fusion.68
  249.5 11.4 %collective-permute-done.19 = bf16[2944,256]{1,0:T(8,128)(2,1)S(1)} collective-permute-done((bf16[2944,256]{1,0:T(8,128)(2,1)}, bf16[2944,256]{1,0:T(8,128)(2,1)S(1)}, u32[]{:S(2)}, u32[]{:S(2)}) %collective-permute-start.19) | collective-permute-done | bytes 1507360 | tf_op jit(solution)/shard_map/ppermute | solution.py:204
  265.0 10.0 %collective-permute-done.13.source = bf16[104,128,128]{2,1,0:T(8,128)(2,1)S(1)} collective-permute-done((bf16[104,128,128]{2,1,0:T(8,128)(2,1)S(1)}, bf16[104,128,128]{2,1,0:T(8,128)(2,1)S(1)}, u32[]{:S(2)}, u32[]{:S(2)}) %collective-permute-start.13) | collective-permute-done | bytes 3407904 | tf_op jit(solution)/shard_map/ppermute | solution.py:204
  275.0 3.1 spread_tiles.15
  278.1 3.3 slice_dynamic-update-slice_fusion.3
  281.4 42.1 %collective-permute-start.14 = (bf16[2304,256]{1,0:T(8,128)(2,1)}, bf16[2304,256]{1,0:T(8,128)(2,1)}, u32[]{:S(2)}, u32[]{:S(2)}) collective-permute-start(bf16[2304,256]{1,0:T(8,128)(2,1)} %get-tuple-element.135), channel_id=1, source_target_pairs={{0,8},{24,16},{1,9},{25,17},{2,10},{26,18},{3,11},{27,19},{4,12},{... | collective-permute-start | bytes 3538952 | tf_op jit(solution)/shard_map/ppermute | solution.py:204
  327.3 2.9 fusion.67
  332.3 3.0 convolution_add_fusion.4
  335.4 3.0 fusion.66
  338.4 3.3 fusion.11
  343.0 3.3 fusion.38
  346.3 34.3 %collective-permute-start.15 = (bf16[2304,256]{1,0:T(8,128)(2,1)}, bf16[2304,256]{1,0:T(8,128)(2,1)}, u32[]{:S(2)}, u32[]{:S(2)}) collective-permute-start(bf16[2304,256]{1,0:T(8,128)(2,1)} %get-tuple-element.138), channel_id=1, source_target_pairs={{0,8},{24,16},{1,9},{25,17},{2,10},{26,18},{3,11},{27,19},{4,12},{... | collective-permute-start | bytes 3538952 | tf_op jit(solution)/shard_map/ppermute | solution.py:204
  390.5 4.9 collective-permute-done.23
  404.3 3.3 fusion.19
  410.7 23.9 %collective-permute-start.43 = (bf16[104,128,128]{2,1,0:T(8,128)(2,1)S(1)}, bf16[104,128,128]{2,1,0:T(8,128)(2,1)S(1)}, u32[]{:S(2)}, u32[]{:S(2)}) collective-permute-start(bf16[104,128,128]{2,1,0:T(8,128)(2,1)S(1)} %collective-permute-done.7.source), channel_id=1, source_target_pairs={{0,8},{24,16},{1,9},{25,17},{2,10},{26,18},{3,11},{27,19},{4,12},{... | collective-permute-start | bytes 10223624 | tf_op jit(solution)/shard_map/ppermute | solution.py:204
  434.7 3.6 spread_tiles.10
  438.3 3.7 fusion.62
  442.0 3.0 fusion.61
  446.6 3.0 fusion.79
  452.8 3.0 fusion.72
  455.9 3.0 fusion.71
  461.9 20.8 %collective-permute-done.34 = bf16[2944,256]{1,0:T(8,128)(2,1)S(1)} collective-permute-done((bf16[2944,256]{1,0:T(8,128)(2,1)S(1)}, bf16[2944,256]{1,0:T(8,128)(2,1)S(1)}, u32[]{:S(2)}, u32[]{:S(2)}) %collective-permute-start.34) | collective-permute-done | bytes 1507360 | tf_op jit(solution)/shard_map/ppermute | solution.py:204
  483.9 2.9 fusion.85
  486.8 3.1 fusion.83
  493.6 22.2 %collective-permute-done.35 = bf16[2944,256]{1,0:T(8,128)(2,1)S(1)} collective-permute-done((bf16[2944,256]{1,0:T(8,128)(2,1)}, bf16[2944,256]{1,0:T(8,128)(2,1)S(1)}, u32[]{:S(2)}, u32[]{:S(2)}) %collective-permute-start.35) | collective-permute-done | bytes 1507360 | tf_op jit(solution)/shard_map/ppermute | solution.py:204
  518.9 3.1 spread_tiles.14
  535.3 4.8 spread_tiles.9
  568.0 2.6 fusion.47
  570.6 2.8 fusion.35
  573.5 2.6 broadcast_select_fusion.27
  596.6 19.8 %collective-permute-done.40 = f32[1,64,1024]{1,2,0:T(8,128)} collective-permute-done((f32[1,64,1024]{1,2,0:T(8,128)}, f32[1,64,1024]{1,2,0:T(8,128)}, u32[]{:S(2)}, u32[]{:S(2)}) %collective-permute-start.40) | collective-permute-done | bytes 262176 | tf_op jit(solution)/shard_map/ppermute | solution.py:186
  621.5 11.1 %collective-permute-done.31 = f32[3,64,1024]{2,1,0:T(8,128)} collective-permute-done((f32[3,64,1024]{2,1,0:T(8,128)}, f32[3,64,1024]{2,1,0:T(8,128)}, u32[]{:S(2)}, u32[]{:S(2)}) %collective-permute-start.31) | collective-permute-done | bytes 786464 | tf_op jit(solution)/shard_map/ppermute | solution.py:186
  636.7 5.8 collective-permute-done.41
  642.8 5.8 collective-permute-done.32
  651.6 3.6 collective-permute-start.48
  655.9 10.0 %collective-permute-done.48 = f32[136,1024]{1,0:T(8,128)S(1)} collective-permute-done((f32[136,1024]{1,0:T(8,128)S(1)}, f32[136,1024]{1,0:T(8,128)S(1)}, u32[]{:S(2)}, u32[]{:S(2)}) %collective-permute-start.48) | collective-permute-done | bytes 557088 | tf_op jit(solution)/shard_map/ppermute | solution.py:210
  673.2 13.5 %collective-permute-done.50 = f32[136,1024]{1,0:T(8,128)S(1)} collective-permute-done((f32[136,1024]{1,0:T(8,128)S(1)}, f32[136,1024]{1,0:T(8,128)S(1)}, u32[]{:S(2)}, u32[]{:S(2)}) %collective-permute-start.50) | collective-permute-done | bytes 557088 | tf_op jit(solution)/shard_map/ppermute | solution.py:213
  686.7 8.9 %collective-permute-done.52 = f32[136,1024]{1,0:T(8,128)S(1)} collective-permute-done((f32[136,1024]{1,0:T(8,128)S(1)}, f32[136,1024]{1,0:T(8,128)S(1)}, u32[]{:S(2)}, u32[]{:S(2)}) %collective-permute-start.52) | collective-permute-done | bytes 557088 | tf_op jit(solution)/shard_map/ppermute | solution.py:214
  695.9 9.0 %pair_dots.1 = f32[32,136,128]{2,1,0:T(8,128)S(1)} custom-call(s32[2,2,32]{2,1,0:T(2,128)S(1)} %pad_add_fusion.2.ids, f32[4,136,1024]{2,1,0:T(8,128)S(1)} %pad_maximum_fusion.2.blocks), custom_call_target="tpu_custom_call" | custom-call | tf_op jit(solution)/shard_map/pair_dots/pallas_call | solution.py:162
  705.1 2.9 collective-permute-done.53
  709.9 14.2 %collective-permute-done.54 = f32[1,2,1,4,136,128]{5,4,3,2,1,0:T(8,128)S(1)} collective-permute-done((f32[1,2,1,4,136,128]{5,4,3,2,1,0:T(8,128)S(1)}, f32[1,2,1,4,136,128]{5,4,3,2,1,0:T(8,128)S(1)}, u32[]{:S(2)}, u32[]{:S(2)}) %collective-permute-start.54) | collective-permute-done | bytes 557088 | tf_op jit(solution)/shard_map/ppermute | solution.py:186
  725.9 6.3 collective-permute-done.55
  (417 shorter events, 202.3 us)
Async XLA Ops:
  9.6 20.1 %collective-permute-start.2 = (bf16[2944,128]{1,0:T(8,128)(2,1)}, bf16[2944,128]{1,0:T(8,128)(2,1)}, u32[]{:S(2)}, u32[]{:S(2)}) collective-permute-start(bf16[2944,128]{1,0:T(8,128)(2,1)} %get-tuple-element.187), channel_id=1, source_target_pairs={{0,4},{4,0},{1,5},{5,1},{2,6},{6,2},{3,7},{7,3},{8,12},{12,8},{9,1... | collective-permute-start | bytes 2261000 | tf_op jit(solution)/shard_map/ppermute | solution.py:204
  12.6 77.0 %copy-start.75 = (s32[4,256]{1,0:T(4,128)}, s32[4,256]{1,0:T(4,128)S(1)}, u32[]{:S(2)}) copy-start(s32[4,256]{1,0:T(4,128)S(1)} %compare_convert_fusion.1) | copy-start | bytes 12292
  12.6 78.3 %collective-permute-start.1 = (s32[4,128]{1,0:T(4,128)S(1)}, s32[4,128]{1,0:T(4,128)S(1)}, u32[]{:S(2)}, u32[]{:S(2)}) collective-permute-start(s32[4,128]{1,0:T(4,128)S(1)} %get-tuple-element.213), channel_id=1, source_target_pairs={{0,4},{4,0},{1,5},{5,1},{2,6},{6,2},{3,7},{7,3},{8,12},{12,8},{9,1... | collective-permute-start | bytes 6152 | tf_op jit(solution)/shard_map/ppermute | solution.py:268
  29.7 18.3 %collective-permute-start.3 = (bf16[2944,128]{1,0:T(8,128)(2,1)}, bf16[2944,128]{1,0:T(8,128)(2,1)}, u32[]{:S(2)}, u32[]{:S(2)}) collective-permute-start(bf16[2944,128]{1,0:T(8,128)(2,1)} %get-tuple-element.98), channel_id=1, source_target_pairs={{0,4},{4,0},{1,5},{5,1},{2,6},{6,2},{3,7},{7,3},{8,12},{12,8},{9,1... | collective-permute-start | bytes 2261000 | tf_op jit(solution)/shard_map/ppermute | solution.py:204
  48.1 33.2 %collective-permute-start.4 = (bf16[5888,128]{1,0:T(8,128)(2,1)S(1)}, bf16[5888,128]{1,0:T(8,128)(2,1)S(1)}, u32[]{:S(2)}, u32[]{:S(2)}) collective-permute-start(bf16[5888,128]{1,0:T(8,128)(2,1)S(1)} %constant_dynamic-slice_fusion.11), channel_id=1, source_target_pairs={{0,4},{4,0},{1,5},{5,1},{2,6},{6,2},{3,7},{7,3},{8,12},{12,8},{9,1... | collective-permute-start | bytes 4521992 | tf_op jit(solution)/shard_map/ppermute | solution.py:204
  54.9 33.2 %collective-permute-start.9 = (bf16[2944,256]{1,0:T(8,128)(2,1)}, bf16[2944,256]{1,0:T(8,128)(2,1)}, u32[]{:S(2)}, u32[]{:S(2)}) collective-permute-start(bf16[2944,256]{1,0:T(8,128)(2,1)} %constant_dynamic-update-slice_fusion), channel_id=1, source_target_pairs={{0,8},{8,0},{16,24},{24,16},{1,9},{9,1},{17,25},{25,17},{2,10},{10... | collective-permute-start | bytes 4521992 | tf_op jit(solution)/shard_map/ppermute | solution.py:204
  61.9 28.6 %copy-start.25 = (bf16[2944,256]{1,0:T(8,128)(2,1)}, bf16[2944,256]{1,0:T(8,128)(2,1)S(1)}, u32[]{:S(2)}) copy-start(bf16[2944,256]{1,0:T(8,128)(2,1)S(1)} %constant_dynamic-update-slice_fusion.1) | copy-start | bytes 4521988
  61.9 92.2 %collective-permute-start.16 = (bf16[2944,256]{1,0:T(8,128)(2,1)S(1)}, bf16[2944,256]{1,0:T(8,128)(2,1)}, u32[]{:S(2)}, u32[]{:S(2)}) collective-permute-start(bf16[2944,256]{1,0:T(8,128)(2,1)S(1)} %constant_dynamic-update-slice_fusion.1), channel_id=1, source_target_pairs={{8,16},{16,8},{9,17},{17,9},{10,18},{18,10},{11,19},{19,11},{12,20... | collective-permute-start | bytes 4521992 | tf_op jit(solution)/shard_map/ppermute | solution.py:204
  63.7 33.9 %collective-permute-start.18 = (bf16[2944,256]{1,0:T(8,128)(2,1)}, bf16[2944,256]{1,0:T(8,128)(2,1)}, u32[]{:S(2)}, u32[]{:S(2)}) collective-permute-start(bf16[2944,256]{1,0:T(8,128)(2,1)} %constant_dynamic-update-slice_fusion), channel_id=1, source_target_pairs={{8,16},{16,8},{9,17},{17,9},{10,18},{18,10},{11,19},{19,11},{12,20... | collective-permute-start | bytes 4521992 | tf_op jit(solution)/shard_map/ppermute | solution.py:204
  88.0 67.8 %collective-permute-start.12 = (bf16[2944,256]{1,0:T(8,128)(2,1)}, bf16[2944,256]{1,0:T(8,128)(2,1)}, u32[]{:S(2)}, u32[]{:S(2)}) collective-permute-start(bf16[2944,256]{1,0:T(8,128)(2,1)} %get-tuple-element.131), channel_id=1, source_target_pairs={{0,8},{8,0},{16,24},{24,16},{1,9},{9,1},{17,25},{25,17},{2,10},{10... | collective-permute-start | bytes 4521992 | tf_op jit(solution)/shard_map/ppermute | solution.py:204
  90.4 70.9 %collective-permute-start.10 = (bf16[2944,256]{1,0:T(8,128)(2,1)S(1)}, bf16[2944,256]{1,0:T(8,128)(2,1)}, u32[]{:S(2)}, u32[]{:S(2)}) collective-permute-start(bf16[2944,256]{1,0:T(8,128)(2,1)S(1)} %constant_dynamic-update-slice_fusion.1), channel_id=1, source_target_pairs={{0,8},{8,0},{16,24},{24,16},{1,9},{9,1},{17,25},{25,17},{2,10},{10... | collective-permute-start | bytes 4521992 | tf_op jit(solution)/shard_map/ppermute | solution.py:204
  96.0 141.7 %collective-permute-start.5 = (bf16[128,128,128]{2,1,0:T(8,128)(2,1)}, bf16[128,128,128]{2,1,0:T(8,128)(2,1)}, u32[]{:S(2)}, u32[]{:S(2)}) collective-permute-start(bf16[128,128,128]{2,1,0:T(8,128)(2,1)} %pack_tiles.4), channel_id=1, source_target_pairs={{0,4},{4,0},{1,5},{5,1},{2,6},{6,2},{3,7},{7,3},{8,12},{12,8},{9,1... | collective-permute-start | bytes 12582920 | tf_op jit(solution)/shard_map/ppermute | solution.py:204
  97.6 53.9 %collective-permute-start.42 = (s32[2,4,36]{2,1,0:T(4,128)S(1)}, s32[2,4,36]{2,1,0:T(4,128)S(1)}, u32[]{:S(2)}, u32[]{:S(2)}) collective-permute-start(s32[2,4,36]{2,1,0:T(4,128)S(1)} %pad_add_fusion), channel_id=1, source_target_pairs={{0,8},{24,16},{1,9},{25,17},{2,10},{26,18},{3,11},{27,19},{4,12},{... | collective-permute-start | bytes 3464 | tf_op jit(solution)/shard_map/ppermute | solution.py:269
  151.5 41.1 %collective-permute-start.22 = (bf16[2944,256]{1,0:T(8,128)(2,1)}, bf16[2944,256]{1,0:T(8,128)(2,1)}, u32[]{:S(2)}, u32[]{:S(2)}) collective-permute-start(bf16[2944,256]{1,0:T(8,128)(2,1)} %get-tuple-element.131), channel_id=1, source_target_pairs={{8,16},{16,8},{9,17},{17,9},{10,18},{18,10},{11,19},{19,11},{12,20... | collective-permute-start | bytes 4521992 | tf_op jit(solution)/shard_map/ppermute | solution.py:204
  154.1 42.6 %collective-permute-start.20 = (bf16[2944,256]{1,0:T(8,128)(2,1)}, bf16[2944,256]{1,0:T(8,128)(2,1)}, u32[]{:S(2)}, u32[]{:S(2)}) collective-permute-start(bf16[2944,256]{1,0:T(8,128)(2,1)} %copy-done.49), channel_id=1, source_target_pairs={{8,16},{16,8},{9,17},{17,9},{10,18},{18,10},{11,19},{19,11},{12,20... | collective-permute-start | bytes 4521992 | tf_op jit(solution)/shard_map/ppermute | solution.py:204
  155.9 41.6 %collective-permute-start.17 = (bf16[2944,256]{1,0:T(8,128)(2,1)}, bf16[2944,256]{1,0:T(8,128)(2,1)}, u32[]{:S(2)}, u32[]{:S(2)}) collective-permute-start(bf16[2944,256]{1,0:T(8,128)(2,1)} %collective-permute-done.16), channel_id=1, source_target_pairs={{8,0},{16,24},{9,1},{17,25},{10,2},{18,26},{11,3},{19,27},{12,4},{... | collective-permute-start | bytes 4521992 | tf_op jit(solution)/shard_map/ppermute | solution.py:204
  167.8 55.4 %collective-permute-start.11 = (bf16[2944,256]{1,0:T(8,128)(2,1)}, bf16[2944,256]{1,0:T(8,128)(2,1)}, u32[]{:S(2)}, u32[]{:S(2)}) collective-permute-start(bf16[2944,256]{1,0:T(8,128)(2,1)} %copy-done.49), channel_id=1, source_target_pairs={{0,8},{8,0},{16,24},{24,16},{1,9},{9,1},{17,25},{25,17},{2,10},{10... | collective-permute-start | bytes 4521992 | tf_op jit(solution)/shard_map/ppermute | solution.py:204
  192.6 82.4 %collective-permute-start.13 = (bf16[104,128,128]{2,1,0:T(8,128)(2,1)S(1)}, bf16[104,128,128]{2,1,0:T(8,128)(2,1)S(1)}, u32[]{:S(2)}, u32[]{:S(2)}) collective-permute-start(bf16[104,128,128]{2,1,0:T(8,128)(2,1)S(1)} %copy-done.3), channel_id=1, source_target_pairs={{0,8},{24,16},{1,9},{25,17},{2,10},{26,18},{3,11},{27,19},{4,12},{... | collective-permute-start | bytes 10223624 | tf_op jit(solution)/shard_map/ppermute | solution.py:204
  196.7 37.3 %collective-permute-start.27 = (bf16[2944,256]{1,0:T(8,128)(2,1)}, bf16[2944,256]{1,0:T(8,128)(2,1)S(1)}, u32[]{:S(2)}, u32[]{:S(2)}) collective-permute-start(bf16[2944,256]{1,0:T(8,128)(2,1)} %collective-permute-done.9), channel_id=1, source_target_pairs={{8,16},{16,8},{9,17},{17,9},{10,18},{18,10},{11,19},{19,11},{12,20... | collective-permute-start | bytes 4521992 | tf_op jit(solution)/shard_map/ppermute | solution.py:204
  197.5 38.3 %collective-permute-start.24 = (bf16[2944,256]{1,0:T(8,128)(2,1)}, bf16[2944,256]{1,0:T(8,128)(2,1)S(1)}, u32[]{:S(2)}, u32[]{:S(2)}) collective-permute-start(bf16[2944,256]{1,0:T(8,128)(2,1)} %collective-permute-done.10), channel_id=1, source_target_pairs={{8,16},{16,8},{9,17},{17,9},{10,18},{18,10},{11,19},{19,11},{12,20... | collective-permute-start | bytes 4521992 | tf_op jit(solution)/shard_map/ppermute | solution.py:204
  223.2 37.7 %collective-permute-start.19 = (bf16[2944,256]{1,0:T(8,128)(2,1)}, bf16[2944,256]{1,0:T(8,128)(2,1)S(1)}, u32[]{:S(2)}, u32[]{:S(2)}) collective-permute-start(bf16[2944,256]{1,0:T(8,128)(2,1)} %collective-permute-done.18), channel_id=1, source_target_pairs={{8,0},{16,24},{9,1},{17,25},{10,2},{18,26},{11,3},{19,27},{12,4},{... | collective-permute-start | bytes 4521992 | tf_op jit(solution)/shard_map/ppermute | solution.py:204
  234.0 89.5 %collective-permute-start.28 = (bf16[2944,256]{1,0:T(8,128)(2,1)}, bf16[2944,256]{1,0:T(8,128)(2,1)}, u32[]{:S(2)}, u32[]{:S(2)}) collective-permute-start(bf16[2944,256]{1,0:T(8,128)(2,1)} %collective-permute-done.12), channel_id=1, source_target_pairs={{8,16},{16,8},{9,17},{17,9},{10,18},{18,10},{11,19},{19,11},{12,20... | collective-permute-start | bytes 4521992 | tf_op jit(solution)/shard_map/ppermute | solution.py:204
  235.8 159.6 %copy-start.34 = (bf16[2944,256]{1,0:T(8,128)(2,1)}, bf16[2944,256]{1,0:T(8,128)(2,1)S(1)}, u32[]{:S(2)}) copy-start(bf16[2944,256]{1,0:T(8,128)(2,1)S(1)} %collective-permute-done.24) | copy-start | bytes 4521988
  235.8 89.3 %collective-permute-start.25 = (bf16[2944,256]{1,0:T(8,128)(2,1)}, bf16[2944,256]{1,0:T(8,128)(2,1)}, u32[]{:S(2)}, u32[]{:S(2)}) collective-permute-start(bf16[2944,256]{1,0:T(8,128)(2,1)} %collective-permute-done.11), channel_id=1, source_target_pairs={{8,16},{16,8},{9,17},{17,9},{10,18},{18,10},{11,19},{19,11},{12,20... | collective-permute-start | bytes 4521992 | tf_op jit(solution)/shard_map/ppermute | solution.py:204
  237.8 40.3 %collective-permute-start.6 = (bf16[4608,128]{1,0:T(8,128)(2,1)}, bf16[4608,128]{1,0:T(8,128)(2,1)}, u32[]{:S(2)}, u32[]{:S(2)}) collective-permute-start(bf16[4608,128]{1,0:T(8,128)(2,1)} %constant_dynamic-slice_fusion.9), channel_id=1, source_target_pairs={{0,4},{4,0},{1,5},{5,1},{2,6},{6,2},{3,7},{7,3},{8,12},{12,8},{9,1... | collective-permute-start | bytes 3538952 | tf_op jit(solution)/shard_map/ppermute | solution.py:204
  260.8 80.9 %collective-permute-start.21 = (bf16[2944,256]{1,0:T(8,128)(2,1)}, bf16[2944,256]{1,0:T(8,128)(2,1)}, u32[]{:S(2)}, u32[]{:S(2)}) collective-permute-start(bf16[2944,256]{1,0:T(8,128)(2,1)} %collective-permute-done.20), channel_id=1, source_target_pairs={{8,0},{16,24},{9,1},{17,25},{10,2},{18,26},{11,3},{19,27},{12,4},{... | collective-permute-start | bytes 4521992 | tf_op jit(solution)/shard_map/ppermute | solution.py:204
  275.0 50.9 %copy-start.1 = (bf16[104,128,128]{2,1,0:T(8,128)(2,1)S(1)}, bf16[104,128,128]{2,1,0:T(8,128)(2,1)}, u32[]{:S(2)}) copy-start(bf16[104,128,128]{2,1,0:T(8,128)(2,1)} %copy-done) | copy-start | bytes 10223620
  278.1 106.6 %copy-start.21 = (bf16[512,2304]{1,0:T(8,128)(2,1)}, bf16[512,2304]{1,0:T(8,128)(2,1)S(1)}, u32[]{:S(2)}) copy-start(bf16[512,2304]{1,0:T(8,128)(2,1)S(1)} %get-tuple-element.149) | copy-start | bytes 7077892
  278.1 49.3 %copy-start.17 = (bf16[512,2304]{1,0:T(8,128)(2,1)S(1)}, bf16[512,2304]{1,0:T(8,128)(2,1)}, u32[]{:S(2)}) copy-start(bf16[512,2304]{1,0:T(8,128)(2,1)} %copy-done.16) | copy-start | bytes 7077892
  281.4 64.9 %collective-permute-start.14 = (bf16[2304,256]{1,0:T(8,128)(2,1)}, bf16[2304,256]{1,0:T(8,128)(2,1)}, u32[]{:S(2)}, u32[]{:S(2)}) collective-permute-start(bf16[2304,256]{1,0:T(8,128)(2,1)} %get-tuple-element.135), channel_id=1, source_target_pairs={{0,8},{24,16},{1,9},{25,17},{2,10},{26,18},{3,11},{27,19},{4,12},{... | collective-permute-start | bytes 3538952 | tf_op jit(solution)/shard_map/ppermute | solution.py:204
  323.4 59.1 %collective-permute-start.29 = (bf16[2304,256]{1,0:T(8,128)(2,1)}, bf16[2304,256]{1,0:T(8,128)(2,1)}, u32[]{:S(2)}, u32[]{:S(2)}) collective-permute-start(bf16[2304,256]{1,0:T(8,128)(2,1)} %get-tuple-element.138), channel_id=1, source_target_pairs={{8,16},{16,8},{9,17},{17,9},{10,18},{18,10},{11,19},{19,11},{12,20... | collective-permute-start | bytes 3538952 | tf_op jit(solution)/shard_map/ppermute | solution.py:204
  325.1 55.5 %collective-permute-start.26 = (bf16[2304,256]{1,0:T(8,128)(2,1)}, bf16[2304,256]{1,0:T(8,128)(2,1)S(1)}, u32[]{:S(2)}, u32[]{:S(2)}) collective-permute-start(bf16[2304,256]{1,0:T(8,128)(2,1)} %get-tuple-element.135), channel_id=1, source_target_pairs={{8,16},{16,8},{9,17},{17,9},{10,18},{18,10},{11,19},{19,11},{12,20... | collective-permute-start | bytes 3538952 | tf_op jit(solution)/shard_map/ppermute | solution.py:204
  325.9 83.4 %collective-permute-start.7 = (bf16[104,128,128]{2,1,0:T(8,128)(2,1)S(1)}, bf16[104,128,128]{2,1,0:T(8,128)(2,1)S(1)}, u32[]{:S(2)}, u32[]{:S(2)}) collective-permute-start(bf16[104,128,128]{2,1,0:T(8,128)(2,1)S(1)} %copy-done.1), channel_id=1, source_target_pairs={{0,4},{4,0},{1,5},{5,1},{2,6},{6,2},{3,7},{7,3},{8,12},{12,8},{9,1... | collective-permute-start | bytes 10223624 | tf_op jit(solution)/shard_map/ppermute | solution.py:204
  341.7 53.7 %collective-permute-start.23 = (bf16[2944,256]{1,0:T(8,128)(2,1)}, bf16[2944,256]{1,0:T(8,128)(2,1)S(1)}, u32[]{:S(2)}, u32[]{:S(2)}) collective-permute-start(bf16[2944,256]{1,0:T(8,128)(2,1)} %collective-permute-done.22), channel_id=1, source_target_pairs={{8,0},{16,24},{9,1},{17,25},{10,2},{18,26},{11,3},{19,27},{12,4},{... | collective-permute-start | bytes 4521992 | tf_op jit(solution)/shard_map/ppermute | solution.py:204
  346.3 54.1 %collective-permute-start.15 = (bf16[2304,256]{1,0:T(8,128)(2,1)}, bf16[2304,256]{1,0:T(8,128)(2,1)}, u32[]{:S(2)}, u32[]{:S(2)}) collective-permute-start(bf16[2304,256]{1,0:T(8,128)(2,1)} %get-tuple-element.138), channel_id=1, source_target_pairs={{0,8},{24,16},{1,9},{25,17},{2,10},{26,18},{3,11},{27,19},{4,12},{... | collective-permute-start | bytes 3538952 | tf_op jit(solution)/shard_map/ppermute | solution.py:204
  380.6 27.0 %collective-permute-start.37 = (bf16[2304,256]{1,0:T(8,128)(2,1)}, bf16[2304,256]{1,0:T(8,128)(2,1)S(1)}, u32[]{:S(2)}, u32[]{:S(2)}) collective-permute-start(bf16[2304,256]{1,0:T(8,128)(2,1)} %collective-permute-done.14), channel_id=1, source_target_pairs={{8,16},{16,8},{9,17},{17,9},{10,18},{18,10},{11,19},{19,11},{12,20... | collective-permute-start | bytes 3538952 | tf_op jit(solution)/shard_map/ppermute | solution.py:204
  395.4 54.2 %collective-permute-start.33 = (bf16[2944,256]{1,0:T(8,128)(2,1)S(1)}, bf16[2944,256]{1,0:T(8,128)(2,1)}, u32[]{:S(2)}, u32[]{:S(2)}) collective-permute-start(bf16[2944,256]{1,0:T(8,128)(2,1)S(1)} %collective-permute-done.24), channel_id=1, source_target_pairs={{8,0},{16,24},{9,1},{17,25},{10,2},{18,26},{11,3},{19,27},{12,4},{... | collective-permute-start | bytes 4521992 | tf_op jit(solution)/shard_map/ppermute | solution.py:204
  400.4 58.6 %collective-permute-start.38 = (bf16[2304,256]{1,0:T(8,128)(2,1)}, bf16[2304,256]{1,0:T(8,128)(2,1)}, u32[]{:S(2)}, u32[]{:S(2)}) collective-permute-start(bf16[2304,256]{1,0:T(8,128)(2,1)} %collective-permute-done.15), channel_id=1, source_target_pairs={{8,16},{16,8},{9,17},{17,9},{10,18},{18,10},{11,19},{19,11},{12,20... | collective-permute-start | bytes 3538952 | tf_op jit(solution)/shard_map/ppermute | solution.py:204
  409.2 126.0 %collective-permute-start.8 = (bf16[128,128,128]{2,1,0:T(8,128)(2,1)S(1)}, bf16[128,128,128]{2,1,0:T(8,128)(2,1)S(1)}, u32[]{:S(2)}, u32[]{:S(2)}) collective-permute-start(bf16[128,128,128]{2,1,0:T(8,128)(2,1)S(1)} %pack_tiles.5), channel_id=1, source_target_pairs={{0,4},{4,0},{1,5},{5,1},{2,6},{6,2},{3,7},{7,3},{8,12},{12,8},{9,1... | collective-permute-start | bytes 12582920 | tf_op jit(solution)/shard_map/ppermute | solution.py:204
  410.7 108.2 %collective-permute-start.43 = (bf16[104,128,128]{2,1,0:T(8,128)(2,1)S(1)}, bf16[104,128,128]{2,1,0:T(8,128)(2,1)S(1)}, u32[]{:S(2)}, u32[]{:S(2)}) collective-permute-start(bf16[104,128,128]{2,1,0:T(8,128)(2,1)S(1)} %collective-permute-done.7.source), channel_id=1, source_target_pairs={{0,8},{24,16},{1,9},{25,17},{2,10},{26,18},{3,11},{27,19},{4,12},{... | collective-permute-start | bytes 10223624 | tf_op jit(solution)/shard_map/ppermute | solution.py:204
  449.7 32.9 %collective-permute-start.34 = (bf16[2944,256]{1,0:T(8,128)(2,1)S(1)}, bf16[2944,256]{1,0:T(8,128)(2,1)S(1)}, u32[]{:S(2)}, u32[]{:S(2)}) collective-permute-start(bf16[2944,256]{1,0:T(8,128)(2,1)S(1)} %copy-done.80), channel_id=1, source_target_pairs={{8,0},{16,24},{9,1},{17,25},{10,2},{18,26},{11,3},{19,27},{12,4},{... | collective-permute-start | bytes 4521992 | tf_op jit(solution)/shard_map/ppermute | solution.py:204
  482.6 33.2 %collective-permute-start.35 = (bf16[2944,256]{1,0:T(8,128)(2,1)}, bf16[2944,256]{1,0:T(8,128)(2,1)S(1)}, u32[]{:S(2)}, u32[]{:S(2)}) collective-permute-start(bf16[2944,256]{1,0:T(8,128)(2,1)} %collective-permute-done.25), channel_id=1, source_target_pairs={{8,0},{16,24},{9,1},{17,25},{10,2},{18,26},{11,3},{19,27},{12,4},{... | collective-permute-start | bytes 4521992 | tf_op jit(solution)/shard_map/ppermute | solution.py:204
  491.8 25.3 %copy-start.9 = (bf16[512,2944]{1,0:T(8,128)(2,1)S(1)}, bf16[512,2944]{1,0:T(8,128)(2,1)}, u32[]{:S(2)}) copy-start(bf16[512,2944]{1,0:T(8,128)(2,1)} %copy-done.6) | copy-start | bytes 9043972
  515.8 49.7 %collective-permute-start.36 = (bf16[2944,256]{1,0:T(8,128)(2,1)}, bf16[2944,256]{1,0:T(8,128)(2,1)}, u32[]{:S(2)}, u32[]{:S(2)}) collective-permute-start(bf16[2944,256]{1,0:T(8,128)(2,1)} %collective-permute-done.28), channel_id=1, source_target_pairs={{8,0},{16,24},{9,1},{17,25},{10,2},{18,26},{11,3},{19,27},{12,4},{... | collective-permute-start | bytes 4521992 | tf_op jit(solution)/shard_map/ppermute | solution.py:204
  535.3 46.5 %collective-permute-start.44 = (f32[3,1024,128]{1,2,0:T(8,128)}, f32[3,1024,128]{1,2,0:T(8,128)}, u32[]{:S(2)}, u32[]{:S(2)}) collective-permute-start(f32[3,1024,128]{1,2,0:T(8,128)} %constant_dynamic-slice_fusion.4), channel_id=1, source_target_pairs={{0,1},{1,0},{2,3},{3,2},{4,5},{5,4},{6,7},{7,6},{8,9},{9,8},{10,11... | collective-permute-start | bytes 4718600 | tf_op jit(solution)/shard_map/ppermute | solution.py:186
  563.8 25.1 %collective-permute-start.30 = (f32[3,1024,128]{1,2,0:T(8,128)}, f32[3,1024,128]{1,2,0:T(8,128)}, u32[]{:S(2)}, u32[]{:S(2)}) collective-permute-start(f32[3,1024,128]{1,2,0:T(8,128)} %constant_dynamic-slice_fusion.7), channel_id=1, source_target_pairs={{0,1},{1,0},{2,3},{3,2},{4,5},{5,4},{6,7},{7,6},{8,9},{9,8},{10,11... | collective-permute-start | bytes 4718600 | tf_op jit(solution)/shard_map/ppermute | solution.py:186
  579.4 6.6 collective-permute-start.39
  584.5 33.3 %collective-permute-start.45 = (f32[3,64,1024]{2,1,0:T(8,128)}, f32[3,64,1024]{2,1,0:T(8,128)}, u32[]{:S(2)}, u32[]{:S(2)}) collective-permute-start(f32[3,64,1024]{2,1,0:T(8,128)} %dynamic-slice_bitcast_fusion), channel_id=1, source_target_pairs={{0,4},{4,0},{1,5},{5,1},{2,6},{6,2},{3,7},{7,3},{8,12},{12,8},{9,1... | collective-permute-start | bytes 2359304 | tf_op jit(solution)/shard_map/ppermute | solution.py:186
  588.1 28.3 %collective-permute-start.40 = (f32[1,64,1024]{1,2,0:T(8,128)}, f32[1,64,1024]{1,2,0:T(8,128)}, u32[]{:S(2)}, u32[]{:S(2)}) collective-permute-start(f32[1,64,1024]{1,2,0:T(8,128)} %dynamic-slice_bitcast_fusion.2), channel_id=1, source_target_pairs={{0,4},{4,0},{1,5},{5,1},{2,6},{6,2},{3,7},{7,3},{8,12},{12,8},{9,1... | collective-permute-start | bytes 786440 | tf_op jit(solution)/shard_map/ppermute | solution.py:186
  590.6 27.2 %copy-start.33 = (f32[3,1024,128]{1,2,0:T(8,128)S(1)}, f32[3,1024,128]{1,2,0:T(8,128)}, u32[]{:S(2)}) copy-start(f32[3,1024,128]{1,2,0:T(8,128)} %copy-done.32) | copy-start | bytes 4718596
  591.6 41.0 %collective-permute-start.31 = (f32[3,64,1024]{2,1,0:T(8,128)}, f32[3,64,1024]{2,1,0:T(8,128)}, u32[]{:S(2)}, u32[]{:S(2)}) collective-permute-start(f32[3,64,1024]{2,1,0:T(8,128)} %dynamic-slice_bitcast_fusion.1), channel_id=1, source_target_pairs={{0,4},{4,0},{1,5},{5,1},{2,6},{6,2},{3,7},{7,3},{8,12},{12,8},{9,1... | collective-permute-start | bytes 2359304 | tf_op jit(solution)/shard_map/ppermute | solution.py:186
  619.1 16.2 %collective-permute-start.46 = (f32[3,32,1024]{2,1,0:T(8,128)S(1)}, f32[3,32,1024]{2,1,0:T(8,128)S(1)}, u32[]{:S(2)}, u32[]{:S(2)}) collective-permute-start(f32[3,32,1024]{2,1,0:T(8,128)S(1)} %constant_dynamic-slice_fusion.3), channel_id=1, source_target_pairs={{0,2},{2,0},{1,3},{3,1},{4,6},{6,4},{5,7},{7,5},{8,10},{10,8},{9,1... | collective-permute-start | bytes 1179656 | tf_op jit(solution)/shard_map/ppermute | solution.py:186
  620.8 21.7 %collective-permute-start.41 = (f32[1,32,1024]{1,2,0:T(8,128)S(1)}, f32[1,32,1024]{1,2,0:T(8,128)S(1)}, u32[]{:S(2)}, u32[]{:S(2)}) collective-permute-start(f32[1,32,1024]{1,2,0:T(8,128)S(1)} %constant_dynamic-slice_fusion.5), channel_id=1, source_target_pairs={{0,2},{2,0},{1,3},{3,1},{4,6},{6,4},{5,7},{7,5},{8,10},{10,8},{9,1... | collective-permute-start | bytes 393224 | tf_op jit(solution)/shard_map/ppermute | solution.py:186
  633.9 14.8 %collective-permute-start.32 = (f32[3,32,1024]{2,1,0:T(8,128)S(1)}, f32[3,32,1024]{2,1,0:T(8,128)S(1)}, u32[]{:S(2)}, u32[]{:S(2)}) collective-permute-start(f32[3,32,1024]{2,1,0:T(8,128)S(1)} %constant_dynamic-slice_fusion.6), channel_id=1, source_target_pairs={{0,2},{2,0},{1,3},{3,1},{4,6},{6,4},{5,7},{7,5},{8,10},{10,8},{9,1... | collective-permute-start | bytes 1179656 | tf_op jit(solution)/shard_map/ppermute | solution.py:186
  635.4 15.4 %collective-permute-start.47 = (f32[3,32,1024]{2,1,0:T(8,128)S(1)}, f32[3,32,1024]{2,1,0:T(8,128)S(1)}, u32[]{:S(2)}, u32[]{:S(2)}) collective-permute-start(f32[3,32,1024]{2,1,0:T(8,128)S(1)} %dynamic-slice_add_fusion.5), channel_id=1, source_target_pairs={{8,0},{16,24},{9,1},{17,25},{10,2},{18,26},{11,3},{19,27},{12,4},{... | collective-permute-start | bytes 1179656 | tf_op jit(solution)/shard_map/ppermute | solution.py:383
  651.6 14.3 %collective-permute-start.48 = (f32[136,1024]{1,0:T(8,128)S(1)}, f32[136,1024]{1,0:T(8,128)S(1)}, u32[]{:S(2)}, u32[]{:S(2)}) collective-permute-start(f32[136,1024]{1,0:T(8,128)S(1)} %get-tuple-element.209), channel_id=1, source_target_pairs={{0,8},{8,0},{16,24},{24,16},{1,9},{9,1},{17,25},{25,17},{2,10},{10... | collective-permute-start | bytes 1671176 | tf_op jit(solution)/shard_map/ppermute | solution.py:210
  655.2 12.7 %collective-permute-start.49 = (f32[136,1024]{1,0:T(8,128)S(1)}, f32[136,1024]{1,0:T(8,128)S(1)}, u32[]{:S(2)}, u32[]{:S(2)}) collective-permute-start(f32[136,1024]{1,0:T(8,128)S(1)} %get-tuple-element.209), channel_id=1, source_target_pairs={{8,16},{16,8},{9,17},{17,9},{10,18},{18,10},{11,19},{19,11},{12,20... | collective-permute-start | bytes 1671176 | tf_op jit(solution)/shard_map/ppermute | solution.py:211
  665.9 5.0 collective-permute-start.51
  666.6 3.6 collective-permute-start
  668.0 18.7 %collective-permute-start.50 = (f32[136,1024]{1,0:T(8,128)S(1)}, f32[136,1024]{1,0:T(8,128)S(1)}, u32[]{:S(2)}, u32[]{:S(2)}) collective-permute-start(f32[136,1024]{1,0:T(8,128)S(1)} %collective-permute-done.49), channel_id=1, source_target_pairs={{8,0},{16,24},{9,1},{17,25},{10,2},{18,26},{11,3},{19,27},{12,4},{... | collective-permute-start | bytes 1671176 | tf_op jit(solution)/shard_map/ppermute | solution.py:213
  670.9 24.8 %collective-permute-start.52 = (f32[136,1024]{1,0:T(8,128)S(1)}, f32[136,1024]{1,0:T(8,128)S(1)}, u32[]{:S(2)}, u32[]{:S(2)}) collective-permute-start(f32[136,1024]{1,0:T(8,128)S(1)} %collective-permute-done.51), channel_id=1, source_target_pairs={{8,0},{16,24},{9,1},{17,25},{10,2},{18,26},{11,3},{19,27},{12,4},{... | collective-permute-start | bytes 1671176 | tf_op jit(solution)/shard_map/ppermute | solution.py:214
  705.0 3.0 collective-permute-start.53
  709.4 14.7 %collective-permute-start.54 = (f32[1,2,1,4,136,128]{5,4,3,2,1,0:T(8,128)S(1)}, f32[1,2,1,4,136,128]{5,4,3,2,1,0:T(8,128)S(1)}, u32[]{:S(2)}, u32[]{:S(2)}) collective-permute-start(f32[1,2,1,4,136,128]{5,4,3,2,1,0:T(8,128)S(1)} %constant_dynamic-slice_fusion.1), channel_id=1, source_target_pairs={{0,4},{4,0},{1,5},{5,1},{2,6},{6,2},{3,7},{7,3},{8,12},{12,8},{9,1... | collective-permute-start | bytes 1671176 | tf_op jit(solution)/shard_map/ppermute | solution.py:186
  724.2 7.9 %collective-permute-start.55 = (f32[1,1,1,4,136,128]{5,4,3,2,1,0:T(8,128)S(1)}, f32[1,1,1,4,136,128]{5,4,3,2,1,0:T(8,128)S(1)}, u32[]{:S(2)}, u32[]{:S(2)}) collective-permute-start(f32[1,1,1,4,136,128]{5,4,3,2,1,0:T(8,128)S(1)} %constant_dynamic-slice_fusion), channel_id=1, source_target_pairs={{0,2},{2,0},{1,3},{3,1},{4,6},{6,4},{5,7},{7,5},{8,10},{10,8},{9,1... | collective-permute-start | bytes 835592 | tf_op jit(solution)/shard_map/ppermute | solution.py:186
  (77 other events, 327.6 us)

commit v5 on v4

--- a/solution.py
+++ b/solution.py
@@ -136,14 +136,24 @@
     )(info, source)
 
 
-def dots_kernel(blk, count, depth, ids, blocks, out):
-    flag = jnp.sum(blocks[:, depth : depth + 1, :blk], axis=0)
+def dots_kernel(blk, count, ids, early, late, out):
+    groups, share = early.shape[1] - 1, late.shape[1] - 8
+    flag = jnp.sum(late[:, share : share + 1, :blk], axis=0)
     rest = jnp.zeros((out.shape[1] - blk - 3, blk), jnp.float32)
 
     def one(k, carry):
         def side(which):
-            start = pl.multiple_of(ids[which, 1, k] * blk, blk)
-            return blocks[ids[which, 0, k], :depth, pl.ds(start, blk)]
+            place, start = ids[which, 0, k], pl.multiple_of(ids[which, 1, k] * blk, blk)
+            held = [early[place, g, :, pl.ds(start, blk)] for g in range(groups + 1)]
+            held.append(late[place, :share, pl.ds(start, blk)])
+            order = [ids[which, 2 + g, k] for g in range(groups + 2)]
+            picked = []
+            for g in range(groups + 2):
+                part = held[0]
+                for s in range(1, groups + 2):
+                    part = jnp.where(order[g] == s, held[s], part)
+                picked.append(part)
+            return jnp.concatenate(picked)
 
         left, right = side(0), side(1)
         out[k, :blk, :] = lax.dot_general(
@@ -157,16 +167,16 @@
     lax.fori_loop(0, count, one, 0)
 
 
-def pair_dots(blocks, ids, blk):
+def pair_dots(early, late, ids, blk):
     count = ids.shape[2]
     return pl.pallas_call(
-        functools.partial(dots_kernel, blk, count, blocks.shape[1] - 8),
+        functools.partial(dots_kernel, blk, count),
         out_shape=jax.ShapeDtypeStruct((count, blk + 8, blk), jnp.float32),
-        in_specs=[pl.BlockSpec(memory_space=pltpu.SMEM), pl.BlockSpec(memory_space=pltpu.VMEM)],
+        in_specs=[pl.BlockSpec(memory_space=pltpu.SMEM)] + [pl.BlockSpec(memory_space=pltpu.VMEM)] * 2,
         out_specs=pl.BlockSpec(memory_space=pltpu.VMEM),
         compiler_params=params(vmem_limit_bytes=48 << 20),
         name="pair_dots",
-    )(ids, blocks)
+    )(ids, early, late)
 
 
 def turn(count, k):
@@ -191,19 +201,46 @@
     return lax.optimization_barrier((values, arrived))[0]
 
 
-class Lane:
-    def __init__(self, depth):
-        self.depth = depth
-        self.arrived = []
-
-    def send(self, values, axis, pairs, later=None):
-        if len(self.arrived) >= self.depth:
-            values = after(values, self.arrived[-self.depth])
-        if later is not None:
-            values = after(values, later)
-        got = lax.ppermute(values, axis, pairs)
-        self.arrived.append(got)
-        return got
+class Transfers:
+    RATE = 1e5
+    SLOTS = 5
+    LATENCY = 2.0
+    STEP = 1.0
+
+    def __init__(self, depths):
+        self.depths = depths
+        self.listed = []
+        self.got = {}
+
+    def add(self, name, links, size, needs, make, axis, routes):
+        self.listed.append((name, links, CORES * size / self.RATE, needs, make, axis, routes))
+
+    def run(self):
+        now, free, ends, waiting = 0.0, {}, {}, list(self.listed)
+        while waiting:
+            flying = [t for t in self.listed if ends.get(t[0], -1.0) > now]
+            chosen = None
+            for t in waiting:
+                ready = all(ends.get(n, 1e9) <= now for n in t[3])
+                room_left = all(sum(link in f[1] for f in flying) < self.depths[link] for link in t[1])
+                if ready and room_left and len(flying) < self.SLOTS:
+                    chosen = t
+                    break
+            if chosen is None:
+                now = min(e for e in ends.values() if e > now)
+                continue
+            waiting.remove(chosen)
+            name, links, length, _, make, axis, routes = chosen
+            arrived = sorted((n for n in ends if ends[n] <= now), key=ends.get)[-self.SLOTS :]
+            values = make()
+            if arrived:
+                values = after(values, [self.got[n] for n in arrived])
+            self.got[name] = [lax.ppermute(v, axis, route) for v, route in zip(values, routes)]
+            now += self.STEP
+            end = max([now + self.LATENCY] + [free.get(link, 0.0) for link in links]) + length
+            for link in links:
+                free[link] = end
+            ends[name] = end + self.STEP
 
 
 def along_line(block, inner):
@@ -255,7 +292,7 @@
 
     lent = columns * LENT[0] // LENT[1]
     kept = columns - lent
-    cuts = bounds(kept, 4) + [kept + c for c in bounds(lent, 2)[1:]]
+    cuts = [0] + [kept * c // 9 for c in (1, 3, 6, 9)] + [kept + c for c in bounds(lent, 2)[1:]]
     widths = [b - a for a, b in zip(cuts[:-1], cuts[1:])]
     streams = {"lent": (4, 6), "early": (0, 2), "late": (2, 4)}
 
@@ -265,76 +302,96 @@
     def over_x(make):
         return [lax.ppermute(make((x + k) % wide), "x", turn(wide, k)) for k in range(1, wide)]
 
-    masks = [mask_of(x)] + [lax.ppermute(mask_of((x + k) % wide), "x", turn(wide, k)) for k in range(1, wide)]
-    guest_masks = lax.ppermute(jnp.stack([m[:, kept:] for m in masks]), "z", INWARD)
-
-    over_x, inward, outward, middle = Lane(1), Lane(2), Lane(1), Lane(2)
-
-    def planes_of(owner, c):
-        return lax.dynamic_slice_in_dim(planes, (owner * columns + cuts[c]) * blk, widths[c] * blk, 0)
-
-    def planes_over_x(first, last):
-        def part(owner):
-            start = (owner * columns + cuts[first]) * blk
-            return lax.dynamic_slice_in_dim(planes, start, (cuts[last] - cuts[first]) * blk, 0)
-
-        got = [over_x.send(part((x + k) % wide), "x", turn(wide, k)) for k in range(1, wide)]
-        groups = []
-        for c in range(first, last):
+    moves = Transfers({"x": 1, "in": 2, "out": 2, "mid": 2})
+    row_routes = [turn(wide, k) for k in range(1, wide)]
+    others = [(x + k) % wide for k in range(1, wide)]
+    slots_of = {n: room((cuts[b] - cuts[a]) * row_blocks) for n, (a, b) in streams.items()}
+    tile_bytes = blk * blk * 2
+    groups, packs = {}, {}
+
+    def planes_of(owner, first, last):
+        start = (owner * columns + cuts[first]) * blk
+        return lax.dynamic_slice_in_dim(planes, start, (cuts[last] - cuts[first]) * blk, 0)
+
+    def group(c):
+        if c not in groups:
+            name, first = next((n, a) for n, a, b in plane_moves if a <= c < b)
             whole = jnp.zeros((widths[c] * blk, wide * own_planes), planes.dtype)
-            whole = lax.dynamic_update_slice_in_dim(whole, planes_of(x, c), x * own_planes, 1)
+            whole = lax.dynamic_update_slice_in_dim(whole, planes_of(x, c, c + 1), x * own_planes, 1)
             for k in range(1, wide):
-                rows_of = slice((cuts[c] - cuts[first]) * blk, (cuts[c + 1] - cuts[first]) * blk)
-                whole = lax.dynamic_update_slice_in_dim(
-                    whole, got[k - 1][rows_of], ((x - k) % wide) * own_planes, 1
-                )
-            groups.append(whole)
-        return groups
-
-    def tiles_of(name, later):
+                part = moves.got[name][k - 1][(cuts[c] - cuts[first]) * blk : (cuts[c + 1] - cuts[first]) * blk]
+                whole = lax.dynamic_update_slice_in_dim(whole, part, ((x - k) % wide) * own_planes, 1)
+            groups[c] = whole
+        return groups[c]
+
+    def packed(name, owner, later):
         low, high = (cuts[c] for c in streams[name])
-        slots = room((high - low) * row_blocks)
-        got = []
-        for k in range(1, wide):
-            owner = (x + k) % wide
-            mask = after(mask_of(owner)[:, low:high], later)
-            tiles = pack(hist, mask, owner * columns + low, slots)
-            got.append(over_x.send(tiles, "x", turn(wide, k)))
-        return got
-
-    groups = planes_over_x(0, 1)
-    groups += planes_over_x(1, 2)
-    groups += planes_over_x(2, 4)
-    tiles = {"early": tiles_of("early", groups[0])}
-    groups += planes_over_x(4, 6)
-    tiles["lent"] = tiles_of("lent", groups[1])
-    tiles["late"] = tiles_of("late", groups[2])
-
-    near, mid, far = {}, {}, {}
+        mask = after(mask_of(owner)[:, low:high], moves.got[later])
+        return pack(hist, mask, owner * columns + low, slots_of[name])
+
+    plane_moves = [("planes0", 0, 1), ("planes1", 1, 2), ("planes2", 2, 4), ("planes4", 4, 6)]
+    source_of = ["planes0", "planes1", "planes2", "planes2", "planes4", "planes4"]
+
+    def add_planes(name, first, last):
+        size = (cuts[last] - cuts[first]) * blk * own_planes * 2 * len(others)
+        moves.add(
+            name, ["x"], size, [], lambda: [planes_of(o, first, last) for o in others], "x", row_routes
+        )
+
+    def add_tiles(name, later):
+        size = slots_of[name] * tile_bytes * len(others)
+        moves.add(
+            name, ["x"], size, [later], lambda: [packed(name, o, later) for o in others], "x", row_routes
+        )
+
+    def add_group(name, links, c, needs, make, routes):
+        size = widths[c] * blk * wide * own_planes * 2
+        moves.add(name, links, size, needs, lambda: [make()], "z", [routes])
+
+    moves.add("masks", ["x"], 0, [], lambda: [mask_of(o) for o in others], "x", row_routes)
     for c in range(4):
-        near[c] = inward.send(groups[c], "z", NEAR)
-        mid[c] = middle.send(groups[c], "z", MIDDLE)
-    inward.depth = 1
-    outward.arrived = [near[3]]
-    own_tiles = pack(hist, after(masks[0], groups[3])[:, kept:], x * columns + kept, room(lent * row_blocks))
-    lent_tiles = [inward.send(own_tiles, "z", INWARD)]
+        add_group(f"out2{c}", ["out"], c, [f"far{c}"], lambda c=c: moves.got[f"far{c}"][0], OUTWARD)
     for c in range(4):
-        far[c] = middle.send(near[c], "z", MIDDLE)
+        add_group(f"out1{c}", ["out"], c, [f"mid{c}"], lambda c=c: moves.got[f"mid{c}"][0], OUTWARD)
+    for c in range(4):
+        add_group(f"near{c}", ["in", "out"], c, [source_of[c]], lambda c=c: group(c), NEAR)
+    for c in range(4):
+        add_group(f"mid{c}", ["mid"], c, [source_of[c]], lambda c=c: group(c), MIDDLE)
+    for c in range(4):
+        add_group(f"far{c}", ["mid"], c, [f"near{c}"], lambda c=c: moves.got[f"near{c}"][0], MIDDLE)
     for c in (4, 5):
-        near[c] = inward.send(groups[c], "z", INWARD)
+        add_group(f"mid{c}", ["mid"], c, [source_of[c]], lambda c=c: group(c), MIDDLE)
     for c in (4, 5):
-        mid[c] = middle.send(groups[c], "z", MIDDLE)
+        add_group(f"far{c}", ["mid"], c, [f"near{c}"], lambda c=c: moves.got[f"near{c}"][0], MIDDLE)
+    for name, first, last in plane_moves[:3]:
+        add_planes(name, first, last)
+    moves.add(
+        "guests", ["in"], 0, ["masks", "planes0"],
+        lambda: [jnp.stack([mask_of(x)[:, kept:]] + [m[:, kept:] for m in moves.got["masks"]])], "z", [INWARD],
+    )
+    add_tiles("early", "planes0")
+    add_planes(*plane_moves[3])
+    add_tiles("lent", "planes1")
+    add_tiles("late", "planes2")
+    lent_bytes = slots_of["lent"] * tile_bytes
+    moves.add("loan0", ["in"], lent_bytes, ["near3"], lambda: [packed("lent", x, "planes2")], "z", [INWARD])
     for c in (4, 5):
-        far[c] = middle.send(near[c], "z", MIDDLE)
-    out1 = [outward.send(mid[c], "z", OUTWARD) for c in range(4)]
-    out2 = [outward.send(far[c], "z", OUTWARD) for c in range(4)]
-    lent_tiles += [inward.send(t, "z", INWARD) for t in tiles["lent"]]
+        add_group(f"near{c}", ["in"], c, [source_of[c]], lambda c=c: group(c), INWARD)
+    moves.add(
+        "loan1", ["in"], lent_bytes * len(others), ["lent"],
+        lambda: moves.got["lent"], "z", [INWARD] * len(others),
+    )
+    moves.run()
+    got = moves.got
     held = []
     for c in range(6):
+        near, mid, far = got[f"near{c}"][0], got[f"mid{c}"][0], got[f"far{c}"][0]
         if c < 4:
-            held.append([groups[c], near[c], jnp.where(inner, mid[c], out1[c]), jnp.where(inner, far[c], out2[c])])
-        else:
-            held.append([groups[c], near[c], mid[c], far[c]])
+            mid = jnp.where(inner, mid, got[f"out1{c}"][0])
+            far = jnp.where(inner, far, got[f"out2{c}"][0])
+        held.append([groups[c], near, mid, far])
+    masks = [mask_of(x)] + got["masks"]
+    guest_masks = got["guests"][0]
 
     over = jnp.int32(0)
     sessions = [[None] * 6 for _ in range(wide)]
@@ -347,12 +404,12 @@
         for k in range(wide):
             mask = masks[k][:, low:high]
             if k == 0:
-                later = groups[3] if name == "early" else near[0] if name == "lent" else near[1]
+                later = got[{"early": "near0", "lent": "near1", "late": "near2"}[name]]
                 sessions[k][first:last] = spread(hist, after(mask, later), x * columns + low, parts)
             else:
-                sessions[k][first:last] = spread(tiles[name][k - 1], mask, None, parts)
+                sessions[k][first:last] = spread(got[name][k - 1], mask, None, parts)
     guests = [
-        spread(t, guest_masks[k], None, tuple(widths[4:])) for k, t in enumerate(lent_tiles)
+        spread(t, guest_masks[k], None, tuple(widths[4:])) for k, t in enumerate(got["loan0"] + got["loan1"])
     ]
 
     def total(sources, chunks, s):
@@ -381,19 +438,22 @@
     guest_chunks = [{4: g[0], 5: g[1]} for g in guests]
     visitors = summed([total(guest_chunks, (4, 5), s) for s in (0, 2, 3)])
     visitors = lax.ppermute(visitors, "z", OUTWARD)
-    last_one = summed([total(sessions, every, 3)])
-    shares = jnp.concatenate([first_three, last_one]) + jnp.concatenate([jnp.zeros_like(last_one), visitors])
-    proj = shares[jnp.asarray(PLACE)[z]].reshape(-1, wide * rows)
-    flags = jnp.full((8, proj.shape[1]), over.astype(jnp.float32))
-    proj = jnp.concatenate([proj, flags])
-
-    blocks = jnp.stack(along_line(proj, inner))
-    got = [pairs] + [lax.ppermute(pairs, "x", turn(wide, k)) for k in range(1, wide)]
+    early = first_three.at[1:].add(visitors[:2])
+    early = jnp.stack(along_line(early, inner))
+    last_one = summed([total(sessions, every, 3)])[0] + visitors[2]
+    flags = jnp.full((8, last_one.shape[1]), over.astype(jnp.float32))
+    late = jnp.stack(along_line(jnp.concatenate([last_one, flags]), inner))
+
+    listed = [pairs] + [lax.ppermute(pairs, "x", route) for route in row_routes]
     order = (x - jnp.arange(wide)) % wide
-    all_pairs = jnp.stack(got)[order].reshape(-1, 2).T
+    all_pairs = jnp.stack(listed)[order].reshape(-1, 2).T
     plane_blocks = wide * row_blocks
-    ids = jnp.stack([jnp.asarray(PLACE)[z][all_pairs // plane_blocks], all_pairs % plane_blocks], axis=1)
-    sums = pair_dots(blocks, ids, blk)
+    of_plane = all_pairs // plane_blocks
+    places = jnp.moveaxis(jnp.asarray(PLACE)[of_plane], 2, 1)
+    ids = jnp.concatenate(
+        [jnp.asarray(PLACE)[z][of_plane][:, None], (all_pairs % plane_blocks)[:, None], places], axis=1
+    )
+    sums = pair_dots(early, late, ids, blk)
     high, cores = lax.axis_size("y"), lax.axis_size("core")
     sums = sums.reshape((wide, high, cores, -1) + sums.shape[1:])
     for axis, dim in (("core", 2), ("x", 0), ("y", 1)):

time: 754 us -> 779 us (1.033)
  waiting for transfers between devices: 252 us -> 353 us
  starting transfers between devices: 206 us -> 146 us
  local copies, waits for them, and re-layouts: 60.1 us -> 48.6 us
    ppermute x38, waiting for transfers between devices: 152 us -> 264 us  [the longest x37 264 us: run(): lax.ppermute(v, axis, route)]
    ppermute x38, starting transfers between devices: 187 us -> 122 us  [the longest x37 121 us: run(): lax.ppermute(v, axis, route)]
    ppermute x12, waiting for transfers between devices: 65.9 us -> 56.5 us  [scatter_sum(): total = total + lax.ppermute(part((here + k) % count), axis, turn(count, k))]
  transfers between devices with their start and end apart: 56 -> 61, of which waited for: 23 -> 26; matrix products, arithmetic and copies ran while one was open for 26% -> 24% of each run, Pallas kernels for 5% -> 5%
where the time goes in v5:
time: 779 us; the launch traced here: 769 us
  waiting for transfers between devices  353 us (45%)
  starting transfers between devices  146 us (19%)
  matrix products  137 us (18%)
  Pallas kernels  49.9 us (6%)
  local copies, waits for them, and re-layouts  48.6 us (6%)
  between operations  20.1 us (3%)
  other arithmetic  14.5 us (2%)
    ppermute x37, waiting for transfers between devices, run(): lax.ppermute(v, axis, route)  264 us
    dot_general x60, matrix products, total(): term = jnp.dot(source[c], held[c][s], preferred_element_type=jnp.float32)  137 us
    ppermute x37, starting transfers between devices, run(): lax.ppermute(v, axis, route)  121 us
    ppermute x12, waiting for transfers between devices, scatter_sum(): total = total + lax.ppermute(part((here + k) % count), axis, turn(count, k))  56.5 us
    pallas_call x8, Pallas kernels, spread(): pl.pallas_call(functools.partial(spread_kernel, blk, row_blocks, parts, s...  30.2 us
  transfers between devices with their start and end apart: 61, of which 26 were waited for; matrix products, arithmetic and copies ran while one was open for 24% of the time, Pallas kernels for 5%

profile of v5, /device:TPU:0, one launch (start us, length us, event | category | flops | bytes accessed | tf_op | source)
XLA Modules:
  0.0 769.1 jit_solution(9220721844994510305)
XLA Ops:
  7.2 2.9 collective-permute-start.1
  15.0 3.0 constant_dynamic-slice_fusion.9
  34.1 7.8 %collective-permute-done.2 = bf16[1280,128]{1,0:T(8,128)(2,1)S(1)} collective-permute-done((bf16[1280,128]{1,0:T(8,128)(2,1)S(1)}, bf16[1280,128]{1,0:T(8,128)(2,1)S(1)}, u32[]{:S(2)}, u32[]{:S(2)}) %collective-permute-start.2) | collective-permute-done | bytes 327712 | tf_op jit(solution)/shard_map/ppermute | solution.py:238
  48.1 6.3 collective-permute-start.4
  56.5 3.2 collective-permute-done.8
  63.0 4.1 collective-permute-start.10
  78.4 28.9 %collective-permute-done.7 = bf16[1280,256]{1,0:T(8,128)(2,1)} collective-permute-done((bf16[1280,256]{1,0:T(8,128)(2,1)S(1)}, bf16[1280,256]{1,0:T(8,128)(2,1)}, u32[]{:S(2)}, u32[]{:S(2)}) %collective-permute-start.7) | collective-permute-done | bytes 655392 | tf_op jit(solution)/shard_map/ppermute | solution.py:238
  112.0 3.0 slice_dynamic-update-slice_fusion.1
  115.0 40.7 %collective-permute-done.14 = bf16[1280,256]{1,0:T(8,128)(2,1)S(1)} collective-permute-done((bf16[1280,256]{1,0:T(8,128)(2,1)}, bf16[1280,256]{1,0:T(8,128)(2,1)S(1)}, u32[]{:S(2)}, u32[]{:S(2)}) %collective-permute-start.14) | collective-permute-done | bytes 655392 | tf_op jit(solution)/shard_map/ppermute | solution.py:238
  168.9 3.0 spread_tiles.13
  173.3 3.9 fusion.76
  179.4 3.0 pack_tiles.5
  190.0 3.0 fusion.49
  193.0 32.6 %collective-permute-done.16 = bf16[2560,256]{1,0:T(8,128)(2,1)} collective-permute-done((bf16[2560,256]{1,0:T(8,128)(2,1)}, bf16[2560,256]{1,0:T(8,128)(2,1)}, u32[]{:S(2)}, u32[]{:S(2)}) %collective-permute-start.16) | collective-permute-done | bytes 1310752 | tf_op jit(solution)/shard_map/ppermute | solution.py:238
  225.7 3.0 fusion.51
  229.0 4.4 spread_tiles.12
  233.4 4.3 fusion.68
  240.6 3.8 fusion.77
  251.8 3.1 fusion.50
  256.6 3.0 fusion.71
  259.7 3.2 fusion.52
  262.8 7.7 collective-permute-done.22
  273.6 3.5 collective-permute-start.25
  278.0 17.0 %collective-permute-done.20 = bf16[3968,256]{1,0:T(8,128)(2,1)S(1)} collective-permute-done((bf16[3968,256]{1,0:T(8,128)(2,1)}, bf16[3968,256]{1,0:T(8,128)(2,1)S(1)}, u32[]{:S(2)}, u32[]{:S(2)}) %collective-permute-start.20) | collective-permute-done | bytes 2031648 | tf_op jit(solution)/shard_map/ppermute | solution.py:238
  304.1 34.6 %collective-permute-done.25 = bf16[3968,256]{1,0:T(8,128)(2,1)} collective-permute-done((bf16[3968,256]{1,0:T(8,128)(2,1)}, bf16[3968,256]{1,0:T(8,128)(2,1)}, u32[]{:S(2)}, u32[]{:S(2)}) %collective-permute-start.25) | collective-permute-done | bytes 2031648 | tf_op jit(solution)/shard_map/ppermute | solution.py:238
  338.6 3.8 fusion.78
  342.5 25.1 %collective-permute-start.27 = (bf16[2304,256]{1,0:T(8,128)(2,1)S(1)}, bf16[2304,256]{1,0:T(8,128)(2,1)}, u32[]{:S(2)}, u32[]{:S(2)}) collective-permute-start(bf16[2304,256]{1,0:T(8,128)(2,1)S(1)} %get-tuple-element.154), channel_id=1, source_target_pairs={{0,8},{24,16},{1,9},{25,17},{2,10},{26,18},{3,11},{27,19},{4,12},{... | collective-permute-start | bytes 3538952 | tf_op jit(solution)/shard_map/ppermute | solution.py:238
  367.5 7.7 %collective-permute-done.29 = bf16[3968,256]{1,0:T(8,128)(2,1)} collective-permute-done((bf16[3968,256]{1,0:T(8,128)(2,1)}, bf16[3968,256]{1,0:T(8,128)(2,1)}, u32[]{:S(2)}, u32[]{:S(2)}) %collective-permute-start.29) | collective-permute-done | bytes 2031648 | tf_op jit(solution)/shard_map/ppermute | solution.py:238
  384.8 5.1 spread_tiles.10
  389.9 3.8 fusion.65
  393.6 3.4 fusion.64
  399.4 3.4 fusion.81
  402.8 7.1 collective-permute-start.37
  412.0 3.6 fusion.74
  418.1 3.6 collective-permute-done.36
  421.7 28.8 %collective-permute-start.32 = (bf16[2304,256]{1,0:T(8,128)(2,1)}, bf16[2304,256]{1,0:T(8,128)(2,1)}, u32[]{:S(2)}, u32[]{:S(2)}) collective-permute-start(bf16[2304,256]{1,0:T(8,128)(2,1)} %get-tuple-element.159), channel_id=1, source_target_pairs={{0,8},{24,16},{1,9},{25,17},{2,10},{26,18},{3,11},{27,19},{4,12},{... | collective-permute-start | bytes 3538952 | tf_op jit(solution)/shard_map/ppermute | solution.py:238
  450.5 4.9 fusion.40
  455.4 3.3 fusion.93
  458.7 3.3 fusion.91
  462.0 38.3 %collective-permute-done.32 = bf16[2304,256]{1,0:T(8,128)(2,1)} collective-permute-done((bf16[2304,256]{1,0:T(8,128)(2,1)}, bf16[2304,256]{1,0:T(8,128)(2,1)}, u32[]{:S(2)}, u32[]{:S(2)}) %collective-permute-start.32) | collective-permute-done | bytes 1179680 | tf_op jit(solution)/shard_map/ppermute | solution.py:238
  502.5 3.0 fusion.75
  507.0 3.7 fusion.42
  510.6 3.1 spread_tiles.15
  518.4 5.8 spread_tiles.9
  527.2 3.0 fusion.62
  531.9 6.9 collective-permute-start.38
  542.4 3.0 fusion.72
  549.0 3.0 fusion.37
  561.8 41.0 %collective-permute-done.38.source = bf16[104,128,128]{2,1,0:T(8,128)(2,1)S(1)} collective-permute-done((bf16[104,128,128]{2,1,0:T(8,128)(2,1)S(1)}, bf16[104,128,128]{2,1,0:T(8,128)(2,1)S(1)}, u32[]{:S(2)}, u32[]{:S(2)}) %collective-permute-start.38) | collective-permute-done | bytes 3407904 | tf_op jit(solution)/shard_map/ppermute | solution.py:238
  602.8 3.3 spread_tiles.14
  615.0 3.0 fusion.41
  633.8 14.0 %collective-permute-done.42 = f32[3,64,1024]{2,1,0:T(8,128)} collective-permute-done((f32[3,64,1024]{2,1,0:T(8,128)}, f32[3,64,1024]{2,1,0:T(8,128)}, u32[]{:S(2)}, u32[]{:S(2)}) %collective-permute-start.42) | collective-permute-done | bytes 786464 | tf_op jit(solution)/shard_map/ppermute | solution.py:196
  652.2 12.4 %collective-permute-done.34 = f32[3,64,1024]{2,1,0:T(8,128)} collective-permute-done((f32[3,64,1024]{2,1,0:T(8,128)}, f32[3,64,1024]{2,1,0:T(8,128)}, u32[]{:S(2)}, u32[]{:S(2)}) %collective-permute-start.34) | collective-permute-done | bytes 786464 | tf_op jit(solution)/shard_map/ppermute | solution.py:196
  671.2 5.8 collective-permute-done.35
  677.1 4.3 collective-permute-done.44
  682.8 3.1 collective-permute-start.53
  686.6 7.1 collective-permute-done.53
  700.6 4.8 collective-permute-done.55
  707.0 3.6 collective-permute-done.57
  710.7 8.1 %collective-permute-done.47 = f32[3,32,1024]{2,1,0:T(8,128)S(1)} collective-permute-done((f32[3,32,1024]{2,1,0:T(8,128)S(1)}, f32[3,32,1024]{2,1,0:T(8,128)S(1)}, u32[]{:S(2)}, u32[]{:S(2)}) %collective-permute-start.47) | collective-permute-done | bytes 393248 | tf_op jit(solution)/shard_map/ppermute | solution.py:250
  718.9 4.2 collective-permute-done.49
  723.2 9.3 %pair_dots.1 = f32[32,136,128]{2,1,0:T(8,128)S(1)} custom-call(s32[2,6,32]{2,1,0:T(8,128)S(1)} %pad_add_fusion.ids, f32[4,3,32,1024]{3,2,1,0:T(8,128)S(1)} %pad_maximum_fusion.2.early, f32[4,40,1024]{2,1,0:T(8,128)S(1)} %pad_maximum_fusion.3.late), custom_call_target="tpu_custom_call" | custom-call | tf_op jit(solution)/shard_map/pair_dots/pallas_call | solution.py:172
  738.3 13.4 %collective-permute-done.59 = f32[1,2,1,4,136,128]{5,4,3,2,1,0:T(8,128)S(1)} collective-permute-done((f32[1,2,1,4,136,128]{5,4,3,2,1,0:T(8,128)S(1)}, f32[1,2,1,4,136,128]{5,4,3,2,1,0:T(8,128)S(1)}, u32[]{:S(2)}, u32[]{:S(2)}) %collective-permute-start.59) | collective-permute-done | bytes 557088 | tf_op jit(solution)/shard_map/ppermute | solution.py:196
  752.1 7.6 collective-permute-done.60
  (402 shorter events, 194.5 us)
Async XLA Ops:
  7.2 25.4 %collective-permute-start.1 = (s32[4,128]{1,0:T(4,128)S(1)}, s32[4,128]{1,0:T(4,128)S(1)}, u32[]{:S(2)}, u32[]{:S(2)}) collective-permute-start(s32[4,128]{1,0:T(4,128)S(1)} %get-tuple-element.224), channel_id=1, source_target_pairs={{0,4},{4,0},{1,5},{5,1},{2,6},{6,2},{3,7},{7,3},{8,12},{12,8},{9,1... | collective-permute-start | bytes 6152 | tf_op jit(solution)/shard_map/ppermute | solution.py:238
  32.7 9.2 %collective-permute-start.2 = (bf16[1280,128]{1,0:T(8,128)(2,1)S(1)}, bf16[1280,128]{1,0:T(8,128)(2,1)S(1)}, u32[]{:S(2)}, u32[]{:S(2)}) collective-permute-start(bf16[1280,128]{1,0:T(8,128)(2,1)S(1)} %get-tuple-element.113), channel_id=1, source_target_pairs={{0,4},{4,0},{1,5},{5,1},{2,6},{6,2},{3,7},{7,3},{8,12},{12,8},{9,1... | collective-permute-start | bytes 983048 | tf_op jit(solution)/shard_map/ppermute | solution.py:238
  42.0 17.7 %collective-permute-start.3 = (bf16[1280,256]{1,0:T(8,128)(2,1)S(1)}, bf16[1280,256]{1,0:T(8,128)(2,1)S(1)}, u32[]{:S(2)}, u32[]{:S(2)}) collective-permute-start(bf16[1280,256]{1,0:T(8,128)(2,1)S(1)} %constant_dynamic-update-slice_fusion.1), channel_id=1, source_target_pairs={{0,8},{8,0},{16,24},{24,16},{1,9},{9,1},{17,25},{25,17},{2,10},{10... | collective-permute-start | bytes 1966088 | tf_op jit(solution)/shard_map/ppermute | solution.py:238
  43.6 16.1 %collective-permute-start.6 = (bf16[1280,256]{1,0:T(8,128)(2,1)S(1)}, bf16[1280,256]{1,0:T(8,128)(2,1)S(1)}, u32[]{:S(2)}, u32[]{:S(2)}) collective-permute-start(bf16[1280,256]{1,0:T(8,128)(2,1)S(1)} %constant_dynamic-update-slice_fusion.1), channel_id=1, source_target_pairs={{8,16},{16,8},{9,17},{17,9},{10,18},{18,10},{11,19},{19,11},{12,20... | collective-permute-start | bytes 1966088 | tf_op jit(solution)/shard_map/ppermute | solution.py:238
  44.3 15.4 %collective-permute-start.8 = (bf16[2560,128]{1,0:T(8,128)(2,1)}, bf16[2560,128]{1,0:T(8,128)(2,1)}, u32[]{:S(2)}, u32[]{:S(2)}) collective-permute-start(bf16[2560,128]{1,0:T(8,128)(2,1)} %get-tuple-element.119), channel_id=1, source_target_pairs={{0,4},{4,0},{1,5},{5,1},{2,6},{6,2},{3,7},{7,3},{8,12},{12,8},{9,1... | collective-permute-start | bytes 1966088 | tf_op jit(solution)/shard_map/ppermute | solution.py:238
  48.1 8.4 %collective-permute-start.4 = (s32[2,4,36]{2,1,0:T(4,128)S(1)}, s32[2,4,36]{2,1,0:T(4,128)S(1)}, u32[]{:S(2)}, u32[]{:S(2)}) collective-permute-start(s32[2,4,36]{2,1,0:T(4,128)S(1)} %pad_add_fusion.1), channel_id=1, source_target_pairs={{0,8},{24,16},{1,9},{25,17},{2,10},{26,18},{3,11},{27,19},{4,12},{... | collective-permute-start | bytes 3464 | tf_op jit(solution)/shard_map/ppermute | solution.py:238
  59.7 52.2 %collective-permute-start.11 = (bf16[7936,128]{1,0:T(8,128)(2,1)}, bf16[7936,128]{1,0:T(8,128)(2,1)}, u32[]{:S(2)}, u32[]{:S(2)}) collective-permute-start(bf16[7936,128]{1,0:T(8,128)(2,1)} %constant_dynamic-slice_fusion.9), channel_id=1, source_target_pairs={{0,4},{4,0},{1,5},{5,1},{2,6},{6,2},{3,7},{7,3},{8,12},{12,8},{9,1... | collective-permute-start | bytes 6094856 | tf_op jit(solution)/shard_map/ppermute | solution.py:238
  63.0 44.3 %collective-permute-start.10 = (bf16[2560,256]{1,0:T(8,128)(2,1)}, bf16[2560,256]{1,0:T(8,128)(2,1)}, u32[]{:S(2)}, u32[]{:S(2)}) collective-permute-start(bf16[2560,256]{1,0:T(8,128)(2,1)} %constant_dynamic-update-slice_fusion), channel_id=1, source_target_pairs={{0,8},{8,0},{16,24},{24,16},{1,9},{9,1},{17,25},{25,17},{2,10},{10... | collective-permute-start | bytes 3932168 | tf_op jit(solution)/shard_map/ppermute | solution.py:238
  67.1 40.2 %collective-permute-start.9 = (bf16[2560,256]{1,0:T(8,128)(2,1)}, bf16[2560,256]{1,0:T(8,128)(2,1)}, u32[]{:S(2)}, u32[]{:S(2)}) collective-permute-start(bf16[2560,256]{1,0:T(8,128)(2,1)} %constant_dynamic-update-slice_fusion), channel_id=1, source_target_pairs={{8,16},{16,8},{9,17},{17,9},{10,18},{18,10},{11,19},{19,11},{12,20... | collective-permute-start | bytes 3932168 | tf_op jit(solution)/shard_map/ppermute | solution.py:238
  70.9 7.5 collective-permute-start.5
  72.4 34.9 %collective-permute-start.7 = (bf16[1280,256]{1,0:T(8,128)(2,1)S(1)}, bf16[1280,256]{1,0:T(8,128)(2,1)}, u32[]{:S(2)}, u32[]{:S(2)}) collective-permute-start(bf16[1280,256]{1,0:T(8,128)(2,1)S(1)} %collective-permute-done.6), channel_id=1, source_target_pairs={{8,0},{16,24},{9,1},{17,25},{10,2},{18,26},{11,3},{19,27},{12,4},{... | collective-permute-start | bytes 1966088 | tf_op jit(solution)/shard_map/ppermute | solution.py:238
  107.3 56.7 %collective-permute-start.13 = (bf16[2560,256]{1,0:T(8,128)(2,1)}, bf16[2560,256]{1,0:T(8,128)(2,1)}, u32[]{:S(2)}, u32[]{:S(2)}) collective-permute-start(bf16[2560,256]{1,0:T(8,128)(2,1)} %collective-permute-done.10), channel_id=1, source_target_pairs={{8,16},{16,8},{9,17},{17,9},{10,18},{18,10},{11,19},{19,11},{12,20... | collective-permute-start | bytes 3932168 | tf_op jit(solution)/shard_map/ppermute | solution.py:238
  109.1 55.0 %collective-permute-start.15 = (bf16[2560,256]{1,0:T(8,128)(2,1)}, bf16[2560,256]{1,0:T(8,128)(2,1)}, u32[]{:S(2)}, u32[]{:S(2)}) collective-permute-start(bf16[2560,256]{1,0:T(8,128)(2,1)} %collective-permute-done.9), channel_id=1, source_target_pairs={{8,0},{16,24},{9,1},{17,25},{10,2},{18,26},{11,3},{19,27},{12,4},{... | collective-permute-start | bytes 3932168 | tf_op jit(solution)/shard_map/ppermute | solution.py:238
  110.7 45.0 %collective-permute-start.14 = (bf16[1280,256]{1,0:T(8,128)(2,1)}, bf16[1280,256]{1,0:T(8,128)(2,1)S(1)}, u32[]{:S(2)}, u32[]{:S(2)}) collective-permute-start(bf16[1280,256]{1,0:T(8,128)(2,1)} %collective-permute-done.5), channel_id=1, source_target_pairs={{8,0},{16,24},{9,1},{17,25},{10,2},{18,26},{11,3},{19,27},{12,4},{... | collective-permute-start | bytes 1966088 | tf_op jit(solution)/shard_map/ppermute | solution.py:238
  155.7 73.0 %collective-permute-start.19 = (bf16[3968,256]{1,0:T(8,128)(2,1)}, bf16[3968,256]{1,0:T(8,128)(2,1)}, u32[]{:S(2)}, u32[]{:S(2)}) collective-permute-start(bf16[3968,256]{1,0:T(8,128)(2,1)} %get-tuple-element.132), channel_id=1, source_target_pairs={{0,8},{8,0},{16,24},{24,16},{1,9},{9,1},{17,25},{25,17},{2,10},{10... | collective-permute-start | bytes 6094856 | tf_op jit(solution)/shard_map/ppermute | solution.py:238
  164.1 61.6 %collective-permute-start.16 = (bf16[2560,256]{1,0:T(8,128)(2,1)}, bf16[2560,256]{1,0:T(8,128)(2,1)}, u32[]{:S(2)}, u32[]{:S(2)}) collective-permute-start(bf16[2560,256]{1,0:T(8,128)(2,1)} %collective-permute-done.13), channel_id=1, source_target_pairs={{8,0},{16,24},{9,1},{17,25},{10,2},{18,26},{11,3},{19,27},{12,4},{... | collective-permute-start | bytes 3932168 | tf_op jit(solution)/shard_map/ppermute | solution.py:238
  167.3 77.0 %collective-permute-start.12 = (bf16[88,128,128]{2,1,0:T(8,128)(2,1)}, bf16[88,128,128]{2,1,0:T(8,128)(2,1)}, u32[]{:S(2)}, u32[]{:S(2)}) collective-permute-start(bf16[88,128,128]{2,1,0:T(8,128)(2,1)} %copy-done.5), channel_id=1, source_target_pairs={{0,4},{4,0},{1,5},{5,1},{2,6},{6,2},{3,7},{7,3},{8,12},{12,8},{9,1... | collective-permute-start | bytes 8650760 | tf_op jit(solution)/shard_map/ppermute | solution.py:238
  177.2 68.6 %collective-permute-start.18 = (bf16[3968,256]{1,0:T(8,128)(2,1)}, bf16[3968,256]{1,0:T(8,128)(2,1)}, u32[]{:S(2)}, u32[]{:S(2)}) collective-permute-start(bf16[3968,256]{1,0:T(8,128)(2,1)} %get-tuple-element.132), channel_id=1, source_target_pairs={{8,16},{16,8},{9,17},{17,9},{10,18},{18,10},{11,19},{19,11},{12,20... | collective-permute-start | bytes 6094856 | tf_op jit(solution)/shard_map/ppermute | solution.py:238
  187.6 85.3 %collective-permute-start.17 = (bf16[3968,256]{1,0:T(8,128)(2,1)}, bf16[3968,256]{1,0:T(8,128)(2,1)}, u32[]{:S(2)}, u32[]{:S(2)}) collective-permute-start(bf16[3968,256]{1,0:T(8,128)(2,1)} %get-tuple-element.152), channel_id=1, source_target_pairs={{8,16},{16,8},{9,17},{17,9},{10,18},{18,10},{11,19},{19,11},{12,20... | collective-permute-start | bytes 6094856 | tf_op jit(solution)/shard_map/ppermute | solution.py:238
  233.4 67.5 %copy-start.6 = (bf16[512,3968]{1,0:T(8,128)(2,1)}, bf16[512,3968]{1,0:T(8,128)(2,1)S(1)}, u32[]{:S(2)}) copy-start(bf16[512,3968]{1,0:T(8,128)(2,1)S(1)} %get-tuple-element.147) | copy-start | bytes 12189700
  244.4 26.1 %collective-permute-start.22 = (bf16[4608,128]{1,0:T(8,128)(2,1)S(1)}, bf16[4608,128]{1,0:T(8,128)(2,1)S(1)}, u32[]{:S(2)}, u32[]{:S(2)}) collective-permute-start(bf16[4608,128]{1,0:T(8,128)(2,1)S(1)} %copy-done.41), channel_id=1, source_target_pairs={{0,4},{4,0},{1,5},{5,1},{2,6},{6,2},{3,7},{7,3},{8,12},{12,8},{9,1... | collective-permute-start | bytes 3538952 | tf_op jit(solution)/shard_map/ppermute | solution.py:238
  245.7 49.3 %collective-permute-start.20 = (bf16[3968,256]{1,0:T(8,128)(2,1)}, bf16[3968,256]{1,0:T(8,128)(2,1)S(1)}, u32[]{:S(2)}, u32[]{:S(2)}) collective-permute-start(bf16[3968,256]{1,0:T(8,128)(2,1)} %collective-permute-done.18), channel_id=1, source_target_pairs={{8,0},{16,24},{9,1},{17,25},{10,2},{18,26},{11,3},{19,27},{12,4},{... | collective-permute-start | bytes 6094856 | tf_op jit(solution)/shard_map/ppermute | solution.py:238
  247.0 51.4 %collective-permute-start.21 = (bf16[3968,256]{1,0:T(8,128)(2,1)}, bf16[3968,256]{1,0:T(8,128)(2,1)}, u32[]{:S(2)}, u32[]{:S(2)}) collective-permute-start(bf16[3968,256]{1,0:T(8,128)(2,1)} %collective-permute-done.19), channel_id=1, source_target_pairs={{8,16},{16,8},{9,17},{17,9},{10,18},{18,10},{11,19},{19,11},{12,20... | collective-permute-start | bytes 6094856 | tf_op jit(solution)/shard_map/ppermute | solution.py:238
  270.5 71.9 %collective-permute-start.23 = (bf16[104,128,128]{2,1,0:T(8,128)(2,1)S(1)}, bf16[104,128,128]{2,1,0:T(8,128)(2,1)S(1)}, u32[]{:S(2)}, u32[]{:S(2)}) collective-permute-start(bf16[104,128,128]{2,1,0:T(8,128)(2,1)S(1)} %copy-done.4), channel_id=1, source_target_pairs={{0,4},{4,0},{1,5},{5,1},{2,6},{6,2},{3,7},{7,3},{8,12},{12,8},{9,1... | collective-permute-start | bytes 10223624 | tf_op jit(solution)/shard_map/ppermute | solution.py:238
  272.9 29.3 %collective-permute-start.26 = (bf16[2304,256]{1,0:T(8,128)(2,1)S(1)}, bf16[2304,256]{1,0:T(8,128)(2,1)S(1)}, u32[]{:S(2)}, u32[]{:S(2)}) collective-permute-start(bf16[2304,256]{1,0:T(8,128)(2,1)S(1)} %get-tuple-element.154), channel_id=1, source_target_pairs={{8,16},{16,8},{9,17},{17,9},{10,18},{18,10},{11,19},{19,11},{12,20... | collective-permute-start | bytes 3538952 | tf_op jit(solution)/shard_map/ppermute | solution.py:238
  273.6 65.0 %collective-permute-start.25 = (bf16[3968,256]{1,0:T(8,128)(2,1)}, bf16[3968,256]{1,0:T(8,128)(2,1)}, u32[]{:S(2)}, u32[]{:S(2)}) collective-permute-start(bf16[3968,256]{1,0:T(8,128)(2,1)} %get-tuple-element.152), channel_id=1, source_target_pairs={{0,8},{8,0},{16,24},{24,16},{1,9},{9,1},{17,25},{25,17},{2,10},{10... | collective-permute-start | bytes 6094856 | tf_op jit(solution)/shard_map/ppermute | solution.py:238
  295.0 80.3 %collective-permute-start.29 = (bf16[3968,256]{1,0:T(8,128)(2,1)}, bf16[3968,256]{1,0:T(8,128)(2,1)}, u32[]{:S(2)}, u32[]{:S(2)}) collective-permute-start(bf16[3968,256]{1,0:T(8,128)(2,1)} %collective-permute-done.17), channel_id=1, source_target_pairs={{8,0},{16,24},{9,1},{17,25},{10,2},{18,26},{11,3},{19,27},{12,4},{... | collective-permute-start | bytes 6094856 | tf_op jit(solution)/shard_map/ppermute | solution.py:238
  298.5 4.6 collective-permute-start.28
  338.6 45.4 %slice-start = ((s8[5373952]{0:T(1024)(128)(4,1)}), s8[4194304]{0:T(1024)(128)(4,1)S(1)}, s32[]{:S(2)}) async-start(s8[5373952]{0:T(1024)(128)(4,1)} %bitcast.247), calls=%async_computation.6 | async-start | bytes 8388608
  342.5 54.5 %collective-permute-start.27 = (bf16[2304,256]{1,0:T(8,128)(2,1)S(1)}, bf16[2304,256]{1,0:T(8,128)(2,1)}, u32[]{:S(2)}, u32[]{:S(2)}) collective-permute-start(bf16[2304,256]{1,0:T(8,128)(2,1)S(1)} %get-tuple-element.154), channel_id=1, source_target_pairs={{0,8},{24,16},{1,9},{25,17},{2,10},{26,18},{3,11},{27,19},{4,12},{... | collective-permute-start | bytes 3538952 | tf_op jit(solution)/shard_map/ppermute | solution.py:238
  378.2 37.4 %collective-permute-start.30 = (bf16[3968,256]{1,0:T(8,128)(2,1)}, bf16[3968,256]{1,0:T(8,128)(2,1)}, u32[]{:S(2)}, u32[]{:S(2)}) collective-permute-start(bf16[3968,256]{1,0:T(8,128)(2,1)} %collective-permute-done.25), channel_id=1, source_target_pairs={{8,16},{16,8},{9,17},{17,9},{10,18},{18,10},{11,19},{19,11},{12,20... | collective-permute-start | bytes 6094856 | tf_op jit(solution)/shard_map/ppermute | solution.py:238
  380.1 41.6 %collective-permute-start.36 = (bf16[3968,256]{1,0:T(8,128)(2,1)}, bf16[3968,256]{1,0:T(8,128)(2,1)}, u32[]{:S(2)}, u32[]{:S(2)}) collective-permute-start(bf16[3968,256]{1,0:T(8,128)(2,1)} %collective-permute-done.21), channel_id=1, source_target_pairs={{8,0},{16,24},{9,1},{17,25},{10,2},{18,26},{11,3},{19,27},{12,4},{... | collective-permute-start | bytes 6094856 | tf_op jit(solution)/shard_map/ppermute | solution.py:238
  384.0 134.4 %collective-permute-start.24 = (bf16[164,128,128]{2,1,0:T(8,128)(2,1)S(1)}, bf16[164,128,128]{2,1,0:T(8,128)(2,1)S(1)}, u32[]{:S(2)}, u32[]{:S(2)}) collective-permute-start(bf16[164,128,128]{2,1,0:T(8,128)(2,1)S(1)} %bitcast.248), channel_id=1, source_target_pairs={{0,4},{4,0},{1,5},{5,1},{2,6},{6,2},{3,7},{7,3},{8,12},{12,8},{9,1... | collective-permute-start | bytes 16121864 | tf_op jit(solution)/shard_map/ppermute | solution.py:238
  397.0 19.8 %collective-permute-start.31 = (bf16[2304,256]{1,0:T(8,128)(2,1)}, bf16[2304,256]{1,0:T(8,128)(2,1)S(1)}, u32[]{:S(2)}, u32[]{:S(2)}) collective-permute-start(bf16[2304,256]{1,0:T(8,128)(2,1)} %collective-permute-done.27), channel_id=1, source_target_pairs={{8,16},{16,8},{9,17},{17,9},{10,18},{18,10},{11,19},{19,11},{12,20... | collective-permute-start | bytes 3538952 | tf_op jit(solution)/shard_map/ppermute | solution.py:238
  402.8 107.8 %collective-permute-start.37 = (bf16[104,128,128]{2,1,0:T(8,128)(2,1)S(1)}, bf16[104,128,128]{2,1,0:T(8,128)(2,1)S(1)}, u32[]{:S(2)}, u32[]{:S(2)}) collective-permute-start(bf16[104,128,128]{2,1,0:T(8,128)(2,1)S(1)} %copy-done.2), channel_id=1, source_target_pairs={{0,8},{24,16},{1,9},{25,17},{2,10},{26,18},{3,11},{27,19},{4,12},{... | collective-permute-start | bytes 10223624 | tf_op jit(solution)/shard_map/ppermute | solution.py:238
  415.6 216.2 %collective-permute-start = (s32[16,2]{0,1:T(2,128)S(1)}, s32[16,2]{0,1:T(2,128)S(1)}, u32[]{:S(2)}, u32[]{:S(2)}) collective-permute-start(s32[16,2]{0,1:T(2,128)S(1)} %copy-done.65), channel_id=1, source_target_pairs={{0,4},{4,0},{1,5},{5,1},{2,6},{6,2},{3,7},{7,3},{8,12},{12,8},{9,1... | collective-permute-start | bytes 392 | tf_op jit(solution)/shard_map/ppermute | solution.py:447
  416.8 41.9 %copy-start.24 = (bf16[2304,256]{1,0:T(8,128)(2,1)}, bf16[2304,256]{1,0:T(8,128)(2,1)S(1)}, u32[]{:S(2)}) copy-start(bf16[2304,256]{1,0:T(8,128)(2,1)S(1)} %collective-permute-done.31) | copy-start | bytes 3538948
  416.8 90.1 %collective-permute-start.39 = (bf16[3968,256]{1,0:T(8,128)(2,1)}, bf16[3968,256]{1,0:T(8,128)(2,1)}, u32[]{:S(2)}, u32[]{:S(2)}) collective-permute-start(bf16[3968,256]{1,0:T(8,128)(2,1)} %collective-permute-done.30), channel_id=1, source_target_pairs={{8,0},{16,24},{9,1},{17,25},{10,2},{18,26},{11,3},{19,27},{12,4},{... | collective-permute-start | bytes 6094856 | tf_op jit(solution)/shard_map/ppermute | solution.py:238
  421.7 78.6 %collective-permute-start.32 = (bf16[2304,256]{1,0:T(8,128)(2,1)}, bf16[2304,256]{1,0:T(8,128)(2,1)}, u32[]{:S(2)}, u32[]{:S(2)}) collective-permute-start(bf16[2304,256]{1,0:T(8,128)(2,1)} %get-tuple-element.159), channel_id=1, source_target_pairs={{0,8},{24,16},{1,9},{25,17},{2,10},{26,18},{3,11},{27,19},{4,12},{... | collective-permute-start | bytes 3538952 | tf_op jit(solution)/shard_map/ppermute | solution.py:238
  530.2 28.6 %collective-permute-start.40 = (bf16[2304,256]{1,0:T(8,128)(2,1)}, bf16[2304,256]{1,0:T(8,128)(2,1)}, u32[]{:S(2)}, u32[]{:S(2)}) collective-permute-start(bf16[2304,256]{1,0:T(8,128)(2,1)} %collective-permute-done.32), channel_id=1, source_target_pairs={{8,16},{16,8},{9,17},{17,9},{10,18},{18,10},{11,19},{19,11},{12,20... | collective-permute-start | bytes 3538952 | tf_op jit(solution)/shard_map/ppermute | solution.py:238
  531.9 71.0 %collective-permute-start.38 = (bf16[104,128,128]{2,1,0:T(8,128)(2,1)S(1)}, bf16[104,128,128]{2,1,0:T(8,128)(2,1)S(1)}, u32[]{:S(2)}, u32[]{:S(2)}) collective-permute-start(bf16[104,128,128]{2,1,0:T(8,128)(2,1)S(1)} %collective-permute-done.23.source), channel_id=1, source_target_pairs={{0,8},{24,16},{1,9},{25,17},{2,10},{26,18},{3,11},{27,19},{4,12},{... | collective-permute-start | bytes 10223624 | tf_op jit(solution)/shard_map/ppermute | solution.py:238
  555.9 72.3 %collective-permute-start.33 = (f32[3,1024,128]{1,2,0:T(8,128)}, f32[3,1024,128]{1,2,0:T(8,128)}, u32[]{:S(2)}, u32[]{:S(2)}) collective-permute-start(f32[3,1024,128]{1,2,0:T(8,128)} %constant_dynamic-slice_fusion.7), channel_id=1, source_target_pairs={{0,1},{1,0},{2,3},{3,2},{4,5},{5,4},{6,7},{7,6},{8,9},{9,8},{10,11... | collective-permute-start | bytes 4718600 | tf_op jit(solution)/shard_map/ppermute | solution.py:196
  615.0 10.9 %collective-permute-start.41 = (f32[3,1024,128]{1,2,0:T(8,128)S(1)}, f32[3,1024,128]{1,2,0:T(8,128)S(1)}, u32[]{:S(2)}, u32[]{:S(2)}) collective-permute-start(f32[3,1024,128]{1,2,0:T(8,128)S(1)} %constant_dynamic-slice_fusion.5), channel_id=1, source_target_pairs={{0,1},{1,0},{2,3},{3,2},{4,5},{5,4},{6,7},{7,6},{8,9},{9,8},{10,11... | collective-permute-start | bytes 4718600 | tf_op jit(solution)/shard_map/ppermute | solution.py:196
  625.5 7.0 collective-permute-start.50
  627.1 20.7 %collective-permute-start.42 = (f32[3,64,1024]{2,1,0:T(8,128)}, f32[3,64,1024]{2,1,0:T(8,128)}, u32[]{:S(2)}, u32[]{:S(2)}) collective-permute-start(f32[3,64,1024]{2,1,0:T(8,128)} %dynamic-slice_bitcast_fusion), channel_id=1, source_target_pairs={{0,4},{4,0},{1,5},{5,1},{2,6},{6,2},{3,7},{7,3},{8,12},{12,8},{9,1... | collective-permute-start | bytes 2359304 | tf_op jit(solution)/shard_map/ppermute | solution.py:196
  630.8 33.9 %collective-permute-start.34 = (f32[3,64,1024]{2,1,0:T(8,128)}, f32[3,64,1024]{2,1,0:T(8,128)}, u32[]{:S(2)}, u32[]{:S(2)}) collective-permute-start(f32[3,64,1024]{2,1,0:T(8,128)} %dynamic-slice_bitcast_fusion.1), channel_id=1, source_target_pairs={{0,4},{4,0},{1,5},{5,1},{2,6},{6,2},{3,7},{7,3},{8,12},{12,8},{9,1... | collective-permute-start | bytes 2359304 | tf_op jit(solution)/shard_map/ppermute | solution.py:196
  649.1 18.6 %collective-permute-start.43 = (f32[3,32,1024]{2,1,0:T(8,128)S(1)}, f32[3,32,1024]{2,1,0:T(8,128)S(1)}, u32[]{:S(2)}, u32[]{:S(2)}) collective-permute-start(f32[3,32,1024]{2,1,0:T(8,128)S(1)} %constant_dynamic-slice_fusion.4), channel_id=1, source_target_pairs={{0,2},{2,0},{1,3},{3,1},{4,6},{6,4},{5,7},{7,5},{8,10},{10,8},{9,1... | collective-permute-start | bytes 1179656 | tf_op jit(solution)/shard_map/ppermute | solution.py:196
  650.8 18.6 %collective-permute-start.51 = (f32[1,64,1024]{2,1,0:T(8,128)S(1)}, f32[1,64,1024]{2,1,0:T(8,128)S(1)}, u32[]{:S(2)}, u32[]{:S(2)}) collective-permute-start(f32[1,64,1024]{2,1,0:T(8,128)S(1)} %dynamic-slice_bitcast_fusion.2), channel_id=1, source_target_pairs={{0,4},{4,0},{1,5},{5,1},{2,6},{6,2},{3,7},{7,3},{8,12},{12,8},{9,1... | collective-permute-start | bytes 786440 | tf_op jit(solution)/shard_map/ppermute | solution.py:196
  665.9 11.1 %collective-permute-start.35 = (f32[3,32,1024]{2,1,0:T(8,128)S(1)}, f32[3,32,1024]{2,1,0:T(8,128)S(1)}, u32[]{:S(2)}, u32[]{:S(2)}) collective-permute-start(f32[3,32,1024]{2,1,0:T(8,128)S(1)} %constant_dynamic-slice_fusion.6), channel_id=1, source_target_pairs={{0,2},{2,0},{1,3},{3,1},{4,6},{6,4},{5,7},{7,5},{8,10},{10,8},{9,1... | collective-permute-start | bytes 1179656 | tf_op jit(solution)/shard_map/ppermute | solution.py:196
  667.8 13.6 %collective-permute-start.44 = (f32[3,32,1024]{2,1,0:T(8,128)S(1)}, f32[3,32,1024]{2,1,0:T(8,128)S(1)}, u32[]{:S(2)}, u32[]{:S(2)}) collective-permute-start(f32[3,32,1024]{2,1,0:T(8,128)S(1)} %dynamic-slice_add_fusion.4), channel_id=1, source_target_pairs={{8,0},{16,24},{9,1},{17,25},{10,2},{18,26},{11,3},{19,27},{12,4},{... | collective-permute-start | bytes 1179656 | tf_op jit(solution)/shard_map/ppermute | solution.py:440
  669.5 13.2 %collective-permute-start.52 = (f32[1,32,1024]{2,1,0:T(8,128)S(1)}, f32[1,32,1024]{2,1,0:T(8,128)S(1)}, u32[]{:S(2)}, u32[]{:S(2)}) collective-permute-start(f32[1,32,1024]{2,1,0:T(8,128)S(1)} %constant_dynamic-slice_fusion.3), channel_id=1, source_target_pairs={{0,2},{2,0},{1,3},{3,1},{4,6},{6,4},{5,7},{7,5},{8,10},{10,8},{9,1... | collective-permute-start | bytes 393224 | tf_op jit(solution)/shard_map/ppermute | solution.py:196
  681.5 14.2 %collective-permute-start.45 = (f32[3,32,1024]{2,1,0:T(8,128)S(1)}, f32[3,32,1024]{2,1,0:T(8,128)S(1)}, u32[]{:S(2)}, u32[]{:S(2)}) collective-permute-start(f32[3,32,1024]{2,1,0:T(8,128)S(1)} %fusion.53), channel_id=1, source_target_pairs={{0,8},{8,0},{16,24},{24,16},{1,9},{9,1},{17,25},{25,17},{2,10},{10... | collective-permute-start | bytes 1179656 | tf_op jit(solution)/shard_map/ppermute | solution.py:247
  682.0 17.3 %collective-permute-start.46 = (f32[3,32,1024]{2,1,0:T(8,128)S(1)}, f32[3,32,1024]{2,1,0:T(8,128)S(1)}, u32[]{:S(2)}, u32[]{:S(2)}) collective-permute-start(f32[3,32,1024]{2,1,0:T(8,128)S(1)} %fusion.53), channel_id=1, source_target_pairs={{8,16},{16,8},{9,17},{17,9},{10,18},{18,10},{11,19},{19,11},{12,20... | collective-permute-start | bytes 1179656 | tf_op jit(solution)/shard_map/ppermute | solution.py:248
  682.8 11.0 %collective-permute-start.53 = (f32[40,1024]{1,0:T(8,128)S(1)}, f32[40,1024]{1,0:T(8,128)S(1)}, u32[]{:S(2)}, u32[]{:S(2)}) collective-permute-start(f32[40,1024]{1,0:T(8,128)S(1)} %get-tuple-element.220), channel_id=1, source_target_pairs={{0,8},{8,0},{16,24},{24,16},{1,9},{9,1},{17,25},{25,17},{2,10},{10... | collective-permute-start | bytes 491528 | tf_op jit(solution)/shard_map/ppermute | solution.py:247
  685.8 8.6 %collective-permute-start.54 = (f32[40,1024]{1,0:T(8,128)S(1)}, f32[40,1024]{1,0:T(8,128)S(1)}, u32[]{:S(2)}, u32[]{:S(2)}) collective-permute-start(f32[40,1024]{1,0:T(8,128)S(1)} %get-tuple-element.220), channel_id=1, source_target_pairs={{8,16},{16,8},{9,17},{17,9},{10,18},{18,10},{11,19},{19,11},{12,20... | collective-permute-start | bytes 491528 | tf_op jit(solution)/shard_map/ppermute | solution.py:248
  693.7 4.3 collective-permute-start.56
  694.4 11.0 %collective-permute-start.55 = (f32[40,1024]{1,0:T(8,128)S(1)}, f32[40,1024]{1,0:T(8,128)S(1)}, u32[]{:S(2)}, u32[]{:S(2)}) collective-permute-start(f32[40,1024]{1,0:T(8,128)S(1)} %collective-permute-done.54), channel_id=1, source_target_pairs={{8,0},{16,24},{9,1},{17,25},{10,2},{18,26},{11,3},{19,27},{12,4},{... | collective-permute-start | bytes 491528 | tf_op jit(solution)/shard_map/ppermute | solution.py:250
  695.7 9.7 %collective-permute-start.48 = (f32[3,32,1024]{2,1,0:T(8,128)S(1)}, f32[3,32,1024]{2,1,0:T(8,128)S(1)}, u32[]{:S(2)}, u32[]{:S(2)}) collective-permute-start(f32[3,32,1024]{2,1,0:T(8,128)S(1)} %collective-permute-done.45), channel_id=1, source_target_pairs={{8,16},{16,8},{9,17},{17,9},{10,18},{18,10},{11,19},{19,11},{12,20... | collective-permute-start | bytes 1179656 | tf_op jit(solution)/shard_map/ppermute | solution.py:249
  698.0 12.6 %collective-permute-start.57 = (f32[40,1024]{1,0:T(8,128)S(1)}, f32[40,1024]{1,0:T(8,128)S(1)}, u32[]{:S(2)}, u32[]{:S(2)}) collective-permute-start(f32[40,1024]{1,0:T(8,128)S(1)} %collective-permute-done.56), channel_id=1, source_target_pairs={{8,0},{16,24},{9,1},{17,25},{10,2},{18,26},{11,3},{19,27},{12,4},{... | collective-permute-start | bytes 491528 | tf_op jit(solution)/shard_map/ppermute | solution.py:251
  699.3 19.5 %collective-permute-start.47 = (f32[3,32,1024]{2,1,0:T(8,128)S(1)}, f32[3,32,1024]{2,1,0:T(8,128)S(1)}, u32[]{:S(2)}, u32[]{:S(2)}) collective-permute-start(f32[3,32,1024]{2,1,0:T(8,128)S(1)} %collective-permute-done.46), channel_id=1, source_target_pairs={{8,0},{16,24},{9,1},{17,25},{10,2},{18,26},{11,3},{19,27},{12,4},{... | collective-permute-start | bytes 1179656 | tf_op jit(solution)/shard_map/ppermute | solution.py:250
  705.5 17.6 %collective-permute-start.49 = (f32[3,32,1024]{2,1,0:T(8,128)S(1)}, f32[3,32,1024]{2,1,0:T(8,128)S(1)}, u32[]{:S(2)}, u32[]{:S(2)}) collective-permute-start(f32[3,32,1024]{2,1,0:T(8,128)S(1)} %collective-permute-done.48), channel_id=1, source_target_pairs={{8,0},{16,24},{9,1},{17,25},{10,2},{18,26},{11,3},{19,27},{12,4},{... | collective-permute-start | bytes 1179656 | tf_op jit(solution)/shard_map/ppermute | solution.py:251
  732.6 3.0 collective-permute-start.58
  737.0 14.7 %collective-permute-start.59 = (f32[1,2,1,4,136,128]{5,4,3,2,1,0:T(8,128)S(1)}, f32[1,2,1,4,136,128]{5,4,3,2,1,0:T(8,128)S(1)}, u32[]{:S(2)}, u32[]{:S(2)}) collective-permute-start(f32[1,2,1,4,136,128]{5,4,3,2,1,0:T(8,128)S(1)} %constant_dynamic-slice_fusion.1), channel_id=1, source_target_pairs={{0,4},{4,0},{1,5},{5,1},{2,6},{6,2},{3,7},{7,3},{8,12},{12,8},{9,1... | collective-permute-start | bytes 1671176 | tf_op jit(solution)/shard_map/ppermute | solution.py:196
  751.8 7.9 %collective-permute-start.60 = (f32[1,1,1,4,136,128]{5,4,3,2,1,0:T(8,128)S(1)}, f32[1,1,1,4,136,128]{5,4,3,2,1,0:T(8,128)S(1)}, u32[]{:S(2)}, u32[]{:S(2)}) collective-permute-start(f32[1,1,1,4,136,128]{5,4,3,2,1,0:T(8,128)S(1)} %constant_dynamic-slice_fusion), channel_id=1, source_target_pairs={{0,2},{2,0},{1,3},{3,1},{4,6},{6,4},{5,7},{7,5},{8,10},{10,8},{9,1... | collective-permute-start | bytes 835592 | tf_op jit(solution)/shard_map/ppermute | solution.py:196
  (69 other events, 535.6 us)

commit v6 on v5

--- a/solution.py
+++ b/solution.py
@@ -201,46 +201,15 @@
     return lax.optimization_barrier((values, arrived))[0]
 
 
-class Transfers:
-    RATE = 1e5
-    SLOTS = 5
-    LATENCY = 2.0
-    STEP = 1.0
-
-    def __init__(self, depths):
-        self.depths = depths
-        self.listed = []
-        self.got = {}
-
-    def add(self, name, links, size, needs, make, axis, routes):
-        self.listed.append((name, links, CORES * size / self.RATE, needs, make, axis, routes))
-
-    def run(self):
-        now, free, ends, waiting = 0.0, {}, {}, list(self.listed)
-        while waiting:
-            flying = [t for t in self.listed if ends.get(t[0], -1.0) > now]
-            chosen = None
-            for t in waiting:
-                ready = all(ends.get(n, 1e9) <= now for n in t[3])
-                room_left = all(sum(link in f[1] for f in flying) < self.depths[link] for link in t[1])
-                if ready and room_left and len(flying) < self.SLOTS:
-                    chosen = t
-                    break
-            if chosen is None:
-                now = min(e for e in ends.values() if e > now)
-                continue
-            waiting.remove(chosen)
-            name, links, length, _, make, axis, routes = chosen
-            arrived = sorted((n for n in ends if ends[n] <= now), key=ends.get)[-self.SLOTS :]
-            values = make()
-            if arrived:
-                values = after(values, [self.got[n] for n in arrived])
-            self.got[name] = [lax.ppermute(v, axis, route) for v, route in zip(values, routes)]
-            now += self.STEP
-            end = max([now + self.LATENCY] + [free.get(link, 0.0) for link in links]) + length
-            for link in links:
-                free[link] = end
-            ends[name] = end + self.STEP
+class Lane:
+    def __init__(self, arrived=None):
+        self.arrived = arrived
+
+    def send(self, values, axis, routes):
+        if self.arrived is not None:
+            values = after(values, self.arrived)
+        self.arrived = [lax.ppermute(v, axis, route) for v, route in zip(values, routes)]
+        return self.arrived
 
 
 def along_line(block, inner):
@@ -292,9 +261,9 @@
 
     lent = columns * LENT[0] // LENT[1]
     kept = columns - lent
-    cuts = [0] + [kept * c // 9 for c in (1, 3, 6, 9)] + [kept + c for c in bounds(lent, 2)[1:]]
+    cuts = [0, kept // 3, kept, columns]
     widths = [b - a for a, b in zip(cuts[:-1], cuts[1:])]
-    streams = {"lent": (4, 6), "early": (0, 2), "late": (2, 4)}
+    slots = [room(w * row_blocks) for w in widths]
 
     def mask_of(owner):
         return lax.dynamic_slice_in_dim(tile_mask, owner * columns, columns, 1)
@@ -302,115 +271,74 @@
     def over_x(make):
         return [lax.ppermute(make((x + k) % wide), "x", turn(wide, k)) for k in range(1, wide)]
 
-    moves = Transfers({"x": 1, "in": 2, "out": 2, "mid": 2})
+    others = [(x + k) % wide for k in range(1, wide)]
     row_routes = [turn(wide, k) for k in range(1, wide)]
-    others = [(x + k) % wide for k in range(1, wide)]
-    slots_of = {n: room((cuts[b] - cuts[a]) * row_blocks) for n, (a, b) in streams.items()}
-    tile_bytes = blk * blk * 2
-    groups, packs = {}, {}
-
-    def planes_of(owner, first, last):
-        start = (owner * columns + cuts[first]) * blk
-        return lax.dynamic_slice_in_dim(planes, start, (cuts[last] - cuts[first]) * blk, 0)
-
-    def group(c):
-        if c not in groups:
-            name, first = next((n, a) for n, a, b in plane_moves if a <= c < b)
-            whole = jnp.zeros((widths[c] * blk, wide * own_planes), planes.dtype)
-            whole = lax.dynamic_update_slice_in_dim(whole, planes_of(x, c, c + 1), x * own_planes, 1)
+
+    def in_row_order(parts, dim):
+        ordered = []
+        for owner in range(wide):
+            chosen = parts[0]
             for k in range(1, wide):
-                part = moves.got[name][k - 1][(cuts[c] - cuts[first]) * blk : (cuts[c + 1] - cuts[first]) * blk]
-                whole = lax.dynamic_update_slice_in_dim(whole, part, ((x - k) % wide) * own_planes, 1)
-            groups[c] = whole
-        return groups[c]
-
-    def packed(name, owner, later):
-        low, high = (cuts[c] for c in streams[name])
-        mask = after(mask_of(owner)[:, low:high], moves.got[later])
-        return pack(hist, mask, owner * columns + low, slots_of[name])
-
-    plane_moves = [("planes0", 0, 1), ("planes1", 1, 2), ("planes2", 2, 4), ("planes4", 4, 6)]
-    source_of = ["planes0", "planes1", "planes2", "planes2", "planes4", "planes4"]
-
-    def add_planes(name, first, last):
-        size = (cuts[last] - cuts[first]) * blk * own_planes * 2 * len(others)
-        moves.add(
-            name, ["x"], size, [], lambda: [planes_of(o, first, last) for o in others], "x", row_routes
-        )
-
-    def add_tiles(name, later):
-        size = slots_of[name] * tile_bytes * len(others)
-        moves.add(
-            name, ["x"], size, [later], lambda: [packed(name, o, later) for o in others], "x", row_routes
-        )
-
-    def add_group(name, links, c, needs, make, routes):
-        size = widths[c] * blk * wide * own_planes * 2
-        moves.add(name, links, size, needs, lambda: [make()], "z", [routes])
-
-    moves.add("masks", ["x"], 0, [], lambda: [mask_of(o) for o in others], "x", row_routes)
-    for c in range(4):
-        add_group(f"out2{c}", ["out"], c, [f"far{c}"], lambda c=c: moves.got[f"far{c}"][0], OUTWARD)
-    for c in range(4):
-        add_group(f"out1{c}", ["out"], c, [f"mid{c}"], lambda c=c: moves.got[f"mid{c}"][0], OUTWARD)
-    for c in range(4):
-        add_group(f"near{c}", ["in", "out"], c, [source_of[c]], lambda c=c: group(c), NEAR)
-    for c in range(4):
-        add_group(f"mid{c}", ["mid"], c, [source_of[c]], lambda c=c: group(c), MIDDLE)
-    for c in range(4):
-        add_group(f"far{c}", ["mid"], c, [f"near{c}"], lambda c=c: moves.got[f"near{c}"][0], MIDDLE)
-    for c in (4, 5):
-        add_group(f"mid{c}", ["mid"], c, [source_of[c]], lambda c=c: group(c), MIDDLE)
-    for c in (4, 5):
-        add_group(f"far{c}", ["mid"], c, [f"near{c}"], lambda c=c: moves.got[f"near{c}"][0], MIDDLE)
-    for name, first, last in plane_moves[:3]:
-        add_planes(name, first, last)
-    moves.add(
-        "guests", ["in"], 0, ["masks", "planes0"],
-        lambda: [jnp.stack([mask_of(x)[:, kept:]] + [m[:, kept:] for m in moves.got["masks"]])], "z", [INWARD],
-    )
-    add_tiles("early", "planes0")
-    add_planes(*plane_moves[3])
-    add_tiles("lent", "planes1")
-    add_tiles("late", "planes2")
-    lent_bytes = slots_of["lent"] * tile_bytes
-    moves.add("loan0", ["in"], lent_bytes, ["near3"], lambda: [packed("lent", x, "planes2")], "z", [INWARD])
-    for c in (4, 5):
-        add_group(f"near{c}", ["in"], c, [source_of[c]], lambda c=c: group(c), INWARD)
-    moves.add(
-        "loan1", ["in"], lent_bytes * len(others), ["lent"],
-        lambda: moves.got["lent"], "z", [INWARD] * len(others),
-    )
-    moves.run()
-    got = moves.got
-    held = []
-    for c in range(6):
-        near, mid, far = got[f"near{c}"][0], got[f"mid{c}"][0], got[f"far{c}"][0]
-        if c < 4:
-            mid = jnp.where(inner, mid, got[f"out1{c}"][0])
-            far = jnp.where(inner, far, got[f"out2{c}"][0])
-        held.append([groups[c], near, mid, far])
-    masks = [mask_of(x)] + got["masks"]
-    guest_masks = got["guests"][0]
+                chosen = jnp.where((x - owner) % wide == k, parts[k], chosen)
+            ordered.append(chosen)
+        return jnp.concatenate(ordered, axis=dim)
+
+    def planes_of(owner, c):
+        return lax.dynamic_slice_in_dim(planes, (owner * columns + cuts[c]) * blk, widths[c] * blk, 0)
+
+    def packed(owner, c, later):
+        mask = after(mask_of(owner)[:, cuts[c] : cuts[c + 1]], later)
+        return pack(hist, mask, owner * columns + cuts[c], slots[c])
+
+    over_x = Lane()
+    groups = []
+    for c in range(3):
+        got = over_x.send([planes_of(o, c) for o in others], "x", row_routes)
+        groups.append(in_row_order([planes_of(x, c)] + got, 1))
+        if c == 0:
+            start = got
+            others_masks = [
+                lax.ppermute(after(mask_of(o), start), "x", r) for o, r in zip(others, row_routes)
+            ]
+    tiles = [None] * 3
+    for c in (0, 2, 1):
+        tiles[c] = over_x.send([packed(o, c, groups[0]) for o in others], "x", row_routes)
+
+    ends, middle = Lane(), Lane()
+    near, mid, far = [], [], []
+    for c in range(2):
+        near += ends.send([groups[c]], "z", [NEAR])
+        mid += middle.send([groups[c]], "z", [MIDDLE])
+    inward, outward = Lane(near[1:]), Lane(near[1:])
+    for c in range(2):
+        far += middle.send([near[c]], "z", [MIDDLE])
+    loans = inward.send([packed(x, 2, near[0])], "z", [INWARD])
+    near += inward.send([groups[2]], "z", [INWARD])
+    mid += middle.send([groups[2]], "z", [MIDDLE])
+    far += middle.send([near[2]], "z", [MIDDLE])
+    outer = [outward.send([v], "z", [OUTWARD])[0] for v in mid[:2] + far[:2]]
+    loans = loans + inward.send(tiles[2], "z", [INWARD] * len(others))
+    masks = [mask_of(x)] + others_masks
+    guest_masks = lax.ppermute(jnp.stack([m[:, kept:] for m in masks]), "z", INWARD)
+    held = [
+        [groups[c], near[c], jnp.where(inner, mid[c], outer[c]), jnp.where(inner, far[c], outer[2 + c])]
+        for c in range(2)
+    ]
+    held.append([groups[2], near[2], mid[2], far[2]])
 
     over = jnp.int32(0)
-    sessions = [[None] * 6 for _ in range(wide)]
-    for name, (first, last) in streams.items():
-        low, high = cuts[first], cuts[last]
+    sessions = [[None] * 3 for _ in range(wide)]
+    for c in range(3):
         for owner in range(wide):
-            count = jnp.sum(tile_mask[:, owner * columns + low : owner * columns + high])
-            over = jnp.maximum(over, (count > room((high - low) * row_blocks)).astype(jnp.int32))
-        parts = tuple(widths[first:last])
+            count = jnp.sum(tile_mask[:, owner * columns + cuts[c] : owner * columns + cuts[c + 1]])
+            over = jnp.maximum(over, (count > slots[c]).astype(jnp.int32))
         for k in range(wide):
-            mask = masks[k][:, low:high]
+            mask = masks[k][:, cuts[c] : cuts[c + 1]]
             if k == 0:
-                later = got[{"early": "near0", "lent": "near1", "late": "near2"}[name]]
-                sessions[k][first:last] = spread(hist, after(mask, later), x * columns + low, parts)
+                (sessions[k][c],) = spread(hist, after(mask, near[0]), x * columns + cuts[c], (widths[c],))
             else:
-                sessions[k][first:last] = spread(got[name][k - 1], mask, None, parts)
-    guests = [
-        spread(t, guest_masks[k], None, tuple(widths[4:])) for k, t in enumerate(got["loan0"] + got["loan1"])
-    ]
+                (sessions[k][c],) = spread(tiles[c][k - 1], mask, None, (widths[c],))
+    guests = [{2: spread(t, guest_masks[k], None, (widths[2],))[0]} for k, t in enumerate(loans)]
 
     def total(sources, chunks, s):
         found = []
@@ -420,23 +348,16 @@
                 term = jnp.dot(source[c], held[c][s], preferred_element_type=jnp.float32)
                 one = term if one is None else one + term
             found.append(one)
-        rows_in_order = []
-        for owner in range(wide):
-            part = found[0]
-            for k in range(1, wide):
-                part = jnp.where((x - owner) % wide == k, found[k], part)
-            rows_in_order.append(part)
-        return jnp.concatenate(rows_in_order)
+        return in_row_order(found, 0)
 
     def summed(totals):
         whole = scatter_sum(jnp.stack(totals), "core", 2)
         whole = jnp.swapaxes(whole, 1, 2)
         return scatter_sum(scatter_sum(whole, "x", 1), "y", 1)
 
-    every = range(6)
+    every = range(3)
     first_three = summed([total(sessions, every, s) for s in range(3)])
-    guest_chunks = [{4: g[0], 5: g[1]} for g in guests]
-    visitors = summed([total(guest_chunks, (4, 5), s) for s in (0, 2, 3)])
+    visitors = summed([total(guests, (2,), s) for s in (0, 2, 3)])
     visitors = lax.ppermute(visitors, "z", OUTWARD)
     early = first_three.at[1:].add(visitors[:2])
     early = jnp.stack(along_line(early, inner))

time: 779 us -> 641 us (0.82)
  starting transfers between devices: 146 us -> 80.4 us
  waiting for transfers between devices: 353 us -> 300 us
  matrix products: 137 us -> 119 us
  local copies, waits for them, and re-layouts: 48.6 us -> 34.3 us
  other arithmetic: 14.5 us -> 24.7 us
    ppermute x37 -> x23, starting transfers between devices: 121 us -> 56.8 us  [the longest x21 51.6 us: send(): lax.ppermute(v, axis, route)]
    ppermute x37 -> x23, waiting for transfers between devices: 264 us -> 216 us  [the longest x21 170 us: send(): lax.ppermute(v, axis, route)]
    dot_general x60 -> x30, matrix products: 137 us -> 119 us  [total(): term = jnp.dot(source[c], held[c][s], preferred_element_type=jnp.float32)]
    dynamic_update_slice x10 -> x0, local copies, waits for them, and re-layouts: 17.4 us -> none  [the longest x6 11.2 us: group(): lax.dynamic_update_slice_in_dim(whole, planes_of(x, c, c + 1), x * own_pl...]
    unnamed x144 -> x120, local copies, waits for them, and re-layouts: 10.8 us -> 17.2 us
  transfers between devices with their start and end apart: 61 -> 47, of which waited for: 26 -> 23; matrix products, arithmetic and copies ran while one was open for 24% -> 25% of each run, Pallas kernels for 5% -> 7%
where the time goes in v6:
time: 641 us; the launch traced here: 631 us
  waiting for transfers between devices  300 us (47%)
  matrix products  119 us (19%)
  starting transfers between devices  80.4 us (13%)
  Pallas kernels  53.2 us (8%)
  local copies, waits for them, and re-layouts  34.3 us (5%)
  other arithmetic  24.7 us (4%)
  between operations  19.4 us (3%)
    ppermute x21, waiting for transfers between devices, send(): lax.ppermute(v, axis, route)  170 us
    dot_general x30, matrix products, total(): term = jnp.dot(source[c], held[c][s], preferred_element_type=jnp.float32)  119 us
    ppermute x12, waiting for transfers between devices, scatter_sum(): total = total + lax.ppermute(part((here + k) % count), axis, turn(count, k))  53 us
    ppermute x21, starting transfers between devices, send(): lax.ppermute(v, axis, route)  51.6 us
    ppermute x1, waiting for transfers between devices, body(): lax.ppermute(after(mask_of(o), start), 'x', r)  44.2 us
    pallas_call x8, Pallas kernels, spread(): pl.pallas_call(functools.partial(spread_kernel, blk, row_blocks, parts, s...  26.5 us
    pallas_call x4, Pallas kernels, pack(): pl.pallas_call(functools.partial(pack_kernel, blk, row_blocks, columns, s...  17.5 us
    unnamed x120, local copies, waits for them, and re-layouts  17.2 us
  transfers between devices with their start and end apart: 47, of which 23 were waited for; matrix products, arithmetic and copies ran while one was open for 25% of the time, Pallas kernels for 7%

profile of v6, /device:TPU:0, one launch (start us, length us, event | category | flops | bytes accessed | tf_op | source)
XLA Modules:
  0.0 630.7 jit_solution(1701672747916957256)
XLA Ops:
  7.8 3.0 collective-permute-start.1
  10.8 3.0 constant_dynamic-slice_fusion.9
  13.8 18.8 %collective-permute-done.1 = bf16[3840,128]{1,0:T(8,128)(2,1)S(1)} collective-permute-done((bf16[3840,128]{1,0:T(8,128)(2,1)S(1)}, bf16[3840,128]{1,0:T(8,128)(2,1)S(1)}, u32[]{:S(2)}, u32[]{:S(2)}) %collective-permute-start.1) | collective-permute-done | bytes 983072 | tf_op jit(solution)/shard_map/ppermute | solution.py:211
  41.1 37.0 %collective-permute-done.3 = bf16[7936,128]{1,0:T(8,128)(2,1)S(1)} collective-permute-done((bf16[7936,128]{1,0:T(8,128)(2,1)}, bf16[7936,128]{1,0:T(8,128)(2,1)S(1)}, u32[]{:S(2)}, u32[]{:S(2)}) %collective-permute-start.3) | collective-permute-done | bytes 2031648 | tf_op jit(solution)/shard_map/ppermute | solution.py:211
  86.4 3.3 collective-permute-start.9
  97.7 3.8 pack_tiles.4
  101.5 15.2 %collective-permute-done.4 = bf16[4608,128]{1,0:T(8,128)(2,1)} collective-permute-done((bf16[4608,128]{1,0:T(8,128)(2,1)S(1)}, bf16[4608,128]{1,0:T(8,128)(2,1)}, u32[]{:S(2)}, u32[]{:S(2)}) %collective-permute-start.4) | collective-permute-done | bytes 1179680 | tf_op jit(solution)/shard_map/ppermute | solution.py:211
  124.0 4.2 pack_tiles.6
  128.3 5.3 pack_tiles.5
  133.6 44.2 %collective-permute-done.2 = s32[4,128]{1,0:T(4,128)S(1)} collective-permute-done((s32[4,128]{1,0:T(4,128)S(1)}, s32[4,128]{1,0:T(4,128)S(1)}, u32[]{:S(2)}, u32[]{:S(2)}) %collective-permute-start.2) | collective-permute-done | bytes 2080 | tf_op jit(solution)/shard_map/ppermute | solution.py:301
  180.7 4.1 collective-permute-start.22
  187.0 3.0 spread_tiles.13
  192.1 4.1 pack_tiles.7
  196.5 4.2 spread_tiles.12
  200.7 3.2 copy-done
  204.2 6.1 collective-permute-start.10
  210.4 3.5 spread_tiles.11
  218.2 3.9 fusion.26
  227.1 29.9 %collective-permute-done.13 = bf16[3840,256]{1,0:T(8,128)(2,1)} collective-permute-done((bf16[3840,256]{1,0:T(8,128)(2,1)}, bf16[3840,256]{1,0:T(8,128)(2,1)}, u32[]{:S(2)}, u32[]{:S(2)}) %collective-permute-start.13) | collective-permute-done | bytes 1966112 | tf_op jit(solution)/shard_map/ppermute | solution.py:211
  261.5 16.4 %collective-permute-done.10.source = bf16[104,128,128]{2,1,0:T(8,128)(2,1)} collective-permute-done((bf16[104,128,128]{2,1,0:T(8,128)(2,1)}, bf16[104,128,128]{2,1,0:T(8,128)(2,1)}, u32[]{:S(2)}, u32[]{:S(2)}) %collective-permute-start.10) | collective-permute-done | bytes 3407904 | tf_op jit(solution)/shard_map/ppermute | solution.py:211
  277.9 6.3 collective-permute-start.11
  292.0 5.3 fusion.36
  297.3 3.0 spread_tiles.8
  300.3 3.6 spread_tiles.10
  312.2 17.2 %collective-permute-done.11 = bf16[4608,256]{1,0:T(8,128)(2,1)} collective-permute-done((bf16[4608,256]{1,0:T(8,128)(2,1)}, bf16[4608,256]{1,0:T(8,128)(2,1)}, u32[]{:S(2)}, u32[]{:S(2)}) %collective-permute-start.11) | collective-permute-done | bytes 2359328 | tf_op jit(solution)/shard_map/ppermute | solution.py:211
  329.4 6.1 collective-permute-start.23
  337.6 3.1 fusion.37
  340.7 4.3 collective-permute-done.15
  346.4 3.6 fusion.11
  350.0 3.9 fusion.35
  353.9 5.3 fusion.4
  359.3 28.7 %collective-permute-done.34 = bf16[3840,256]{1,0:T(8,128)(2,1)} collective-permute-done((bf16[3840,256]{1,0:T(8,128)(2,1)}, bf16[3840,256]{1,0:T(8,128)(2,1)}, u32[]{:S(2)}, u32[]{:S(2)}) %collective-permute-start.34) | collective-permute-done | bytes 1966112 | tf_op jit(solution)/shard_map/ppermute | solution.py:211
  391.4 4.5 fusion.39
  395.9 4.0 fusion.38
  399.9 3.6 fusion.13
  403.5 4.5 spread_tiles.9
  408.1 3.2 copy-done.2
  411.3 7.1 %fusion.27 = f32[512,256]{0,1:T(8,128)} fusion(bf16[512,7936]{1,0:T(8,128)(2,1)} %copy-done.2, bf16[7936,128]{1,0:T(8,128)(2,1)} %copy-done.19, bf16[7936,128]{1,0:T(8,128)(2,1)S(1)} %copy-done.18), kind=kOutput, calls=%fused_computation.174 | convolution fusion | flops 2088501248 | bytes 12713984 | tf_op jit(solution)/shard_map/dot_general | solution.py:348
  418.4 7.6 %fusion.5 = f32[512,256]{0,1:T(8,128)} fusion(bf16[512,7936]{1,0:T(8,128)(2,1)} %copy-done.2, bf16[7936,256]{1,0:T(8,128)(2,1)} %collective-permute-done.14, bf16[7936,256]{1,0:T(8,128)(2,1)} %collective-permute-done.15, pred[]{:T(512)S(6)} %or.3), kind=kOutput, calls=%fused_computation.40 | convolution fusion | flops 2082406400 | bytes 16777216 | tf_op jit(solution)/shard_map/dot_general | solution.py:348
  426.1 3.4 broadcast_select_fusion.29
  431.9 6.8 %fusion.34 = f32[512,256]{0,1:T(8,128)S(1)} fusion(bf16[512,7936]{1,0:T(8,128)(2,1)} %copy-done.2, bf16[7936,256]{1,0:T(8,128)(2,1)} %collective-permute-done.9), kind=kOutput, calls=%fused_computation.181 | convolution fusion | flops 2080374784 | bytes 12713984 | tf_op jit(solution)/shard_map/dot_general | solution.py:348
  438.8 2.9 broadcast_select_fusion.30
  444.6 4.4 fusion.40
  454.2 3.1 broadcast_select_fusion.27
  462.6 3.2 fusion.41
  465.9 3.2 broadcast_select_fusion.26
  472.5 4.4 fusion.43
  476.9 3.9 fusion.42
  480.8 5.3 fusion.6
  486.2 3.3 fusion.15
  489.4 6.9 %fusion.7 = f32[512,256]{0,1:T(8,128)S(1)} fusion(bf16[512,7936]{1,0:T(8,128)(2,1)} %copy-done.2, bf16[7936,256]{1,0:T(8,128)(2,1)} %collective-permute-done.17, bf16[7936,256]{1,0:T(8,128)(2,1)} %collective-permute-done.35, pred[]{:T(512)S(6)} %or.3), kind=kOutput, calls=%fused_computation.42 | convolution fusion | flops 2082406400 | bytes 16777216 | tf_op jit(solution)/shard_map/dot_general | solution.py:348
  503.3 14.5 %collective-permute-done.26 = f32[3,64,1024]{2,1,0:T(8,128)S(1)} collective-permute-done((f32[3,64,1024]{2,1,0:T(8,128)S(1)}, f32[3,64,1024]{2,1,0:T(8,128)S(1)}, u32[]{:S(2)}, u32[]{:S(2)}) %collective-permute-start.26) | collective-permute-done | bytes 786464 | tf_op jit(solution)/shard_map/ppermute | solution.py:196
  521.0 9.0 %collective-permute-done.27 = f32[3,32,1024]{2,1,0:T(8,128)S(1)} collective-permute-done((f32[3,32,1024]{2,1,0:T(8,128)S(1)}, f32[3,32,1024]{2,1,0:T(8,128)S(1)}, u32[]{:S(2)}, u32[]{:S(2)}) %collective-permute-start.27) | collective-permute-done | bytes 393248 | tf_op jit(solution)/shard_map/ppermute | solution.py:196
  531.4 5.2 collective-permute-done.21
  538.3 4.1 collective-permute-done.28
  544.3 4.2 collective-permute-start.39
  549.3 5.1 collective-permute-done.39
  561.2 4.2 collective-permute-done.41
  566.8 4.8 collective-permute-done.43
  571.6 8.3 %collective-permute-done.31 = f32[3,32,1024]{2,1,0:T(8,128)S(1)} collective-permute-done((f32[3,32,1024]{2,1,0:T(8,128)S(1)}, f32[3,32,1024]{2,1,0:T(8,128)S(1)}, u32[]{:S(2)}, u32[]{:S(2)}) %collective-permute-start.31) | collective-permute-done | bytes 393248 | tf_op jit(solution)/shard_map/ppermute | solution.py:219
  580.0 4.9 collective-permute-done.33
  585.1 9.3 %pair_dots.1 = f32[32,136,128]{2,1,0:T(8,128)S(1)} custom-call(s32[2,6,32]{2,1,0:T(8,128)S(1)} %pad_add_fusion.ids, f32[4,3,32,1024]{3,2,1,0:T(8,128)S(1)} %pad_maximum_fusion.5.early, f32[4,40,1024]{2,1,0:T(8,128)S(1)} %pad_maximum_fusion.6.late), custom_call_target="tpu_custom_call" | custom-call | tf_op jit(solution)/shard_map/pair_dots/pallas_call | solution.py:172
  599.4 14.1 %collective-permute-done.45 = f32[1,2,1,4,136,128]{5,4,3,2,1,0:T(8,128)S(1)} collective-permute-done((f32[1,2,1,4,136,128]{5,4,3,2,1,0:T(8,128)S(1)}, f32[1,2,1,4,136,128]{5,4,3,2,1,0:T(8,128)S(1)}, u32[]{:S(2)}, u32[]{:S(2)}) %collective-permute-start.45) | collective-permute-done | bytes 557088 | tf_op jit(solution)/shard_map/ppermute | solution.py:196
  614.2 7.4 %collective-permute-done.46 = f32[1,1,1,4,136,128]{5,4,3,2,1,0:T(8,128)S(1)} collective-permute-done((f32[1,1,1,4,136,128]{5,4,3,2,1,0:T(8,128)S(1)}, f32[1,1,1,4,136,128]{5,4,3,2,1,0:T(8,128)S(1)}, u32[]{:S(2)}, u32[]{:S(2)}) %collective-permute-start.46) | collective-permute-done | bytes 278560 | tf_op jit(solution)/shard_map/ppermute | solution.py:196
  (311 shorter events, 124.3 us)
Async XLA Ops:
  7.8 24.8 %collective-permute-start.1 = (bf16[3840,128]{1,0:T(8,128)(2,1)S(1)}, bf16[3840,128]{1,0:T(8,128)(2,1)S(1)}, u32[]{:S(2)}, u32[]{:S(2)}) collective-permute-start(bf16[3840,128]{1,0:T(8,128)(2,1)S(1)} %constant_dynamic-slice_fusion.11), channel_id=1, source_target_pairs={{0,4},{4,0},{1,5},{5,1},{2,6},{6,2},{3,7},{7,3},{8,12},{12,8},{9,1... | collective-permute-start | bytes 2949128 | tf_op jit(solution)/shard_map/ppermute | solution.py:211
  32.6 45.6 %collective-permute-start.3 = (bf16[7936,128]{1,0:T(8,128)(2,1)}, bf16[7936,128]{1,0:T(8,128)(2,1)S(1)}, u32[]{:S(2)}, u32[]{:S(2)}) collective-permute-start(bf16[7936,128]{1,0:T(8,128)(2,1)} %constant_dynamic-slice_fusion.9), channel_id=1, source_target_pairs={{0,4},{4,0},{1,5},{5,1},{2,6},{6,2},{3,7},{7,3},{8,12},{12,8},{9,1... | collective-permute-start | bytes 6094856 | tf_op jit(solution)/shard_map/ppermute | solution.py:211
  37.6 48.8 %collective-permute-start.8 = (bf16[3840,256]{1,0:T(8,128)(2,1)}, bf16[3840,256]{1,0:T(8,128)(2,1)}, u32[]{:S(2)}, u32[]{:S(2)}) collective-permute-start(bf16[3840,256]{1,0:T(8,128)(2,1)} %pad_maximum_fusion.4), channel_id=1, source_target_pairs={{0,8},{8,0},{16,24},{24,16},{1,9},{9,1},{17,25},{25,17},{2,10},{10... | collective-permute-start | bytes 5898248 | tf_op jit(solution)/shard_map/ppermute | solution.py:211
  39.2 44.6 %collective-permute-start.12 = (bf16[3840,256]{1,0:T(8,128)(2,1)}, bf16[3840,256]{1,0:T(8,128)(2,1)}, u32[]{:S(2)}, u32[]{:S(2)}) collective-permute-start(bf16[3840,256]{1,0:T(8,128)(2,1)} %pad_maximum_fusion.4), channel_id=1, source_target_pairs={{8,16},{16,8},{9,17},{17,9},{10,18},{18,10},{11,19},{19,11},{12,20... | collective-permute-start | bytes 5898248 | tf_op jit(solution)/shard_map/ppermute | solution.py:211
  80.6 12.5 %copy-start.45 = (s32[4,256]{1,0:T(4,128)S(1)}, s32[4,256]{1,0:T(4,128)}, u32[]{:S(2)}) copy-start(s32[4,256]{1,0:T(4,128)} %param.10) | copy-start | bytes 12292
  83.8 94.6 %collective-permute-start.14 = (bf16[7936,256]{1,0:T(8,128)(2,1)}, bf16[7936,256]{1,0:T(8,128)(2,1)}, u32[]{:S(2)}, u32[]{:S(2)}) collective-permute-start(bf16[7936,256]{1,0:T(8,128)(2,1)} %pad_maximum_fusion), channel_id=1, source_target_pairs={{8,16},{16,8},{9,17},{17,9},{10,18},{18,10},{11,19},{19,11},{12,20... | collective-permute-start | bytes 12189704 | tf_op jit(solution)/shard_map/ppermute | solution.py:211
  86.4 117.8 %collective-permute-start.9 = (bf16[7936,256]{1,0:T(8,128)(2,1)}, bf16[7936,256]{1,0:T(8,128)(2,1)}, u32[]{:S(2)}, u32[]{:S(2)}) collective-permute-start(bf16[7936,256]{1,0:T(8,128)(2,1)} %pad_maximum_fusion), channel_id=1, source_target_pairs={{0,8},{8,0},{16,24},{24,16},{1,9},{9,1},{17,25},{25,17},{2,10},{10... | collective-permute-start | bytes 12189704 | tf_op jit(solution)/shard_map/ppermute | solution.py:211
  91.0 25.7 %collective-permute-start.4 = (bf16[4608,128]{1,0:T(8,128)(2,1)S(1)}, bf16[4608,128]{1,0:T(8,128)(2,1)}, u32[]{:S(2)}, u32[]{:S(2)}) collective-permute-start(bf16[4608,128]{1,0:T(8,128)(2,1)S(1)} %constant_dynamic-slice_fusion.10), channel_id=1, source_target_pairs={{0,4},{4,0},{1,5},{5,1},{2,6},{6,2},{3,7},{7,3},{8,12},{12,8},{9,1... | collective-permute-start | bytes 3538952 | tf_op jit(solution)/shard_map/ppermute | solution.py:211
  91.8 29.4 %collective-permute-start = (s32[16,2]{0,1:T(2,128)S(1)}, s32[16,2]{0,1:T(2,128)S(1)}, u32[]{:S(2)}, u32[]{:S(2)}) collective-permute-start(s32[16,2]{0,1:T(2,128)S(1)} %copy-done.46), channel_id=1, source_target_pairs={{0,4},{4,0},{1,5},{5,1},{2,6},{6,2},{3,7},{7,3},{8,12},{12,8},{9,1... | collective-permute-start | bytes 392 | tf_op jit(solution)/shard_map/ppermute | solution.py:368
  93.1 24.6 %copy-start.42 = (s32[4,256]{1,0:T(4,128)}, s32[4,256]{1,0:T(4,128)S(1)}, u32[]{:S(2)}) copy-start(s32[4,256]{1,0:T(4,128)S(1)} %compare_convert_fusion.1) | copy-start | bytes 12292
  116.7 98.6 %collective-permute-start.5 = (bf16[88,128,128]{2,1,0:T(8,128)(2,1)}, bf16[88,128,128]{2,1,0:T(8,128)(2,1)S(1)}, u32[]{:S(2)}, u32[]{:S(2)}) collective-permute-start(bf16[88,128,128]{2,1,0:T(8,128)(2,1)} %pack_tiles.4), channel_id=1, source_target_pairs={{0,4},{4,0},{1,5},{5,1},{2,6},{6,2},{3,7},{7,3},{8,12},{12,8},{9,1... | collective-permute-start | bytes 8650760 | tf_op jit(solution)/shard_map/ppermute | solution.py:211
  122.5 55.3 %collective-permute-start.2 = (s32[4,128]{1,0:T(4,128)S(1)}, s32[4,128]{1,0:T(4,128)S(1)}, u32[]{:S(2)}, u32[]{:S(2)}) collective-permute-start(s32[4,128]{1,0:T(4,128)S(1)} %get-tuple-element.81), channel_id=1, source_target_pairs={{0,4},{4,0},{1,5},{5,1},{2,6},{6,2},{3,7},{7,3},{8,12},{12,8},{9,1... | collective-permute-start | bytes 6152 | tf_op jit(solution)/shard_map/ppermute | solution.py:301
  178.4 43.8 %collective-permute-start.16 = (bf16[3840,256]{1,0:T(8,128)(2,1)}, bf16[3840,256]{1,0:T(8,128)(2,1)}, u32[]{:S(2)}, u32[]{:S(2)}) collective-permute-start(bf16[3840,256]{1,0:T(8,128)(2,1)} %collective-permute-done.8), channel_id=1, source_target_pairs={{8,16},{16,8},{9,17},{17,9},{10,18},{18,10},{11,19},{19,11},{12,20... | collective-permute-start | bytes 5898248 | tf_op jit(solution)/shard_map/ppermute | solution.py:211
  180.7 5.4 collective-permute-start.22
  204.2 73.8 %collective-permute-start.10 = (bf16[104,128,128]{2,1,0:T(8,128)(2,1)}, bf16[104,128,128]{2,1,0:T(8,128)(2,1)}, u32[]{:S(2)}, u32[]{:S(2)}) collective-permute-start(bf16[104,128,128]{2,1,0:T(8,128)(2,1)} %pack_tiles.7), channel_id=1, source_target_pairs={{0,8},{24,16},{1,9},{25,17},{2,10},{26,18},{3,11},{27,19},{4,12},{... | collective-permute-start | bytes 10223624 | tf_op jit(solution)/shard_map/ppermute | solution.py:211
  213.9 43.1 %collective-permute-start.13 = (bf16[3840,256]{1,0:T(8,128)(2,1)}, bf16[3840,256]{1,0:T(8,128)(2,1)}, u32[]{:S(2)}, u32[]{:S(2)}) collective-permute-start(bf16[3840,256]{1,0:T(8,128)(2,1)} %collective-permute-done.12), channel_id=1, source_target_pairs={{8,0},{16,24},{9,1},{17,25},{10,2},{18,26},{11,3},{19,27},{12,4},{... | collective-permute-start | bytes 5898248 | tf_op jit(solution)/shard_map/ppermute | solution.py:211
  216.9 72.0 %collective-permute-start.6 = (bf16[104,128,128]{2,1,0:T(8,128)(2,1)}, bf16[104,128,128]{2,1,0:T(8,128)(2,1)S(1)}, u32[]{:S(2)}, u32[]{:S(2)}) collective-permute-start(bf16[104,128,128]{2,1,0:T(8,128)(2,1)} %pack_tiles.6), channel_id=1, source_target_pairs={{0,4},{4,0},{1,5},{5,1},{2,6},{6,2},{3,7},{7,3},{8,12},{12,8},{9,1... | collective-permute-start | bytes 10223624 | tf_op jit(solution)/shard_map/ppermute | solution.py:211
  222.1 36.2 %copy-start.7 = (bf16[512,4608]{1,0:T(8,128)(2,1)S(1)}, bf16[512,4608]{1,0:T(8,128)(2,1)}, u32[]{:S(2)}) copy-start(bf16[512,4608]{1,0:T(8,128)(2,1)} %copy-done.6) | copy-start | bytes 14155780
  222.2 113.3 %collective-permute-start.17 = (bf16[7936,256]{1,0:T(8,128)(2,1)}, bf16[7936,256]{1,0:T(8,128)(2,1)}, u32[]{:S(2)}, u32[]{:S(2)}) collective-permute-start(bf16[7936,256]{1,0:T(8,128)(2,1)} %collective-permute-done.9), channel_id=1, source_target_pairs={{8,16},{16,8},{9,17},{17,9},{10,18},{18,10},{11,19},{19,11},{12,20... | collective-permute-start | bytes 12189704 | tf_op jit(solution)/shard_map/ppermute | solution.py:211
  227.1 32.7 %copy-start.22 = (bf16[4608,128]{1,0:T(8,128)(2,1)}, bf16[4608,128]{1,0:T(8,128)(2,1)S(1)}, u32[]{:S(2)}) copy-start(bf16[4608,128]{1,0:T(8,128)(2,1)S(1)} %get-tuple-element.135) | copy-start | bytes 3538948
  227.1 32.7 %copy-start.25 = (bf16[4608,128]{1,0:T(8,128)(2,1)}, bf16[4608,128]{1,0:T(8,128)(2,1)S(1)}, u32[]{:S(2)}) copy-start(bf16[4608,128]{1,0:T(8,128)(2,1)S(1)} %get-tuple-element.136) | copy-start | bytes 3538948
  257.0 87.9 %collective-permute-start.15 = (bf16[7936,256]{1,0:T(8,128)(2,1)}, bf16[7936,256]{1,0:T(8,128)(2,1)}, u32[]{:S(2)}, u32[]{:S(2)}) collective-permute-start(bf16[7936,256]{1,0:T(8,128)(2,1)} %collective-permute-done.14), channel_id=1, source_target_pairs={{8,0},{16,24},{9,1},{17,25},{10,2},{18,26},{11,3},{19,27},{12,4},{... | collective-permute-start | bytes 12189704 | tf_op jit(solution)/shard_map/ppermute | solution.py:211
  259.8 24.5 %copy-start.29 = (bf16[3840,128]{1,0:T(8,128)(2,1)S(1)}, bf16[3840,128]{1,0:T(8,128)(2,1)}, u32[]{:S(2)}) copy-start(bf16[3840,128]{1,0:T(8,128)(2,1)} %copy-done.28) | copy-start | bytes 2949124
  259.8 24.5 %copy-start.32 = (bf16[3840,128]{1,0:T(8,128)(2,1)S(1)}, bf16[3840,128]{1,0:T(8,128)(2,1)}, u32[]{:S(2)}) copy-start(bf16[3840,128]{1,0:T(8,128)(2,1)} %copy-done.31) | copy-start | bytes 2949124
  277.9 51.4 %collective-permute-start.11 = (bf16[4608,256]{1,0:T(8,128)(2,1)}, bf16[4608,256]{1,0:T(8,128)(2,1)}, u32[]{:S(2)}, u32[]{:S(2)}) collective-permute-start(bf16[4608,256]{1,0:T(8,128)(2,1)} %pad_maximum_fusion.3), channel_id=1, source_target_pairs={{0,8},{24,16},{1,9},{25,17},{2,10},{26,18},{3,11},{27,19},{4,12},{... | collective-permute-start | bytes 7077896 | tf_op jit(solution)/shard_map/ppermute | solution.py:211
  290.6 112.9 %collective-permute-start.7 = (bf16[164,128,128]{2,1,0:T(8,128)(2,1)}, bf16[164,128,128]{2,1,0:T(8,128)(2,1)}, u32[]{:S(2)}, u32[]{:S(2)}) collective-permute-start(bf16[164,128,128]{2,1,0:T(8,128)(2,1)} %pack_tiles.5), channel_id=1, source_target_pairs={{0,4},{4,0},{1,5},{5,1},{2,6},{6,2},{3,7},{7,3},{8,12},{12,8},{9,1... | collective-permute-start | bytes 16121864 | tf_op jit(solution)/shard_map/ppermute | solution.py:211
  303.9 46.1 %copy-start.3 = (bf16[512,4608]{1,0:T(8,128)(2,1)}, bf16[512,4608]{1,0:T(8,128)(2,1)S(1)}, u32[]{:S(2)}) copy-start(bf16[512,4608]{1,0:T(8,128)(2,1)S(1)} %spread_tiles.10) | copy-start | bytes 14155780
  307.3 30.3 %slice-start.4 = ((s8[4718592]{0:T(1024)(128)(4,1)}), s8[4194304]{0:T(1024)(128)(4,1)S(1)}, s32[]{:S(2)}) async-start(s8[4718592]{0:T(1024)(128)(4,1)} %bitcast.190), calls=%async_computation.10 | async-start | bytes 8388608
  309.9 27.6 %slice-start.5 = ((s8[4718592]{0:T(1024)(128)(4,1)}), s8[524288]{0:T(1024)(128)(4,1)S(1)}, s32[]{:S(2)}) async-start(s8[4718592]{0:T(1024)(128)(4,1)} %bitcast.190), calls=%async_computation.11 | async-start | bytes 1048576
  312.2 34.3 %copy-start.52 = (f32[512,256]{0,1:T(8,128)S(1)}, f32[512,256]{0,1:T(8,128)}, u32[]{:S(2)}) copy-start(f32[512,256]{0,1:T(8,128)} %fusion.36) | copy-start | bytes 1572868
  329.4 119.6 %collective-permute-start.23 = (bf16[104,128,128]{2,1,0:T(8,128)(2,1)}, bf16[104,128,128]{2,1,0:T(8,128)(2,1)}, u32[]{:S(2)}, u32[]{:S(2)}) collective-permute-start(bf16[104,128,128]{2,1,0:T(8,128)(2,1)} %copy-done.8), channel_id=1, source_target_pairs={{0,8},{24,16},{1,9},{25,17},{2,10},{26,18},{3,11},{27,19},{4,12},{... | collective-permute-start | bytes 10223624 | tf_op jit(solution)/shard_map/ppermute | solution.py:211
  335.5 53.8 %collective-permute-start.18 = (bf16[4608,256]{1,0:T(8,128)(2,1)}, bf16[4608,256]{1,0:T(8,128)(2,1)}, u32[]{:S(2)}, u32[]{:S(2)}) collective-permute-start(bf16[4608,256]{1,0:T(8,128)(2,1)} %pad_maximum_fusion.3), channel_id=1, source_target_pairs={{8,16},{16,8},{9,17},{17,9},{10,18},{18,10},{11,19},{19,11},{12,20... | collective-permute-start | bytes 7077896 | tf_op jit(solution)/shard_map/ppermute | solution.py:211
  345.0 43.0 %collective-permute-start.34 = (bf16[3840,256]{1,0:T(8,128)(2,1)}, bf16[3840,256]{1,0:T(8,128)(2,1)}, u32[]{:S(2)}, u32[]{:S(2)}) collective-permute-start(bf16[3840,256]{1,0:T(8,128)(2,1)} %collective-permute-done.16), channel_id=1, source_target_pairs={{8,0},{16,24},{9,1},{17,25},{10,2},{18,26},{11,3},{19,27},{12,4},{... | collective-permute-start | bytes 5898248 | tf_op jit(solution)/shard_map/ppermute | solution.py:211
  359.3 36.6 %copy-start.4 = (bf16[512,4608]{1,0:T(8,128)(2,1)S(1)}, bf16[512,4608]{1,0:T(8,128)(2,1)}, u32[]{:S(2)}) copy-start(bf16[512,4608]{1,0:T(8,128)(2,1)} %copy-done.3) | copy-start | bytes 14155780
  387.9 92.9 %collective-permute-start.35 = (bf16[7936,256]{1,0:T(8,128)(2,1)}, bf16[7936,256]{1,0:T(8,128)(2,1)}, u32[]{:S(2)}, u32[]{:S(2)}) collective-permute-start(bf16[7936,256]{1,0:T(8,128)(2,1)} %collective-permute-done.17), channel_id=1, source_target_pairs={{8,0},{16,24},{9,1},{17,25},{10,2},{18,26},{11,3},{19,27},{12,4},{... | collective-permute-start | bytes 12189704 | tf_op jit(solution)/shard_map/ppermute | solution.py:211
  389.2 73.4 %collective-permute-start.24 = (bf16[4608,256]{1,0:T(8,128)(2,1)}, bf16[4608,256]{1,0:T(8,128)(2,1)}, u32[]{:S(2)}, u32[]{:S(2)}) collective-permute-start(bf16[4608,256]{1,0:T(8,128)(2,1)} %collective-permute-done.11), channel_id=1, source_target_pairs={{8,16},{16,8},{9,17},{17,9},{10,18},{18,10},{11,19},{19,11},{12,20... | collective-permute-start | bytes 7077896 | tf_op jit(solution)/shard_map/ppermute | solution.py:211
  443.6 14.8 %collective-permute-start.19 = (f32[3,1024,128]{1,2,0:T(8,128)}, f32[3,1024,128]{1,2,0:T(8,128)}, u32[]{:S(2)}, u32[]{:S(2)}) collective-permute-start(f32[3,1024,128]{1,2,0:T(8,128)} %constant_dynamic-slice_fusion.7), channel_id=1, source_target_pairs={{0,1},{1,0},{2,3},{3,2},{4,5},{5,4},{6,7},{7,6},{8,9},{9,8},{10,11... | collective-permute-start | bytes 4718600 | tf_op jit(solution)/shard_map/ppermute | solution.py:196
  461.3 40.7 %collective-permute-start.20 = (f32[3,64,1024]{2,1,0:T(8,128)}, f32[3,64,1024]{2,1,0:T(8,128)}, u32[]{:S(2)}, u32[]{:S(2)}) collective-permute-start(f32[3,64,1024]{2,1,0:T(8,128)} %dynamic-slice_bitcast_fusion.1), channel_id=1, source_target_pairs={{0,4},{4,0},{1,5},{5,1},{2,6},{6,2},{3,7},{7,3},{8,12},{12,8},{9,1... | collective-permute-start | bytes 2359304 | tf_op jit(solution)/shard_map/ppermute | solution.py:196
  472.5 23.9 %collective-permute-start.25 = (f32[3,1024,128]{1,2,0:T(8,128)}, f32[3,1024,128]{1,2,0:T(8,128)}, u32[]{:S(2)}, u32[]{:S(2)}) collective-permute-start(f32[3,1024,128]{1,2,0:T(8,128)} %constant_dynamic-slice_fusion.5), channel_id=1, source_target_pairs={{0,1},{1,0},{2,3},{3,2},{4,5},{5,4},{6,7},{7,6},{8,9},{9,8},{10,11... | collective-permute-start | bytes 4718600 | tf_op jit(solution)/shard_map/ppermute | solution.py:196
  498.3 19.5 %collective-permute-start.26 = (f32[3,64,1024]{2,1,0:T(8,128)S(1)}, f32[3,64,1024]{2,1,0:T(8,128)S(1)}, u32[]{:S(2)}, u32[]{:S(2)}) collective-permute-start(f32[3,64,1024]{2,1,0:T(8,128)S(1)} %dynamic-slice_bitcast_fusion), channel_id=1, source_target_pairs={{0,4},{4,0},{1,5},{5,1},{2,6},{6,2},{3,7},{7,3},{8,12},{12,8},{9,1... | collective-permute-start | bytes 2359304 | tf_op jit(solution)/shard_map/ppermute | solution.py:196
  501.9 18.2 %collective-permute-start.36 = (f32[1,1024,128]{1,2,0:T(8,128)S(1)}, f32[1,1024,128]{1,2,0:T(8,128)S(1)}, u32[]{:S(2)}, u32[]{:S(2)}) collective-permute-start(f32[1,1024,128]{1,2,0:T(8,128)S(1)} %fusion.17), channel_id=1, source_target_pairs={{0,1},{1,0},{2,3},{3,2},{4,5},{5,4},{6,7},{7,6},{8,9},{9,8},{10,11... | collective-permute-start | bytes 1572872 | tf_op jit(solution)/shard_map/ppermute | solution.py:196
  517.9 12.1 %collective-permute-start.27 = (f32[3,32,1024]{2,1,0:T(8,128)S(1)}, f32[3,32,1024]{2,1,0:T(8,128)S(1)}, u32[]{:S(2)}, u32[]{:S(2)}) collective-permute-start(f32[3,32,1024]{2,1,0:T(8,128)S(1)} %constant_dynamic-slice_fusion.4), channel_id=1, source_target_pairs={{0,2},{2,0},{1,3},{3,1},{4,6},{6,4},{5,7},{7,5},{8,10},{10,8},{9,1... | collective-permute-start | bytes 1179656 | tf_op jit(solution)/shard_map/ppermute | solution.py:196
  519.6 17.0 %collective-permute-start.21 = (f32[3,32,1024]{2,1,0:T(8,128)S(1)}, f32[3,32,1024]{2,1,0:T(8,128)S(1)}, u32[]{:S(2)}, u32[]{:S(2)}) collective-permute-start(f32[3,32,1024]{2,1,0:T(8,128)S(1)} %constant_dynamic-slice_fusion.6), channel_id=1, source_target_pairs={{0,2},{2,0},{1,3},{3,1},{4,6},{6,4},{5,7},{7,5},{8,10},{10,8},{9,1... | collective-permute-start | bytes 1179656 | tf_op jit(solution)/shard_map/ppermute | solution.py:196
  520.2 29.0 %copy-start.44 = (s32[32,2]{0,1:T(2,128)S(1)}, s32[32,2]{0,1:T(2,128)}, u32[]{:S(2)}) copy-start(s32[32,2]{0,1:T(2,128)} %reshape.166) | copy-start | bytes 772
  520.2 36.8 %copy-start.13 = (s32[4,4]{1,0:T(4,128)S(1)}, s32[4,4]{1,0:T(4,128)}, u32[]{:S(2)}) copy-start(s32[4,4]{1,0:T(4,128)} %constant.238.clone) | copy-start | bytes 196
  520.2 37.5 %copy-start.12 = (s32[4]{0:T(128)S(1)}, s32[4]{0:T(128)}, u32[]{:S(2)}) copy-start(s32[4]{0:T(128)} %fusion.25) | copy-start | bytes 52
  520.2 16.4 %collective-permute-start.37 = (f32[1,64,1024]{2,1,0:T(8,128)S(1)}, f32[1,64,1024]{2,1,0:T(8,128)S(1)}, u32[]{:S(2)}, u32[]{:S(2)}) collective-permute-start(f32[1,64,1024]{2,1,0:T(8,128)S(1)} %dynamic-slice_bitcast_fusion.2), channel_id=1, source_target_pairs={{0,4},{4,0},{1,5},{5,1},{2,6},{6,2},{3,7},{7,3},{8,12},{12,8},{9,1... | collective-permute-start | bytes 786440 | tf_op jit(solution)/shard_map/ppermute | solution.py:196
  530.1 12.3 %collective-permute-start.28 = (f32[3,32,1024]{2,1,0:T(8,128)S(1)}, f32[3,32,1024]{2,1,0:T(8,128)S(1)}, u32[]{:S(2)}, u32[]{:S(2)}) collective-permute-start(f32[3,32,1024]{2,1,0:T(8,128)S(1)} %dynamic-slice_add_fusion.4), channel_id=1, source_target_pairs={{8,0},{16,24},{9,1},{17,25},{10,2},{18,26},{11,3},{19,27},{12,4},{... | collective-permute-start | bytes 1179656 | tf_op jit(solution)/shard_map/ppermute | solution.py:361
  536.7 7.5 %collective-permute-start.38 = (f32[1,32,1024]{2,1,0:T(8,128)S(1)}, f32[1,32,1024]{2,1,0:T(8,128)S(1)}, u32[]{:S(2)}, u32[]{:S(2)}) collective-permute-start(f32[1,32,1024]{2,1,0:T(8,128)S(1)} %constant_dynamic-slice_fusion.3), channel_id=1, source_target_pairs={{0,2},{2,0},{1,3},{3,1},{4,6},{6,4},{5,7},{7,5},{8,10},{10,8},{9,1... | collective-permute-start | bytes 393224 | tf_op jit(solution)/shard_map/ppermute | solution.py:196
  542.5 13.8 %collective-permute-start.29 = (f32[3,32,1024]{2,1,0:T(8,128)S(1)}, f32[3,32,1024]{2,1,0:T(8,128)S(1)}, u32[]{:S(2)}, u32[]{:S(2)}) collective-permute-start(f32[3,32,1024]{2,1,0:T(8,128)S(1)} %fusion.21), channel_id=1, source_target_pairs={{0,8},{8,0},{16,24},{24,16},{1,9},{9,1},{17,25},{25,17},{2,10},{10... | collective-permute-start | bytes 1179656 | tf_op jit(solution)/shard_map/ppermute | solution.py:216
  543.5 16.4 %collective-permute-start.30 = (f32[3,32,1024]{2,1,0:T(8,128)S(1)}, f32[3,32,1024]{2,1,0:T(8,128)S(1)}, u32[]{:S(2)}, u32[]{:S(2)}) collective-permute-start(f32[3,32,1024]{2,1,0:T(8,128)S(1)} %fusion.21), channel_id=1, source_target_pairs={{8,16},{16,8},{9,17},{17,9},{10,18},{18,10},{11,19},{19,11},{12,20... | collective-permute-start | bytes 1179656 | tf_op jit(solution)/shard_map/ppermute | solution.py:217
  544.3 10.0 %collective-permute-start.39 = (f32[40,1024]{1,0:T(8,128)S(1)}, f32[40,1024]{1,0:T(8,128)S(1)}, u32[]{:S(2)}, u32[]{:S(2)}) collective-permute-start(f32[40,1024]{1,0:T(8,128)S(1)} %get-tuple-element.154), channel_id=1, source_target_pairs={{0,8},{8,0},{16,24},{24,16},{1,9},{9,1},{17,25},{25,17},{2,10},{10... | collective-permute-start | bytes 491528 | tf_op jit(solution)/shard_map/ppermute | solution.py:216
  548.5 6.5 %collective-permute-start.40 = (f32[40,1024]{1,0:T(8,128)S(1)}, f32[40,1024]{1,0:T(8,128)S(1)}, u32[]{:S(2)}, u32[]{:S(2)}) collective-permute-start(f32[40,1024]{1,0:T(8,128)S(1)} %get-tuple-element.154), channel_id=1, source_target_pairs={{8,16},{16,8},{9,17},{17,9},{10,18},{18,10},{11,19},{19,11},{12,20... | collective-permute-start | bytes 491528 | tf_op jit(solution)/shard_map/ppermute | solution.py:217
  554.3 4.3 collective-permute-start.42
  555.0 10.4 %collective-permute-start.41 = (f32[40,1024]{1,0:T(8,128)S(1)}, f32[40,1024]{1,0:T(8,128)S(1)}, u32[]{:S(2)}, u32[]{:S(2)}) collective-permute-start(f32[40,1024]{1,0:T(8,128)S(1)} %collective-permute-done.40), channel_id=1, source_target_pairs={{8,0},{16,24},{9,1},{17,25},{10,2},{18,26},{11,3},{19,27},{12,4},{... | collective-permute-start | bytes 491528 | tf_op jit(solution)/shard_map/ppermute | solution.py:219
  556.3 9.2 %collective-permute-start.32 = (f32[3,32,1024]{2,1,0:T(8,128)S(1)}, f32[3,32,1024]{2,1,0:T(8,128)S(1)}, u32[]{:S(2)}, u32[]{:S(2)}) collective-permute-start(f32[3,32,1024]{2,1,0:T(8,128)S(1)} %collective-permute-done.29), channel_id=1, source_target_pairs={{8,16},{16,8},{9,17},{17,9},{10,18},{18,10},{11,19},{19,11},{12,20... | collective-permute-start | bytes 1179656 | tf_op jit(solution)/shard_map/ppermute | solution.py:218
  558.6 12.9 %collective-permute-start.43 = (f32[40,1024]{1,0:T(8,128)S(1)}, f32[40,1024]{1,0:T(8,128)S(1)}, u32[]{:S(2)}, u32[]{:S(2)}) collective-permute-start(f32[40,1024]{1,0:T(8,128)S(1)} %collective-permute-done.42), channel_id=1, source_target_pairs={{8,0},{16,24},{9,1},{17,25},{10,2},{18,26},{11,3},{19,27},{12,4},{... | collective-permute-start | bytes 491528 | tf_op jit(solution)/shard_map/ppermute | solution.py:220
  559.9 20.0 %collective-permute-start.31 = (f32[3,32,1024]{2,1,0:T(8,128)S(1)}, f32[3,32,1024]{2,1,0:T(8,128)S(1)}, u32[]{:S(2)}, u32[]{:S(2)}) collective-permute-start(f32[3,32,1024]{2,1,0:T(8,128)S(1)} %collective-permute-done.30), channel_id=1, source_target_pairs={{8,0},{16,24},{9,1},{17,25},{10,2},{18,26},{11,3},{19,27},{12,4},{... | collective-permute-start | bytes 1179656 | tf_op jit(solution)/shard_map/ppermute | solution.py:219
  565.5 19.4 %collective-permute-start.33 = (f32[3,32,1024]{2,1,0:T(8,128)S(1)}, f32[3,32,1024]{2,1,0:T(8,128)S(1)}, u32[]{:S(2)}, u32[]{:S(2)}) collective-permute-start(f32[3,32,1024]{2,1,0:T(8,128)S(1)} %collective-permute-done.32), channel_id=1, source_target_pairs={{8,0},{16,24},{9,1},{17,25},{10,2},{18,26},{11,3},{19,27},{12,4},{... | collective-permute-start | bytes 1179656 | tf_op jit(solution)/shard_map/ppermute | solution.py:220
  594.5 3.0 collective-permute-start.44
  594.5 28.3 %copy-start.43 = (s32[4,256]{1,0:T(4,128)S(1)}, s32[4,256]{1,0:T(4,128)}, u32[]{:S(2)}) copy-start(s32[4,256]{1,0:T(4,128)} %copy-done.42) | copy-start | bytes 12292
  594.6 28.3 %copy-start.47 = (s32[16,2]{0,1:T(2,128)S(1)}, s32[16,2]{0,1:T(2,128)}, u32[]{:S(2)}) copy-start(s32[16,2]{0,1:T(2,128)} %param.12) | copy-start | bytes 388
  598.8 14.7 %collective-permute-start.45 = (f32[1,2,1,4,136,128]{5,4,3,2,1,0:T(8,128)S(1)}, f32[1,2,1,4,136,128]{5,4,3,2,1,0:T(8,128)S(1)}, u32[]{:S(2)}, u32[]{:S(2)}) collective-permute-start(f32[1,2,1,4,136,128]{5,4,3,2,1,0:T(8,128)S(1)} %constant_dynamic-slice_fusion.1), channel_id=1, source_target_pairs={{0,4},{4,0},{1,5},{5,1},{2,6},{6,2},{3,7},{7,3},{8,12},{12,8},{9,1... | collective-permute-start | bytes 1671176 | tf_op jit(solution)/shard_map/ppermute | solution.py:196
  613.7 7.9 %collective-permute-start.46 = (f32[1,1,1,4,136,128]{5,4,3,2,1,0:T(8,128)S(1)}, f32[1,1,1,4,136,128]{5,4,3,2,1,0:T(8,128)S(1)}, u32[]{:S(2)}, u32[]{:S(2)}) collective-permute-start(f32[1,1,1,4,136,128]{5,4,3,2,1,0:T(8,128)S(1)} %constant_dynamic-slice_fusion), channel_id=1, source_target_pairs={{0,2},{2,0},{1,3},{3,1},{4,6},{6,4},{5,7},{7,5},{8,10},{10,8},{9,1... | collective-permute-start | bytes 835592 | tf_op jit(solution)/shard_map/ppermute | solution.py:196
  (43 other events, 185.5 us)

commit v7 on v6

--- a/solution.py
+++ b/solution.py
@@ -291,15 +291,20 @@
         return pack(hist, mask, owner * columns + cuts[c], slots[c])
 
     over_x = Lane()
+    both_masks = jnp.stack([tile_mask, lax.ppermute(tile_mask, "z", INWARD)])
+
+    def both_of(owner):
+        return lax.dynamic_slice_in_dim(both_masks, owner * columns, columns, 2)
+
+    known = [both_of(x)] + [lax.ppermute(both_of(o), "x", r) for o, r in zip(others, row_routes)]
+    listed = [pairs] + [lax.ppermute(pairs, "x", route) for route in row_routes]
+    masks, guest_masks = [m[0] for m in known], [m[1][:, kept:] for m in known]
     groups = []
     for c in range(3):
         got = over_x.send([planes_of(o, c) for o in others], "x", row_routes)
         groups.append(in_row_order([planes_of(x, c)] + got, 1))
         if c == 0:
-            start = got
-            others_masks = [
-                lax.ppermute(after(mask_of(o), start), "x", r) for o, r in zip(others, row_routes)
-            ]
+            over_x.arrived = got + known[1:] + listed[1:]
     tiles = [None] * 3
     for c in (0, 2, 1):
         tiles[c] = over_x.send([packed(o, c, groups[0]) for o in others], "x", row_routes)
@@ -316,12 +321,10 @@
     near += inward.send([groups[2]], "z", [INWARD])
     mid += middle.send([groups[2]], "z", [MIDDLE])
     far += middle.send([near[2]], "z", [MIDDLE])
-    outer = [outward.send([v], "z", [OUTWARD])[0] for v in mid[:2] + far[:2]]
+    outer = [outward.send([v], "z", [OUTWARD])[0] for v in (mid[0], mid[1], far[1], far[0])]
     loans = loans + inward.send(tiles[2], "z", [INWARD] * len(others))
-    masks = [mask_of(x)] + others_masks
-    guest_masks = lax.ppermute(jnp.stack([m[:, kept:] for m in masks]), "z", INWARD)
     held = [
-        [groups[c], near[c], jnp.where(inner, mid[c], outer[c]), jnp.where(inner, far[c], outer[2 + c])]
+        [groups[c], near[c], jnp.where(inner, mid[c], outer[c]), jnp.where(inner, far[c], outer[3 - c])]
         for c in range(2)
     ]
     held.append([groups[2], near[2], mid[2], far[2]])
@@ -365,7 +368,6 @@
     flags = jnp.full((8, last_one.shape[1]), over.astype(jnp.float32))
     late = jnp.stack(along_line(jnp.concatenate([last_one, flags]), inner))
 
-    listed = [pairs] + [lax.ppermute(pairs, "x", route) for route in row_routes]
     order = (x - jnp.arange(wide)) % wide
     all_pairs = jnp.stack(listed)[order].reshape(-1, 2).T
     plane_blocks = wide * row_blocks

time: 641 us -> 664 us (1.036)
  starting transfers between devices: 80.4 us -> 101 us
  waiting for transfers between devices: 300 us -> 293 us
    ppermute x2, waiting for transfers between devices: 45.4 us -> 18 us  [the longest x1 18 us: body(): lax.ppermute(both_of(o), 'x', r)]
    ppermute x21, waiting for transfers between devices: 170 us -> 195 us  [send(): lax.ppermute(v, axis, route)]
    ppermute x21, starting transfers between devices: 51.6 us -> 71.6 us  [send(): lax.ppermute(v, axis, route)]
    pallas_call x8, Pallas kernels: 26.5 us -> 36 us  [spread(): pl.pallas_call(functools.partial(spread_kernel, blk, row_blocks, parts, s...]
    unnamed x120 -> x118, local copies, waits for them, and re-layouts: 17.2 us -> 18.7 us
  transfers between devices with their start and end apart: 47 -> 47, of which waited for: 23 -> 21; matrix products, arithmetic and copies ran while one was open for 25% -> 24% of each run, Pallas kernels for 7% -> 8%
where the time goes in v7:
time: 664 us; the launch traced here: 652 us
  waiting for transfers between devices  293 us (44%)
  matrix products  121 us (18%)
  starting transfers between devices  101 us (15%)
  Pallas kernels  58.8 us (9%)
  local copies, waits for them, and re-layouts  33.9 us (5%)
  other arithmetic  25.2 us (4%)
  between operations  19.7 us (3%)
    ppermute x21, waiting for transfers between devices, send(): lax.ppermute(v, axis, route)  195 us
    dot_general x30, matrix products, total(): term = jnp.dot(source[c], held[c][s], preferred_element_type=jnp.float32)  121 us
    ppermute x21, starting transfers between devices, send(): lax.ppermute(v, axis, route)  71.6 us
    ppermute x12, waiting for transfers between devices, scatter_sum(): total = total + lax.ppermute(part((here + k) % count), axis, turn(count, k))  51.5 us
    pallas_call x8, Pallas kernels, spread(): pl.pallas_call(functools.partial(spread_kernel, blk, row_blocks, parts, s...  36 us
    unnamed x118, local copies, waits for them, and re-layouts  18.7 us
    ppermute x1, waiting for transfers between devices, body(): lax.ppermute(both_of(o), 'x', r)  18 us
    pallas_call x4, Pallas kernels, pack(): pl.pallas_call(functools.partial(pack_kernel, blk, row_blocks, columns, s...  13.4 us
  transfers between devices with their start and end apart: 47, of which 21 were waited for; matrix products, arithmetic and copies ran while one was open for 24% of the time, Pallas kernels for 8%

profile of v7, /device:TPU:0, one launch (start us, length us, event | category | flops | bytes accessed | tf_op | source)
XLA Modules:
  0.0 652.1 jit_solution(15861427687975540938)
XLA Ops:
  6.5 2.9 collective-permute-start
  10.2 3.5 collective-permute-start.1
  17.0 3.0 constant_dynamic-slice_fusion.12
  20.0 18.0 %collective-permute-done.2 = s32[2,4,128]{2,1,0:T(4,128)S(1)} collective-permute-done((s32[2,4,128]{2,1,0:T(4,128)S(1)}, s32[2,4,128]{2,1,0:T(4,128)S(1)}, u32[]{:S(2)}, u32[]{:S(2)}) %collective-permute-start.2) | collective-permute-done | bytes 4128 | tf_op jit(solution)/shard_map/ppermute | solution.py:299
  43.8 38.9 %collective-permute-done.4 = bf16[7936,128]{1,0:T(8,128)(2,1)S(1)} collective-permute-done((bf16[7936,128]{1,0:T(8,128)(2,1)}, bf16[7936,128]{1,0:T(8,128)(2,1)S(1)}, u32[]{:S(2)}, u32[]{:S(2)}) %collective-permute-start.4) | collective-permute-done | bytes 2031648 | tf_op jit(solution)/shard_map/ppermute | solution.py:211
  104.9 3.7 pack_tiles.4
  108.7 15.1 %collective-permute-done.5 = bf16[4608,128]{1,0:T(8,128)(2,1)S(1)} collective-permute-done((bf16[4608,128]{1,0:T(8,128)(2,1)S(1)}, bf16[4608,128]{1,0:T(8,128)(2,1)S(1)}, u32[]{:S(2)}, u32[]{:S(2)}) %collective-permute-start.5) | collective-permute-done | bytes 1179680 | tf_op jit(solution)/shard_map/ppermute | solution.py:211
  133.3 3.0 pack_tiles.5
  139.0 3.0 spread_tiles.13
  144.4 4.2 spread_tiles.12
  148.6 3.2 copy-done
  152.3 4.3 pack_tiles.7
  156.7 21.7 %collective-permute-done.10 = bf16[7936,256]{1,0:T(8,128)(2,1)} collective-permute-done((bf16[7936,256]{1,0:T(8,128)(2,1)}, bf16[7936,256]{1,0:T(8,128)(2,1)}, u32[]{:S(2)}, u32[]{:S(2)}) %collective-permute-start.10) | collective-permute-done | bytes 4063264 | tf_op jit(solution)/shard_map/ppermute | solution.py:211
  178.4 34.0 %collective-permute-start.11 = (bf16[104,128,128]{2,1,0:T(8,128)(2,1)}, bf16[104,128,128]{2,1,0:T(8,128)(2,1)S(1)}, u32[]{:S(2)}, u32[]{:S(2)}) collective-permute-start(bf16[104,128,128]{2,1,0:T(8,128)(2,1)} %pack_tiles.7), channel_id=1, source_target_pairs={{0,8},{24,16},{1,9},{25,17},{2,10},{26,18},{3,11},{27,19},{4,12},{... | collective-permute-start | bytes 10223624 | tf_op jit(solution)/shard_map/ppermute | solution.py:211
  212.5 3.3 spread_tiles.11
  217.1 3.9 fusion.29
  228.6 30.2 %collective-permute-done.14 = bf16[3840,256]{1,0:T(8,128)(2,1)} collective-permute-done((bf16[3840,256]{1,0:T(8,128)(2,1)}, bf16[3840,256]{1,0:T(8,128)(2,1)}, u32[]{:S(2)}, u32[]{:S(2)}) %collective-permute-start.14) | collective-permute-done | bytes 1966112 | tf_op jit(solution)/shard_map/ppermute | solution.py:211
  260.1 3.8 fusion.33
  263.9 17.9 %collective-permute-done.11.source = bf16[104,128,128]{2,1,0:T(8,128)(2,1)S(1)} collective-permute-done((bf16[104,128,128]{2,1,0:T(8,128)(2,1)}, bf16[104,128,128]{2,1,0:T(8,128)(2,1)S(1)}, u32[]{:S(2)}, u32[]{:S(2)}) %collective-permute-start.11) | collective-permute-done | bytes 3407904 | tf_op jit(solution)/shard_map/ppermute | solution.py:211
  283.6 5.7 collective-permute-start.12
  291.5 3.0 spread_tiles.8
  294.5 4.5 fusion.39
  299.4 3.1 spread_tiles.10
  306.3 3.1 spread_tiles.15
  312.0 22.9 %collective-permute-done.12 = bf16[4608,256]{1,0:T(8,128)(2,1)} collective-permute-done((bf16[4608,256]{1,0:T(8,128)(2,1)}, bf16[4608,256]{1,0:T(8,128)(2,1)}, u32[]{:S(2)}, u32[]{:S(2)}) %collective-permute-start.12) | collective-permute-done | bytes 2359328 | tf_op jit(solution)/shard_map/ppermute | solution.py:211
  334.9 6.1 collective-permute-start.23
  343.2 3.1 fusion.40
  346.3 3.6 fusion.11
  349.9 3.9 fusion.38
  355.1 5.4 fusion.4
  362.7 4.7 fusion.42
  367.4 3.9 fusion.41
  371.4 4.0 fusion.43
  375.4 3.6 fusion.13
  379.0 33.2 %collective-permute-done.8.source = bf16[164,128,128]{2,1,0:T(8,128)(2,1)} collective-permute-done((bf16[164,128,128]{2,1,0:T(8,128)(2,1)}, bf16[164,128,128]{2,1,0:T(8,128)(2,1)}, u32[]{:S(2)}, u32[]{:S(2)}) %collective-permute-start.8) | collective-permute-done | bytes 5373984 | tf_op jit(solution)/shard_map/ppermute | solution.py:211
  412.2 14.1 %spread_tiles.9 = bf16[512,7936]{1,0:T(8,128)(2,1)S(1)} custom-call(s32[249]{0:T(256)S(1)} %pad_add_fusion.7.info, bf16[164,128,128]{2,1,0:T(8,128)(2,1)} %collective-permute-done.8.source), custom_call_target="tpu_custom_call" | custom-call | bytes 16252928 | tf_op jit(solution)/shard_map/spread_tiles/pallas_call | solution.py:125
  426.3 3.2 copy-done.1
  429.5 7.6 %fusion.5 = f32[512,256]{0,1:T(8,128)} fusion(bf16[512,7936]{1,0:T(8,128)(2,1)} %copy-done.1, bf16[7936,256]{1,0:T(8,128)(2,1)} %collective-permute-done.15, bf16[7936,256]{1,0:T(8,128)(2,1)} %collective-permute-done.16, pred[]{:T(512)S(6)} %or.3), kind=kOutput, calls=%fused_computation.40 | convolution fusion | flops 2082406400 | bytes 16777216 | tf_op jit(solution)/shard_map/dot_general | solution.py:351
  437.1 7.7 %fusion.37 = f32[512,256]{0,1:T(8,128)} fusion(bf16[512,7936]{1,0:T(8,128)(2,1)} %copy-done.1, bf16[7936,256]{1,0:T(8,128)(2,1)} %collective-permute-done.10), kind=kOutput, calls=%fused_computation.190 | convolution fusion | flops 2080374784 | bytes 12713984 | tf_op jit(solution)/shard_map/dot_general | solution.py:351
  444.9 3.0 broadcast_select_fusion.29
  448.0 2.9 broadcast_select_fusion.30
  452.0 7.1 %fusion.30 = f32[512,256]{0,1:T(8,128)} fusion(bf16[512,7936]{1,0:T(8,128)(2,1)} %copy-done.1, bf16[7936,128]{1,0:T(8,128)(2,1)} %copy-done.18, bf16[7936,128]{1,0:T(8,128)(2,1)S(1)} %copy-done.17), kind=kOutput, calls=%fused_computation.183 | convolution fusion | flops 2088501248 | bytes 12713984 | tf_op jit(solution)/shard_map/dot_general | solution.py:351
  459.1 3.3 broadcast_select_fusion.31
  467.4 4.8 broadcast_select_fusion.27
  477.6 5.4 fusion.6
  483.0 6.9 %fusion.7 = f32[512,256]{0,1:T(8,128)S(1)} fusion(bf16[512,7936]{1,0:T(8,128)(2,1)} %copy-done.1, bf16[7936,256]{1,0:T(8,128)(2,1)} %collective-permute-done.18, bf16[7936,256]{1,0:T(8,128)(2,1)} %collective-permute-done.34, pred[]{:T(512)S(6)} %or.3), kind=kOutput, calls=%fused_computation.42 | convolution fusion | flops 2082406400 | bytes 16777216 | tf_op jit(solution)/shard_map/dot_general | solution.py:351
  492.1 4.8 fusion.44
  497.0 3.2 broadcast_select_fusion.26
  501.1 3.2 fusion.46
  504.3 3.2 fusion.45
  507.5 15.0 %collective-permute-done.35 = bf16[3840,256]{1,0:T(8,128)(2,1)} collective-permute-done((bf16[3840,256]{1,0:T(8,128)(2,1)}, bf16[3840,256]{1,0:T(8,128)(2,1)}, u32[]{:S(2)}, u32[]{:S(2)}) %collective-permute-start.35) | collective-permute-done | bytes 1966112 | tf_op jit(solution)/shard_map/ppermute | solution.py:211
  529.5 14.8 %collective-permute-done.26 = f32[3,64,1024]{2,1,0:T(8,128)S(1)} collective-permute-done((f32[3,64,1024]{2,1,0:T(8,128)S(1)}, f32[3,64,1024]{2,1,0:T(8,128)S(1)}, u32[]{:S(2)}, u32[]{:S(2)}) %collective-permute-start.26) | collective-permute-done | bytes 786464 | tf_op jit(solution)/shard_map/ppermute | solution.py:196
  547.2 9.3 %collective-permute-done.27 = f32[3,32,1024]{2,1,0:T(8,128)S(1)} collective-permute-done((f32[3,32,1024]{2,1,0:T(8,128)S(1)}, f32[3,32,1024]{2,1,0:T(8,128)S(1)}, u32[]{:S(2)}, u32[]{:S(2)}) %collective-permute-start.27) | collective-permute-done | bytes 393248 | tf_op jit(solution)/shard_map/ppermute | solution.py:196
  557.9 4.1 collective-permute-done.22
  564.0 5.4 collective-permute-done.28
  570.3 4.2 collective-permute-start.39
  575.2 5.4 collective-permute-done.39
  587.6 4.4 collective-permute-done.41
  593.3 4.5 collective-permute-done.43
  597.9 4.1 collective-permute-done.31
  602.1 4.2 collective-permute-done.33
  606.4 9.3 %pair_dots.1 = f32[32,136,128]{2,1,0:T(8,128)S(1)} custom-call(s32[2,6,32]{2,1,0:T(8,128)S(1)} %pad_add_fusion.ids, f32[4,3,32,1024]{3,2,1,0:T(8,128)S(1)} %pad_maximum_fusion.5.early, f32[4,40,1024]{2,1,0:T(8,128)S(1)} %pad_maximum_fusion.6.late), custom_call_target="tpu_custom_call" | custom-call | tf_op jit(solution)/shard_map/pair_dots/pallas_call | solution.py:172
  620.6 14.3 %collective-permute-done.45 = f32[1,2,1,4,136,128]{5,4,3,2,1,0:T(8,128)S(1)} collective-permute-done((f32[1,2,1,4,136,128]{5,4,3,2,1,0:T(8,128)S(1)}, f32[1,2,1,4,136,128]{5,4,3,2,1,0:T(8,128)S(1)}, u32[]{:S(2)}, u32[]{:S(2)}) %collective-permute-start.45) | collective-permute-done | bytes 557088 | tf_op jit(solution)/shard_map/ppermute | solution.py:196
  636.7 6.2 collective-permute-done.46
  (319 shorter events, 115.3 us)
Async XLA Ops:
  6.5 13.5 %collective-permute-start = (s32[16,2]{0,1:T(2,128)}, s32[16,2]{0,1:T(2,128)S(1)}, u32[]{:S(2)}, u32[]{:S(2)}) collective-permute-start(s32[16,2]{0,1:T(2,128)} %param.12), channel_id=1, source_target_pairs={{0,4},{4,0},{1,5},{5,1},{2,6},{6,2},{3,7},{7,3},{8,12},{12,8},{9,1... | collective-permute-start | bytes 392 | tf_op jit(solution)/shard_map/ppermute | solution.py:300
  10.2 89.3 %copy-start.41 = (s32[4,256]{1,0:T(4,128)}, s32[4,256]{1,0:T(4,128)S(1)}, u32[]{:S(2)}) copy-start(s32[4,256]{1,0:T(4,128)S(1)} %get-tuple-element.164) | copy-start | bytes 12292
  10.2 5.4 collective-permute-start.1
  14.9 23.1 %collective-permute-start.3 = (bf16[3840,128]{1,0:T(8,128)(2,1)S(1)}, bf16[3840,128]{1,0:T(8,128)(2,1)S(1)}, u32[]{:S(2)}, u32[]{:S(2)}) collective-permute-start(bf16[3840,128]{1,0:T(8,128)(2,1)S(1)} %constant_dynamic-slice_fusion.14), channel_id=1, source_target_pairs={{0,4},{4,0},{1,5},{5,1},{2,6},{6,2},{3,7},{7,3},{8,12},{12,8},{9,1... | collective-permute-start | bytes 2949128 | tf_op jit(solution)/shard_map/ppermute | solution.py:211
  15.5 22.5 %collective-permute-start.2 = (s32[2,4,128]{2,1,0:T(4,128)S(1)}, s32[2,4,128]{2,1,0:T(4,128)S(1)}, u32[]{:S(2)}, u32[]{:S(2)}) collective-permute-start(s32[2,4,128]{2,1,0:T(4,128)S(1)} %get-tuple-element.156), channel_id=1, source_target_pairs={{0,4},{4,0},{1,5},{5,1},{2,6},{6,2},{3,7},{7,3},{8,12},{12,8},{9,1... | collective-permute-start | bytes 12296 | tf_op jit(solution)/shard_map/ppermute | solution.py:299
  38.0 44.7 %collective-permute-start.4 = (bf16[7936,128]{1,0:T(8,128)(2,1)}, bf16[7936,128]{1,0:T(8,128)(2,1)S(1)}, u32[]{:S(2)}, u32[]{:S(2)}) collective-permute-start(bf16[7936,128]{1,0:T(8,128)(2,1)} %constant_dynamic-slice_fusion.12), channel_id=1, source_target_pairs={{0,4},{4,0},{1,5},{5,1},{2,6},{6,2},{3,7},{7,3},{8,12},{12,8},{9,1... | collective-permute-start | bytes 6094856 | tf_op jit(solution)/shard_map/ppermute | solution.py:211
  41.9 49.0 %collective-permute-start.9 = (bf16[3840,256]{1,0:T(8,128)(2,1)}, bf16[3840,256]{1,0:T(8,128)(2,1)}, u32[]{:S(2)}, u32[]{:S(2)}) collective-permute-start(bf16[3840,256]{1,0:T(8,128)(2,1)} %pad_maximum_fusion.4), channel_id=1, source_target_pairs={{0,8},{8,0},{16,24},{24,16},{1,9},{9,1},{17,25},{25,17},{2,10},{10... | collective-permute-start | bytes 5898248 | tf_op jit(solution)/shard_map/ppermute | solution.py:211
  41.9 46.4 %collective-permute-start.13 = (bf16[3840,256]{1,0:T(8,128)(2,1)}, bf16[3840,256]{1,0:T(8,128)(2,1)}, u32[]{:S(2)}, u32[]{:S(2)}) collective-permute-start(bf16[3840,256]{1,0:T(8,128)(2,1)} %pad_maximum_fusion.4), channel_id=1, source_target_pairs={{8,16},{16,8},{9,17},{17,9},{10,18},{18,10},{11,19},{19,11},{12,20... | collective-permute-start | bytes 5898248 | tf_op jit(solution)/shard_map/ppermute | solution.py:211
  85.1 17.8 %copy-start.44 = (s32[16,2]{0,1:T(2,128)S(1)}, s32[16,2]{0,1:T(2,128)}, u32[]{:S(2)}) copy-start(s32[16,2]{0,1:T(2,128)} %param.12) | copy-start | bytes 388
  88.3 37.6 %collective-permute-start.15 = (bf16[7936,256]{1,0:T(8,128)(2,1)}, bf16[7936,256]{1,0:T(8,128)(2,1)}, u32[]{:S(2)}, u32[]{:S(2)}) collective-permute-start(bf16[7936,256]{1,0:T(8,128)(2,1)} %pad_maximum_fusion), channel_id=1, source_target_pairs={{8,16},{16,8},{9,17},{17,9},{10,18},{18,10},{11,19},{19,11},{12,20... | collective-permute-start | bytes 12189704 | tf_op jit(solution)/shard_map/ppermute | solution.py:211
  90.9 87.5 %collective-permute-start.10 = (bf16[7936,256]{1,0:T(8,128)(2,1)}, bf16[7936,256]{1,0:T(8,128)(2,1)}, u32[]{:S(2)}, u32[]{:S(2)}) collective-permute-start(bf16[7936,256]{1,0:T(8,128)(2,1)} %pad_maximum_fusion), channel_id=1, source_target_pairs={{0,8},{8,0},{16,24},{24,16},{1,9},{9,1},{17,25},{25,17},{2,10},{10... | collective-permute-start | bytes 12189704 | tf_op jit(solution)/shard_map/ppermute | solution.py:211
  97.9 25.9 %collective-permute-start.5 = (bf16[4608,128]{1,0:T(8,128)(2,1)S(1)}, bf16[4608,128]{1,0:T(8,128)(2,1)S(1)}, u32[]{:S(2)}, u32[]{:S(2)}) collective-permute-start(bf16[4608,128]{1,0:T(8,128)(2,1)S(1)} %constant_dynamic-slice_fusion.13), channel_id=1, source_target_pairs={{0,4},{4,0},{1,5},{5,1},{2,6},{6,2},{3,7},{7,3},{8,12},{12,8},{9,1... | collective-permute-start | bytes 3538952 | tf_op jit(solution)/shard_map/ppermute | solution.py:211
  123.8 97.2 %collective-permute-start.6 = (bf16[88,128,128]{2,1,0:T(8,128)(2,1)}, bf16[88,128,128]{2,1,0:T(8,128)(2,1)}, u32[]{:S(2)}, u32[]{:S(2)}) collective-permute-start(bf16[88,128,128]{2,1,0:T(8,128)(2,1)} %pack_tiles.4), channel_id=1, source_target_pairs={{0,4},{4,0},{1,5},{5,1},{2,6},{6,2},{3,7},{7,3},{8,12},{12,8},{9,1... | collective-permute-start | bytes 8650760 | tf_op jit(solution)/shard_map/ppermute | solution.py:211
  125.9 96.1 %collective-permute-start.17 = (bf16[3840,256]{1,0:T(8,128)(2,1)}, bf16[3840,256]{1,0:T(8,128)(2,1)}, u32[]{:S(2)}, u32[]{:S(2)}) collective-permute-start(bf16[3840,256]{1,0:T(8,128)(2,1)} %collective-permute-done.9), channel_id=1, source_target_pairs={{8,16},{16,8},{9,17},{17,9},{10,18},{18,10},{11,19},{19,11},{12,20... | collective-permute-start | bytes 5898248 | tf_op jit(solution)/shard_map/ppermute | solution.py:211
  152.3 64.8 %slice-start = ((s8[8126464]{0:T(1024)(128)(4,1)}), s8[4194304]{0:T(1024)(128)(4,1)S(1)}, s32[]{:S(2)}) async-start(s8[8126464]{0:T(1024)(128)(4,1)} %bitcast.190), calls=%async_computation.6 | async-start | bytes 8388608
  178.4 103.4 %collective-permute-start.11 = (bf16[104,128,128]{2,1,0:T(8,128)(2,1)}, bf16[104,128,128]{2,1,0:T(8,128)(2,1)S(1)}, u32[]{:S(2)}, u32[]{:S(2)}) collective-permute-start(bf16[104,128,128]{2,1,0:T(8,128)(2,1)} %pack_tiles.7), channel_id=1, source_target_pairs={{0,8},{24,16},{1,9},{25,17},{2,10},{26,18},{3,11},{27,19},{4,12},{... | collective-permute-start | bytes 10223624 | tf_op jit(solution)/shard_map/ppermute | solution.py:211
  215.8 43.0 %collective-permute-start.14 = (bf16[3840,256]{1,0:T(8,128)(2,1)}, bf16[3840,256]{1,0:T(8,128)(2,1)}, u32[]{:S(2)}, u32[]{:S(2)}) collective-permute-start(bf16[3840,256]{1,0:T(8,128)(2,1)} %collective-permute-done.13), channel_id=1, source_target_pairs={{8,0},{16,24},{9,1},{17,25},{10,2},{18,26},{11,3},{19,27},{12,4},{... | collective-permute-start | bytes 5898248 | tf_op jit(solution)/shard_map/ppermute | solution.py:211
  221.1 77.9 %collective-permute-start.7 = (bf16[104,128,128]{2,1,0:T(8,128)(2,1)}, bf16[104,128,128]{2,1,0:T(8,128)(2,1)}, u32[]{:S(2)}, u32[]{:S(2)}) collective-permute-start(bf16[104,128,128]{2,1,0:T(8,128)(2,1)} %copy-done.10), channel_id=1, source_target_pairs={{0,4},{4,0},{1,5},{5,1},{2,6},{6,2},{3,7},{7,3},{8,12},{12,8},{9,1... | collective-permute-start | bytes 10223624 | tf_op jit(solution)/shard_map/ppermute | solution.py:211
  222.0 119.0 %collective-permute-start.18 = (bf16[7936,256]{1,0:T(8,128)(2,1)}, bf16[7936,256]{1,0:T(8,128)(2,1)}, u32[]{:S(2)}, u32[]{:S(2)}) collective-permute-start(bf16[7936,256]{1,0:T(8,128)(2,1)} %collective-permute-done.10), channel_id=1, source_target_pairs={{8,16},{16,8},{9,17},{17,9},{10,18},{18,10},{11,19},{19,11},{12,20... | collective-permute-start | bytes 12189704 | tf_op jit(solution)/shard_map/ppermute | solution.py:211
  226.7 82.7 %copy-start.19 = (bf16[4608,128]{1,0:T(8,128)(2,1)}, bf16[4608,128]{1,0:T(8,128)(2,1)S(1)}, u32[]{:S(2)}) copy-start(bf16[4608,128]{1,0:T(8,128)(2,1)S(1)} %get-tuple-element.135) | copy-start | bytes 3538948
  226.7 82.7 %copy-start.21 = (bf16[4608,128]{1,0:T(8,128)(2,1)}, bf16[4608,128]{1,0:T(8,128)(2,1)S(1)}, u32[]{:S(2)}) copy-start(bf16[4608,128]{1,0:T(8,128)(2,1)S(1)} %get-tuple-element.136) | copy-start | bytes 3538948
  228.6 60.8 %copy-start.27 = (bf16[3840,128]{1,0:T(8,128)(2,1)S(1)}, bf16[3840,128]{1,0:T(8,128)(2,1)}, u32[]{:S(2)}) copy-start(bf16[3840,128]{1,0:T(8,128)(2,1)} %copy-done.26) | copy-start | bytes 2949124
  228.6 60.8 %copy-start.29 = (bf16[3840,128]{1,0:T(8,128)(2,1)S(1)}, bf16[3840,128]{1,0:T(8,128)(2,1)}, u32[]{:S(2)}) copy-start(bf16[3840,128]{1,0:T(8,128)(2,1)} %copy-done.28) | copy-start | bytes 2949124
  258.8 95.0 %collective-permute-start.16 = (bf16[7936,256]{1,0:T(8,128)(2,1)}, bf16[7936,256]{1,0:T(8,128)(2,1)}, u32[]{:S(2)}, u32[]{:S(2)}) collective-permute-start(bf16[7936,256]{1,0:T(8,128)(2,1)} %collective-permute-done.15), channel_id=1, source_target_pairs={{8,0},{16,24},{9,1},{17,25},{10,2},{18,26},{11,3},{19,27},{12,4},{... | collective-permute-start | bytes 12189704 | tf_op jit(solution)/shard_map/ppermute | solution.py:211
  283.6 51.3 %collective-permute-start.12 = (bf16[4608,256]{1,0:T(8,128)(2,1)}, bf16[4608,256]{1,0:T(8,128)(2,1)}, u32[]{:S(2)}, u32[]{:S(2)}) collective-permute-start(bf16[4608,256]{1,0:T(8,128)(2,1)} %pad_maximum_fusion.3), channel_id=1, source_target_pairs={{0,8},{24,16},{1,9},{25,17},{2,10},{26,18},{3,11},{27,19},{4,12},{... | collective-permute-start | bytes 7077896 | tf_op jit(solution)/shard_map/ppermute | solution.py:211
  299.0 113.2 %collective-permute-start.8 = (bf16[164,128,128]{2,1,0:T(8,128)(2,1)}, bf16[164,128,128]{2,1,0:T(8,128)(2,1)}, u32[]{:S(2)}, u32[]{:S(2)}) collective-permute-start(bf16[164,128,128]{2,1,0:T(8,128)(2,1)} %copy-done.2), channel_id=1, source_target_pairs={{0,4},{4,0},{1,5},{5,1},{2,6},{6,2},{3,7},{7,3},{8,12},{12,8},{9,1... | collective-permute-start | bytes 16121864 | tf_op jit(solution)/shard_map/ppermute | solution.py:211
  302.4 47.5 %copy-start.3 = (bf16[512,4608]{1,0:T(8,128)(2,1)}, bf16[512,4608]{1,0:T(8,128)(2,1)S(1)}, u32[]{:S(2)}) copy-start(bf16[512,4608]{1,0:T(8,128)(2,1)S(1)} %spread_tiles.10) | copy-start | bytes 14155780
  306.3 36.9 %slice-start.8 = ((s8[4718592]{0:T(1024)(128)(4,1)}), s8[524288]{0:T(1024)(128)(4,1)S(1)}, s32[]{:S(2)}) async-start(s8[4718592]{0:T(1024)(128)(4,1)} %bitcast.198), calls=%async_computation.14 | async-start | bytes 1048576
  309.4 33.8 %slice-start.9 = ((s8[4718592]{0:T(1024)(128)(4,1)}), s8[4194304]{0:T(1024)(128)(4,1)S(1)}, s32[]{:S(2)}) async-start(s8[4718592]{0:T(1024)(128)(4,1)} %bitcast.198), calls=%async_computation.15 | async-start | bytes 8388608
  334.9 130.1 %collective-permute-start.23 = (bf16[104,128,128]{2,1,0:T(8,128)(2,1)}, bf16[104,128,128]{2,1,0:T(8,128)(2,1)}, u32[]{:S(2)}, u32[]{:S(2)}) collective-permute-start(bf16[104,128,128]{2,1,0:T(8,128)(2,1)} %collective-permute-done.7.source), channel_id=1, source_target_pairs={{0,8},{24,16},{1,9},{25,17},{2,10},{26,18},{3,11},{27,19},{4,12},{... | collective-permute-start | bytes 10223624 | tf_op jit(solution)/shard_map/ppermute | solution.py:211
  341.1 19.4 %collective-permute-start.19 = (bf16[4608,256]{1,0:T(8,128)(2,1)}, bf16[4608,256]{1,0:T(8,128)(2,1)}, u32[]{:S(2)}, u32[]{:S(2)}) collective-permute-start(bf16[4608,256]{1,0:T(8,128)(2,1)} %pad_maximum_fusion.3), channel_id=1, source_target_pairs={{8,16},{16,8},{9,17},{17,9},{10,18},{18,10},{11,19},{19,11},{12,20... | collective-permute-start | bytes 7077896 | tf_op jit(solution)/shard_map/ppermute | solution.py:211
  353.8 122.1 %collective-permute-start.34 = (bf16[7936,256]{1,0:T(8,128)(2,1)}, bf16[7936,256]{1,0:T(8,128)(2,1)}, u32[]{:S(2)}, u32[]{:S(2)}) collective-permute-start(bf16[7936,256]{1,0:T(8,128)(2,1)} %collective-permute-done.18), channel_id=1, source_target_pairs={{8,0},{16,24},{9,1},{17,25},{10,2},{18,26},{11,3},{19,27},{12,4},{... | collective-permute-start | bytes 12189704 | tf_op jit(solution)/shard_map/ppermute | solution.py:211
  360.5 131.7 %collective-permute-start.24 = (bf16[4608,256]{1,0:T(8,128)(2,1)}, bf16[4608,256]{1,0:T(8,128)(2,1)}, u32[]{:S(2)}, u32[]{:S(2)}) collective-permute-start(bf16[4608,256]{1,0:T(8,128)(2,1)} %collective-permute-done.12), channel_id=1, source_target_pairs={{8,16},{16,8},{9,17},{17,9},{10,18},{18,10},{11,19},{19,11},{12,20... | collective-permute-start | bytes 7077896 | tf_op jit(solution)/shard_map/ppermute | solution.py:211
  464.3 25.6 %collective-permute-start.20 = (f32[3,1024,128]{1,2,0:T(8,128)}, f32[3,1024,128]{1,2,0:T(8,128)}, u32[]{:S(2)}, u32[]{:S(2)}) collective-permute-start(f32[3,1024,128]{1,2,0:T(8,128)} %constant_dynamic-slice_fusion.9), channel_id=1, source_target_pairs={{0,1},{1,0},{2,3},{3,2},{4,5},{5,4},{6,7},{7,6},{8,9},{9,8},{10,11... | collective-permute-start | bytes 4718600 | tf_op jit(solution)/shard_map/ppermute | solution.py:196
  475.9 46.7 %collective-permute-start.35 = (bf16[3840,256]{1,0:T(8,128)(2,1)}, bf16[3840,256]{1,0:T(8,128)(2,1)}, u32[]{:S(2)}, u32[]{:S(2)}) collective-permute-start(bf16[3840,256]{1,0:T(8,128)(2,1)} %collective-permute-done.17), channel_id=1, source_target_pairs={{8,0},{16,24},{9,1},{17,25},{10,2},{18,26},{11,3},{19,27},{12,4},{... | collective-permute-start | bytes 5898248 | tf_op jit(solution)/shard_map/ppermute | solution.py:211
  491.7 37.7 %collective-permute-start.21 = (f32[3,64,1024]{2,1,0:T(8,128)S(1)}, f32[3,64,1024]{2,1,0:T(8,128)S(1)}, u32[]{:S(2)}, u32[]{:S(2)}) collective-permute-start(f32[3,64,1024]{2,1,0:T(8,128)S(1)} %dynamic-slice_bitcast_fusion.1), channel_id=1, source_target_pairs={{0,4},{4,0},{1,5},{5,1},{2,6},{6,2},{3,7},{7,3},{8,12},{12,8},{9,1... | collective-permute-start | bytes 2359304 | tf_op jit(solution)/shard_map/ppermute | solution.py:196
  492.1 8.9 %slice-start.10 = ((s8[4718592]{0:T(1024)(128)(4,1)}), s8[4194304]{0:T(1024)(128)(4,1)S(1)}, s32[]{:S(2)}) async-start(s8[4718592]{0:T(1024)(128)(4,1)} %bitcast.200), calls=%async_computation.16 | async-start | bytes 8388608
  500.9 24.5 %collective-permute-start.25 = (f32[3,1024,128]{1,2,0:T(8,128)S(1)}, f32[3,1024,128]{1,2,0:T(8,128)S(1)}, u32[]{:S(2)}, u32[]{:S(2)}) collective-permute-start(f32[3,1024,128]{1,2,0:T(8,128)S(1)} %constant_dynamic-slice_fusion.7), channel_id=1, source_target_pairs={{0,1},{1,0},{2,3},{3,2},{4,5},{5,4},{6,7},{7,6},{8,9},{9,8},{10,11... | collective-permute-start | bytes 4718600 | tf_op jit(solution)/shard_map/ppermute | solution.py:196
  504.3 18.2 %copy-start.38 = (f32[512,256]{0,1:T(8,128)S(1)}, f32[512,256]{0,1:T(8,128)}, u32[]{:S(2)}) copy-start(f32[512,256]{0,1:T(8,128)} %fusion.6) | copy-start | bytes 1572868
  525.9 18.4 %collective-permute-start.26 = (f32[3,64,1024]{2,1,0:T(8,128)S(1)}, f32[3,64,1024]{2,1,0:T(8,128)S(1)}, u32[]{:S(2)}, u32[]{:S(2)}) collective-permute-start(f32[3,64,1024]{2,1,0:T(8,128)S(1)} %dynamic-slice_bitcast_fusion), channel_id=1, source_target_pairs={{0,4},{4,0},{1,5},{5,1},{2,6},{6,2},{3,7},{7,3},{8,12},{12,8},{9,1... | collective-permute-start | bytes 2359304 | tf_op jit(solution)/shard_map/ppermute | solution.py:196
  529.3 17.4 %collective-permute-start.36 = (f32[1,1024,128]{1,2,0:T(8,128)S(1)}, f32[1,1024,128]{1,2,0:T(8,128)S(1)}, u32[]{:S(2)}, u32[]{:S(2)}) collective-permute-start(f32[1,1024,128]{1,2,0:T(8,128)S(1)} %fusion.17), channel_id=1, source_target_pairs={{0,1},{1,0},{2,3},{3,2},{4,5},{5,4},{6,7},{7,6},{8,9},{9,8},{10,11... | collective-permute-start | bytes 1572872 | tf_op jit(solution)/shard_map/ppermute | solution.py:196
  544.5 12.1 %collective-permute-start.27 = (f32[3,32,1024]{2,1,0:T(8,128)S(1)}, f32[3,32,1024]{2,1,0:T(8,128)S(1)}, u32[]{:S(2)}, u32[]{:S(2)}) collective-permute-start(f32[3,32,1024]{2,1,0:T(8,128)S(1)} %constant_dynamic-slice_fusion.6), channel_id=1, source_target_pairs={{0,2},{2,0},{1,3},{3,1},{4,6},{6,4},{5,7},{7,5},{8,10},{10,8},{9,1... | collective-permute-start | bytes 1179656 | tf_op jit(solution)/shard_map/ppermute | solution.py:196
  546.3 15.8 %collective-permute-start.22 = (f32[3,32,1024]{2,1,0:T(8,128)S(1)}, f32[3,32,1024]{2,1,0:T(8,128)S(1)}, u32[]{:S(2)}, u32[]{:S(2)}) collective-permute-start(f32[3,32,1024]{2,1,0:T(8,128)S(1)} %constant_dynamic-slice_fusion.8), channel_id=1, source_target_pairs={{0,2},{2,0},{1,3},{3,1},{4,6},{6,4},{5,7},{7,5},{8,10},{10,8},{9,1... | collective-permute-start | bytes 1179656 | tf_op jit(solution)/shard_map/ppermute | solution.py:196
  546.7 28.4 %copy-start.43 = (s32[32,2]{0,1:T(2,128)S(1)}, s32[32,2]{0,1:T(2,128)}, u32[]{:S(2)}) copy-start(s32[32,2]{0,1:T(2,128)} %reshape.168) | copy-start | bytes 772
  546.7 36.6 %copy-start.12 = (s32[4,4]{1,0:T(4,128)S(1)}, s32[4,4]{1,0:T(4,128)}, u32[]{:S(2)}) copy-start(s32[4,4]{1,0:T(4,128)} %constant.238.clone) | copy-start | bytes 196
  546.8 37.3 %copy-start.11 = (s32[4]{0:T(128)S(1)}, s32[4]{0:T(128)}, u32[]{:S(2)}) copy-start(s32[4]{0:T(128)} %fusion.27) | copy-start | bytes 52
  546.8 15.3 %collective-permute-start.37 = (f32[1,64,1024]{2,1,0:T(8,128)S(1)}, f32[1,64,1024]{2,1,0:T(8,128)S(1)}, u32[]{:S(2)}, u32[]{:S(2)}) collective-permute-start(f32[1,64,1024]{2,1,0:T(8,128)S(1)} %dynamic-slice_bitcast_fusion.2), channel_id=1, source_target_pairs={{0,4},{4,0},{1,5},{5,1},{2,6},{6,2},{3,7},{7,3},{8,12},{12,8},{9,1... | collective-permute-start | bytes 786440 | tf_op jit(solution)/shard_map/ppermute | solution.py:196
  556.6 12.7 %collective-permute-start.28 = (f32[3,32,1024]{2,1,0:T(8,128)S(1)}, f32[3,32,1024]{2,1,0:T(8,128)S(1)}, u32[]{:S(2)}, u32[]{:S(2)}) collective-permute-start(f32[3,32,1024]{2,1,0:T(8,128)S(1)} %dynamic-slice_add_fusion.4), channel_id=1, source_target_pairs={{8,0},{16,24},{9,1},{17,25},{10,2},{18,26},{11,3},{19,27},{12,4},{... | collective-permute-start | bytes 1179656 | tf_op jit(solution)/shard_map/ppermute | solution.py:364
  562.2 8.0 %collective-permute-start.38 = (f32[1,32,1024]{2,1,0:T(8,128)S(1)}, f32[1,32,1024]{2,1,0:T(8,128)S(1)}, u32[]{:S(2)}, u32[]{:S(2)}) collective-permute-start(f32[1,32,1024]{2,1,0:T(8,128)S(1)} %constant_dynamic-slice_fusion.5), channel_id=1, source_target_pairs={{0,2},{2,0},{1,3},{3,1},{4,6},{6,4},{5,7},{7,5},{8,10},{10,8},{9,1... | collective-permute-start | bytes 393224 | tf_op jit(solution)/shard_map/ppermute | solution.py:196
  569.4 13.2 %collective-permute-start.29 = (f32[3,32,1024]{2,1,0:T(8,128)S(1)}, f32[3,32,1024]{2,1,0:T(8,128)S(1)}, u32[]{:S(2)}, u32[]{:S(2)}) collective-permute-start(f32[3,32,1024]{2,1,0:T(8,128)S(1)} %fusion.21), channel_id=1, source_target_pairs={{0,8},{8,0},{16,24},{24,16},{1,9},{9,1},{17,25},{25,17},{2,10},{10... | collective-permute-start | bytes 1179656 | tf_op jit(solution)/shard_map/ppermute | solution.py:216
  569.5 16.8 %collective-permute-start.30 = (f32[3,32,1024]{2,1,0:T(8,128)S(1)}, f32[3,32,1024]{2,1,0:T(8,128)S(1)}, u32[]{:S(2)}, u32[]{:S(2)}) collective-permute-start(f32[3,32,1024]{2,1,0:T(8,128)S(1)} %fusion.21), channel_id=1, source_target_pairs={{8,16},{16,8},{9,17},{17,9},{10,18},{18,10},{11,19},{19,11},{12,20... | collective-permute-start | bytes 1179656 | tf_op jit(solution)/shard_map/ppermute | solution.py:217
  570.3 10.4 %collective-permute-start.39 = (f32[40,1024]{1,0:T(8,128)S(1)}, f32[40,1024]{1,0:T(8,128)S(1)}, u32[]{:S(2)}, u32[]{:S(2)}) collective-permute-start(f32[40,1024]{1,0:T(8,128)S(1)} %get-tuple-element.154), channel_id=1, source_target_pairs={{0,8},{8,0},{16,24},{24,16},{1,9},{9,1},{17,25},{25,17},{2,10},{10... | collective-permute-start | bytes 491528 | tf_op jit(solution)/shard_map/ppermute | solution.py:216
  574.5 6.9 %collective-permute-start.40 = (f32[40,1024]{1,0:T(8,128)S(1)}, f32[40,1024]{1,0:T(8,128)S(1)}, u32[]{:S(2)}, u32[]{:S(2)}) collective-permute-start(f32[40,1024]{1,0:T(8,128)S(1)} %get-tuple-element.154), channel_id=1, source_target_pairs={{8,16},{16,8},{9,17},{17,9},{10,18},{18,10},{11,19},{19,11},{12,20... | collective-permute-start | bytes 491528 | tf_op jit(solution)/shard_map/ppermute | solution.py:217
  580.7 4.3 collective-permute-start.42
  581.3 10.6 %collective-permute-start.41 = (f32[40,1024]{1,0:T(8,128)S(1)}, f32[40,1024]{1,0:T(8,128)S(1)}, u32[]{:S(2)}, u32[]{:S(2)}) collective-permute-start(f32[40,1024]{1,0:T(8,128)S(1)} %collective-permute-done.40), channel_id=1, source_target_pairs={{8,0},{16,24},{9,1},{17,25},{10,2},{18,26},{11,3},{19,27},{12,4},{... | collective-permute-start | bytes 491528 | tf_op jit(solution)/shard_map/ppermute | solution.py:219
  582.7 9.3 %collective-permute-start.32 = (f32[3,32,1024]{2,1,0:T(8,128)S(1)}, f32[3,32,1024]{2,1,0:T(8,128)S(1)}, u32[]{:S(2)}, u32[]{:S(2)}) collective-permute-start(f32[3,32,1024]{2,1,0:T(8,128)S(1)} %collective-permute-done.29), channel_id=1, source_target_pairs={{8,16},{16,8},{9,17},{17,9},{10,18},{18,10},{11,19},{19,11},{12,20... | collective-permute-start | bytes 1179656 | tf_op jit(solution)/shard_map/ppermute | solution.py:218
  584.9 12.9 %collective-permute-start.43 = (f32[40,1024]{1,0:T(8,128)S(1)}, f32[40,1024]{1,0:T(8,128)S(1)}, u32[]{:S(2)}, u32[]{:S(2)}) collective-permute-start(f32[40,1024]{1,0:T(8,128)S(1)} %collective-permute-done.42), channel_id=1, source_target_pairs={{8,0},{16,24},{9,1},{17,25},{10,2},{18,26},{11,3},{19,27},{12,4},{... | collective-permute-start | bytes 491528 | tf_op jit(solution)/shard_map/ppermute | solution.py:220
  586.3 15.8 %collective-permute-start.31 = (f32[3,32,1024]{2,1,0:T(8,128)S(1)}, f32[3,32,1024]{2,1,0:T(8,128)S(1)}, u32[]{:S(2)}, u32[]{:S(2)}) collective-permute-start(f32[3,32,1024]{2,1,0:T(8,128)S(1)} %collective-permute-done.30), channel_id=1, source_target_pairs={{8,0},{16,24},{9,1},{17,25},{10,2},{18,26},{11,3},{19,27},{12,4},{... | collective-permute-start | bytes 1179656 | tf_op jit(solution)/shard_map/ppermute | solution.py:219
  592.0 14.3 %collective-permute-start.33 = (f32[3,32,1024]{2,1,0:T(8,128)S(1)}, f32[3,32,1024]{2,1,0:T(8,128)S(1)}, u32[]{:S(2)}, u32[]{:S(2)}) collective-permute-start(f32[3,32,1024]{2,1,0:T(8,128)S(1)} %collective-permute-done.32), channel_id=1, source_target_pairs={{8,0},{16,24},{9,1},{17,25},{10,2},{18,26},{11,3},{19,27},{12,4},{... | collective-permute-start | bytes 1179656 | tf_op jit(solution)/shard_map/ppermute | solution.py:220
  615.8 3.0 collective-permute-start.44
  615.9 28.3 %copy-start.42 = (s32[4,256]{1,0:T(4,128)S(1)}, s32[4,256]{1,0:T(4,128)}, u32[]{:S(2)}) copy-start(s32[4,256]{1,0:T(4,128)} %copy-done.41) | copy-start | bytes 12292
  615.9 28.3 %copy-start.45 = (s32[16,2]{0,1:T(2,128)S(1)}, s32[16,2]{0,1:T(2,128)}, u32[]{:S(2)}) copy-start(s32[16,2]{0,1:T(2,128)} %param.12) | copy-start | bytes 388
  620.2 14.7 %collective-permute-start.45 = (f32[1,2,1,4,136,128]{5,4,3,2,1,0:T(8,128)S(1)}, f32[1,2,1,4,136,128]{5,4,3,2,1,0:T(8,128)S(1)}, u32[]{:S(2)}, u32[]{:S(2)}) collective-permute-start(f32[1,2,1,4,136,128]{5,4,3,2,1,0:T(8,128)S(1)} %constant_dynamic-slice_fusion.3), channel_id=1, source_target_pairs={{0,4},{4,0},{1,5},{5,1},{2,6},{6,2},{3,7},{7,3},{8,12},{12,8},{9,1... | collective-permute-start | bytes 1671176 | tf_op jit(solution)/shard_map/ppermute | solution.py:196
  635.0 7.9 %collective-permute-start.46 = (f32[1,1,1,4,136,128]{5,4,3,2,1,0:T(8,128)S(1)}, f32[1,1,1,4,136,128]{5,4,3,2,1,0:T(8,128)S(1)}, u32[]{:S(2)}, u32[]{:S(2)}) collective-permute-start(f32[1,1,1,4,136,128]{5,4,3,2,1,0:T(8,128)S(1)} %constant_dynamic-slice_fusion.2), channel_id=1, source_target_pairs={{0,2},{2,0},{1,3},{3,1},{4,6},{6,4},{5,7},{7,5},{8,10},{10,8},{9,1... | collective-permute-start | bytes 835592 | tf_op jit(solution)/shard_map/ppermute | solution.py:196
  (42 other events, 179.6 us)

commit v8 on v7

--- a/solution.py
+++ b/solution.py
@@ -76,64 +76,132 @@
     )(info, hist)
 
 
-def spread_kernel(blk, row_blocks, parts, slots, info, source, *refs):
-    outs, sem = refs[: len(parts)], refs[len(parts)]
-    base = info[0]
-    used = jnp.int32(0)
-    first = 0
-    for out, columns in zip(outs, parts):
-
-        def one_column(c, used, out=out, first=first):
-            start = pl.multiple_of((base + first + c) * blk, blk)
-            place = pl.multiple_of(c * blk, blk)
-            for b in range(row_blocks):
-                there = info[1 + (first + c) * row_blocks + b] != 0
-                if slots is not None:
-                    there = jnp.logical_and(there, used < slots)
-                rows = pl.ds(b * blk, blk)
-
-                @pl.when(there)
+STRIDE = 4
+
+
+def product_kernel(blk, row_blocks, steps, slots, paired, info, *refs):
+    count, groups = len(slots), len(paired)
+    sources, refs = refs[:count], refs[count:]
+    planes, at = [], 0
+    for two in paired:
+        planes.append(refs[at : at + 1 + two])
+        at += 1 + two
+    out, total, tiles, held, tile_sem, held_sem = refs[at:]
+    rows = row_blocks * blk
+    depth = STRIDE * blk
+    inner, base = info[0] != 0, info[1]
+    per_source = steps * STRIDE * row_blocks
+
+    def fetch(i, slot, used, active):
+        first = pl.multiple_of(i * depth, depth)
+        for g, choice in enumerate(planes):
+            for which, ref in enumerate(choice):
+                wanted = active
+                if len(choice) == 2:
+                    wanted = jnp.logical_and(active, inner if which == 0 else jnp.logical_not(inner))
+
+                @pl.when(wanted)
                 def _():
-                    tile = source.at[rows, pl.ds(start, blk)] if slots is None else source.at[used]
-                    pltpu.make_async_copy(tile, out.at[rows, pl.ds(place, blk)], sem).start()
-
-                @pl.when(jnp.logical_not(there))
-                def _():
-                    out[rows, pl.ds(place, blk)] = jnp.zeros((blk, blk), out.dtype)
-
-                used = used + there.astype(jnp.int32)
-            return used
-
-        used = lax.fori_loop(0, columns, one_column, used)
-        first += columns
-
-    def one_wait(_, carry):
-        tile = source.at[pl.ds(0, blk), pl.ds(0, blk)] if slots is None else source.at[0]
-        pltpu.make_async_copy(tile, outs[0].at[pl.ds(0, blk), pl.ds(0, blk)], sem).wait()
-        return carry
-
-    lax.fori_loop(0, used, one_wait, 0)
-
-
-def spread(source, mask, base, parts):
-    row_blocks = mask.shape[0]
-    packed = base is None
-    blk = source.shape[1] if packed else source.shape[0] // row_blocks
-    base = 0 if packed else base
-    info = jnp.concatenate([jnp.reshape(base, (1,)).astype(jnp.int32), mask.T.reshape(-1)])
-    shapes = [jax.ShapeDtypeStruct((row_blocks * blk, columns * blk), source.dtype) for columns in parts]
+                    pltpu.make_async_copy(ref.at[pl.ds(first, depth)], held.at[slot, g], held_sem.at[slot]).start()
+
+        started = jnp.int32(0)
+        following = []
+        for k in range(count):
+            mine = used[k]
+            for j in range(STRIDE):
+                column = i * STRIDE + j
+                start = pl.multiple_of((base + column) * blk, blk)
+                for b in range(row_blocks):
+                    there = info[2 + count + k * per_source + column * row_blocks + b] != 0
+                    there = jnp.logical_and(there, active)
+                    if slots[k] is not None:
+                        there = jnp.logical_and(there, mine < slots[k])
+                    place = (pl.ds(k * rows + b * blk, blk), pl.ds(j * blk, blk))
+
+                    @pl.when(there)
+                    def _():
+                        if slots[k] is None:
+                            tile = sources[k].at[pl.ds(b * blk, blk), pl.ds(start, blk)]
+                        else:
+                            tile = sources[k].at[mine]
+                        pltpu.make_async_copy(tile, tiles.at[(slot,) + place], tile_sem.at[slot]).start()
+
+                    @pl.when(jnp.logical_not(there))
+                    def _():
+                        tiles[(slot,) + place] = jnp.zeros((blk, blk), tiles.dtype)
+
+                    mine = mine + there.astype(jnp.int32)
+                    started = started + there.astype(jnp.int32)
+            following.append(mine)
+        return tuple(following), started
+
+    total[...] = jnp.zeros_like(total)
+    first_used, first_started = fetch(0, 0, (jnp.int32(0),) * count, True)
+
+    def one_step(i, carry):
+        used, started = carry
+        slot = lax.rem(i, 2)
+        after_used, after_started = fetch(
+            jnp.minimum(i + 1, steps - 1), 1 - slot, used, i + 1 < steps
+        )
+
+        def one_wait(_, nothing):
+            tile = tiles.at[slot, pl.ds(0, blk), pl.ds(0, blk)]
+            pltpu.make_async_copy(tile, tile, tile_sem.at[slot]).wait()
+            return nothing
+
+        lax.fori_loop(0, started, one_wait, 0)
+        for g in range(groups):
+            pltpu.make_async_copy(held.at[slot, g], held.at[slot, g], held_sem.at[slot]).wait()
+        for k in range(count):
+            block = tiles[slot, k * rows : (k + 1) * rows, :]
+            for g in range(groups):
+                total[g, k * rows : (k + 1) * rows, :] += jnp.dot(
+                    block, held[slot, g], preferred_element_type=jnp.float32
+                )
+        return after_used, after_started
+
+    lax.fori_loop(0, steps, one_step, (first_used, first_started))
+    for k in range(count):
+        place = pl.ds(pl.multiple_of(info[2 + k], rows), rows)
+        for g in range(groups):
+            out[g, :, place] = total[g, k * rows : (k + 1) * rows, :].T
+
+
+def product(sources, masks, planes, inner, base, places):
+    row_blocks, columns = masks[0].shape
+    packed = [v.ndim == 3 for v in sources]
+    blk = next(v.shape[1] if p else v.shape[0] // row_blocks for v, p in zip(sources, packed))
+    rows = row_blocks * blk
+    wide = planes[0][0].shape[1]
+    dtype = sources[0].dtype
+    head = [jnp.asarray(v, jnp.int32).reshape(1) for v in [inner, base] + list(places)]
+    info = jnp.concatenate(head + [m.T.reshape(-1) for m in masks])
+    flat = [v for choice in planes for v in choice]
+    shape = (len(planes), wide, len(sources) * rows)
+    flops = 2 * shape[0] * shape[1] * shape[2] * columns * blk
+    size = columns * blk * (wide * len(planes) + rows * len(sources) // 2) * 2
     return pl.pallas_call(
-        functools.partial(spread_kernel, blk, row_blocks, parts, source.shape[0] if packed else None),
-        out_shape=shapes,
-        in_specs=[pl.BlockSpec(memory_space=pltpu.SMEM), pl.BlockSpec(memory_space=pl.ANY)],
-        out_specs=[pl.BlockSpec(memory_space=pltpu.VMEM)] * len(parts),
-        scratch_shapes=[pltpu.SemaphoreType.DMA],
+        functools.partial(
+            product_kernel, blk, row_blocks, columns // STRIDE,
+            [v.shape[0] if p else None for v, p in zip(sources, packed)],
+            [len(choice) - 1 for choice in planes],
+        ),
+        out_shape=jax.ShapeDtypeStruct(shape, jnp.float32),
+        in_specs=[pl.BlockSpec(memory_space=pltpu.SMEM)]
+        + [pl.BlockSpec(memory_space=pl.ANY)] * (len(sources) + len(flat)),
+        out_specs=pl.BlockSpec(memory_space=pltpu.VMEM),
+        scratch_shapes=[
+            pltpu.VMEM((len(planes), len(sources) * rows, wide), jnp.float32),
+            pltpu.VMEM((2, len(sources) * rows, STRIDE * blk), dtype),
+            pltpu.VMEM((2, len(planes), STRIDE * blk, wide), dtype),
+            pltpu.SemaphoreType.DMA((2,)),
+            pltpu.SemaphoreType.DMA((2,)),
+        ],
         compiler_params=params(vmem_limit_bytes=32 << 20),
-        cost_estimate=pl.CostEstimate(
-            flops=0, bytes_accessed=4 * sum(parts) * row_blocks * blk * blk, transcendentals=0
-        ),
-        name="spread_tiles",
-    )(info, source)
+        cost_estimate=pl.CostEstimate(flops=flops, bytes_accessed=size, transcendentals=0),
+        name="tiles_times_planes",
+    )(info, *sources, *flat)
 
 
 def dots_kernel(blk, count, ids, early, late, out):
@@ -259,9 +327,9 @@
     columns = act_blocks // wide
     tile_mask = (tile_mask != 0).astype(jnp.int32)
 
-    lent = columns * LENT[0] // LENT[1]
+    lent = columns * LENT[0] // LENT[1] // STRIDE * STRIDE
     kept = columns - lent
-    cuts = [0, kept // 3, kept, columns]
+    cuts = [0, (kept // 3 + STRIDE // 2) // STRIDE * STRIDE, kept, columns]
     widths = [b - a for a, b in zip(cuts[:-1], cuts[1:])]
     slots = [room(w * row_blocks) for w in widths]
 
@@ -323,48 +391,43 @@
     far += middle.send([near[2]], "z", [MIDDLE])
     outer = [outward.send([v], "z", [OUTWARD])[0] for v in (mid[0], mid[1], far[1], far[0])]
     loans = loans + inward.send(tiles[2], "z", [INWARD] * len(others))
-    held = [
-        [groups[c], near[c], jnp.where(inner, mid[c], outer[c]), jnp.where(inner, far[c], outer[3 - c])]
-        for c in range(2)
-    ]
-    held.append([groups[2], near[2], mid[2], far[2]])
-
     over = jnp.int32(0)
-    sessions = [[None] * 3 for _ in range(wide)]
     for c in range(3):
         for owner in range(wide):
             count = jnp.sum(tile_mask[:, owner * columns + cuts[c] : owner * columns + cuts[c + 1]])
             over = jnp.maximum(over, (count > slots[c]).astype(jnp.int32))
-        for k in range(wide):
-            mask = masks[k][:, cuts[c] : cuts[c + 1]]
-            if k == 0:
-                (sessions[k][c],) = spread(hist, after(mask, near[0]), x * columns + cuts[c], (widths[c],))
-            else:
-                (sessions[k][c],) = spread(tiles[c][k - 1], mask, None, (widths[c],))
-    guests = [{2: spread(t, guest_masks[k], None, (widths[2],))[0]} for k, t in enumerate(loans)]
-
-    def total(sources, chunks, s):
-        found = []
-        for source in sources:
-            one = None
-            for c in chunks:
-                term = jnp.dot(source[c], held[c][s], preferred_element_type=jnp.float32)
-                one = term if one is None else one + term
-            found.append(one)
-        return in_row_order(found, 0)
+    row_places = [(x - k) % wide * rows for k in range(wide)]
+    early_groups = [[[groups[c]], [near[c]], [mid[c], outer[c]]] for c in range(2)]
+    last_group = [[[far[c], outer[3 - c]]] for c in range(2)]
+
+    def times(c, sources, which, held, places):
+        own = [masks[k][:, cuts[c] : cuts[c + 1]] for k in which]
+        return product(sources, own, held, inner, x * columns + cuts[c], places)
+
+    every = range(wide)
+    part0 = times(0, [hist] + tiles[0], every, early_groups[0], row_places)
+    part2 = times(2, [hist] + tiles[2], every, [[groups[2]], [near[2]], [mid[2]], [far[2]]], row_places)
+    part1 = [times(1, [([hist] + tiles[1])[k]], [k], early_groups[1], [0]) for k in every]
+    first_three = part0 + part2[:3] + in_row_order(part1, 2)
+    end1 = times(1, [hist] + tiles[1], every, last_group[1], row_places)
+    end0 = times(0, [hist] + tiles[0], every, last_group[0], row_places)
+    last_one = end0 + (end1 + part2[3:])
+    visitors = in_row_order(
+        [
+            product([t], [m], [[groups[2]], [mid[2]], [far[2]]], inner, 0, [0])
+            for t, m in zip(loans, guest_masks)
+        ],
+        2,
+    )
 
     def summed(totals):
-        whole = scatter_sum(jnp.stack(totals), "core", 2)
-        whole = jnp.swapaxes(whole, 1, 2)
-        return scatter_sum(scatter_sum(whole, "x", 1), "y", 1)
-
-    every = range(3)
-    first_three = summed([total(sessions, every, s) for s in range(3)])
-    visitors = summed([total(guests, (2,), s) for s in (0, 2, 3)])
-    visitors = lax.ppermute(visitors, "z", OUTWARD)
+        return scatter_sum(scatter_sum(scatter_sum(totals, "core", 1), "x", 1), "y", 1)
+
+    first_three = summed(first_three)
+    visitors = lax.ppermute(summed(visitors), "z", OUTWARD)
     early = first_three.at[1:].add(visitors[:2])
     early = jnp.stack(along_line(early, inner))
-    last_one = summed([total(sessions, every, 3)])[0] + visitors[2]
+    last_one = summed(last_one)[0] + visitors[2]
     flags = jnp.full((8, last_one.shape[1]), over.astype(jnp.float32))
     late = jnp.stack(along_line(jnp.concatenate([last_one, flags]), inner))
 

time: 664 us -> 629 us (0.947); the launches traced: 652 us -> 627 us
  matrix products: 121 us -> 0 us
  Pallas kernels: 58.8 us -> 133 us
  waiting for transfers between devices: 293 us -> 345 us
  starting transfers between devices: 101 us -> 81.3 us
  local copies, waits for them, and re-layouts: 33.9 us -> 20.5 us
    dot_general x30 -> x0, matrix products: 121 us -> none  [total(): term = jnp.dot(source[c], held[c][s], preferred_element_type=jnp.float32)]
    pallas_call x8, Pallas kernels: 36 us -> 106 us  [product(): pl.pallas_call(functools.partial(product_kernel, blk, row_blocks, columns...]
    ppermute x21, waiting for transfers between devices: 195 us -> 225 us  [send(): lax.ppermute(v, axis, route)]
    ppermute x21, starting transfers between devices: 71.6 us -> 48.8 us  [send(): lax.ppermute(v, axis, route)]
    unnamed x118 -> x28, local copies, waits for them, and re-layouts: 18.7 us -> 4.31 us
    ppermute x1, waiting for transfers between devices: 5.36 us -> 14.6 us  [body(): visitors = lax.ppermute(summed(visitors), 'z', OUTWARD)]
  transfers between devices with their start and end apart: 47 -> 47, of which waited for: 21 -> 24; matrix products, arithmetic and copies ran while one was open for 24% -> 7% of each run, Pallas kernels for 8% -> 20%
where the time goes in v8:
time: 629 us; the launch traced here: 627 us
  waiting for transfers between devices  345 us (55%)
  Pallas kernels  133 us (21%)
  starting transfers between devices  81.3 us (13%)
  other arithmetic  28.7 us (5%)
  local copies, waits for them, and re-layouts  20.5 us (3%)
  between operations  18.7 us (3%)
    ppermute x21, waiting for transfers between devices, send(): lax.ppermute(v, axis, route)  225 us
    pallas_call x8, Pallas kernels, product(): pl.pallas_call(functools.partial(product_kernel, blk, row_blocks, columns...  106 us
    ppermute x12, waiting for transfers between devices, scatter_sum(): total = total + lax.ppermute(part((here + k) % count), axis, turn(count, k))  57 us
    ppermute x21, starting transfers between devices, send(): lax.ppermute(v, axis, route)  48.8 us
    ppermute x1, waiting for transfers between devices, body(): lax.ppermute(both_of(o), 'x', r)  19.4 us
    pallas_call x4, Pallas kernels, pack(): pl.pallas_call(functools.partial(pack_kernel, blk, row_blocks, columns, s...  17.5 us
    ppermute x1, waiting for transfers between devices, body(): visitors = lax.ppermute(summed(visitors), 'z', OUTWARD)  14.6 us
    ppermute x2, waiting for transfers between devices, along_line(): out1 = lax.ppermute(middle, 'z', OUTWARD)  13.1 us
  transfers between devices with their start and end apart: 47, of which 24 were waited for; matrix products, arithmetic and copies ran while one was open for 7% of the time, Pallas kernels for 20%

profile of v8, /device:TPU:0, one launch (start us, length us, event | category | flops | bytes accessed | tf_op | source)
XLA Modules:
  0.0 626.8 jit_solution(10494378043605512356)
XLA Ops:
  6.5 2.9 collective-permute-start
  10.2 3.5 collective-permute-start.1
  15.6 1.5 collective-permute-start.2
  17.1 3.0 constant_dynamic-slice_fusion.14
  20.0 19.4 %collective-permute-done.2 = s32[2,4,128]{2,1,0:T(4,128)S(1)} collective-permute-done((s32[2,4,128]{2,1,0:T(4,128)S(1)}, s32[2,4,128]{2,1,0:T(4,128)S(1)}, u32[]{:S(2)}, u32[]{:S(2)}) %collective-permute-start.2) | collective-permute-done | bytes 4128 | tf_op jit(solution)/shard_map/ppermute | solution.py:367
  40.0 1.6 broadcast_select_fusion.5
  42.0 2.0 collective-permute-start.8
  43.9 38.9 %collective-permute-done.4 = bf16[7680,128]{1,0:T(8,128)(2,1)} collective-permute-done((bf16[7680,128]{1,0:T(8,128)(2,1)}, bf16[7680,128]{1,0:T(8,128)(2,1)}, u32[]{:S(2)}, u32[]{:S(2)}) %collective-permute-start.4) | collective-permute-done | bytes 1966112 | tf_op jit(solution)/shard_map/ppermute | solution.py:279
  82.8 2.9 broadcast_select_fusion.1
  85.8 2.3 pad_maximum_fusion.refs_1_
  88.1 2.6 collective-permute-start.14
  90.7 4.2 collective-permute-start.9
  96.2 1.6 collective-permute-start.5
  98.0 4.0 pack_tiles.4
  102.0 20.2 %collective-permute-done.5 = bf16[4608,128]{1,0:T(8,128)(2,1)} collective-permute-done((bf16[4608,128]{1,0:T(8,128)(2,1)S(1)}, bf16[4608,128]{1,0:T(8,128)(2,1)}, u32[]{:S(2)}, u32[]{:S(2)}) %collective-permute-start.5) | collective-permute-done | bytes 1179680 | tf_op jit(solution)/shard_map/ppermute | solution.py:279
  122.2 1.5 collective-permute-start.6
  123.7 2.0 collective-permute-start.15
  125.7 51.2 %collective-permute-done.9.refs_2_ = bf16[7680,256]{1,0:T(8,128)(2,1)} collective-permute-done((bf16[7680,256]{1,0:T(8,128)(2,1)}, bf16[7680,256]{1,0:T(8,128)(2,1)}, u32[]{:S(2)}, u32[]{:S(2)}) %collective-permute-start.9) | collective-permute-done | bytes 3932192 | tf_op jit(solution)/shard_map/ppermute | solution.py:279
  178.5 4.0 pack_tiles.5
  182.5 6.5 %collective-permute-done.6.refs_1_ = bf16[94,128,128]{2,1,0:T(8,128)(2,1)S(1)} collective-permute-done((bf16[94,128,128]{2,1,0:T(8,128)(2,1)}, bf16[94,128,128]{2,1,0:T(8,128)(2,1)S(1)}, u32[]{:S(2)}, u32[]{:S(2)}) %collective-permute-start.6) | collective-permute-done | bytes 3080224 | tf_op jit(solution)/shard_map/ppermute | solution.py:279
  189.0 1.5 collective-permute-start.11
  190.9 4.1 pack_tiles.6
  195.0 3.0 collective-permute-start.12
  198.0 2.6 collective-permute-start.16
  200.6 23.3 %collective-permute-done.10.refs_5_ = bf16[4096,256]{1,0:T(8,128)(2,1)} collective-permute-done((bf16[4096,256]{1,0:T(8,128)(2,1)}, bf16[4096,256]{1,0:T(8,128)(2,1)}, u32[]{:S(2)}, u32[]{:S(2)}) %collective-permute-start.10) | collective-permute-done | bytes 2097184 | tf_op jit(solution)/shard_map/ppermute | solution.py:279
  225.5 5.4 pack_tiles.7
  231.0 2.1 broadcast_select_fusion.3
  233.1 29.9 %collective-permute-done.11.refs_1_ = bf16[104,128,128]{2,1,0:T(8,128)(2,1)} collective-permute-done((bf16[104,128,128]{2,1,0:T(8,128)(2,1)}, bf16[104,128,128]{2,1,0:T(8,128)(2,1)}, u32[]{:S(2)}, u32[]{:S(2)}) %collective-permute-start.11) | collective-permute-done | bytes 3407904 | tf_op jit(solution)/shard_map/ppermute | solution.py:279
  264.4 1.7 pad_maximum_fusion.1.refs_2_.refs_1_
  266.1 5.4 collective-permute-start.13
  271.6 2.0 collective-permute-start.17
  279.8 28.2 %collective-permute-done.20.refs_4_ = bf16[7680,256]{1,0:T(8,128)(2,1)} collective-permute-done((bf16[7680,256]{1,0:T(8,128)(2,1)}, bf16[7680,256]{1,0:T(8,128)(2,1)}, u32[]{:S(2)}, u32[]{:S(2)}) %collective-permute-start.20) | collective-permute-done | bytes 3932192 | tf_op jit(solution)/shard_map/ppermute | solution.py:279
  310.3 4.8 collective-permute-done.13.refs_3_
  315.1 10.6 %collective-permute-start.24 = (bf16[104,128,128]{2,1,0:T(8,128)(2,1)}, bf16[104,128,128]{2,1,0:T(8,128)(2,1)}, u32[]{:S(2)}, u32[]{:S(2)}) collective-permute-start(bf16[104,128,128]{2,1,0:T(8,128)(2,1)} %collective-permute-done.11.refs_1_), channel_id=1, source_target_pairs={{0,8},{24,16},{1,9},{25,17},{2,10},{26,18},{3,11},{27,19},{4,12},{... | collective-permute-start | bytes 10223624 | tf_op jit(solution)/shard_map/ppermute | solution.py:279
  325.7 2.1 collective-permute-start.18
  329.1 1.6 copy-done.2
  330.7 14.5 %tiles_times_planes.8 = f32[3,256,1024]{2,1,0:T(8,128)S(1)} custom-call(s32[260]{0:T(512)S(1)} %concatenate.58.info, bf16[512,32768]{1,0:T(8,128)(2,1)} %refs_0_.9, bf16[94,128,128]{2,1,0:T(8,128)(2,1)S(1)} %collective-permute-done.6.refs_1_, bf16[4096,256]{1,0:T(8,128)(2,1)S(1)} %copy-done.2, bf16[4096,256]{1,0:T(8,128)(2,1)} %collective-permute-done.7.refs_3_, ...), custom_call_target="tpu_custom_call" | custom-call | flops 6442450944 | bytes 10485760 | tf_op jit(solution)/shard_map/tiles_times_planes/pallas_call | solution.py:184
  345.2 15.0 %tiles_times_planes.11 = f32[3,256,512]{2,1,0:T(8,128)S(1)} custom-call(s32[243]{0:T(256)S(1)} %get-tuple-element.154.info, bf16[512,32768]{1,0:T(8,128)(2,1)} %refs_0_.9, bf16[7680,256]{1,0:T(8,128)(2,1)} %pad_maximum_fusion.refs_1_, bf16[7680,256]{1,0:T(8,128)(2,1)} %collective-permute-done.9.refs_2_, bf16[7680,256]{1,0:T(8,128)(2,1)} %collective-permute-done.14.refs_3_, ...), custom_call_target="tpu_custom_call" | custom-call | flops 6039797760 | bytes 15728640 | tf_op jit(solution)/shard_map/tiles_times_planes/pallas_call | solution.py:184
  360.2 11.8 %collective-permute-done.19.refs_0_.refs_1_ = bf16[160,128,128]{2,1,0:T(8,128)(2,1)} collective-permute-done((bf16[160,128,128]{2,1,0:T(8,128)(2,1)}, bf16[160,128,128]{2,1,0:T(8,128)(2,1)}, u32[]{:S(2)}, u32[]{:S(2)}) %collective-permute-start.19) | collective-permute-done | bytes 5242912 | tf_op jit(solution)/shard_map/ppermute | solution.py:279
  371.9 15.0 %tiles_times_planes.10 = f32[3,256,512]{2,1,0:T(8,128)S(1)} custom-call(s32[243]{0:T(256)S(1)} %get-tuple-element.153.info, bf16[160,128,128]{2,1,0:T(8,128)(2,1)} %collective-permute-done.19.refs_0_.refs_1_, bf16[7680,256]{1,0:T(8,128)(2,1)} %pad_maximum_fusion.refs_1_, bf16[7680,256]{1,0:T(8,128)(2,1)} %collective-permute-done.9.refs_2_, ...), custom_call_target="tpu_custom_call" | custom-call | flops 6039797760 | bytes 15728640 | tf_op jit(solution)/shard_map/tiles_times_planes/pallas_call | solution.py:184
  387.4 10.1 %collective-permute-done.34.refs_3_ = bf16[7680,256]{1,0:T(8,128)(2,1)} collective-permute-done((bf16[7680,256]{1,0:T(8,128)(2,1)}, bf16[7680,256]{1,0:T(8,128)(2,1)}, u32[]{:S(2)}, u32[]{:S(2)}) %collective-permute-start.34) | collective-permute-done | bytes 3932192 | tf_op jit(solution)/shard_map/ppermute | solution.py:279
  398.8 9.6 %tiles_times_planes.13 = f32[3,256,512]{2,1,0:T(8,128)S(1)} custom-call(s32[147]{0:T(256)S(1)} %get-tuple-element.151.info, bf16[104,128,128]{2,1,0:T(8,128)(2,1)} %collective-permute-done.12.refs_0_, bf16[4608,256]{1,0:T(8,128)(2,1)} %pad_maximum_fusion.1.refs_2_.refs_1_, bf16[4608,256]{1,0:T(8,128)(2,1)} %collective-permute-done.17.refs_4_.refs_2_, ...), custom_call_target="tpu_custom_call" | custom-call | flops 3623878656 | bytes 9437184 | tf_op jit(solution)/shard_map/tiles_times_planes/pallas_call | solution.py:184
  408.4 9.6 %tiles_times_planes.12 = f32[3,256,512]{2,1,0:T(8,128)S(1)} custom-call(s32[147]{0:T(256)S(1)} %get-tuple-element.152.info, bf16[104,128,128]{2,1,0:T(8,128)(2,1)} %collective-permute-done.24.refs_0_, bf16[4608,256]{1,0:T(8,128)(2,1)} %pad_maximum_fusion.1.refs_2_.refs_1_, bf16[4608,256]{1,0:T(8,128)(2,1)} %collective-permute-done.17.refs_4_.refs_2_, ...), custom_call_target="tpu_custom_call" | custom-call | flops 3623878656 | bytes 9437184 | tf_op jit(solution)/shard_map/tiles_times_planes/pallas_call | solution.py:184
  420.7 18.1 %tiles_times_planes.9 = f32[4,256,1024]{2,1,0:T(8,128)S(1)} custom-call(s32[292]{0:T(512)S(1)} %concatenate.62.info, bf16[512,32768]{1,0:T(8,128)(2,1)} %refs_0_.9, bf16[104,128,128]{2,1,0:T(8,128)(2,1)} %collective-permute-done.11.refs_1_, bf16[4608,256]{1,0:T(8,128)(2,1)} %pad_maximum_fusion.1.refs_2_.refs_1_, ...), custom_call_target="tpu_custom_call" | custom-call | flops 9663676416 | bytes 14155776 | tf_op jit(solution)/shard_map/tiles_times_planes/pallas_call | solution.py:184
  443.3 15.0 %tiles_times_planes.15 = f32[1,256,1024]{2,1,0:T(8,128)S(1)} custom-call(s32[484]{0:T(512)S(1)} %concatenate.73.info, bf16[512,32768]{1,0:T(8,128)(2,1)} %refs_0_.9, bf16[160,128,128]{2,1,0:T(8,128)(2,1)} %collective-permute-done.19.refs_0_.refs_1_, bf16[7680,256]{1,0:T(8,128)(2,1)} %collective-permute-done.16.refs_2_, ...), custom_call_target="tpu_custom_call" | custom-call | flops 4026531840 | bytes 11796480 | tf_op jit(solution)/shard_map/tiles_times_planes/pallas_call | solution.py:184
  458.4 9.4 %tiles_times_planes.14 = f32[1,256,1024]{2,1,0:T(8,128)S(1)} custom-call(s32[260]{0:T(512)S(1)} %concatenate.58.info, bf16[512,32768]{1,0:T(8,128)(2,1)} %refs_0_.9, bf16[94,128,128]{2,1,0:T(8,128)(2,1)S(1)} %collective-permute-done.6.refs_1_, bf16[4096,256]{1,0:T(8,128)(2,1)} %collective-permute-done.15.refs_2_, ...), custom_call_target="tpu_custom_call" | custom-call | flops 2147483648 | bytes 6291456 | tf_op jit(solution)/shard_map/tiles_times_planes/pallas_call | solution.py:184
  467.8 1.6 fusion.8
  471.0 1.8 fusion.7
  475.3 1.7 dynamic-slice_add_fusion
  480.4 14.2 %collective-permute-done.26 = f32[3,64,1024]{2,1,0:T(8,128)} collective-permute-done((f32[3,64,1024]{2,1,0:T(8,128)}, f32[3,64,1024]{2,1,0:T(8,128)}, u32[]{:S(2)}, u32[]{:S(2)}) %collective-permute-start.26) | collective-permute-done | bytes 786464 | tf_op jit(solution)/shard_map/ppermute | solution.py:264
  498.8 12.7 %collective-permute-done.22 = f32[3,64,1024]{2,1,0:T(8,128)} collective-permute-done((f32[3,64,1024]{2,1,0:T(8,128)}, f32[3,64,1024]{2,1,0:T(8,128)}, u32[]{:S(2)}, u32[]{:S(2)}) %collective-permute-start.22) | collective-permute-done | bytes 786464 | tf_op jit(solution)/shard_map/ppermute | solution.py:264
  517.5 5.9 collective-permute-done.23
  523.5 14.6 %collective-permute-done.28 = f32[3,32,1024]{2,1,0:T(8,128)S(1)} collective-permute-done((f32[3,32,1024]{2,1,0:T(8,128)S(1)}, f32[3,32,1024]{2,1,0:T(8,128)S(1)}, u32[]{:S(2)}, u32[]{:S(2)}) %collective-permute-start.28) | collective-permute-done | bytes 393248 | tf_op jit(solution)/shard_map/ppermute | solution.py:427
  539.4 3.0 collective-permute-start.39
  543.1 7.4 %collective-permute-done.39 = f32[40,1024]{1,0:T(8,128)S(1)} collective-permute-done((f32[40,1024]{1,0:T(8,128)S(1)}, f32[40,1024]{1,0:T(8,128)S(1)}, u32[]{:S(2)}, u32[]{:S(2)}) %collective-permute-start.39) | collective-permute-done | bytes 163872 | tf_op jit(solution)/shard_map/ppermute | solution.py:284
  557.4 4.8 collective-permute-done.41
  563.5 3.9 collective-permute-done.43
  567.5 8.3 %collective-permute-done.31 = f32[3,32,1024]{2,1,0:T(8,128)S(1)} collective-permute-done((f32[3,32,1024]{2,1,0:T(8,128)S(1)}, f32[3,32,1024]{2,1,0:T(8,128)S(1)}, u32[]{:S(2)}, u32[]{:S(2)}) %collective-permute-start.31) | collective-permute-done | bytes 393248 | tf_op jit(solution)/shard_map/ppermute | solution.py:287
  575.9 4.2 collective-permute-done.33
  580.2 9.3 %pair_dots.1 = f32[32,136,128]{2,1,0:T(8,128)S(1)} custom-call(s32[2,6,32]{2,1,0:T(8,128)S(1)} %pad_add_fusion.ids, f32[4,3,32,1024]{3,2,1,0:T(8,128)S(1)} %pad_maximum_fusion.3.early, f32[4,40,1024]{2,1,0:T(8,128)S(1)} %pad_maximum_fusion.4.late), custom_call_target="tpu_custom_call" | custom-call | tf_op jit(solution)/shard_map/pair_dots/pallas_call | solution.py:240
  589.7 2.9 collective-permute-done.44
  594.0 2.6 collective-permute-start.45
  596.6 12.9 %collective-permute-done.45 = f32[1,2,1,4,136,128]{5,4,3,2,1,0:T(8,128)S(1)} collective-permute-done((f32[1,2,1,4,136,128]{5,4,3,2,1,0:T(8,128)S(1)}, f32[1,2,1,4,136,128]{5,4,3,2,1,0:T(8,128)S(1)}, u32[]{:S(2)}, u32[]{:S(2)}) %collective-permute-start.45) | collective-permute-done | bytes 557088 | tf_op jit(solution)/shard_map/ppermute | solution.py:264
  609.9 8.0 %collective-permute-done.46 = f32[1,1,1,4,136,128]{5,4,3,2,1,0:T(8,128)S(1)} collective-permute-done((f32[1,1,1,4,136,128]{5,4,3,2,1,0:T(8,128)S(1)}, f32[1,1,1,4,136,128]{5,4,3,2,1,0:T(8,128)S(1)}, u32[]{:S(2)}, u32[]{:S(2)}) %collective-permute-start.46) | collective-permute-done | bytes 278560 | tf_op jit(solution)/shard_map/ppermute | solution.py:264
  (187 shorter events, 56.4 us)
Async XLA Ops:
  6.5 13.5 %collective-permute-start = (s32[16,2]{0,1:T(2,128)}, s32[16,2]{0,1:T(2,128)S(1)}, u32[]{:S(2)}, u32[]{:S(2)}) collective-permute-start(s32[16,2]{0,1:T(2,128)} %param.12), channel_id=1, source_target_pairs={{0,4},{4,0},{1,5},{5,1},{2,6},{6,2},{3,7},{7,3},{8,12},{12,8},{9,1... | collective-permute-start | bytes 392 | tf_op jit(solution)/shard_map/ppermute | solution.py:368
  10.2 5.4 collective-permute-start.1
  15.0 24.5 %collective-permute-start.3 = (bf16[4096,128]{1,0:T(8,128)(2,1)S(1)}, bf16[4096,128]{1,0:T(8,128)(2,1)S(1)}, u32[]{:S(2)}, u32[]{:S(2)}) collective-permute-start(bf16[4096,128]{1,0:T(8,128)(2,1)S(1)} %constant_dynamic-slice_fusion.16), channel_id=1, source_target_pairs={{0,4},{4,0},{1,5},{5,1},{2,6},{6,2},{3,7},{7,3},{8,12},{12,8},{9,1... | collective-permute-start | bytes 3145736 | tf_op jit(solution)/shard_map/ppermute | solution.py:279
  15.6 23.9 %collective-permute-start.2 = (s32[2,4,128]{2,1,0:T(4,128)S(1)}, s32[2,4,128]{2,1,0:T(4,128)S(1)}, u32[]{:S(2)}, u32[]{:S(2)}) collective-permute-start(s32[2,4,128]{2,1,0:T(4,128)S(1)} %get-tuple-element.139), channel_id=1, source_target_pairs={{0,4},{4,0},{1,5},{5,1},{2,6},{6,2},{3,7},{7,3},{8,12},{12,8},{9,1... | collective-permute-start | bytes 12296 | tf_op jit(solution)/shard_map/ppermute | solution.py:367
  39.5 43.4 %collective-permute-start.4 = (bf16[7680,128]{1,0:T(8,128)(2,1)}, bf16[7680,128]{1,0:T(8,128)(2,1)}, u32[]{:S(2)}, u32[]{:S(2)}) collective-permute-start(bf16[7680,128]{1,0:T(8,128)(2,1)} %constant_dynamic-slice_fusion.14), channel_id=1, source_target_pairs={{0,4},{4,0},{1,5},{5,1},{2,6},{6,2},{3,7},{7,3},{8,12},{12,8},{9,1... | collective-permute-start | bytes 5898248 | tf_op jit(solution)/shard_map/ppermute | solution.py:279
  41.9 43.9 %copy-start.1 = (bf16[4096,256]{1,0:T(8,128)(2,1)}, bf16[4096,256]{1,0:T(8,128)(2,1)S(1)}, u32[]{:S(2)}) copy-start(bf16[4096,256]{1,0:T(8,128)(2,1)S(1)} %pad_maximum_fusion.2.refs_2_) | copy-start | bytes 6291460
  41.9 48.8 %collective-permute-start.7 = (bf16[4096,256]{1,0:T(8,128)(2,1)S(1)}, bf16[4096,256]{1,0:T(8,128)(2,1)}, u32[]{:S(2)}, u32[]{:S(2)}) collective-permute-start(bf16[4096,256]{1,0:T(8,128)(2,1)S(1)} %pad_maximum_fusion.2.refs_2_), channel_id=1, source_target_pairs={{0,8},{8,0},{16,24},{24,16},{1,9},{9,1},{17,25},{25,17},{2,10},{10... | collective-permute-start | bytes 6291464 | tf_op jit(solution)/shard_map/ppermute | solution.py:279
  42.0 46.1 %collective-permute-start.8 = (bf16[4096,256]{1,0:T(8,128)(2,1)S(1)}, bf16[4096,256]{1,0:T(8,128)(2,1)}, u32[]{:S(2)}, u32[]{:S(2)}) collective-permute-start(bf16[4096,256]{1,0:T(8,128)(2,1)S(1)} %pad_maximum_fusion.2.refs_2_), channel_id=1, source_target_pairs={{8,16},{16,8},{9,17},{17,9},{10,18},{18,10},{11,19},{19,11},{12,20... | collective-permute-start | bytes 6291464 | tf_op jit(solution)/shard_map/ppermute | solution.py:279
  88.1 35.6 %collective-permute-start.14 = (bf16[7680,256]{1,0:T(8,128)(2,1)}, bf16[7680,256]{1,0:T(8,128)(2,1)}, u32[]{:S(2)}, u32[]{:S(2)}) collective-permute-start(bf16[7680,256]{1,0:T(8,128)(2,1)} %pad_maximum_fusion.refs_1_), channel_id=1, source_target_pairs={{8,16},{16,8},{9,17},{17,9},{10,18},{18,10},{11,19},{19,11},{12,20... | collective-permute-start | bytes 11796488 | tf_op jit(solution)/shard_map/ppermute | solution.py:279
  90.7 86.2 %collective-permute-start.9 = (bf16[7680,256]{1,0:T(8,128)(2,1)}, bf16[7680,256]{1,0:T(8,128)(2,1)}, u32[]{:S(2)}, u32[]{:S(2)}) collective-permute-start(bf16[7680,256]{1,0:T(8,128)(2,1)} %pad_maximum_fusion.refs_1_), channel_id=1, source_target_pairs={{0,8},{8,0},{16,24},{24,16},{1,9},{9,1},{17,25},{25,17},{2,10},{10... | collective-permute-start | bytes 11796488 | tf_op jit(solution)/shard_map/ppermute | solution.py:279
  96.2 26.0 %collective-permute-start.5 = (bf16[4608,128]{1,0:T(8,128)(2,1)S(1)}, bf16[4608,128]{1,0:T(8,128)(2,1)}, u32[]{:S(2)}, u32[]{:S(2)}) collective-permute-start(bf16[4608,128]{1,0:T(8,128)(2,1)S(1)} %constant_dynamic-slice_fusion.15), channel_id=1, source_target_pairs={{0,4},{4,0},{1,5},{5,1},{2,6},{6,2},{3,7},{7,3},{8,12},{12,8},{9,1... | collective-permute-start | bytes 3538952 | tf_op jit(solution)/shard_map/ppermute | solution.py:279
  122.2 66.9 %collective-permute-start.6 = (bf16[94,128,128]{2,1,0:T(8,128)(2,1)}, bf16[94,128,128]{2,1,0:T(8,128)(2,1)S(1)}, u32[]{:S(2)}, u32[]{:S(2)}) collective-permute-start(bf16[94,128,128]{2,1,0:T(8,128)(2,1)} %pack_tiles.4), channel_id=1, source_target_pairs={{0,4},{4,0},{1,5},{5,1},{2,6},{6,2},{3,7},{7,3},{8,12},{12,8},{9,1... | collective-permute-start | bytes 9240584 | tf_op jit(solution)/shard_map/ppermute | solution.py:279
  123.7 74.3 %collective-permute-start.15 = (bf16[4096,256]{1,0:T(8,128)(2,1)}, bf16[4096,256]{1,0:T(8,128)(2,1)}, u32[]{:S(2)}, u32[]{:S(2)}) collective-permute-start(bf16[4096,256]{1,0:T(8,128)(2,1)} %collective-permute-done.7.refs_3_), channel_id=1, source_target_pairs={{8,16},{16,8},{9,17},{17,9},{10,18},{18,10},{11,19},{19,11},{12,20... | collective-permute-start | bytes 6291464 | tf_op jit(solution)/shard_map/ppermute | solution.py:279
  176.9 47.0 %collective-permute-start.10 = (bf16[4096,256]{1,0:T(8,128)(2,1)}, bf16[4096,256]{1,0:T(8,128)(2,1)}, u32[]{:S(2)}, u32[]{:S(2)}) collective-permute-start(bf16[4096,256]{1,0:T(8,128)(2,1)} %collective-permute-done.8.refs_4_), channel_id=1, source_target_pairs={{8,0},{16,24},{9,1},{17,25},{10,2},{18,26},{11,3},{19,27},{12,4},{... | collective-permute-start | bytes 6291464 | tf_op jit(solution)/shard_map/ppermute | solution.py:279
  189.0 73.9 %collective-permute-start.11 = (bf16[104,128,128]{2,1,0:T(8,128)(2,1)}, bf16[104,128,128]{2,1,0:T(8,128)(2,1)}, u32[]{:S(2)}, u32[]{:S(2)}) collective-permute-start(bf16[104,128,128]{2,1,0:T(8,128)(2,1)} %pack_tiles.5), channel_id=1, source_target_pairs={{0,4},{4,0},{1,5},{5,1},{2,6},{6,2},{3,7},{7,3},{8,12},{12,8},{9,1... | collective-permute-start | bytes 10223624 | tf_op jit(solution)/shard_map/ppermute | solution.py:279
  195.0 71.2 %collective-permute-start.12 = (bf16[104,128,128]{2,1,0:T(8,128)(2,1)}, bf16[104,128,128]{2,1,0:T(8,128)(2,1)}, u32[]{:S(2)}, u32[]{:S(2)}) collective-permute-start(bf16[104,128,128]{2,1,0:T(8,128)(2,1)} %pack_tiles.6), channel_id=1, source_target_pairs={{0,8},{24,16},{1,9},{25,17},{2,10},{26,18},{3,11},{27,19},{4,12},{... | collective-permute-start | bytes 10223624 | tf_op jit(solution)/shard_map/ppermute | solution.py:279
  198.0 73.6 %collective-permute-start.16 = (bf16[7680,256]{1,0:T(8,128)(2,1)}, bf16[7680,256]{1,0:T(8,128)(2,1)}, u32[]{:S(2)}, u32[]{:S(2)}) collective-permute-start(bf16[7680,256]{1,0:T(8,128)(2,1)} %collective-permute-done.9.refs_2_), channel_id=1, source_target_pairs={{8,16},{16,8},{9,17},{17,9},{10,18},{18,10},{11,19},{19,11},{12,20... | collective-permute-start | bytes 11796488 | tf_op jit(solution)/shard_map/ppermute | solution.py:279
  223.9 84.2 %collective-permute-start.20 = (bf16[7680,256]{1,0:T(8,128)(2,1)}, bf16[7680,256]{1,0:T(8,128)(2,1)}, u32[]{:S(2)}, u32[]{:S(2)}) collective-permute-start(bf16[7680,256]{1,0:T(8,128)(2,1)} %collective-permute-done.14.refs_3_), channel_id=1, source_target_pairs={{8,0},{16,24},{9,1},{17,25},{10,2},{18,26},{11,3},{19,27},{12,4},{... | collective-permute-start | bytes 11796488 | tf_op jit(solution)/shard_map/ppermute | solution.py:279
  262.9 109.0 %collective-permute-start.19 = (bf16[160,128,128]{2,1,0:T(8,128)(2,1)}, bf16[160,128,128]{2,1,0:T(8,128)(2,1)}, u32[]{:S(2)}, u32[]{:S(2)}) collective-permute-start(bf16[160,128,128]{2,1,0:T(8,128)(2,1)} %pack_tiles.7), channel_id=1, source_target_pairs={{0,4},{4,0},{1,5},{5,1},{2,6},{6,2},{3,7},{7,3},{8,12},{12,8},{9,1... | collective-permute-start | bytes 15728648 | tf_op jit(solution)/shard_map/ppermute | solution.py:279
  266.1 49.0 %collective-permute-start.13 = (bf16[4608,256]{1,0:T(8,128)(2,1)}, bf16[4608,256]{1,0:T(8,128)(2,1)}, u32[]{:S(2)}, u32[]{:S(2)}) collective-permute-start(bf16[4608,256]{1,0:T(8,128)(2,1)} %pad_maximum_fusion.1.refs_2_.refs_1_), channel_id=1, source_target_pairs={{0,8},{24,16},{1,9},{25,17},{2,10},{26,18},{3,11},{27,19},{4,12},{... | collective-permute-start | bytes 7077896 | tf_op jit(solution)/shard_map/ppermute | solution.py:279
  271.6 54.2 %collective-permute-start.17 = (bf16[4608,256]{1,0:T(8,128)(2,1)}, bf16[4608,256]{1,0:T(8,128)(2,1)}, u32[]{:S(2)}, u32[]{:S(2)}) collective-permute-start(bf16[4608,256]{1,0:T(8,128)(2,1)} %pad_maximum_fusion.1.refs_2_.refs_1_), channel_id=1, source_target_pairs={{8,16},{16,8},{9,17},{17,9},{10,18},{18,10},{11,19},{19,11},{12,20... | collective-permute-start | bytes 7077896 | tf_op jit(solution)/shard_map/ppermute | solution.py:279
  308.0 89.5 %collective-permute-start.34 = (bf16[7680,256]{1,0:T(8,128)(2,1)}, bf16[7680,256]{1,0:T(8,128)(2,1)}, u32[]{:S(2)}, u32[]{:S(2)}) collective-permute-start(bf16[7680,256]{1,0:T(8,128)(2,1)} %collective-permute-done.16.refs_2_), channel_id=1, source_target_pairs={{8,0},{16,24},{9,1},{17,25},{10,2},{18,26},{11,3},{19,27},{12,4},{... | collective-permute-start | bytes 11796488 | tf_op jit(solution)/shard_map/ppermute | solution.py:279
  315.1 93.3 %collective-permute-start.24 = (bf16[104,128,128]{2,1,0:T(8,128)(2,1)}, bf16[104,128,128]{2,1,0:T(8,128)(2,1)}, u32[]{:S(2)}, u32[]{:S(2)}) collective-permute-start(bf16[104,128,128]{2,1,0:T(8,128)(2,1)} %collective-permute-done.11.refs_1_), channel_id=1, source_target_pairs={{0,8},{24,16},{1,9},{25,17},{2,10},{26,18},{3,11},{27,19},{4,12},{... | collective-permute-start | bytes 10223624 | tf_op jit(solution)/shard_map/ppermute | solution.py:279
  325.7 73.0 %collective-permute-start.18 = (bf16[4608,256]{1,0:T(8,128)(2,1)}, bf16[4608,256]{1,0:T(8,128)(2,1)}, u32[]{:S(2)}, u32[]{:S(2)}) collective-permute-start(bf16[4608,256]{1,0:T(8,128)(2,1)} %collective-permute-done.13.refs_3_), channel_id=1, source_target_pairs={{8,16},{16,8},{9,17},{17,9},{10,18},{18,10},{11,19},{19,11},{12,20... | collective-permute-start | bytes 7077896 | tf_op jit(solution)/shard_map/ppermute | solution.py:279
  329.1 1.6 copy-start.2
  397.5 60.9 %collective-permute-start.35 = (bf16[4096,256]{1,0:T(8,128)(2,1)}, bf16[4096,256]{1,0:T(8,128)(2,1)}, u32[]{:S(2)}, u32[]{:S(2)}) collective-permute-start(bf16[4096,256]{1,0:T(8,128)(2,1)} %collective-permute-done.15.refs_2_), channel_id=1, source_target_pairs={{8,0},{16,24},{9,1},{17,25},{10,2},{18,26},{11,3},{19,27},{12,4},{... | collective-permute-start | bytes 6291464 | tf_op jit(solution)/shard_map/ppermute | solution.py:279
  418.4 1.6 copy-start.4
  418.5 2.2 copy-start.6
  420.7 50.3 %collective-permute-start.25 = (f32[3,128,1024]{2,1,0:T(8,128)}, f32[3,128,1024]{2,1,0:T(8,128)}, u32[]{:S(2)}, u32[]{:S(2)}) collective-permute-start(f32[3,128,1024]{2,1,0:T(8,128)} %fusion.5), channel_id=1, source_target_pairs={{0,1},{1,0},{2,3},{3,2},{4,5},{5,4},{6,7},{7,6},{8,9},{9,8},{10,11... | collective-permute-start | bytes 4718600 | tf_op jit(solution)/shard_map/ppermute | solution.py:264
  438.8 2.3 copy-start
  441.1 2.1 copy-start.8
  441.1 2.1 copy-start.3
  442.5 32.8 %collective-permute-start.21 = (f32[3,128,1024]{2,1,0:T(8,128)}, f32[3,128,1024]{2,1,0:T(8,128)}, u32[]{:S(2)}, u32[]{:S(2)}) collective-permute-start(f32[3,128,1024]{2,1,0:T(8,128)} %constant_dynamic-slice_fusion.12), channel_id=1, source_target_pairs={{0,1},{1,0},{2,3},{3,2},{4,5},{5,4},{6,7},{7,6},{8,9},{9,8},{10,11... | collective-permute-start | bytes 4718600 | tf_op jit(solution)/shard_map/ppermute | solution.py:264
  467.7 3.2 copy-start.5
  467.8 3.2 copy-start.7
  470.3 8.9 %collective-permute-start.36 = (f32[1,128,1024]{2,1,0:T(8,128)}, f32[1,128,1024]{2,1,0:T(8,128)}, u32[]{:S(2)}, u32[]{:S(2)}) collective-permute-start(f32[1,128,1024]{2,1,0:T(8,128)} %constant_dynamic-slice_fusion.7), channel_id=1, source_target_pairs={{0,1},{1,0},{2,3},{3,2},{4,5},{5,4},{6,7},{7,6},{8,9},{9,8},{10,11... | collective-permute-start | bytes 1572872 | tf_op jit(solution)/shard_map/ppermute | solution.py:264
  471.0 4.3 copy-start.9
  472.8 4.2 copy-start.10
  473.9 4.7 copy-start.14
  473.9 20.7 %collective-permute-start.26 = (f32[3,64,1024]{2,1,0:T(8,128)}, f32[3,64,1024]{2,1,0:T(8,128)}, u32[]{:S(2)}, u32[]{:S(2)}) collective-permute-start(f32[3,64,1024]{2,1,0:T(8,128)} %constant_dynamic-slice_fusion.9), channel_id=1, source_target_pairs={{0,4},{4,0},{1,5},{5,1},{2,6},{6,2},{3,7},{7,3},{8,12},{12,8},{9,1... | collective-permute-start | bytes 2359304 | tf_op jit(solution)/shard_map/ppermute | solution.py:264
  477.9 33.5 %collective-permute-start.22 = (f32[3,64,1024]{2,1,0:T(8,128)}, f32[3,64,1024]{2,1,0:T(8,128)}, u32[]{:S(2)}, u32[]{:S(2)}) collective-permute-start(f32[3,64,1024]{2,1,0:T(8,128)} %constant_dynamic-slice_fusion.11), channel_id=1, source_target_pairs={{0,4},{4,0},{1,5},{5,1},{2,6},{6,2},{3,7},{7,3},{8,12},{12,8},{9,1... | collective-permute-start | bytes 2359304 | tf_op jit(solution)/shard_map/ppermute | solution.py:264
  479.2 15.4 %copy-start.11 = (f32[3,128,1024]{2,1,0:T(8,128)S(1)}, f32[3,128,1024]{2,1,0:T(8,128)}, u32[]{:S(2)}) copy-start(f32[3,128,1024]{2,1,0:T(8,128)} %copy-done.10) | copy-start | bytes 4718596
  495.9 18.2 %collective-permute-start.27 = (f32[3,32,1024]{2,1,0:T(8,128)S(1)}, f32[3,32,1024]{2,1,0:T(8,128)S(1)}, u32[]{:S(2)}, u32[]{:S(2)}) collective-permute-start(f32[3,32,1024]{2,1,0:T(8,128)S(1)} %constant_dynamic-slice_fusion.8), channel_id=1, source_target_pairs={{0,2},{2,0},{1,3},{3,1},{4,6},{6,4},{5,7},{7,5},{8,10},{10,8},{9,1... | collective-permute-start | bytes 1179656 | tf_op jit(solution)/shard_map/ppermute | solution.py:264
  497.3 18.7 %collective-permute-start.37 = (f32[1,64,1024]{2,1,0:T(8,128)S(1)}, f32[1,64,1024]{2,1,0:T(8,128)S(1)}, u32[]{:S(2)}, u32[]{:S(2)}) collective-permute-start(f32[1,64,1024]{2,1,0:T(8,128)S(1)} %constant_dynamic-slice_fusion.6), channel_id=1, source_target_pairs={{0,4},{4,0},{1,5},{5,1},{2,6},{6,2},{3,7},{7,3},{8,12},{12,8},{9,1... | collective-permute-start | bytes 786440 | tf_op jit(solution)/shard_map/ppermute | solution.py:264
  512.7 10.7 %collective-permute-start.23 = (f32[3,32,1024]{2,1,0:T(8,128)S(1)}, f32[3,32,1024]{2,1,0:T(8,128)S(1)}, u32[]{:S(2)}, u32[]{:S(2)}) collective-permute-start(f32[3,32,1024]{2,1,0:T(8,128)S(1)} %constant_dynamic-slice_fusion.10), channel_id=1, source_target_pairs={{0,2},{2,0},{1,3},{3,1},{4,6},{6,4},{5,7},{7,5},{8,10},{10,8},{9,1... | collective-permute-start | bytes 1179656 | tf_op jit(solution)/shard_map/ppermute | solution.py:264
  514.2 23.9 %collective-permute-start.28 = (f32[3,32,1024]{2,1,0:T(8,128)S(1)}, f32[3,32,1024]{2,1,0:T(8,128)S(1)}, u32[]{:S(2)}, u32[]{:S(2)}) collective-permute-start(f32[3,32,1024]{2,1,0:T(8,128)S(1)} %dynamic-slice_add_fusion.6), channel_id=1, source_target_pairs={{8,0},{16,24},{9,1},{17,25},{10,2},{18,26},{11,3},{19,27},{12,4},{... | collective-permute-start | bytes 1179656 | tf_op jit(solution)/shard_map/ppermute | solution.py:427
  516.1 23.2 %collective-permute-start.38 = (f32[1,32,1024]{2,1,0:T(8,128)S(1)}, f32[1,32,1024]{2,1,0:T(8,128)S(1)}, u32[]{:S(2)}, u32[]{:S(2)}) collective-permute-start(f32[1,32,1024]{2,1,0:T(8,128)S(1)} %constant_dynamic-slice_fusion.5), channel_id=1, source_target_pairs={{0,2},{2,0},{1,3},{3,1},{4,6},{6,4},{5,7},{7,5},{8,10},{10,8},{9,1... | collective-permute-start | bytes 393224 | tf_op jit(solution)/shard_map/ppermute | solution.py:264
  538.1 14.4 %collective-permute-start.29 = (f32[3,32,1024]{2,1,0:T(8,128)S(1)}, f32[3,32,1024]{2,1,0:T(8,128)S(1)}, u32[]{:S(2)}, u32[]{:S(2)}) collective-permute-start(f32[3,32,1024]{2,1,0:T(8,128)S(1)} %fusion.9), channel_id=1, source_target_pairs={{0,8},{8,0},{16,24},{24,16},{1,9},{9,1},{17,25},{25,17},{2,10},{10... | collective-permute-start | bytes 1179656 | tf_op jit(solution)/shard_map/ppermute | solution.py:284
  538.6 17.5 %collective-permute-start.30 = (f32[3,32,1024]{2,1,0:T(8,128)S(1)}, f32[3,32,1024]{2,1,0:T(8,128)S(1)}, u32[]{:S(2)}, u32[]{:S(2)}) collective-permute-start(f32[3,32,1024]{2,1,0:T(8,128)S(1)} %fusion.9), channel_id=1, source_target_pairs={{8,16},{16,8},{9,17},{17,9},{10,18},{18,10},{11,19},{19,11},{12,20... | collective-permute-start | bytes 1179656 | tf_op jit(solution)/shard_map/ppermute | solution.py:285
  539.4 11.1 %collective-permute-start.39 = (f32[40,1024]{1,0:T(8,128)S(1)}, f32[40,1024]{1,0:T(8,128)S(1)}, u32[]{:S(2)}, u32[]{:S(2)}) collective-permute-start(f32[40,1024]{1,0:T(8,128)S(1)} %get-tuple-element.138), channel_id=1, source_target_pairs={{0,8},{8,0},{16,24},{24,16},{1,9},{9,1},{17,25},{25,17},{2,10},{10... | collective-permute-start | bytes 491528 | tf_op jit(solution)/shard_map/ppermute | solution.py:284
  542.3 8.8 %collective-permute-start.40 = (f32[40,1024]{1,0:T(8,128)S(1)}, f32[40,1024]{1,0:T(8,128)S(1)}, u32[]{:S(2)}, u32[]{:S(2)}) collective-permute-start(f32[40,1024]{1,0:T(8,128)S(1)} %get-tuple-element.138), channel_id=1, source_target_pairs={{8,16},{16,8},{9,17},{17,9},{10,18},{18,10},{11,19},{19,11},{12,20... | collective-permute-start | bytes 491528 | tf_op jit(solution)/shard_map/ppermute | solution.py:285
  550.5 4.3 collective-permute-start.42
  551.2 11.0 %collective-permute-start.41 = (f32[40,1024]{1,0:T(8,128)S(1)}, f32[40,1024]{1,0:T(8,128)S(1)}, u32[]{:S(2)}, u32[]{:S(2)}) collective-permute-start(f32[40,1024]{1,0:T(8,128)S(1)} %collective-permute-done.40), channel_id=1, source_target_pairs={{8,0},{16,24},{9,1},{17,25},{10,2},{18,26},{11,3},{19,27},{12,4},{... | collective-permute-start | bytes 491528 | tf_op jit(solution)/shard_map/ppermute | solution.py:287
  552.5 9.7 %collective-permute-start.32 = (f32[3,32,1024]{2,1,0:T(8,128)S(1)}, f32[3,32,1024]{2,1,0:T(8,128)S(1)}, u32[]{:S(2)}, u32[]{:S(2)}) collective-permute-start(f32[3,32,1024]{2,1,0:T(8,128)S(1)} %collective-permute-done.29), channel_id=1, source_target_pairs={{8,16},{16,8},{9,17},{17,9},{10,18},{18,10},{11,19},{19,11},{12,20... | collective-permute-start | bytes 1179656 | tf_op jit(solution)/shard_map/ppermute | solution.py:286
  554.8 12.6 %collective-permute-start.43 = (f32[40,1024]{1,0:T(8,128)S(1)}, f32[40,1024]{1,0:T(8,128)S(1)}, u32[]{:S(2)}, u32[]{:S(2)}) collective-permute-start(f32[40,1024]{1,0:T(8,128)S(1)} %collective-permute-done.42), channel_id=1, source_target_pairs={{8,0},{16,24},{9,1},{17,25},{10,2},{18,26},{11,3},{19,27},{12,4},{... | collective-permute-start | bytes 491528 | tf_op jit(solution)/shard_map/ppermute | solution.py:288
  556.1 19.7 %collective-permute-start.31 = (f32[3,32,1024]{2,1,0:T(8,128)S(1)}, f32[3,32,1024]{2,1,0:T(8,128)S(1)}, u32[]{:S(2)}, u32[]{:S(2)}) collective-permute-start(f32[3,32,1024]{2,1,0:T(8,128)S(1)} %collective-permute-done.30), channel_id=1, source_target_pairs={{8,0},{16,24},{9,1},{17,25},{10,2},{18,26},{11,3},{19,27},{12,4},{... | collective-permute-start | bytes 1179656 | tf_op jit(solution)/shard_map/ppermute | solution.py:287
  562.2 17.8 %collective-permute-start.33 = (f32[3,32,1024]{2,1,0:T(8,128)S(1)}, f32[3,32,1024]{2,1,0:T(8,128)S(1)}, u32[]{:S(2)}, u32[]{:S(2)}) collective-permute-start(f32[3,32,1024]{2,1,0:T(8,128)S(1)} %collective-permute-done.32), channel_id=1, source_target_pairs={{8,0},{16,24},{9,1},{17,25},{10,2},{18,26},{11,3},{19,27},{12,4},{... | collective-permute-start | bytes 1179656 | tf_op jit(solution)/shard_map/ppermute | solution.py:288
  589.6 3.0 collective-permute-start.44
  594.0 15.6 %collective-permute-start.45 = (f32[1,2,1,4,136,128]{5,4,3,2,1,0:T(8,128)S(1)}, f32[1,2,1,4,136,128]{5,4,3,2,1,0:T(8,128)S(1)}, u32[]{:S(2)}, u32[]{:S(2)}) collective-permute-start(f32[1,2,1,4,136,128]{5,4,3,2,1,0:T(8,128)S(1)} %constant_dynamic-slice_fusion.3), channel_id=1, source_target_pairs={{0,4},{4,0},{1,5},{5,1},{2,6},{6,2},{3,7},{7,3},{8,12},{12,8},{9,1... | collective-permute-start | bytes 1671176 | tf_op jit(solution)/shard_map/ppermute | solution.py:264
  609.6 8.3 %collective-permute-start.46 = (f32[1,1,1,4,136,128]{5,4,3,2,1,0:T(8,128)S(1)}, f32[1,1,1,4,136,128]{5,4,3,2,1,0:T(8,128)S(1)}, u32[]{:S(2)}, u32[]{:S(2)}) collective-permute-start(f32[1,1,1,4,136,128]{5,4,3,2,1,0:T(8,128)S(1)} %constant_dynamic-slice_fusion.2), channel_id=1, source_target_pairs={{0,2},{2,0},{1,3},{3,1},{4,6},{6,4},{5,7},{7,5},{8,10},{10,8},{9,1... | collective-permute-start | bytes 835592 | tf_op jit(solution)/shard_map/ppermute | solution.py:264
  619.3 0.7 copy-start.13

commit v9 on v8

--- a/solution.py
+++ b/solution.py
@@ -86,11 +86,17 @@
     for two in paired:
         planes.append(refs[at : at + 1 + two])
         at += 1 + two
-    out, total, tiles, held, tile_sem, held_sem = refs[at:]
+    out, total, tiles, held, tile_sem, held_sem, own_sem = refs[at:]
     rows = row_blocks * blk
     depth = STRIDE * blk
     inner, base = info[0] != 0, info[1]
     per_source = steps * STRIDE * row_blocks
+
+    def present(k, column, b):
+        return info[2 + count + k * per_source + column * row_blocks + b] != 0
+
+    def own_block(k, slot):
+        return tiles.at[slot, pl.ds(k * rows, rows)]
 
     def fetch(i, slot, used, active):
         first = pl.multiple_of(i * depth, depth)
@@ -108,23 +114,27 @@
         following = []
         for k in range(count):
             mine = used[k]
+            if slots[k] is None:
+                start = pl.multiple_of((base + i * STRIDE) * blk, blk)
+
+                @pl.when(active)
+                def _():
+                    pltpu.make_async_copy(
+                        sources[k].at[:, pl.ds(start, depth)], own_block(k, slot), own_sem.at[slot]
+                    ).start()
+
+                following.append(mine)
+                continue
             for j in range(STRIDE):
                 column = i * STRIDE + j
-                start = pl.multiple_of((base + column) * blk, blk)
                 for b in range(row_blocks):
-                    there = info[2 + count + k * per_source + column * row_blocks + b] != 0
-                    there = jnp.logical_and(there, active)
-                    if slots[k] is not None:
-                        there = jnp.logical_and(there, mine < slots[k])
+                    there = present(k, column, b)
+                    there = jnp.logical_and(there, jnp.logical_and(active, mine < slots[k]))
                     place = (pl.ds(k * rows + b * blk, blk), pl.ds(j * blk, blk))
 
                     @pl.when(there)
                     def _():
-                        if slots[k] is None:
-                            tile = sources[k].at[pl.ds(b * blk, blk), pl.ds(start, blk)]
-                        else:
-                            tile = sources[k].at[mine]
-                        pltpu.make_async_copy(tile, tiles.at[(slot,) + place], tile_sem.at[slot]).start()
+                        pltpu.make_async_copy(sources[k].at[mine], tiles.at[(slot,) + place], tile_sem.at[slot]).start()
 
                     @pl.when(jnp.logical_not(there))
                     def _():
@@ -151,6 +161,17 @@
             return nothing
 
         lax.fori_loop(0, started, one_wait, 0)
+        for k in range(count):
+            if slots[k] is None:
+                pltpu.make_async_copy(own_block(k, slot), own_block(k, slot), own_sem.at[slot]).wait()
+                for j in range(STRIDE):
+                    for b in range(row_blocks):
+
+                        @pl.when(jnp.logical_not(present(k, i * STRIDE + j, b)))
+                        def _():
+                            place = (slot, pl.ds(k * rows + b * blk, blk), pl.ds(j * blk, blk))
+                            tiles[place] = jnp.zeros((blk, blk), tiles.dtype)
+
         for g in range(groups):
             pltpu.make_async_copy(held.at[slot, g], held.at[slot, g], held_sem.at[slot]).wait()
         for k in range(count):
@@ -197,6 +218,7 @@
             pltpu.VMEM((2, len(planes), STRIDE * blk, wide), dtype),
             pltpu.SemaphoreType.DMA((2,)),
             pltpu.SemaphoreType.DMA((2,)),
+            pltpu.SemaphoreType.DMA((2,)),
         ],
         compiler_params=params(vmem_limit_bytes=32 << 20),
         cost_estimate=pl.CostEstimate(flops=flops, bytes_accessed=size, transcendentals=0),
@@ -389,7 +411,7 @@
     near += inward.send([groups[2]], "z", [INWARD])
     mid += middle.send([groups[2]], "z", [MIDDLE])
     far += middle.send([near[2]], "z", [MIDDLE])
-    outer = [outward.send([v], "z", [OUTWARD])[0] for v in (mid[0], mid[1], far[1], far[0])]
+    outer = [outward.send([v], "z", [OUTWARD])[0] for v in mid[:2]]
     loans = loans + inward.send(tiles[2], "z", [INWARD] * len(others))
     over = jnp.int32(0)
     for c in range(3):
@@ -398,7 +420,6 @@
             over = jnp.maximum(over, (count > slots[c]).astype(jnp.int32))
     row_places = [(x - k) % wide * rows for k in range(wide)]
     early_groups = [[[groups[c]], [near[c]], [mid[c], outer[c]]] for c in range(2)]
-    last_group = [[[far[c], outer[3 - c]]] for c in range(2)]
 
     def times(c, sources, which, held, places):
         own = [masks[k][:, cuts[c] : cuts[c + 1]] for k in which]
@@ -406,16 +427,24 @@
 
     every = range(wide)
     part0 = times(0, [hist] + tiles[0], every, early_groups[0], row_places)
-    part2 = times(2, [hist] + tiles[2], every, [[groups[2]], [near[2]], [mid[2]], [far[2]]], row_places)
-    part1 = [times(1, [([hist] + tiles[1])[k]], [k], early_groups[1], [0]) for k in every]
-    first_three = part0 + part2[:3] + in_row_order(part1, 2)
-    end1 = times(1, [hist] + tiles[1], every, last_group[1], row_places)
-    end0 = times(0, [hist] + tiles[0], every, last_group[0], row_places)
-    last_one = end0 + (end1 + part2[3:])
+    outer += outward.send([after(far[1], part0)], "z", [OUTWARD])
+    part1 = [times(1, [hist], [0], early_groups[1], [0])]
+    part2 = times(2, [hist] + tiles[2], every, [[groups[2]], [near[2]], [mid[2]]], row_places)
+    guest = product([loans[0]], [guest_masks[0]], [[groups[2]], [mid[2]]], inner, 0, [0])
+    outer += outward.send([after(far[0], [part1[0], part2, guest])], "z", [OUTWARD])
+    part1 += [times(1, [tiles[1][k - 1]], [k], early_groups[1], [0]) for k in range(1, wide)]
+    first_three = part0 + part2 + in_row_order(part1, 2)
+
+    end2 = times(2, [hist] + tiles[2], every, [[far[2]]], row_places)
+    end1 = times(1, [hist] + tiles[1], every, [[far[1], outer[2]]], row_places)
+    end0 = times(0, [hist] + tiles[0], every, [[far[0], outer[3]]], row_places)
+    last_one = end0 + (end1 + end2)
+    guest = jnp.concatenate([guest, product([loans[0]], [guest_masks[0]], [[far[2]]], inner, 0, [0])])
     visitors = in_row_order(
-        [
+        [guest]
+        + [
             product([t], [m], [[groups[2]], [mid[2]], [far[2]]], inner, 0, [0])
-            for t, m in zip(loans, guest_masks)
+            for t, m in zip(loans[1:], guest_masks[1:])
         ],
         2,
     )

time: 629 us -> 607 us (0.965)
  waiting for transfers between devices: 345 us -> 309 us
  Pallas kernels: 133 us -> 147 us
    ppermute x21, waiting for transfers between devices: 225 us -> 205 us  [send(): lax.ppermute(v, axis, route)]
    pallas_call x8 -> x10, Pallas kernels: 106 us -> 120 us  [product(): pl.pallas_call(functools.partial(product_kernel, blk, row_blocks, columns...]
    ppermute x1, waiting for transfers between devices: 14.6 us -> 4.08 us  [body(): visitors = lax.ppermute(summed(visitors), 'z', OUTWARD)]
  transfers between devices with their start and end apart: 47 -> 47, of which waited for: 24 -> 22; matrix products, arithmetic and copies ran while one was open for 7% -> 6% of each run, Pallas kernels for 20% -> 23%
where the time goes in v9:
time: 607 us; the launch traced here: 604 us
  waiting for transfers between devices  309 us (51%)
  Pallas kernels  147 us (24%)
  starting transfers between devices  82.3 us (14%)
  other arithmetic  24.2 us (4%)
  local copies, waits for them, and re-layouts  22.8 us (4%)
  between operations  18.8 us (3%)
    ppermute x21, waiting for transfers between devices, send(): lax.ppermute(v, axis, route)  205 us
    pallas_call x10, Pallas kernels, product(): pl.pallas_call(functools.partial(product_kernel, blk, row_blocks, columns...  120 us
    ppermute x21, starting transfers between devices, send(): lax.ppermute(v, axis, route)  51.9 us
    ppermute x12, waiting for transfers between devices, scatter_sum(): total = total + lax.ppermute(part((here + k) % count), axis, turn(count, k))  51.2 us
    ppermute x1, waiting for transfers between devices, body(): lax.ppermute(both_of(o), 'x', r)  20.9 us
    pallas_call x4, Pallas kernels, pack(): pl.pallas_call(functools.partial(pack_kernel, blk, row_blocks, columns, s...  17.3 us
  transfers between devices with their start and end apart: 47, of which 22 were waited for; matrix products, arithmetic and copies ran while one was open for 6% of the time, Pallas kernels for 23%

profile of v9, /device:TPU:0, one launch (start us, length us, event | category | flops | bytes accessed | tf_op | source)
XLA Modules:
  0.0 604.3 jit_solution(14706848240983951968)
XLA Ops:
  6.5 2.9 collective-permute-start
  10.2 3.5 collective-permute-start.1
  13.7 2.3 constant_dynamic-slice_fusion.16
  18.0 1.7 constant_dynamic-slice_fusion.14
  19.7 20.9 %collective-permute-done.2 = s32[2,4,128]{2,1,0:T(4,128)S(1)} collective-permute-done((s32[2,4,128]{2,1,0:T(4,128)S(1)}, s32[2,4,128]{2,1,0:T(4,128)S(1)}, u32[]{:S(2)}, u32[]{:S(2)}) %collective-permute-start.2) | collective-permute-done | bytes 4128 | tf_op jit(solution)/shard_map/ppermute | solution.py:389
  43.8 1.6 broadcast_select_fusion.5
  45.4 1.5 pad_maximum_fusion.2.refs_2_
  46.9 2.0 collective-permute-start.8
  48.9 35.8 %collective-permute-done.4 = bf16[7680,128]{1,0:T(8,128)(2,1)S(1)} collective-permute-done((bf16[7680,128]{1,0:T(8,128)(2,1)S(1)}, bf16[7680,128]{1,0:T(8,128)(2,1)S(1)}, u32[]{:S(2)}, u32[]{:S(2)}) %collective-permute-start.4) | collective-permute-done | bytes 1966112 | tf_op jit(solution)/shard_map/ppermute | solution.py:301
  85.3 2.3 broadcast_select_fusion.1
  87.6 2.3 pad_maximum_fusion.refs_1_
  89.9 2.6 collective-permute-start.14
  92.8 3.9 pack_tiles.4
  96.7 13.9 %collective-permute-done.5 = bf16[4608,128]{1,0:T(8,128)(2,1)} collective-permute-done((bf16[4608,128]{1,0:T(8,128)(2,1)S(1)}, bf16[4608,128]{1,0:T(8,128)(2,1)}, u32[]{:S(2)}, u32[]{:S(2)}) %collective-permute-start.5) | collective-permute-done | bytes 1179680 | tf_op jit(solution)/shard_map/ppermute | solution.py:301
  111.5 4.1 pack_tiles.5
  115.6 60.5 %collective-permute-done.6.refs_1_ = bf16[94,128,128]{2,1,0:T(8,128)(2,1)S(1)} collective-permute-done((bf16[94,128,128]{2,1,0:T(8,128)(2,1)}, bf16[94,128,128]{2,1,0:T(8,128)(2,1)S(1)}, u32[]{:S(2)}, u32[]{:S(2)}) %collective-permute-start.6) | collective-permute-done | bytes 3080224 | tf_op jit(solution)/shard_map/ppermute | solution.py:301
  176.1 1.6 copy-done.5
  178.3 2.0 collective-permute-start.15
  180.3 14.1 %collective-permute-done.9.refs_2_ = bf16[7680,256]{1,0:T(8,128)(2,1)} collective-permute-done((bf16[7680,256]{1,0:T(8,128)(2,1)}, bf16[7680,256]{1,0:T(8,128)(2,1)}, u32[]{:S(2)}, u32[]{:S(2)}) %collective-permute-start.9) | collective-permute-done | bytes 3932192 | tf_op jit(solution)/shard_map/ppermute | solution.py:301
  196.1 4.1 pack_tiles.6
  200.2 7.5 %collective-permute-start.12 = (bf16[104,128,128]{2,1,0:T(8,128)(2,1)}, bf16[104,128,128]{2,1,0:T(8,128)(2,1)}, u32[]{:S(2)}, u32[]{:S(2)}) collective-permute-start(bf16[104,128,128]{2,1,0:T(8,128)(2,1)} %pack_tiles.6), channel_id=1, source_target_pairs={{0,8},{24,16},{1,9},{25,17},{2,10},{26,18},{3,11},{27,19},{4,12},{... | collective-permute-start | bytes 10223624 | tf_op jit(solution)/shard_map/ppermute | solution.py:301
  207.7 2.6 collective-permute-start.16
  210.4 29.8 %collective-permute-done.10.refs_5_ = bf16[4096,256]{1,0:T(8,128)(2,1)} collective-permute-done((bf16[4096,256]{1,0:T(8,128)(2,1)}, bf16[4096,256]{1,0:T(8,128)(2,1)}, u32[]{:S(2)}, u32[]{:S(2)}) %collective-permute-start.10) | collective-permute-done | bytes 2097184 | tf_op jit(solution)/shard_map/ppermute | solution.py:301
  243.7 5.2 pack_tiles.7
  248.9 2.7 collective-permute-done.11.refs_1_
  252.2 2.7 broadcast_select_fusion.3
  255.2 20.5 %collective-permute-done.12.refs_0_ = bf16[104,128,128]{2,1,0:T(8,128)(2,1)} collective-permute-done((bf16[104,128,128]{2,1,0:T(8,128)(2,1)}, bf16[104,128,128]{2,1,0:T(8,128)(2,1)}, u32[]{:S(2)}, u32[]{:S(2)}) %collective-permute-start.12) | collective-permute-done | bytes 3407904 | tf_op jit(solution)/shard_map/ppermute | solution.py:301
  275.7 5.7 collective-permute-start.13
  283.8 2.0 collective-permute-start.17
  286.1 1.9 copy-done.6
  288.0 14.0 %tiles_times_planes.10 = f32[3,256,1024]{2,1,0:T(8,128)S(1)} custom-call(s32[260]{0:T(512)S(1)} %concatenate.63.info, bf16[512,32768]{1,0:T(8,128)(2,1)} %refs_0_.11, bf16[94,128,128]{2,1,0:T(8,128)(2,1)S(1)} %copy-done.6, bf16[4096,256]{1,0:T(8,128)(2,1)} %pad_maximum_fusion.2.refs_2_, bf16[4096,256]{1,0:T(8,128)(2,1)} %collective-permute-done.7.refs_3_, ...), custom_call_target="tpu_custom_call" | custom-call | flops 6442450944 | bytes 10485760 | tf_op jit(solution)/shard_map/tiles_times_planes/pallas_call | solution.py:205
  301.9 1.7 copy-done.3
  303.6 19.8 %collective-permute-done.19.refs_4_ = bf16[7680,256]{1,0:T(8,128)(2,1)} collective-permute-done((bf16[7680,256]{1,0:T(8,128)(2,1)}, bf16[7680,256]{1,0:T(8,128)(2,1)}, u32[]{:S(2)}, u32[]{:S(2)}) %collective-permute-start.19) | collective-permute-done | bytes 3932192 | tf_op jit(solution)/shard_map/ppermute | solution.py:301
  325.9 17.0 %collective-permute-start.23 = (bf16[104,128,128]{2,1,0:T(8,128)(2,1)}, bf16[104,128,128]{2,1,0:T(8,128)(2,1)}, u32[]{:S(2)}, u32[]{:S(2)}) collective-permute-start(bf16[104,128,128]{2,1,0:T(8,128)(2,1)} %copy-done), channel_id=1, source_target_pairs={{0,8},{24,16},{1,9},{25,17},{2,10},{26,18},{3,11},{27,19},{4,12},{... | collective-permute-start | bytes 10223624 | tf_op jit(solution)/shard_map/ppermute | solution.py:301
  343.6 17.2 %tiles_times_planes.13 = f32[3,256,512]{2,1,0:T(8,128)S(1)} custom-call(s32[243]{0:T(256)S(1)} %pad_add_fusion.8.info, bf16[512,32768]{1,0:T(8,128)(2,1)} %refs_0_.11, bf16[7680,256]{1,0:T(8,128)(2,1)} %pad_maximum_fusion.refs_1_, bf16[7680,256]{1,0:T(8,128)(2,1)} %collective-permute-done.9.refs_2_, bf16[7680,256]{1,0:T(8,128)(2,1)} %collective-permute-done.14.refs_3_, ...), custom_call_target="tpu_custom_call" | custom-call | flops 6039797760 | bytes 15728640 | tf_op jit(solution)/shard_map/tiles_times_planes/pallas_call | solution.py:205
  360.8 2.1 collective-permute-start.24
  362.9 8.4 %tiles_times_planes.15 = f32[2,256,512]{2,1,0:T(8,128)S(1)} custom-call(s32[147]{0:T(256)S(1)} %get-tuple-element.155.info, bf16[104,128,128]{2,1,0:T(8,128)(2,1)} %collective-permute-done.12.refs_0_, bf16[4608,256]{1,0:T(8,128)(2,1)S(1)} %pad_maximum_fusion.1.refs_2_.refs_1_, bf16[4608,256]{1,0:T(8,128)(2,1)} %collective-permute-done.17.refs_4_.refs_2_), custom_call_target="tpu_custom_call" | custom-call | flops 2415919104 | bytes 7077888 | tf_op jit(solution)/shard_map/tiles_times_planes/pallas_call | solution.py:205
  371.3 15.7 %tiles_times_planes.11 = f32[3,256,1024]{2,1,0:T(8,128)S(1)} custom-call(s32[292]{0:T(512)S(1)} %concatenate.67.info, bf16[512,32768]{1,0:T(8,128)(2,1)} %refs_0_.11, bf16[104,128,128]{2,1,0:T(8,128)(2,1)S(1)} %copy-done.1, bf16[4608,256]{1,0:T(8,128)(2,1)S(1)} %pad_maximum_fusion.1.refs_2_.refs_1_, bf16[4608,256]{1,0:T(8,128)(2,1)} %collective-permute-done.13.refs_3_, ...), custom_call_target="tpu_custom_call" | custom-call | flops 7247757312 | bytes 11796480 | tf_op jit(solution)/shard_map/tiles_times_planes/pallas_call | solution.py:205
  387.0 15.0 %tiles_times_planes.12 = f32[3,256,512]{2,1,0:T(8,128)S(1)} custom-call(s32[243]{0:T(256)S(1)} %pad_add_fusion.5.info, bf16[160,128,128]{2,1,0:T(8,128)(2,1)} %collective-permute-done.18.refs_0_.refs_1_, bf16[7680,256]{1,0:T(8,128)(2,1)} %pad_maximum_fusion.refs_1_, bf16[7680,256]{1,0:T(8,128)(2,1)} %collective-permute-done.9.refs_2_, ...), custom_call_target="tpu_custom_call" | custom-call | flops 6039797760 | bytes 15728640 | tf_op jit(solution)/shard_map/tiles_times_planes/pallas_call | solution.py:205
  406.6 7.6 %collective-permute-done.34.refs_3_ = bf16[7680,256]{1,0:T(8,128)(2,1)} collective-permute-done((bf16[7680,256]{1,0:T(8,128)(2,1)}, bf16[7680,256]{1,0:T(8,128)(2,1)}, u32[]{:S(2)}, u32[]{:S(2)}) %collective-permute-start.34) | collective-permute-done | bytes 3932192 | tf_op jit(solution)/shard_map/ppermute | solution.py:301
  415.6 9.4 %tiles_times_planes.14 = f32[3,256,512]{2,1,0:T(8,128)S(1)} custom-call(s32[147]{0:T(256)S(1)} %get-tuple-element.156.info, bf16[104,128,128]{2,1,0:T(8,128)(2,1)} %collective-permute-done.23.refs_0_, bf16[4608,256]{1,0:T(8,128)(2,1)S(1)} %pad_maximum_fusion.1.refs_2_.refs_1_, bf16[4608,256]{1,0:T(8,128)(2,1)} %collective-permute-done.17.refs_4_.refs_2_, ...), custom_call_target="tpu_custom_call" | custom-call | flops 3623878656 | bytes 9437184 | tf_op jit(solution)/shard_map/tiles_times_planes/pallas_call | solution.py:205
  425.0 7.1 %tiles_times_planes.16 = f32[1,256,512]{2,1,0:T(8,128)S(1)} custom-call(s32[147]{0:T(256)S(1)} %get-tuple-element.155.info, bf16[104,128,128]{2,1,0:T(8,128)(2,1)} %collective-permute-done.12.refs_0_, bf16[4608,256]{1,0:T(8,128)(2,1)} %collective-permute-done.24.refs_3_.refs_1_.refs_2_), custom_call_target="tpu_custom_call" | custom-call | flops 1207959552 | bytes 4718592 | tf_op jit(solution)/shard_map/tiles_times_planes/pallas_call | solution.py:205
  437.6 14.9 %tiles_times_planes.18 = f32[1,256,1024]{2,1,0:T(8,128)S(1)} custom-call(s32[484]{0:T(512)S(1)} %concatenate.79.info, bf16[512,32768]{1,0:T(8,128)(2,1)} %refs_0_.11, bf16[160,128,128]{2,1,0:T(8,128)(2,1)} %collective-permute-done.18.refs_0_.refs_1_, bf16[7680,256]{1,0:T(8,128)(2,1)} %collective-permute-done.16.refs_2_, ...), custom_call_target="tpu_custom_call" | custom-call | flops 4026531840 | bytes 11796480 | tf_op jit(solution)/shard_map/tiles_times_planes/pallas_call | solution.py:205
  452.6 1.9 dynamic-slice_add_fusion
  454.6 1.5 collective-permute-start.21
  456.2 9.7 %tiles_times_planes.19 = f32[1,256,1024]{2,1,0:T(8,128)S(1)} custom-call(s32[292]{0:T(512)S(1)} %concatenate.67.info, bf16[512,32768]{1,0:T(8,128)(2,1)} %refs_0_.11, bf16[104,128,128]{2,1,0:T(8,128)(2,1)S(1)} %copy-done.2, bf16[4608,256]{1,0:T(8,128)(2,1)} %collective-permute-done.24.refs_3_.refs_1_.refs_2_), custom_call_target="tpu_custom_call" | custom-call | flops 2415919104 | bytes 7077888 | tf_op jit(solution)/shard_map/tiles_times_planes/pallas_call | solution.py:205
  465.9 1.9 fusion.6
  468.6 8.8 %tiles_times_planes.17 = f32[1,256,1024]{2,1,0:T(8,128)S(1)} custom-call(s32[260]{0:T(512)S(1)} %concatenate.63.info, bf16[512,32768]{1,0:T(8,128)(2,1)} %refs_0_.11, bf16[94,128,128]{2,1,0:T(8,128)(2,1)S(1)} %copy-done.7, bf16[4096,256]{1,0:T(8,128)(2,1)} %collective-permute-done.15.refs_2_, bf16[4096,256]{1,0:T(8,128)(2,1)} %collective-permute-done.35.refs_3_), custom_call_target="tpu_custom_call" | custom-call | flops 2147483648 | bytes 6291456 | tf_op jit(solution)/shard_map/tiles_times_planes/pallas_call | solution.py:205
  478.1 13.5 %collective-permute-done.26 = f32[3,64,1024]{2,1,0:T(8,128)S(1)} collective-permute-done((f32[3,64,1024]{2,1,0:T(8,128)S(1)}, f32[3,64,1024]{2,1,0:T(8,128)S(1)}, u32[]{:S(2)}, u32[]{:S(2)}) %collective-permute-start.26) | collective-permute-done | bytes 786464 | tf_op jit(solution)/shard_map/ppermute | solution.py:286
  491.7 1.5 collective-permute-start.27
  494.0 1.6 collective-permute-start.37
  495.6 8.2 %collective-permute-done.27 = f32[3,32,1024]{2,1,0:T(8,128)S(1)} collective-permute-done((f32[3,32,1024]{2,1,0:T(8,128)S(1)}, f32[3,32,1024]{2,1,0:T(8,128)S(1)}, u32[]{:S(2)}, u32[]{:S(2)}) %collective-permute-start.27) | collective-permute-done | bytes 393248 | tf_op jit(solution)/shard_map/ppermute | solution.py:286
  505.1 5.8 collective-permute-done.22
  512.4 4.1 collective-permute-done.28
  518.0 3.4 collective-permute-start.39
  522.1 6.4 %collective-permute-done.39 = f32[40,1024]{1,0:T(8,128)S(1)} collective-permute-done((f32[40,1024]{1,0:T(8,128)S(1)}, f32[40,1024]{1,0:T(8,128)S(1)}, u32[]{:S(2)}, u32[]{:S(2)}) %collective-permute-start.39) | collective-permute-done | bytes 163872 | tf_op jit(solution)/shard_map/ppermute | solution.py:306
  535.4 2.1 collective-permute-done.41
  538.9 6.6 %collective-permute-done.43 = f32[40,1024]{1,0:T(8,128)S(1)} collective-permute-done((f32[40,1024]{1,0:T(8,128)S(1)}, f32[40,1024]{1,0:T(8,128)S(1)}, u32[]{:S(2)}, u32[]{:S(2)}) %collective-permute-start.43) | collective-permute-done | bytes 163872 | tf_op jit(solution)/shard_map/ppermute | solution.py:310
  545.5 8.3 %collective-permute-done.31 = f32[3,32,1024]{2,1,0:T(8,128)S(1)} collective-permute-done((f32[3,32,1024]{2,1,0:T(8,128)S(1)}, f32[3,32,1024]{2,1,0:T(8,128)S(1)}, u32[]{:S(2)}, u32[]{:S(2)}) %collective-permute-start.31) | collective-permute-done | bytes 393248 | tf_op jit(solution)/shard_map/ppermute | solution.py:309
  553.9 4.7 collective-permute-done.33
  558.8 9.3 %pair_dots.1 = f32[32,136,128]{2,1,0:T(8,128)S(1)} custom-call(s32[2,6,32]{2,1,0:T(8,128)S(1)} %pad_add_fusion.ids, f32[4,3,32,1024]{3,2,1,0:T(8,128)S(1)} %pad_maximum_fusion.4.early, f32[4,40,1024]{2,1,0:T(8,128)S(1)} %pad_maximum_fusion.5.late), custom_call_target="tpu_custom_call" | custom-call | tf_op jit(solution)/shard_map/pair_dots/pallas_call | solution.py:262
  568.3 2.9 collective-permute-done.44
  574.1 13.2 %collective-permute-done.45 = f32[1,2,1,4,136,128]{5,4,3,2,1,0:T(8,128)S(1)} collective-permute-done((f32[1,2,1,4,136,128]{5,4,3,2,1,0:T(8,128)S(1)}, f32[1,2,1,4,136,128]{5,4,3,2,1,0:T(8,128)S(1)}, u32[]{:S(2)}, u32[]{:S(2)}) %collective-permute-start.45) | collective-permute-done | bytes 557088 | tf_op jit(solution)/shard_map/ppermute | solution.py:286
  587.6 7.7 %collective-permute-done.46 = f32[1,1,1,4,136,128]{5,4,3,2,1,0:T(8,128)S(1)} collective-permute-done((f32[1,1,1,4,136,128]{5,4,3,2,1,0:T(8,128)S(1)}, f32[1,1,1,4,136,128]{5,4,3,2,1,0:T(8,128)S(1)}, u32[]{:S(2)}, u32[]{:S(2)}) %collective-permute-start.46) | collective-permute-done | bytes 278560 | tf_op jit(solution)/shard_map/ppermute | solution.py:286
  (204 shorter events, 48.0 us)
Async XLA Ops:
  6.5 13.2 %collective-permute-start = (s32[16,2]{0,1:T(2,128)}, s32[16,2]{0,1:T(2,128)S(1)}, u32[]{:S(2)}, u32[]{:S(2)}) collective-permute-start(s32[16,2]{0,1:T(2,128)} %param.12), channel_id=1, source_target_pairs={{0,4},{4,0},{1,5},{5,1},{2,6},{6,2},{3,7},{7,3},{8,12},{12,8},{9,1... | collective-permute-start | bytes 392 | tf_op jit(solution)/shard_map/ppermute | solution.py:390
  10.2 6.4 %collective-permute-start.1 = (s32[4,256]{1,0:T(4,128)S(1)}, s32[4,256]{1,0:T(4,128)S(1)}, u32[]{:S(2)}, u32[]{:S(2)}) collective-permute-start(s32[4,256]{1,0:T(4,128)S(1)} %get-tuple-element.152), channel_id=1, source_target_pairs={{0,8},{24,16},{1,9},{25,17},{2,10},{26,18},{3,11},{27,19},{4,12},{... | collective-permute-start | bytes 12296 | tf_op jit(solution)/shard_map/ppermute | solution.py:384
  16.0 24.6 %collective-permute-start.3 = (bf16[4096,128]{1,0:T(8,128)(2,1)}, bf16[4096,128]{1,0:T(8,128)(2,1)S(1)}, u32[]{:S(2)}, u32[]{:S(2)}) collective-permute-start(bf16[4096,128]{1,0:T(8,128)(2,1)} %constant_dynamic-slice_fusion.16), channel_id=1, source_target_pairs={{0,4},{4,0},{1,5},{5,1},{2,6},{6,2},{3,7},{7,3},{8,12},{12,8},{9,1... | collective-permute-start | bytes 3145736 | tf_op jit(solution)/shard_map/ppermute | solution.py:301
  16.5 24.1 %collective-permute-start.2 = (s32[2,4,128]{2,1,0:T(4,128)S(1)}, s32[2,4,128]{2,1,0:T(4,128)S(1)}, u32[]{:S(2)}, u32[]{:S(2)}) collective-permute-start(s32[2,4,128]{2,1,0:T(4,128)S(1)} %get-tuple-element.144), channel_id=1, source_target_pairs={{0,4},{4,0},{1,5},{5,1},{2,6},{6,2},{3,7},{7,3},{8,12},{12,8},{9,1... | collective-permute-start | bytes 12296 | tf_op jit(solution)/shard_map/ppermute | solution.py:389
  41.6 43.1 %collective-permute-start.4 = (bf16[7680,128]{1,0:T(8,128)(2,1)S(1)}, bf16[7680,128]{1,0:T(8,128)(2,1)S(1)}, u32[]{:S(2)}, u32[]{:S(2)}) collective-permute-start(bf16[7680,128]{1,0:T(8,128)(2,1)S(1)} %constant_dynamic-slice_fusion.14), channel_id=1, source_target_pairs={{0,4},{4,0},{1,5},{5,1},{2,6},{6,2},{3,7},{7,3},{8,12},{12,8},{9,1... | collective-permute-start | bytes 5898248 | tf_op jit(solution)/shard_map/ppermute | solution.py:301
  46.9 64.3 %collective-permute-start.7 = (bf16[4096,256]{1,0:T(8,128)(2,1)}, bf16[4096,256]{1,0:T(8,128)(2,1)}, u32[]{:S(2)}, u32[]{:S(2)}) collective-permute-start(bf16[4096,256]{1,0:T(8,128)(2,1)} %pad_maximum_fusion.2.refs_2_), channel_id=1, source_target_pairs={{0,8},{8,0},{16,24},{24,16},{1,9},{9,1},{17,25},{25,17},{2,10},{10... | collective-permute-start | bytes 6291464 | tf_op jit(solution)/shard_map/ppermute | solution.py:301
  46.9 43.0 %collective-permute-start.8 = (bf16[4096,256]{1,0:T(8,128)(2,1)}, bf16[4096,256]{1,0:T(8,128)(2,1)}, u32[]{:S(2)}, u32[]{:S(2)}) collective-permute-start(bf16[4096,256]{1,0:T(8,128)(2,1)} %pad_maximum_fusion.2.refs_2_), channel_id=1, source_target_pairs={{8,16},{16,8},{9,17},{17,9},{10,18},{18,10},{11,19},{19,11},{12,20... | collective-permute-start | bytes 6291464 | tf_op jit(solution)/shard_map/ppermute | solution.py:301
  84.7 25.9 %collective-permute-start.5 = (bf16[4608,128]{1,0:T(8,128)(2,1)S(1)}, bf16[4608,128]{1,0:T(8,128)(2,1)}, u32[]{:S(2)}, u32[]{:S(2)}) collective-permute-start(bf16[4608,128]{1,0:T(8,128)(2,1)S(1)} %constant_dynamic-slice_fusion.15), channel_id=1, source_target_pairs={{0,4},{4,0},{1,5},{5,1},{2,6},{6,2},{3,7},{7,3},{8,12},{12,8},{9,1... | collective-permute-start | bytes 3538952 | tf_op jit(solution)/shard_map/ppermute | solution.py:301
  89.9 88.4 %collective-permute-start.14 = (bf16[7680,256]{1,0:T(8,128)(2,1)}, bf16[7680,256]{1,0:T(8,128)(2,1)}, u32[]{:S(2)}, u32[]{:S(2)}) collective-permute-start(bf16[7680,256]{1,0:T(8,128)(2,1)} %pad_maximum_fusion.refs_1_), channel_id=1, source_target_pairs={{8,16},{16,8},{9,17},{17,9},{10,18},{18,10},{11,19},{19,11},{12,20... | collective-permute-start | bytes 11796488 | tf_op jit(solution)/shard_map/ppermute | solution.py:301
  110.6 65.5 %collective-permute-start.6 = (bf16[94,128,128]{2,1,0:T(8,128)(2,1)}, bf16[94,128,128]{2,1,0:T(8,128)(2,1)S(1)}, u32[]{:S(2)}, u32[]{:S(2)}) collective-permute-start(bf16[94,128,128]{2,1,0:T(8,128)(2,1)} %pack_tiles.4), channel_id=1, source_target_pairs={{0,4},{4,0},{1,5},{5,1},{2,6},{6,2},{3,7},{7,3},{8,12},{12,8},{9,1... | collective-permute-start | bytes 9240584 | tf_op jit(solution)/shard_map/ppermute | solution.py:301
  111.2 83.2 %collective-permute-start.9 = (bf16[7680,256]{1,0:T(8,128)(2,1)}, bf16[7680,256]{1,0:T(8,128)(2,1)}, u32[]{:S(2)}, u32[]{:S(2)}) collective-permute-start(bf16[7680,256]{1,0:T(8,128)(2,1)} %pad_maximum_fusion.refs_1_), channel_id=1, source_target_pairs={{0,8},{8,0},{16,24},{24,16},{1,9},{9,1},{17,25},{25,17},{2,10},{10... | collective-permute-start | bytes 11796488 | tf_op jit(solution)/shard_map/ppermute | solution.py:301
  177.7 73.9 %collective-permute-start.11 = (bf16[104,128,128]{2,1,0:T(8,128)(2,1)}, bf16[104,128,128]{2,1,0:T(8,128)(2,1)S(1)}, u32[]{:S(2)}, u32[]{:S(2)}) collective-permute-start(bf16[104,128,128]{2,1,0:T(8,128)(2,1)} %pack_tiles.5), channel_id=1, source_target_pairs={{0,4},{4,0},{1,5},{5,1},{2,6},{6,2},{3,7},{7,3},{8,12},{12,8},{9,1... | collective-permute-start | bytes 10223624 | tf_op jit(solution)/shard_map/ppermute | solution.py:301
  178.3 29.5 %collective-permute-start.15 = (bf16[4096,256]{1,0:T(8,128)(2,1)}, bf16[4096,256]{1,0:T(8,128)(2,1)}, u32[]{:S(2)}, u32[]{:S(2)}) collective-permute-start(bf16[4096,256]{1,0:T(8,128)(2,1)} %collective-permute-done.7.refs_3_), channel_id=1, source_target_pairs={{8,16},{16,8},{9,17},{17,9},{10,18},{18,10},{11,19},{19,11},{12,20... | collective-permute-start | bytes 6291464 | tf_op jit(solution)/shard_map/ppermute | solution.py:301
  194.4 45.8 %collective-permute-start.10 = (bf16[4096,256]{1,0:T(8,128)(2,1)}, bf16[4096,256]{1,0:T(8,128)(2,1)}, u32[]{:S(2)}, u32[]{:S(2)}) collective-permute-start(bf16[4096,256]{1,0:T(8,128)(2,1)} %collective-permute-done.8.refs_4_), channel_id=1, source_target_pairs={{8,0},{16,24},{9,1},{17,25},{10,2},{18,26},{11,3},{19,27},{12,4},{... | collective-permute-start | bytes 6291464 | tf_op jit(solution)/shard_map/ppermute | solution.py:301
  200.2 75.5 %collective-permute-start.12 = (bf16[104,128,128]{2,1,0:T(8,128)(2,1)}, bf16[104,128,128]{2,1,0:T(8,128)(2,1)}, u32[]{:S(2)}, u32[]{:S(2)}) collective-permute-start(bf16[104,128,128]{2,1,0:T(8,128)(2,1)} %pack_tiles.6), channel_id=1, source_target_pairs={{0,8},{24,16},{1,9},{25,17},{2,10},{26,18},{3,11},{27,19},{4,12},{... | collective-permute-start | bytes 10223624 | tf_op jit(solution)/shard_map/ppermute | solution.py:301
  207.7 76.0 %collective-permute-start.16 = (bf16[7680,256]{1,0:T(8,128)(2,1)}, bf16[7680,256]{1,0:T(8,128)(2,1)}, u32[]{:S(2)}, u32[]{:S(2)}) collective-permute-start(bf16[7680,256]{1,0:T(8,128)(2,1)} %collective-permute-done.9.refs_2_), channel_id=1, source_target_pairs={{8,16},{16,8},{9,17},{17,9},{10,18},{18,10},{11,19},{19,11},{12,20... | collective-permute-start | bytes 11796488 | tf_op jit(solution)/shard_map/ppermute | solution.py:301
  240.2 83.3 %collective-permute-start.19 = (bf16[7680,256]{1,0:T(8,128)(2,1)}, bf16[7680,256]{1,0:T(8,128)(2,1)}, u32[]{:S(2)}, u32[]{:S(2)}) collective-permute-start(bf16[7680,256]{1,0:T(8,128)(2,1)} %collective-permute-done.14.refs_3_), channel_id=1, source_target_pairs={{8,0},{16,24},{9,1},{17,25},{10,2},{18,26},{11,3},{19,27},{12,4},{... | collective-permute-start | bytes 11796488 | tf_op jit(solution)/shard_map/ppermute | solution.py:301
  251.6 3.3 copy-start
  251.6 135.3 %collective-permute-start.18 = (bf16[160,128,128]{2,1,0:T(8,128)(2,1)}, bf16[160,128,128]{2,1,0:T(8,128)(2,1)}, u32[]{:S(2)}, u32[]{:S(2)}) collective-permute-start(bf16[160,128,128]{2,1,0:T(8,128)(2,1)} %pack_tiles.7), channel_id=1, source_target_pairs={{0,4},{4,0},{1,5},{5,1},{2,6},{6,2},{3,7},{7,3},{8,12},{12,8},{9,1... | collective-permute-start | bytes 15728648 | tf_op jit(solution)/shard_map/ppermute | solution.py:301
  275.7 50.1 %collective-permute-start.13 = (bf16[4608,256]{1,0:T(8,128)(2,1)S(1)}, bf16[4608,256]{1,0:T(8,128)(2,1)}, u32[]{:S(2)}, u32[]{:S(2)}) collective-permute-start(bf16[4608,256]{1,0:T(8,128)(2,1)S(1)} %pad_maximum_fusion.1.refs_2_.refs_1_), channel_id=1, source_target_pairs={{0,8},{24,16},{1,9},{25,17},{2,10},{26,18},{3,11},{27,19},{4,12},{... | collective-permute-start | bytes 7077896 | tf_op jit(solution)/shard_map/ppermute | solution.py:301
  283.8 77.0 %collective-permute-start.17 = (bf16[4608,256]{1,0:T(8,128)(2,1)S(1)}, bf16[4608,256]{1,0:T(8,128)(2,1)}, u32[]{:S(2)}, u32[]{:S(2)}) collective-permute-start(bf16[4608,256]{1,0:T(8,128)(2,1)S(1)} %pad_maximum_fusion.1.refs_2_.refs_1_), channel_id=1, source_target_pairs={{8,16},{16,8},{9,17},{17,9},{10,18},{18,10},{11,19},{19,11},{12,20... | collective-permute-start | bytes 7077896 | tf_op jit(solution)/shard_map/ppermute | solution.py:301
  286.1 1.9 copy-start.6
  301.9 1.7 copy-start.3
  323.5 90.8 %collective-permute-start.34 = (bf16[7680,256]{1,0:T(8,128)(2,1)}, bf16[7680,256]{1,0:T(8,128)(2,1)}, u32[]{:S(2)}, u32[]{:S(2)}) collective-permute-start(bf16[7680,256]{1,0:T(8,128)(2,1)} %collective-permute-done.16.refs_2_), channel_id=1, source_target_pairs={{8,0},{16,24},{9,1},{17,25},{10,2},{18,26},{11,3},{19,27},{12,4},{... | collective-permute-start | bytes 11796488 | tf_op jit(solution)/shard_map/ppermute | solution.py:301
  325.9 89.7 %collective-permute-start.23 = (bf16[104,128,128]{2,1,0:T(8,128)(2,1)}, bf16[104,128,128]{2,1,0:T(8,128)(2,1)}, u32[]{:S(2)}, u32[]{:S(2)}) collective-permute-start(bf16[104,128,128]{2,1,0:T(8,128)(2,1)} %copy-done), channel_id=1, source_target_pairs={{0,8},{24,16},{1,9},{25,17},{2,10},{26,18},{3,11},{27,19},{4,12},{... | collective-permute-start | bytes 10223624 | tf_op jit(solution)/shard_map/ppermute | solution.py:301
  360.8 10.5 %copy-start.8 = (f32[3,256,512]{2,1,0:T(8,128)}, f32[3,256,512]{2,1,0:T(8,128)S(1)}, u32[]{:S(2)}) copy-start(f32[3,256,512]{2,1,0:T(8,128)S(1)} %tiles_times_planes.13) | copy-start | bytes 4718596
  360.8 54.8 %collective-permute-start.24 = (bf16[4608,256]{1,0:T(8,128)(2,1)}, bf16[4608,256]{1,0:T(8,128)(2,1)}, u32[]{:S(2)}, u32[]{:S(2)}) collective-permute-start(bf16[4608,256]{1,0:T(8,128)(2,1)} %collective-permute-done.13.refs_3_), channel_id=1, source_target_pairs={{8,16},{16,8},{9,17},{17,9},{10,18},{18,10},{11,19},{19,11},{12,20... | collective-permute-start | bytes 7077896 | tf_op jit(solution)/shard_map/ppermute | solution.py:301
  362.9 8.4 %copy-start.1 = (bf16[104,128,128]{2,1,0:T(8,128)(2,1)S(1)}, bf16[104,128,128]{2,1,0:T(8,128)(2,1)}, u32[]{:S(2)}) copy-start(bf16[104,128,128]{2,1,0:T(8,128)(2,1)} %copy-done) | copy-start | bytes 10223620
  387.0 15.1 %copy-start.9 = (f32[3,256,512]{2,1,0:T(8,128)S(1)}, f32[3,256,512]{2,1,0:T(8,128)}, u32[]{:S(2)}) copy-start(f32[3,256,512]{2,1,0:T(8,128)} %copy-done.8) | copy-start | bytes 4718596
  402.0 1.9 copy-start.4
  405.2 19.8 %copy-start.15 = (f32[3,256,1024]{2,1,0:T(8,128)}, f32[3,256,1024]{2,1,0:T(8,128)S(1)}, u32[]{:S(2)}) copy-start(f32[3,256,1024]{2,1,0:T(8,128)S(1)} %maximum_add_fusion) | copy-start | bytes 9437188
  406.6 46.0 %collective-permute-start.20 = (f32[3,128,1024]{2,1,0:T(8,128)}, f32[3,128,1024]{2,1,0:T(8,128)}, u32[]{:S(2)}, u32[]{:S(2)}) collective-permute-start(f32[3,128,1024]{2,1,0:T(8,128)} %constant_dynamic-slice_fusion.12), channel_id=1, source_target_pairs={{0,1},{1,0},{2,3},{3,2},{4,5},{5,4},{6,7},{7,6},{8,9},{9,8},{10,11... | collective-permute-start | bytes 4718600 | tf_op jit(solution)/shard_map/ppermute | solution.py:286
  414.3 54.3 %collective-permute-start.35 = (bf16[4096,256]{1,0:T(8,128)(2,1)}, bf16[4096,256]{1,0:T(8,128)(2,1)}, u32[]{:S(2)}, u32[]{:S(2)}) collective-permute-start(bf16[4096,256]{1,0:T(8,128)(2,1)} %collective-permute-done.15.refs_2_), channel_id=1, source_target_pairs={{8,0},{16,24},{9,1},{17,25},{10,2},{18,26},{11,3},{19,27},{12,4},{... | collective-permute-start | bytes 6291464 | tf_op jit(solution)/shard_map/ppermute | solution.py:301
  432.5 1.7 copy-start.11
  432.5 2.2 copy-start.13
  432.5 4.4 copy-start.10
  432.5 4.4 copy-start.21
  434.6 31.2 %collective-permute-start.25 = (f32[3,128,1024]{2,1,0:T(8,128)}, f32[3,128,1024]{2,1,0:T(8,128)}, u32[]{:S(2)}, u32[]{:S(2)}) collective-permute-start(f32[3,128,1024]{2,1,0:T(8,128)} %fusion.4), channel_id=1, source_target_pairs={{0,1},{1,0},{2,3},{3,2},{4,5},{5,4},{6,7},{7,6},{8,9},{9,8},{10,11... | collective-permute-start | bytes 4718600 | tf_op jit(solution)/shard_map/ppermute | solution.py:286
  437.6 15.0 %copy-start.16 = (f32[3,256,1024]{2,1,0:T(8,128)S(1)}, f32[3,256,1024]{2,1,0:T(8,128)}, u32[]{:S(2)}) copy-start(f32[3,256,1024]{2,1,0:T(8,128)} %copy-done.15) | copy-start | bytes 9437188
  452.6 3.6 copy-start.2
  454.6 11.3 %copy-start.12 = (f32[3,256,512]{2,1,0:T(8,128)S(1)}, f32[3,256,512]{2,1,0:T(8,128)}, u32[]{:S(2)}) copy-start(f32[3,256,512]{2,1,0:T(8,128)} %copy-done.11) | copy-start | bytes 4718596
  454.6 11.3 %copy-start.14 = (f32[3,256,512]{2,1,0:T(8,128)S(1)}, f32[3,256,512]{2,1,0:T(8,128)}, u32[]{:S(2)}) copy-start(f32[3,256,512]{2,1,0:T(8,128)} %copy-done.13) | copy-start | bytes 4718596
  454.6 23.3 %collective-permute-start.21 = (f32[3,64,1024]{2,1,0:T(8,128)S(1)}, f32[3,64,1024]{2,1,0:T(8,128)S(1)}, u32[]{:S(2)}, u32[]{:S(2)}) collective-permute-start(f32[3,64,1024]{2,1,0:T(8,128)S(1)} %constant_dynamic-slice_fusion.11), channel_id=1, source_target_pairs={{0,4},{4,0},{1,5},{5,1},{2,6},{6,2},{3,7},{7,3},{8,12},{12,8},{9,1... | collective-permute-start | bytes 2359304 | tf_op jit(solution)/shard_map/ppermute | solution.py:286
  465.9 2.7 copy-start.7
  467.9 23.7 %collective-permute-start.26 = (f32[3,64,1024]{2,1,0:T(8,128)S(1)}, f32[3,64,1024]{2,1,0:T(8,128)S(1)}, u32[]{:S(2)}, u32[]{:S(2)}) collective-permute-start(f32[3,64,1024]{2,1,0:T(8,128)S(1)} %constant_dynamic-slice_fusion.9), channel_id=1, source_target_pairs={{0,4},{4,0},{1,5},{5,1},{2,6},{6,2},{3,7},{7,3},{8,12},{12,8},{9,1... | collective-permute-start | bytes 2359304 | tf_op jit(solution)/shard_map/ppermute | solution.py:286
  477.8 16.1 %collective-permute-start.36 = (f32[1,128,1024]{2,1,0:T(8,128)S(1)}, f32[1,128,1024]{2,1,0:T(8,128)S(1)}, u32[]{:S(2)}, u32[]{:S(2)}) collective-permute-start(f32[1,128,1024]{2,1,0:T(8,128)S(1)} %constant_dynamic-slice_fusion.7), channel_id=1, source_target_pairs={{0,1},{1,0},{2,3},{3,2},{4,5},{5,4},{6,7},{7,6},{8,9},{9,8},{10,11... | collective-permute-start | bytes 1572872 | tf_op jit(solution)/shard_map/ppermute | solution.py:286
  491.7 12.1 %collective-permute-start.27 = (f32[3,32,1024]{2,1,0:T(8,128)S(1)}, f32[3,32,1024]{2,1,0:T(8,128)S(1)}, u32[]{:S(2)}, u32[]{:S(2)}) collective-permute-start(f32[3,32,1024]{2,1,0:T(8,128)S(1)} %constant_dynamic-slice_fusion.8), channel_id=1, source_target_pairs={{0,2},{2,0},{1,3},{3,1},{4,6},{6,4},{5,7},{7,5},{8,10},{10,8},{9,1... | collective-permute-start | bytes 1179656 | tf_op jit(solution)/shard_map/ppermute | solution.py:286
  493.3 17.7 %collective-permute-start.22 = (f32[3,32,1024]{2,1,0:T(8,128)S(1)}, f32[3,32,1024]{2,1,0:T(8,128)S(1)}, u32[]{:S(2)}, u32[]{:S(2)}) collective-permute-start(f32[3,32,1024]{2,1,0:T(8,128)S(1)} %constant_dynamic-slice_fusion.10), channel_id=1, source_target_pairs={{0,2},{2,0},{1,3},{3,1},{4,6},{6,4},{5,7},{7,5},{8,10},{10,8},{9,1... | collective-permute-start | bytes 1179656 | tf_op jit(solution)/shard_map/ppermute | solution.py:286
  494.0 17.0 %collective-permute-start.37 = (f32[1,64,1024]{2,1,0:T(8,128)S(1)}, f32[1,64,1024]{2,1,0:T(8,128)S(1)}, u32[]{:S(2)}, u32[]{:S(2)}) collective-permute-start(f32[1,64,1024]{2,1,0:T(8,128)S(1)} %constant_dynamic-slice_fusion.6), channel_id=1, source_target_pairs={{0,4},{4,0},{1,5},{5,1},{2,6},{6,2},{3,7},{7,3},{8,12},{12,8},{9,1... | collective-permute-start | bytes 786440 | tf_op jit(solution)/shard_map/ppermute | solution.py:286
  503.8 12.7 %collective-permute-start.28 = (f32[3,32,1024]{2,1,0:T(8,128)S(1)}, f32[3,32,1024]{2,1,0:T(8,128)S(1)}, u32[]{:S(2)}, u32[]{:S(2)}) collective-permute-start(f32[3,32,1024]{2,1,0:T(8,128)S(1)} %dynamic-slice_add_fusion.6), channel_id=1, source_target_pairs={{8,0},{16,24},{9,1},{17,25},{10,2},{18,26},{11,3},{19,27},{12,4},{... | collective-permute-start | bytes 1179656 | tf_op jit(solution)/shard_map/ppermute | solution.py:456
  511.1 6.8 %collective-permute-start.38 = (f32[1,32,1024]{2,1,0:T(8,128)S(1)}, f32[1,32,1024]{2,1,0:T(8,128)S(1)}, u32[]{:S(2)}, u32[]{:S(2)}) collective-permute-start(f32[1,32,1024]{2,1,0:T(8,128)S(1)} %constant_dynamic-slice_fusion.5), channel_id=1, source_target_pairs={{0,2},{2,0},{1,3},{3,1},{4,6},{6,4},{5,7},{7,5},{8,10},{10,8},{9,1... | collective-permute-start | bytes 393224 | tf_op jit(solution)/shard_map/ppermute | solution.py:286
  516.6 14.0 %collective-permute-start.29 = (f32[3,32,1024]{2,1,0:T(8,128)S(1)}, f32[3,32,1024]{2,1,0:T(8,128)S(1)}, u32[]{:S(2)}, u32[]{:S(2)}) collective-permute-start(f32[3,32,1024]{2,1,0:T(8,128)S(1)} %fusion.9), channel_id=1, source_target_pairs={{0,8},{8,0},{16,24},{24,16},{1,9},{9,1},{17,25},{25,17},{2,10},{10... | collective-permute-start | bytes 1179656 | tf_op jit(solution)/shard_map/ppermute | solution.py:306
  517.2 16.9 %collective-permute-start.30 = (f32[3,32,1024]{2,1,0:T(8,128)S(1)}, f32[3,32,1024]{2,1,0:T(8,128)S(1)}, u32[]{:S(2)}, u32[]{:S(2)}) collective-permute-start(f32[3,32,1024]{2,1,0:T(8,128)S(1)} %fusion.9), channel_id=1, source_target_pairs={{8,16},{16,8},{9,17},{17,9},{10,18},{18,10},{11,19},{19,11},{12,20... | collective-permute-start | bytes 1179656 | tf_op jit(solution)/shard_map/ppermute | solution.py:307
  518.0 10.6 %collective-permute-start.39 = (f32[40,1024]{1,0:T(8,128)S(1)}, f32[40,1024]{1,0:T(8,128)S(1)}, u32[]{:S(2)}, u32[]{:S(2)}) collective-permute-start(f32[40,1024]{1,0:T(8,128)S(1)} %get-tuple-element.142), channel_id=1, source_target_pairs={{0,8},{8,0},{16,24},{24,16},{1,9},{9,1},{17,25},{25,17},{2,10},{10... | collective-permute-start | bytes 491528 | tf_op jit(solution)/shard_map/ppermute | solution.py:306
  521.3 7.9 %collective-permute-start.40 = (f32[40,1024]{1,0:T(8,128)S(1)}, f32[40,1024]{1,0:T(8,128)S(1)}, u32[]{:S(2)}, u32[]{:S(2)}) collective-permute-start(f32[40,1024]{1,0:T(8,128)S(1)} %get-tuple-element.142), channel_id=1, source_target_pairs={{8,16},{16,8},{9,17},{17,9},{10,18},{18,10},{11,19},{19,11},{12,20... | collective-permute-start | bytes 491528 | tf_op jit(solution)/shard_map/ppermute | solution.py:307
  528.5 4.3 collective-permute-start.42
  529.2 8.3 %collective-permute-start.41 = (f32[40,1024]{1,0:T(8,128)S(1)}, f32[40,1024]{1,0:T(8,128)S(1)}, u32[]{:S(2)}, u32[]{:S(2)}) collective-permute-start(f32[40,1024]{1,0:T(8,128)S(1)} %collective-permute-done.40), channel_id=1, source_target_pairs={{8,0},{16,24},{9,1},{17,25},{10,2},{18,26},{11,3},{19,27},{12,4},{... | collective-permute-start | bytes 491528 | tf_op jit(solution)/shard_map/ppermute | solution.py:309
  530.5 7.0 %collective-permute-start.32 = (f32[3,32,1024]{2,1,0:T(8,128)S(1)}, f32[3,32,1024]{2,1,0:T(8,128)S(1)}, u32[]{:S(2)}, u32[]{:S(2)}) collective-permute-start(f32[3,32,1024]{2,1,0:T(8,128)S(1)} %collective-permute-done.29), channel_id=1, source_target_pairs={{8,16},{16,8},{9,17},{17,9},{10,18},{18,10},{11,19},{19,11},{12,20... | collective-permute-start | bytes 1179656 | tf_op jit(solution)/shard_map/ppermute | solution.py:308
  532.8 12.6 %collective-permute-start.43 = (f32[40,1024]{1,0:T(8,128)S(1)}, f32[40,1024]{1,0:T(8,128)S(1)}, u32[]{:S(2)}, u32[]{:S(2)}) collective-permute-start(f32[40,1024]{1,0:T(8,128)S(1)} %collective-permute-done.42), channel_id=1, source_target_pairs={{8,0},{16,24},{9,1},{17,25},{10,2},{18,26},{11,3},{19,27},{12,4},{... | collective-permute-start | bytes 491528 | tf_op jit(solution)/shard_map/ppermute | solution.py:310
  534.1 19.7 %collective-permute-start.31 = (f32[3,32,1024]{2,1,0:T(8,128)S(1)}, f32[3,32,1024]{2,1,0:T(8,128)S(1)}, u32[]{:S(2)}, u32[]{:S(2)}) collective-permute-start(f32[3,32,1024]{2,1,0:T(8,128)S(1)} %collective-permute-done.30), channel_id=1, source_target_pairs={{8,0},{16,24},{9,1},{17,25},{10,2},{18,26},{11,3},{19,27},{12,4},{... | collective-permute-start | bytes 1179656 | tf_op jit(solution)/shard_map/ppermute | solution.py:309
  537.6 21.0 %collective-permute-start.33 = (f32[3,32,1024]{2,1,0:T(8,128)S(1)}, f32[3,32,1024]{2,1,0:T(8,128)S(1)}, u32[]{:S(2)}, u32[]{:S(2)}) collective-permute-start(f32[3,32,1024]{2,1,0:T(8,128)S(1)} %collective-permute-done.32), channel_id=1, source_target_pairs={{8,0},{16,24},{9,1},{17,25},{10,2},{18,26},{11,3},{19,27},{12,4},{... | collective-permute-start | bytes 1179656 | tf_op jit(solution)/shard_map/ppermute | solution.py:310
  568.2 3.0 collective-permute-start.44
  572.6 14.7 %collective-permute-start.45 = (f32[1,2,1,4,136,128]{5,4,3,2,1,0:T(8,128)S(1)}, f32[1,2,1,4,136,128]{5,4,3,2,1,0:T(8,128)S(1)}, u32[]{:S(2)}, u32[]{:S(2)}) collective-permute-start(f32[1,2,1,4,136,128]{5,4,3,2,1,0:T(8,128)S(1)} %constant_dynamic-slice_fusion.3), channel_id=1, source_target_pairs={{0,4},{4,0},{1,5},{5,1},{2,6},{6,2},{3,7},{7,3},{8,12},{12,8},{9,1... | collective-permute-start | bytes 1671176 | tf_op jit(solution)/shard_map/ppermute | solution.py:286
  587.4 7.9 %collective-permute-start.46 = (f32[1,1,1,4,136,128]{5,4,3,2,1,0:T(8,128)S(1)}, f32[1,1,1,4,136,128]{5,4,3,2,1,0:T(8,128)S(1)}, u32[]{:S(2)}, u32[]{:S(2)}) collective-permute-start(f32[1,1,1,4,136,128]{5,4,3,2,1,0:T(8,128)S(1)} %constant_dynamic-slice_fusion.2), channel_id=1, source_target_pairs={{0,2},{2,0},{1,3},{3,1},{4,6},{6,4},{5,7},{7,5},{8,10},{10,8},{9,1... | collective-permute-start | bytes 835592 | tf_op jit(solution)/shard_map/ppermute | solution.py:286
  (4 other events, 4.9 us)

commit v10 on v8

--- a/solution.py
+++ b/solution.py
@@ -19,7 +19,7 @@
 SOURCE = np.array([[0, 1, 2, 3], [1, 0, 2, 3], [2, 3, 1, 0], [3, 2, 1, 0]], np.int32)
 PLACE = np.argsort(SOURCE, axis=1).astype(np.int32)
 
-LENT = (9, 32)
+LENT = (5, 16)
 
 
 def bounds(total, parts):
@@ -76,7 +76,7 @@
     )(info, hist)
 
 
-STRIDE = 4
+STRIDE = 8
 
 
 def product_kernel(blk, row_blocks, steps, slots, paired, info, *refs):
@@ -86,106 +86,105 @@
     for two in paired:
         planes.append(refs[at : at + 1 + two])
         at += 1 + two
-    out, total, tiles, held, tile_sem, held_sem = refs[at:]
+    out, total, work, own, packed, held, source_sem, held_sem = refs[at:]
     rows = row_blocks * blk
     depth = STRIDE * blk
+    step_tiles = STRIDE * row_blocks
     inner, base = info[0] != 0, info[1]
-    per_source = steps * STRIDE * row_blocks
-
-    def fetch(i, slot, used, active):
+    lists = 2 + count
+    starts = lists + count * steps * step_tiles
+
+    def landing(k, slot):
+        return own.at[slot] if slots[k] is None else packed.at[slot, sum(v is not None for v in slots[:k])]
+
+    def fetch(i, slot):
         first = pl.multiple_of(i * depth, depth)
         for g, choice in enumerate(planes):
             for which, ref in enumerate(choice):
-                wanted = active
-                if len(choice) == 2:
-                    wanted = jnp.logical_and(active, inner if which == 0 else jnp.logical_not(inner))
+                wanted = True if len(choice) == 1 else inner if which == 0 else jnp.logical_not(inner)
 
                 @pl.when(wanted)
                 def _():
                     pltpu.make_async_copy(ref.at[pl.ds(first, depth)], held.at[slot, g], held_sem.at[slot]).start()
 
-        started = jnp.int32(0)
-        following = []
         for k in range(count):
-            mine = used[k]
+            if slots[k] is None:
+                start = pl.multiple_of((base + i * STRIDE) * blk, blk)
+                part = sources[k].at[:, pl.ds(start, depth)]
+            else:
+                part = sources[k].at[pl.ds(info[starts + k * steps + i], step_tiles)]
+            pltpu.make_async_copy(part, landing(k, slot), source_sem.at[slot, k]).start()
+
+    total[...] = jnp.zeros_like(total)
+    fetch(0, 0)
+
+    def one_step(i, nothing):
+        slot = lax.rem(i, 2)
+
+        @pl.when(i + 1 < steps)
+        def _():
+            fetch(i + 1, 1 - slot)
+
+        for k in range(count):
+            pltpu.make_async_copy(landing(k, slot), landing(k, slot), source_sem.at[slot, k]).wait()
             for j in range(STRIDE):
-                column = i * STRIDE + j
-                start = pl.multiple_of((base + column) * blk, blk)
                 for b in range(row_blocks):
-                    there = info[2 + count + k * per_source + column * row_blocks + b] != 0
-                    there = jnp.logical_and(there, active)
-                    if slots[k] is not None:
-                        there = jnp.logical_and(there, mine < slots[k])
-                    place = (pl.ds(k * rows + b * blk, blk), pl.ds(j * blk, blk))
-
-                    @pl.when(there)
-                    def _():
-                        if slots[k] is None:
-                            tile = sources[k].at[pl.ds(b * blk, blk), pl.ds(start, blk)]
-                        else:
-                            tile = sources[k].at[mine]
-                        pltpu.make_async_copy(tile, tiles.at[(slot,) + place], tile_sem.at[slot]).start()
-
-                    @pl.when(jnp.logical_not(there))
-                    def _():
-                        tiles[(slot,) + place] = jnp.zeros((blk, blk), tiles.dtype)
-
-                    mine = mine + there.astype(jnp.int32)
-                    started = started + there.astype(jnp.int32)
-            following.append(mine)
-        return tuple(following), started
-
-    total[...] = jnp.zeros_like(total)
-    first_used, first_started = fetch(0, 0, (jnp.int32(0),) * count, True)
-
-    def one_step(i, carry):
-        used, started = carry
-        slot = lax.rem(i, 2)
-        after_used, after_started = fetch(
-            jnp.minimum(i + 1, steps - 1), 1 - slot, used, i + 1 < steps
-        )
-
-        def one_wait(_, nothing):
-            tile = tiles.at[slot, pl.ds(0, blk), pl.ds(0, blk)]
-            pltpu.make_async_copy(tile, tile, tile_sem.at[slot]).wait()
-            return nothing
-
-        lax.fori_loop(0, started, one_wait, 0)
+                    found = info[lists + (k * steps + i) * step_tiles + j * row_blocks + b]
+                    area = (pl.ds(b * blk, blk), pl.ds(j * blk, blk))
+                    if slots[k] is None:
+                        tile = own[(slot,) + area]
+                    else:
+                        tile = landing(k, slot)[jnp.maximum(found, 0)]
+                    work[pl.ds(k * rows + b * blk, blk), pl.ds(j * blk, blk)] = jnp.where(
+                        found >= 0, tile, jnp.zeros_like(tile)
+                    )
         for g in range(groups):
             pltpu.make_async_copy(held.at[slot, g], held.at[slot, g], held_sem.at[slot]).wait()
         for k in range(count):
-            block = tiles[slot, k * rows : (k + 1) * rows, :]
+            block = work[k * rows : (k + 1) * rows, :]
             for g in range(groups):
                 total[g, k * rows : (k + 1) * rows, :] += jnp.dot(
                     block, held[slot, g], preferred_element_type=jnp.float32
                 )
-        return after_used, after_started
-
-    lax.fori_loop(0, steps, one_step, (first_used, first_started))
+        return nothing
+
+    lax.fori_loop(0, steps, one_step, 0)
     for k in range(count):
         place = pl.ds(pl.multiple_of(info[2 + k], rows), rows)
         for g in range(groups):
             out[g, :, place] = total[g, k * rows : (k + 1) * rows, :].T
 
 
+def places_of(mask, slots):
+    steps = mask.shape[1] // STRIDE
+    there = mask.T.reshape(steps, -1)
+    size = there.shape[1]
+    if slots is None:
+        return there - 1, jnp.zeros((steps,), jnp.int32)
+    before = jnp.cumsum(there.reshape(-1)).reshape(steps, size) - there
+    first = jnp.minimum(before[:, 0], slots - size)
+    found = jnp.where((there != 0) & (before < slots), before - first[:, None], -1)
+    return found, first
+
+
 def product(sources, masks, planes, inner, base, places):
     row_blocks, columns = masks[0].shape
-    packed = [v.ndim == 3 for v in sources]
-    blk = next(v.shape[1] if p else v.shape[0] // row_blocks for v, p in zip(sources, packed))
+    slots = [v.shape[0] if v.ndim == 3 else None for v in sources]
+    blk = next(v.shape[1] if n is not None else v.shape[0] // row_blocks for v, n in zip(sources, slots))
     rows = row_blocks * blk
     wide = planes[0][0].shape[1]
     dtype = sources[0].dtype
     head = [jnp.asarray(v, jnp.int32).reshape(1) for v in [inner, base] + list(places)]
-    info = jnp.concatenate(head + [m.T.reshape(-1) for m in masks])
+    found, first = zip(*[places_of(m, n) for m, n in zip(masks, slots)])
+    info = jnp.concatenate(head + [v.reshape(-1) for v in found] + list(first)).astype(jnp.int32)
     flat = [v for choice in planes for v in choice]
     shape = (len(planes), wide, len(sources) * rows)
     flops = 2 * shape[0] * shape[1] * shape[2] * columns * blk
-    size = columns * blk * (wide * len(planes) + rows * len(sources) // 2) * 2
+    size = columns * blk * (wide * len(planes) + rows * len(sources)) * 2
+    lists = max(1, sum(n is not None for n in slots))
     return pl.pallas_call(
         functools.partial(
-            product_kernel, blk, row_blocks, columns // STRIDE,
-            [v.shape[0] if p else None for v, p in zip(sources, packed)],
-            [len(choice) - 1 for choice in planes],
+            product_kernel, blk, row_blocks, columns // STRIDE, slots, [len(choice) - 1 for choice in planes]
         ),
         out_shape=jax.ShapeDtypeStruct(shape, jnp.float32),
         in_specs=[pl.BlockSpec(memory_space=pltpu.SMEM)]
@@ -193,12 +192,14 @@
         out_specs=pl.BlockSpec(memory_space=pltpu.VMEM),
         scratch_shapes=[
             pltpu.VMEM((len(planes), len(sources) * rows, wide), jnp.float32),
-            pltpu.VMEM((2, len(sources) * rows, STRIDE * blk), dtype),
+            pltpu.VMEM((len(sources) * rows, STRIDE * blk), dtype),
+            pltpu.VMEM((2, rows, STRIDE * blk), dtype),
+            pltpu.VMEM((2, lists, STRIDE * row_blocks, blk, blk), dtype),
             pltpu.VMEM((2, len(planes), STRIDE * blk, wide), dtype),
-            pltpu.SemaphoreType.DMA((2,)),
+            pltpu.SemaphoreType.DMA((2, len(sources))),
             pltpu.SemaphoreType.DMA((2,)),
         ],
-        compiler_params=params(vmem_limit_bytes=32 << 20),
+        compiler_params=params(vmem_limit_bytes=48 << 20),
         cost_estimate=pl.CostEstimate(flops=flops, bytes_accessed=size, transcendentals=0),
         name="tiles_times_planes",
     )(info, *sources, *flat)
@@ -280,15 +281,6 @@
         return self.arrived
 
 
-def along_line(block, inner):
-    near = lax.ppermute(block, "z", NEAR)
-    middle = lax.ppermute(block, "z", MIDDLE)
-    far = lax.ppermute(near, "z", MIDDLE)
-    out1 = lax.ppermute(middle, "z", OUTWARD)
-    out2 = lax.ppermute(far, "z", OUTWARD)
-    return [block, near, jnp.where(inner, middle, out1), jnp.where(inner, far, out2)]
-
-
 def dense(hist, tile_mask, planes, pairs):
     sess, act = ("z", "x"), ("y", "core")
     rows, acts = hist.shape
@@ -367,69 +359,86 @@
     known = [both_of(x)] + [lax.ppermute(both_of(o), "x", r) for o, r in zip(others, row_routes)]
     listed = [pairs] + [lax.ppermute(pairs, "x", route) for route in row_routes]
     masks, guest_masks = [m[0] for m in known], [m[1][:, kept:] for m in known]
-    groups = []
+    ends, middle = Lane(), Lane()
+    near, mid, far, groups = [], [], [], []
     for c in range(3):
+        if c == 2:
+            over_x.arrived = over_x.arrived + near[:1]
         got = over_x.send([planes_of(o, c) for o in others], "x", row_routes)
         groups.append(in_row_order([planes_of(x, c)] + got, 1))
         if c == 0:
             over_x.arrived = got + known[1:] + listed[1:]
+        if c < 2:
+            near += ends.send([groups[c]], "z", [NEAR])
+            mid += middle.send([groups[c]], "z", [MIDDLE])
     tiles = [None] * 3
     for c in (0, 2, 1):
         tiles[c] = over_x.send([packed(o, c, groups[0]) for o in others], "x", row_routes)
 
-    ends, middle = Lane(), Lane()
-    near, mid, far = [], [], []
-    for c in range(2):
-        near += ends.send([groups[c]], "z", [NEAR])
-        mid += middle.send([groups[c]], "z", [MIDDLE])
     inward, outward = Lane(near[1:]), Lane(near[1:])
-    for c in range(2):
-        far += middle.send([near[c]], "z", [MIDDLE])
+    middle.arrived = mid[1:] + near[1:]
+    far += middle.send([near[0]], "z", [MIDDLE])
+    outer = outward.send([mid[0]], "z", [OUTWARD])
+    middle.arrived = far + outer
+    far += middle.send([near[1]], "z", [MIDDLE])
+    outer += outward.send([mid[1]], "z", [OUTWARD])
+    middle.arrived = far[1:] + outer[1:]
+    near += inward.send([groups[2]], "z", [INWARD])
     loans = inward.send([packed(x, 2, near[0])], "z", [INWARD])
-    near += inward.send([groups[2]], "z", [INWARD])
+    far += middle.send([near[2]], "z", [MIDDLE])
     mid += middle.send([groups[2]], "z", [MIDDLE])
-    far += middle.send([near[2]], "z", [MIDDLE])
-    outer = [outward.send([v], "z", [OUTWARD])[0] for v in (mid[0], mid[1], far[1], far[0])]
-    loans = loans + inward.send(tiles[2], "z", [INWARD] * len(others))
+
     over = jnp.int32(0)
     for c in range(3):
         for owner in range(wide):
             count = jnp.sum(tile_mask[:, owner * columns + cuts[c] : owner * columns + cuts[c + 1]])
             over = jnp.maximum(over, (count > slots[c]).astype(jnp.int32))
     row_places = [(x - k) % wide * rows for k in range(wide)]
-    early_groups = [[[groups[c]], [near[c]], [mid[c], outer[c]]] for c in range(2)]
-    last_group = [[[far[c], outer[3 - c]]] for c in range(2)]
+    every = range(wide)
 
     def times(c, sources, which, held, places):
         own = [masks[k][:, cuts[c] : cuts[c + 1]] for k in which]
         return product(sources, own, held, inner, x * columns + cuts[c], places)
 
-    every = range(wide)
+    early_groups = [[[groups[c]], [near[c]], [mid[c], outer[c]]] for c in range(2)]
     part0 = times(0, [hist] + tiles[0], every, early_groups[0], row_places)
-    part2 = times(2, [hist] + tiles[2], every, [[groups[2]], [near[2]], [mid[2]], [far[2]]], row_places)
-    part1 = [times(1, [([hist] + tiles[1])[k]], [k], early_groups[1], [0]) for k in every]
-    first_three = part0 + part2[:3] + in_row_order(part1, 2)
-    end1 = times(1, [hist] + tiles[1], every, last_group[1], row_places)
-    end0 = times(0, [hist] + tiles[0], every, last_group[0], row_places)
-    last_one = end0 + (end1 + part2[3:])
-    visitors = in_row_order(
-        [
-            product([t], [m], [[groups[2]], [mid[2]], [far[2]]], inner, 0, [0])
-            for t, m in zip(loans, guest_masks)
-        ],
-        2,
-    )
-
-    def summed(totals):
-        return scatter_sum(scatter_sum(scatter_sum(totals, "core", 1), "x", 1), "y", 1)
-
-    first_three = summed(first_three)
-    visitors = lax.ppermute(summed(visitors), "z", OUTWARD)
-    early = first_three.at[1:].add(visitors[:2])
-    early = jnp.stack(along_line(early, inner))
-    last_one = summed(last_one)[0] + visitors[2]
-    flags = jnp.full((8, last_one.shape[1]), over.astype(jnp.float32))
-    late = jnp.stack(along_line(jnp.concatenate([last_one, flags]), inner))
+    loans += inward.send([after(t, part0) for t in tiles[2]], "z", [INWARD] * len(others))
+    outer += outward.send([far[1]], "z", [OUTWARD])
+    part1 = [times(1, [hist], [0], early_groups[1], [0])]
+    part2 = times(2, [hist] + tiles[2], every, [[groups[2]], [near[2]]], row_places)
+    end2 = times(2, [hist] + tiles[2], every, [[far[2]]], row_places)
+    outer += outward.send([after(far[0], [part1, part2, end2])], "z", [OUTWARD])
+    part1 += [times(1, [tiles[1][k - 1]], [k], early_groups[1], [0]) for k in range(1, wide)]
+    end1 = times(1, [hist] + tiles[1], every, [[far[1], outer[2]]], row_places)
+    guests = in_row_order(
+        [product([t], [m], [[groups[2]], [far[2]]], inner, 0, [0]) for t, m in zip(loans, guest_masks)], 2
+    )
+    part2 = jnp.concatenate([part2, times(2, [hist] + tiles[2], every, [[mid[2]]], row_places)])
+    first_three = part0 + part2 + in_row_order(part1, 2)
+    guests_mid = product(loans, guest_masks, [[mid[2]]], inner, 0, row_places)
+    end0 = times(0, [hist] + tiles[0], every, [[far[0], outer[3]]], row_places)
+    last_one = end0 + (end1 + end2)
+    visitors = jnp.concatenate([guests[:1], guests_mid, guests[1:]])
+
+    def summed(share):
+        return scatter_sum(scatter_sum(scatter_sum(share, "core", 1), "x", 1), "y", 1)
+
+    first_three, visitors, last_one = summed(first_three), summed(visitors), summed(last_one)
+
+    def all_along_line(share, extra):
+        near = lax.ppermute(share, "z", NEAR) + extra
+        mid = lax.ppermute(share, "z", MIDDLE)
+        far = lax.ppermute(near, "z", MIDDLE)
+        out1 = lax.ppermute(mid, "z", OUTWARD)
+        out2 = lax.ppermute(far, "z", OUTWARD)
+        own = share + lax.ppermute(extra, "z", OUTWARD)
+        return jnp.stack([own, near, jnp.where(inner, mid, out1), jnp.where(inner, far, out2)])
+
+    early = all_along_line(first_three, jnp.concatenate([jnp.zeros_like(visitors[:1]), visitors[:2]]))
+    flags = jnp.full((8, last_one.shape[2]), over.astype(jnp.float32))
+    late = all_along_line(
+        jnp.concatenate([last_one[0], flags]), jnp.concatenate([visitors[2], jnp.zeros_like(flags)])
+    )
 
     order = (x - jnp.arange(wide)) % wide
     all_pairs = jnp.stack(listed)[order].reshape(-1, 2).T

time: 629 us -> 624 us (level); the launches traced: 627 us -> 615 us
  waiting for transfers between devices: 345 us -> 321 us
  Pallas kernels: 133 us -> 145 us
    ppermute x21, waiting for transfers between devices: 225 us -> 200 us  [send(): lax.ppermute(v, axis, route)]
    ppermute x1, waiting for transfers between devices: 19.4 us -> 0.01 us  [body(): lax.ppermute(both_of(o), 'x', r)]
    ppermute x1, waiting for transfers between devices: 0.01 us -> 16.3 us  [body(): listed = [pairs] + [lax.ppermute(pairs, 'x', route) for route in row_routes]]
    pallas_call x8 -> x11, Pallas kernels: 106 us -> 118 us  [product(): pl.pallas_call(functools.partial(product_kernel, blk, row_blocks, columns...]
    ppermute x11 -> x12, waiting for transfers between devices: 43.2 us -> 47.9 us  [the longest x2 18.4 us: all_along_line(): own = share + lax.ppermute(extra, 'z', OUTWARD)]
    ppermute x11 -> x12, starting transfers between devices: 12.6 us -> 12.8 us  [the longest x2 2.58 us: all_along_line(): own = share + lax.ppermute(extra, 'z', OUTWARD)]
  transfers between devices with their start and end apart: 47 -> 48, of which waited for: 24 -> 23; matrix products, arithmetic and copies ran while one was open for 7% -> 7% of each run, Pallas kernels for 20% -> 22%
where the time goes in v10:
time: 624 us; the launch traced here: 615 us
  waiting for transfers between devices  321 us (51%)
  Pallas kernels  145 us (23%)
  starting transfers between devices  77.9 us (12%)
  other arithmetic  28.7 us (5%)
  local copies, waits for them, and re-layouts  22.8 us (4%)
  between operations  19.5 us (3%)
    ppermute x21, waiting for transfers between devices, send(): lax.ppermute(v, axis, route)  200 us
    pallas_call x11, Pallas kernels, product(): pl.pallas_call(functools.partial(product_kernel, blk, row_blocks, columns...  118 us
    ppermute x12, waiting for transfers between devices, scatter_sum(): total = total + lax.ppermute(part((here + k) % count), axis, turn(count, k))  56.6 us
    ppermute x21, starting transfers between devices, send(): lax.ppermute(v, axis, route)  52.1 us
    ppermute x2, waiting for transfers between devices, all_along_line(): own = share + lax.ppermute(extra, 'z', OUTWARD)  18.4 us
    pallas_call x4, Pallas kernels, pack(): pl.pallas_call(functools.partial(pack_kernel, blk, row_blocks, columns, s...  17.4 us
    ppermute x1, waiting for transfers between devices, body(): listed = [pairs] + [lax.ppermute(pairs, 'x', route) for route in row_routes]  16.3 us
  transfers between devices with their start and end apart: 48, of which 23 were waited for; matrix products, arithmetic and copies ran while one was open for 7% of the time, Pallas kernels for 22%

profile of v10, /device:TPU:0, one launch (start us, length us, event | category | flops | bytes accessed | tf_op | source)
XLA Modules:
  0.0 614.6 jit_solution(8055304319480078568)
XLA Ops:
  6.5 2.3 constant_dynamic-slice_fusion.17
  8.8 2.9 collective-permute-start.3
  11.8 3.5 collective-permute-start.1
  17.4 1.6 constant_dynamic-slice_fusion.15
  19.0 16.3 %collective-permute-done = s32[16,2]{0,1:T(2,128)S(1)} collective-permute-done((s32[16,2]{0,1:T(2,128)S(1)}, s32[16,2]{0,1:T(2,128)S(1)}, u32[]{:S(2)}, u32[]{:S(2)}) %collective-permute-start) | collective-permute-done | bytes 160 | tf_op jit(solution)/shard_map/ppermute | solution.py:360
  35.3 1.8 collective-permute-start.4
  37.1 1.6 broadcast_select_fusion.5
  38.9 1.6 collective-permute-start.5
  40.6 2.0 collective-permute-start.8
  42.6 34.0 %collective-permute-done.4 = bf16[7168,128]{1,0:T(8,128)(2,1)} collective-permute-done((bf16[7168,128]{1,0:T(8,128)(2,1)S(1)}, bf16[7168,128]{1,0:T(8,128)(2,1)}, u32[]{:S(2)}, u32[]{:S(2)}) %collective-permute-start.4) | collective-permute-done | bytes 1835040 | tf_op jit(solution)/shard_map/ppermute | solution.py:280
  76.6 2.8 broadcast_select_fusion.1
  79.3 2.3 pad_maximum_fusion.refs_1_
  81.6 3.6 collective-permute-done.5.refs_3_
  85.3 1.6 collective-permute-start.9
  86.9 2.4 collective-permute-start.13
  91.6 3.9 pack_tiles.4
  95.4 23.9 %collective-permute-done.6 = bf16[5120,128]{1,0:T(8,128)(2,1)S(1)} collective-permute-done((bf16[5120,128]{1,0:T(8,128)(2,1)S(1)}, bf16[5120,128]{1,0:T(8,128)(2,1)S(1)}, u32[]{:S(2)}, u32[]{:S(2)}) %collective-permute-start.6) | collective-permute-done | bytes 1310752 | tf_op jit(solution)/shard_map/ppermute | solution.py:280
  122.1 42.4 %collective-permute-done.9.refs_2_ = bf16[7168,256]{1,0:T(8,128)(2,1)} collective-permute-done((bf16[7168,256]{1,0:T(8,128)(2,1)}, bf16[7168,256]{1,0:T(8,128)(2,1)}, u32[]{:S(2)}, u32[]{:S(2)}) %collective-permute-start.9) | collective-permute-done | bytes 3670048 | tf_op jit(solution)/shard_map/ppermute | solution.py:280
  165.8 2.0 collective-permute-start.14
  167.8 1.8 broadcast_select_fusion.3
  169.9 10.0 %collective-permute-start.12 = (bf16[5120,256]{1,0:T(8,128)(2,1)S(1)}, bf16[5120,256]{1,0:T(8,128)(2,1)}, u32[]{:S(2)}, u32[]{:S(2)}) collective-permute-start(bf16[5120,256]{1,0:T(8,128)(2,1)S(1)} %pad_maximum_fusion.1.refs_2_.refs_1_), channel_id=1, source_target_pairs={{0,8},{24,16},{1,9},{25,17},{2,10},{26,18},{3,11},{27,19},{4,12},{... | collective-permute-start | bytes 7864328 | tf_op jit(solution)/shard_map/ppermute | solution.py:280
  180.2 4.3 pack_tiles.5
  184.5 1.8 collective-permute-done.7.refs_1_
  188.0 23.1 %collective-permute-done.10.refs_5_ = bf16[4096,256]{1,0:T(8,128)(2,1)} collective-permute-done((bf16[4096,256]{1,0:T(8,128)(2,1)}, bf16[4096,256]{1,0:T(8,128)(2,1)}, u32[]{:S(2)}, u32[]{:S(2)}) %collective-permute-start.10) | collective-permute-done | bytes 2097184 | tf_op jit(solution)/shard_map/ppermute | solution.py:280
  211.0 2.5 collective-permute-start.15
  217.1 4.2 pack_tiles.7
  221.3 9.6 %collective-permute-done.12.refs_3_ = bf16[5120,256]{1,0:T(8,128)(2,1)} collective-permute-done((bf16[5120,256]{1,0:T(8,128)(2,1)S(1)}, bf16[5120,256]{1,0:T(8,128)(2,1)}, u32[]{:S(2)}, u32[]{:S(2)}) %collective-permute-start.12) | collective-permute-done | bytes 2621472 | tf_op jit(solution)/shard_map/ppermute | solution.py:280
  230.9 6.4 %collective-permute-start.23 = (bf16[112,128,128]{2,1,0:T(8,128)(2,1)}, bf16[112,128,128]{2,1,0:T(8,128)(2,1)}, u32[]{:S(2)}, u32[]{:S(2)}) collective-permute-start(bf16[112,128,128]{2,1,0:T(8,128)(2,1)} %pack_tiles.7), channel_id=1, source_target_pairs={{0,8},{24,16},{1,9},{25,17},{2,10},{26,18},{3,11},{27,19},{4,12},{... | collective-permute-start | bytes 11010056 | tf_op jit(solution)/shard_map/ppermute | solution.py:280
  240.2 5.0 pack_tiles.6
  245.2 20.5 %collective-permute-done.11.refs_1_ = bf16[112,128,128]{2,1,0:T(8,128)(2,1)} collective-permute-done((bf16[112,128,128]{2,1,0:T(8,128)(2,1)}, bf16[112,128,128]{2,1,0:T(8,128)(2,1)}, u32[]{:S(2)}, u32[]{:S(2)}) %collective-permute-start.11) | collective-permute-done | bytes 3670048 | tf_op jit(solution)/shard_map/ppermute | solution.py:280
  266.7 30.3 %collective-permute-done.16.refs_4_ = bf16[7168,256]{1,0:T(8,128)(2,1)} collective-permute-done((bf16[7168,256]{1,0:T(8,128)(2,1)}, bf16[7168,256]{1,0:T(8,128)(2,1)}, u32[]{:S(2)}, u32[]{:S(2)}) %collective-permute-start.16) | collective-permute-done | bytes 3670048 | tf_op jit(solution)/shard_map/ppermute | solution.py:280
  297.0 2.1 collective-permute-start.17
  301.8 1.6 copy-done.1
  303.4 14.7 %tiles_times_planes.11 = f32[3,256,1024]{2,1,0:T(8,128)} custom-call(s32[268]{0:T(512)S(1)} %concatenate.73.info, bf16[512,32768]{1,0:T(8,128)(2,1)} %refs_0_.13, bf16[94,128,128]{2,1,0:T(8,128)(2,1)} %collective-permute-done.7.refs_1_, bf16[4096,256]{1,0:T(8,128)(2,1)S(1)} %copy-done.1, bf16[4096,256]{1,0:T(8,128)(2,1)} %collective-permute-done.5.refs_3_, ...), custom_call_target="tpu_custom_call" | custom-call | flops 6442450944 | bytes 14680064 | tf_op jit(solution)/shard_map/tiles_times_planes/pallas_call | solution.py:185
  318.1 8.3 %collective-permute-start.24 = (bf16[112,128,128]{2,1,0:T(8,128)(2,1)}, bf16[112,128,128]{2,1,0:T(8,128)(2,1)}, u32[]{:S(2)}, u32[]{:S(2)}) collective-permute-start(bf16[112,128,128]{2,1,0:T(8,128)(2,1)} %collective-permute-done.11.refs_1_), channel_id=1, source_target_pairs={{0,8},{24,16},{1,9},{25,17},{2,10},{26,18},{3,11},{27,19},{4,12},{... | collective-permute-start | bytes 11010056 | tf_op jit(solution)/shard_map/ppermute | solution.py:280
  327.1 12.3 %tiles_times_planes.12 = f32[2,256,1024]{2,1,0:T(8,128)S(1)} custom-call(s32[334]{0:T(512)S(1)} %concatenate.77.info, bf16[512,32768]{1,0:T(8,128)(2,1)} %refs_0_.13, bf16[112,128,128]{2,1,0:T(8,128)(2,1)} %collective-permute-done.11.refs_1_, bf16[5120,256]{1,0:T(8,128)(2,1)S(1)} %pad_maximum_fusion.1.refs_2_.refs_1_, ...), custom_call_target="tpu_custom_call" | custom-call | flops 5368709120 | bytes 15728640 | tf_op jit(solution)/shard_map/tiles_times_planes/pallas_call | solution.py:185
  340.2 13.0 %tiles_times_planes.15 = f32[3,256,512]{2,1,0:T(8,128)S(1)} custom-call(s32[234]{0:T(256)S(1)} %concatenate.83.info, bf16[512,32768]{1,0:T(8,128)(2,1)} %refs_0_.13, bf16[7168,256]{1,0:T(8,128)(2,1)} %pad_maximum_fusion.refs_1_, bf16[7168,256]{1,0:T(8,128)(2,1)} %collective-permute-done.9.refs_2_, bf16[7168,256]{1,0:T(8,128)(2,1)} %collective-permute-done.13.refs_3_, ...), custom_call_target="tpu_custom_call" | custom-call | flops 5637144576 | bytes 18350080 | tf_op jit(solution)/shard_map/tiles_times_planes/pallas_call | solution.py:185
  353.3 9.2 %tiles_times_planes.19 = f32[1,256,1024]{2,1,0:T(8,128)S(1)} custom-call(s32[334]{0:T(512)S(1)} %concatenate.77.info, bf16[512,32768]{1,0:T(8,128)(2,1)} %refs_0_.13, bf16[112,128,128]{2,1,0:T(8,128)(2,1)} %collective-permute-done.11.refs_1_, bf16[5120,256]{1,0:T(8,128)(2,1)} %collective-permute-done.17.refs_2_), custom_call_target="tpu_custom_call" | custom-call | flops 2684354560 | bytes 13107200 | tf_op jit(solution)/shard_map/tiles_times_planes/pallas_call | solution.py:185
  363.6 8.4 %tiles_times_planes.17 = f32[2,256,512]{2,1,0:T(8,128)S(1)} custom-call(s32[168]{0:T(256)S(1)} %get-tuple-element.149.info, bf16[112,128,128]{2,1,0:T(8,128)(2,1)} %collective-permute-done.23.refs_0_, bf16[5120,256]{1,0:T(8,128)(2,1)S(1)} %pad_maximum_fusion.1.refs_2_.refs_1_, bf16[5120,256]{1,0:T(8,128)(2,1)} %collective-permute-done.17.refs_2_), custom_call_target="tpu_custom_call" | custom-call | flops 2684354560 | bytes 10485760 | tf_op jit(solution)/shard_map/tiles_times_planes/pallas_call | solution.py:185
  372.0 13.1 %tiles_times_planes.14 = f32[3,256,512]{2,1,0:T(8,128)S(1)} custom-call(s32[234]{0:T(256)S(1)} %concatenate.81.info, bf16[150,128,128]{2,1,0:T(8,128)(2,1)} %collective-permute-done.19.refs_0_.refs_1_, bf16[7168,256]{1,0:T(8,128)(2,1)} %pad_maximum_fusion.refs_1_, bf16[7168,256]{1,0:T(8,128)(2,1)} %collective-permute-done.9.refs_2_, ...), custom_call_target="tpu_custom_call" | custom-call | flops 5637144576 | bytes 18350080 | tf_op jit(solution)/shard_map/tiles_times_planes/pallas_call | solution.py:185
  385.1 2.0 broadcast_select_fusion.7
  388.6 12.1 %tiles_times_planes.21 = f32[1,256,1024]{2,1,0:T(8,128)S(1)} custom-call(s32[466]{0:T(512)S(1)} %concatenate.92.info, bf16[512,32768]{1,0:T(8,128)(2,1)} %refs_0_.13, bf16[150,128,128]{2,1,0:T(8,128)(2,1)} %collective-permute-done.19.refs_0_.refs_1_, bf16[7168,256]{1,0:T(8,128)(2,1)} %collective-permute-done.15.refs_2_, ...), custom_call_target="tpu_custom_call" | custom-call | flops 3758096384 | bytes 18350080 | tf_op jit(solution)/shard_map/tiles_times_planes/pallas_call | solution.py:185
  400.7 8.4 %tiles_times_planes.16 = f32[2,256,512]{2,1,0:T(8,128)S(1)} custom-call(s32[168]{0:T(256)S(1)} %get-tuple-element.150.info, bf16[112,128,128]{2,1,0:T(8,128)(2,1)} %collective-permute-done.24.refs_0_.refs_1_, bf16[5120,256]{1,0:T(8,128)(2,1)S(1)} %pad_maximum_fusion.1.refs_2_.refs_1_, bf16[5120,256]{1,0:T(8,128)(2,1)} %collective-permute-done.17.refs_2_), custom_call_target="tpu_custom_call" | custom-call | flops 2684354560 | bytes 10485760 | tf_op jit(solution)/shard_map/tiles_times_planes/pallas_call | solution.py:185
  409.5 9.5 %tiles_times_planes.18 = f32[1,256,1024]{2,1,0:T(8,128)S(1)} custom-call(s32[334]{0:T(512)S(1)} %concatenate.89.info, bf16[112,128,128]{2,1,0:T(8,128)(2,1)} %collective-permute-done.23.refs_0_, bf16[112,128,128]{2,1,0:T(8,128)(2,1)} %collective-permute-done.24.refs_0_.refs_1_, bf16[5120,256]{1,0:T(8,128)(2,1)S(1)} %collective-permute-done.18.refs_2_), custom_call_target="tpu_custom_call" | custom-call | flops 2684354560 | bytes 13107200 | tf_op jit(solution)/shard_map/tiles_times_planes/pallas_call | solution.py:185
  420.8 9.5 %tiles_times_planes.13 = f32[1,256,1024]{2,1,0:T(8,128)S(1)} custom-call(s32[334]{0:T(512)S(1)} %concatenate.77.info, bf16[512,32768]{1,0:T(8,128)(2,1)} %refs_0_.13, bf16[112,128,128]{2,1,0:T(8,128)(2,1)} %collective-permute-done.11.refs_1_, bf16[5120,256]{1,0:T(8,128)(2,1)S(1)} %collective-permute-done.18.refs_2_), custom_call_target="tpu_custom_call" | custom-call | flops 2684354560 | bytes 13107200 | tf_op jit(solution)/shard_map/tiles_times_planes/pallas_call | solution.py:185
  433.5 10.2 %collective-permute-done.35.refs_3_ = bf16[4096,256]{1,0:T(8,128)(2,1)} collective-permute-done((bf16[4096,256]{1,0:T(8,128)(2,1)}, bf16[4096,256]{1,0:T(8,128)(2,1)}, u32[]{:S(2)}, u32[]{:S(2)}) %collective-permute-start.35) | collective-permute-done | bytes 2097184 | tf_op jit(solution)/shard_map/ppermute | solution.py:280
  443.7 7.8 %tiles_times_planes.20 = f32[1,256,1024]{2,1,0:T(8,128)S(1)} custom-call(s32[268]{0:T(512)S(1)} %concatenate.73.info, bf16[512,32768]{1,0:T(8,128)(2,1)} %refs_0_.13, bf16[94,128,128]{2,1,0:T(8,128)(2,1)} %collective-permute-done.7.refs_1_, bf16[4096,256]{1,0:T(8,128)(2,1)} %collective-permute-done.14.refs_2_, bf16[4096,256]{1,0:T(8,128)(2,1)} %collective-permute-done.35.refs_3_), custom_call_target="tpu_custom_call" | custom-call | flops 2147483648 | bytes 10485760 | tf_op jit(solution)/shard_map/tiles_times_planes/pallas_call | solution.py:185
  456.5 2.4 dynamic-slice_add_fusion
  462.0 1.7 dynamic-slice_add_fusion.1
  465.8 20.3 %collective-permute-done.37 = f32[1,64,1024]{2,1,0:T(8,128)} collective-permute-done((f32[1,64,1024]{2,1,0:T(8,128)S(1)}, f32[1,64,1024]{2,1,0:T(8,128)}, u32[]{:S(2)}, u32[]{:S(2)}) %collective-permute-start.37) | collective-permute-done | bytes 262176 | tf_op jit(solution)/shard_map/ppermute | solution.py:265
  488.5 1.6 collective-permute-start.27
  490.7 11.9 %collective-permute-done.21 = f32[3,64,1024]{2,1,0:T(8,128)} collective-permute-done((f32[3,64,1024]{2,1,0:T(8,128)}, f32[3,64,1024]{2,1,0:T(8,128)}, u32[]{:S(2)}, u32[]{:S(2)}) %collective-permute-start.21) | collective-permute-done | bytes 786464 | tf_op jit(solution)/shard_map/ppermute | solution.py:265
  503.9 1.6 collective-permute-start.22
  508.3 18.4 %collective-permute-done.39 = f32[40,1024]{1,0:T(8,128)S(1)} collective-permute-done((f32[40,1024]{1,0:T(8,128)S(1)}, f32[40,1024]{1,0:T(8,128)S(1)}, u32[]{:S(2)}, u32[]{:S(2)}) %collective-permute-start.39) | collective-permute-done | bytes 163872 | tf_op jit(solution)/shard_map/ppermute | solution.py:434
  526.8 2.1 collective-permute-start.29
  529.7 4.2 collective-permute-done.40
  536.8 4.8 collective-permute-done.29
  547.9 5.4 collective-permute-done.44
  553.3 10.3 %collective-permute-done.31 = f32[3,32,1024]{2,1,0:T(8,128)S(1)} collective-permute-done((f32[3,32,1024]{2,1,0:T(8,128)S(1)}, f32[3,32,1024]{2,1,0:T(8,128)S(1)}, u32[]{:S(2)}, u32[]{:S(2)}) %collective-permute-start.31) | collective-permute-done | bytes 393248 | tf_op jit(solution)/shard_map/ppermute | solution.py:432
  563.7 4.8 collective-permute-done.33
  568.7 9.3 %pair_dots.1 = f32[32,136,128]{2,1,0:T(8,128)S(1)} custom-call(s32[2,6,32]{2,1,0:T(8,128)S(1)} %pad_add_fusion.1.ids, f32[4,3,32,1024]{3,2,1,0:T(8,128)S(1)} %pad_maximum_fusion.3.early, f32[4,40,1024]{2,1,0:T(8,128)S(1)} %pad_maximum_fusion.4.late), custom_call_target="tpu_custom_call" | custom-call | tf_op jit(solution)/shard_map/pair_dots/pallas_call | solution.py:241
  578.2 2.9 collective-permute-done.45
  583.1 14.1 %collective-permute-done.46 = f32[1,2,1,4,136,128]{5,4,3,2,1,0:T(8,128)S(1)} collective-permute-done((f32[1,2,1,4,136,128]{5,4,3,2,1,0:T(8,128)S(1)}, f32[1,2,1,4,136,128]{5,4,3,2,1,0:T(8,128)S(1)}, u32[]{:S(2)}, u32[]{:S(2)}) %collective-permute-start.46) | collective-permute-done | bytes 557088 | tf_op jit(solution)/shard_map/ppermute | solution.py:265
  597.9 7.4 %collective-permute-done.47 = f32[1,1,1,4,136,128]{5,4,3,2,1,0:T(8,128)S(1)} collective-permute-done((f32[1,1,1,4,136,128]{5,4,3,2,1,0:T(8,128)S(1)}, f32[1,1,1,4,136,128]{5,4,3,2,1,0:T(8,128)S(1)}, u32[]{:S(2)}, u32[]{:S(2)}) %collective-permute-start.47) | collective-permute-done | bytes 278560 | tf_op jit(solution)/shard_map/ppermute | solution.py:265
  (282 shorter events, 57.8 us)
Async XLA Ops:
  6.5 5.2 copy-start.16
  6.5 8.7 %copy-start.17 = (s32[16,2]{0,1:T(2,128)S(1)}, s32[16,2]{0,1:T(2,128)}, u32[]{:S(2)}) copy-start(s32[16,2]{0,1:T(2,128)} %param.10) | copy-start | bytes 388
  8.8 26.4 %collective-permute-start.3 = (bf16[4096,128]{1,0:T(8,128)(2,1)}, bf16[4096,128]{1,0:T(8,128)(2,1)S(1)}, u32[]{:S(2)}, u32[]{:S(2)}) collective-permute-start(bf16[4096,128]{1,0:T(8,128)(2,1)} %constant_dynamic-slice_fusion.17), channel_id=1, source_target_pairs={{0,4},{4,0},{1,5},{5,1},{2,6},{6,2},{3,7},{7,3},{8,12},{12,8},{9,1... | collective-permute-start | bytes 3145736 | tf_op jit(solution)/shard_map/ppermute | solution.py:280
  11.8 4.8 collective-permute-start.1
  15.3 20.0 %collective-permute-start = (s32[16,2]{0,1:T(2,128)S(1)}, s32[16,2]{0,1:T(2,128)S(1)}, u32[]{:S(2)}, u32[]{:S(2)}) collective-permute-start(s32[16,2]{0,1:T(2,128)S(1)} %copy-done.17), channel_id=1, source_target_pairs={{0,4},{4,0},{1,5},{5,1},{2,6},{6,2},{3,7},{7,3},{8,12},{12,8},{9,1... | collective-permute-start | bytes 392 | tf_op jit(solution)/shard_map/ppermute | solution.py:360
  16.6 18.7 %collective-permute-start.2 = (s32[2,4,128]{2,1,0:T(4,128)S(1)}, s32[2,4,128]{2,1,0:T(4,128)S(1)}, u32[]{:S(2)}, u32[]{:S(2)}) collective-permute-start(s32[2,4,128]{2,1,0:T(4,128)S(1)} %get-tuple-element.138), channel_id=1, source_target_pairs={{0,4},{4,0},{1,5},{5,1},{2,6},{6,2},{3,7},{7,3},{8,12},{12,8},{9,1... | collective-permute-start | bytes 12296 | tf_op jit(solution)/shard_map/ppermute | solution.py:359
  35.3 41.3 %collective-permute-start.4 = (bf16[7168,128]{1,0:T(8,128)(2,1)S(1)}, bf16[7168,128]{1,0:T(8,128)(2,1)}, u32[]{:S(2)}, u32[]{:S(2)}) collective-permute-start(bf16[7168,128]{1,0:T(8,128)(2,1)S(1)} %constant_dynamic-slice_fusion.15), channel_id=1, source_target_pairs={{0,4},{4,0},{1,5},{5,1},{2,6},{6,2},{3,7},{7,3},{8,12},{12,8},{9,1... | collective-permute-start | bytes 5505032 | tf_op jit(solution)/shard_map/ppermute | solution.py:280
  38.9 40.4 %copy-start = (bf16[4096,256]{1,0:T(8,128)(2,1)}, bf16[4096,256]{1,0:T(8,128)(2,1)S(1)}, u32[]{:S(2)}) copy-start(bf16[4096,256]{1,0:T(8,128)(2,1)S(1)} %pad_maximum_fusion.2.refs_2_) | copy-start | bytes 6291460
  38.9 46.3 %collective-permute-start.5 = (bf16[4096,256]{1,0:T(8,128)(2,1)S(1)}, bf16[4096,256]{1,0:T(8,128)(2,1)}, u32[]{:S(2)}, u32[]{:S(2)}) collective-permute-start(bf16[4096,256]{1,0:T(8,128)(2,1)S(1)} %pad_maximum_fusion.2.refs_2_), channel_id=1, source_target_pairs={{0,8},{8,0},{16,24},{24,16},{1,9},{9,1},{17,25},{25,17},{2,10},{10... | collective-permute-start | bytes 6291464 | tf_op jit(solution)/shard_map/ppermute | solution.py:280
  40.6 46.3 %collective-permute-start.8 = (bf16[4096,256]{1,0:T(8,128)(2,1)S(1)}, bf16[4096,256]{1,0:T(8,128)(2,1)}, u32[]{:S(2)}, u32[]{:S(2)}) collective-permute-start(bf16[4096,256]{1,0:T(8,128)(2,1)S(1)} %pad_maximum_fusion.2.refs_2_), channel_id=1, source_target_pairs={{8,16},{16,8},{9,17},{17,9},{10,18},{18,10},{11,19},{19,11},{12,20... | collective-permute-start | bytes 6291464 | tf_op jit(solution)/shard_map/ppermute | solution.py:280
  85.3 79.3 %collective-permute-start.9 = (bf16[7168,256]{1,0:T(8,128)(2,1)}, bf16[7168,256]{1,0:T(8,128)(2,1)}, u32[]{:S(2)}, u32[]{:S(2)}) collective-permute-start(bf16[7168,256]{1,0:T(8,128)(2,1)} %pad_maximum_fusion.refs_1_), channel_id=1, source_target_pairs={{0,8},{8,0},{16,24},{24,16},{1,9},{9,1},{17,25},{25,17},{2,10},{10... | collective-permute-start | bytes 11010056 | tf_op jit(solution)/shard_map/ppermute | solution.py:280
  86.9 79.0 %collective-permute-start.13 = (bf16[7168,256]{1,0:T(8,128)(2,1)}, bf16[7168,256]{1,0:T(8,128)(2,1)}, u32[]{:S(2)}, u32[]{:S(2)}) collective-permute-start(bf16[7168,256]{1,0:T(8,128)(2,1)} %pad_maximum_fusion.refs_1_), channel_id=1, source_target_pairs={{8,16},{16,8},{9,17},{17,9},{10,18},{18,10},{11,19},{19,11},{12,20... | collective-permute-start | bytes 11010056 | tf_op jit(solution)/shard_map/ppermute | solution.py:280
  90.7 28.7 %collective-permute-start.6 = (bf16[5120,128]{1,0:T(8,128)(2,1)S(1)}, bf16[5120,128]{1,0:T(8,128)(2,1)S(1)}, u32[]{:S(2)}, u32[]{:S(2)}) collective-permute-start(bf16[5120,128]{1,0:T(8,128)(2,1)S(1)} %constant_dynamic-slice_fusion.16), channel_id=1, source_target_pairs={{0,4},{4,0},{1,5},{5,1},{2,6},{6,2},{3,7},{7,3},{8,12},{12,8},{9,1... | collective-permute-start | bytes 3932168 | tf_op jit(solution)/shard_map/ppermute | solution.py:280
  119.4 66.9 %collective-permute-start.7 = (bf16[94,128,128]{2,1,0:T(8,128)(2,1)}, bf16[94,128,128]{2,1,0:T(8,128)(2,1)}, u32[]{:S(2)}, u32[]{:S(2)}) collective-permute-start(bf16[94,128,128]{2,1,0:T(8,128)(2,1)} %pack_tiles.4), channel_id=1, source_target_pairs={{0,4},{4,0},{1,5},{5,1},{2,6},{6,2},{3,7},{7,3},{8,12},{12,8},{9,1... | collective-permute-start | bytes 9240584 | tf_op jit(solution)/shard_map/ppermute | solution.py:280
  164.5 46.5 %collective-permute-start.10 = (bf16[4096,256]{1,0:T(8,128)(2,1)}, bf16[4096,256]{1,0:T(8,128)(2,1)}, u32[]{:S(2)}, u32[]{:S(2)}) collective-permute-start(bf16[4096,256]{1,0:T(8,128)(2,1)} %collective-permute-done.8.refs_4_), channel_id=1, source_target_pairs={{8,0},{16,24},{9,1},{17,25},{10,2},{18,26},{11,3},{19,27},{12,4},{... | collective-permute-start | bytes 6291464 | tf_op jit(solution)/shard_map/ppermute | solution.py:280
  165.8 45.2 %collective-permute-start.14 = (bf16[4096,256]{1,0:T(8,128)(2,1)}, bf16[4096,256]{1,0:T(8,128)(2,1)}, u32[]{:S(2)}, u32[]{:S(2)}) collective-permute-start(bf16[4096,256]{1,0:T(8,128)(2,1)} %collective-permute-done.5.refs_3_), channel_id=1, source_target_pairs={{8,16},{16,8},{9,17},{17,9},{10,18},{18,10},{11,19},{19,11},{12,20... | collective-permute-start | bytes 6291464 | tf_op jit(solution)/shard_map/ppermute | solution.py:280
  169.9 61.0 %collective-permute-start.12 = (bf16[5120,256]{1,0:T(8,128)(2,1)S(1)}, bf16[5120,256]{1,0:T(8,128)(2,1)}, u32[]{:S(2)}, u32[]{:S(2)}) collective-permute-start(bf16[5120,256]{1,0:T(8,128)(2,1)S(1)} %pad_maximum_fusion.1.refs_2_.refs_1_), channel_id=1, source_target_pairs={{0,8},{24,16},{1,9},{25,17},{2,10},{26,18},{3,11},{27,19},{4,12},{... | collective-permute-start | bytes 7864328 | tf_op jit(solution)/shard_map/ppermute | solution.py:280
  186.2 79.5 %collective-permute-start.11 = (bf16[112,128,128]{2,1,0:T(8,128)(2,1)}, bf16[112,128,128]{2,1,0:T(8,128)(2,1)}, u32[]{:S(2)}, u32[]{:S(2)}) collective-permute-start(bf16[112,128,128]{2,1,0:T(8,128)(2,1)} %pack_tiles.5), channel_id=1, source_target_pairs={{0,4},{4,0},{1,5},{5,1},{2,6},{6,2},{3,7},{7,3},{8,12},{12,8},{9,1... | collective-permute-start | bytes 11010056 | tf_op jit(solution)/shard_map/ppermute | solution.py:280
  211.0 55.6 %collective-permute-start.15 = (bf16[7168,256]{1,0:T(8,128)(2,1)}, bf16[7168,256]{1,0:T(8,128)(2,1)}, u32[]{:S(2)}, u32[]{:S(2)}) collective-permute-start(bf16[7168,256]{1,0:T(8,128)(2,1)} %collective-permute-done.9.refs_2_), channel_id=1, source_target_pairs={{8,16},{16,8},{9,17},{17,9},{10,18},{18,10},{11,19},{19,11},{12,20... | collective-permute-start | bytes 11010056 | tf_op jit(solution)/shard_map/ppermute | solution.py:280
  213.6 83.4 %collective-permute-start.16 = (bf16[7168,256]{1,0:T(8,128)(2,1)}, bf16[7168,256]{1,0:T(8,128)(2,1)}, u32[]{:S(2)}, u32[]{:S(2)}) collective-permute-start(bf16[7168,256]{1,0:T(8,128)(2,1)} %collective-permute-done.13.refs_3_), channel_id=1, source_target_pairs={{8,0},{16,24},{9,1},{17,25},{10,2},{18,26},{11,3},{19,27},{12,4},{... | collective-permute-start | bytes 11010056 | tf_op jit(solution)/shard_map/ppermute | solution.py:280
  230.9 87.2 %collective-permute-start.23 = (bf16[112,128,128]{2,1,0:T(8,128)(2,1)}, bf16[112,128,128]{2,1,0:T(8,128)(2,1)}, u32[]{:S(2)}, u32[]{:S(2)}) collective-permute-start(bf16[112,128,128]{2,1,0:T(8,128)(2,1)} %pack_tiles.7), channel_id=1, source_target_pairs={{0,8},{24,16},{1,9},{25,17},{2,10},{26,18},{3,11},{27,19},{4,12},{... | collective-permute-start | bytes 11010056 | tf_op jit(solution)/shard_map/ppermute | solution.py:280
  265.7 106.2 %collective-permute-start.19 = (bf16[150,128,128]{2,1,0:T(8,128)(2,1)}, bf16[150,128,128]{2,1,0:T(8,128)(2,1)}, u32[]{:S(2)}, u32[]{:S(2)}) collective-permute-start(bf16[150,128,128]{2,1,0:T(8,128)(2,1)} %pack_tiles.6), channel_id=1, source_target_pairs={{0,4},{4,0},{1,5},{5,1},{2,6},{6,2},{3,7},{7,3},{8,12},{12,8},{9,1... | collective-permute-start | bytes 14745608 | tf_op jit(solution)/shard_map/ppermute | solution.py:280
  297.0 42.4 %collective-permute-start.17 = (bf16[5120,256]{1,0:T(8,128)(2,1)}, bf16[5120,256]{1,0:T(8,128)(2,1)}, u32[]{:S(2)}, u32[]{:S(2)}) collective-permute-start(bf16[5120,256]{1,0:T(8,128)(2,1)} %collective-permute-done.12.refs_3_), channel_id=1, source_target_pairs={{8,16},{16,8},{9,17},{17,9},{10,18},{18,10},{11,19},{19,11},{12,20... | collective-permute-start | bytes 7864328 | tf_op jit(solution)/shard_map/ppermute | solution.py:280
  300.5 86.6 %collective-permute-start.34 = (bf16[7168,256]{1,0:T(8,128)(2,1)}, bf16[7168,256]{1,0:T(8,128)(2,1)}, u32[]{:S(2)}, u32[]{:S(2)}) collective-permute-start(bf16[7168,256]{1,0:T(8,128)(2,1)} %collective-permute-done.15.refs_2_), channel_id=1, source_target_pairs={{8,0},{16,24},{9,1},{17,25},{10,2},{18,26},{11,3},{19,27},{12,4},{... | collective-permute-start | bytes 11010056 | tf_op jit(solution)/shard_map/ppermute | solution.py:280
  318.1 82.6 %collective-permute-start.24 = (bf16[112,128,128]{2,1,0:T(8,128)(2,1)}, bf16[112,128,128]{2,1,0:T(8,128)(2,1)}, u32[]{:S(2)}, u32[]{:S(2)}) collective-permute-start(bf16[112,128,128]{2,1,0:T(8,128)(2,1)} %collective-permute-done.11.refs_1_), channel_id=1, source_target_pairs={{0,8},{24,16},{1,9},{25,17},{2,10},{26,18},{3,11},{27,19},{4,12},{... | collective-permute-start | bytes 11010056 | tf_op jit(solution)/shard_map/ppermute | solution.py:280
  339.4 70.0 %collective-permute-start.18 = (bf16[5120,256]{1,0:T(8,128)(2,1)S(1)}, bf16[5120,256]{1,0:T(8,128)(2,1)S(1)}, u32[]{:S(2)}, u32[]{:S(2)}) collective-permute-start(bf16[5120,256]{1,0:T(8,128)(2,1)S(1)} %pad_maximum_fusion.1.refs_2_.refs_1_), channel_id=1, source_target_pairs={{8,16},{16,8},{9,17},{17,9},{10,18},{18,10},{11,19},{19,11},{12,20... | collective-permute-start | bytes 7864328 | tf_op jit(solution)/shard_map/ppermute | solution.py:280
  387.1 56.7 %collective-permute-start.35 = (bf16[4096,256]{1,0:T(8,128)(2,1)}, bf16[4096,256]{1,0:T(8,128)(2,1)}, u32[]{:S(2)}, u32[]{:S(2)}) collective-permute-start(bf16[4096,256]{1,0:T(8,128)(2,1)} %collective-permute-done.14.refs_2_), channel_id=1, source_target_pairs={{8,0},{16,24},{9,1},{17,25},{10,2},{18,26},{11,3},{19,27},{12,4},{... | collective-permute-start | bytes 6291464 | tf_op jit(solution)/shard_map/ppermute | solution.py:280
  400.7 8.4 %copy-start.4 = (f32[1,256,1024]{2,1,0:T(8,128)}, f32[1,256,1024]{2,1,0:T(8,128)S(1)}, u32[]{:S(2)}) copy-start(f32[1,256,1024]{2,1,0:T(8,128)S(1)} %tiles_times_planes.21) | copy-start | bytes 3145732
  419.3 11.1 %copy-start.7 = (f32[3,256,1024]{2,1,0:T(8,128)}, f32[3,256,1024]{2,1,0:T(8,128)S(1)}, u32[]{:S(2)}) copy-start(f32[3,256,1024]{2,1,0:T(8,128)S(1)} %fusion.4) | copy-start | bytes 9437188
  420.8 9.6 %copy-start.11 = (f32[3,256,512]{2,1,0:T(8,128)S(1)}, f32[3,256,512]{2,1,0:T(8,128)}, u32[]{:S(2)}) copy-start(f32[3,256,512]{2,1,0:T(8,128)} %get-tuple-element.131) | copy-start | bytes 4718596
  420.8 9.6 %copy-start.12 = (f32[3,256,512]{2,1,0:T(8,128)S(1)}, f32[3,256,512]{2,1,0:T(8,128)}, u32[]{:S(2)}) copy-start(f32[3,256,512]{2,1,0:T(8,128)} %get-tuple-element.132) | copy-start | bytes 4718596
  420.8 35.7 %collective-permute-start.25 = (f32[3,128,1024]{2,1,0:T(8,128)}, f32[3,128,1024]{2,1,0:T(8,128)}, u32[]{:S(2)}, u32[]{:S(2)}) collective-permute-start(f32[3,128,1024]{2,1,0:T(8,128)} %constant_dynamic-slice_fusion.10), channel_id=1, source_target_pairs={{0,1},{1,0},{2,3},{3,2},{4,5},{5,4},{6,7},{7,6},{8,9},{9,8},{10,11... | collective-permute-start | bytes 4718600 | tf_op jit(solution)/shard_map/ppermute | solution.py:265
  420.8 9.6 %copy-start.8 = (f32[3,256,1024]{2,1,0:T(8,128)S(1)}, f32[3,256,1024]{2,1,0:T(8,128)}, u32[]{:S(2)}) copy-start(f32[3,256,1024]{2,1,0:T(8,128)} %tiles_times_planes.11) | copy-start | bytes 9437188
  431.6 20.0 %copy-start.9 = (f32[3,256,1024]{2,1,0:T(8,128)}, f32[3,256,1024]{2,1,0:T(8,128)S(1)}, u32[]{:S(2)}) copy-start(f32[3,256,1024]{2,1,0:T(8,128)S(1)} %fusion.5) | copy-start | bytes 9437188
  433.1 18.5 %copy-start.3 = (f32[1,256,1024]{2,1,0:T(8,128)S(1)}, f32[1,256,1024]{2,1,0:T(8,128)}, u32[]{:S(2)}) copy-start(f32[1,256,1024]{2,1,0:T(8,128)} %copy-done.2) | copy-start | bytes 3145732
  433.1 18.5 %copy-start.5 = (f32[1,256,1024]{2,1,0:T(8,128)S(1)}, f32[1,256,1024]{2,1,0:T(8,128)}, u32[]{:S(2)}) copy-start(f32[1,256,1024]{2,1,0:T(8,128)} %copy-done.4) | copy-start | bytes 3145732
  433.2 28.9 %collective-permute-start.20 = (f32[3,128,1024]{2,1,0:T(8,128)}, f32[3,128,1024]{2,1,0:T(8,128)}, u32[]{:S(2)}, u32[]{:S(2)}) collective-permute-start(f32[3,128,1024]{2,1,0:T(8,128)} %constant_dynamic-slice_fusion.14), channel_id=1, source_target_pairs={{0,1},{1,0},{2,3},{3,2},{4,5},{5,4},{6,7},{7,6},{8,9},{9,8},{10,11... | collective-permute-start | bytes 4718600 | tf_op jit(solution)/shard_map/ppermute | solution.py:265
  451.6 4.7 copy-start.6
  452.0 4.4 collective-permute-start.36
  456.5 3.9 copy-start.14
  456.5 5.5 copy-start.10
  459.9 27.3 %collective-permute-start.26 = (f32[3,64,1024]{2,1,0:T(8,128)}, f32[3,64,1024]{2,1,0:T(8,128)}, u32[]{:S(2)}, u32[]{:S(2)}) collective-permute-start(f32[3,64,1024]{2,1,0:T(8,128)} %constant_dynamic-slice_fusion.9), channel_id=1, source_target_pairs={{0,4},{4,0},{1,5},{5,1},{2,6},{6,2},{3,7},{7,3},{8,12},{12,8},{9,1... | collective-permute-start | bytes 2359304 | tf_op jit(solution)/shard_map/ppermute | solution.py:265
  460.4 4.8 copy-start.18
  460.4 4.7 copy-start.20
  460.4 25.7 %collective-permute-start.37 = (f32[1,64,1024]{2,1,0:T(8,128)S(1)}, f32[1,64,1024]{2,1,0:T(8,128)}, u32[]{:S(2)}, u32[]{:S(2)}) collective-permute-start(f32[1,64,1024]{2,1,0:T(8,128)S(1)} %constant_dynamic-slice_fusion.6), channel_id=1, source_target_pairs={{0,4},{4,0},{1,5},{5,1},{2,6},{6,2},{3,7},{7,3},{8,12},{12,8},{9,1... | collective-permute-start | bytes 786440 | tf_op jit(solution)/shard_map/ppermute | solution.py:265
  464.6 38.0 %collective-permute-start.21 = (f32[3,64,1024]{2,1,0:T(8,128)}, f32[3,64,1024]{2,1,0:T(8,128)}, u32[]{:S(2)}, u32[]{:S(2)}) collective-permute-start(f32[3,64,1024]{2,1,0:T(8,128)} %constant_dynamic-slice_fusion.13), channel_id=1, source_target_pairs={{0,4},{4,0},{1,5},{5,1},{2,6},{6,2},{3,7},{7,3},{8,12},{12,8},{9,1... | collective-permute-start | bytes 2359304 | tf_op jit(solution)/shard_map/ppermute | solution.py:265
  488.5 17.0 %collective-permute-start.27 = (f32[3,32,1024]{2,1,0:T(8,128)S(1)}, f32[3,32,1024]{2,1,0:T(8,128)S(1)}, u32[]{:S(2)}, u32[]{:S(2)}) collective-permute-start(f32[3,32,1024]{2,1,0:T(8,128)S(1)} %constant_dynamic-slice_fusion.8), channel_id=1, source_target_pairs={{0,2},{2,0},{1,3},{3,1},{4,6},{6,4},{5,7},{7,5},{8,10},{10,8},{9,1... | collective-permute-start | bytes 1179656 | tf_op jit(solution)/shard_map/ppermute | solution.py:265
  490.1 18.1 %collective-permute-start.38 = (f32[1,32,1024]{2,1,0:T(8,128)S(1)}, f32[1,32,1024]{2,1,0:T(8,128)S(1)}, u32[]{:S(2)}, u32[]{:S(2)}) collective-permute-start(f32[1,32,1024]{2,1,0:T(8,128)S(1)} %constant_dynamic-slice_fusion.5), channel_id=1, source_target_pairs={{0,2},{2,0},{1,3},{3,1},{4,6},{6,4},{5,7},{7,5},{8,10},{10,8},{9,1... | collective-permute-start | bytes 393224 | tf_op jit(solution)/shard_map/ppermute | solution.py:265
  503.9 22.8 %collective-permute-start.22 = (f32[3,32,1024]{2,1,0:T(8,128)S(1)}, f32[3,32,1024]{2,1,0:T(8,128)S(1)}, u32[]{:S(2)}, u32[]{:S(2)}) collective-permute-start(f32[3,32,1024]{2,1,0:T(8,128)S(1)} %constant_dynamic-slice_fusion.12), channel_id=1, source_target_pairs={{0,2},{2,0},{1,3},{3,1},{4,6},{6,4},{5,7},{7,5},{8,10},{10,8},{9,1... | collective-permute-start | bytes 1179656 | tf_op jit(solution)/shard_map/ppermute | solution.py:265
  505.6 21.1 %collective-permute-start.28 = (f32[3,32,1024]{2,1,0:T(8,128)S(1)}, f32[3,32,1024]{2,1,0:T(8,128)S(1)}, u32[]{:S(2)}, u32[]{:S(2)}) collective-permute-start(f32[3,32,1024]{2,1,0:T(8,128)S(1)} %concatenate.91), channel_id=1, source_target_pairs={{8,0},{16,24},{9,1},{17,25},{10,2},{18,26},{11,3},{19,27},{12,4},{... | collective-permute-start | bytes 1179656 | tf_op jit(solution)/shard_map/ppermute | solution.py:434
  506.9 19.7 %collective-permute-start.39 = (f32[40,1024]{1,0:T(8,128)S(1)}, f32[40,1024]{1,0:T(8,128)S(1)}, u32[]{:S(2)}, u32[]{:S(2)}) collective-permute-start(f32[40,1024]{1,0:T(8,128)S(1)} %concatenate.94), channel_id=1, source_target_pairs={{8,0},{16,24},{9,1},{17,25},{10,2},{18,26},{11,3},{19,27},{12,4},{... | collective-permute-start | bytes 491528 | tf_op jit(solution)/shard_map/ppermute | solution.py:434
  526.6 7.2 %collective-permute-start.40 = (f32[40,1024]{1,0:T(8,128)S(1)}, f32[40,1024]{1,0:T(8,128)S(1)}, u32[]{:S(2)}, u32[]{:S(2)}) collective-permute-start(f32[40,1024]{1,0:T(8,128)S(1)} %get-tuple-element.136), channel_id=1, source_target_pairs={{0,8},{8,0},{16,24},{24,16},{1,9},{9,1},{17,25},{25,17},{2,10},{10... | collective-permute-start | bytes 491528 | tf_op jit(solution)/shard_map/ppermute | solution.py:429
  526.8 14.8 %collective-permute-start.29 = (f32[3,32,1024]{2,1,0:T(8,128)S(1)}, f32[3,32,1024]{2,1,0:T(8,128)S(1)}, u32[]{:S(2)}, u32[]{:S(2)}) collective-permute-start(f32[3,32,1024]{2,1,0:T(8,128)S(1)} %get-tuple-element.118), channel_id=1, source_target_pairs={{0,8},{8,0},{16,24},{24,16},{1,9},{9,1},{17,25},{25,17},{2,10},{10... | collective-permute-start | bytes 1179656 | tf_op jit(solution)/shard_map/ppermute | solution.py:429
  529.0 5.6 collective-permute-start.41
  533.9 10.1 %collective-permute-start.43 = (f32[40,1024]{1,0:T(8,128)S(1)}, f32[40,1024]{1,0:T(8,128)S(1)}, u32[]{:S(2)}, u32[]{:S(2)}) collective-permute-start(f32[40,1024]{1,0:T(8,128)S(1)} %pad_add_fusion.2), channel_id=1, source_target_pairs={{8,16},{16,8},{9,17},{17,9},{10,18},{18,10},{11,19},{19,11},{12,20... | collective-permute-start | bytes 491528 | tf_op jit(solution)/shard_map/ppermute | solution.py:431
  534.6 12.0 %collective-permute-start.42 = (f32[40,1024]{1,0:T(8,128)S(1)}, f32[40,1024]{1,0:T(8,128)S(1)}, u32[]{:S(2)}, u32[]{:S(2)}) collective-permute-start(f32[40,1024]{1,0:T(8,128)S(1)} %collective-permute-done.41), channel_id=1, source_target_pairs={{8,0},{16,24},{9,1},{17,25},{10,2},{18,26},{11,3},{19,27},{12,4},{... | collective-permute-start | bytes 491528 | tf_op jit(solution)/shard_map/ppermute | solution.py:432
  535.9 9.4 %collective-permute-start.30 = (f32[3,32,1024]{2,1,0:T(8,128)S(1)}, f32[3,32,1024]{2,1,0:T(8,128)S(1)}, u32[]{:S(2)}, u32[]{:S(2)}) collective-permute-start(f32[3,32,1024]{2,1,0:T(8,128)S(1)} %get-tuple-element.118), channel_id=1, source_target_pairs={{8,16},{16,8},{9,17},{17,9},{10,18},{18,10},{11,19},{19,11},{12,20... | collective-permute-start | bytes 1179656 | tf_op jit(solution)/shard_map/ppermute | solution.py:430
  541.7 4.9 collective-permute-start.32
  543.9 9.3 %collective-permute-start.44 = (f32[40,1024]{1,0:T(8,128)S(1)}, f32[40,1024]{1,0:T(8,128)S(1)}, u32[]{:S(2)}, u32[]{:S(2)}) collective-permute-start(f32[40,1024]{1,0:T(8,128)S(1)} %collective-permute-done.43), channel_id=1, source_target_pairs={{8,0},{16,24},{9,1},{17,25},{10,2},{18,26},{11,3},{19,27},{12,4},{... | collective-permute-start | bytes 491528 | tf_op jit(solution)/shard_map/ppermute | solution.py:433
  545.3 18.4 %collective-permute-start.31 = (f32[3,32,1024]{2,1,0:T(8,128)S(1)}, f32[3,32,1024]{2,1,0:T(8,128)S(1)}, u32[]{:S(2)}, u32[]{:S(2)}) collective-permute-start(f32[3,32,1024]{2,1,0:T(8,128)S(1)} %collective-permute-done.30), channel_id=1, source_target_pairs={{8,0},{16,24},{9,1},{17,25},{10,2},{18,26},{11,3},{19,27},{12,4},{... | collective-permute-start | bytes 1179656 | tf_op jit(solution)/shard_map/ppermute | solution.py:432
  546.6 21.9 %collective-permute-start.33 = (f32[3,32,1024]{2,1,0:T(8,128)S(1)}, f32[3,32,1024]{2,1,0:T(8,128)S(1)}, u32[]{:S(2)}, u32[]{:S(2)}) collective-permute-start(f32[3,32,1024]{2,1,0:T(8,128)S(1)} %collective-permute-done.32), channel_id=1, source_target_pairs={{8,0},{16,24},{9,1},{17,25},{10,2},{18,26},{11,3},{19,27},{12,4},{... | collective-permute-start | bytes 1179656 | tf_op jit(solution)/shard_map/ppermute | solution.py:433
  578.1 3.0 collective-permute-start.45
  582.5 14.7 %collective-permute-start.46 = (f32[1,2,1,4,136,128]{5,4,3,2,1,0:T(8,128)S(1)}, f32[1,2,1,4,136,128]{5,4,3,2,1,0:T(8,128)S(1)}, u32[]{:S(2)}, u32[]{:S(2)}) collective-permute-start(f32[1,2,1,4,136,128]{5,4,3,2,1,0:T(8,128)S(1)} %constant_dynamic-slice_fusion.3), channel_id=1, source_target_pairs={{0,4},{4,0},{1,5},{5,1},{2,6},{6,2},{3,7},{7,3},{8,12},{12,8},{9,1... | collective-permute-start | bytes 1671176 | tf_op jit(solution)/shard_map/ppermute | solution.py:265
  597.3 7.9 %collective-permute-start.47 = (f32[1,1,1,4,136,128]{5,4,3,2,1,0:T(8,128)S(1)}, f32[1,1,1,4,136,128]{5,4,3,2,1,0:T(8,128)S(1)}, u32[]{:S(2)}, u32[]{:S(2)}) collective-permute-start(f32[1,1,1,4,136,128]{5,4,3,2,1,0:T(8,128)S(1)} %constant_dynamic-slice_fusion.2), channel_id=1, source_target_pairs={{0,2},{2,0},{1,3},{3,1},{4,6},{6,4},{5,7},{7,5},{8,10},{10,8},{9,1... | collective-permute-start | bytes 835592 | tf_op jit(solution)/shard_map/ppermute | solution.py:265
  (4 other events, 6.8 us)

commit v11 on v10

--- a/solution.py
+++ b/solution.py
@@ -372,7 +372,7 @@
             near += ends.send([groups[c]], "z", [NEAR])
             mid += middle.send([groups[c]], "z", [MIDDLE])
     tiles = [None] * 3
-    for c in (0, 2, 1):
+    for c in (0, 2):
         tiles[c] = over_x.send([packed(o, c, groups[0]) for o in others], "x", row_routes)
 
     inward, outward = Lane(near[1:]), Lane(near[1:])
@@ -402,28 +402,42 @@
 
     early_groups = [[[groups[c]], [near[c]], [mid[c], outer[c]]] for c in range(2)]
     part0 = times(0, [hist] + tiles[0], every, early_groups[0], row_places)
-    loans += inward.send([after(t, part0) for t in tiles[2]], "z", [INWARD] * len(others))
+    tiles[1] = over_x.send([packed(o, 1, part0) for o in others], "x", row_routes)
+    loans += inward.send(tiles[2], "z", [INWARD] * len(others))
+    part2 = times(2, [hist] + tiles[2], every, [[groups[2]], [near[2]]], row_places)
     outer += outward.send([far[1]], "z", [OUTWARD])
     part1 = [times(1, [hist], [0], early_groups[1], [0])]
-    part2 = times(2, [hist] + tiles[2], every, [[groups[2]], [near[2]]], row_places)
+    outer += outward.send([after(far[0], part1)], "z", [OUTWARD])
     end2 = times(2, [hist] + tiles[2], every, [[far[2]]], row_places)
-    outer += outward.send([after(far[0], [part1, part2, end2])], "z", [OUTWARD])
-    part1 += [times(1, [tiles[1][k - 1]], [k], early_groups[1], [0]) for k in range(1, wide)]
+    inner_late = after(inner, [outer[2], part2, end2])
+    part1 += [
+        product(
+            [tiles[1][k - 1]], [masks[k][:, cuts[1] : cuts[2]]], early_groups[1], inner_late, x * columns + cuts[1], [0]
+        )
+        for k in range(1, wide)
+    ]
     end1 = times(1, [hist] + tiles[1], every, [[far[1], outer[2]]], row_places)
     guests = in_row_order(
         [product([t], [m], [[groups[2]], [far[2]]], inner, 0, [0]) for t, m in zip(loans, guest_masks)], 2
     )
-    part2 = jnp.concatenate([part2, times(2, [hist] + tiles[2], every, [[mid[2]]], row_places)])
+    part2_mid = product(
+        [hist] + tiles[2], [m[:, cuts[2] :] for m in masks], [[mid[2]]], after(inner, end1), x * columns + cuts[2],
+        row_places,
+    )
+    part2 = jnp.concatenate([part2, part2_mid])
     first_three = part0 + part2 + in_row_order(part1, 2)
-    guests_mid = product(loans, guest_masks, [[mid[2]]], inner, 0, row_places)
-    end0 = times(0, [hist] + tiles[0], every, [[far[0], outer[3]]], row_places)
+    guests_mid = product(loans, guest_masks, [[mid[2]]], after(inner, first_three), 0, row_places)
+    visitors = jnp.concatenate([guests[:1], guests_mid, guests[1:]])
+
+    first_three = scatter_sum(first_three, "core", 1)
+    inner_last = after(inner, first_three)
+    end0 = product(
+        [hist] + tiles[0], [m[:, : cuts[1]] for m in masks], [[far[0], outer[3]]], inner_last, x * columns, row_places
+    )
     last_one = end0 + (end1 + end2)
-    visitors = jnp.concatenate([guests[:1], guests_mid, guests[1:]])
-
-    def summed(share):
-        return scatter_sum(scatter_sum(scatter_sum(share, "core", 1), "x", 1), "y", 1)
-
-    first_three, visitors, last_one = summed(first_three), summed(visitors), summed(last_one)
+    first_three = scatter_sum(scatter_sum(first_three, "x", 1), "y", 1)
+    visitors = scatter_sum(scatter_sum(scatter_sum(visitors, "core", 1), "x", 1), "y", 1)
+    last_one = scatter_sum(scatter_sum(scatter_sum(last_one, "core", 1), "x", 1), "y", 1)
 
     def all_along_line(share, extra):
         near = lax.ppermute(share, "z", NEAR) + extra

time: 624 us -> 647 us (1.037)
  waiting for transfers between devices: 321 us -> 336 us
    ppermute x2, waiting for transfers between devices: 18.4 us -> 27.5 us  [all_along_line(): own = share + lax.ppermute(extra, 'z', OUTWARD)]
  transfers between devices with their start and end apart: 48 -> 48, of which waited for: 23 -> 28; matrix products, arithmetic and copies ran while one was open for 7% -> 7% of each run, Pallas kernels for 22% -> 21%
where the time goes in v11:
time: 647 us; the launch traced here: 637 us
  waiting for transfers between devices  336 us (52%)
  Pallas kernels  145 us (22%)
  starting transfers between devices  80.5 us (12%)
  other arithmetic  28.5 us (4%)
  local copies, waits for them, and re-layouts  27.8 us (4%)
  between operations  19.4 us (3%)
    ppermute x21, waiting for transfers between devices, send(): lax.ppermute(v, axis, route)  200 us
    pallas_call x11, Pallas kernels, product(): pl.pallas_call(functools.partial(product_kernel, blk, row_blocks, columns...  118 us
    ppermute x12, waiting for transfers between devices, scatter_sum(): total = total + lax.ppermute(part((here + k) % count), axis, turn(count, k))  61.1 us
    ppermute x21, starting transfers between devices, send(): lax.ppermute(v, axis, route)  54.2 us
    ppermute x2, waiting for transfers between devices, all_along_line(): own = share + lax.ppermute(extra, 'z', OUTWARD)  27.5 us
    pallas_call x4, Pallas kernels, pack(): pl.pallas_call(functools.partial(pack_kernel, blk, row_blocks, columns, s...  17.5 us
    ppermute x1, waiting for transfers between devices, body(): listed = [pairs] + [lax.ppermute(pairs, 'x', route) for route in row_routes]  16.3 us
  transfers between devices with their start and end apart: 48, of which 28 were waited for; matrix products, arithmetic and copies ran while one was open for 7% of the time, Pallas kernels for 21%

profile of v11, /device:TPU:0, one launch (start us, length us, event | category | flops | bytes accessed | tf_op | source)
XLA Modules:
  0.0 637.0 jit_solution(1638834050258139333)
XLA Ops:
  6.5 2.3 constant_dynamic-slice_fusion.17
  8.8 2.9 collective-permute-start.3
  11.8 3.5 collective-permute-start.1
  19.0 16.3 %collective-permute-done = s32[16,2]{0,1:T(2,128)S(1)} collective-permute-done((s32[16,2]{0,1:T(2,128)S(1)}, s32[16,2]{0,1:T(2,128)S(1)}, u32[]{:S(2)}, u32[]{:S(2)}) %collective-permute-start) | collective-permute-done | bytes 160 | tf_op jit(solution)/shard_map/ppermute | solution.py:360
  35.3 1.8 collective-permute-start.4
  37.1 1.6 broadcast_select_fusion.5
  39.0 1.6 collective-permute-start.5
  40.6 2.0 collective-permute-start.8
  42.6 34.0 %collective-permute-done.4 = bf16[7168,128]{1,0:T(8,128)(2,1)} collective-permute-done((bf16[7168,128]{1,0:T(8,128)(2,1)S(1)}, bf16[7168,128]{1,0:T(8,128)(2,1)}, u32[]{:S(2)}, u32[]{:S(2)}) %collective-permute-start.4) | collective-permute-done | bytes 1835040 | tf_op jit(solution)/shard_map/ppermute | solution.py:280
  76.6 2.8 broadcast_select_fusion.1
  79.3 2.3 pad_maximum_fusion.refs_1_
  81.7 3.6 collective-permute-done.5.refs_3_
  86.9 2.5 collective-permute-start.14
  91.6 3.9 pack_tiles.4
  95.5 23.9 %collective-permute-done.6 = bf16[5120,128]{1,0:T(8,128)(2,1)S(1)} collective-permute-done((bf16[5120,128]{1,0:T(8,128)(2,1)S(1)}, bf16[5120,128]{1,0:T(8,128)(2,1)S(1)}, u32[]{:S(2)}, u32[]{:S(2)}) %collective-permute-start.6) | collective-permute-done | bytes 1310752 | tf_op jit(solution)/shard_map/ppermute | solution.py:280
  120.5 4.4 pack_tiles.5
  124.9 39.7 %collective-permute-done.9.refs_2_ = bf16[7168,256]{1,0:T(8,128)(2,1)} collective-permute-done((bf16[7168,256]{1,0:T(8,128)(2,1)}, bf16[7168,256]{1,0:T(8,128)(2,1)}, u32[]{:S(2)}, u32[]{:S(2)}) %collective-permute-start.9) | collective-permute-done | bytes 3670048 | tf_op jit(solution)/shard_map/ppermute | solution.py:280
  164.5 2.0 collective-permute-start.15
  167.8 1.8 broadcast_select_fusion.3
  170.0 12.6 %collective-permute-start.12 = (bf16[5120,256]{1,0:T(8,128)(2,1)S(1)}, bf16[5120,256]{1,0:T(8,128)(2,1)}, u32[]{:S(2)}, u32[]{:S(2)}) collective-permute-start(bf16[5120,256]{1,0:T(8,128)(2,1)S(1)} %pad_maximum_fusion.1.refs_2_.refs_1_), channel_id=1, source_target_pairs={{0,8},{24,16},{1,9},{25,17},{2,10},{26,18},{3,11},{27,19},{4,12},{... | collective-permute-start | bytes 7864328 | tf_op jit(solution)/shard_map/ppermute | solution.py:280
  182.5 3.8 collective-permute-done.7.refs_1_
  188.2 29.8 %collective-permute-done.10.refs_5_ = bf16[4096,256]{1,0:T(8,128)(2,1)} collective-permute-done((bf16[4096,256]{1,0:T(8,128)(2,1)}, bf16[4096,256]{1,0:T(8,128)(2,1)}, u32[]{:S(2)}, u32[]{:S(2)}) %collective-permute-start.10) | collective-permute-done | bytes 2097184 | tf_op jit(solution)/shard_map/ppermute | solution.py:280
  218.0 2.4 collective-permute-start.16
  223.4 4.2 pack_tiles.7
  227.7 5.9 collective-permute-done.12.refs_3_
  233.5 6.3 collective-permute-start.24
  242.9 14.7 %tiles_times_planes.11 = f32[3,256,1024]{2,1,0:T(8,128)} custom-call(s32[268]{0:T(512)S(1)} %concatenate.77.info, bf16[512,32768]{1,0:T(8,128)(2,1)} %refs_0_.13, bf16[94,128,128]{2,1,0:T(8,128)(2,1)} %collective-permute-done.7.refs_1_, bf16[4096,256]{1,0:T(8,128)(2,1)S(1)} %copy-done.1, bf16[4096,256]{1,0:T(8,128)(2,1)} %collective-permute-done.5.refs_3_, ...), custom_call_target="tpu_custom_call" | custom-call | flops 6442450944 | bytes 14680064 | tf_op jit(solution)/shard_map/tiles_times_planes/pallas_call | solution.py:185
  257.9 5.0 pack_tiles.6
  262.9 2.9 collective-permute-done.11.refs_1_
  267.0 32.5 %collective-permute-done.17.refs_4_ = bf16[7168,256]{1,0:T(8,128)(2,1)} collective-permute-done((bf16[7168,256]{1,0:T(8,128)(2,1)}, bf16[7168,256]{1,0:T(8,128)(2,1)}, u32[]{:S(2)}, u32[]{:S(2)}) %collective-permute-start.17) | collective-permute-done | bytes 3670048 | tf_op jit(solution)/shard_map/ppermute | solution.py:280
  299.5 2.2 collective-permute-start.19
  305.6 7.6 %collective-permute-done.24.refs_0_ = bf16[112,128,128]{2,1,0:T(8,128)(2,1)} collective-permute-done((bf16[112,128,128]{2,1,0:T(8,128)(2,1)}, bf16[112,128,128]{2,1,0:T(8,128)(2,1)}, u32[]{:S(2)}, u32[]{:S(2)}) %collective-permute-start.24) | collective-permute-done | bytes 3670048 | tf_op jit(solution)/shard_map/ppermute | solution.py:280
  313.2 6.3 collective-permute-start.25
  320.0 2.3 collective-permute-start.20
  322.3 12.3 %tiles_times_planes.12 = f32[2,256,1024]{2,1,0:T(8,128)S(1)} custom-call(s32[334]{0:T(512)S(1)} %concatenate.81.info, bf16[512,32768]{1,0:T(8,128)(2,1)} %refs_0_.13, bf16[112,128,128]{2,1,0:T(8,128)(2,1)} %collective-permute-done.11.refs_1_, bf16[5120,256]{1,0:T(8,128)(2,1)S(1)} %pad_maximum_fusion.1.refs_2_.refs_1_, ...), custom_call_target="tpu_custom_call" | custom-call | flops 5368709120 | bytes 15728640 | tf_op jit(solution)/shard_map/tiles_times_planes/pallas_call | solution.py:185
  335.9 13.0 %tiles_times_planes.17 = f32[3,256,512]{2,1,0:T(8,128)S(1)} custom-call(s32[234]{0:T(256)S(1)} %concatenate.89.info, bf16[512,32768]{1,0:T(8,128)(2,1)} %refs_0_.13, bf16[7168,256]{1,0:T(8,128)(2,1)} %pad_maximum_fusion.refs_1_, bf16[7168,256]{1,0:T(8,128)(2,1)} %collective-permute-done.9.refs_2_, bf16[7168,256]{1,0:T(8,128)(2,1)} %collective-permute-done.14.refs_3_, ...), custom_call_target="tpu_custom_call" | custom-call | flops 5637144576 | bytes 18350080 | tf_op jit(solution)/shard_map/tiles_times_planes/pallas_call | solution.py:185
  349.0 9.2 %tiles_times_planes.15 = f32[1,256,1024]{2,1,0:T(8,128)S(1)} custom-call(s32[334]{0:T(512)S(1)} %concatenate.81.info, bf16[512,32768]{1,0:T(8,128)(2,1)} %refs_0_.13, bf16[112,128,128]{2,1,0:T(8,128)(2,1)} %collective-permute-done.11.refs_1_, bf16[5120,256]{1,0:T(8,128)(2,1)} %collective-permute-done.19.refs_2_), custom_call_target="tpu_custom_call" | custom-call | flops 2684354560 | bytes 13107200 | tf_op jit(solution)/shard_map/tiles_times_planes/pallas_call | solution.py:185
  358.3 8.4 %tiles_times_planes.19 = f32[2,256,512]{2,1,0:T(8,128)S(1)} custom-call(s32[168]{0:T(256)S(1)} %get-tuple-element.155.info, bf16[112,128,128]{2,1,0:T(8,128)(2,1)} %collective-permute-done.24.refs_0_, bf16[5120,256]{1,0:T(8,128)(2,1)S(1)} %pad_maximum_fusion.1.refs_2_.refs_1_, bf16[5120,256]{1,0:T(8,128)(2,1)} %collective-permute-done.19.refs_2_), custom_call_target="tpu_custom_call" | custom-call | flops 2684354560 | bytes 10485760 | tf_op jit(solution)/shard_map/tiles_times_planes/pallas_call | solution.py:185
  369.0 12.1 %collective-permute-done.18.refs_3_ = bf16[7168,256]{1,0:T(8,128)(2,1)} collective-permute-done((bf16[7168,256]{1,0:T(8,128)(2,1)}, bf16[7168,256]{1,0:T(8,128)(2,1)}, u32[]{:S(2)}, u32[]{:S(2)}) %collective-permute-start.18) | collective-permute-done | bytes 3670048 | tf_op jit(solution)/shard_map/ppermute | solution.py:280
  381.1 12.1 %tiles_times_planes.13 = f32[1,256,1024]{2,1,0:T(8,128)S(1)} custom-call(s32[466]{0:T(512)S(1)} %concatenate.84.info, bf16[512,32768]{1,0:T(8,128)(2,1)} %refs_0_.13, bf16[150,128,128]{2,1,0:T(8,128)(2,1)} %collective-permute-done.13.refs_1_.refs_0_, bf16[7168,256]{1,0:T(8,128)(2,1)} %collective-permute-done.16.refs_2_, ...), custom_call_target="tpu_custom_call" | custom-call | flops 3758096384 | bytes 18350080 | tf_op jit(solution)/shard_map/tiles_times_planes/pallas_call | solution.py:185
  394.3 1.6 collective-permute-start.35
  395.9 13.1 %tiles_times_planes.16 = f32[3,256,512]{2,1,0:T(8,128)S(1)} custom-call(s32[234]{0:T(256)S(1)} %concatenate.88.info, bf16[150,128,128]{2,1,0:T(8,128)(2,1)} %collective-permute-done.13.refs_1_.refs_0_, bf16[7168,256]{1,0:T(8,128)(2,1)} %pad_maximum_fusion.refs_1_, bf16[7168,256]{1,0:T(8,128)(2,1)} %collective-permute-done.9.refs_2_, ...), custom_call_target="tpu_custom_call" | custom-call | flops 5637144576 | bytes 18350080 | tf_op jit(solution)/shard_map/tiles_times_planes/pallas_call | solution.py:185
  409.8 8.4 %tiles_times_planes.18 = f32[2,256,512]{2,1,0:T(8,128)S(1)} custom-call(s32[168]{0:T(256)S(1)} %get-tuple-element.156.info, bf16[112,128,128]{2,1,0:T(8,128)(2,1)} %collective-permute-done.25.refs_0_.refs_1_, bf16[5120,256]{1,0:T(8,128)(2,1)S(1)} %pad_maximum_fusion.1.refs_2_.refs_1_, bf16[5120,256]{1,0:T(8,128)(2,1)} %collective-permute-done.19.refs_2_), custom_call_target="tpu_custom_call" | custom-call | flops 2684354560 | bytes 10485760 | tf_op jit(solution)/shard_map/tiles_times_planes/pallas_call | solution.py:185
  418.2 9.6 %tiles_times_planes.14 = f32[1,256,1024]{2,1,0:T(8,128)S(1)} custom-call(s32[334]{0:T(512)S(1)} %concatenate.86.info, bf16[512,32768]{1,0:T(8,128)(2,1)} %refs_0_.13, bf16[112,128,128]{2,1,0:T(8,128)(2,1)} %collective-permute-done.11.refs_1_, bf16[5120,256]{1,0:T(8,128)(2,1)} %collective-permute-done.20.refs_2_), custom_call_target="tpu_custom_call" | custom-call | flops 2684354560 | bytes 13107200 | tf_op jit(solution)/shard_map/tiles_times_planes/pallas_call | solution.py:185
  433.8 9.6 %tiles_times_planes.20 = f32[1,256,1024]{2,1,0:T(8,128)S(1)} custom-call(s32[334]{0:T(512)S(1)} %concatenate.95.info, bf16[112,128,128]{2,1,0:T(8,128)(2,1)} %collective-permute-done.24.refs_0_, bf16[112,128,128]{2,1,0:T(8,128)(2,1)} %collective-permute-done.25.refs_0_.refs_1_, bf16[5120,256]{1,0:T(8,128)(2,1)} %collective-permute-done.20.refs_2_), custom_call_target="tpu_custom_call" | custom-call | flops 2684354560 | bytes 13107200 | tf_op jit(solution)/shard_map/tiles_times_planes/pallas_call | solution.py:185
  451.1 3.4 dynamic-slice_add_fusion.1
  454.6 3.3 collective-permute-done.35.refs_3_
  457.9 7.9 %tiles_times_planes.21 = f32[1,256,1024]{2,1,0:T(8,128)S(1)} custom-call(s32[268]{0:T(512)S(1)} %concatenate.98.info, bf16[512,32768]{1,0:T(8,128)(2,1)} %refs_0_.13, bf16[94,128,128]{2,1,0:T(8,128)(2,1)} %collective-permute-done.7.refs_1_, bf16[4096,256]{1,0:T(8,128)(2,1)} %collective-permute-done.15.refs_2_, bf16[4096,256]{1,0:T(8,128)(2,1)} %collective-permute-done.35.refs_3_), custom_call_target="tpu_custom_call" | custom-call | flops 2147483648 | bytes 10485760 | tf_op jit(solution)/shard_map/tiles_times_planes/pallas_call | solution.py:185
  467.1 1.8 dynamic-slice_add_fusion
  475.6 14.9 %collective-permute-done.27 = f32[3,64,1024]{2,1,0:T(8,128)S(1)} collective-permute-done((f32[3,64,1024]{2,1,0:T(8,128)}, f32[3,64,1024]{2,1,0:T(8,128)S(1)}, u32[]{:S(2)}, u32[]{:S(2)}) %collective-permute-start.27) | collective-permute-done | bytes 786464 | tf_op jit(solution)/shard_map/ppermute | solution.py:265
  492.3 15.2 %collective-permute-done.22 = f32[3,64,1024]{2,1,0:T(8,128)} collective-permute-done((f32[3,64,1024]{2,1,0:T(8,128)}, f32[3,64,1024]{2,1,0:T(8,128)}, u32[]{:S(2)}, u32[]{:S(2)}) %collective-permute-start.22) | collective-permute-done | bytes 786464 | tf_op jit(solution)/shard_map/ppermute | solution.py:265
  510.4 2.1 collective-permute-done.37
  517.1 4.6 collective-permute-done.38
  521.7 27.5 %collective-permute-done.39 = f32[40,1024]{1,0:T(8,128)S(1)} collective-permute-done((f32[40,1024]{1,0:T(8,128)S(1)}, f32[40,1024]{1,0:T(8,128)S(1)}, u32[]{:S(2)}, u32[]{:S(2)}) %collective-permute-start.39) | collective-permute-done | bytes 163872 | tf_op jit(solution)/shard_map/ppermute | solution.py:448
  549.4 2.1 collective-permute-start.30
  552.2 4.2 collective-permute-done.40
  559.1 4.8 collective-permute-done.30
  570.2 5.2 collective-permute-done.44
  575.5 10.4 %collective-permute-done.32 = f32[3,32,1024]{2,1,0:T(8,128)S(1)} collective-permute-done((f32[3,32,1024]{2,1,0:T(8,128)S(1)}, f32[3,32,1024]{2,1,0:T(8,128)S(1)}, u32[]{:S(2)}, u32[]{:S(2)}) %collective-permute-start.32) | collective-permute-done | bytes 393248 | tf_op jit(solution)/shard_map/ppermute | solution.py:446
  585.9 5.0 collective-permute-done.34
  591.1 9.3 %pair_dots.1 = f32[32,136,128]{2,1,0:T(8,128)S(1)} custom-call(s32[2,6,32]{2,1,0:T(8,128)S(1)} %pad_add_fusion.1.ids, f32[4,3,32,1024]{3,2,1,0:T(8,128)S(1)} %pad_maximum_fusion.3.early, f32[4,40,1024]{2,1,0:T(8,128)S(1)} %pad_maximum_fusion.4.late), custom_call_target="tpu_custom_call" | custom-call | tf_op jit(solution)/shard_map/pair_dots/pallas_call | solution.py:241
  600.6 2.9 collective-permute-done.45
  605.5 14.1 %collective-permute-done.46 = f32[1,2,1,4,136,128]{5,4,3,2,1,0:T(8,128)S(1)} collective-permute-done((f32[1,2,1,4,136,128]{5,4,3,2,1,0:T(8,128)S(1)}, f32[1,2,1,4,136,128]{5,4,3,2,1,0:T(8,128)S(1)}, u32[]{:S(2)}, u32[]{:S(2)}) %collective-permute-start.46) | collective-permute-done | bytes 557088 | tf_op jit(solution)/shard_map/ppermute | solution.py:265
  620.3 7.4 %collective-permute-done.47 = f32[1,1,1,4,136,128]{5,4,3,2,1,0:T(8,128)S(1)} collective-permute-done((f32[1,1,1,4,136,128]{5,4,3,2,1,0:T(8,128)S(1)}, f32[1,1,1,4,136,128]{5,4,3,2,1,0:T(8,128)S(1)}, u32[]{:S(2)}, u32[]{:S(2)}) %collective-permute-start.47) | collective-permute-done | bytes 278560 | tf_op jit(solution)/shard_map/ppermute | solution.py:265
  (306 shorter events, 70.9 us)
Async XLA Ops:
  6.5 5.3 copy-start.27
  6.5 8.7 %copy-start.28 = (s32[16,2]{0,1:T(2,128)S(1)}, s32[16,2]{0,1:T(2,128)}, u32[]{:S(2)}) copy-start(s32[16,2]{0,1:T(2,128)} %param.10) | copy-start | bytes 388
  8.8 26.4 %collective-permute-start.3 = (bf16[4096,128]{1,0:T(8,128)(2,1)}, bf16[4096,128]{1,0:T(8,128)(2,1)S(1)}, u32[]{:S(2)}, u32[]{:S(2)}) collective-permute-start(bf16[4096,128]{1,0:T(8,128)(2,1)} %constant_dynamic-slice_fusion.17), channel_id=1, source_target_pairs={{0,4},{4,0},{1,5},{5,1},{2,6},{6,2},{3,7},{7,3},{8,12},{12,8},{9,1... | collective-permute-start | bytes 3145736 | tf_op jit(solution)/shard_map/ppermute | solution.py:280
  11.8 4.8 collective-permute-start.1
  15.3 20.0 %collective-permute-start = (s32[16,2]{0,1:T(2,128)S(1)}, s32[16,2]{0,1:T(2,128)S(1)}, u32[]{:S(2)}, u32[]{:S(2)}) collective-permute-start(s32[16,2]{0,1:T(2,128)S(1)} %copy-done.28), channel_id=1, source_target_pairs={{0,4},{4,0},{1,5},{5,1},{2,6},{6,2},{3,7},{7,3},{8,12},{12,8},{9,1... | collective-permute-start | bytes 392 | tf_op jit(solution)/shard_map/ppermute | solution.py:360
  16.6 18.7 %collective-permute-start.2 = (s32[2,4,128]{2,1,0:T(4,128)S(1)}, s32[2,4,128]{2,1,0:T(4,128)S(1)}, u32[]{:S(2)}, u32[]{:S(2)}) collective-permute-start(s32[2,4,128]{2,1,0:T(4,128)S(1)} %get-tuple-element.144), channel_id=1, source_target_pairs={{0,4},{4,0},{1,5},{5,1},{2,6},{6,2},{3,7},{7,3},{8,12},{12,8},{9,1... | collective-permute-start | bytes 12296 | tf_op jit(solution)/shard_map/ppermute | solution.py:359
  35.3 41.3 %collective-permute-start.4 = (bf16[7168,128]{1,0:T(8,128)(2,1)S(1)}, bf16[7168,128]{1,0:T(8,128)(2,1)}, u32[]{:S(2)}, u32[]{:S(2)}) collective-permute-start(bf16[7168,128]{1,0:T(8,128)(2,1)S(1)} %constant_dynamic-slice_fusion.15), channel_id=1, source_target_pairs={{0,4},{4,0},{1,5},{5,1},{2,6},{6,2},{3,7},{7,3},{8,12},{12,8},{9,1... | collective-permute-start | bytes 5505032 | tf_op jit(solution)/shard_map/ppermute | solution.py:280
  39.0 40.4 %copy-start = (bf16[4096,256]{1,0:T(8,128)(2,1)}, bf16[4096,256]{1,0:T(8,128)(2,1)S(1)}, u32[]{:S(2)}) copy-start(bf16[4096,256]{1,0:T(8,128)(2,1)S(1)} %pad_maximum_fusion.2.refs_2_) | copy-start | bytes 6291460
  39.0 46.3 %collective-permute-start.5 = (bf16[4096,256]{1,0:T(8,128)(2,1)S(1)}, bf16[4096,256]{1,0:T(8,128)(2,1)}, u32[]{:S(2)}, u32[]{:S(2)}) collective-permute-start(bf16[4096,256]{1,0:T(8,128)(2,1)S(1)} %pad_maximum_fusion.2.refs_2_), channel_id=1, source_target_pairs={{0,8},{8,0},{16,24},{24,16},{1,9},{9,1},{17,25},{25,17},{2,10},{10... | collective-permute-start | bytes 6291464 | tf_op jit(solution)/shard_map/ppermute | solution.py:280
  40.6 46.3 %collective-permute-start.8 = (bf16[4096,256]{1,0:T(8,128)(2,1)S(1)}, bf16[4096,256]{1,0:T(8,128)(2,1)}, u32[]{:S(2)}, u32[]{:S(2)}) collective-permute-start(bf16[4096,256]{1,0:T(8,128)(2,1)S(1)} %pad_maximum_fusion.2.refs_2_), channel_id=1, source_target_pairs={{8,16},{16,8},{9,17},{17,9},{10,18},{18,10},{11,19},{19,11},{12,20... | collective-permute-start | bytes 6291464 | tf_op jit(solution)/shard_map/ppermute | solution.py:280
  85.3 79.3 %collective-permute-start.9 = (bf16[7168,256]{1,0:T(8,128)(2,1)}, bf16[7168,256]{1,0:T(8,128)(2,1)}, u32[]{:S(2)}, u32[]{:S(2)}) collective-permute-start(bf16[7168,256]{1,0:T(8,128)(2,1)} %pad_maximum_fusion.refs_1_), channel_id=1, source_target_pairs={{0,8},{8,0},{16,24},{24,16},{1,9},{9,1},{17,25},{25,17},{2,10},{10... | collective-permute-start | bytes 11010056 | tf_op jit(solution)/shard_map/ppermute | solution.py:280
  86.9 77.7 %collective-permute-start.14 = (bf16[7168,256]{1,0:T(8,128)(2,1)}, bf16[7168,256]{1,0:T(8,128)(2,1)}, u32[]{:S(2)}, u32[]{:S(2)}) collective-permute-start(bf16[7168,256]{1,0:T(8,128)(2,1)} %pad_maximum_fusion.refs_1_), channel_id=1, source_target_pairs={{8,16},{16,8},{9,17},{17,9},{10,18},{18,10},{11,19},{19,11},{12,20... | collective-permute-start | bytes 11010056 | tf_op jit(solution)/shard_map/ppermute | solution.py:280
  90.7 28.7 %collective-permute-start.6 = (bf16[5120,128]{1,0:T(8,128)(2,1)S(1)}, bf16[5120,128]{1,0:T(8,128)(2,1)S(1)}, u32[]{:S(2)}, u32[]{:S(2)}) collective-permute-start(bf16[5120,128]{1,0:T(8,128)(2,1)S(1)} %constant_dynamic-slice_fusion.16), channel_id=1, source_target_pairs={{0,4},{4,0},{1,5},{5,1},{2,6},{6,2},{3,7},{7,3},{8,12},{12,8},{9,1... | collective-permute-start | bytes 3932168 | tf_op jit(solution)/shard_map/ppermute | solution.py:280
  119.4 66.9 %collective-permute-start.7 = (bf16[94,128,128]{2,1,0:T(8,128)(2,1)}, bf16[94,128,128]{2,1,0:T(8,128)(2,1)}, u32[]{:S(2)}, u32[]{:S(2)}) collective-permute-start(bf16[94,128,128]{2,1,0:T(8,128)(2,1)} %pack_tiles.4), channel_id=1, source_target_pairs={{0,4},{4,0},{1,5},{5,1},{2,6},{6,2},{3,7},{7,3},{8,12},{12,8},{9,1... | collective-permute-start | bytes 9240584 | tf_op jit(solution)/shard_map/ppermute | solution.py:280
  164.5 23.6 %collective-permute-start.15 = (bf16[4096,256]{1,0:T(8,128)(2,1)}, bf16[4096,256]{1,0:T(8,128)(2,1)}, u32[]{:S(2)}, u32[]{:S(2)}) collective-permute-start(bf16[4096,256]{1,0:T(8,128)(2,1)} %collective-permute-done.5.refs_3_), channel_id=1, source_target_pairs={{8,16},{16,8},{9,17},{17,9},{10,18},{18,10},{11,19},{19,11},{12,20... | collective-permute-start | bytes 6291464 | tf_op jit(solution)/shard_map/ppermute | solution.py:280
  166.5 51.5 %collective-permute-start.10 = (bf16[4096,256]{1,0:T(8,128)(2,1)}, bf16[4096,256]{1,0:T(8,128)(2,1)}, u32[]{:S(2)}, u32[]{:S(2)}) collective-permute-start(bf16[4096,256]{1,0:T(8,128)(2,1)} %collective-permute-done.8.refs_4_), channel_id=1, source_target_pairs={{8,0},{16,24},{9,1},{17,25},{10,2},{18,26},{11,3},{19,27},{12,4},{... | collective-permute-start | bytes 6291464 | tf_op jit(solution)/shard_map/ppermute | solution.py:280
  170.0 63.6 %collective-permute-start.12 = (bf16[5120,256]{1,0:T(8,128)(2,1)S(1)}, bf16[5120,256]{1,0:T(8,128)(2,1)}, u32[]{:S(2)}, u32[]{:S(2)}) collective-permute-start(bf16[5120,256]{1,0:T(8,128)(2,1)S(1)} %pad_maximum_fusion.1.refs_2_.refs_1_), channel_id=1, source_target_pairs={{0,8},{24,16},{1,9},{25,17},{2,10},{26,18},{3,11},{27,19},{4,12},{... | collective-permute-start | bytes 7864328 | tf_op jit(solution)/shard_map/ppermute | solution.py:280
  186.3 79.5 %collective-permute-start.11 = (bf16[112,128,128]{2,1,0:T(8,128)(2,1)}, bf16[112,128,128]{2,1,0:T(8,128)(2,1)}, u32[]{:S(2)}, u32[]{:S(2)}) collective-permute-start(bf16[112,128,128]{2,1,0:T(8,128)(2,1)} %pack_tiles.5), channel_id=1, source_target_pairs={{0,4},{4,0},{1,5},{5,1},{2,6},{6,2},{3,7},{7,3},{8,12},{12,8},{9,1... | collective-permute-start | bytes 11010056 | tf_op jit(solution)/shard_map/ppermute | solution.py:280
  218.0 49.0 %collective-permute-start.16 = (bf16[7168,256]{1,0:T(8,128)(2,1)}, bf16[7168,256]{1,0:T(8,128)(2,1)}, u32[]{:S(2)}, u32[]{:S(2)}) collective-permute-start(bf16[7168,256]{1,0:T(8,128)(2,1)} %collective-permute-done.9.refs_2_), channel_id=1, source_target_pairs={{8,16},{16,8},{9,17},{17,9},{10,18},{18,10},{11,19},{19,11},{12,20... | collective-permute-start | bytes 11010056 | tf_op jit(solution)/shard_map/ppermute | solution.py:280
  220.4 79.0 %collective-permute-start.17 = (bf16[7168,256]{1,0:T(8,128)(2,1)}, bf16[7168,256]{1,0:T(8,128)(2,1)}, u32[]{:S(2)}, u32[]{:S(2)}) collective-permute-start(bf16[7168,256]{1,0:T(8,128)(2,1)} %collective-permute-done.14.refs_3_), channel_id=1, source_target_pairs={{8,0},{16,24},{9,1},{17,25},{10,2},{18,26},{11,3},{19,27},{12,4},{... | collective-permute-start | bytes 11010056 | tf_op jit(solution)/shard_map/ppermute | solution.py:280
  233.5 79.6 %collective-permute-start.24 = (bf16[112,128,128]{2,1,0:T(8,128)(2,1)}, bf16[112,128,128]{2,1,0:T(8,128)(2,1)}, u32[]{:S(2)}, u32[]{:S(2)}) collective-permute-start(bf16[112,128,128]{2,1,0:T(8,128)(2,1)} %pack_tiles.7), channel_id=1, source_target_pairs={{0,8},{24,16},{1,9},{25,17},{2,10},{26,18},{3,11},{27,19},{4,12},{... | collective-permute-start | bytes 11010056 | tf_op jit(solution)/shard_map/ppermute | solution.py:280
  265.8 103.2 %collective-permute-start.13 = (bf16[150,128,128]{2,1,0:T(8,128)(2,1)}, bf16[150,128,128]{2,1,0:T(8,128)(2,1)}, u32[]{:S(2)}, u32[]{:S(2)}) collective-permute-start(bf16[150,128,128]{2,1,0:T(8,128)(2,1)} %pack_tiles.6), channel_id=1, source_target_pairs={{0,4},{4,0},{1,5},{5,1},{2,6},{6,2},{3,7},{7,3},{8,12},{12,8},{9,1... | collective-permute-start | bytes 14745608 | tf_op jit(solution)/shard_map/ppermute | solution.py:280
  299.5 20.5 %collective-permute-start.19 = (bf16[5120,256]{1,0:T(8,128)(2,1)}, bf16[5120,256]{1,0:T(8,128)(2,1)}, u32[]{:S(2)}, u32[]{:S(2)}) collective-permute-start(bf16[5120,256]{1,0:T(8,128)(2,1)} %collective-permute-done.12.refs_3_), channel_id=1, source_target_pairs={{8,16},{16,8},{9,17},{17,9},{10,18},{18,10},{11,19},{19,11},{12,20... | collective-permute-start | bytes 7864328 | tf_op jit(solution)/shard_map/ppermute | solution.py:280
  303.0 78.1 %collective-permute-start.18 = (bf16[7168,256]{1,0:T(8,128)(2,1)}, bf16[7168,256]{1,0:T(8,128)(2,1)}, u32[]{:S(2)}, u32[]{:S(2)}) collective-permute-start(bf16[7168,256]{1,0:T(8,128)(2,1)} %collective-permute-done.16.refs_2_), channel_id=1, source_target_pairs={{8,0},{16,24},{9,1},{17,25},{10,2},{18,26},{11,3},{19,27},{12,4},{... | collective-permute-start | bytes 11010056 | tf_op jit(solution)/shard_map/ppermute | solution.py:280
  313.2 96.6 %collective-permute-start.25 = (bf16[112,128,128]{2,1,0:T(8,128)(2,1)}, bf16[112,128,128]{2,1,0:T(8,128)(2,1)}, u32[]{:S(2)}, u32[]{:S(2)}) collective-permute-start(bf16[112,128,128]{2,1,0:T(8,128)(2,1)} %collective-permute-done.11.refs_1_), channel_id=1, source_target_pairs={{0,8},{24,16},{1,9},{25,17},{2,10},{26,18},{3,11},{27,19},{4,12},{... | collective-permute-start | bytes 11010056 | tf_op jit(solution)/shard_map/ppermute | solution.py:280
  320.0 98.2 %collective-permute-start.20 = (bf16[5120,256]{1,0:T(8,128)(2,1)S(1)}, bf16[5120,256]{1,0:T(8,128)(2,1)}, u32[]{:S(2)}, u32[]{:S(2)}) collective-permute-start(bf16[5120,256]{1,0:T(8,128)(2,1)S(1)} %pad_maximum_fusion.1.refs_2_.refs_1_), channel_id=1, source_target_pairs={{8,16},{16,8},{9,17},{17,9},{10,18},{18,10},{11,19},{19,11},{12,20... | collective-permute-start | bytes 7864328 | tf_op jit(solution)/shard_map/ppermute | solution.py:280
  349.0 9.3 %copy-start.4 = (f32[3,256,512]{2,1,0:T(8,128)}, f32[3,256,512]{2,1,0:T(8,128)S(1)}, u32[]{:S(2)}) copy-start(f32[3,256,512]{2,1,0:T(8,128)S(1)} %tiles_times_planes.17) | copy-start | bytes 4718596
  358.2 8.4 %copy-start.8 = (f32[1,256,1024]{2,1,0:T(8,128)}, f32[1,256,1024]{2,1,0:T(8,128)S(1)}, u32[]{:S(2)}) copy-start(f32[1,256,1024]{2,1,0:T(8,128)S(1)} %tiles_times_planes.15) | copy-start | bytes 3145732
  394.3 14.8 %copy-start.5 = (f32[3,256,512]{2,1,0:T(8,128)S(1)}, f32[3,256,512]{2,1,0:T(8,128)}, u32[]{:S(2)}) copy-start(f32[3,256,512]{2,1,0:T(8,128)} %copy-done.4) | copy-start | bytes 4718596
  394.3 63.6 %collective-permute-start.35 = (bf16[4096,256]{1,0:T(8,128)(2,1)}, bf16[4096,256]{1,0:T(8,128)(2,1)}, u32[]{:S(2)}, u32[]{:S(2)}) collective-permute-start(bf16[4096,256]{1,0:T(8,128)(2,1)} %collective-permute-done.15.refs_2_), channel_id=1, source_target_pairs={{8,0},{16,24},{9,1},{17,25},{10,2},{18,26},{11,3},{19,27},{12,4},{... | collective-permute-start | bytes 6291464 | tf_op jit(solution)/shard_map/ppermute | solution.py:280
  418.1 9.7 %copy-start.3 = (f32[2,256,1024]{2,1,0:T(8,128)S(1)}, f32[2,256,1024]{2,1,0:T(8,128)}, u32[]{:S(2)}) copy-start(f32[2,256,1024]{2,1,0:T(8,128)} %copy-done.2) | copy-start | bytes 6291460
  418.2 9.7 %copy-start.13 = (f32[3,256,1024]{2,1,0:T(8,128)S(1)}, f32[3,256,1024]{2,1,0:T(8,128)}, u32[]{:S(2)}) copy-start(f32[3,256,1024]{2,1,0:T(8,128)} %tiles_times_planes.11) | copy-start | bytes 9437188
  430.2 20.9 %collective-permute-start.21 = (f32[3,128,1024]{2,1,0:T(8,128)}, f32[3,128,1024]{2,1,0:T(8,128)}, u32[]{:S(2)}, u32[]{:S(2)}) collective-permute-start(f32[3,128,1024]{2,1,0:T(8,128)} %constant_dynamic-slice_fusion.14), channel_id=1, source_target_pairs={{0,1},{1,0},{2,3},{3,2},{4,5},{5,4},{6,7},{7,6},{8,9},{9,8},{10,11... | collective-permute-start | bytes 4718600 | tf_op jit(solution)/shard_map/ppermute | solution.py:265
  433.8 9.7 %copy-start.16 = (f32[2,256,512]{2,1,0:T(8,128)S(1)}, f32[2,256,512]{2,1,0:T(8,128)}, u32[]{:S(2)}) copy-start(f32[2,256,512]{2,1,0:T(8,128)} %copy-done.15) | copy-start | bytes 3145732
  433.8 9.7 %copy-start.18 = (f32[2,256,512]{2,1,0:T(8,128)S(1)}, f32[2,256,512]{2,1,0:T(8,128)}, u32[]{:S(2)}) copy-start(f32[2,256,512]{2,1,0:T(8,128)} %copy-done.17) | copy-start | bytes 3145732
  433.8 9.7 %copy-start.23 = (f32[1,256,1024]{2,1,0:T(8,128)S(1)}, f32[1,256,1024]{2,1,0:T(8,128)}, u32[]{:S(2)}) copy-start(f32[1,256,1024]{2,1,0:T(8,128)} %fusion.6) | copy-start | bytes 3145732
  445.0 22.1 %collective-permute-start.26 = (f32[3,128,1024]{2,1,0:T(8,128)}, f32[3,128,1024]{2,1,0:T(8,128)}, u32[]{:S(2)}, u32[]{:S(2)}) collective-permute-start(f32[3,128,1024]{2,1,0:T(8,128)} %constant_dynamic-slice_fusion.10), channel_id=1, source_target_pairs={{0,1},{1,0},{2,3},{3,2},{4,5},{5,4},{6,7},{7,6},{8,9},{9,8},{10,11... | collective-permute-start | bytes 4718600 | tf_op jit(solution)/shard_map/ppermute | solution.py:265
  454.6 11.2 %copy-start.9 = (f32[1,256,1024]{2,1,0:T(8,128)S(1)}, f32[1,256,1024]{2,1,0:T(8,128)}, u32[]{:S(2)}) copy-start(f32[1,256,1024]{2,1,0:T(8,128)} %copy-done.8) | copy-start | bytes 3145732
  454.6 11.2 %copy-start.11 = (f32[1,256,1024]{2,1,0:T(8,128)S(1)}, f32[1,256,1024]{2,1,0:T(8,128)}, u32[]{:S(2)}) copy-start(f32[1,256,1024]{2,1,0:T(8,128)} %copy-done.10) | copy-start | bytes 3145732
  467.1 6.5 %collective-permute-start.36 = (f32[1,128,1024]{2,1,0:T(8,128)}, f32[1,128,1024]{2,1,0:T(8,128)}, u32[]{:S(2)}, u32[]{:S(2)}) collective-permute-start(f32[1,128,1024]{2,1,0:T(8,128)} %constant_dynamic-slice_fusion.7), channel_id=1, source_target_pairs={{0,1},{1,0},{2,3},{3,2},{4,5},{5,4},{6,7},{7,6},{8,9},{9,8},{10,11... | collective-permute-start | bytes 1572872 | tf_op jit(solution)/shard_map/ppermute | solution.py:265
  468.9 4.0 copy-start.29
  469.9 20.6 %collective-permute-start.27 = (f32[3,64,1024]{2,1,0:T(8,128)}, f32[3,64,1024]{2,1,0:T(8,128)S(1)}, u32[]{:S(2)}, u32[]{:S(2)}) collective-permute-start(f32[3,64,1024]{2,1,0:T(8,128)} %constant_dynamic-slice_fusion.9), channel_id=1, source_target_pairs={{0,4},{4,0},{1,5},{5,1},{2,6},{6,2},{3,7},{7,3},{8,12},{12,8},{9,1... | collective-permute-start | bytes 2359304 | tf_op jit(solution)/shard_map/ppermute | solution.py:265
  471.5 36.0 %collective-permute-start.22 = (f32[3,64,1024]{2,1,0:T(8,128)}, f32[3,64,1024]{2,1,0:T(8,128)}, u32[]{:S(2)}, u32[]{:S(2)}) collective-permute-start(f32[3,64,1024]{2,1,0:T(8,128)} %constant_dynamic-slice_fusion.13), channel_id=1, source_target_pairs={{0,4},{4,0},{1,5},{5,1},{2,6},{6,2},{3,7},{7,3},{8,12},{12,8},{9,1... | collective-permute-start | bytes 2359304 | tf_op jit(solution)/shard_map/ppermute | solution.py:265
  473.6 16.9 %copy-start.22 = (f32[3,128,1024]{2,1,0:T(8,128)S(1)}, f32[3,128,1024]{2,1,0:T(8,128)}, u32[]{:S(2)}) copy-start(f32[3,128,1024]{2,1,0:T(8,128)} %copy-done.21) | copy-start | bytes 4718596
  475.0 32.5 %copy-start.20 = (f32[3,128,1024]{2,1,0:T(8,128)S(1)}, f32[3,128,1024]{2,1,0:T(8,128)}, u32[]{:S(2)}) copy-start(f32[3,128,1024]{2,1,0:T(8,128)} %dynamic-slice_add_fusion.1) | copy-start | bytes 4718596
  475.1 37.4 %collective-permute-start.37 = (f32[1,64,1024]{2,1,0:T(8,128)S(1)}, f32[1,64,1024]{2,1,0:T(8,128)S(1)}, u32[]{:S(2)}, u32[]{:S(2)}) collective-permute-start(f32[1,64,1024]{2,1,0:T(8,128)S(1)} %constant_dynamic-slice_fusion.6), channel_id=1, source_target_pairs={{0,4},{4,0},{1,5},{5,1},{2,6},{6,2},{3,7},{7,3},{8,12},{12,8},{9,1... | collective-permute-start | bytes 786440 | tf_op jit(solution)/shard_map/ppermute | solution.py:265
  490.7 23.4 %collective-permute-start.28 = (f32[3,32,1024]{2,1,0:T(8,128)S(1)}, f32[3,32,1024]{2,1,0:T(8,128)S(1)}, u32[]{:S(2)}, u32[]{:S(2)}) collective-permute-start(f32[3,32,1024]{2,1,0:T(8,128)S(1)} %constant_dynamic-slice_fusion.8), channel_id=1, source_target_pairs={{0,2},{2,0},{1,3},{3,1},{4,6},{6,4},{5,7},{7,5},{8,10},{10,8},{9,1... | collective-permute-start | bytes 1179656 | tf_op jit(solution)/shard_map/ppermute | solution.py:265
  508.8 40.5 %collective-permute-start.23 = (f32[3,32,1024]{2,1,0:T(8,128)S(1)}, f32[3,32,1024]{2,1,0:T(8,128)S(1)}, u32[]{:S(2)}, u32[]{:S(2)}) collective-permute-start(f32[3,32,1024]{2,1,0:T(8,128)S(1)} %constant_dynamic-slice_fusion.12), channel_id=1, source_target_pairs={{0,2},{2,0},{1,3},{3,1},{4,6},{6,4},{5,7},{7,5},{8,10},{10,8},{9,1... | collective-permute-start | bytes 1179656 | tf_op jit(solution)/shard_map/ppermute | solution.py:265
  512.5 9.2 %collective-permute-start.38 = (f32[1,32,1024]{2,1,0:T(8,128)S(1)}, f32[1,32,1024]{2,1,0:T(8,128)S(1)}, u32[]{:S(2)}, u32[]{:S(2)}) collective-permute-start(f32[1,32,1024]{2,1,0:T(8,128)S(1)} %constant_dynamic-slice_fusion.5), channel_id=1, source_target_pairs={{0,2},{2,0},{1,3},{3,1},{4,6},{6,4},{5,7},{7,5},{8,10},{10,8},{9,1... | collective-permute-start | bytes 393224 | tf_op jit(solution)/shard_map/ppermute | solution.py:265
  514.2 35.1 %collective-permute-start.29 = (f32[3,32,1024]{2,1,0:T(8,128)S(1)}, f32[3,32,1024]{2,1,0:T(8,128)S(1)}, u32[]{:S(2)}, u32[]{:S(2)}) collective-permute-start(f32[3,32,1024]{2,1,0:T(8,128)S(1)} %concatenate.97), channel_id=1, source_target_pairs={{8,0},{16,24},{9,1},{17,25},{10,2},{18,26},{11,3},{19,27},{12,4},{... | collective-permute-start | bytes 1179656 | tf_op jit(solution)/shard_map/ppermute | solution.py:448
  515.5 33.7 %collective-permute-start.39 = (f32[40,1024]{1,0:T(8,128)S(1)}, f32[40,1024]{1,0:T(8,128)S(1)}, u32[]{:S(2)}, u32[]{:S(2)}) collective-permute-start(f32[40,1024]{1,0:T(8,128)S(1)} %concatenate.100), channel_id=1, source_target_pairs={{8,0},{16,24},{9,1},{17,25},{10,2},{18,26},{11,3},{19,27},{12,4},{... | collective-permute-start | bytes 491528 | tf_op jit(solution)/shard_map/ppermute | solution.py:448
  549.2 7.2 %collective-permute-start.40 = (f32[40,1024]{1,0:T(8,128)S(1)}, f32[40,1024]{1,0:T(8,128)S(1)}, u32[]{:S(2)}, u32[]{:S(2)}) collective-permute-start(f32[40,1024]{1,0:T(8,128)S(1)} %get-tuple-element.142), channel_id=1, source_target_pairs={{0,8},{8,0},{16,24},{24,16},{1,9},{9,1},{17,25},{25,17},{2,10},{10... | collective-permute-start | bytes 491528 | tf_op jit(solution)/shard_map/ppermute | solution.py:443
  549.4 14.5 %collective-permute-start.30 = (f32[3,32,1024]{2,1,0:T(8,128)S(1)}, f32[3,32,1024]{2,1,0:T(8,128)S(1)}, u32[]{:S(2)}, u32[]{:S(2)}) collective-permute-start(f32[3,32,1024]{2,1,0:T(8,128)S(1)} %get-tuple-element.124), channel_id=1, source_target_pairs={{0,8},{8,0},{16,24},{24,16},{1,9},{9,1},{17,25},{25,17},{2,10},{10... | collective-permute-start | bytes 1179656 | tf_op jit(solution)/shard_map/ppermute | solution.py:443
  551.6 5.5 collective-permute-start.41
  556.4 9.8 %collective-permute-start.43 = (f32[40,1024]{1,0:T(8,128)S(1)}, f32[40,1024]{1,0:T(8,128)S(1)}, u32[]{:S(2)}, u32[]{:S(2)}) collective-permute-start(f32[40,1024]{1,0:T(8,128)S(1)} %pad_add_fusion.2), channel_id=1, source_target_pairs={{8,16},{16,8},{9,17},{17,9},{10,18},{18,10},{11,19},{19,11},{12,20... | collective-permute-start | bytes 491528 | tf_op jit(solution)/shard_map/ppermute | solution.py:445
  557.1 11.7 %collective-permute-start.42 = (f32[40,1024]{1,0:T(8,128)S(1)}, f32[40,1024]{1,0:T(8,128)S(1)}, u32[]{:S(2)}, u32[]{:S(2)}) collective-permute-start(f32[40,1024]{1,0:T(8,128)S(1)} %collective-permute-done.41), channel_id=1, source_target_pairs={{8,0},{16,24},{9,1},{17,25},{10,2},{18,26},{11,3},{19,27},{12,4},{... | collective-permute-start | bytes 491528 | tf_op jit(solution)/shard_map/ppermute | solution.py:446
  558.4 9.1 %collective-permute-start.31 = (f32[3,32,1024]{2,1,0:T(8,128)S(1)}, f32[3,32,1024]{2,1,0:T(8,128)S(1)}, u32[]{:S(2)}, u32[]{:S(2)}) collective-permute-start(f32[3,32,1024]{2,1,0:T(8,128)S(1)} %get-tuple-element.124), channel_id=1, source_target_pairs={{8,16},{16,8},{9,17},{17,9},{10,18},{18,10},{11,19},{19,11},{12,20... | collective-permute-start | bytes 1179656 | tf_op jit(solution)/shard_map/ppermute | solution.py:444
  564.0 4.9 collective-permute-start.33
  566.3 9.1 %collective-permute-start.44 = (f32[40,1024]{1,0:T(8,128)S(1)}, f32[40,1024]{1,0:T(8,128)S(1)}, u32[]{:S(2)}, u32[]{:S(2)}) collective-permute-start(f32[40,1024]{1,0:T(8,128)S(1)} %collective-permute-done.43), channel_id=1, source_target_pairs={{8,0},{16,24},{9,1},{17,25},{10,2},{18,26},{11,3},{19,27},{12,4},{... | collective-permute-start | bytes 491528 | tf_op jit(solution)/shard_map/ppermute | solution.py:447
  567.6 18.3 %collective-permute-start.32 = (f32[3,32,1024]{2,1,0:T(8,128)S(1)}, f32[3,32,1024]{2,1,0:T(8,128)S(1)}, u32[]{:S(2)}, u32[]{:S(2)}) collective-permute-start(f32[3,32,1024]{2,1,0:T(8,128)S(1)} %collective-permute-done.31), channel_id=1, source_target_pairs={{8,0},{16,24},{9,1},{17,25},{10,2},{18,26},{11,3},{19,27},{12,4},{... | collective-permute-start | bytes 1179656 | tf_op jit(solution)/shard_map/ppermute | solution.py:446
  568.9 22.0 %collective-permute-start.34 = (f32[3,32,1024]{2,1,0:T(8,128)S(1)}, f32[3,32,1024]{2,1,0:T(8,128)S(1)}, u32[]{:S(2)}, u32[]{:S(2)}) collective-permute-start(f32[3,32,1024]{2,1,0:T(8,128)S(1)} %collective-permute-done.33), channel_id=1, source_target_pairs={{8,0},{16,24},{9,1},{17,25},{10,2},{18,26},{11,3},{19,27},{12,4},{... | collective-permute-start | bytes 1179656 | tf_op jit(solution)/shard_map/ppermute | solution.py:447
  600.5 3.0 collective-permute-start.45
  604.9 14.7 %collective-permute-start.46 = (f32[1,2,1,4,136,128]{5,4,3,2,1,0:T(8,128)S(1)}, f32[1,2,1,4,136,128]{5,4,3,2,1,0:T(8,128)S(1)}, u32[]{:S(2)}, u32[]{:S(2)}) collective-permute-start(f32[1,2,1,4,136,128]{5,4,3,2,1,0:T(8,128)S(1)} %constant_dynamic-slice_fusion.3), channel_id=1, source_target_pairs={{0,4},{4,0},{1,5},{5,1},{2,6},{6,2},{3,7},{7,3},{8,12},{12,8},{9,1... | collective-permute-start | bytes 1671176 | tf_op jit(solution)/shard_map/ppermute | solution.py:265
  619.7 7.9 %collective-permute-start.47 = (f32[1,1,1,4,136,128]{5,4,3,2,1,0:T(8,128)S(1)}, f32[1,1,1,4,136,128]{5,4,3,2,1,0:T(8,128)S(1)}, u32[]{:S(2)}, u32[]{:S(2)}) collective-permute-start(f32[1,1,1,4,136,128]{5,4,3,2,1,0:T(8,128)S(1)} %constant_dynamic-slice_fusion.2), channel_id=1, source_target_pairs={{0,2},{2,0},{1,3},{3,1},{4,6},{6,4},{5,7},{7,5},{8,10},{10,8},{9,1... | collective-permute-start | bytes 835592 | tf_op jit(solution)/shard_map/ppermute | solution.py:265
  (15 other events, 31.6 us)

commit v12 on v9

--- a/solution.py
+++ b/solution.py
@@ -389,21 +389,23 @@
     known = [both_of(x)] + [lax.ppermute(both_of(o), "x", r) for o, r in zip(others, row_routes)]
     listed = [pairs] + [lax.ppermute(pairs, "x", route) for route in row_routes]
     masks, guest_masks = [m[0] for m in known], [m[1][:, kept:] for m in known]
-    groups = []
+    ends, middle = Lane(), Lane()
+    near, mid, far, groups = [], [], [], []
     for c in range(3):
+        if c == 2:
+            over_x.arrived = over_x.arrived + near[:1]
         got = over_x.send([planes_of(o, c) for o in others], "x", row_routes)
         groups.append(in_row_order([planes_of(x, c)] + got, 1))
         if c == 0:
             over_x.arrived = got + known[1:] + listed[1:]
+        if c < 2:
+            near += ends.send([groups[c]], "z", [NEAR])
+            mid += middle.send([groups[c]], "z", [MIDDLE])
     tiles = [None] * 3
     for c in (0, 2, 1):
         tiles[c] = over_x.send([packed(o, c, groups[0]) for o in others], "x", row_routes)
 
-    ends, middle = Lane(), Lane()
-    near, mid, far = [], [], []
-    for c in range(2):
-        near += ends.send([groups[c]], "z", [NEAR])
-        mid += middle.send([groups[c]], "z", [MIDDLE])
+    middle.arrived = mid[1:] + near[1:]
     inward, outward = Lane(near[1:]), Lane(near[1:])
     for c in range(2):
         far += middle.send([near[c]], "z", [MIDDLE])
@@ -435,10 +437,11 @@
     part1 += [times(1, [tiles[1][k - 1]], [k], early_groups[1], [0]) for k in range(1, wide)]
     first_three = part0 + part2 + in_row_order(part1, 2)
 
-    end2 = times(2, [hist] + tiles[2], every, [[far[2]]], row_places)
-    end1 = times(1, [hist] + tiles[1], every, [[far[1], outer[2]]], row_places)
-    end0 = times(0, [hist] + tiles[0], every, [[far[0], outer[3]]], row_places)
-    last_one = end0 + (end1 + end2)
+    def end(c, held, later):
+        own = [m[:, cuts[c] : cuts[c + 1]] for m in masks]
+        return product([hist] + tiles[c], own, [held], after(inner, later), x * columns + cuts[c], row_places)
+
+    first_three = scatter_sum(first_three, "core", 1)
     guest = jnp.concatenate([guest, product([loans[0]], [guest_masks[0]], [[far[2]]], inner, 0, [0])])
     visitors = in_row_order(
         [guest]
@@ -448,15 +451,19 @@
         ],
         2,
     )
-
-    def summed(totals):
-        return scatter_sum(scatter_sum(scatter_sum(totals, "core", 1), "x", 1), "y", 1)
-
-    first_three = summed(first_three)
-    visitors = lax.ppermute(summed(visitors), "z", OUTWARD)
+    visitors = scatter_sum(visitors, "core", 1)
+    end1 = end(1, [far[1], outer[2]], first_three)
+    end2 = end(2, [far[2]], visitors)
+    first_three = scatter_sum(first_three, "x", 1)
+    end0 = end(0, [far[0], outer[3]], first_three)
+    last_one = end0 + (end1 + end2)
+    visitors = scatter_sum(visitors, "x", 1)
+    first_three, visitors = scatter_sum(first_three, "y", 1), scatter_sum(visitors, "y", 1)
+    last_one = scatter_sum(scatter_sum(scatter_sum(last_one, "core", 1), "x", 1), "y", 1)
+    visitors = lax.ppermute(visitors, "z", OUTWARD)
     early = first_three.at[1:].add(visitors[:2])
     early = jnp.stack(along_line(early, inner))
-    last_one = summed(last_one)[0] + visitors[2]
+    last_one = last_one[0] + visitors[2]
     flags = jnp.full((8, last_one.shape[1]), over.astype(jnp.float32))
     late = jnp.stack(along_line(jnp.concatenate([last_one, flags]), inner))
 

time: 607 us -> 625 us (1.030)
  starting transfers between devices: 82.3 us -> 106 us
  waiting for transfers between devices: 309 us -> 291 us
  local copies, waits for them, and re-layouts: 22.8 us -> 31 us
    ppermute x21, starting transfers between devices: 51.9 us -> 77.1 us  [send(): lax.ppermute(v, axis, route)]
    ppermute x21, waiting for transfers between devices: 205 us -> 196 us  [send(): lax.ppermute(v, axis, route)]
    ppermute x12, waiting for transfers between devices: 51.2 us -> 44.6 us  [scatter_sum(): total = total + lax.ppermute(part((here + k) % count), axis, turn(count, k))]
    unnamed x42 -> x60, local copies, waits for them, and re-layouts: 9.34 us -> 15.1 us
  transfers between devices with their start and end apart: 47 -> 47, of which waited for: 22 -> 23; matrix products, arithmetic and copies ran while one was open for 6% -> 6% of each run, Pallas kernels for 23% -> 22%
where the time goes in v12:
time: 625 us; the launch traced here: 622 us
  waiting for transfers between devices  291 us (47%)
  Pallas kernels  147 us (24%)
  starting transfers between devices  106 us (17%)
  local copies, waits for them, and re-layouts  31 us (5%)
  other arithmetic  27.1 us (4%)
  between operations  19.1 us (3%)
    ppermute x21, waiting for transfers between devices, send(): lax.ppermute(v, axis, route)  196 us
    pallas_call x10, Pallas kernels, product(): pl.pallas_call(functools.partial(product_kernel, blk, row_blocks, columns...  121 us
    ppermute x21, starting transfers between devices, send(): lax.ppermute(v, axis, route)  77.1 us
    ppermute x12, waiting for transfers between devices, scatter_sum(): total = total + lax.ppermute(part((here + k) % count), axis, turn(count, k))  44.6 us
    ppermute x1, waiting for transfers between devices, body(): lax.ppermute(both_of(o), 'x', r)  20.9 us
    pallas_call x4, Pallas kernels, pack(): pl.pallas_call(functools.partial(pack_kernel, blk, row_blocks, columns, s...  17.3 us
    unnamed x60, local copies, waits for them, and re-layouts  15.1 us
  transfers between devices with their start and end apart: 47, of which 23 were waited for; matrix products, arithmetic and copies ran while one was open for 6% of the time, Pallas kernels for 22%

profile of v12, /device:TPU:0, one launch (start us, length us, event | category | flops | bytes accessed | tf_op | source)
XLA Modules:
  0.0 622.0 jit_solution(7869632324071169011)
XLA Ops:
  6.5 2.9 collective-permute-start
  10.2 3.5 collective-permute-start.1
  13.7 2.3 constant_dynamic-slice_fusion.16
  18.0 1.7 constant_dynamic-slice_fusion.14
  19.7 20.9 %collective-permute-done.2 = s32[2,4,128]{2,1,0:T(4,128)S(1)} collective-permute-done((s32[2,4,128]{2,1,0:T(4,128)S(1)}, s32[2,4,128]{2,1,0:T(4,128)S(1)}, u32[]{:S(2)}, u32[]{:S(2)}) %collective-permute-start.2) | collective-permute-done | bytes 4128 | tf_op jit(solution)/shard_map/ppermute | solution.py:389
  41.1 1.6 broadcast_select_fusion.5
  43.1 2.0 collective-permute-start.8
  45.1 38.7 %collective-permute-done.4 = bf16[7680,128]{1,0:T(8,128)(2,1)} collective-permute-done((bf16[7680,128]{1,0:T(8,128)(2,1)S(1)}, bf16[7680,128]{1,0:T(8,128)(2,1)}, u32[]{:S(2)}, u32[]{:S(2)}) %collective-permute-start.4) | collective-permute-done | bytes 1966112 | tf_op jit(solution)/shard_map/ppermute | solution.py:301
  83.8 2.9 broadcast_select_fusion.1
  86.7 2.4 pad_maximum_fusion.refs_1_
  89.1 2.7 collective-permute-start.14
  93.1 1.6 collective-permute-start.6
  94.9 3.9 pack_tiles.4
  98.8 20.3 %collective-permute-done.6 = bf16[4608,128]{1,0:T(8,128)(2,1)} collective-permute-done((bf16[4608,128]{1,0:T(8,128)(2,1)S(1)}, bf16[4608,128]{1,0:T(8,128)(2,1)}, u32[]{:S(2)}, u32[]{:S(2)}) %collective-permute-start.6) | collective-permute-done | bytes 1179680 | tf_op jit(solution)/shard_map/ppermute | solution.py:301
  120.6 53.1 %collective-permute-done.9.refs_2_ = bf16[7680,256]{1,0:T(8,128)(2,1)} collective-permute-done((bf16[7680,256]{1,0:T(8,128)(2,1)}, bf16[7680,256]{1,0:T(8,128)(2,1)}, u32[]{:S(2)}, u32[]{:S(2)}) %collective-permute-start.9) | collective-permute-done | bytes 3932192 | tf_op jit(solution)/shard_map/ppermute | solution.py:301
  173.7 2.0 collective-permute-start.15
  176.0 4.1 pack_tiles.5
  180.2 4.3 collective-permute-done.7.refs_1_
  184.5 1.6 copy-done.5
  189.0 2.6 collective-permute-start.16
  191.7 4.1 pack_tiles.6
  195.8 39.6 %collective-permute-start.12 = (bf16[104,128,128]{2,1,0:T(8,128)(2,1)}, bf16[104,128,128]{2,1,0:T(8,128)(2,1)}, u32[]{:S(2)}, u32[]{:S(2)}) collective-permute-start(bf16[104,128,128]{2,1,0:T(8,128)(2,1)} %pack_tiles.6), channel_id=1, source_target_pairs={{0,8},{24,16},{1,9},{25,17},{2,10},{26,18},{3,11},{27,19},{4,12},{... | collective-permute-start | bytes 10223624 | tf_op jit(solution)/shard_map/ppermute | solution.py:301
  237.1 5.2 pack_tiles.7
  242.4 17.5 %collective-permute-done.11.refs_1_ = bf16[104,128,128]{2,1,0:T(8,128)(2,1)S(1)} collective-permute-done((bf16[104,128,128]{2,1,0:T(8,128)(2,1)}, bf16[104,128,128]{2,1,0:T(8,128)(2,1)S(1)}, u32[]{:S(2)}, u32[]{:S(2)}) %collective-permute-start.11) | collective-permute-done | bytes 3407904 | tf_op jit(solution)/shard_map/ppermute | solution.py:301
  261.2 2.1 broadcast_select_fusion.3
  263.6 39.9 %collective-permute-done.12.refs_0_ = bf16[104,128,128]{2,1,0:T(8,128)(2,1)} collective-permute-done((bf16[104,128,128]{2,1,0:T(8,128)(2,1)}, bf16[104,128,128]{2,1,0:T(8,128)(2,1)}, u32[]{:S(2)}, u32[]{:S(2)}) %collective-permute-start.12) | collective-permute-done | bytes 3407904 | tf_op jit(solution)/shard_map/ppermute | solution.py:301
  303.5 5.8 collective-permute-start.13
  309.4 2.1 collective-permute-start.17
  312.4 1.9 copy-done.6
  314.3 1.6 copy-done.9
  315.9 14.2 %tiles_times_planes.10 = f32[3,256,1024]{2,1,0:T(8,128)S(1)} custom-call(s32[260]{0:T(512)S(1)} %concatenate.67.info, bf16[512,32768]{1,0:T(8,128)(2,1)} %refs_0_.11, bf16[94,128,128]{2,1,0:T(8,128)(2,1)S(1)} %copy-done.6, bf16[4096,256]{1,0:T(8,128)(2,1)S(1)} %copy-done.9, bf16[4096,256]{1,0:T(8,128)(2,1)} %collective-permute-done.5.refs_3_, ...), custom_call_target="tpu_custom_call" | custom-call | flops 6442450944 | bytes 10485760 | tf_op jit(solution)/shard_map/tiles_times_planes/pallas_call | solution.py:205
  330.1 1.7 copy-done.3
  333.8 20.7 %collective-permute-done.13.refs_3_ = bf16[4608,256]{1,0:T(8,128)(2,1)} collective-permute-done((bf16[4608,256]{1,0:T(8,128)(2,1)S(1)}, bf16[4608,256]{1,0:T(8,128)(2,1)}, u32[]{:S(2)}, u32[]{:S(2)}) %collective-permute-start.13) | collective-permute-done | bytes 2359328 | tf_op jit(solution)/shard_map/ppermute | solution.py:301
  354.6 6.2 collective-permute-start.23
  360.8 17.5 %tiles_times_planes.13 = f32[3,256,512]{2,1,0:T(8,128)S(1)} custom-call(s32[243]{0:T(256)S(1)} %pad_add_fusion.8.info, bf16[512,32768]{1,0:T(8,128)(2,1)} %refs_0_.11, bf16[7680,256]{1,0:T(8,128)(2,1)} %pad_maximum_fusion.refs_1_, bf16[7680,256]{1,0:T(8,128)(2,1)} %collective-permute-done.9.refs_2_, bf16[7680,256]{1,0:T(8,128)(2,1)} %collective-permute-done.14.refs_3_, ...), custom_call_target="tpu_custom_call" | custom-call | flops 6039797760 | bytes 15728640 | tf_op jit(solution)/shard_map/tiles_times_planes/pallas_call | solution.py:205
  378.2 2.1 collective-permute-start.24
  380.3 15.7 %tiles_times_planes.11 = f32[3,256,1024]{2,1,0:T(8,128)S(1)} custom-call(s32[292]{0:T(512)S(1)} %concatenate.71.info, bf16[512,32768]{1,0:T(8,128)(2,1)} %refs_0_.11, bf16[104,128,128]{2,1,0:T(8,128)(2,1)S(1)} %copy-done.1, bf16[4608,256]{1,0:T(8,128)(2,1)S(1)} %pad_maximum_fusion.1.refs_2_.refs_1_, bf16[4608,256]{1,0:T(8,128)(2,1)} %collective-permute-done.13.refs_3_, ...), custom_call_target="tpu_custom_call" | custom-call | flops 7247757312 | bytes 11796480 | tf_op jit(solution)/shard_map/tiles_times_planes/pallas_call | solution.py:205
  396.1 15.1 %tiles_times_planes.12 = f32[3,256,512]{2,1,0:T(8,128)S(1)} custom-call(s32[243]{0:T(256)S(1)} %pad_add_fusion.5.info, bf16[160,128,128]{2,1,0:T(8,128)(2,1)} %collective-permute-done.18.refs_0_.refs_1_, bf16[7680,256]{1,0:T(8,128)(2,1)} %pad_maximum_fusion.refs_1_, bf16[7680,256]{1,0:T(8,128)(2,1)} %collective-permute-done.9.refs_2_, ...), custom_call_target="tpu_custom_call" | custom-call | flops 6039797760 | bytes 15728640 | tf_op jit(solution)/shard_map/tiles_times_planes/pallas_call | solution.py:205
  411.5 1.5 copy-done.4
  414.3 1.7 copy-done.19
  421.9 8.1 %tiles_times_planes.15 = f32[2,256,512]{2,1,0:T(8,128)S(1)} custom-call(s32[147]{0:T(256)S(1)} %get-tuple-element.161.info, bf16[104,128,128]{2,1,0:T(8,128)(2,1)} %collective-permute-done.12.refs_0_, bf16[4608,256]{1,0:T(8,128)(2,1)S(1)} %pad_maximum_fusion.1.refs_2_.refs_1_, bf16[4608,256]{1,0:T(8,128)(2,1)} %collective-permute-done.17.refs_4_.refs_2_), custom_call_target="tpu_custom_call" | custom-call | flops 2415919104 | bytes 7077888 | tf_op jit(solution)/shard_map/tiles_times_planes/pallas_call | solution.py:205
  431.4 9.4 %tiles_times_planes.14 = f32[3,256,512]{2,1,0:T(8,128)S(1)} custom-call(s32[147]{0:T(256)S(1)} %get-tuple-element.162.info, bf16[104,128,128]{2,1,0:T(8,128)(2,1)} %collective-permute-done.23.refs_0_, bf16[4608,256]{1,0:T(8,128)(2,1)S(1)} %pad_maximum_fusion.1.refs_2_.refs_1_, bf16[4608,256]{1,0:T(8,128)(2,1)} %collective-permute-done.17.refs_4_.refs_2_, ...), custom_call_target="tpu_custom_call" | custom-call | flops 3623878656 | bytes 9437184 | tf_op jit(solution)/shard_map/tiles_times_planes/pallas_call | solution.py:205
  440.8 7.1 %tiles_times_planes.16 = f32[1,256,512]{2,1,0:T(8,128)S(1)} custom-call(s32[147]{0:T(256)S(1)} %get-tuple-element.161.info, bf16[104,128,128]{2,1,0:T(8,128)(2,1)} %collective-permute-done.12.refs_0_, bf16[4608,256]{1,0:T(8,128)(2,1)} %collective-permute-done.24.refs_3_.refs_1_.refs_2_), custom_call_target="tpu_custom_call" | custom-call | flops 1207959552 | bytes 4718592 | tf_op jit(solution)/shard_map/tiles_times_planes/pallas_call | solution.py:205
  452.1 1.7 dynamic-slice_add_fusion
  459.4 15.0 %tiles_times_planes.18 = f32[1,256,1024]{2,1,0:T(8,128)S(1)} custom-call(s32[484]{0:T(512)S(1)} %concatenate.84.info, bf16[512,32768]{1,0:T(8,128)(2,1)} %refs_0_.11, bf16[160,128,128]{2,1,0:T(8,128)(2,1)} %collective-permute-done.18.refs_0_.refs_1_, bf16[7680,256]{1,0:T(8,128)(2,1)} %collective-permute-done.16.refs_2_, ...), custom_call_target="tpu_custom_call" | custom-call | flops 4026531840 | bytes 11796480 | tf_op jit(solution)/shard_map/tiles_times_planes/pallas_call | solution.py:205
  476.1 2.1 dynamic-slice_add_fusion.3
  478.4 2.0 collective-permute-done.35.refs_3_
  480.3 8.8 %tiles_times_planes.17 = f32[1,256,1024]{2,1,0:T(8,128)S(1)} custom-call(s32[260]{0:T(512)S(1)} %concatenate.83.info, bf16[512,32768]{1,0:T(8,128)(2,1)} %refs_0_.11, bf16[94,128,128]{2,1,0:T(8,128)(2,1)S(1)} %copy-done.7, bf16[4096,256]{1,0:T(8,128)(2,1)} %collective-permute-done.15.refs_2_, bf16[4096,256]{1,0:T(8,128)(2,1)} %collective-permute-done.35.refs_3_), custom_call_target="tpu_custom_call" | custom-call | flops 2147483648 | bytes 6291456 | tf_op jit(solution)/shard_map/tiles_times_planes/pallas_call | solution.py:205
  489.2 2.1 fusion.6
  494.2 9.8 %tiles_times_planes.19 = f32[1,256,1024]{2,1,0:T(8,128)S(1)} custom-call(s32[292]{0:T(512)S(1)} %concatenate.85.info, bf16[512,32768]{1,0:T(8,128)(2,1)} %refs_0_.11, bf16[104,128,128]{2,1,0:T(8,128)(2,1)S(1)} %copy-done.2, bf16[4608,256]{1,0:T(8,128)(2,1)} %collective-permute-done.24.refs_3_.refs_1_.refs_2_), custom_call_target="tpu_custom_call" | custom-call | flops 2415919104 | bytes 7077888 | tf_op jit(solution)/shard_map/tiles_times_planes/pallas_call | solution.py:205
  505.9 6.4 %collective-permute-done.26 = f32[3,64,1024]{2,1,0:T(8,128)} collective-permute-done((f32[3,64,1024]{2,1,0:T(8,128)}, f32[3,64,1024]{2,1,0:T(8,128)}, u32[]{:S(2)}, u32[]{:S(2)}) %collective-permute-start.26) | collective-permute-done | bytes 786464 | tf_op jit(solution)/shard_map/ppermute | solution.py:286
  513.6 1.5 collective-permute-start.27
  518.3 7.4 %collective-permute-done.27 = f32[3,32,1024]{2,1,0:T(8,128)S(1)} collective-permute-done((f32[3,32,1024]{2,1,0:T(8,128)S(1)}, f32[3,32,1024]{2,1,0:T(8,128)S(1)}, u32[]{:S(2)}, u32[]{:S(2)}) %collective-permute-start.27) | collective-permute-done | bytes 393248 | tf_op jit(solution)/shard_map/ppermute | solution.py:286
  527.1 5.1 collective-permute-done.22
  533.8 2.1 collective-permute-done.28
  537.4 2.7 collective-permute-start.39
  540.8 6.6 %collective-permute-done.39 = f32[40,1024]{1,0:T(8,128)S(1)} collective-permute-done((f32[40,1024]{1,0:T(8,128)S(1)}, f32[40,1024]{1,0:T(8,128)S(1)}, u32[]{:S(2)}, u32[]{:S(2)}) %collective-permute-start.39) | collective-permute-done | bytes 163872 | tf_op jit(solution)/shard_map/ppermute | solution.py:306
  557.0 6.8 %collective-permute-done.43 = f32[40,1024]{1,0:T(8,128)S(1)} collective-permute-done((f32[40,1024]{1,0:T(8,128)S(1)}, f32[40,1024]{1,0:T(8,128)S(1)}, u32[]{:S(2)}, u32[]{:S(2)}) %collective-permute-start.43) | collective-permute-done | bytes 163872 | tf_op jit(solution)/shard_map/ppermute | solution.py:310
  563.9 8.2 %collective-permute-done.31 = f32[3,32,1024]{2,1,0:T(8,128)S(1)} collective-permute-done((f32[3,32,1024]{2,1,0:T(8,128)S(1)}, f32[3,32,1024]{2,1,0:T(8,128)S(1)}, u32[]{:S(2)}, u32[]{:S(2)}) %collective-permute-start.31) | collective-permute-done | bytes 393248 | tf_op jit(solution)/shard_map/ppermute | solution.py:309
  572.2 4.2 collective-permute-done.33
  576.5 9.3 %pair_dots.1 = f32[32,136,128]{2,1,0:T(8,128)S(1)} custom-call(s32[2,6,32]{2,1,0:T(8,128)S(1)} %pad_add_fusion.ids, f32[4,3,32,1024]{3,2,1,0:T(8,128)S(1)} %pad_maximum_fusion.4.early, f32[4,40,1024]{2,1,0:T(8,128)S(1)} %pad_maximum_fusion.5.late), custom_call_target="tpu_custom_call" | custom-call | tf_op jit(solution)/shard_map/pair_dots/pallas_call | solution.py:262
  586.0 2.9 collective-permute-done.44
  590.4 14.6 %collective-permute-done.45 = f32[1,2,1,4,136,128]{5,4,3,2,1,0:T(8,128)S(1)} collective-permute-done((f32[1,2,1,4,136,128]{5,4,3,2,1,0:T(8,128)S(1)}, f32[1,2,1,4,136,128]{5,4,3,2,1,0:T(8,128)S(1)}, u32[]{:S(2)}, u32[]{:S(2)}) %collective-permute-start.45) | collective-permute-done | bytes 557088 | tf_op jit(solution)/shard_map/ppermute | solution.py:286
  605.9 7.1 %collective-permute-done.46 = f32[1,1,1,4,136,128]{5,4,3,2,1,0:T(8,128)S(1)} collective-permute-done((f32[1,1,1,4,136,128]{5,4,3,2,1,0:T(8,128)S(1)}, f32[1,1,1,4,136,128]{5,4,3,2,1,0:T(8,128)S(1)}, u32[]{:S(2)}, u32[]{:S(2)}) %collective-permute-start.46) | collective-permute-done | bytes 278560 | tf_op jit(solution)/shard_map/ppermute | solution.py:286
  (224 shorter events, 61.2 us)
Async XLA Ops:
  6.5 13.1 %collective-permute-start = (s32[16,2]{0,1:T(2,128)}, s32[16,2]{0,1:T(2,128)S(1)}, u32[]{:S(2)}, u32[]{:S(2)}) collective-permute-start(s32[16,2]{0,1:T(2,128)} %param.12), channel_id=1, source_target_pairs={{0,4},{4,0},{1,5},{5,1},{2,6},{6,2},{3,7},{7,3},{8,12},{12,8},{9,1... | collective-permute-start | bytes 392 | tf_op jit(solution)/shard_map/ppermute | solution.py:390
  10.2 6.3 %collective-permute-start.1 = (s32[4,256]{1,0:T(4,128)S(1)}, s32[4,256]{1,0:T(4,128)S(1)}, u32[]{:S(2)}, u32[]{:S(2)}) collective-permute-start(s32[4,256]{1,0:T(4,128)S(1)} %get-tuple-element.158), channel_id=1, source_target_pairs={{0,8},{24,16},{1,9},{25,17},{2,10},{26,18},{3,11},{27,19},{4,12},{... | collective-permute-start | bytes 12296 | tf_op jit(solution)/shard_map/ppermute | solution.py:384
  16.0 24.6 %collective-permute-start.3 = (bf16[4096,128]{1,0:T(8,128)(2,1)}, bf16[4096,128]{1,0:T(8,128)(2,1)S(1)}, u32[]{:S(2)}, u32[]{:S(2)}) collective-permute-start(bf16[4096,128]{1,0:T(8,128)(2,1)} %constant_dynamic-slice_fusion.16), channel_id=1, source_target_pairs={{0,4},{4,0},{1,5},{5,1},{2,6},{6,2},{3,7},{7,3},{8,12},{12,8},{9,1... | collective-permute-start | bytes 3145736 | tf_op jit(solution)/shard_map/ppermute | solution.py:301
  16.5 24.1 %collective-permute-start.2 = (s32[2,4,128]{2,1,0:T(4,128)S(1)}, s32[2,4,128]{2,1,0:T(4,128)S(1)}, u32[]{:S(2)}, u32[]{:S(2)}) collective-permute-start(s32[2,4,128]{2,1,0:T(4,128)S(1)} %get-tuple-element.150), channel_id=1, source_target_pairs={{0,4},{4,0},{1,5},{5,1},{2,6},{6,2},{3,7},{7,3},{8,12},{12,8},{9,1... | collective-permute-start | bytes 12296 | tf_op jit(solution)/shard_map/ppermute | solution.py:389
  19.7 23.1 %copy-start.29 = (s32[16,2]{0,1:T(2,128)}, s32[16,2]{0,1:T(2,128)S(1)}, u32[]{:S(2)}) copy-start(s32[16,2]{0,1:T(2,128)S(1)} %collective-permute-done) | copy-start | bytes 388
  40.6 43.2 %collective-permute-start.4 = (bf16[7680,128]{1,0:T(8,128)(2,1)S(1)}, bf16[7680,128]{1,0:T(8,128)(2,1)}, u32[]{:S(2)}, u32[]{:S(2)}) collective-permute-start(bf16[7680,128]{1,0:T(8,128)(2,1)S(1)} %constant_dynamic-slice_fusion.14), channel_id=1, source_target_pairs={{0,4},{4,0},{1,5},{5,1},{2,6},{6,2},{3,7},{7,3},{8,12},{12,8},{9,1... | collective-permute-start | bytes 5898248 | tf_op jit(solution)/shard_map/ppermute | solution.py:301
  43.0 43.7 %copy-start.8 = (bf16[4096,256]{1,0:T(8,128)(2,1)}, bf16[4096,256]{1,0:T(8,128)(2,1)S(1)}, u32[]{:S(2)}) copy-start(bf16[4096,256]{1,0:T(8,128)(2,1)S(1)} %pad_maximum_fusion.2.refs_2_) | copy-start | bytes 6291460
  43.0 46.0 %collective-permute-start.5 = (bf16[4096,256]{1,0:T(8,128)(2,1)S(1)}, bf16[4096,256]{1,0:T(8,128)(2,1)}, u32[]{:S(2)}, u32[]{:S(2)}) collective-permute-start(bf16[4096,256]{1,0:T(8,128)(2,1)S(1)} %pad_maximum_fusion.2.refs_2_), channel_id=1, source_target_pairs={{0,8},{8,0},{16,24},{24,16},{1,9},{9,1},{17,25},{25,17},{2,10},{10... | collective-permute-start | bytes 6291464 | tf_op jit(solution)/shard_map/ppermute | solution.py:301
  43.1 46.0 %collective-permute-start.8 = (bf16[4096,256]{1,0:T(8,128)(2,1)S(1)}, bf16[4096,256]{1,0:T(8,128)(2,1)}, u32[]{:S(2)}, u32[]{:S(2)}) collective-permute-start(bf16[4096,256]{1,0:T(8,128)(2,1)S(1)} %pad_maximum_fusion.2.refs_2_), channel_id=1, source_target_pairs={{8,16},{16,8},{9,17},{17,9},{10,18},{18,10},{11,19},{19,11},{12,20... | collective-permute-start | bytes 6291464 | tf_op jit(solution)/shard_map/ppermute | solution.py:301
  89.0 84.6 %collective-permute-start.9 = (bf16[7680,256]{1,0:T(8,128)(2,1)}, bf16[7680,256]{1,0:T(8,128)(2,1)}, u32[]{:S(2)}, u32[]{:S(2)}) collective-permute-start(bf16[7680,256]{1,0:T(8,128)(2,1)} %pad_maximum_fusion.refs_1_), channel_id=1, source_target_pairs={{0,8},{8,0},{16,24},{24,16},{1,9},{9,1},{17,25},{25,17},{2,10},{10... | collective-permute-start | bytes 11796488 | tf_op jit(solution)/shard_map/ppermute | solution.py:301
  89.1 84.6 %collective-permute-start.14 = (bf16[7680,256]{1,0:T(8,128)(2,1)}, bf16[7680,256]{1,0:T(8,128)(2,1)}, u32[]{:S(2)}, u32[]{:S(2)}) collective-permute-start(bf16[7680,256]{1,0:T(8,128)(2,1)} %pad_maximum_fusion.refs_1_), channel_id=1, source_target_pairs={{8,16},{16,8},{9,17},{17,9},{10,18},{18,10},{11,19},{19,11},{12,20... | collective-permute-start | bytes 11796488 | tf_op jit(solution)/shard_map/ppermute | solution.py:301
  93.1 26.0 %collective-permute-start.6 = (bf16[4608,128]{1,0:T(8,128)(2,1)S(1)}, bf16[4608,128]{1,0:T(8,128)(2,1)}, u32[]{:S(2)}, u32[]{:S(2)}) collective-permute-start(bf16[4608,128]{1,0:T(8,128)(2,1)S(1)} %constant_dynamic-slice_fusion.15), channel_id=1, source_target_pairs={{0,4},{4,0},{1,5},{5,1},{2,6},{6,2},{3,7},{7,3},{8,12},{12,8},{9,1... | collective-permute-start | bytes 3538952 | tf_op jit(solution)/shard_map/ppermute | solution.py:301
  119.1 65.4 %collective-permute-start.7 = (bf16[94,128,128]{2,1,0:T(8,128)(2,1)}, bf16[94,128,128]{2,1,0:T(8,128)(2,1)S(1)}, u32[]{:S(2)}, u32[]{:S(2)}) collective-permute-start(bf16[94,128,128]{2,1,0:T(8,128)(2,1)} %pack_tiles.4), channel_id=1, source_target_pairs={{0,4},{4,0},{1,5},{5,1},{2,6},{6,2},{3,7},{7,3},{8,12},{12,8},{9,1... | collective-permute-start | bytes 9240584 | tf_op jit(solution)/shard_map/ppermute | solution.py:301
  173.7 15.4 %collective-permute-start.15 = (bf16[4096,256]{1,0:T(8,128)(2,1)}, bf16[4096,256]{1,0:T(8,128)(2,1)}, u32[]{:S(2)}, u32[]{:S(2)}) collective-permute-start(bf16[4096,256]{1,0:T(8,128)(2,1)} %collective-permute-done.5.refs_3_), channel_id=1, source_target_pairs={{8,16},{16,8},{9,17},{17,9},{10,18},{18,10},{11,19},{19,11},{12,20... | collective-permute-start | bytes 6291464 | tf_op jit(solution)/shard_map/ppermute | solution.py:301
  186.1 73.8 %collective-permute-start.11 = (bf16[104,128,128]{2,1,0:T(8,128)(2,1)}, bf16[104,128,128]{2,1,0:T(8,128)(2,1)S(1)}, u32[]{:S(2)}, u32[]{:S(2)}) collective-permute-start(bf16[104,128,128]{2,1,0:T(8,128)(2,1)} %pack_tiles.5), channel_id=1, source_target_pairs={{0,4},{4,0},{1,5},{5,1},{2,6},{6,2},{3,7},{7,3},{8,12},{12,8},{9,1... | collective-permute-start | bytes 10223624 | tf_op jit(solution)/shard_map/ppermute | solution.py:301
  187.4 48.1 %collective-permute-start.10 = (bf16[4096,256]{1,0:T(8,128)(2,1)}, bf16[4096,256]{1,0:T(8,128)(2,1)}, u32[]{:S(2)}, u32[]{:S(2)}) collective-permute-start(bf16[4096,256]{1,0:T(8,128)(2,1)} %collective-permute-done.8.refs_4_), channel_id=1, source_target_pairs={{8,0},{16,24},{9,1},{17,25},{10,2},{18,26},{11,3},{19,27},{12,4},{... | collective-permute-start | bytes 6291464 | tf_op jit(solution)/shard_map/ppermute | solution.py:301
  189.0 120.3 %collective-permute-start.16 = (bf16[7680,256]{1,0:T(8,128)(2,1)}, bf16[7680,256]{1,0:T(8,128)(2,1)}, u32[]{:S(2)}, u32[]{:S(2)}) collective-permute-start(bf16[7680,256]{1,0:T(8,128)(2,1)} %collective-permute-done.9.refs_2_), channel_id=1, source_target_pairs={{8,16},{16,8},{9,17},{17,9},{10,18},{18,10},{11,19},{19,11},{12,20... | collective-permute-start | bytes 11796488 | tf_op jit(solution)/shard_map/ppermute | solution.py:301
  195.8 107.6 %collective-permute-start.12 = (bf16[104,128,128]{2,1,0:T(8,128)(2,1)}, bf16[104,128,128]{2,1,0:T(8,128)(2,1)}, u32[]{:S(2)}, u32[]{:S(2)}) collective-permute-start(bf16[104,128,128]{2,1,0:T(8,128)(2,1)} %pack_tiles.6), channel_id=1, source_target_pairs={{0,8},{24,16},{1,9},{25,17},{2,10},{26,18},{3,11},{27,19},{4,12},{... | collective-permute-start | bytes 10223624 | tf_op jit(solution)/shard_map/ppermute | solution.py:301
  235.5 96.3 %collective-permute-start.19 = (bf16[7680,256]{1,0:T(8,128)(2,1)}, bf16[7680,256]{1,0:T(8,128)(2,1)}, u32[]{:S(2)}, u32[]{:S(2)}) collective-permute-start(bf16[7680,256]{1,0:T(8,128)(2,1)} %collective-permute-done.14.refs_3_), channel_id=1, source_target_pairs={{8,0},{16,24},{9,1},{17,25},{10,2},{18,26},{11,3},{19,27},{12,4},{... | collective-permute-start | bytes 11796488 | tf_op jit(solution)/shard_map/ppermute | solution.py:301
  259.8 3.5 copy-start
  259.8 136.2 %collective-permute-start.18 = (bf16[160,128,128]{2,1,0:T(8,128)(2,1)}, bf16[160,128,128]{2,1,0:T(8,128)(2,1)}, u32[]{:S(2)}, u32[]{:S(2)}) collective-permute-start(bf16[160,128,128]{2,1,0:T(8,128)(2,1)} %pack_tiles.7), channel_id=1, source_target_pairs={{0,4},{4,0},{1,5},{5,1},{2,6},{6,2},{3,7},{7,3},{8,12},{12,8},{9,1... | collective-permute-start | bytes 15728648 | tf_op jit(solution)/shard_map/ppermute | solution.py:301
  303.5 51.1 %collective-permute-start.13 = (bf16[4608,256]{1,0:T(8,128)(2,1)S(1)}, bf16[4608,256]{1,0:T(8,128)(2,1)}, u32[]{:S(2)}, u32[]{:S(2)}) collective-permute-start(bf16[4608,256]{1,0:T(8,128)(2,1)S(1)} %pad_maximum_fusion.1.refs_2_.refs_1_), channel_id=1, source_target_pairs={{0,8},{24,16},{1,9},{25,17},{2,10},{26,18},{3,11},{27,19},{4,12},{... | collective-permute-start | bytes 7077896 | tf_op jit(solution)/shard_map/ppermute | solution.py:301
  309.4 68.9 %collective-permute-start.17 = (bf16[4608,256]{1,0:T(8,128)(2,1)S(1)}, bf16[4608,256]{1,0:T(8,128)(2,1)}, u32[]{:S(2)}, u32[]{:S(2)}) collective-permute-start(bf16[4608,256]{1,0:T(8,128)(2,1)S(1)} %pad_maximum_fusion.1.refs_2_.refs_1_), channel_id=1, source_target_pairs={{8,16},{16,8},{9,17},{17,9},{10,18},{18,10},{11,19},{19,11},{12,20... | collective-permute-start | bytes 7077896 | tf_op jit(solution)/shard_map/ppermute | solution.py:301
  331.8 98.2 %collective-permute-start.34 = (bf16[7680,256]{1,0:T(8,128)(2,1)}, bf16[7680,256]{1,0:T(8,128)(2,1)}, u32[]{:S(2)}, u32[]{:S(2)}) collective-permute-start(bf16[7680,256]{1,0:T(8,128)(2,1)} %collective-permute-done.16.refs_2_), channel_id=1, source_target_pairs={{8,0},{16,24},{9,1},{17,25},{10,2},{18,26},{11,3},{19,27},{12,4},{... | collective-permute-start | bytes 11796488 | tf_op jit(solution)/shard_map/ppermute | solution.py:301
  354.6 76.8 %collective-permute-start.23 = (bf16[104,128,128]{2,1,0:T(8,128)(2,1)}, bf16[104,128,128]{2,1,0:T(8,128)(2,1)}, u32[]{:S(2)}, u32[]{:S(2)}) collective-permute-start(bf16[104,128,128]{2,1,0:T(8,128)(2,1)} %copy-done), channel_id=1, source_target_pairs={{0,8},{24,16},{1,9},{25,17},{2,10},{26,18},{3,11},{27,19},{4,12},{... | collective-permute-start | bytes 10223624 | tf_op jit(solution)/shard_map/ppermute | solution.py:301
  360.8 19.6 %copy-start.1 = (bf16[104,128,128]{2,1,0:T(8,128)(2,1)S(1)}, bf16[104,128,128]{2,1,0:T(8,128)(2,1)}, u32[]{:S(2)}) copy-start(bf16[104,128,128]{2,1,0:T(8,128)(2,1)} %copy-done) | copy-start | bytes 10223620
  378.2 53.1 %collective-permute-start.24 = (bf16[4608,256]{1,0:T(8,128)(2,1)}, bf16[4608,256]{1,0:T(8,128)(2,1)}, u32[]{:S(2)}, u32[]{:S(2)}) collective-permute-start(bf16[4608,256]{1,0:T(8,128)(2,1)} %collective-permute-done.13.refs_3_), channel_id=1, source_target_pairs={{8,16},{16,8},{9,17},{17,9},{10,18},{18,10},{11,19},{19,11},{12,20... | collective-permute-start | bytes 7077896 | tf_op jit(solution)/shard_map/ppermute | solution.py:301
  417.3 34.1 %collective-permute-start.20 = (f32[3,128,1024]{2,1,0:T(8,128)}, f32[3,128,1024]{2,1,0:T(8,128)}, u32[]{:S(2)}, u32[]{:S(2)}) collective-permute-start(f32[3,128,1024]{2,1,0:T(8,128)} %constant_dynamic-slice_fusion.12), channel_id=1, source_target_pairs={{0,1},{1,0},{2,3},{3,2},{4,5},{5,4},{6,7},{7,6},{8,9},{9,8},{10,11... | collective-permute-start | bytes 4718600 | tf_op jit(solution)/shard_map/ppermute | solution.py:286
  430.1 50.3 %collective-permute-start.35 = (bf16[4096,256]{1,0:T(8,128)(2,1)}, bf16[4096,256]{1,0:T(8,128)(2,1)}, u32[]{:S(2)}, u32[]{:S(2)}) collective-permute-start(bf16[4096,256]{1,0:T(8,128)(2,1)} %collective-permute-done.15.refs_2_), channel_id=1, source_target_pairs={{8,0},{16,24},{9,1},{17,25},{10,2},{18,26},{11,3},{19,27},{12,4},{... | collective-permute-start | bytes 6291464 | tf_op jit(solution)/shard_map/ppermute | solution.py:301
  448.5 2.4 copy-start.17
  448.5 3.6 copy-start.20
  450.9 8.4 %copy-start.14 = (s32[4,4]{1,0:T(4,128)S(1)}, s32[4,4]{1,0:T(4,128)}, u32[]{:S(2)}) copy-start(s32[4,4]{1,0:T(4,128)} %constant.222.clone) | copy-start | bytes 196
  450.9 38.3 %collective-permute-start.25 = (f32[3,128,1024]{2,1,0:T(8,128)}, f32[3,128,1024]{2,1,0:T(8,128)}, u32[]{:S(2)}, u32[]{:S(2)}) collective-permute-start(f32[3,128,1024]{2,1,0:T(8,128)} %fusion.4), channel_id=1, source_target_pairs={{0,1},{1,0},{2,3},{3,2},{4,5},{5,4},{6,7},{7,6},{8,9},{9,8},{10,11... | collective-permute-start | bytes 4718600 | tf_op jit(solution)/shard_map/ppermute | solution.py:286
  455.9 20.3 %collective-permute-start.21 = (f32[3,64,1024]{2,1,0:T(8,128)}, f32[3,64,1024]{2,1,0:T(8,128)}, u32[]{:S(2)}, u32[]{:S(2)}) collective-permute-start(f32[3,64,1024]{2,1,0:T(8,128)} %constant_dynamic-slice_fusion.11), channel_id=1, source_target_pairs={{0,4},{4,0},{1,5},{5,1},{2,6},{6,2},{3,7},{7,3},{8,12},{12,8},{9,1... | collective-permute-start | bytes 2359304 | tf_op jit(solution)/shard_map/ppermute | solution.py:286
  459.4 16.7 %copy-start.22 = (f32[3,128,1024]{2,1,0:T(8,128)S(1)}, f32[3,128,1024]{2,1,0:T(8,128)}, u32[]{:S(2)}) copy-start(f32[3,128,1024]{2,1,0:T(8,128)} %copy-done.21) | copy-start | bytes 4718596
  459.4 20.9 %copy-start.7 = (bf16[94,128,128]{2,1,0:T(8,128)(2,1)S(1)}, bf16[94,128,128]{2,1,0:T(8,128)(2,1)}, u32[]{:S(2)}) copy-start(bf16[94,128,128]{2,1,0:T(8,128)(2,1)} %copy-done.5) | copy-start | bytes 9240580
  478.3 10.8 %copy-start.16 = (f32[3,256,512]{2,1,0:T(8,128)S(1)}, f32[3,256,512]{2,1,0:T(8,128)}, u32[]{:S(2)}) copy-start(f32[3,256,512]{2,1,0:T(8,128)} %copy-done.15) | copy-start | bytes 4718596
  478.3 10.8 %copy-start.18 = (f32[3,256,512]{2,1,0:T(8,128)S(1)}, f32[3,256,512]{2,1,0:T(8,128)}, u32[]{:S(2)}) copy-start(f32[3,256,512]{2,1,0:T(8,128)} %copy-done.17) | copy-start | bytes 4718596
  489.1 2.2 copy-start.12
  489.2 5.0 copy-start.2
  492.7 19.7 %collective-permute-start.26 = (f32[3,64,1024]{2,1,0:T(8,128)}, f32[3,64,1024]{2,1,0:T(8,128)}, u32[]{:S(2)}, u32[]{:S(2)}) collective-permute-start(f32[3,64,1024]{2,1,0:T(8,128)} %constant_dynamic-slice_fusion.9), channel_id=1, source_target_pairs={{0,4},{4,0},{1,5},{5,1},{2,6},{6,2},{3,7},{7,3},{8,12},{12,8},{9,1... | collective-permute-start | bytes 2359304 | tf_op jit(solution)/shard_map/ppermute | solution.py:286
  494.2 9.8 %copy-start.11 = (f32[1,256,1024]{2,1,0:T(8,128)S(1)}, f32[1,256,1024]{2,1,0:T(8,128)}, u32[]{:S(2)}) copy-start(f32[1,256,1024]{2,1,0:T(8,128)} %copy-done.10) | copy-start | bytes 3145732
  494.2 9.9 %copy-start.13 = (f32[1,256,1024]{2,1,0:T(8,128)S(1)}, f32[1,256,1024]{2,1,0:T(8,128)}, u32[]{:S(2)}) copy-start(f32[1,256,1024]{2,1,0:T(8,128)} %copy-done.12) | copy-start | bytes 3145732
  504.0 8.3 %copy-start.24 = (f32[3,128,1024]{2,1,0:T(8,128)S(1)}, f32[3,128,1024]{2,1,0:T(8,128)}, u32[]{:S(2)}) copy-start(f32[3,128,1024]{2,1,0:T(8,128)} %copy-done.23) | copy-start | bytes 4718596
  504.3 10.9 %copy-start.25 = (f32[3,64,1024]{2,1,0:T(8,128)S(1)}, f32[3,64,1024]{2,1,0:T(8,128)}, u32[]{:S(2)}) copy-start(f32[3,64,1024]{2,1,0:T(8,128)} %dynamic-slice_add_fusion.3) | copy-start | bytes 2359300
  505.2 10.6 %collective-permute-start.36 = (f32[1,128,1024]{2,1,0:T(8,128)}, f32[1,128,1024]{2,1,0:T(8,128)}, u32[]{:S(2)}, u32[]{:S(2)}) collective-permute-start(f32[1,128,1024]{2,1,0:T(8,128)} %constant_dynamic-slice_fusion.7), channel_id=1, source_target_pairs={{0,1},{1,0},{2,3},{3,2},{4,5},{5,4},{6,7},{7,6},{8,9},{9,8},{10,11... | collective-permute-start | bytes 1572872 | tf_op jit(solution)/shard_map/ppermute | solution.py:286
  513.6 12.1 %collective-permute-start.27 = (f32[3,32,1024]{2,1,0:T(8,128)S(1)}, f32[3,32,1024]{2,1,0:T(8,128)S(1)}, u32[]{:S(2)}, u32[]{:S(2)}) collective-permute-start(f32[3,32,1024]{2,1,0:T(8,128)S(1)} %constant_dynamic-slice_fusion.8), channel_id=1, source_target_pairs={{0,2},{2,0},{1,3},{3,1},{4,6},{6,4},{5,7},{7,5},{8,10},{10,8},{9,1... | collective-permute-start | bytes 1179656 | tf_op jit(solution)/shard_map/ppermute | solution.py:286
  515.2 17.0 %collective-permute-start.22 = (f32[3,32,1024]{2,1,0:T(8,128)S(1)}, f32[3,32,1024]{2,1,0:T(8,128)S(1)}, u32[]{:S(2)}, u32[]{:S(2)}) collective-permute-start(f32[3,32,1024]{2,1,0:T(8,128)S(1)} %constant_dynamic-slice_fusion.10), channel_id=1, source_target_pairs={{0,2},{2,0},{1,3},{3,1},{4,6},{6,4},{5,7},{7,5},{8,10},{10,8},{9,1... | collective-permute-start | bytes 1179656 | tf_op jit(solution)/shard_map/ppermute | solution.py:286
  517.0 15.2 %collective-permute-start.37 = (f32[1,64,1024]{2,1,0:T(8,128)S(1)}, f32[1,64,1024]{2,1,0:T(8,128)S(1)}, u32[]{:S(2)}, u32[]{:S(2)}) collective-permute-start(f32[1,64,1024]{2,1,0:T(8,128)S(1)} %constant_dynamic-slice_fusion.6), channel_id=1, source_target_pairs={{0,4},{4,0},{1,5},{5,1},{2,6},{6,2},{3,7},{7,3},{8,12},{12,8},{9,1... | collective-permute-start | bytes 786440 | tf_op jit(solution)/shard_map/ppermute | solution.py:286
  525.8 10.0 %collective-permute-start.28 = (f32[3,32,1024]{2,1,0:T(8,128)S(1)}, f32[3,32,1024]{2,1,0:T(8,128)S(1)}, u32[]{:S(2)}, u32[]{:S(2)}) collective-permute-start(f32[3,32,1024]{2,1,0:T(8,128)S(1)} %dynamic-slice_add_fusion.6), channel_id=1, source_target_pairs={{8,0},{16,24},{9,1},{17,25},{10,2},{18,26},{11,3},{19,27},{12,4},{... | collective-permute-start | bytes 1179656 | tf_op jit(solution)/shard_map/ppermute | solution.py:463
  532.3 5.0 collective-permute-start.38
  535.9 13.5 %collective-permute-start.29 = (f32[3,32,1024]{2,1,0:T(8,128)S(1)}, f32[3,32,1024]{2,1,0:T(8,128)S(1)}, u32[]{:S(2)}, u32[]{:S(2)}) collective-permute-start(f32[3,32,1024]{2,1,0:T(8,128)S(1)} %fusion.9), channel_id=1, source_target_pairs={{0,8},{8,0},{16,24},{24,16},{1,9},{9,1},{17,25},{25,17},{2,10},{10... | collective-permute-start | bytes 1179656 | tf_op jit(solution)/shard_map/ppermute | solution.py:306
  536.4 16.6 %collective-permute-start.30 = (f32[3,32,1024]{2,1,0:T(8,128)S(1)}, f32[3,32,1024]{2,1,0:T(8,128)S(1)}, u32[]{:S(2)}, u32[]{:S(2)}) collective-permute-start(f32[3,32,1024]{2,1,0:T(8,128)S(1)} %fusion.9), channel_id=1, source_target_pairs={{8,16},{16,8},{9,17},{17,9},{10,18},{18,10},{11,19},{19,11},{12,20... | collective-permute-start | bytes 1179656 | tf_op jit(solution)/shard_map/ppermute | solution.py:307
  537.4 10.0 %collective-permute-start.39 = (f32[40,1024]{1,0:T(8,128)S(1)}, f32[40,1024]{1,0:T(8,128)S(1)}, u32[]{:S(2)}, u32[]{:S(2)}) collective-permute-start(f32[40,1024]{1,0:T(8,128)S(1)} %get-tuple-element.148), channel_id=1, source_target_pairs={{0,8},{8,0},{16,24},{24,16},{1,9},{9,1},{17,25},{25,17},{2,10},{10... | collective-permute-start | bytes 491528 | tf_op jit(solution)/shard_map/ppermute | solution.py:306
  540.1 8.0 %collective-permute-start.40 = (f32[40,1024]{1,0:T(8,128)S(1)}, f32[40,1024]{1,0:T(8,128)S(1)}, u32[]{:S(2)}, u32[]{:S(2)}) collective-permute-start(f32[40,1024]{1,0:T(8,128)S(1)} %get-tuple-element.148), channel_id=1, source_target_pairs={{8,16},{16,8},{9,17},{17,9},{10,18},{18,10},{11,19},{19,11},{12,20... | collective-permute-start | bytes 491528 | tf_op jit(solution)/shard_map/ppermute | solution.py:307
  547.4 4.3 collective-permute-start.42
  548.1 7.6 %collective-permute-start.41 = (f32[40,1024]{1,0:T(8,128)S(1)}, f32[40,1024]{1,0:T(8,128)S(1)}, u32[]{:S(2)}, u32[]{:S(2)}) collective-permute-start(f32[40,1024]{1,0:T(8,128)S(1)} %collective-permute-done.40), channel_id=1, source_target_pairs={{8,0},{16,24},{9,1},{17,25},{10,2},{18,26},{11,3},{19,27},{12,4},{... | collective-permute-start | bytes 491528 | tf_op jit(solution)/shard_map/ppermute | solution.py:309
  549.4 6.3 %collective-permute-start.32 = (f32[3,32,1024]{2,1,0:T(8,128)S(1)}, f32[3,32,1024]{2,1,0:T(8,128)S(1)}, u32[]{:S(2)}, u32[]{:S(2)}) collective-permute-start(f32[3,32,1024]{2,1,0:T(8,128)S(1)} %collective-permute-done.29), channel_id=1, source_target_pairs={{8,16},{16,8},{9,17},{17,9},{10,18},{18,10},{11,19},{19,11},{12,20... | collective-permute-start | bytes 1179656 | tf_op jit(solution)/shard_map/ppermute | solution.py:308
  551.7 12.1 %collective-permute-start.43 = (f32[40,1024]{1,0:T(8,128)S(1)}, f32[40,1024]{1,0:T(8,128)S(1)}, u32[]{:S(2)}, u32[]{:S(2)}) collective-permute-start(f32[40,1024]{1,0:T(8,128)S(1)} %collective-permute-done.42), channel_id=1, source_target_pairs={{8,0},{16,24},{9,1},{17,25},{10,2},{18,26},{11,3},{19,27},{12,4},{... | collective-permute-start | bytes 491528 | tf_op jit(solution)/shard_map/ppermute | solution.py:310
  553.0 19.1 %collective-permute-start.31 = (f32[3,32,1024]{2,1,0:T(8,128)S(1)}, f32[3,32,1024]{2,1,0:T(8,128)S(1)}, u32[]{:S(2)}, u32[]{:S(2)}) collective-permute-start(f32[3,32,1024]{2,1,0:T(8,128)S(1)} %collective-permute-done.30), channel_id=1, source_target_pairs={{8,0},{16,24},{9,1},{17,25},{10,2},{18,26},{11,3},{19,27},{12,4},{... | collective-permute-start | bytes 1179656 | tf_op jit(solution)/shard_map/ppermute | solution.py:309
  555.8 20.6 %collective-permute-start.33 = (f32[3,32,1024]{2,1,0:T(8,128)S(1)}, f32[3,32,1024]{2,1,0:T(8,128)S(1)}, u32[]{:S(2)}, u32[]{:S(2)}) collective-permute-start(f32[3,32,1024]{2,1,0:T(8,128)S(1)} %collective-permute-done.32), channel_id=1, source_target_pairs={{8,0},{16,24},{9,1},{17,25},{10,2},{18,26},{11,3},{19,27},{12,4},{... | collective-permute-start | bytes 1179656 | tf_op jit(solution)/shard_map/ppermute | solution.py:310
  585.9 3.0 collective-permute-start.44
  590.3 14.7 %collective-permute-start.45 = (f32[1,2,1,4,136,128]{5,4,3,2,1,0:T(8,128)S(1)}, f32[1,2,1,4,136,128]{5,4,3,2,1,0:T(8,128)S(1)}, u32[]{:S(2)}, u32[]{:S(2)}) collective-permute-start(f32[1,2,1,4,136,128]{5,4,3,2,1,0:T(8,128)S(1)} %constant_dynamic-slice_fusion.3), channel_id=1, source_target_pairs={{0,4},{4,0},{1,5},{5,1},{2,6},{6,2},{3,7},{7,3},{8,12},{12,8},{9,1... | collective-permute-start | bytes 1671176 | tf_op jit(solution)/shard_map/ppermute | solution.py:286
  605.1 7.9 %collective-permute-start.46 = (f32[1,1,1,4,136,128]{5,4,3,2,1,0:T(8,128)S(1)}, f32[1,1,1,4,136,128]{5,4,3,2,1,0:T(8,128)S(1)}, u32[]{:S(2)}, u32[]{:S(2)}) collective-permute-start(f32[1,1,1,4,136,128]{5,4,3,2,1,0:T(8,128)S(1)} %constant_dynamic-slice_fusion.2), channel_id=1, source_target_pairs={{0,2},{2,0},{1,3},{3,1},{4,6},{6,4},{5,7},{7,5},{8,10},{10,8},{9,1... | collective-permute-start | bytes 835592 | tf_op jit(solution)/shard_map/ppermute | solution.py:286
  (13 other events, 18.7 us)

commit v13 on v10

--- a/solution.py
+++ b/solution.py
@@ -19,7 +19,7 @@
 SOURCE = np.array([[0, 1, 2, 3], [1, 0, 2, 3], [2, 3, 1, 0], [3, 2, 1, 0]], np.int32)
 PLACE = np.argsort(SOURCE, axis=1).astype(np.int32)
 
-LENT = (5, 16)
+LENT = (9, 32)
 
 
 def bounds(total, parts):
@@ -27,7 +27,7 @@
 
 
 def room(tiles):
-    return min(tiles, -(-(tiles // 2 + int(2.6 * tiles**0.5)) // 2) * 2)
+    return min(tiles, max(48, -(-(tiles // 2 + int(2.6 * tiles**0.5)) // 2) * 2))
 
 
 def params(**kwargs):
@@ -76,10 +76,10 @@
     )(info, hist)
 
 
-STRIDE = 8
-
-
-def product_kernel(blk, row_blocks, steps, slots, paired, info, *refs):
+STRIDE = 4
+
+
+def product_kernel(blk, row_blocks, stride, steps, slots, paired, info, *refs):
     count, groups = len(slots), len(paired)
     sources, refs = refs[:count], refs[count:]
     planes, at = [], 0
@@ -88,8 +88,8 @@
         at += 1 + two
     out, total, work, own, packed, held, source_sem, held_sem = refs[at:]
     rows = row_blocks * blk
-    depth = STRIDE * blk
-    step_tiles = STRIDE * row_blocks
+    depth = stride * blk
+    step_tiles = stride * row_blocks
     inner, base = info[0] != 0, info[1]
     lists = 2 + count
     starts = lists + count * steps * step_tiles
@@ -109,7 +109,7 @@
 
         for k in range(count):
             if slots[k] is None:
-                start = pl.multiple_of((base + i * STRIDE) * blk, blk)
+                start = pl.multiple_of((base + i * stride) * blk, blk)
                 part = sources[k].at[:, pl.ds(start, depth)]
             else:
                 part = sources[k].at[pl.ds(info[starts + k * steps + i], step_tiles)]
@@ -127,7 +127,7 @@
 
         for k in range(count):
             pltpu.make_async_copy(landing(k, slot), landing(k, slot), source_sem.at[slot, k]).wait()
-            for j in range(STRIDE):
+            for j in range(stride):
                 for b in range(row_blocks):
                     found = info[lists + (k * steps + i) * step_tiles + j * row_blocks + b]
                     area = (pl.ds(b * blk, blk), pl.ds(j * blk, blk))
@@ -155,8 +155,8 @@
             out[g, :, place] = total[g, k * rows : (k + 1) * rows, :].T
 
 
-def places_of(mask, slots):
-    steps = mask.shape[1] // STRIDE
+def places_of(mask, slots, stride):
+    steps = mask.shape[1] // stride
     there = mask.T.reshape(steps, -1)
     size = there.shape[1]
     if slots is None:
@@ -171,20 +171,21 @@
     row_blocks, columns = masks[0].shape
     slots = [v.shape[0] if v.ndim == 3 else None for v in sources]
     blk = next(v.shape[1] if n is not None else v.shape[0] // row_blocks for v, n in zip(sources, slots))
+    stride = next(n for n in (3 * STRIDE, 2 * STRIDE, STRIDE) if columns % n == 0)
     rows = row_blocks * blk
     wide = planes[0][0].shape[1]
     dtype = sources[0].dtype
     head = [jnp.asarray(v, jnp.int32).reshape(1) for v in [inner, base] + list(places)]
-    found, first = zip(*[places_of(m, n) for m, n in zip(masks, slots)])
+    found, first = zip(*[places_of(m, n, stride) for m, n in zip(masks, slots)])
     info = jnp.concatenate(head + [v.reshape(-1) for v in found] + list(first)).astype(jnp.int32)
     flat = [v for choice in planes for v in choice]
     shape = (len(planes), wide, len(sources) * rows)
     flops = 2 * shape[0] * shape[1] * shape[2] * columns * blk
-    size = columns * blk * (wide * len(planes) + rows * len(sources)) * 2
+    size = columns * blk * (wide * len(planes) + rows * len(sources) // 2) * 2
     lists = max(1, sum(n is not None for n in slots))
     return pl.pallas_call(
         functools.partial(
-            product_kernel, blk, row_blocks, columns // STRIDE, slots, [len(choice) - 1 for choice in planes]
+            product_kernel, blk, row_blocks, stride, columns // stride, slots, [len(choice) - 1 for choice in planes]
         ),
         out_shape=jax.ShapeDtypeStruct(shape, jnp.float32),
         in_specs=[pl.BlockSpec(memory_space=pltpu.SMEM)]
@@ -192,10 +193,10 @@
         out_specs=pl.BlockSpec(memory_space=pltpu.VMEM),
         scratch_shapes=[
             pltpu.VMEM((len(planes), len(sources) * rows, wide), jnp.float32),
-            pltpu.VMEM((len(sources) * rows, STRIDE * blk), dtype),
-            pltpu.VMEM((2, rows, STRIDE * blk), dtype),
-            pltpu.VMEM((2, lists, STRIDE * row_blocks, blk, blk), dtype),
-            pltpu.VMEM((2, len(planes), STRIDE * blk, wide), dtype),
+            pltpu.VMEM((len(sources) * rows, stride * blk), dtype),
+            pltpu.VMEM((2, rows, stride * blk), dtype),
+            pltpu.VMEM((2, lists, stride * row_blocks, blk, blk), dtype),
+            pltpu.VMEM((2, len(planes), stride * blk, wide), dtype),
             pltpu.SemaphoreType.DMA((2, len(sources))),
             pltpu.SemaphoreType.DMA((2,)),
         ],
@@ -281,6 +282,15 @@
         return self.arrived
 
 
+def along_line(block, inner):
+    near = lax.ppermute(block, "z", NEAR)
+    middle = lax.ppermute(block, "z", MIDDLE)
+    far = lax.ppermute(near, "z", MIDDLE)
+    out1 = lax.ppermute(middle, "z", OUTWARD)
+    out2 = lax.ppermute(far, "z", OUTWARD)
+    return [block, near, jnp.where(inner, middle, out1), jnp.where(inner, far, out2)]
+
+
 def dense(hist, tile_mask, planes, pairs):
     sess, act = ("z", "x"), ("y", "core")
     rows, acts = hist.shape
@@ -359,86 +369,76 @@
     known = [both_of(x)] + [lax.ppermute(both_of(o), "x", r) for o, r in zip(others, row_routes)]
     listed = [pairs] + [lax.ppermute(pairs, "x", route) for route in row_routes]
     masks, guest_masks = [m[0] for m in known], [m[1][:, kept:] for m in known]
-    ends, middle = Lane(), Lane()
-    near, mid, far, groups = [], [], [], []
+    groups = []
     for c in range(3):
-        if c == 2:
-            over_x.arrived = over_x.arrived + near[:1]
         got = over_x.send([planes_of(o, c) for o in others], "x", row_routes)
         groups.append(in_row_order([planes_of(x, c)] + got, 1))
         if c == 0:
             over_x.arrived = got + known[1:] + listed[1:]
-        if c < 2:
-            near += ends.send([groups[c]], "z", [NEAR])
-            mid += middle.send([groups[c]], "z", [MIDDLE])
     tiles = [None] * 3
     for c in (0, 2, 1):
         tiles[c] = over_x.send([packed(o, c, groups[0]) for o in others], "x", row_routes)
 
+    ends, middle = Lane(), Lane()
+    near, mid, far = [], [], []
+    for c in range(2):
+        near += ends.send([groups[c]], "z", [NEAR])
+        mid += middle.send([groups[c]], "z", [MIDDLE])
     inward, outward = Lane(near[1:]), Lane(near[1:])
-    middle.arrived = mid[1:] + near[1:]
-    far += middle.send([near[0]], "z", [MIDDLE])
-    outer = outward.send([mid[0]], "z", [OUTWARD])
-    middle.arrived = far + outer
-    far += middle.send([near[1]], "z", [MIDDLE])
-    outer += outward.send([mid[1]], "z", [OUTWARD])
-    middle.arrived = far[1:] + outer[1:]
+    for c in range(2):
+        far += middle.send([near[c]], "z", [MIDDLE])
+    loans = inward.send([packed(x, 2, near[0])], "z", [INWARD])
     near += inward.send([groups[2]], "z", [INWARD])
-    loans = inward.send([packed(x, 2, near[0])], "z", [INWARD])
+    mid += middle.send([groups[2]], "z", [MIDDLE])
     far += middle.send([near[2]], "z", [MIDDLE])
-    mid += middle.send([groups[2]], "z", [MIDDLE])
-
+    outer = [outward.send([v], "z", [OUTWARD])[0] for v in mid[:2]]
+    loans = loans + inward.send(tiles[2], "z", [INWARD] * len(others))
     over = jnp.int32(0)
     for c in range(3):
         for owner in range(wide):
             count = jnp.sum(tile_mask[:, owner * columns + cuts[c] : owner * columns + cuts[c + 1]])
             over = jnp.maximum(over, (count > slots[c]).astype(jnp.int32))
     row_places = [(x - k) % wide * rows for k in range(wide)]
-    every = range(wide)
+    early_groups = [[[groups[c]], [near[c]], [mid[c], outer[c]]] for c in range(2)]
 
     def times(c, sources, which, held, places):
         own = [masks[k][:, cuts[c] : cuts[c + 1]] for k in which]
         return product(sources, own, held, inner, x * columns + cuts[c], places)
 
-    early_groups = [[[groups[c]], [near[c]], [mid[c], outer[c]]] for c in range(2)]
+    every = range(wide)
     part0 = times(0, [hist] + tiles[0], every, early_groups[0], row_places)
-    loans += inward.send([after(t, part0) for t in tiles[2]], "z", [INWARD] * len(others))
-    outer += outward.send([far[1]], "z", [OUTWARD])
+    outer += outward.send([after(far[1], part0)], "z", [OUTWARD])
     part1 = [times(1, [hist], [0], early_groups[1], [0])]
-    part2 = times(2, [hist] + tiles[2], every, [[groups[2]], [near[2]]], row_places)
+    part2 = times(2, [hist] + tiles[2], every, [[groups[2]], [near[2]], [mid[2]]], row_places)
+    guest = product([loans[0]], [guest_masks[0]], [[groups[2]], [mid[2]]], inner, 0, [0])
+    outer += outward.send([after(far[0], [part1[0], part2, guest])], "z", [OUTWARD])
+    part1 += [times(1, [tiles[1][k - 1]], [k], early_groups[1], [0]) for k in range(1, wide)]
+    first_three = part0 + part2 + in_row_order(part1, 2)
+
     end2 = times(2, [hist] + tiles[2], every, [[far[2]]], row_places)
-    outer += outward.send([after(far[0], [part1, part2, end2])], "z", [OUTWARD])
-    part1 += [times(1, [tiles[1][k - 1]], [k], early_groups[1], [0]) for k in range(1, wide)]
     end1 = times(1, [hist] + tiles[1], every, [[far[1], outer[2]]], row_places)
-    guests = in_row_order(
-        [product([t], [m], [[groups[2]], [far[2]]], inner, 0, [0]) for t, m in zip(loans, guest_masks)], 2
-    )
-    part2 = jnp.concatenate([part2, times(2, [hist] + tiles[2], every, [[mid[2]]], row_places)])
-    first_three = part0 + part2 + in_row_order(part1, 2)
-    guests_mid = product(loans, guest_masks, [[mid[2]]], inner, 0, row_places)
     end0 = times(0, [hist] + tiles[0], every, [[far[0], outer[3]]], row_places)
     last_one = end0 + (end1 + end2)
-    visitors = jnp.concatenate([guests[:1], guests_mid, guests[1:]])
-
-    def summed(share):
-        return scatter_sum(scatter_sum(scatter_sum(share, "core", 1), "x", 1), "y", 1)
-
-    first_three, visitors, last_one = summed(first_three), summed(visitors), summed(last_one)
-
-    def all_along_line(share, extra):
-        near = lax.ppermute(share, "z", NEAR) + extra
-        mid = lax.ppermute(share, "z", MIDDLE)
-        far = lax.ppermute(near, "z", MIDDLE)
-        out1 = lax.ppermute(mid, "z", OUTWARD)
-        out2 = lax.ppermute(far, "z", OUTWARD)
-        own = share + lax.ppermute(extra, "z", OUTWARD)
-        return jnp.stack([own, near, jnp.where(inner, mid, out1), jnp.where(inner, far, out2)])
-
-    early = all_along_line(first_three, jnp.concatenate([jnp.zeros_like(visitors[:1]), visitors[:2]]))
-    flags = jnp.full((8, last_one.shape[2]), over.astype(jnp.float32))
-    late = all_along_line(
-        jnp.concatenate([last_one[0], flags]), jnp.concatenate([visitors[2], jnp.zeros_like(flags)])
-    )
+    guest = jnp.concatenate([guest, product([loans[0]], [guest_masks[0]], [[far[2]]], inner, 0, [0])])
+    visitors = in_row_order(
+        [guest]
+        + [
+            product([t], [m], [[groups[2]], [mid[2]], [far[2]]], inner, 0, [0])
+            for t, m in zip(loans[1:], guest_masks[1:])
+        ],
+        2,
+    )
+
+    def summed(totals):
+        return scatter_sum(scatter_sum(scatter_sum(totals, "core", 1), "x", 1), "y", 1)
+
+    first_three = summed(first_three)
+    visitors = lax.ppermute(summed(visitors), "z", OUTWARD)
+    early = first_three.at[1:].add(visitors[:2])
+    early = jnp.stack(along_line(early, inner))
+    last_one = summed(last_one)[0] + visitors[2]
+    flags = jnp.full((8, last_one.shape[1]), over.astype(jnp.float32))
+    late = jnp.stack(along_line(jnp.concatenate([last_one, flags]), inner))
 
     order = (x - jnp.arange(wide)) % wide
     all_pairs = jnp.stack(listed)[order].reshape(-1, 2).T
@@ -451,8 +451,11 @@
     sums = pair_dots(early, late, ids, blk)
     high, cores = lax.axis_size("y"), lax.axis_size("core")
     sums = sums.reshape((wide, high, cores, -1) + sums.shape[1:])
-    for axis, dim in (("core", 2), ("x", 0), ("y", 1)):
-        sums = scatter_sum(sums, axis, dim)
+    sums = scatter_sum(sums, "core", 2)
+    half = sums.shape[3] // 2
+    by_x = scatter_sum(scatter_sum(sums[:, :, :, :half], "x", 0), "y", 1)
+    by_y = scatter_sum(scatter_sum(sums[:, :, :, half:], "y", 1), "x", 0)
+    sums = jnp.concatenate([by_x, by_y], axis=3)
     own = sums.reshape((-1,) + sums.shape[4:])
     scale = lax.rsqrt(own[:, blk : blk + 2] / P_SIZE + 1e-06)
     scores = own[:, :blk] / P_SIZE * scale[:, 0, :, None] * scale[:, 1, None, :]

time: 624 us -> 603 us (0.966)
  Pallas kernels: 145 us -> 130 us
  waiting for transfers between devices: 321 us -> 306 us
  local copies, waits for them, and re-layouts: 22.8 us -> 31.2 us
    ppermute x1, waiting for transfers between devices: 0.01 us -> 19.5 us  [body(): lax.ppermute(both_of(o), 'x', r)]
    ppermute x12 -> x11, waiting for transfers between devices: 47.9 us -> 31.4 us  [the longest x2 11.3 us: along_line(): out2 = lax.ppermute(far, 'z', OUTWARD)]
    ppermute x1, waiting for transfers between devices: 16.3 us -> 0.01 us  [body(): listed = [pairs] + [lax.ppermute(pairs, 'x', route) for route in row_routes]]
    pallas_call x11 -> x10, Pallas kernels: 118 us -> 105 us  [product(): pl.pallas_call(functools.partial(product_kernel, blk, row_blocks, stride,...]
    ppermute x12 -> x14, waiting for transfers between devices: 56.6 us -> 45.2 us  [scatter_sum(): total = total + lax.ppermute(part((here + k) % count), axis, turn(count, k))]
    ppermute x21, waiting for transfers between devices: 200 us -> 210 us  [send(): lax.ppermute(v, axis, route)]
    unnamed x40 -> x62, local copies, waits for them, and re-layouts: 3.36 us -> 9.98 us
    ppermute x12 -> x11, starting transfers between devices: 12.8 us -> 13.2 us  [the longest x2 3.83 us: along_line(): near = lax.ppermute(block, 'z', NEAR)]
  transfers between devices with their start and end apart: 48 -> 49, of which waited for: 23 -> 25; matrix products, arithmetic and copies ran while one was open for 7% -> 7% of each run, Pallas kernels for 22% -> 20%
where the time goes in v13:
time: 603 us; the launch traced here: 593 us
  waiting for transfers between devices  306 us (51%)
  Pallas kernels  130 us (22%)
  starting transfers between devices  80.8 us (13%)
  local copies, waits for them, and re-layouts  31.2 us (5%)
  other arithmetic  25.2 us (4%)
  between operations  19.4 us (3%)
    ppermute x21, waiting for transfers between devices, send(): lax.ppermute(v, axis, route)  210 us
    pallas_call x10, Pallas kernels, product(): pl.pallas_call(functools.partial(product_kernel, blk, row_blocks, stride,...  105 us
    ppermute x21, starting transfers between devices, send(): lax.ppermute(v, axis, route)  48.4 us
    ppermute x14, waiting for transfers between devices, scatter_sum(): total = total + lax.ppermute(part((here + k) % count), axis, turn(count, k))  45.2 us
    ppermute x1, waiting for transfers between devices, body(): lax.ppermute(both_of(o), 'x', r)  19.5 us
    pallas_call x4, Pallas kernels, pack(): pl.pallas_call(functools.partial(pack_kernel, blk, row_blocks, columns, s...  15.6 us
  transfers between devices with their start and end apart: 49, of which 25 were waited for; matrix products, arithmetic and copies ran while one was open for 7% of the time, Pallas kernels for 20%

profile of v13, /device:TPU:0, one launch (start us, length us, event | category | flops | bytes accessed | tf_op | source)
XLA Modules:
  0.0 593.1 jit_solution(14392839962880693649)
XLA Ops:
  6.5 2.9 collective-permute-start
  10.2 3.5 collective-permute-start.1
  17.1 2.9 constant_dynamic-slice_fusion.16
  20.0 19.5 %collective-permute-done.2 = s32[2,4,128]{2,1,0:T(4,128)S(1)} collective-permute-done((s32[2,4,128]{2,1,0:T(4,128)S(1)}, s32[2,4,128]{2,1,0:T(4,128)S(1)}, u32[]{:S(2)}, u32[]{:S(2)}) %collective-permute-start.2) | collective-permute-done | bytes 4128 | tf_op jit(solution)/shard_map/ppermute | solution.py:369
  41.3 1.6 broadcast_select_fusion.5
  44.1 38.6 %collective-permute-done.4 = bf16[7680,128]{1,0:T(8,128)(2,1)S(1)} collective-permute-done((bf16[7680,128]{1,0:T(8,128)(2,1)}, bf16[7680,128]{1,0:T(8,128)(2,1)S(1)}, u32[]{:S(2)}, u32[]{:S(2)}) %collective-permute-start.4) | collective-permute-done | bytes 1966112 | tf_op jit(solution)/shard_map/ppermute | solution.py:281
  83.3 2.3 broadcast_select_fusion.1
  85.6 2.4 pad_maximum_fusion.refs_1_
  89.3 2.5 collective-permute-start.14
  92.1 3.9 pack_tiles.4
  96.0 12.6 %collective-permute-done.5 = bf16[4608,128]{1,0:T(8,128)(2,1)} collective-permute-done((bf16[4608,128]{1,0:T(8,128)(2,1)S(1)}, bf16[4608,128]{1,0:T(8,128)(2,1)}, u32[]{:S(2)}, u32[]{:S(2)}) %collective-permute-start.5) | collective-permute-done | bytes 1179680 | tf_op jit(solution)/shard_map/ppermute | solution.py:281
  114.3 2.4 pack_tiles.5
  116.6 59.1 %collective-permute-done.6.refs_1_ = bf16[94,128,128]{2,1,0:T(8,128)(2,1)} collective-permute-done((bf16[94,128,128]{2,1,0:T(8,128)(2,1)}, bf16[94,128,128]{2,1,0:T(8,128)(2,1)}, u32[]{:S(2)}, u32[]{:S(2)}) %collective-permute-start.6) | collective-permute-done | bytes 3080224 | tf_op jit(solution)/shard_map/ppermute | solution.py:281
  176.3 2.0 collective-permute-start.15
  181.0 11.4 %collective-permute-done.9.refs_2_ = bf16[7680,256]{1,0:T(8,128)(2,1)} collective-permute-done((bf16[7680,256]{1,0:T(8,128)(2,1)}, bf16[7680,256]{1,0:T(8,128)(2,1)}, u32[]{:S(2)}, u32[]{:S(2)}) %collective-permute-start.9) | collective-permute-done | bytes 3932192 | tf_op jit(solution)/shard_map/ppermute | solution.py:281
  195.0 4.1 pack_tiles.6
  199.1 7.7 %collective-permute-start.12 = (bf16[104,128,128]{2,1,0:T(8,128)(2,1)}, bf16[104,128,128]{2,1,0:T(8,128)(2,1)}, u32[]{:S(2)}, u32[]{:S(2)}) collective-permute-start(bf16[104,128,128]{2,1,0:T(8,128)(2,1)} %pack_tiles.6), channel_id=1, source_target_pairs={{0,8},{24,16},{1,9},{25,17},{2,10},{26,18},{3,11},{27,19},{4,12},{... | collective-permute-start | bytes 10223624 | tf_op jit(solution)/shard_map/ppermute | solution.py:281
  207.0 2.6 collective-permute-start.16
  215.6 22.6 %collective-permute-done.10.refs_5_ = bf16[4096,256]{1,0:T(8,128)(2,1)} collective-permute-done((bf16[4096,256]{1,0:T(8,128)(2,1)}, bf16[4096,256]{1,0:T(8,128)(2,1)}, u32[]{:S(2)}, u32[]{:S(2)}) %collective-permute-start.10) | collective-permute-done | bytes 2097184 | tf_op jit(solution)/shard_map/ppermute | solution.py:281
  239.6 5.2 pack_tiles.7
  244.9 4.6 collective-permute-done.11.refs_1_
  249.9 2.1 broadcast_select_fusion.3
  252.4 22.5 %collective-permute-done.12.refs_0_ = bf16[104,128,128]{2,1,0:T(8,128)(2,1)} collective-permute-done((bf16[104,128,128]{2,1,0:T(8,128)(2,1)}, bf16[104,128,128]{2,1,0:T(8,128)(2,1)}, u32[]{:S(2)}, u32[]{:S(2)}) %collective-permute-start.12) | collective-permute-done | bytes 3407904 | tf_op jit(solution)/shard_map/ppermute | solution.py:281
  274.8 5.8 collective-permute-start.13
  282.3 2.0 collective-permute-start.17
  284.9 1.6 copy-done.4
  286.5 14.8 %tiles_times_planes.10 = f32[3,256,1024]{2,1,0:T(8,128)} custom-call(s32[268]{0:T(512)S(1)} %concatenate.66.info, bf16[512,32768]{1,0:T(8,128)(2,1)} %refs_0_.11, bf16[94,128,128]{2,1,0:T(8,128)(2,1)} %collective-permute-done.6.refs_1_, bf16[4096,256]{1,0:T(8,128)(2,1)S(1)} %copy-done.4, bf16[4096,256]{1,0:T(8,128)(2,1)} %collective-permute-done.7.refs_3_, ...), custom_call_target="tpu_custom_call" | custom-call | flops 6442450944 | bytes 10485760 | tf_op jit(solution)/shard_map/tiles_times_planes/pallas_call | solution.py:186
  301.3 20.2 %collective-permute-done.19.refs_4_ = bf16[7680,256]{1,0:T(8,128)(2,1)} collective-permute-done((bf16[7680,256]{1,0:T(8,128)(2,1)}, bf16[7680,256]{1,0:T(8,128)(2,1)}, u32[]{:S(2)}, u32[]{:S(2)}) %collective-permute-start.19) | collective-permute-done | bytes 3932192 | tf_op jit(solution)/shard_map/ppermute | solution.py:281
  323.4 15.4 %collective-permute-start.23 = (bf16[104,128,128]{2,1,0:T(8,128)(2,1)}, bf16[104,128,128]{2,1,0:T(8,128)(2,1)}, u32[]{:S(2)}, u32[]{:S(2)}) collective-permute-start(bf16[104,128,128]{2,1,0:T(8,128)(2,1)} %collective-permute-done.11.refs_1_), channel_id=1, source_target_pairs={{0,8},{24,16},{1,9},{25,17},{2,10},{26,18},{3,11},{27,19},{4,12},{... | collective-permute-start | bytes 10223624 | tf_op jit(solution)/shard_map/ppermute | solution.py:281
  339.3 12.7 %tiles_times_planes.13 = f32[3,256,512]{2,1,0:T(8,128)S(1)} custom-call(s32[248]{0:T(256)S(1)} %concatenate.76.info, bf16[512,32768]{1,0:T(8,128)(2,1)} %refs_0_.11, bf16[7680,256]{1,0:T(8,128)(2,1)} %pad_maximum_fusion.refs_1_, bf16[7680,256]{1,0:T(8,128)(2,1)} %collective-permute-done.9.refs_2_, bf16[7680,256]{1,0:T(8,128)(2,1)} %collective-permute-done.14.refs_3_, ...), custom_call_target="tpu_custom_call" | custom-call | flops 6039797760 | bytes 15728640 | tf_op jit(solution)/shard_map/tiles_times_planes/pallas_call | solution.py:186
  352.8 7.2 %tiles_times_planes.15 = f32[2,256,512]{2,1,0:T(8,128)S(1)} custom-call(s32[150]{0:T(256)S(1)} %get-tuple-element.161.info, bf16[104,128,128]{2,1,0:T(8,128)(2,1)} %collective-permute-done.12.refs_0_, bf16[4608,256]{1,0:T(8,128)(2,1)S(1)} %pad_maximum_fusion.1.refs_2_.refs_1_, bf16[4608,256]{1,0:T(8,128)(2,1)} %collective-permute-done.17.refs_4_.refs_2_), custom_call_target="tpu_custom_call" | custom-call | flops 2415919104 | bytes 7077888 | tf_op jit(solution)/shard_map/tiles_times_planes/pallas_call | solution.py:186
  360.0 15.6 %tiles_times_planes.11 = f32[3,256,1024]{2,1,0:T(8,128)} custom-call(s32[298]{0:T(512)S(1)} %concatenate.70.info, bf16[512,32768]{1,0:T(8,128)(2,1)} %refs_0_.11, bf16[104,128,128]{2,1,0:T(8,128)(2,1)} %collective-permute-done.11.refs_1_, bf16[4608,256]{1,0:T(8,128)(2,1)S(1)} %pad_maximum_fusion.1.refs_2_.refs_1_, ...), custom_call_target="tpu_custom_call" | custom-call | flops 7247757312 | bytes 11796480 | tf_op jit(solution)/shard_map/tiles_times_planes/pallas_call | solution.py:186
  375.6 12.8 %tiles_times_planes.12 = f32[3,256,512]{2,1,0:T(8,128)S(1)} custom-call(s32[248]{0:T(256)S(1)} %concatenate.74.info, bf16[160,128,128]{2,1,0:T(8,128)(2,1)} %collective-permute-done.18.refs_0_.refs_1_, bf16[7680,256]{1,0:T(8,128)(2,1)} %pad_maximum_fusion.refs_1_, bf16[7680,256]{1,0:T(8,128)(2,1)} %collective-permute-done.9.refs_2_, ...), custom_call_target="tpu_custom_call" | custom-call | flops 6039797760 | bytes 15728640 | tf_op jit(solution)/shard_map/tiles_times_planes/pallas_call | solution.py:186
  393.8 18.5 %collective-permute-done.34.refs_3_ = bf16[7680,256]{1,0:T(8,128)(2,1)} collective-permute-done((bf16[7680,256]{1,0:T(8,128)(2,1)}, bf16[7680,256]{1,0:T(8,128)(2,1)}, u32[]{:S(2)}, u32[]{:S(2)}) %collective-permute-start.34) | collective-permute-done | bytes 3932192 | tf_op jit(solution)/shard_map/ppermute | solution.py:281
  415.3 8.6 %tiles_times_planes.14 = f32[3,256,512]{2,1,0:T(8,128)S(1)} custom-call(s32[150]{0:T(256)S(1)} %get-tuple-element.162.info, bf16[104,128,128]{2,1,0:T(8,128)(2,1)} %collective-permute-done.23.refs_0_, bf16[4608,256]{1,0:T(8,128)(2,1)S(1)} %pad_maximum_fusion.1.refs_2_.refs_1_, bf16[4608,256]{1,0:T(8,128)(2,1)} %collective-permute-done.17.refs_4_.refs_2_, ...), custom_call_target="tpu_custom_call" | custom-call | flops 3623878656 | bytes 9437184 | tf_op jit(solution)/shard_map/tiles_times_planes/pallas_call | solution.py:186
  423.9 1.7 copy-done.1
  425.5 5.7 tiles_times_planes.16
  436.7 11.9 %tiles_times_planes.18 = f32[1,256,1024]{2,1,0:T(8,128)S(1)} custom-call(s32[494]{0:T(512)S(1)} %concatenate.82.info, bf16[512,32768]{1,0:T(8,128)(2,1)} %refs_0_.11, bf16[160,128,128]{2,1,0:T(8,128)(2,1)} %collective-permute-done.18.refs_0_.refs_1_, bf16[7680,256]{1,0:T(8,128)(2,1)} %collective-permute-done.16.refs_2_, ...), custom_call_target="tpu_custom_call" | custom-call | flops 4026531840 | bytes 11796480 | tf_op jit(solution)/shard_map/tiles_times_planes/pallas_call | solution.py:186
  448.7 1.9 dynamic-slice_add_fusion
  450.7 1.6 collective-permute-start.21
  452.2 7.9 %tiles_times_planes.19 = f32[1,256,1024]{2,1,0:T(8,128)S(1)} custom-call(s32[298]{0:T(512)S(1)} %concatenate.70.info, bf16[512,32768]{1,0:T(8,128)(2,1)} %refs_0_.11, bf16[104,128,128]{2,1,0:T(8,128)(2,1)} %collective-permute-done.11.refs_1_, bf16[4608,256]{1,0:T(8,128)(2,1)S(1)} %copy-done.2), custom_call_target="tpu_custom_call" | custom-call | flops 2415919104 | bytes 7077888 | tf_op jit(solution)/shard_map/tiles_times_planes/pallas_call | solution.py:186
  460.2 1.7 fusion.6
  462.6 7.9 %tiles_times_planes.17 = f32[1,256,1024]{2,1,0:T(8,128)S(1)} custom-call(s32[268]{0:T(512)S(1)} %concatenate.66.info, bf16[512,32768]{1,0:T(8,128)(2,1)} %refs_0_.11, bf16[94,128,128]{2,1,0:T(8,128)(2,1)} %collective-permute-done.6.refs_1_, bf16[4096,256]{1,0:T(8,128)(2,1)} %collective-permute-done.15.refs_2_, bf16[4096,256]{1,0:T(8,128)(2,1)} %collective-permute-done.35.refs_3_), custom_call_target="tpu_custom_call" | custom-call | flops 2147483648 | bytes 6291456 | tf_op jit(solution)/shard_map/tiles_times_planes/pallas_call | solution.py:186
  471.2 16.3 %collective-permute-done.26 = f32[3,64,1024]{2,1,0:T(8,128)S(1)} collective-permute-done((f32[3,64,1024]{2,1,0:T(8,128)S(1)}, f32[3,64,1024]{2,1,0:T(8,128)S(1)}, u32[]{:S(2)}, u32[]{:S(2)}) %collective-permute-start.26) | collective-permute-done | bytes 786464 | tf_op jit(solution)/shard_map/ppermute | solution.py:266
  487.7 1.6 collective-permute-start.27
  490.0 1.6 collective-permute-start.37
  491.6 8.2 %collective-permute-done.27 = f32[3,32,1024]{2,1,0:T(8,128)S(1)} collective-permute-done((f32[3,32,1024]{2,1,0:T(8,128)S(1)}, f32[3,32,1024]{2,1,0:T(8,128)S(1)}, u32[]{:S(2)}, u32[]{:S(2)}) %collective-permute-start.27) | collective-permute-done | bytes 393248 | tf_op jit(solution)/shard_map/ppermute | solution.py:266
  501.2 5.8 collective-permute-done.22
  507.1 1.6 collective-permute-start.38
  508.7 3.2 collective-permute-done.28
  513.5 3.1 collective-permute-start.39
  517.3 6.8 %collective-permute-done.39 = f32[40,1024]{1,0:T(8,128)S(1)} collective-permute-done((f32[40,1024]{1,0:T(8,128)S(1)}, f32[40,1024]{1,0:T(8,128)S(1)}, u32[]{:S(2)}, u32[]{:S(2)}) %collective-permute-start.39) | collective-permute-done | bytes 163872 | tf_op jit(solution)/shard_map/ppermute | solution.py:286
  530.9 1.8 collective-permute-done.41
  532.8 1.5 collective-permute-start.33
  534.3 6.7 %collective-permute-done.43 = f32[40,1024]{1,0:T(8,128)S(1)} collective-permute-done((f32[40,1024]{1,0:T(8,128)S(1)}, f32[40,1024]{1,0:T(8,128)S(1)}, u32[]{:S(2)}, u32[]{:S(2)}) %collective-permute-start.43) | collective-permute-done | bytes 163872 | tf_op jit(solution)/shard_map/ppermute | solution.py:290
  541.1 8.3 %collective-permute-done.31 = f32[3,32,1024]{2,1,0:T(8,128)S(1)} collective-permute-done((f32[3,32,1024]{2,1,0:T(8,128)S(1)}, f32[3,32,1024]{2,1,0:T(8,128)S(1)}, u32[]{:S(2)}, u32[]{:S(2)}) %collective-permute-start.31) | collective-permute-done | bytes 393248 | tf_op jit(solution)/shard_map/ppermute | solution.py:289
  549.5 4.6 collective-permute-done.33
  554.3 9.3 %pair_dots.1 = f32[32,136,128]{2,1,0:T(8,128)S(1)} custom-call(s32[2,6,32]{2,1,0:T(8,128)S(1)} %pad_add_fusion.ids, f32[4,3,32,1024]{3,2,1,0:T(8,128)S(1)} %pad_maximum_fusion.4.early, f32[4,40,1024]{2,1,0:T(8,128)S(1)} %pad_maximum_fusion.5.late), custom_call_target="tpu_custom_call" | custom-call | tf_op jit(solution)/shard_map/pair_dots/pallas_call | solution.py:242
  563.8 2.9 collective-permute-done.44
  568.4 1.6 collective-permute-start.45
  569.9 7.0 %collective-permute-done.47 = f32[2,1,1,2,136,128]{5,4,3,2,1,0:T(8,128)S(1)} collective-permute-done((f32[2,1,1,2,136,128]{5,4,3,2,1,0:T(8,128)S(1)}, f32[2,1,1,2,136,128]{5,4,3,2,1,0:T(8,128)S(1)}, u32[]{:S(2)}, u32[]{:S(2)}) %collective-permute-start.47) | collective-permute-done | bytes 278560 | tf_op jit(solution)/shard_map/ppermute | solution.py:266
  577.0 1.6 collective-permute-start.48
  579.0 3.1 collective-permute-done.48
  582.1 1.6 collective-permute-done.46
  (299 shorter events, 61.2 us)
Async XLA Ops:
  6.5 13.5 %collective-permute-start = (s32[16,2]{0,1:T(2,128)}, s32[16,2]{0,1:T(2,128)S(1)}, u32[]{:S(2)}, u32[]{:S(2)}) collective-permute-start(s32[16,2]{0,1:T(2,128)} %param.12), channel_id=1, source_target_pairs={{0,4},{4,0},{1,5},{5,1},{2,6},{6,2},{3,7},{7,3},{8,12},{12,8},{9,1... | collective-permute-start | bytes 392 | tf_op jit(solution)/shard_map/ppermute | solution.py:370
  10.2 5.4 collective-permute-start.1
  15.0 24.5 %collective-permute-start.3 = (bf16[4096,128]{1,0:T(8,128)(2,1)S(1)}, bf16[4096,128]{1,0:T(8,128)(2,1)S(1)}, u32[]{:S(2)}, u32[]{:S(2)}) collective-permute-start(bf16[4096,128]{1,0:T(8,128)(2,1)S(1)} %constant_dynamic-slice_fusion.18), channel_id=1, source_target_pairs={{0,4},{4,0},{1,5},{5,1},{2,6},{6,2},{3,7},{7,3},{8,12},{12,8},{9,1... | collective-permute-start | bytes 3145736 | tf_op jit(solution)/shard_map/ppermute | solution.py:281
  15.6 23.9 %collective-permute-start.2 = (s32[2,4,128]{2,1,0:T(4,128)S(1)}, s32[2,4,128]{2,1,0:T(4,128)S(1)}, u32[]{:S(2)}, u32[]{:S(2)}) collective-permute-start(s32[2,4,128]{2,1,0:T(4,128)S(1)} %get-tuple-element.150), channel_id=1, source_target_pairs={{0,4},{4,0},{1,5},{5,1},{2,6},{6,2},{3,7},{7,3},{8,12},{12,8},{9,1... | collective-permute-start | bytes 12296 | tf_op jit(solution)/shard_map/ppermute | solution.py:369
  20.0 23.0 %copy-start.30 = (s32[16,2]{0,1:T(2,128)}, s32[16,2]{0,1:T(2,128)S(1)}, u32[]{:S(2)}) copy-start(s32[16,2]{0,1:T(2,128)S(1)} %collective-permute-done) | copy-start | bytes 388
  39.5 43.3 %collective-permute-start.4 = (bf16[7680,128]{1,0:T(8,128)(2,1)}, bf16[7680,128]{1,0:T(8,128)(2,1)S(1)}, u32[]{:S(2)}, u32[]{:S(2)}) collective-permute-start(bf16[7680,128]{1,0:T(8,128)(2,1)} %constant_dynamic-slice_fusion.16), channel_id=1, source_target_pairs={{0,4},{4,0},{1,5},{5,1},{2,6},{6,2},{3,7},{7,3},{8,12},{12,8},{9,1... | collective-permute-start | bytes 5898248 | tf_op jit(solution)/shard_map/ppermute | solution.py:281
  43.2 42.4 %copy-start.3 = (bf16[4096,256]{1,0:T(8,128)(2,1)}, bf16[4096,256]{1,0:T(8,128)(2,1)S(1)}, u32[]{:S(2)}) copy-start(bf16[4096,256]{1,0:T(8,128)(2,1)S(1)} %pad_maximum_fusion.2.refs_2_) | copy-start | bytes 6291460
  43.2 66.0 %collective-permute-start.7 = (bf16[4096,256]{1,0:T(8,128)(2,1)S(1)}, bf16[4096,256]{1,0:T(8,128)(2,1)}, u32[]{:S(2)}, u32[]{:S(2)}) collective-permute-start(bf16[4096,256]{1,0:T(8,128)(2,1)S(1)} %pad_maximum_fusion.2.refs_2_), channel_id=1, source_target_pairs={{0,8},{8,0},{16,24},{24,16},{1,9},{9,1},{17,25},{25,17},{2,10},{10... | collective-permute-start | bytes 6291464 | tf_op jit(solution)/shard_map/ppermute | solution.py:281
  43.3 44.7 %collective-permute-start.8 = (bf16[4096,256]{1,0:T(8,128)(2,1)S(1)}, bf16[4096,256]{1,0:T(8,128)(2,1)S(1)}, u32[]{:S(2)}, u32[]{:S(2)}) collective-permute-start(bf16[4096,256]{1,0:T(8,128)(2,1)S(1)} %pad_maximum_fusion.2.refs_2_), channel_id=1, source_target_pairs={{8,16},{16,8},{9,17},{17,9},{10,18},{18,10},{11,19},{19,11},{12,20... | collective-permute-start | bytes 6291464 | tf_op jit(solution)/shard_map/ppermute | solution.py:281
  82.7 25.9 %collective-permute-start.5 = (bf16[4608,128]{1,0:T(8,128)(2,1)S(1)}, bf16[4608,128]{1,0:T(8,128)(2,1)}, u32[]{:S(2)}, u32[]{:S(2)}) collective-permute-start(bf16[4608,128]{1,0:T(8,128)(2,1)S(1)} %constant_dynamic-slice_fusion.17), channel_id=1, source_target_pairs={{0,4},{4,0},{1,5},{5,1},{2,6},{6,2},{3,7},{7,3},{8,12},{12,8},{9,1... | collective-permute-start | bytes 3538952 | tf_op jit(solution)/shard_map/ppermute | solution.py:281
  89.3 87.0 %collective-permute-start.14 = (bf16[7680,256]{1,0:T(8,128)(2,1)}, bf16[7680,256]{1,0:T(8,128)(2,1)}, u32[]{:S(2)}, u32[]{:S(2)}) collective-permute-start(bf16[7680,256]{1,0:T(8,128)(2,1)} %pad_maximum_fusion.refs_1_), channel_id=1, source_target_pairs={{8,16},{16,8},{9,17},{17,9},{10,18},{18,10},{11,19},{19,11},{12,20... | collective-permute-start | bytes 11796488 | tf_op jit(solution)/shard_map/ppermute | solution.py:281
  108.7 67.1 %collective-permute-start.6 = (bf16[94,128,128]{2,1,0:T(8,128)(2,1)}, bf16[94,128,128]{2,1,0:T(8,128)(2,1)}, u32[]{:S(2)}, u32[]{:S(2)}) collective-permute-start(bf16[94,128,128]{2,1,0:T(8,128)(2,1)} %pack_tiles.4), channel_id=1, source_target_pairs={{0,4},{4,0},{1,5},{5,1},{2,6},{6,2},{3,7},{7,3},{8,12},{12,8},{9,1... | collective-permute-start | bytes 9240584 | tf_op jit(solution)/shard_map/ppermute | solution.py:281
  109.2 83.2 %collective-permute-start.9 = (bf16[7680,256]{1,0:T(8,128)(2,1)}, bf16[7680,256]{1,0:T(8,128)(2,1)}, u32[]{:S(2)}, u32[]{:S(2)}) collective-permute-start(bf16[7680,256]{1,0:T(8,128)(2,1)} %pad_maximum_fusion.refs_1_), channel_id=1, source_target_pairs={{0,8},{8,0},{16,24},{24,16},{1,9},{9,1},{17,25},{25,17},{2,10},{10... | collective-permute-start | bytes 11796488 | tf_op jit(solution)/shard_map/ppermute | solution.py:281
  175.7 73.7 %collective-permute-start.11 = (bf16[104,128,128]{2,1,0:T(8,128)(2,1)S(1)}, bf16[104,128,128]{2,1,0:T(8,128)(2,1)}, u32[]{:S(2)}, u32[]{:S(2)}) collective-permute-start(bf16[104,128,128]{2,1,0:T(8,128)(2,1)S(1)} %pack_tiles.5), channel_id=1, source_target_pairs={{0,4},{4,0},{1,5},{5,1},{2,6},{6,2},{3,7},{7,3},{8,12},{12,8},{9,1... | collective-permute-start | bytes 10223624 | tf_op jit(solution)/shard_map/ppermute | solution.py:281
  176.3 30.7 %collective-permute-start.15 = (bf16[4096,256]{1,0:T(8,128)(2,1)}, bf16[4096,256]{1,0:T(8,128)(2,1)}, u32[]{:S(2)}, u32[]{:S(2)}) collective-permute-start(bf16[4096,256]{1,0:T(8,128)(2,1)} %collective-permute-done.7.refs_3_), channel_id=1, source_target_pairs={{8,16},{16,8},{9,17},{17,9},{10,18},{18,10},{11,19},{19,11},{12,20... | collective-permute-start | bytes 6291464 | tf_op jit(solution)/shard_map/ppermute | solution.py:281
  192.4 45.8 %collective-permute-start.10 = (bf16[4096,256]{1,0:T(8,128)(2,1)}, bf16[4096,256]{1,0:T(8,128)(2,1)}, u32[]{:S(2)}, u32[]{:S(2)}) collective-permute-start(bf16[4096,256]{1,0:T(8,128)(2,1)} %copy-done.14), channel_id=1, source_target_pairs={{8,0},{16,24},{9,1},{17,25},{10,2},{18,26},{11,3},{19,27},{12,4},{... | collective-permute-start | bytes 6291464 | tf_op jit(solution)/shard_map/ppermute | solution.py:281
  199.1 75.8 %collective-permute-start.12 = (bf16[104,128,128]{2,1,0:T(8,128)(2,1)}, bf16[104,128,128]{2,1,0:T(8,128)(2,1)}, u32[]{:S(2)}, u32[]{:S(2)}) collective-permute-start(bf16[104,128,128]{2,1,0:T(8,128)(2,1)} %pack_tiles.6), channel_id=1, source_target_pairs={{0,8},{24,16},{1,9},{25,17},{2,10},{26,18},{3,11},{27,19},{4,12},{... | collective-permute-start | bytes 10223624 | tf_op jit(solution)/shard_map/ppermute | solution.py:281
  207.0 75.4 %collective-permute-start.16 = (bf16[7680,256]{1,0:T(8,128)(2,1)}, bf16[7680,256]{1,0:T(8,128)(2,1)}, u32[]{:S(2)}, u32[]{:S(2)}) collective-permute-start(bf16[7680,256]{1,0:T(8,128)(2,1)} %collective-permute-done.9.refs_2_), channel_id=1, source_target_pairs={{8,16},{16,8},{9,17},{17,9},{10,18},{18,10},{11,19},{19,11},{12,20... | collective-permute-start | bytes 11796488 | tf_op jit(solution)/shard_map/ppermute | solution.py:281
  238.2 83.3 %collective-permute-start.19 = (bf16[7680,256]{1,0:T(8,128)(2,1)}, bf16[7680,256]{1,0:T(8,128)(2,1)}, u32[]{:S(2)}, u32[]{:S(2)}) collective-permute-start(bf16[7680,256]{1,0:T(8,128)(2,1)} %collective-permute-done.14.refs_3_), channel_id=1, source_target_pairs={{8,0},{16,24},{9,1},{17,25},{10,2},{18,26},{11,3},{19,27},{12,4},{... | collective-permute-start | bytes 11796488 | tf_op jit(solution)/shard_map/ppermute | solution.py:281
  249.4 126.2 %collective-permute-start.18 = (bf16[160,128,128]{2,1,0:T(8,128)(2,1)}, bf16[160,128,128]{2,1,0:T(8,128)(2,1)}, u32[]{:S(2)}, u32[]{:S(2)}) collective-permute-start(bf16[160,128,128]{2,1,0:T(8,128)(2,1)} %pack_tiles.7), channel_id=1, source_target_pairs={{0,4},{4,0},{1,5},{5,1},{2,6},{6,2},{3,7},{7,3},{8,12},{12,8},{9,1... | collective-permute-start | bytes 15728648 | tf_op jit(solution)/shard_map/ppermute | solution.py:281
  252.0 29.2 %copy-start.19 = (s32[4,32]{1,0:T(4,128)S(1)}, s32[4,32]{1,0:T(4,128)}, u32[]{:S(2)}) copy-start(s32[4,32]{1,0:T(4,128)} %reshape.348) | copy-start | bytes 1540
  252.0 29.5 %copy-start.29 = (s32[2]{0:T(128)S(1)}, s32[2]{0:T(128)}, u32[]{:S(2)}) copy-start(s32[2]{0:T(128)} %get-tuple-element.166) | copy-start | bytes 28
  252.1 30.1 %copy-start.22 = (s32[3,48]{1,0:T(4,128)S(1)}, s32[3,48]{1,0:T(4,128)}, u32[]{:S(2)}) copy-start(s32[3,48]{1,0:T(4,128)} %reshape.356) | copy-start | bytes 1732
  252.1 30.2 %copy-start.28 = (s32[128]{0:T(128)S(1)}, s32[128]{0:T(128)}, u32[]{:S(2)}) copy-start(s32[128]{0:T(128)} %reshape.344) | copy-start | bytes 1540
  252.1 32.7 %copy-start.21 = (s32[3,48]{1,0:T(4,128)S(1)}, s32[3,48]{1,0:T(4,128)}, u32[]{:S(2)}) copy-start(s32[3,48]{1,0:T(4,128)} %reshape.372) | copy-start | bytes 1732
  252.1 32.7 %copy-start.27 = (s32[128]{0:T(128)S(1)}, s32[128]{0:T(128)}, u32[]{:S(2)}) copy-start(s32[128]{0:T(128)} %sub.172) | copy-start | bytes 1540
  274.8 48.5 %collective-permute-start.13 = (bf16[4608,256]{1,0:T(8,128)(2,1)S(1)}, bf16[4608,256]{1,0:T(8,128)(2,1)}, u32[]{:S(2)}, u32[]{:S(2)}) collective-permute-start(bf16[4608,256]{1,0:T(8,128)(2,1)S(1)} %pad_maximum_fusion.1.refs_2_.refs_1_), channel_id=1, source_target_pairs={{0,8},{24,16},{1,9},{25,17},{2,10},{26,18},{3,11},{27,19},{4,12},{... | collective-permute-start | bytes 7077896 | tf_op jit(solution)/shard_map/ppermute | solution.py:281
  282.3 69.7 %collective-permute-start.17 = (bf16[4608,256]{1,0:T(8,128)(2,1)S(1)}, bf16[4608,256]{1,0:T(8,128)(2,1)}, u32[]{:S(2)}, u32[]{:S(2)}) collective-permute-start(bf16[4608,256]{1,0:T(8,128)(2,1)S(1)} %pad_maximum_fusion.1.refs_2_.refs_1_), channel_id=1, source_target_pairs={{8,16},{16,8},{9,17},{17,9},{10,18},{18,10},{11,19},{19,11},{12,20... | collective-permute-start | bytes 7077896 | tf_op jit(solution)/shard_map/ppermute | solution.py:281
  286.5 36.3 %copy-start.20 = (s32[3,48]{1,0:T(4,128)S(1)}, s32[3,48]{1,0:T(4,128)}, u32[]{:S(2)}) copy-start(s32[3,48]{1,0:T(4,128)} %sub.204) | copy-start | bytes 1732
  286.5 36.6 %copy-start.18 = (s32[144]{0:T(256)S(1)}, s32[144]{0:T(256)}, u32[]{:S(2)}) copy-start(s32[144]{0:T(256)} %copy-done.17) | copy-start | bytes 1732
  286.5 52.6 %copy-start.24 = (s32[144]{0:T(256)S(1)}, s32[144]{0:T(256)}, u32[]{:S(2)}) copy-start(s32[144]{0:T(256)} %sub.181) | copy-start | bytes 1732
  321.5 90.8 %collective-permute-start.34 = (bf16[7680,256]{1,0:T(8,128)(2,1)}, bf16[7680,256]{1,0:T(8,128)(2,1)}, u32[]{:S(2)}, u32[]{:S(2)}) collective-permute-start(bf16[7680,256]{1,0:T(8,128)(2,1)} %collective-permute-done.16.refs_2_), channel_id=1, source_target_pairs={{8,0},{16,24},{9,1},{17,25},{10,2},{18,26},{11,3},{19,27},{12,4},{... | collective-permute-start | bytes 11796488 | tf_op jit(solution)/shard_map/ppermute | solution.py:281
  323.4 90.4 %collective-permute-start.23 = (bf16[104,128,128]{2,1,0:T(8,128)(2,1)}, bf16[104,128,128]{2,1,0:T(8,128)(2,1)}, u32[]{:S(2)}, u32[]{:S(2)}) collective-permute-start(bf16[104,128,128]{2,1,0:T(8,128)(2,1)} %collective-permute-done.11.refs_1_), channel_id=1, source_target_pairs={{0,8},{24,16},{1,9},{25,17},{2,10},{26,18},{3,11},{27,19},{4,12},{... | collective-permute-start | bytes 10223624 | tf_op jit(solution)/shard_map/ppermute | solution.py:281
  352.0 61.8 %collective-permute-start.24 = (bf16[4608,256]{1,0:T(8,128)(2,1)}, bf16[4608,256]{1,0:T(8,128)(2,1)S(1)}, u32[]{:S(2)}, u32[]{:S(2)}) collective-permute-start(bf16[4608,256]{1,0:T(8,128)(2,1)} %collective-permute-done.13.refs_3_), channel_id=1, source_target_pairs={{8,16},{16,8},{9,17},{17,9},{10,18},{18,10},{11,19},{19,11},{12,20... | collective-permute-start | bytes 7077896 | tf_op jit(solution)/shard_map/ppermute | solution.py:281
  392.4 21.4 %copy-start.12 = (f32[3,256,1024]{2,1,0:T(8,128)}, f32[3,256,1024]{2,1,0:T(8,128)S(1)}, u32[]{:S(2)}) copy-start(f32[3,256,1024]{2,1,0:T(8,128)S(1)} %maximum_add_fusion) | copy-start | bytes 9437188
  393.8 54.8 %collective-permute-start.20 = (f32[3,128,1024]{2,1,0:T(8,128)}, f32[3,128,1024]{2,1,0:T(8,128)}, u32[]{:S(2)}, u32[]{:S(2)}) collective-permute-start(f32[3,128,1024]{2,1,0:T(8,128)} %constant_dynamic-slice_fusion.14), channel_id=1, source_target_pairs={{0,1},{1,0},{2,3},{3,2},{4,5},{5,4},{6,7},{7,6},{8,9},{9,8},{10,11... | collective-permute-start | bytes 4718600 | tf_op jit(solution)/shard_map/ppermute | solution.py:266
  412.3 50.2 %collective-permute-start.35 = (bf16[4096,256]{1,0:T(8,128)(2,1)}, bf16[4096,256]{1,0:T(8,128)(2,1)}, u32[]{:S(2)}, u32[]{:S(2)}) collective-permute-start(bf16[4096,256]{1,0:T(8,128)(2,1)} %collective-permute-done.15.refs_2_), channel_id=1, source_target_pairs={{8,0},{16,24},{9,1},{17,25},{10,2},{18,26},{11,3},{19,27},{12,4},{... | collective-permute-start | bytes 6291464 | tf_op jit(solution)/shard_map/ppermute | solution.py:281
  433.9 26.2 %collective-permute-start.25 = (f32[3,128,1024]{2,1,0:T(8,128)}, f32[3,128,1024]{2,1,0:T(8,128)}, u32[]{:S(2)}, u32[]{:S(2)}) collective-permute-start(f32[3,128,1024]{2,1,0:T(8,128)} %fusion.4), channel_id=1, source_target_pairs={{0,1},{1,0},{2,3},{3,2},{4,5},{5,4},{6,7},{7,6},{8,9},{9,8},{10,11... | collective-permute-start | bytes 4718600 | tf_op jit(solution)/shard_map/ppermute | solution.py:266
  436.7 11.9 %copy-start.13 = (f32[3,256,1024]{2,1,0:T(8,128)S(1)}, f32[3,256,1024]{2,1,0:T(8,128)}, u32[]{:S(2)}) copy-start(f32[3,256,1024]{2,1,0:T(8,128)} %copy-done.12) | copy-start | bytes 9437188
  450.7 9.5 %copy-start.7 = (f32[3,256,512]{2,1,0:T(8,128)S(1)}, f32[3,256,512]{2,1,0:T(8,128)}, u32[]{:S(2)}) copy-start(f32[3,256,512]{2,1,0:T(8,128)} %copy-done.6) | copy-start | bytes 4718596
  450.7 9.5 %copy-start.9 = (f32[3,256,512]{2,1,0:T(8,128)S(1)}, f32[3,256,512]{2,1,0:T(8,128)}, u32[]{:S(2)}) copy-start(f32[3,256,512]{2,1,0:T(8,128)} %copy-done.8) | copy-start | bytes 4718596
  450.7 20.4 %collective-permute-start.21 = (f32[3,64,1024]{2,1,0:T(8,128)S(1)}, f32[3,64,1024]{2,1,0:T(8,128)S(1)}, u32[]{:S(2)}, u32[]{:S(2)}) collective-permute-start(f32[3,64,1024]{2,1,0:T(8,128)S(1)} %constant_dynamic-slice_fusion.13), channel_id=1, source_target_pairs={{0,4},{4,0},{1,5},{5,1},{2,6},{6,2},{3,7},{7,3},{8,12},{12,8},{9,1... | collective-permute-start | bytes 2359304 | tf_op jit(solution)/shard_map/ppermute | solution.py:266
  462.0 25.6 %collective-permute-start.26 = (f32[3,64,1024]{2,1,0:T(8,128)S(1)}, f32[3,64,1024]{2,1,0:T(8,128)S(1)}, u32[]{:S(2)}, u32[]{:S(2)}) collective-permute-start(f32[3,64,1024]{2,1,0:T(8,128)S(1)} %constant_dynamic-slice_fusion.11), channel_id=1, source_target_pairs={{0,4},{4,0},{1,5},{5,1},{2,6},{6,2},{3,7},{7,3},{8,12},{12,8},{9,1... | collective-permute-start | bytes 2359304 | tf_op jit(solution)/shard_map/ppermute | solution.py:266
  470.8 19.1 %collective-permute-start.36 = (f32[1,128,1024]{2,1,0:T(8,128)S(1)}, f32[1,128,1024]{2,1,0:T(8,128)S(1)}, u32[]{:S(2)}, u32[]{:S(2)}) collective-permute-start(f32[1,128,1024]{2,1,0:T(8,128)S(1)} %constant_dynamic-slice_fusion.9), channel_id=1, source_target_pairs={{0,1},{1,0},{2,3},{3,2},{4,5},{5,4},{6,7},{7,6},{8,9},{9,8},{10,11... | collective-permute-start | bytes 1572872 | tf_op jit(solution)/shard_map/ppermute | solution.py:266
  487.7 12.1 %collective-permute-start.27 = (f32[3,32,1024]{2,1,0:T(8,128)S(1)}, f32[3,32,1024]{2,1,0:T(8,128)S(1)}, u32[]{:S(2)}, u32[]{:S(2)}) collective-permute-start(f32[3,32,1024]{2,1,0:T(8,128)S(1)} %constant_dynamic-slice_fusion.10), channel_id=1, source_target_pairs={{0,2},{2,0},{1,3},{3,1},{4,6},{6,4},{5,7},{7,5},{8,10},{10,8},{9,1... | collective-permute-start | bytes 1179656 | tf_op jit(solution)/shard_map/ppermute | solution.py:266
  489.3 17.6 %collective-permute-start.22 = (f32[3,32,1024]{2,1,0:T(8,128)S(1)}, f32[3,32,1024]{2,1,0:T(8,128)S(1)}, u32[]{:S(2)}, u32[]{:S(2)}) collective-permute-start(f32[3,32,1024]{2,1,0:T(8,128)S(1)} %constant_dynamic-slice_fusion.12), channel_id=1, source_target_pairs={{0,2},{2,0},{1,3},{3,1},{4,6},{6,4},{5,7},{7,5},{8,10},{10,8},{9,1... | collective-permute-start | bytes 1179656 | tf_op jit(solution)/shard_map/ppermute | solution.py:266
  490.0 17.0 %collective-permute-start.37 = (f32[1,64,1024]{2,1,0:T(8,128)S(1)}, f32[1,64,1024]{2,1,0:T(8,128)S(1)}, u32[]{:S(2)}, u32[]{:S(2)}) collective-permute-start(f32[1,64,1024]{2,1,0:T(8,128)S(1)} %constant_dynamic-slice_fusion.8), channel_id=1, source_target_pairs={{0,4},{4,0},{1,5},{5,1},{2,6},{6,2},{3,7},{7,3},{8,12},{12,8},{9,1... | collective-permute-start | bytes 786440 | tf_op jit(solution)/shard_map/ppermute | solution.py:266
  499.9 12.0 %collective-permute-start.28 = (f32[3,32,1024]{2,1,0:T(8,128)S(1)}, f32[3,32,1024]{2,1,0:T(8,128)S(1)}, u32[]{:S(2)}, u32[]{:S(2)}) collective-permute-start(f32[3,32,1024]{2,1,0:T(8,128)S(1)} %dynamic-slice_add_fusion.5), channel_id=1, source_target_pairs={{8,0},{16,24},{9,1},{17,25},{10,2},{18,26},{11,3},{19,27},{12,4},{... | collective-permute-start | bytes 1179656 | tf_op jit(solution)/shard_map/ppermute | solution.py:436
  507.1 6.3 %collective-permute-start.38 = (f32[1,32,1024]{2,1,0:T(8,128)S(1)}, f32[1,32,1024]{2,1,0:T(8,128)S(1)}, u32[]{:S(2)}, u32[]{:S(2)}) collective-permute-start(f32[1,32,1024]{2,1,0:T(8,128)S(1)} %constant_dynamic-slice_fusion.7), channel_id=1, source_target_pairs={{0,2},{2,0},{1,3},{3,1},{4,6},{6,4},{5,7},{7,5},{8,10},{10,8},{9,1... | collective-permute-start | bytes 393224 | tf_op jit(solution)/shard_map/ppermute | solution.py:266
  511.9 14.1 %collective-permute-start.29 = (f32[3,32,1024]{2,1,0:T(8,128)S(1)}, f32[3,32,1024]{2,1,0:T(8,128)S(1)}, u32[]{:S(2)}, u32[]{:S(2)}) collective-permute-start(f32[3,32,1024]{2,1,0:T(8,128)S(1)} %fusion.9), channel_id=1, source_target_pairs={{0,8},{8,0},{16,24},{24,16},{1,9},{9,1},{17,25},{25,17},{2,10},{10... | collective-permute-start | bytes 1179656 | tf_op jit(solution)/shard_map/ppermute | solution.py:286
  512.7 16.9 %collective-permute-start.30 = (f32[3,32,1024]{2,1,0:T(8,128)S(1)}, f32[3,32,1024]{2,1,0:T(8,128)S(1)}, u32[]{:S(2)}, u32[]{:S(2)}) collective-permute-start(f32[3,32,1024]{2,1,0:T(8,128)S(1)} %fusion.9), channel_id=1, source_target_pairs={{8,16},{16,8},{9,17},{17,9},{10,18},{18,10},{11,19},{19,11},{12,20... | collective-permute-start | bytes 1179656 | tf_op jit(solution)/shard_map/ppermute | solution.py:287
  513.5 10.6 %collective-permute-start.39 = (f32[40,1024]{1,0:T(8,128)S(1)}, f32[40,1024]{1,0:T(8,128)S(1)}, u32[]{:S(2)}, u32[]{:S(2)}) collective-permute-start(f32[40,1024]{1,0:T(8,128)S(1)} %get-tuple-element.148), channel_id=1, source_target_pairs={{0,8},{8,0},{16,24},{24,16},{1,9},{9,1},{17,25},{25,17},{2,10},{10... | collective-permute-start | bytes 491528 | tf_op jit(solution)/shard_map/ppermute | solution.py:286
  516.5 8.2 %collective-permute-start.40 = (f32[40,1024]{1,0:T(8,128)S(1)}, f32[40,1024]{1,0:T(8,128)S(1)}, u32[]{:S(2)}, u32[]{:S(2)}) collective-permute-start(f32[40,1024]{1,0:T(8,128)S(1)} %get-tuple-element.148), channel_id=1, source_target_pairs={{8,16},{16,8},{9,17},{17,9},{10,18},{18,10},{11,19},{19,11},{12,20... | collective-permute-start | bytes 491528 | tf_op jit(solution)/shard_map/ppermute | solution.py:287
  524.1 4.3 collective-permute-start.42
  524.7 8.0 %collective-permute-start.41 = (f32[40,1024]{1,0:T(8,128)S(1)}, f32[40,1024]{1,0:T(8,128)S(1)}, u32[]{:S(2)}, u32[]{:S(2)}) collective-permute-start(f32[40,1024]{1,0:T(8,128)S(1)} %collective-permute-done.40), channel_id=1, source_target_pairs={{8,0},{16,24},{9,1},{17,25},{10,2},{18,26},{11,3},{19,27},{12,4},{... | collective-permute-start | bytes 491528 | tf_op jit(solution)/shard_map/ppermute | solution.py:289
  526.1 6.7 %collective-permute-start.32 = (f32[3,32,1024]{2,1,0:T(8,128)S(1)}, f32[3,32,1024]{2,1,0:T(8,128)S(1)}, u32[]{:S(2)}, u32[]{:S(2)}) collective-permute-start(f32[3,32,1024]{2,1,0:T(8,128)S(1)} %collective-permute-done.29), channel_id=1, source_target_pairs={{8,16},{16,8},{9,17},{17,9},{10,18},{18,10},{11,19},{19,11},{12,20... | collective-permute-start | bytes 1179656 | tf_op jit(solution)/shard_map/ppermute | solution.py:288
  528.3 12.7 %collective-permute-start.43 = (f32[40,1024]{1,0:T(8,128)S(1)}, f32[40,1024]{1,0:T(8,128)S(1)}, u32[]{:S(2)}, u32[]{:S(2)}) collective-permute-start(f32[40,1024]{1,0:T(8,128)S(1)} %collective-permute-done.42), channel_id=1, source_target_pairs={{8,0},{16,24},{9,1},{17,25},{10,2},{18,26},{11,3},{19,27},{12,4},{... | collective-permute-start | bytes 491528 | tf_op jit(solution)/shard_map/ppermute | solution.py:290
  529.6 19.8 %collective-permute-start.31 = (f32[3,32,1024]{2,1,0:T(8,128)S(1)}, f32[3,32,1024]{2,1,0:T(8,128)S(1)}, u32[]{:S(2)}, u32[]{:S(2)}) collective-permute-start(f32[3,32,1024]{2,1,0:T(8,128)S(1)} %collective-permute-done.30), channel_id=1, source_target_pairs={{8,0},{16,24},{9,1},{17,25},{10,2},{18,26},{11,3},{19,27},{12,4},{... | collective-permute-start | bytes 1179656 | tf_op jit(solution)/shard_map/ppermute | solution.py:289
  532.8 21.4 %collective-permute-start.33 = (f32[3,32,1024]{2,1,0:T(8,128)S(1)}, f32[3,32,1024]{2,1,0:T(8,128)S(1)}, u32[]{:S(2)}, u32[]{:S(2)}) collective-permute-start(f32[3,32,1024]{2,1,0:T(8,128)S(1)} %collective-permute-done.32), channel_id=1, source_target_pairs={{8,0},{16,24},{9,1},{17,25},{10,2},{18,26},{11,3},{19,27},{12,4},{... | collective-permute-start | bytes 1179656 | tf_op jit(solution)/shard_map/ppermute | solution.py:290
  563.7 3.0 collective-permute-start.44
  568.2 8.8 %collective-permute-start.47 = (f32[2,1,1,2,136,128]{5,4,3,2,1,0:T(8,128)S(1)}, f32[2,1,1,2,136,128]{5,4,3,2,1,0:T(8,128)S(1)}, u32[]{:S(2)}, u32[]{:S(2)}) collective-permute-start(f32[2,1,1,2,136,128]{5,4,3,2,1,0:T(8,128)S(1)} %constant_dynamic-slice_fusion.3), channel_id=1, source_target_pairs={{0,2},{2,0},{1,3},{3,1},{4,6},{6,4},{5,7},{7,5},{8,10},{10,8},{9,1... | collective-permute-start | bytes 835592 | tf_op jit(solution)/shard_map/ppermute | solution.py:266
  568.4 10.2 %collective-permute-start.45 = (f32[1,2,1,2,136,128]{5,4,3,2,1,0:T(8,128)S(1)}, f32[1,2,1,2,136,128]{5,4,3,2,1,0:T(8,128)S(1)}, u32[]{:S(2)}, u32[]{:S(2)}) collective-permute-start(f32[1,2,1,2,136,128]{5,4,3,2,1,0:T(8,128)S(1)} %constant_dynamic-slice_fusion.5), channel_id=1, source_target_pairs={{0,4},{4,0},{1,5},{5,1},{2,6},{6,2},{3,7},{7,3},{8,12},{12,8},{9,1... | collective-permute-start | bytes 835592 | tf_op jit(solution)/shard_map/ppermute | solution.py:266
  577.0 5.1 collective-permute-start.48
  578.6 5.1 collective-permute-start.46
  (16 other events, 43.9 us)

commit v14 on v13

--- a/solution.py
+++ b/solution.py
@@ -416,7 +416,11 @@
     first_three = part0 + part2 + in_row_order(part1, 2)
 
     end2 = times(2, [hist] + tiles[2], every, [[far[2]]], row_places)
-    end1 = times(1, [hist] + tiles[1], every, [[far[1], outer[2]]], row_places)
+    first_three = scatter_sum(first_three, "core", 1)
+    end1 = product(
+        [hist] + tiles[1], [m[:, cuts[1] : cuts[2]] for m in masks], [[far[1], outer[2]]],
+        after(inner, first_three), x * columns + cuts[1], row_places,
+    )
     end0 = times(0, [hist] + tiles[0], every, [[far[0], outer[3]]], row_places)
     last_one = end0 + (end1 + end2)
     guest = jnp.concatenate([guest, product([loans[0]], [guest_masks[0]], [[far[2]]], inner, 0, [0])])
@@ -432,7 +436,7 @@
     def summed(totals):
         return scatter_sum(scatter_sum(scatter_sum(totals, "core", 1), "x", 1), "y", 1)
 
-    first_three = summed(first_three)
+    first_three = scatter_sum(scatter_sum(first_three, "x", 1), "y", 1)
     visitors = lax.ppermute(summed(visitors), "z", OUTWARD)
     early = first_three.at[1:].add(visitors[:2])
     early = jnp.stack(along_line(early, inner))

time: 603 us -> 593 us (0.983)
    ppermute x14, waiting for transfers between devices: 45.2 us -> 39 us  [scatter_sum(): total = total + lax.ppermute(part((here + k) % count), axis, turn(count, k))]
  transfers between devices with their start and end apart: 49 -> 49, of which waited for: 25 -> 23; matrix products, arithmetic and copies ran while one was open for 7% -> 7% of each run, Pallas kernels for 20% -> 21%
where the time goes in v14:
time: 593 us; the launch traced here: 584 us
  waiting for transfers between devices  305 us (51%)
  Pallas kernels  130 us (22%)
  starting transfers between devices  79.3 us (13%)
  local copies, waits for them, and re-layouts  25.7 us (4%)
  other arithmetic  24.8 us (4%)
  between operations  19.5 us (3%)
    ppermute x21, waiting for transfers between devices, send(): lax.ppermute(v, axis, route)  215 us
    pallas_call x10, Pallas kernels, product(): pl.pallas_call(functools.partial(product_kernel, blk, row_blocks, stride,...  105 us
    ppermute x21, starting transfers between devices, send(): lax.ppermute(v, axis, route)  48.6 us
    ppermute x14, waiting for transfers between devices, scatter_sum(): total = total + lax.ppermute(part((here + k) % count), axis, turn(count, k))  39 us
    ppermute x1, waiting for transfers between devices, body(): lax.ppermute(both_of(o), 'x', r)  19.4 us
    pallas_call x4, Pallas kernels, pack(): pl.pallas_call(functools.partial(pack_kernel, blk, row_blocks, columns, s...  15.6 us
  transfers between devices with their start and end apart: 49, of which 23 were waited for; matrix products, arithmetic and copies ran while one was open for 7% of the time, Pallas kernels for 21%

profile of v14, /device:TPU:0, one launch (start us, length us, event | category | flops | bytes accessed | tf_op | source)
XLA Modules:
  0.0 584.0 jit_solution(16623229846382186250)
XLA Ops:
  6.5 2.9 collective-permute-start
  10.2 3.5 collective-permute-start.1
  15.6 1.5 collective-permute-start.2
  17.1 3.0 constant_dynamic-slice_fusion.16
  20.0 19.4 %collective-permute-done.2 = s32[2,4,128]{2,1,0:T(4,128)S(1)} collective-permute-done((s32[2,4,128]{2,1,0:T(4,128)S(1)}, s32[2,4,128]{2,1,0:T(4,128)S(1)}, u32[]{:S(2)}, u32[]{:S(2)}) %collective-permute-start.2) | collective-permute-done | bytes 4128 | tf_op jit(solution)/shard_map/ppermute | solution.py:369
  41.3 1.6 broadcast_select_fusion.5
  44.1 38.6 %collective-permute-done.4 = bf16[7680,128]{1,0:T(8,128)(2,1)S(1)} collective-permute-done((bf16[7680,128]{1,0:T(8,128)(2,1)}, bf16[7680,128]{1,0:T(8,128)(2,1)S(1)}, u32[]{:S(2)}, u32[]{:S(2)}) %collective-permute-start.4) | collective-permute-done | bytes 1966112 | tf_op jit(solution)/shard_map/ppermute | solution.py:281
  83.3 2.3 broadcast_select_fusion.1
  85.6 2.3 pad_maximum_fusion.refs_1_
  89.2 2.6 collective-permute-start.14
  92.1 3.9 pack_tiles.4
  96.0 12.7 %collective-permute-done.5 = bf16[4608,128]{1,0:T(8,128)(2,1)} collective-permute-done((bf16[4608,128]{1,0:T(8,128)(2,1)S(1)}, bf16[4608,128]{1,0:T(8,128)(2,1)}, u32[]{:S(2)}, u32[]{:S(2)}) %collective-permute-start.5) | collective-permute-done | bytes 1179680 | tf_op jit(solution)/shard_map/ppermute | solution.py:281
  113.8 2.4 pack_tiles.5
  116.2 59.5 %collective-permute-done.6.refs_1_ = bf16[94,128,128]{2,1,0:T(8,128)(2,1)} collective-permute-done((bf16[94,128,128]{2,1,0:T(8,128)(2,1)}, bf16[94,128,128]{2,1,0:T(8,128)(2,1)}, u32[]{:S(2)}, u32[]{:S(2)}) %collective-permute-start.6) | collective-permute-done | bytes 3080224 | tf_op jit(solution)/shard_map/ppermute | solution.py:281
  176.3 2.0 collective-permute-start.15
  179.4 13.0 %collective-permute-done.9.refs_2_ = bf16[7680,256]{1,0:T(8,128)(2,1)} collective-permute-done((bf16[7680,256]{1,0:T(8,128)(2,1)}, bf16[7680,256]{1,0:T(8,128)(2,1)}, u32[]{:S(2)}, u32[]{:S(2)}) %collective-permute-start.9) | collective-permute-done | bytes 3932192 | tf_op jit(solution)/shard_map/ppermute | solution.py:281
  194.8 4.1 pack_tiles.6
  198.9 7.6 %collective-permute-start.12 = (bf16[104,128,128]{2,1,0:T(8,128)(2,1)}, bf16[104,128,128]{2,1,0:T(8,128)(2,1)}, u32[]{:S(2)}, u32[]{:S(2)}) collective-permute-start(bf16[104,128,128]{2,1,0:T(8,128)(2,1)} %pack_tiles.6), channel_id=1, source_target_pairs={{0,8},{24,16},{1,9},{25,17},{2,10},{26,18},{3,11},{27,19},{4,12},{... | collective-permute-start | bytes 10223624 | tf_op jit(solution)/shard_map/ppermute | solution.py:281
  207.6 2.6 collective-permute-start.16
  211.2 27.0 %collective-permute-done.10.refs_5_ = bf16[4096,256]{1,0:T(8,128)(2,1)} collective-permute-done((bf16[4096,256]{1,0:T(8,128)(2,1)}, bf16[4096,256]{1,0:T(8,128)(2,1)}, u32[]{:S(2)}, u32[]{:S(2)}) %collective-permute-start.10) | collective-permute-done | bytes 2097184 | tf_op jit(solution)/shard_map/ppermute | solution.py:281
  239.8 5.2 pack_tiles.7
  245.1 4.3 collective-permute-done.11.refs_1_
  249.9 2.1 broadcast_select_fusion.3
  252.3 22.2 %collective-permute-done.12.refs_0_ = bf16[104,128,128]{2,1,0:T(8,128)(2,1)} collective-permute-done((bf16[104,128,128]{2,1,0:T(8,128)(2,1)}, bf16[104,128,128]{2,1,0:T(8,128)(2,1)}, u32[]{:S(2)}, u32[]{:S(2)}) %collective-permute-start.12) | collective-permute-done | bytes 3407904 | tf_op jit(solution)/shard_map/ppermute | solution.py:281
  274.5 5.7 collective-permute-start.13
  282.6 2.0 collective-permute-start.17
  285.1 1.6 copy-done.3
  286.7 14.8 %tiles_times_planes.10 = f32[3,256,1024]{2,1,0:T(8,128)} custom-call(s32[268]{0:T(512)S(1)} %concatenate.66.info, bf16[512,32768]{1,0:T(8,128)(2,1)} %refs_0_.11, bf16[94,128,128]{2,1,0:T(8,128)(2,1)} %collective-permute-done.6.refs_1_, bf16[4096,256]{1,0:T(8,128)(2,1)S(1)} %copy-done.3, bf16[4096,256]{1,0:T(8,128)(2,1)} %collective-permute-done.7.refs_3_, ...), custom_call_target="tpu_custom_call" | custom-call | flops 6442450944 | bytes 10485760 | tf_op jit(solution)/shard_map/tiles_times_planes/pallas_call | solution.py:186
  301.5 20.0 %collective-permute-done.19.refs_4_ = bf16[7680,256]{1,0:T(8,128)(2,1)} collective-permute-done((bf16[7680,256]{1,0:T(8,128)(2,1)}, bf16[7680,256]{1,0:T(8,128)(2,1)}, u32[]{:S(2)}, u32[]{:S(2)}) %collective-permute-start.19) | collective-permute-done | bytes 3932192 | tf_op jit(solution)/shard_map/ppermute | solution.py:281
  323.4 15.7 %collective-permute-start.23 = (bf16[104,128,128]{2,1,0:T(8,128)(2,1)}, bf16[104,128,128]{2,1,0:T(8,128)(2,1)}, u32[]{:S(2)}, u32[]{:S(2)}) collective-permute-start(bf16[104,128,128]{2,1,0:T(8,128)(2,1)} %collective-permute-done.11.refs_1_), channel_id=1, source_target_pairs={{0,8},{24,16},{1,9},{25,17},{2,10},{26,18},{3,11},{27,19},{4,12},{... | collective-permute-start | bytes 10223624 | tf_op jit(solution)/shard_map/ppermute | solution.py:281
  339.2 12.7 %tiles_times_planes.13 = f32[3,256,512]{2,1,0:T(8,128)S(1)} custom-call(s32[248]{0:T(256)S(1)} %concatenate.76.info, bf16[512,32768]{1,0:T(8,128)(2,1)} %refs_0_.11, bf16[7680,256]{1,0:T(8,128)(2,1)} %pad_maximum_fusion.refs_1_, bf16[7680,256]{1,0:T(8,128)(2,1)} %collective-permute-done.9.refs_2_, bf16[7680,256]{1,0:T(8,128)(2,1)} %collective-permute-done.14.refs_3_, ...), custom_call_target="tpu_custom_call" | custom-call | flops 6039797760 | bytes 15728640 | tf_op jit(solution)/shard_map/tiles_times_planes/pallas_call | solution.py:186
  352.7 15.6 %tiles_times_planes.11 = f32[3,256,1024]{2,1,0:T(8,128)} custom-call(s32[298]{0:T(512)S(1)} %concatenate.70.info, bf16[512,32768]{1,0:T(8,128)(2,1)} %refs_0_.11, bf16[104,128,128]{2,1,0:T(8,128)(2,1)} %collective-permute-done.11.refs_1_, bf16[4608,256]{1,0:T(8,128)(2,1)S(1)} %pad_maximum_fusion.1.refs_2_.refs_1_, ...), custom_call_target="tpu_custom_call" | custom-call | flops 7247757312 | bytes 11796480 | tf_op jit(solution)/shard_map/tiles_times_planes/pallas_call | solution.py:186
  368.4 12.8 %tiles_times_planes.12 = f32[3,256,512]{2,1,0:T(8,128)S(1)} custom-call(s32[248]{0:T(256)S(1)} %concatenate.74.info, bf16[160,128,128]{2,1,0:T(8,128)(2,1)} %collective-permute-done.18.refs_0_.refs_1_, bf16[7680,256]{1,0:T(8,128)(2,1)} %pad_maximum_fusion.refs_1_, bf16[7680,256]{1,0:T(8,128)(2,1)} %collective-permute-done.9.refs_2_, ...), custom_call_target="tpu_custom_call" | custom-call | flops 6039797760 | bytes 15728640 | tf_op jit(solution)/shard_map/tiles_times_planes/pallas_call | solution.py:186
  381.6 1.5 copy-done.9
  385.2 1.4 constant_dynamic-slice_fusion.14
  387.3 7.2 %tiles_times_planes.15 = f32[2,256,512]{2,1,0:T(8,128)S(1)} custom-call(s32[150]{0:T(256)S(1)} %get-tuple-element.163.info, bf16[104,128,128]{2,1,0:T(8,128)(2,1)} %collective-permute-done.12.refs_0_, bf16[4608,256]{1,0:T(8,128)(2,1)S(1)} %pad_maximum_fusion.1.refs_2_.refs_1_, bf16[4608,256]{1,0:T(8,128)(2,1)} %collective-permute-done.17.refs_4_.refs_2_), custom_call_target="tpu_custom_call" | custom-call | flops 2415919104 | bytes 7077888 | tf_op jit(solution)/shard_map/tiles_times_planes/pallas_call | solution.py:186
  394.4 17.9 %collective-permute-done.34.refs_3_ = bf16[7680,256]{1,0:T(8,128)(2,1)} collective-permute-done((bf16[7680,256]{1,0:T(8,128)(2,1)}, bf16[7680,256]{1,0:T(8,128)(2,1)}, u32[]{:S(2)}, u32[]{:S(2)}) %collective-permute-start.34) | collective-permute-done | bytes 3932192 | tf_op jit(solution)/shard_map/ppermute | solution.py:281
  412.4 1.5 collective-permute-start.35
  413.9 5.9 %tiles_times_planes.16 = f32[1,256,512]{2,1,0:T(8,128)S(1)} custom-call(s32[150]{0:T(256)S(1)} %get-tuple-element.163.info, bf16[104,128,128]{2,1,0:T(8,128)(2,1)} %collective-permute-done.12.refs_0_, bf16[4608,256]{1,0:T(8,128)(2,1)S(1)} %collective-permute-done.24.refs_3_.refs_1_.refs_2_), custom_call_target="tpu_custom_call" | custom-call | flops 1207959552 | bytes 4718592 | tf_op jit(solution)/shard_map/tiles_times_planes/pallas_call | solution.py:186
  419.8 8.6 %tiles_times_planes.14 = f32[3,256,512]{2,1,0:T(8,128)S(1)} custom-call(s32[150]{0:T(256)S(1)} %get-tuple-element.164.info, bf16[104,128,128]{2,1,0:T(8,128)(2,1)} %collective-permute-done.23.refs_0_, bf16[4608,256]{1,0:T(8,128)(2,1)S(1)} %pad_maximum_fusion.1.refs_2_.refs_1_, bf16[4608,256]{1,0:T(8,128)(2,1)} %collective-permute-done.17.refs_4_.refs_2_, ...), custom_call_target="tpu_custom_call" | custom-call | flops 3623878656 | bytes 9437184 | tf_op jit(solution)/shard_map/tiles_times_planes/pallas_call | solution.py:186
  428.9 1.4 fusion.4
  433.8 2.2 dynamic-slice_add_fusion
  437.0 1.5 collective-permute-start.21
  438.6 11.7 %tiles_times_planes.18 = f32[1,256,1024]{2,1,0:T(8,128)S(1)} custom-call(s32[494]{0:T(512)S(1)} %concatenate.82.info, bf16[512,32768]{1,0:T(8,128)(2,1)} %refs_0_.11, bf16[160,128,128]{2,1,0:T(8,128)(2,1)} %collective-permute-done.18.refs_0_.refs_1_, bf16[7680,256]{1,0:T(8,128)(2,1)} %collective-permute-done.16.refs_2_, ...), custom_call_target="tpu_custom_call" | custom-call | flops 4026531840 | bytes 11796480 | tf_op jit(solution)/shard_map/tiles_times_planes/pallas_call | solution.py:186
  450.4 8.2 %tiles_times_planes.19 = f32[1,256,1024]{2,1,0:T(8,128)S(1)} custom-call(s32[298]{0:T(512)S(1)} %concatenate.70.info, bf16[512,32768]{1,0:T(8,128)(2,1)} %refs_0_.11, bf16[104,128,128]{2,1,0:T(8,128)(2,1)} %collective-permute-done.11.refs_1_, bf16[4608,256]{1,0:T(8,128)(2,1)S(1)} %copy-done.1), custom_call_target="tpu_custom_call" | custom-call | flops 2415919104 | bytes 7077888 | tf_op jit(solution)/shard_map/tiles_times_planes/pallas_call | solution.py:186
  458.6 1.7 fusion.6
  461.0 7.9 %tiles_times_planes.17 = f32[1,256,1024]{2,1,0:T(8,128)S(1)} custom-call(s32[268]{0:T(512)S(1)} %concatenate.66.info, bf16[512,32768]{1,0:T(8,128)(2,1)} %refs_0_.11, bf16[94,128,128]{2,1,0:T(8,128)(2,1)} %collective-permute-done.6.refs_1_, bf16[4096,256]{1,0:T(8,128)(2,1)} %collective-permute-done.15.refs_2_, bf16[4096,256]{1,0:T(8,128)(2,1)} %collective-permute-done.35.refs_3_), custom_call_target="tpu_custom_call" | custom-call | flops 2147483648 | bytes 6291456 | tf_op jit(solution)/shard_map/tiles_times_planes/pallas_call | solution.py:186
  470.4 9.7 %collective-permute-done.26 = f32[3,64,1024]{2,1,0:T(8,128)S(1)} collective-permute-done((f32[3,64,1024]{2,1,0:T(8,128)S(1)}, f32[3,64,1024]{2,1,0:T(8,128)S(1)}, u32[]{:S(2)}, u32[]{:S(2)}) %collective-permute-start.26) | collective-permute-done | bytes 786464 | tf_op jit(solution)/shard_map/ppermute | solution.py:266
  480.3 1.6 collective-permute-start.27
  483.2 9.2 %collective-permute-done.27 = f32[3,32,1024]{2,1,0:T(8,128)S(1)} collective-permute-done((f32[3,32,1024]{2,1,0:T(8,128)S(1)}, f32[3,32,1024]{2,1,0:T(8,128)S(1)}, u32[]{:S(2)}, u32[]{:S(2)}) %collective-permute-start.27) | collective-permute-done | bytes 393248 | tf_op jit(solution)/shard_map/ppermute | solution.py:266
  493.7 5.5 collective-permute-done.22
  499.3 1.6 collective-permute-start.38
  500.9 3.0 collective-permute-done.28
  505.8 2.7 collective-permute-start.39
  509.3 6.7 %collective-permute-done.39 = f32[40,1024]{1,0:T(8,128)S(1)} collective-permute-done((f32[40,1024]{1,0:T(8,128)S(1)}, f32[40,1024]{1,0:T(8,128)S(1)}, u32[]{:S(2)}, u32[]{:S(2)}) %collective-permute-start.39) | collective-permute-done | bytes 163872 | tf_op jit(solution)/shard_map/ppermute | solution.py:286
  523.0 1.8 collective-permute-done.41
  524.8 1.5 collective-permute-start.33
  526.3 6.8 %collective-permute-done.43 = f32[40,1024]{1,0:T(8,128)S(1)} collective-permute-done((f32[40,1024]{1,0:T(8,128)S(1)}, f32[40,1024]{1,0:T(8,128)S(1)}, u32[]{:S(2)}, u32[]{:S(2)}) %collective-permute-start.43) | collective-permute-done | bytes 163872 | tf_op jit(solution)/shard_map/ppermute | solution.py:290
  533.2 8.3 %collective-permute-done.31 = f32[3,32,1024]{2,1,0:T(8,128)S(1)} collective-permute-done((f32[3,32,1024]{2,1,0:T(8,128)S(1)}, f32[3,32,1024]{2,1,0:T(8,128)S(1)}, u32[]{:S(2)}, u32[]{:S(2)}) %collective-permute-start.31) | collective-permute-done | bytes 393248 | tf_op jit(solution)/shard_map/ppermute | solution.py:289
  541.6 4.2 collective-permute-done.33
  546.0 9.3 %pair_dots.1 = f32[32,136,128]{2,1,0:T(8,128)S(1)} custom-call(s32[2,6,32]{2,1,0:T(8,128)S(1)} %pad_add_fusion.ids, f32[4,3,32,1024]{3,2,1,0:T(8,128)S(1)} %pad_maximum_fusion.4.early, f32[4,40,1024]{2,1,0:T(8,128)S(1)} %pad_maximum_fusion.5.late), custom_call_target="tpu_custom_call" | custom-call | tf_op jit(solution)/shard_map/pair_dots/pallas_call | solution.py:242
  555.5 2.9 collective-permute-done.44
  560.8 7.7 %collective-permute-done.47 = f32[2,1,1,2,136,128]{5,4,3,2,1,0:T(8,128)S(1)} collective-permute-done((f32[2,1,1,2,136,128]{5,4,3,2,1,0:T(8,128)S(1)}, f32[2,1,1,2,136,128]{5,4,3,2,1,0:T(8,128)S(1)}, u32[]{:S(2)}, u32[]{:S(2)}) %collective-permute-start.47) | collective-permute-done | bytes 278560 | tf_op jit(solution)/shard_map/ppermute | solution.py:266
  570.5 3.2 collective-permute-done.48
  (271 shorter events, 53.1 us)
Async XLA Ops:
  6.5 13.5 %collective-permute-start = (s32[16,2]{0,1:T(2,128)}, s32[16,2]{0,1:T(2,128)S(1)}, u32[]{:S(2)}, u32[]{:S(2)}) collective-permute-start(s32[16,2]{0,1:T(2,128)} %param.12), channel_id=1, source_target_pairs={{0,4},{4,0},{1,5},{5,1},{2,6},{6,2},{3,7},{7,3},{8,12},{12,8},{9,1... | collective-permute-start | bytes 392 | tf_op jit(solution)/shard_map/ppermute | solution.py:370
  10.2 5.4 collective-permute-start.1
  15.0 24.5 %collective-permute-start.3 = (bf16[4096,128]{1,0:T(8,128)(2,1)S(1)}, bf16[4096,128]{1,0:T(8,128)(2,1)S(1)}, u32[]{:S(2)}, u32[]{:S(2)}) collective-permute-start(bf16[4096,128]{1,0:T(8,128)(2,1)S(1)} %constant_dynamic-slice_fusion.18), channel_id=1, source_target_pairs={{0,4},{4,0},{1,5},{5,1},{2,6},{6,2},{3,7},{7,3},{8,12},{12,8},{9,1... | collective-permute-start | bytes 3145736 | tf_op jit(solution)/shard_map/ppermute | solution.py:281
  15.6 23.9 %collective-permute-start.2 = (s32[2,4,128]{2,1,0:T(4,128)S(1)}, s32[2,4,128]{2,1,0:T(4,128)S(1)}, u32[]{:S(2)}, u32[]{:S(2)}) collective-permute-start(s32[2,4,128]{2,1,0:T(4,128)S(1)} %get-tuple-element.152), channel_id=1, source_target_pairs={{0,4},{4,0},{1,5},{5,1},{2,6},{6,2},{3,7},{7,3},{8,12},{12,8},{9,1... | collective-permute-start | bytes 12296 | tf_op jit(solution)/shard_map/ppermute | solution.py:369
  39.5 43.3 %collective-permute-start.4 = (bf16[7680,128]{1,0:T(8,128)(2,1)}, bf16[7680,128]{1,0:T(8,128)(2,1)S(1)}, u32[]{:S(2)}, u32[]{:S(2)}) collective-permute-start(bf16[7680,128]{1,0:T(8,128)(2,1)} %constant_dynamic-slice_fusion.16), channel_id=1, source_target_pairs={{0,4},{4,0},{1,5},{5,1},{2,6},{6,2},{3,7},{7,3},{8,12},{12,8},{9,1... | collective-permute-start | bytes 5898248 | tf_op jit(solution)/shard_map/ppermute | solution.py:281
  43.2 42.4 %copy-start.2 = (bf16[4096,256]{1,0:T(8,128)(2,1)}, bf16[4096,256]{1,0:T(8,128)(2,1)S(1)}, u32[]{:S(2)}) copy-start(bf16[4096,256]{1,0:T(8,128)(2,1)S(1)} %pad_maximum_fusion.2.refs_2_) | copy-start | bytes 6291460
  43.2 66.0 %collective-permute-start.7 = (bf16[4096,256]{1,0:T(8,128)(2,1)S(1)}, bf16[4096,256]{1,0:T(8,128)(2,1)}, u32[]{:S(2)}, u32[]{:S(2)}) collective-permute-start(bf16[4096,256]{1,0:T(8,128)(2,1)S(1)} %pad_maximum_fusion.2.refs_2_), channel_id=1, source_target_pairs={{0,8},{8,0},{16,24},{24,16},{1,9},{9,1},{17,25},{25,17},{2,10},{10... | collective-permute-start | bytes 6291464 | tf_op jit(solution)/shard_map/ppermute | solution.py:281
  43.3 44.6 %collective-permute-start.8 = (bf16[4096,256]{1,0:T(8,128)(2,1)S(1)}, bf16[4096,256]{1,0:T(8,128)(2,1)S(1)}, u32[]{:S(2)}, u32[]{:S(2)}) collective-permute-start(bf16[4096,256]{1,0:T(8,128)(2,1)S(1)} %pad_maximum_fusion.2.refs_2_), channel_id=1, source_target_pairs={{8,16},{16,8},{9,17},{17,9},{10,18},{18,10},{11,19},{19,11},{12,20... | collective-permute-start | bytes 6291464 | tf_op jit(solution)/shard_map/ppermute | solution.py:281
  82.7 25.9 %collective-permute-start.5 = (bf16[4608,128]{1,0:T(8,128)(2,1)S(1)}, bf16[4608,128]{1,0:T(8,128)(2,1)}, u32[]{:S(2)}, u32[]{:S(2)}) collective-permute-start(bf16[4608,128]{1,0:T(8,128)(2,1)S(1)} %constant_dynamic-slice_fusion.17), channel_id=1, source_target_pairs={{0,4},{4,0},{1,5},{5,1},{2,6},{6,2},{3,7},{7,3},{8,12},{12,8},{9,1... | collective-permute-start | bytes 3538952 | tf_op jit(solution)/shard_map/ppermute | solution.py:281
  89.2 87.1 %collective-permute-start.14 = (bf16[7680,256]{1,0:T(8,128)(2,1)}, bf16[7680,256]{1,0:T(8,128)(2,1)}, u32[]{:S(2)}, u32[]{:S(2)}) collective-permute-start(bf16[7680,256]{1,0:T(8,128)(2,1)} %pad_maximum_fusion.refs_1_), channel_id=1, source_target_pairs={{8,16},{16,8},{9,17},{17,9},{10,18},{18,10},{11,19},{19,11},{12,20... | collective-permute-start | bytes 11796488 | tf_op jit(solution)/shard_map/ppermute | solution.py:281
  108.7 67.1 %collective-permute-start.6 = (bf16[94,128,128]{2,1,0:T(8,128)(2,1)}, bf16[94,128,128]{2,1,0:T(8,128)(2,1)}, u32[]{:S(2)}, u32[]{:S(2)}) collective-permute-start(bf16[94,128,128]{2,1,0:T(8,128)(2,1)} %pack_tiles.4), channel_id=1, source_target_pairs={{0,4},{4,0},{1,5},{5,1},{2,6},{6,2},{3,7},{7,3},{8,12},{12,8},{9,1... | collective-permute-start | bytes 9240584 | tf_op jit(solution)/shard_map/ppermute | solution.py:281
  109.2 83.2 %collective-permute-start.9 = (bf16[7680,256]{1,0:T(8,128)(2,1)}, bf16[7680,256]{1,0:T(8,128)(2,1)}, u32[]{:S(2)}, u32[]{:S(2)}) collective-permute-start(bf16[7680,256]{1,0:T(8,128)(2,1)} %pad_maximum_fusion.refs_1_), channel_id=1, source_target_pairs={{0,8},{8,0},{16,24},{24,16},{1,9},{9,1},{17,25},{25,17},{2,10},{10... | collective-permute-start | bytes 11796488 | tf_op jit(solution)/shard_map/ppermute | solution.py:281
  175.7 73.7 %collective-permute-start.11 = (bf16[104,128,128]{2,1,0:T(8,128)(2,1)S(1)}, bf16[104,128,128]{2,1,0:T(8,128)(2,1)}, u32[]{:S(2)}, u32[]{:S(2)}) collective-permute-start(bf16[104,128,128]{2,1,0:T(8,128)(2,1)S(1)} %pack_tiles.5), channel_id=1, source_target_pairs={{0,4},{4,0},{1,5},{5,1},{2,6},{6,2},{3,7},{7,3},{8,12},{12,8},{9,1... | collective-permute-start | bytes 10223624 | tf_op jit(solution)/shard_map/ppermute | solution.py:281
  176.3 31.3 %collective-permute-start.15 = (bf16[4096,256]{1,0:T(8,128)(2,1)}, bf16[4096,256]{1,0:T(8,128)(2,1)}, u32[]{:S(2)}, u32[]{:S(2)}) collective-permute-start(bf16[4096,256]{1,0:T(8,128)(2,1)} %collective-permute-done.7.refs_3_), channel_id=1, source_target_pairs={{8,16},{16,8},{9,17},{17,9},{10,18},{18,10},{11,19},{19,11},{12,20... | collective-permute-start | bytes 6291464 | tf_op jit(solution)/shard_map/ppermute | solution.py:281
  192.4 45.8 %collective-permute-start.10 = (bf16[4096,256]{1,0:T(8,128)(2,1)}, bf16[4096,256]{1,0:T(8,128)(2,1)}, u32[]{:S(2)}, u32[]{:S(2)}) collective-permute-start(bf16[4096,256]{1,0:T(8,128)(2,1)} %copy-done.14), channel_id=1, source_target_pairs={{8,0},{16,24},{9,1},{17,25},{10,2},{18,26},{11,3},{19,27},{12,4},{... | collective-permute-start | bytes 6291464 | tf_op jit(solution)/shard_map/ppermute | solution.py:281
  198.9 75.6 %collective-permute-start.12 = (bf16[104,128,128]{2,1,0:T(8,128)(2,1)}, bf16[104,128,128]{2,1,0:T(8,128)(2,1)}, u32[]{:S(2)}, u32[]{:S(2)}) collective-permute-start(bf16[104,128,128]{2,1,0:T(8,128)(2,1)} %pack_tiles.6), channel_id=1, source_target_pairs={{0,8},{24,16},{1,9},{25,17},{2,10},{26,18},{3,11},{27,19},{4,12},{... | collective-permute-start | bytes 10223624 | tf_op jit(solution)/shard_map/ppermute | solution.py:281
  207.6 75.0 %collective-permute-start.16 = (bf16[7680,256]{1,0:T(8,128)(2,1)}, bf16[7680,256]{1,0:T(8,128)(2,1)}, u32[]{:S(2)}, u32[]{:S(2)}) collective-permute-start(bf16[7680,256]{1,0:T(8,128)(2,1)} %collective-permute-done.9.refs_2_), channel_id=1, source_target_pairs={{8,16},{16,8},{9,17},{17,9},{10,18},{18,10},{11,19},{19,11},{12,20... | collective-permute-start | bytes 11796488 | tf_op jit(solution)/shard_map/ppermute | solution.py:281
  238.2 83.3 %collective-permute-start.19 = (bf16[7680,256]{1,0:T(8,128)(2,1)}, bf16[7680,256]{1,0:T(8,128)(2,1)}, u32[]{:S(2)}, u32[]{:S(2)}) collective-permute-start(bf16[7680,256]{1,0:T(8,128)(2,1)} %collective-permute-done.14.refs_3_), channel_id=1, source_target_pairs={{8,0},{16,24},{9,1},{17,25},{10,2},{18,26},{11,3},{19,27},{12,4},{... | collective-permute-start | bytes 11796488 | tf_op jit(solution)/shard_map/ppermute | solution.py:281
  249.4 118.9 %collective-permute-start.18 = (bf16[160,128,128]{2,1,0:T(8,128)(2,1)}, bf16[160,128,128]{2,1,0:T(8,128)(2,1)}, u32[]{:S(2)}, u32[]{:S(2)}) collective-permute-start(bf16[160,128,128]{2,1,0:T(8,128)(2,1)} %pack_tiles.7), channel_id=1, source_target_pairs={{0,4},{4,0},{1,5},{5,1},{2,6},{6,2},{3,7},{7,3},{8,12},{12,8},{9,1... | collective-permute-start | bytes 15728648 | tf_op jit(solution)/shard_map/ppermute | solution.py:281
  274.5 48.9 %collective-permute-start.13 = (bf16[4608,256]{1,0:T(8,128)(2,1)S(1)}, bf16[4608,256]{1,0:T(8,128)(2,1)}, u32[]{:S(2)}, u32[]{:S(2)}) collective-permute-start(bf16[4608,256]{1,0:T(8,128)(2,1)S(1)} %pad_maximum_fusion.1.refs_2_.refs_1_), channel_id=1, source_target_pairs={{0,8},{24,16},{1,9},{25,17},{2,10},{26,18},{3,11},{27,19},{4,12},{... | collective-permute-start | bytes 7077896 | tf_op jit(solution)/shard_map/ppermute | solution.py:281
  282.6 69.3 %collective-permute-start.17 = (bf16[4608,256]{1,0:T(8,128)(2,1)S(1)}, bf16[4608,256]{1,0:T(8,128)(2,1)}, u32[]{:S(2)}, u32[]{:S(2)}) collective-permute-start(bf16[4608,256]{1,0:T(8,128)(2,1)S(1)} %pad_maximum_fusion.1.refs_2_.refs_1_), channel_id=1, source_target_pairs={{8,16},{16,8},{9,17},{17,9},{10,18},{18,10},{11,19},{19,11},{12,20... | collective-permute-start | bytes 7077896 | tf_op jit(solution)/shard_map/ppermute | solution.py:281
  285.1 1.6 copy-start.3
  321.5 90.9 %collective-permute-start.34 = (bf16[7680,256]{1,0:T(8,128)(2,1)}, bf16[7680,256]{1,0:T(8,128)(2,1)}, u32[]{:S(2)}, u32[]{:S(2)}) collective-permute-start(bf16[7680,256]{1,0:T(8,128)(2,1)} %collective-permute-done.16.refs_2_), channel_id=1, source_target_pairs={{8,0},{16,24},{9,1},{17,25},{10,2},{18,26},{11,3},{19,27},{12,4},{... | collective-permute-start | bytes 11796488 | tf_op jit(solution)/shard_map/ppermute | solution.py:281
  323.4 96.4 %collective-permute-start.23 = (bf16[104,128,128]{2,1,0:T(8,128)(2,1)}, bf16[104,128,128]{2,1,0:T(8,128)(2,1)}, u32[]{:S(2)}, u32[]{:S(2)}) collective-permute-start(bf16[104,128,128]{2,1,0:T(8,128)(2,1)} %collective-permute-done.11.refs_1_), channel_id=1, source_target_pairs={{0,8},{24,16},{1,9},{25,17},{2,10},{26,18},{3,11},{27,19},{4,12},{... | collective-permute-start | bytes 10223624 | tf_op jit(solution)/shard_map/ppermute | solution.py:281
  351.9 62.0 %collective-permute-start.24 = (bf16[4608,256]{1,0:T(8,128)(2,1)}, bf16[4608,256]{1,0:T(8,128)(2,1)S(1)}, u32[]{:S(2)}, u32[]{:S(2)}) collective-permute-start(bf16[4608,256]{1,0:T(8,128)(2,1)} %collective-permute-done.13.refs_3_), channel_id=1, source_target_pairs={{8,16},{16,8},{9,17},{17,9},{10,18},{18,10},{11,19},{19,11},{12,20... | collective-permute-start | bytes 7077896 | tf_op jit(solution)/shard_map/ppermute | solution.py:281
  381.2 1.9 copy-start.9
  381.2 2.8 copy-start.10
  385.2 2.1 copy-start.11
  386.6 47.2 %collective-permute-start.20 = (f32[3,128,1024]{2,1,0:T(8,128)}, f32[3,128,1024]{2,1,0:T(8,128)}, u32[]{:S(2)}, u32[]{:S(2)}) collective-permute-start(f32[3,128,1024]{2,1,0:T(8,128)} %constant_dynamic-slice_fusion.14), channel_id=1, source_target_pairs={{0,1},{1,0},{2,3},{3,2},{4,5},{5,4},{6,7},{7,6},{8,9},{9,8},{10,11... | collective-permute-start | bytes 4718600 | tf_op jit(solution)/shard_map/ppermute | solution.py:266
  412.4 48.6 %collective-permute-start.35 = (bf16[4096,256]{1,0:T(8,128)(2,1)}, bf16[4096,256]{1,0:T(8,128)(2,1)}, u32[]{:S(2)}, u32[]{:S(2)}) collective-permute-start(bf16[4096,256]{1,0:T(8,128)(2,1)} %collective-permute-done.15.refs_2_), channel_id=1, source_target_pairs={{8,0},{16,24},{9,1},{17,25},{10,2},{18,26},{11,3},{19,27},{12,4},{... | collective-permute-start | bytes 6291464 | tf_op jit(solution)/shard_map/ppermute | solution.py:281
  413.9 5.9 %copy-start = (bf16[4608,256]{1,0:T(8,128)(2,1)}, bf16[4608,256]{1,0:T(8,128)(2,1)S(1)}, u32[]{:S(2)}) copy-start(bf16[4608,256]{1,0:T(8,128)(2,1)S(1)} %collective-permute-done.24.refs_3_.refs_1_.refs_2_) | copy-start | bytes 7077892
  428.8 1.6 copy-start.5
  428.8 2.2 copy-start.7
  428.8 4.2 copy-start.4
  428.9 4.2 copy-start.17
  431.0 27.5 %collective-permute-start.25 = (f32[3,128,1024]{2,1,0:T(8,128)}, f32[3,128,1024]{2,1,0:T(8,128)}, u32[]{:S(2)}, u32[]{:S(2)}) collective-permute-start(f32[3,128,1024]{2,1,0:T(8,128)} %fusion.4), channel_id=1, source_target_pairs={{0,1},{1,0},{2,3},{3,2},{4,5},{5,4},{6,7},{7,6},{8,9},{9,8},{10,11... | collective-permute-start | bytes 4718600 | tf_op jit(solution)/shard_map/ppermute | solution.py:266
  435.9 2.6 copy-start.12
  437.0 32.3 %collective-permute-start.21 = (f32[3,64,1024]{2,1,0:T(8,128)}, f32[3,64,1024]{2,1,0:T(8,128)S(1)}, u32[]{:S(2)}, u32[]{:S(2)}) collective-permute-start(f32[3,64,1024]{2,1,0:T(8,128)} %constant_dynamic-slice_fusion.13), channel_id=1, source_target_pairs={{0,4},{4,0},{1,5},{5,1},{2,6},{6,2},{3,7},{7,3},{8,12},{12,8},{9,1... | collective-permute-start | bytes 2359304 | tf_op jit(solution)/shard_map/ppermute | solution.py:266
  438.6 11.8 %copy-start.1 = (bf16[4608,256]{1,0:T(8,128)(2,1)S(1)}, bf16[4608,256]{1,0:T(8,128)(2,1)}, u32[]{:S(2)}) copy-start(bf16[4608,256]{1,0:T(8,128)(2,1)} %copy-done) | copy-start | bytes 7077892
  450.3 8.2 %copy-start.6 = (f32[3,256,512]{2,1,0:T(8,128)S(1)}, f32[3,256,512]{2,1,0:T(8,128)}, u32[]{:S(2)}) copy-start(f32[3,256,512]{2,1,0:T(8,128)} %copy-done.5) | copy-start | bytes 4718596
  450.4 8.2 %copy-start.8 = (f32[3,256,512]{2,1,0:T(8,128)S(1)}, f32[3,256,512]{2,1,0:T(8,128)}, u32[]{:S(2)}) copy-start(f32[3,256,512]{2,1,0:T(8,128)} %copy-done.7) | copy-start | bytes 4718596
  460.4 19.7 %collective-permute-start.26 = (f32[3,64,1024]{2,1,0:T(8,128)S(1)}, f32[3,64,1024]{2,1,0:T(8,128)S(1)}, u32[]{:S(2)}, u32[]{:S(2)}) collective-permute-start(f32[3,64,1024]{2,1,0:T(8,128)S(1)} %constant_dynamic-slice_fusion.11), channel_id=1, source_target_pairs={{0,4},{4,0},{1,5},{5,1},{2,6},{6,2},{3,7},{7,3},{8,12},{12,8},{9,1... | collective-permute-start | bytes 2359304 | tf_op jit(solution)/shard_map/ppermute | solution.py:266
  468.8 1.4 copy-start.13
  469.2 13.2 %collective-permute-start.36 = (f32[1,128,1024]{2,1,0:T(8,128)S(1)}, f32[1,128,1024]{2,1,0:T(8,128)S(1)}, u32[]{:S(2)}, u32[]{:S(2)}) collective-permute-start(f32[1,128,1024]{2,1,0:T(8,128)S(1)} %constant_dynamic-slice_fusion.9), channel_id=1, source_target_pairs={{0,1},{1,0},{2,3},{3,2},{4,5},{5,4},{6,7},{7,6},{8,9},{9,8},{10,11... | collective-permute-start | bytes 1572872 | tf_op jit(solution)/shard_map/ppermute | solution.py:266
  480.3 12.1 %collective-permute-start.27 = (f32[3,32,1024]{2,1,0:T(8,128)S(1)}, f32[3,32,1024]{2,1,0:T(8,128)S(1)}, u32[]{:S(2)}, u32[]{:S(2)}) collective-permute-start(f32[3,32,1024]{2,1,0:T(8,128)S(1)} %constant_dynamic-slice_fusion.10), channel_id=1, source_target_pairs={{0,2},{2,0},{1,3},{3,1},{4,6},{6,4},{5,7},{7,5},{8,10},{10,8},{9,1... | collective-permute-start | bytes 1179656 | tf_op jit(solution)/shard_map/ppermute | solution.py:266
  481.9 17.3 %collective-permute-start.22 = (f32[3,32,1024]{2,1,0:T(8,128)S(1)}, f32[3,32,1024]{2,1,0:T(8,128)S(1)}, u32[]{:S(2)}, u32[]{:S(2)}) collective-permute-start(f32[3,32,1024]{2,1,0:T(8,128)S(1)} %constant_dynamic-slice_fusion.12), channel_id=1, source_target_pairs={{0,2},{2,0},{1,3},{3,1},{4,6},{6,4},{5,7},{7,5},{8,10},{10,8},{9,1... | collective-permute-start | bytes 1179656 | tf_op jit(solution)/shard_map/ppermute | solution.py:266
  482.6 16.7 %collective-permute-start.37 = (f32[1,64,1024]{2,1,0:T(8,128)S(1)}, f32[1,64,1024]{2,1,0:T(8,128)S(1)}, u32[]{:S(2)}, u32[]{:S(2)}) collective-permute-start(f32[1,64,1024]{2,1,0:T(8,128)S(1)} %constant_dynamic-slice_fusion.8), channel_id=1, source_target_pairs={{0,4},{4,0},{1,5},{5,1},{2,6},{6,2},{3,7},{7,3},{8,12},{12,8},{9,1... | collective-permute-start | bytes 786440 | tf_op jit(solution)/shard_map/ppermute | solution.py:266
  492.4 11.4 %collective-permute-start.28 = (f32[3,32,1024]{2,1,0:T(8,128)S(1)}, f32[3,32,1024]{2,1,0:T(8,128)S(1)}, u32[]{:S(2)}, u32[]{:S(2)}) collective-permute-start(f32[3,32,1024]{2,1,0:T(8,128)S(1)} %dynamic-slice_add_fusion.5), channel_id=1, source_target_pairs={{8,0},{16,24},{9,1},{17,25},{10,2},{18,26},{11,3},{19,27},{12,4},{... | collective-permute-start | bytes 1179656 | tf_op jit(solution)/shard_map/ppermute | solution.py:440
  499.3 6.5 %collective-permute-start.38 = (f32[1,32,1024]{2,1,0:T(8,128)S(1)}, f32[1,32,1024]{2,1,0:T(8,128)S(1)}, u32[]{:S(2)}, u32[]{:S(2)}) collective-permute-start(f32[1,32,1024]{2,1,0:T(8,128)S(1)} %constant_dynamic-slice_fusion.7), channel_id=1, source_target_pairs={{0,2},{2,0},{1,3},{3,1},{4,6},{6,4},{5,7},{7,5},{8,10},{10,8},{9,1... | collective-permute-start | bytes 393224 | tf_op jit(solution)/shard_map/ppermute | solution.py:266
  503.9 14.1 %collective-permute-start.29 = (f32[3,32,1024]{2,1,0:T(8,128)S(1)}, f32[3,32,1024]{2,1,0:T(8,128)S(1)}, u32[]{:S(2)}, u32[]{:S(2)}) collective-permute-start(f32[3,32,1024]{2,1,0:T(8,128)S(1)} %fusion.9), channel_id=1, source_target_pairs={{0,8},{8,0},{16,24},{24,16},{1,9},{9,1},{17,25},{25,17},{2,10},{10... | collective-permute-start | bytes 1179656 | tf_op jit(solution)/shard_map/ppermute | solution.py:286
  505.1 16.6 %collective-permute-start.30 = (f32[3,32,1024]{2,1,0:T(8,128)S(1)}, f32[3,32,1024]{2,1,0:T(8,128)S(1)}, u32[]{:S(2)}, u32[]{:S(2)}) collective-permute-start(f32[3,32,1024]{2,1,0:T(8,128)S(1)} %fusion.9), channel_id=1, source_target_pairs={{8,16},{16,8},{9,17},{17,9},{10,18},{18,10},{11,19},{19,11},{12,20... | collective-permute-start | bytes 1179656 | tf_op jit(solution)/shard_map/ppermute | solution.py:287
  505.8 10.2 %collective-permute-start.39 = (f32[40,1024]{1,0:T(8,128)S(1)}, f32[40,1024]{1,0:T(8,128)S(1)}, u32[]{:S(2)}, u32[]{:S(2)}) collective-permute-start(f32[40,1024]{1,0:T(8,128)S(1)} %get-tuple-element.150), channel_id=1, source_target_pairs={{0,8},{8,0},{16,24},{24,16},{1,9},{9,1},{17,25},{25,17},{2,10},{10... | collective-permute-start | bytes 491528 | tf_op jit(solution)/shard_map/ppermute | solution.py:286
  508.6 8.2 %collective-permute-start.40 = (f32[40,1024]{1,0:T(8,128)S(1)}, f32[40,1024]{1,0:T(8,128)S(1)}, u32[]{:S(2)}, u32[]{:S(2)}) collective-permute-start(f32[40,1024]{1,0:T(8,128)S(1)} %get-tuple-element.150), channel_id=1, source_target_pairs={{8,16},{16,8},{9,17},{17,9},{10,18},{18,10},{11,19},{19,11},{12,20... | collective-permute-start | bytes 491528 | tf_op jit(solution)/shard_map/ppermute | solution.py:287
  516.1 4.3 collective-permute-start.42
  516.8 8.0 %collective-permute-start.41 = (f32[40,1024]{1,0:T(8,128)S(1)}, f32[40,1024]{1,0:T(8,128)S(1)}, u32[]{:S(2)}, u32[]{:S(2)}) collective-permute-start(f32[40,1024]{1,0:T(8,128)S(1)} %collective-permute-done.40), channel_id=1, source_target_pairs={{8,0},{16,24},{9,1},{17,25},{10,2},{18,26},{11,3},{19,27},{12,4},{... | collective-permute-start | bytes 491528 | tf_op jit(solution)/shard_map/ppermute | solution.py:289
  518.1 6.7 %collective-permute-start.32 = (f32[3,32,1024]{2,1,0:T(8,128)S(1)}, f32[3,32,1024]{2,1,0:T(8,128)S(1)}, u32[]{:S(2)}, u32[]{:S(2)}) collective-permute-start(f32[3,32,1024]{2,1,0:T(8,128)S(1)} %collective-permute-done.29), channel_id=1, source_target_pairs={{8,16},{16,8},{9,17},{17,9},{10,18},{18,10},{11,19},{19,11},{12,20... | collective-permute-start | bytes 1179656 | tf_op jit(solution)/shard_map/ppermute | solution.py:288
  520.3 12.8 %collective-permute-start.43 = (f32[40,1024]{1,0:T(8,128)S(1)}, f32[40,1024]{1,0:T(8,128)S(1)}, u32[]{:S(2)}, u32[]{:S(2)}) collective-permute-start(f32[40,1024]{1,0:T(8,128)S(1)} %collective-permute-done.42), channel_id=1, source_target_pairs={{8,0},{16,24},{9,1},{17,25},{10,2},{18,26},{11,3},{19,27},{12,4},{... | collective-permute-start | bytes 491528 | tf_op jit(solution)/shard_map/ppermute | solution.py:290
  521.7 19.9 %collective-permute-start.31 = (f32[3,32,1024]{2,1,0:T(8,128)S(1)}, f32[3,32,1024]{2,1,0:T(8,128)S(1)}, u32[]{:S(2)}, u32[]{:S(2)}) collective-permute-start(f32[3,32,1024]{2,1,0:T(8,128)S(1)} %collective-permute-done.30), channel_id=1, source_target_pairs={{8,0},{16,24},{9,1},{17,25},{10,2},{18,26},{11,3},{19,27},{12,4},{... | collective-permute-start | bytes 1179656 | tf_op jit(solution)/shard_map/ppermute | solution.py:289
  524.8 21.0 %collective-permute-start.33 = (f32[3,32,1024]{2,1,0:T(8,128)S(1)}, f32[3,32,1024]{2,1,0:T(8,128)S(1)}, u32[]{:S(2)}, u32[]{:S(2)}) collective-permute-start(f32[3,32,1024]{2,1,0:T(8,128)S(1)} %collective-permute-done.32), channel_id=1, source_target_pairs={{8,0},{16,24},{9,1},{17,25},{10,2},{18,26},{11,3},{19,27},{12,4},{... | collective-permute-start | bytes 1179656 | tf_op jit(solution)/shard_map/ppermute | solution.py:290
  555.4 3.0 collective-permute-start.44
  559.8 8.8 %collective-permute-start.47 = (f32[2,1,1,2,136,128]{5,4,3,2,1,0:T(8,128)S(1)}, f32[2,1,1,2,136,128]{5,4,3,2,1,0:T(8,128)S(1)}, u32[]{:S(2)}, u32[]{:S(2)}) collective-permute-start(f32[2,1,1,2,136,128]{5,4,3,2,1,0:T(8,128)S(1)} %constant_dynamic-slice_fusion.3), channel_id=1, source_target_pairs={{0,2},{2,0},{1,3},{3,1},{4,6},{6,4},{5,7},{7,5},{8,10},{10,8},{9,1... | collective-permute-start | bytes 835592 | tf_op jit(solution)/shard_map/ppermute | solution.py:266
  560.0 9.4 %collective-permute-start.45 = (f32[1,2,1,2,136,128]{5,4,3,2,1,0:T(8,128)S(1)}, f32[1,2,1,2,136,128]{5,4,3,2,1,0:T(8,128)S(1)}, u32[]{:S(2)}, u32[]{:S(2)}) collective-permute-start(f32[1,2,1,2,136,128]{5,4,3,2,1,0:T(8,128)S(1)} %constant_dynamic-slice_fusion.5), channel_id=1, source_target_pairs={{0,4},{4,0},{1,5},{5,1},{2,6},{6,2},{3,7},{7,3},{8,12},{12,8},{9,1... | collective-permute-start | bytes 835592 | tf_op jit(solution)/shard_map/ppermute | solution.py:266
  568.6 5.1 collective-permute-start.48
  569.5 5.1 collective-permute-start.46
  (2 other events, 2.0 us)
